TPU v7x, 32 devices: a whole 2x2x4 slice. The times are simulated.
32 devices in a mesh: narrow: 4 (over y, core), wide: 8 (over z, x).
Axes of the slice: x: 2, y: 2, z: 4, core: 2. Of those that a mesh axis runs over, the one named last changes fastest.
Arguments:
- queries: bfloat16 [32768, 128], P(('wide', 'narrow')), may hold values from -0.5 to 0.5
- keys: bfloat16 [32768, 128], P(('wide', 'narrow')), may hold values from -6 to 6
- values: bfloat16 [32768, 1024], P(('wide', 'narrow')), may hold values from -6 to 6
- log_decay: float32 [8, 32768], P(None, ('wide', 'narrow')), may hold values from -1 to 0
- level_weight: float32 [8, 8, 32768], P(None, None, ('wide', 'narrow')), may hold values from 0 to 2
- norm_gain: float32 [1024], replicated, may hold values from 0.5 to 1.5
Outputs:
- layer_output: bfloat16 [32768, 1024], P(('wide', 'narrow'))
All inputs are finite; a program needn't handle non-finite values.
Results may differ from a plain program's by a relative error of at most 0.005.
Values sent between devices are 32-bit elements; how exact they have to be, the bound alone decides.
No kernel may reach another device: no remote copies, remote signals or barrier semaphores. Data moves between devices by JAX's collectives and lax.ppermute only.
A program may use at most 128 MiB of HBM per device.

v0:
```python
import jax
import jax.numpy as jnp
import numpy as np
from jax import lax
from jax.sharding import PartitionSpec as P

SPAN = 256


def partner(value, axis, distance):
    mask = 2**distance
    pairs = [(source, source ^ mask) for source in range(lax.axis_size(axis))]
    return lax.ppermute(value, axis, pairs)


def doubling(state, total, trade, bit_count, position):
    prefix = jnp.zeros_like(total)
    found = []
    for bit in range(bit_count):
        other_state, other_total = trade(state, total, bit)
        upper = jnp.bitwise_and(jnp.right_shift(position, bit), 1) == 1
        found.append(jnp.where(upper, other_state * jnp.exp(prefix)[:, None, None], 0.0))
        prefix = jnp.where(upper, prefix + other_total, prefix)
        state = jnp.where(
            upper,
            other_state * jnp.exp(total)[:, None, None] + state,
            state * jnp.exp(other_total)[:, None, None] + other_state,
        )
        total = total + other_total
    levels_found = jnp.stack(found)
    return (levels_found, state, total, prefix)


def per_device(queries, keys, values, log_decay, level_weight, norm_gain):
    tokens_here, key_width = queries.shape
    heads = log_decay.shape[0]
    head_width = values.shape[1] // heads
    level_count = level_weight.shape[0]
    blocks = tokens_here // SPAN
    local_bits = blocks.bit_length() - 1
    query_blocks = queries.reshape(blocks, SPAN, key_width)
    key_blocks = keys.reshape(blocks, SPAN, key_width)
    value_blocks = values.reshape(blocks, SPAN, heads, head_width)
    decay_blocks = log_decay.reshape(heads, blocks, SPAN).transpose(1, 0, 2)
    within = jnp.cumsum(decay_blocks, axis=2)
    block_totals = within[:, :, -1]
    weights = level_weight.reshape(level_count, heads, blocks, SPAN).transpose(0, 2, 1, 3)
    scores = jnp.einsum(
        "cin,cjn->cij", query_blocks, key_blocks, preferred_element_type=jnp.float32
    )
    positions = jnp.arange(SPAN)
    causal = positions[:, None] >= positions[None, :]
    spread = jnp.where(causal, within[:, :, :, None] - within[:, :, None, :], -1e30)
    mixing = (scores[:, None] * jnp.exp(spread) * weights[0][:, :, :, None]).astype(jnp.bfloat16)
    intra = jnp.einsum("chij,cjhp->chip", mixing, value_blocks, preferred_element_type=jnp.float32)
    decayed_keys = (
        jnp.exp(block_totals[:, :, None] - within)[:, :, :, None]
        * key_blocks[:, None].astype(jnp.float32)
    ).astype(jnp.bfloat16)
    states = jnp.einsum(
        "chjn,cjhp->chnp", decayed_keys, value_blocks, preferred_element_type=jnp.float32
    )
    ends = jnp.cumsum(block_totals, axis=0)
    starts = ends - block_totals
    device_state = jnp.einsum(
        "ch,chnp->hnp", jnp.exp(ends[-1][None, :] - ends), states, precision=lax.Precision.HIGHEST
    )
    device_total = ends[-1]
    narrow_place = lax.axis_index("narrow")
    narrow_bits = lax.axis_size("narrow").bit_length() - 1
    narrow_levels, group_state, group_total, narrow_prefix = doubling(
        device_state,
        device_total,
        lambda state, total, bit: partner((state, total), "narrow", bit),
        narrow_bits,
        narrow_place,
    )
    wide_place = lax.axis_index("wide")
    wide_bits = lax.axis_size("wide").bit_length() - 1
    wide_levels, outer_state, outer_total, wide_prefix = doubling(
        group_state,
        group_total,
        lambda state, total, bit: partner((state, total), "wide", bit),
        wide_bits,
        wide_place,
    )
    inter = jnp.zeros_like(intra)
    members = np.zeros((local_bits, blocks, blocks), np.float32)
    for bit in range(local_bits):
        for target in range(blocks):
            for source in range(blocks):
                if target >> bit & 1 == 1 and source >> bit == target >> bit ^ 1:
                    members[bit, target, source] = 1.0
    later = np.arange(blocks)[:, None] > np.arange(blocks)[None, :]
    later_mask = jnp.asarray(later)[:, :, None]
    fades = jnp.where(
        later_mask, jnp.exp(jnp.where(later_mask, starts[:, None, :] - ends[None, :, :], 0.0)), 0.0
    )
    for bit in range(local_bits):
        factors = jnp.asarray(members[bit])[:, :, None] * fades
        level_here = jnp.einsum(
            "cdh,dhnp->chnp", factors, states, precision=lax.Precision.HIGHEST
        ).astype(jnp.bfloat16)
        projected = jnp.einsum(
            "cin,chnp->chip", query_blocks, level_here, preferred_element_type=jnp.float32
        )
        inter = inter + weights[1 + bit][:, :, :, None] * projected
    device_levels = jnp.concatenate(
        [narrow_levels, wide_levels * jnp.exp(narrow_prefix)[None, :, None, None]], axis=0
    )
    start_fades = jnp.exp(starts)[:, :, None, None]

    def add_level(level, running):
        chosen = lax.dynamic_index_in_dim(device_levels, level, 0, keepdims=False)
        per_block = (start_fades * chosen[None]).astype(jnp.bfloat16)
        projected = jnp.einsum(
            "cin,chnp->chip", query_blocks, per_block, preferred_element_type=jnp.float32
        )
        level_scale = lax.dynamic_index_in_dim(weights, 1 + local_bits + level, 0, keepdims=False)
        return running + level_scale[:, :, :, None] * projected

    inter = lax.fori_loop(0, device_levels.shape[0], add_level, inter)
    mixed = intra + jnp.exp(within)[:, :, :, None] * inter
    square = jnp.mean(mixed * mixed, axis=-1, keepdims=True)
    gain_rows = norm_gain.reshape(heads, head_width)
    normed = mixed * lax.rsqrt(square + 1e-05) * gain_rows[None, :, None, :]
    return (
        normed.transpose(0, 2, 1, 3).reshape(tokens_here, heads * head_width).astype(jnp.bfloat16)
    )


def solution(mesh):
    placed = (
        P(("wide", "narrow"), None),
        P(("wide", "narrow"), None),
        P(("wide", "narrow"), None),
        P(None, ("wide", "narrow")),
        P(None, None, ("wide", "narrow")),
        P(),
    )
    return jax.shard_map(
        per_device,
        mesh=mesh,
        in_specs=placed,
        out_specs=P(("wide", "narrow"), None),
        check_vma=False,
    )
```

profile of v0, /device:TPU:0, one launch (start us, length us, event | category | flops | bytes accessed | tf_op | source)
XLA Modules:
  0.0 132.5 jit_solution(8161862845234676182)
XLA Ops:
  0.0 4.2 %reduce-window.6 = f32[4,8,2,128]{3,1,2,0:T(8,128)S(1)} reduce-window(f32[4,8,2,128]{3,1,2,0:T(8,128)} %bitcast.119, f32[]{:T(128)} %constant.83.clone.1), window={size=1x1x1x128 pad=0_0x0_0x0_0x127_0}, to_apply=%region_0.0 | reduce-window | flops 1040384 | bytes 65540 | tf_op jit(solution)/shard_map/reduce-window
  5.3 3.5 %copy.48 = bf16[128,8,8,128]{3,2,1,0:T(8,128)(2,1)} copy(bf16[128,8,8,128]{3,1,2,0:T(8,128)(2,1)} %bitcast.111) | data formatting | bytes 4194304
  9.0 3.3 %multiply_reduce_fusion.1 = (f32[8,128,128]{2,1,0:T(8,128)}, f32[4,8,128,128]{3,2,1,0:T(8,128)S(1)}) fusion(f32[8,4]{0,1:T(4,128)S(1)} %get-tuple-element.192, bf16[4,256,8,128]{3,2,1,0:T(8,128)(2,1)} %bitcast.112, f32[4,256,128]{1,2,0:T(8,128)S(1)} %copy.28, f32[4,8,256]{2,1,0:T(8,128)S(1)} %subtract_exponential_fusion), kind=kOutput, calls=%fused_computation.24 | convolution fusion | flops 271450112 | bytes 5275776 | tf_op jit(solution)/shard_map/chjn,cjhp->chnp/dot_general | solution.py:60
  13.9 5.2 %fusion.29 = bf16[4,8,128,128]{3,0,2,1:T(4,128)(2,1)} fusion(f32[4,8,128,128]{3,2,1,0:T(8,128)S(1)} %get-tuple-element.205, f32[4,8]{0,1:T(8,128)S(1)} %copy.31, f32[4,8]{0,1:T(8,128)S(1)} %copy.30, f32[4,4]{1,0:T(4,128)S(1)} %copy-done.10, pred[4,4]{1,0:T(4,128)(4,1)S(1)} %copy-done.11), kind=kOutput, calls=%fused_computation.37 | convolution fusion | flops 25690624 | bytes 3146064 | tf_op jit(solution)/shard_map/cdh,dhnp->chnp/dot_general | solution.py:101
  19.1 3.0 %collective-permute-start.3 = (f32[8]{0:T(128)S(1)}, f32[8]{0:T(128)S(1)}, u32[]{:S(2)}, u32[]{:S(2)}) collective-permute-start(f32[8]{0:T(128)S(1)} %get-tuple-element.179), channel_id=1, source_target_pairs={{0,16},{8,24},{16,0},{24,8},{1,17},{9,25},{17,1},{25,9},{2,18},{10... | collective-permute-start | bytes 104 | tf_op jit(solution)/shard_map/ppermute | solution.py:13
  24.2 2.0 %select_bitcast_fusion.4 = (f32[1,8,128,128]{2,3,1,0:T(8,128)}, f32[8,128,128]{1,2,0:T(8,128)S(1)}) fusion(f32[8,128,128]{1,2,0:T(8,128)} %collective-permute-done, pred[]{:T(512)S(6)} %eq.15, f32[8,128,128]{1,2,0:T(8,128)S(1)} %copy.46, f32[8]{0:T(128)S(1)} %get-tuple-element.199, f32[8]{0:T(128)S(1)} %get-tuple-element.191), kind=kLoop, calls=%fused_computation.49 | loop fusion | flops 786432 | bytes 2097217 | tf_op jit(solution)/shard_map/stack | solution.py:30
  26.2 2.0 %collective-permute-start.2 = (f32[8,128,128]{1,2,0:T(8,128)S(1)}, f32[8,128,128]{1,2,0:T(8,128)S(1)}, u32[]{:S(2)}, u32[]{:S(2)}) collective-permute-start(f32[8,128,128]{1,2,0:T(8,128)S(1)} %get-tuple-element.181), channel_id=1, source_target_pairs={{0,16},{8,24},{16,0},{24,8},{1,17},{9,25},{17,1},{25,9},{2,18},{10... | collective-permute-start | bytes 1572872 | tf_op jit(solution)/shard_map/ppermute | solution.py:13
  29.5 4.4 %fusion.26 = bf16[4,8,128,128]{3,0,2,1:T(4,128)(2,1)S(1)} fusion(f32[4,8,128,128]{3,2,1,0:T(8,128)S(1)} %get-tuple-element.205, f32[4,4]{1,0:T(4,128)S(1)} %copy-done.9, f32[4,8]{0,1:T(8,128)S(1)} %copy.31, f32[4,8]{0,1:T(8,128)S(1)} %copy.30, pred[4,4]{1,0:T(4,128)(4,1)S(1)} %copy-done.11), kind=kOutput, calls=%fused_computation.36 | convolution fusion | flops 25690624 | bytes 3146064 | tf_op jit(solution)/shard_map/cdh,dhnp->chnp/dot_general | solution.py:101
  33.9 5.2 %collective-permute-done.2 = f32[8,128,128]{1,2,0:T(8,128)S(1)} collective-permute-done((f32[8,128,128]{1,2,0:T(8,128)S(1)}, f32[8,128,128]{1,2,0:T(8,128)S(1)}, u32[]{:S(2)}, u32[]{:S(2)}) %collective-permute-start.2) | collective-permute-done | bytes 524320 | tf_op jit(solution)/shard_map/ppermute | solution.py:13
  43.6 8.7 %collective-permute-done.5 = f32[8]{0:T(128)S(1)} collective-permute-done((f32[8]{0:T(128)S(1)}, f32[8]{0:T(128)S(1)}, u32[]{:S(2)}, u32[]{:S(2)}) %collective-permute-start.5) | collective-permute-done | bytes 64 | tf_op jit(solution)/shard_map/ppermute | solution.py:13
  53.8 2.0 %collective-permute-done.7 = f32[8]{0:T(128)S(1)} collective-permute-done((f32[8]{0:T(128)S(1)}, f32[8]{0:T(128)S(1)}, u32[]{:S(2)}, u32[]{:S(2)}) %collective-permute-start.7) | collective-permute-done | bytes 64 | tf_op jit(solution)/shard_map/ppermute | solution.py:13
  59.5 2.7 %fusion.33 = f32[4,8,128,256]{3,2,1,0:T(8,128)} fusion(bf16[4,256,128,1]{2,1,3,0:T(8,128)(2,1)S(1)} %bitcast.107, bf16[4,8,128,128]{3,0,2,1:T(4,128)(2,1)S(1)} %copy-done.1), kind=kOutput, calls=%fused_computation.39 | convolution fusion | flops 268435456 | bytes 5505024 | tf_op jit(solution)/shard_map/cin,chnp->chip/dot_general | solution.py:104
  62.2 7.2 %collective-permute-done.6 = f32[8,128,128]{1,2,0:T(8,128)S(1)} collective-permute-done((f32[8,128,128]{1,2,0:T(8,128)S(1)}, f32[8,128,128]{1,2,0:T(8,128)S(1)}, u32[]{:S(2)}, u32[]{:S(2)}) %collective-permute-start.6) | collective-permute-done | bytes 524320 | tf_op jit(solution)/shard_map/ppermute | solution.py:13
  69.6 3.1 %collective-permute-start.8 = (f32[8,128,128]{1,2,0:T(8,128)S(1)}, f32[8,128,128]{1,2,0:T(8,128)S(1)}, u32[]{:S(2)}, u32[]{:S(2)}) collective-permute-start(f32[8,128,128]{1,2,0:T(8,128)S(1)} %get-tuple-element.187), channel_id=1, source_target_pairs={{0,4},{1,5},{2,6},{3,7},{4,0},{5,1},{6,2},{7,3},{8,12},{9,13},{10,... | collective-permute-start | bytes 1572872 | tf_op jit(solution)/shard_map/ppermute | solution.py:13
  73.3 5.0 %add_bitcast_fusion = f32[4,8,256,128]{2,3,1,0:T(8,128)} fusion(f32[4,8,128,256]{3,2,1,0:T(8,128)} %fusion.33, bf16[4,256,128,1]{2,1,3,0:T(8,128)(2,1)S(1)} %bitcast.108, f32[4,8,256]{2,1,0:T(8,128)S(1)} %get-tuple-element.189, f32[4,8,256]{2,1,0:T(8,128)S(1)} %get-tuple-element.190, bf16[4,8,128,128]{3,0,2,1:T(4,128)(2,1)S(1)} %fusion.26), kind=kOutput, calls=%fused_computation.12 | convolution fusion | flops 271581184 | bytes 9764864 | tf_op jit(solution)/shard_map/cin,chnp->chip/dot_general | solution.py:104
  78.3 11.6 %collective-permute-done.8 = f32[8,128,128]{1,2,0:T(8,128)S(1)} collective-permute-done((f32[8,128,128]{1,2,0:T(8,128)S(1)}, f32[8,128,128]{1,2,0:T(8,128)S(1)}, u32[]{:S(2)}, u32[]{:S(2)}) %collective-permute-start.8) | collective-permute-done | bytes 524320 | tf_op jit(solution)/shard_map/ppermute | solution.py:13
  90.5 28.7 %while.15 = (s32[]{:T(128)}, f32[4,8,256,128]{2,3,1,0:T(8,128)}, f32[8,4,8,256]{3,2,1,0:T(8,128)}, f32[4,8,1,1]{1,0,3,2:T(4,128)S(1)}, f32[5,8,128,128]{2,3,1,0:...) while((s32[]{:T(128)}, f32[4,8,256,128]{2,3,1,0:T(8,128)}, ...), condition=%wide.region_4.5_spmd, body=%wide.region_3.4_spmd.sunk | while | flops 271581184 | bytes 10322211 | solution.py:122
  91.3 4.9 %bitcast_add_fusion.2 = f32[4,8,256,128]{2,3,1,0:T(8,128)} fusion(f32[4,8,256,128]{2,3,1,0:T(8,128)} %get-tuple-element.256, f32[4,8,256]{2,1,0:T(8,128)S(1)} %dynamic-slice_bitcast_fusion.4, f32[8,128,128]{1,2,0:T(8,128)S(1)} %dynamic-slice_bitcast_fusion.5, f32[4,8]{1,0:T(4,128)S(1)} %bitcast.118, bf16[4,256,128]{2,1,0:T(8,128)(2,1)S(1)} %get-tuple-element.270), kind=kOutput, calls=%fused_computation.clone.1 | convolution fusion | flops 271581184 | bytes 9207936 | tf_op jit(solution)/shard_map/while/body/eval_jaxpr/cin,chnp->chip/dot_general | solution.py:116
  97.0 4.9 %bitcast_add_fusion.2 = f32[4,8,256,128]{2,3,1,0:T(8,128)} fusion(f32[4,8,256,128]{2,3,1,0:T(8,128)} %get-tuple-element.256, f32[4,8,256]{2,1,0:T(8,128)S(1)} %dynamic-slice_bitcast_fusion.4, f32[8,128,128]{1,2,0:T(8,128)S(1)} %dynamic-slice_bitcast_fusion.5, f32[4,8]{1,0:T(4,128)S(1)} %bitcast.118, bf16[4,256,128]{2,1,0:T(8,128)(2,1)S(1)} %get-tuple-element.270), kind=kOutput, calls=%fused_computation.clone.1 | convolution fusion | flops 271581184 | bytes 9207936 | tf_op jit(solution)/shard_map/while/body/eval_jaxpr/cin,chnp->chip/dot_general | solution.py:116
  102.7 4.9 %bitcast_add_fusion.2 = f32[4,8,256,128]{2,3,1,0:T(8,128)} fusion(f32[4,8,256,128]{2,3,1,0:T(8,128)} %get-tuple-element.256, f32[4,8,256]{2,1,0:T(8,128)S(1)} %dynamic-slice_bitcast_fusion.4, f32[8,128,128]{1,2,0:T(8,128)S(1)} %dynamic-slice_bitcast_fusion.5, f32[4,8]{1,0:T(4,128)S(1)} %bitcast.118, bf16[4,256,128]{2,1,0:T(8,128)(2,1)S(1)} %get-tuple-element.270), kind=kOutput, calls=%fused_computation.clone.1 | convolution fusion | flops 271581184 | bytes 9207936 | tf_op jit(solution)/shard_map/while/body/eval_jaxpr/cin,chnp->chip/dot_general | solution.py:116
  108.5 4.9 %bitcast_add_fusion.2 = f32[4,8,256,128]{2,3,1,0:T(8,128)} fusion(f32[4,8,256,128]{2,3,1,0:T(8,128)} %get-tuple-element.256, f32[4,8,256]{2,1,0:T(8,128)S(1)} %dynamic-slice_bitcast_fusion.4, f32[8,128,128]{1,2,0:T(8,128)S(1)} %dynamic-slice_bitcast_fusion.5, f32[4,8]{1,0:T(4,128)S(1)} %bitcast.118, bf16[4,256,128]{2,1,0:T(8,128)(2,1)S(1)} %get-tuple-element.270), kind=kOutput, calls=%fused_computation.clone.1 | convolution fusion | flops 271581184 | bytes 9207936 | tf_op jit(solution)/shard_map/while/body/eval_jaxpr/cin,chnp->chip/dot_general | solution.py:116
  114.2 4.9 %bitcast_add_fusion.2 = f32[4,8,256,128]{2,3,1,0:T(8,128)} fusion(f32[4,8,256,128]{2,3,1,0:T(8,128)} %get-tuple-element.256, f32[4,8,256]{2,1,0:T(8,128)S(1)} %dynamic-slice_bitcast_fusion.4, f32[8,128,128]{1,2,0:T(8,128)S(1)} %dynamic-slice_bitcast_fusion.5, f32[4,8]{1,0:T(4,128)S(1)} %bitcast.118, bf16[4,256,128]{2,1,0:T(8,128)(2,1)S(1)} %get-tuple-element.270), kind=kOutput, calls=%fused_computation.clone.1 | convolution fusion | flops 271581184 | bytes 9207936 | tf_op jit(solution)/shard_map/while/body/eval_jaxpr/cin,chnp->chip/dot_general | solution.py:116
  119.1 6.3 %multiply_reduce_fusion = (f32[4,8,256]{2,1,0:T(8,128)S(1)}, f32[4,8,256,128]{2,3,1,0:T(8,128)S(1)}) fusion(f32[4,8,256,128]{2,3,1,0:T(8,128)} %get-tuple-element.159, f32[4,8,256]{2,1,0:T(8,128)S(1)} %get-tuple-element.172, bf16[4,256,8,128]{3,2,1,0:T(8,128)(2,1)} %bitcast.113, f32[4,8,256]{2,1,0:T(8,128)S(1)} %copy-done.7, ...), kind=kOutput, calls=%fused_computation.10 | convolution fusion | flops 551542784 | bytes 11730944 | tf_op jit(solution)/shard_map/chij,cjhp->chip/dot_general | solution.py:55
  127.4 3.1 %copy.36 = bf16[4,256,8,128]{3,2,1,0:T(8,128)(2,1)S(1)} copy(bf16[4,256,8,128]{1,3,2,0:T(8,128)(2,1)} %fusion.11) | data formatting | bytes 4194304 | tf_op jit(solution)/shard_map/convert_element_type | solution.py:128
  (78 shorter events, 24.9 us)
Async XLA Ops:
  0.0 8.8 %copy-start.4 = (bf16[1024,128]{1,0:T(8,128)(2,1)S(1)}, bf16[1024,128]{1,0:T(8,128)(2,1)}, u32[]{:S(2)}) copy-start(bf16[1024,128]{1,0:T(8,128)(2,1)} %param.12) | copy-start | bytes 786436
  4.7 14.4 %collective-permute-start.1 = (f32[8]{0:T(128)S(1)}, f32[8]{0:T(128)S(1)}, u32[]{:S(2)}, u32[]{:S(2)}) collective-permute-start(f32[8]{0:T(128)S(1)} %slice_bitcast_fusion.3), channel_id=1, source_target_pairs={{0,8},{8,0},{16,24},{24,16},{1,9},{9,1},{17,25},{25,17},{2,10},{10... | collective-permute-start | bytes 104 | tf_op jit(solution)/shard_map/ppermute | solution.py:13
  9.0 4.9 %copy-start.10 = (f32[4,4]{1,0:T(4,128)S(1)}, f32[4,4]{1,0:T(4,128)}, u32[]{:S(2)}) copy-start(f32[4,4]{1,0:T(4,128)} %constant.93.clone) | copy-start | bytes 196
  9.0 4.8 %copy-start.11 = (pred[4,4]{1,0:T(4,128)(4,1)S(1)}, pred[4,4]{1,0:T(4,128)(4,1)}, u32[]{:S(2)}) copy-start(pred[4,4]{1,0:T(4,128)(4,1)} %constant.92.clone) | copy-start | bytes 52
  13.6 10.6 %collective-permute-start = (f32[8,128,128]{1,2,0:T(8,128)S(1)}, f32[8,128,128]{1,2,0:T(8,128)}, u32[]{:S(2)}, u32[]{:S(2)}) collective-permute-start(f32[8,128,128]{1,2,0:T(8,128)S(1)} %copy.46), channel_id=1, source_target_pairs={{0,8},{8,0},{16,24},{24,16},{1,9},{9,1},{17,25},{25,17},{2,10},{10... | collective-permute-start | bytes 1572872 | tf_op jit(solution)/shard_map/ppermute | solution.py:13
  13.8 14.3 %copy-start = (bf16[1024,128]{1,0:T(8,128)(2,1)S(1)}, bf16[1024,128]{1,0:T(8,128)(2,1)}, u32[]{:S(2)}) copy-start(bf16[1024,128]{1,0:T(8,128)(2,1)} %param.11) | copy-start | bytes 786436
  19.0 10.5 %copy-start.9 = (f32[4,4]{1,0:T(4,128)S(1)}, f32[4,4]{1,0:T(4,128)}, u32[]{:S(2)}) copy-start(f32[4,4]{1,0:T(4,128)} %constant.94.clone) | copy-start | bytes 196
  19.1 4.6 %collective-permute-start.3 = (f32[8]{0:T(128)S(1)}, f32[8]{0:T(128)S(1)}, u32[]{:S(2)}, u32[]{:S(2)}) collective-permute-start(f32[8]{0:T(128)S(1)} %get-tuple-element.179), channel_id=1, source_target_pairs={{0,16},{8,24},{16,0},{24,8},{1,17},{9,25},{17,1},{25,9},{2,18},{10... | collective-permute-start | bytes 104 | tf_op jit(solution)/shard_map/ppermute | solution.py:13
  26.2 13.0 %collective-permute-start.2 = (f32[8,128,128]{1,2,0:T(8,128)S(1)}, f32[8,128,128]{1,2,0:T(8,128)S(1)}, u32[]{:S(2)}, u32[]{:S(2)}) collective-permute-start(f32[8,128,128]{1,2,0:T(8,128)S(1)} %get-tuple-element.181), channel_id=1, source_target_pairs={{0,16},{8,24},{16,0},{24,8},{1,17},{9,25},{17,1},{25,9},{2,18},{10... | collective-permute-start | bytes 1572872 | tf_op jit(solution)/shard_map/ppermute | solution.py:13
  33.9 25.5 %copy-start.1 = (bf16[4,8,128,128]{3,0,2,1:T(4,128)(2,1)S(1)}, bf16[4,8,128,128]{3,0,2,1:T(4,128)(2,1)}, u32[]{:S(2)}) copy-start(bf16[4,8,128,128]{3,0,2,1:T(4,128)(2,1)} %fusion.29) | copy-start | bytes 3145732
  40.2 15.7 %collective-permute-start.4 = (f32[8,128,128]{1,2,0:T(8,128)S(1)}, f32[8,128,128]{1,2,0:T(8,128)S(1)}, u32[]{:S(2)}, u32[]{:S(2)}) collective-permute-start(f32[8,128,128]{1,2,0:T(8,128)S(1)} %get-tuple-element.183), channel_id=1, source_target_pairs={{0,1},{1,0},{2,3},{3,2},{4,5},{5,4},{6,7},{7,6},{8,9},{9,8},{10,11... | collective-permute-start | bytes 1572872 | tf_op jit(solution)/shard_map/ppermute | solution.py:13
  43.3 9.0 %collective-permute-start.5 = (f32[8]{0:T(128)S(1)}, f32[8]{0:T(128)S(1)}, u32[]{:S(2)}, u32[]{:S(2)}) collective-permute-start(f32[8]{0:T(128)S(1)} %get-tuple-element.197), channel_id=1, source_target_pairs={{0,1},{1,0},{2,3},{3,2},{4,5},{5,4},{6,7},{7,6},{8,9},{9,8},{10,11... | collective-permute-start | bytes 104 | tf_op jit(solution)/shard_map/ppermute | solution.py:13
  52.3 3.5 %collective-permute-start.7 = (f32[8]{0:T(128)S(1)}, f32[8]{0:T(128)S(1)}, u32[]{:S(2)}, u32[]{:S(2)}) collective-permute-start(f32[8]{0:T(128)S(1)} %get-tuple-element.175), channel_id=1, source_target_pairs={{0,2},{1,3},{2,0},{3,1},{4,6},{5,7},{6,4},{7,5},{8,10},{9,11},{10,... | collective-permute-start | bytes 104 | tf_op jit(solution)/shard_map/ppermute | solution.py:13
  55.9 0.8 copy-start.5
  57.9 11.5 %collective-permute-start.6 = (f32[8,128,128]{1,2,0:T(8,128)S(1)}, f32[8,128,128]{1,2,0:T(8,128)S(1)}, u32[]{:S(2)}, u32[]{:S(2)}) collective-permute-start(f32[8,128,128]{1,2,0:T(8,128)S(1)} %get-tuple-element.185), channel_id=1, source_target_pairs={{0,2},{1,3},{2,0},{3,1},{4,6},{5,7},{6,4},{7,5},{8,10},{9,11},{10,... | collective-permute-start | bytes 1572872 | tf_op jit(solution)/shard_map/ppermute | solution.py:13
  69.6 20.3 %collective-permute-start.8 = (f32[8,128,128]{1,2,0:T(8,128)S(1)}, f32[8,128,128]{1,2,0:T(8,128)S(1)}, u32[]{:S(2)}, u32[]{:S(2)}) collective-permute-start(f32[8,128,128]{1,2,0:T(8,128)S(1)} %get-tuple-element.187), channel_id=1, source_target_pairs={{0,4},{1,5},{2,6},{3,7},{4,0},{5,1},{6,2},{7,3},{8,12},{9,13},{10,... | collective-permute-start | bytes 1572872 | tf_op jit(solution)/shard_map/ppermute | solution.py:13
  73.3 16.7 %copy-start.12 = (f32[8]{0:T(128)S(1)}, f32[8]{0:T(128)}, u32[]{:S(2)}) copy-start(f32[8]{0:T(128)} %get-tuple-element.195) | copy-start | bytes 100
  78.3 11.9 %copy-start.2 = (f32[1,8,128,128]{2,3,1,0:T(8,128)S(1)}, f32[1,8,128,128]{2,3,1,0:T(8,128)}, u32[]{:S(2)}) copy-start(f32[1,8,128,128]{2,3,1,0:T(8,128)} %get-tuple-element.182) | copy-start | bytes 1572868
  78.3 11.9 %copy-start.3 = (f32[1,8,128,128]{2,3,1,0:T(8,128)S(1)}, f32[1,8,128,128]{2,3,1,0:T(8,128)}, u32[]{:S(2)}) copy-start(f32[1,8,128,128]{2,3,1,0:T(8,128)} %get-tuple-element.180) | copy-start | bytes 1572868
  90.4 28.7 %copy-start.6 = (pred[256,256]{1,0:T(8,128)(4,1)S(1)}, pred[256,256]{1,0:T(8,128)(4,1)}, u32[]{:S(2)}) copy-start(pred[256,256]{1,0:T(8,128)(4,1)} %iota_compare_fusion) | copy-start | bytes 196612
  90.4 28.7 %copy-start.7 = (f32[4,8,256]{2,1,0:T(8,128)S(1)}, f32[4,8,256]{2,1,0:T(8,128)}, u32[]{:S(2)}) copy-start(f32[4,8,256]{2,1,0:T(8,128)} %get-tuple-element.188) | copy-start | bytes 98308
  119.1 6.4 %copy-start.8 = (f32[1024]{0:T(1024)S(1)}, f32[1024]{0:T(1024)}, u32[]{:S(2)}) copy-start(f32[1024]{0:T(1024)} %param.16) | copy-start | bytes 12292
where the time goes:
time: 134 us; the launch traced here: 132 us
  matrix products  52.9 us (39%)
  waiting for transfers between devices  36.2 us (27%)
  local copies, waits for them, and re-layouts  16.8 us (13%)
  starting transfers between devices  13.9 us (10%)
  other arithmetic  12.4 us (9%)
    ppermute x9, waiting for transfers between devices, partner(): return lax.ppermute(value, axis, pairs)  36.2 us
    dot_general x5, matrix products, add_level(): jnp.einsum('cin,chnp->chip', query_blocks, per_block, preferred_element_t...  24.7 us
    ppermute x9, starting transfers between devices, partner(): return lax.ppermute(value, axis, pairs)  13.9 us
    dot_general x2, matrix products, per_device(): jnp.einsum('cdh,dhnp->chnp', factors, states, precision=lax.Precision.HIG...  9.58 us
    dot_general x2, matrix products, per_device(): jnp.einsum('cin,chnp->chip', query_blocks, level_here, preferred_element_...  7.7 us
    unnamed x28, local copies, waits for them, and re-layouts  6.35 us
    dot_general x1, matrix products, per_device(): jnp.einsum('chij,cjhp->chip', mixing, value_blocks, preferred_element_typ...  6.35 us
    another operation x5, other arithmetic, doubling(): levels_found = jnp.stack(found)  4.54 us
  transfers between devices with their start and end apart: 9, of which 6 were waited for; matrix products, arithmetic and copies ran while one was open for 22% of the time, Pallas kernels for 0%

commit v1 on v0

v1 whole, which is shorter than its diff:
```python
import functools

import jax
import jax.numpy as jnp
from jax import lax
from jax.experimental import pallas as pl
from jax.experimental.pallas import tpu as pltpu
from jax.sharding import PartitionSpec as P

SPAN = 256
EPS = 1e-05
AXES = ("narrow", "wide")
NT = (((1,), (1,)), ((), ()))
VMEM = 56 * 1024 * 1024


def place():
    return lax.axis_index("wide") * lax.axis_size("narrow") + lax.axis_index("narrow")


def bit_of(value, bit):
    return jnp.bitwise_and(jnp.right_shift(value, bit), 1)


def spread_lanes(column, width):
    return jnp.broadcast_to(column, (column.shape[0], width))


def running_sum(values):
    width = values.shape[1]
    lanes = lax.broadcasted_iota(jnp.int32, values.shape, 1)
    shift = 1
    while shift < width:
        values = values + jnp.where(lanes >= shift, pltpu.roll(values, shift, 1), 0.0)
        shift *= 2
    return values


def state_kernel(k_ref, v_ref, decay_ref, message_ref, local_ref, sums_ref, totals_ref, held, run):
    span = pl.program_id(0)
    heads = decay_ref.shape[0]
    key_width = k_ref.shape[1]
    head_width = v_ref.shape[1] // heads
    local_bits = held.shape[0]

    @pl.when(span == 0)
    def _():
        held[...] = jnp.zeros_like(held)
        run[...] = jnp.zeros_like(run)

    within = running_sum(decay_ref[...])
    total = spread_lanes(within[:, SPAN - 1 :], 128)
    start = run[...]
    sums_ref[0] = within
    sums_ref[1] = within + spread_lanes(start[:, :1], SPAN)
    totals_ref[0] = total
    run[...] = start + total
    fade = jnp.exp(spread_lanes(within[:, SPAN - 1 :], SPAN) - within)
    whole = jnp.exp(total)
    keys_across = k_ref[...].astype(jnp.float32).T
    for head in range(heads):
        columns = slice(head * head_width, (head + 1) * head_width)
        faded = (keys_across * fade[head : head + 1]).astype(jnp.bfloat16)
        state = jnp.dot(faded, v_ref[:, columns], preferred_element_type=jnp.float32)
        offset = 0
        for bit in range(local_bits):
            groups = pl.num_programs(0) >> (bit + 1)
            if bit > 0:
                kept = jnp.where(
                    jnp.bitwise_and(span, 2**bit - 1) == 0, 0.0, held[bit - 1, head]
                )
                merged = kept * whole[head : head + 1] + state
                held[bit - 1, head] = merged
            else:
                merged = state

            @pl.when(
                jnp.logical_and(
                    bit_of(span, bit) == 0,
                    jnp.bitwise_and(span + 1, 2**bit - 1) == 0,
                )
            )
            def _():
                local_ref[offset + jnp.right_shift(span, bit + 1), :, columns] = merged.astype(
                    jnp.bfloat16
                )

            offset = offset + groups
        held[local_bits - 1, head] = held[local_bits - 1, head] * whole[head : head + 1] + state

    @pl.when(span == pl.num_programs(0) - 1)
    def _():
        for head in range(heads):
            message_ref[head * head_width : (head + 1) * head_width] = held[local_bits - 1, head].T
        message_ref[heads * head_width :] = run[...]


def make_states(keys, values, log_decay):
    tokens, key_width = keys.shape
    heads = log_decay.shape[0]
    width = values.shape[1]
    head_width = width // heads
    spans = tokens // SPAN
    local_bits = spans.bit_length() - 1
    return pl.pallas_call(
        state_kernel,
        grid=(spans,),
        in_specs=[
            pl.BlockSpec((SPAN, key_width), lambda c: (c, 0)),
            pl.BlockSpec((SPAN, width), lambda c: (c, 0)),
            pl.BlockSpec((heads, SPAN), lambda c: (0, c)),
        ],
        out_specs=[
            pl.BlockSpec((width + heads, key_width), lambda c: (0, 0)),
            pl.BlockSpec((spans - 1, key_width, width), lambda c: (0, 0, 0)),
            pl.BlockSpec((2, heads, SPAN), lambda c: (0, 0, c)),
            pl.BlockSpec((1, heads, 128), lambda c: (c, 0, 0)),
        ],
        out_shape=[
            jax.ShapeDtypeStruct((width + heads, key_width), jnp.float32),
            jax.ShapeDtypeStruct((spans - 1, key_width, width), jnp.bfloat16),
            jax.ShapeDtypeStruct((2, heads, tokens), jnp.float32),
            jax.ShapeDtypeStruct((spans, heads, 128), jnp.float32),
        ],
        scratch_shapes=[
            pltpu.VMEM((local_bits, heads, key_width, head_width), jnp.float32),
            pltpu.VMEM((heads, 128), jnp.float32),
        ],
        compiler_params=pltpu.CompilerParams(vmem_limit_bytes=VMEM),
        name="states",
    )(keys, values, log_decay)


def local_kernel(
    q_ref, k_ref, v_ref, sums_ref, totals_ref, weight_ref, local_ref, mixed_ref
):
    span = pl.program_id(0)
    heads = weight_ref.shape[1]
    head_width = v_ref.shape[1] // heads
    local_bits = weight_ref.shape[0] - 1
    half = SPAN // 2
    queries = q_ref[...]
    scores = lax.dot_general(k_ref[...], queries, NT, preferred_element_type=jnp.float32)
    within = sums_ref[0]
    within_down = within.T
    values_across = v_ref[...].T
    source = lax.broadcasted_iota(jnp.int32, (half, half), 0)
    target = lax.broadcasted_iota(jnp.int32, (half, half), 1)
    causal = source <= target
    empty = jnp.zeros((half, half), jnp.bfloat16)

    def mix(head, low, high, masked):
        rows = slice(low * half, (low + 1) * half)
        columns = slice(high * half, (high + 1) * half)
        gap = within[head : head + 1, columns] - within_down[rows, head : head + 1]
        if masked:
            gap = jnp.where(causal, gap, -1e30)
        mixing = scores[rows, columns] * jnp.exp(gap) * weight_ref[0, head : head + 1, columns]
        return mixing.astype(jnp.bfloat16)

    for head in range(heads):
        rows = slice(head * head_width, (head + 1) * head_width)
        mixing = jnp.concatenate(
            [
                jnp.concatenate([mix(head, 0, 0, True), mix(head, 0, 1, False)], axis=1),
                jnp.concatenate([empty, mix(head, 1, 1, True)], axis=1),
            ],
            axis=0,
        )
        mixed_ref[rows] = jnp.dot(
            values_across[rows], mixing, preferred_element_type=jnp.float32
        )
    offset = 0
    for bit in range(local_bits):
        since = jnp.zeros((heads, 128), jnp.float32)
        for back in range(1, 2**bit):
            inside = jnp.bitwise_and(span, 2**bit - 1) >= back
            since = since + jnp.where(inside, totals_ref[jnp.maximum(span - back, 0)], 0.0)

        @pl.when(bit_of(span, bit) == 1)
        def _():
            level = local_ref[offset + jnp.right_shift(span, bit + 1)].T
            found = lax.dot_general(level, queries, NT, preferred_element_type=jnp.float32)
            scale = jnp.exp(within + spread_lanes(since[:, :1], SPAN)) * weight_ref[1 + bit]
            for head in range(heads):
                rows = slice(head * head_width, (head + 1) * head_width)
                mixed_ref[rows] += found[rows] * scale[head : head + 1]

        offset = offset + (pl.num_programs(0) >> (bit + 1))


def mix_local(queries, keys, values, sums, totals, level_weight, local):
    tokens, key_width = keys.shape
    heads = level_weight.shape[1]
    width = values.shape[1]
    spans = tokens // SPAN
    local_bits = spans.bit_length() - 1
    return pl.pallas_call(
        local_kernel,
        grid=(spans,),
        in_specs=[
            pl.BlockSpec((SPAN, key_width), lambda c: (c, 0)),
            pl.BlockSpec((SPAN, key_width), lambda c: (c, 0)),
            pl.BlockSpec((SPAN, width), lambda c: (c, 0)),
            pl.BlockSpec((2, heads, SPAN), lambda c: (0, 0, c)),
            pl.BlockSpec((spans, heads, 128), lambda c: (0, 0, 0)),
            pl.BlockSpec((1 + local_bits, heads, SPAN), lambda c: (0, 0, c)),
            pl.BlockSpec((spans - 1, key_width, width), lambda c: (0, 0, 0)),
        ],
        out_specs=pl.BlockSpec((width, SPAN), lambda c: (0, c)),
        out_shape=jax.ShapeDtypeStruct((width, tokens), jnp.float32),
        compiler_params=pltpu.CompilerParams(vmem_limit_bytes=VMEM),
        name="local",
    )(queries, keys, values, sums, totals, level_weight, local)


def merge_kernel(bit, mine_ref, other_ref, prefix_ref, merged_ref, next_ref):
    here = place()
    upper = bit_of(here, bit) == 1
    core = bit_of(here, 0)
    heads = prefix_ref.shape[0]
    held = heads // 2
    rows = merged_ref.shape[0] - heads
    per = rows // held
    width = mine_ref.shape[0] - heads
    first = core * held if width > rows else 0
    mine_total = mine_ref[width:]
    other_total = other_ref[width:]
    fade = jnp.exp(jnp.where(upper, mine_total, other_total))
    for slot in range(held):
        own = jnp.where(
            core == 1, fade[held + slot : held + slot + 1], fade[slot : slot + 1]
        )
        source = pl.ds((first + slot) * per, per)
        mine = mine_ref[source]
        other = other_ref[source]
        merged_ref[slot * per : (slot + 1) * per] = jnp.where(
            upper, other * own + mine, mine * own + other
        )
    merged_ref[rows:] = mine_total + other_total
    next_ref[...] = prefix_ref[...] + jnp.where(upper, other_total, 0.0)


def merge(bit, mine, other, prefix, rows):
    heads = prefix.shape[0]
    return pl.pallas_call(
        functools.partial(merge_kernel, bit),
        out_shape=[
            jax.ShapeDtypeStruct((rows + heads, mine.shape[1]), jnp.float32),
            jax.ShapeDtypeStruct(prefix.shape, jnp.float32),
        ],
        compiler_params=pltpu.CompilerParams(vmem_limit_bytes=VMEM),
        name=f"merge{bit}",
    )(mine, other, prefix)


def finish_kernel(level_count, parts_of, *refs):
    mixed_ref, q_ref, sums_ref, weight_ref, gain_ref = refs[:5]
    prefix_refs = refs[5 : 5 + level_count]
    part_refs = refs[5 + level_count : -2]
    out_ref, levels = refs[-2:]
    heads = weight_ref.shape[1]
    head_width = mixed_ref.shape[0] // heads
    first_level = weight_ref.shape[0] - level_count
    here = place()

    @pl.when(pl.program_id(0) == 0)
    def _():
        at = 0
        for level in range(level_count):
            rows = parts_of[level][0]
            if len(parts_of[level]) == 1:
                levels[level] = part_refs[at][:rows].astype(jnp.bfloat16)
            else:
                mine = bit_of(here, 0) * rows
                levels[level, pl.ds(mine, rows)] = part_refs[at][:rows].astype(jnp.bfloat16)
                levels[level, pl.ds(rows - mine, rows)] = part_refs[at + 1][:rows].astype(
                    jnp.bfloat16
                )
            at += len(parts_of[level])

    queries = q_ref[...]
    since = sums_ref[1]
    gain_down = gain_ref[...].T
    scales = []
    for level in range(level_count):
        active = jnp.where(bit_of(here, level) == 1, 1.0, 0.0)
        reach = jnp.exp(since + spread_lanes(prefix_refs[level][:, :1], SPAN))
        scales.append(reach * weight_ref[first_level + level] * active)
    for head in range(heads):
        rows = slice(head * head_width, (head + 1) * head_width)
        mixed = mixed_ref[rows]
        for level in range(level_count):
            found = lax.dot_general(
                levels[level, rows], queries, NT, preferred_element_type=jnp.float32
            )
            mixed = mixed + found * scales[level][head : head + 1]
        square = jnp.mean(mixed * mixed, axis=0, keepdims=True)
        normed = mixed * lax.rsqrt(square + EPS) * gain_down[:, head : head + 1]
        out_ref[:, rows] = normed.astype(jnp.bfloat16).T


def finish(mixed, queries, sums, level_weight, gain, prefixes, parts):
    width, tokens = mixed.shape
    key_width = queries.shape[1]
    levels, heads, _ = level_weight.shape
    spans = tokens // SPAN
    level_count = len(parts)
    parts_of = []
    for level in parts:
        parts_of.append([width // len(level)] * len(level))
    flat = [part for level in parts for part in level]

    def whole(array):
        return pl.BlockSpec(array.shape, lambda c: (0,) * array.ndim)

    return pl.pallas_call(
        functools.partial(finish_kernel, level_count, parts_of),
        grid=(spans,),
        in_specs=[
            pl.BlockSpec((width, SPAN), lambda c: (0, c)),
            pl.BlockSpec((SPAN, key_width), lambda c: (c, 0)),
            pl.BlockSpec((2, heads, SPAN), lambda c: (0, 0, c)),
            pl.BlockSpec((levels, heads, SPAN), lambda c: (0, 0, c)),
            whole(gain),
            *[whole(array) for array in prefixes],
            *[whole(array) for array in flat],
        ],
        out_specs=pl.BlockSpec((SPAN, width), lambda c: (c, 0)),
        out_shape=jax.ShapeDtypeStruct((tokens, width), jnp.bfloat16),
        scratch_shapes=[pltpu.VMEM((level_count, width, key_width), jnp.bfloat16)],
        compiler_params=pltpu.CompilerParams(vmem_limit_bytes=VMEM),
        name="finish",
    )(mixed, queries, sums, level_weight, gain, *prefixes, *flat)


def trade(value, mask, senders=lambda source: True):
    wide, narrow = lax.axis_size("wide"), lax.axis_size("narrow")

    def ranked(index):
        return index % narrow * wide + index // narrow

    pairs = [
        (ranked(source), ranked(source ^ mask))
        for source in range(wide * narrow)
        if senders(source)
    ]
    return lax.ppermute(value, AXES, pairs)


def swap(value, bit):
    return trade(value, 2**bit)


def per_device(queries, keys, values, log_decay, level_weight, norm_gain):
    heads = log_decay.shape[0]
    width = values.shape[1]
    count = lax.axis_size("wide") * lax.axis_size("narrow")
    message, local, sums, totals = make_states(keys, values, log_decay)
    prefix = jnp.zeros((heads, 128), jnp.float32)
    prefixes, parts = [], []
    rows = width // 2
    for bit in range(count.bit_length() - 1):
        other = swap(message, bit)
        prefixes.append(prefix)
        if bit == 0:
            parts.append([other])
        else:
            parts.append([other, swap(other, 0)])
        if bit < count.bit_length() - 2:
            message, prefix = merge(bit, message, other, prefix, rows)
        elif bit > 0:
            pass
    mixed = mix_local(queries, keys, values, sums, totals, level_weight, local)
    gain = norm_gain.reshape(heads, width // heads)
    return finish(mixed, queries, sums, level_weight, gain, prefixes, parts)


def solution(mesh):
    placed = (
        P(("wide", "narrow"), None),
        P(("wide", "narrow"), None),
        P(("wide", "narrow"), None),
        P(None, ("wide", "narrow")),
        P(None, None, ("wide", "narrow")),
        P(),
    )
    return jax.shard_map(
        per_device,
        mesh=mesh,
        in_specs=placed,
        out_specs=P(("wide", "narrow"), None),
        check_vma=False,
    )
```

time: 134 us -> 77.8 us (0.58)
  matrix products: 52.9 us -> 0 us
  Pallas kernels: 0 us -> 33.1 us
  local copies, waits for them, and re-layouts: 16.8 us -> 3.88 us
  other arithmetic: 12.4 us -> 0 us
  waiting for transfers between devices: 36.2 us -> 31.1 us
  starting transfers between devices: 13.9 us -> 9.28 us
    dot_general x12 -> x0, matrix products: 52.9 us -> none  [the longest x5 24.7 us: add_level(): jnp.einsum('cin,chnp->chip', query_blocks, per_block, preferred_element_t...]
    pallas_call x0 -> x7, Pallas kernels: none -> 33.1 us  [the longest x1 10.5 us: make_states(): pl.pallas_call(state_kernel, grid=(spans,), in_specs=[pl.BlockSpec((SPAN,...]
    another operation x8 -> x0, other arithmetic: 8.76 us -> none  [the longest x5 4.54 us: doubling(): levels_found = jnp.stack(found)]
    mul x11 -> x0, local copies, waits for them, and re-layouts: 5.38 us -> none  [the longest x5 3.81 us: add_level(): return running + level_scale[:, :, :, None] * projected]
    ppermute x9, waiting for transfers between devices: 36.2 us -> 31.1 us  [trade(): return lax.ppermute(value, AXES, pairs)]
    ppermute x9, starting transfers between devices: 13.9 us -> 9.28 us  [trade(): return lax.ppermute(value, AXES, pairs)]
    convert_element_type x2 -> x0, local copies, waits for them, and re-layouts: 3.26 us -> none  [the longest x1 3.12 us: per_device(): normed.transpose(0, 2, 1, 3).reshape(tokens_here, heads * head_width)]
    unnamed x28 -> x18, local copies, waits for them, and re-layouts: 6.35 us -> 3.24 us
  transfers between devices with their start and end apart: 9 -> 9, of which waited for: 6 -> 5; matrix products, arithmetic and copies ran while one was open for 22% -> 0% of each run, Pallas kernels for 0% -> 10%
where the time goes in v1:
time: 77.8 us; the launch traced here: 77.4 us
  Pallas kernels  33.1 us (43%)
  waiting for transfers between devices  31.1 us (40%)
  starting transfers between devices  9.28 us (12%)
  local copies, waits for them, and re-layouts  3.88 us (5%)
    ppermute x9, waiting for transfers between devices, trade(): return lax.ppermute(value, AXES, pairs)  31.1 us
    pallas_call x1, Pallas kernels, make_states(): pl.pallas_call(state_kernel, grid=(spans,), in_specs=[pl.BlockSpec((SPAN,...  10.5 us
    ppermute x9, starting transfers between devices, trade(): return lax.ppermute(value, AXES, pairs)  9.28 us
    pallas_call x1, Pallas kernels, finish(): pl.pallas_call(functools.partial(finish_kernel, level_count, parts_of), g...  7.73 us
    pallas_call x1, Pallas kernels, mix_local(): pl.pallas_call(local_kernel, grid=(spans,), in_specs=[pl.BlockSpec((SPAN,...  7.5 us
    pallas_call x4, Pallas kernels, merge(): pl.pallas_call(functools.partial(merge_kernel, bit), out_shape=[jax.Shape...  7.36 us
    unnamed x18, local copies, waits for them, and re-layouts  3.24 us
  transfers between devices with their start and end apart: 9, of which 5 were waited for; matrix products, arithmetic and copies ran while one was open for 0% of the time, Pallas kernels for 10%

profile of v1, /device:TPU:0, one launch (start us, length us, event | category | flops | bytes accessed | tf_op | source)
XLA Modules:
  0.0 77.4 jit_solution(14902086920950888222)
XLA Ops:
  0.0 10.5 %states.1 = (f32[1032,128]{1,0:T(8,128)}, bf16[3,128,1024]{2,1,0:T(8,128)(2,1)}, f32[2,8,1024]{2,1,0:T(8,128)}, f32[4,8,128]{2,1,0:T(8,128)}) custom-call(bf16[1024,128]{1,0:T(8,128)(2,1)} %k_ref.3, bf16[1024,1024]{1,0:T(8,128)(2,1)} %v_ref.3, f32[8,1024]{1,0:T(8,128)} %decay_ref.1), custom_call_target="tpu_custom_call" | custom-call | tf_op jit(solution)/shard_map/states/pallas_call | solution.py:105
  10.5 0.5 collective-permute-start
  11.1 1.8 %collective-permute-done.other_ref.refs_10_ = f32[1032,128]{1,0:T(8,128)S(1)} collective-permute-done((f32[1032,128]{1,0:T(8,128)}, f32[1032,128]{1,0:T(8,128)S(1)}, u32[]{:S(2)}, u32[]{:S(2)}) %collective-permute-start) | collective-permute-done | bytes 528416 | tf_op jit(solution)/shard_map/ppermute | solution.py:348
  12.8 0.6 broadcast_in_dim.3.prefix_ref.refs_5_
  13.5 0.2 copy-done
  13.6 2.0 %merge0.1 = (f32[520,128]{1,0:T(8,128)}, f32[8,128]{1,0:T(8,128)}) custom-call(f32[1032,128]{1,0:T(8,128)} %get-tuple-element.20.mine_ref, f32[1032,128]{1,0:T(8,128)} %copy-done, f32[8,128]{1,0:T(8,128)} %broadcast_in_dim.3.prefix_ref.refs_5_), custom_call_target="tpu_custom_call" | custom-call | tf_op jit(solution)/shard_map/merge0/pallas_call | solution.py:246
  15.6 2.9 %collective-permute-start.1 = (f32[520,128]{1,0:T(8,128)}, f32[520,128]{1,0:T(8,128)S(1)}, u32[]{:S(2)}, u32[]{:S(2)}) collective-permute-start(f32[520,128]{1,0:T(8,128)} %get-tuple-element.22.mine_ref), channel_id=1, source_target_pairs={{0,16},{8,24},{16,0},{24,8},{1,17},{9,25},{17,1},{25,9},{2,18},{10... | collective-permute-start | bytes 798728 | tf_op jit(solution)/shard_map/ppermute | solution.py:348
  18.5 6.9 %collective-permute-done.1.other_ref.refs_11_ = f32[520,128]{1,0:T(8,128)S(1)} collective-permute-done((f32[520,128]{1,0:T(8,128)}, f32[520,128]{1,0:T(8,128)S(1)}, u32[]{:S(2)}, u32[]{:S(2)}) %collective-permute-start.1) | collective-permute-done | bytes 266272 | tf_op jit(solution)/shard_map/ppermute | solution.py:348
  25.4 0.7 copy-done.1
  26.1 1.8 %merge1.1 = (f32[520,128]{1,0:T(8,128)}, f32[8,128]{1,0:T(8,128)}) custom-call(f32[520,128]{1,0:T(8,128)} %get-tuple-element.22.mine_ref, f32[520,128]{1,0:T(8,128)} %copy-done.1, f32[8,128]{1,0:T(8,128)} %get-tuple-element.21.prefix_ref.refs_6_), custom_call_target="tpu_custom_call" | custom-call | tf_op jit(solution)/shard_map/merge1/pallas_call | solution.py:246
  27.9 1.7 %collective-permute-start.2 = (f32[520,128]{1,0:T(8,128)}, f32[520,128]{1,0:T(8,128)S(1)}, u32[]{:S(2)}, u32[]{:S(2)}) collective-permute-start(f32[520,128]{1,0:T(8,128)} %get-tuple-element.24.mine_ref), channel_id=1, source_target_pairs={{0,1},{8,9},{16,17},{24,25},{1,0},{9,8},{17,16},{25,24},{2,3},{10,... | collective-permute-start | bytes 798728 | tf_op jit(solution)/shard_map/ppermute | solution.py:348
  29.6 6.4 %collective-permute-done.2.other_ref.refs_13_ = f32[520,128]{1,0:T(8,128)S(1)} collective-permute-done((f32[520,128]{1,0:T(8,128)}, f32[520,128]{1,0:T(8,128)S(1)}, u32[]{:S(2)}, u32[]{:S(2)}) %collective-permute-start.2) | collective-permute-done | bytes 266272 | tf_op jit(solution)/shard_map/ppermute | solution.py:348
  36.0 0.7 copy-done.2
  36.7 1.8 %merge2.1 = (f32[520,128]{1,0:T(8,128)}, f32[8,128]{1,0:T(8,128)}) custom-call(f32[520,128]{1,0:T(8,128)} %get-tuple-element.24.mine_ref, f32[520,128]{1,0:T(8,128)} %copy-done.2, f32[8,128]{1,0:T(8,128)} %get-tuple-element.23.prefix_ref.refs_7_), custom_call_target="tpu_custom_call" | custom-call | tf_op jit(solution)/shard_map/merge2/pallas_call | solution.py:246
  38.5 1.5 %collective-permute-start.3 = (f32[520,128]{1,0:T(8,128)}, f32[520,128]{1,0:T(8,128)S(1)}, u32[]{:S(2)}, u32[]{:S(2)}) collective-permute-start(f32[520,128]{1,0:T(8,128)} %get-tuple-element.26.mine_ref), channel_id=1, source_target_pairs={{0,2},{8,10},{16,18},{24,26},{1,3},{9,11},{17,19},{25,27},{2,0},{1... | collective-permute-start | bytes 798728 | tf_op jit(solution)/shard_map/ppermute | solution.py:348
  40.0 5.8 %collective-permute-done.3.other_ref.refs_15_ = f32[520,128]{1,0:T(8,128)S(1)} collective-permute-done((f32[520,128]{1,0:T(8,128)}, f32[520,128]{1,0:T(8,128)S(1)}, u32[]{:S(2)}, u32[]{:S(2)}) %collective-permute-start.3) | collective-permute-done | bytes 266272 | tf_op jit(solution)/shard_map/ppermute | solution.py:348
  45.8 0.7 copy-done.3
  46.5 1.8 %merge3.1 = (f32[520,128]{1,0:T(8,128)}, f32[8,128]{1,0:T(8,128)}) custom-call(f32[520,128]{1,0:T(8,128)} %get-tuple-element.26.mine_ref, f32[520,128]{1,0:T(8,128)} %copy-done.3, f32[8,128]{1,0:T(8,128)} %get-tuple-element.25.prefix_ref.refs_8_), custom_call_target="tpu_custom_call" | custom-call | tf_op jit(solution)/shard_map/merge3/pallas_call | solution.py:246
  48.3 2.2 %collective-permute-start.7 = (f32[520,128]{1,0:T(8,128)}, f32[520,128]{1,0:T(8,128)S(1)}, u32[]{:S(2)}, u32[]{:S(2)}) collective-permute-start(f32[520,128]{1,0:T(8,128)} %get-tuple-element.28), channel_id=1, source_target_pairs={{0,4},{8,12},{16,20},{24,28},{1,5},{9,13},{17,21},{25,29},{2,6},{1... | collective-permute-start | bytes 798728 | tf_op jit(solution)/shard_map/ppermute | solution.py:348
  50.4 0.5 collective-permute-start.5
  51.0 10.2 %collective-permute-done.7.refs_17_ = f32[520,128]{1,0:T(8,128)S(1)} collective-permute-done((f32[520,128]{1,0:T(8,128)}, f32[520,128]{1,0:T(8,128)S(1)}, u32[]{:S(2)}, u32[]{:S(2)}) %collective-permute-start.7) | collective-permute-done | bytes 266272 | tf_op jit(solution)/shard_map/ppermute | solution.py:348
  61.2 7.5 %local.1.refs_0_ = f32[1024,1024]{1,0:T(8,128)} custom-call(bf16[1024,128]{1,0:T(8,128)(2,1)} %refs_1_.1, bf16[1024,128]{1,0:T(8,128)(2,1)} %k_ref.3, bf16[1024,1024]{1,0:T(8,128)(2,1)} %v_ref.3, f32[2,8,1024]{2,1,0:T(8,128)} %get-tuple-element.17.sums_ref.refs_2_, f32[4,8,128]{2,1,0:T(8,128)} %get-tuple-element.18.totals_ref, f32[8,8,1024]{2,1,0:T(8,128)} %refs_3_.1, ...), custom_call_target="tpu_custom_call" | custom-call | tf_op jit(solution)/shard_map/local/pallas_call | solution.py:198
  68.8 0.6 copy-done.5
  69.7 7.7 %finish.1 = bf16[1024,1024]{1,0:T(8,128)(2,1)} custom-call(f32[1024,1024]{1,0:T(8,128)} %local.1.refs_0_, bf16[1024,128]{1,0:T(8,128)(2,1)} %refs_1_.1, f32[2,8,1024]{2,1,0:T(8,128)} %get-tuple-element.17.sums_ref.refs_2_, f32[8,8,1024]{2,1,0:T(8,128)} %refs_3_.1, f32[8,128]{1,0:T(8,128)} %bitcast.1, f32[8,128]{1,0:T(8,128)} %broadcast_in_dim.3.prefix_ref.refs_5_, ...), custom_call_target="tpu_custom_call" | custom-call | tf_op jit(solution)/shard_map/finish/pallas_call | solution.py:317
  (20 shorter events, 0.3 us)
Async XLA Ops:
  10.5 2.3 %collective-permute-start = (f32[1032,128]{1,0:T(8,128)}, f32[1032,128]{1,0:T(8,128)S(1)}, u32[]{:S(2)}, u32[]{:S(2)}) collective-permute-start(f32[1032,128]{1,0:T(8,128)} %get-tuple-element.20.mine_ref), channel_id=1, source_target_pairs={{0,8},{8,0},{16,24},{24,16},{1,9},{9,1},{17,25},{25,17},{2,10},{10... | collective-permute-start | bytes 1585160 | tf_op jit(solution)/shard_map/ppermute | solution.py:348
  12.8 0.8 %copy-start = (f32[1032,128]{1,0:T(8,128)}, f32[1032,128]{1,0:T(8,128)S(1)}, u32[]{:S(2)}) copy-start(f32[1032,128]{1,0:T(8,128)S(1)} %collective-permute-done.other_ref.refs_10_) | copy-start | bytes 1585156
  15.6 9.8 %collective-permute-start.1 = (f32[520,128]{1,0:T(8,128)}, f32[520,128]{1,0:T(8,128)S(1)}, u32[]{:S(2)}, u32[]{:S(2)}) collective-permute-start(f32[520,128]{1,0:T(8,128)} %get-tuple-element.22.mine_ref), channel_id=1, source_target_pairs={{0,16},{8,24},{16,0},{24,8},{1,17},{9,25},{17,1},{25,9},{2,18},{10... | collective-permute-start | bytes 798728 | tf_op jit(solution)/shard_map/ppermute | solution.py:348
  25.4 0.7 copy-start.1
  27.9 8.1 %collective-permute-start.2 = (f32[520,128]{1,0:T(8,128)}, f32[520,128]{1,0:T(8,128)S(1)}, u32[]{:S(2)}, u32[]{:S(2)}) collective-permute-start(f32[520,128]{1,0:T(8,128)} %get-tuple-element.24.mine_ref), channel_id=1, source_target_pairs={{0,1},{8,9},{16,17},{24,25},{1,0},{9,8},{17,16},{25,24},{2,3},{10,... | collective-permute-start | bytes 798728 | tf_op jit(solution)/shard_map/ppermute | solution.py:348
  36.0 0.7 copy-start.2
  38.5 7.2 %collective-permute-start.3 = (f32[520,128]{1,0:T(8,128)}, f32[520,128]{1,0:T(8,128)S(1)}, u32[]{:S(2)}, u32[]{:S(2)}) collective-permute-start(f32[520,128]{1,0:T(8,128)} %get-tuple-element.26.mine_ref), channel_id=1, source_target_pairs={{0,2},{8,10},{16,18},{24,26},{1,3},{9,11},{17,19},{25,27},{2,0},{1... | collective-permute-start | bytes 798728 | tf_op jit(solution)/shard_map/ppermute | solution.py:348
  45.8 0.7 copy-start.3
  48.3 12.9 %collective-permute-start.7 = (f32[520,128]{1,0:T(8,128)}, f32[520,128]{1,0:T(8,128)S(1)}, u32[]{:S(2)}, u32[]{:S(2)}) collective-permute-start(f32[520,128]{1,0:T(8,128)} %get-tuple-element.28), channel_id=1, source_target_pairs={{0,4},{8,12},{16,20},{24,28},{1,5},{9,13},{17,21},{25,29},{2,6},{1... | collective-permute-start | bytes 798728 | tf_op jit(solution)/shard_map/ppermute | solution.py:348
  50.4 18.3 %collective-permute-start.4 = (f32[520,128]{1,0:T(8,128)}, f32[520,128]{1,0:T(8,128)S(1)}, u32[]{:S(2)}, u32[]{:S(2)}) collective-permute-start(f32[520,128]{1,0:T(8,128)} %copy-done.1), channel_id=1, source_target_pairs={{0,8},{8,0},{16,24},{24,16},{1,9},{9,1},{17,25},{25,17},{2,10},{10... | collective-permute-start | bytes 798728 | tf_op jit(solution)/shard_map/ppermute | solution.py:348
  50.4 18.3 %collective-permute-start.5 = (f32[520,128]{1,0:T(8,128)}, f32[520,128]{1,0:T(8,128)S(1)}, u32[]{:S(2)}, u32[]{:S(2)}) collective-permute-start(f32[520,128]{1,0:T(8,128)} %copy-done.2), channel_id=1, source_target_pairs={{0,8},{8,0},{16,24},{24,16},{1,9},{9,1},{17,25},{25,17},{2,10},{10... | collective-permute-start | bytes 798728 | tf_op jit(solution)/shard_map/ppermute | solution.py:348
  50.9 17.8 %collective-permute-start.6 = (f32[520,128]{1,0:T(8,128)}, f32[520,128]{1,0:T(8,128)S(1)}, u32[]{:S(2)}, u32[]{:S(2)}) collective-permute-start(f32[520,128]{1,0:T(8,128)} %copy-done.3), channel_id=1, source_target_pairs={{0,8},{8,0},{16,24},{24,16},{1,9},{9,1},{17,25},{25,17},{2,10},{10... | collective-permute-start | bytes 798728 | tf_op jit(solution)/shard_map/ppermute | solution.py:348
  61.2 7.5 %copy-start.4 = (f32[520,128]{1,0:T(8,128)}, f32[520,128]{1,0:T(8,128)S(1)}, u32[]{:S(2)}) copy-start(f32[520,128]{1,0:T(8,128)S(1)} %collective-permute-done.7.refs_17_) | copy-start | bytes 798724
  61.2 7.6 %collective-permute-start.8 = (f32[520,128]{1,0:T(8,128)S(1)}, f32[520,128]{1,0:T(8,128)S(1)}, u32[]{:S(2)}, u32[]{:S(2)}) collective-permute-start(f32[520,128]{1,0:T(8,128)S(1)} %collective-permute-done.7.refs_17_), channel_id=1, source_target_pairs={{0,8},{8,0},{16,24},{24,16},{1,9},{9,1},{17,25},{25,17},{2,10},{10... | collective-permute-start | bytes 798728 | tf_op jit(solution)/shard_map/ppermute | solution.py:348
  68.7 0.7 copy-start.5
  68.7 0.8 %copy-start.6 = (f32[520,128]{1,0:T(8,128)}, f32[520,128]{1,0:T(8,128)S(1)}, u32[]{:S(2)}) copy-start(f32[520,128]{1,0:T(8,128)S(1)} %collective-permute-done.5.refs_14_) | copy-start | bytes 798724
  68.8 0.8 %copy-start.7 = (f32[520,128]{1,0:T(8,128)}, f32[520,128]{1,0:T(8,128)S(1)}, u32[]{:S(2)}) copy-start(f32[520,128]{1,0:T(8,128)S(1)} %collective-permute-done.6.refs_16_) | copy-start | bytes 798724
  68.8 0.9 %copy-start.8 = (f32[520,128]{1,0:T(8,128)}, f32[520,128]{1,0:T(8,128)S(1)}, u32[]{:S(2)}) copy-start(f32[520,128]{1,0:T(8,128)S(1)} %collective-permute-done.8.refs_18_) | copy-start | bytes 798724

commit v2 on v1

v2 whole, which is shorter than its diff:
```python
import functools

import jax
import jax.numpy as jnp
from jax import lax
from jax.experimental import pallas as pl
from jax.experimental.pallas import tpu as pltpu
from jax.sharding import PartitionSpec as P

SPAN = 256
EPS = 1e-05
AXES = ("narrow", "wide")
NT = (((1,), (1,)), ((), ()))
VMEM = 56 * 1024 * 1024
PARAMS = pltpu.CompilerParams(vmem_limit_bytes=VMEM)


def place():
    return lax.axis_index("wide") * lax.axis_size("narrow") + lax.axis_index("narrow")


def bit_of(value, bit):
    return jnp.bitwise_and(jnp.right_shift(value, bit), 1)


def spread_lanes(column, width):
    return jnp.broadcast_to(column, (column.shape[0], width))


def whole(array):
    return pl.BlockSpec(array.shape, lambda *_: (0,) * len(array.shape))


ANYWHERE = pl.BlockSpec(memory_space=pl.ANY)


def running_sums(rows):
    high = rows.astype(jnp.bfloat16)
    rest = rows - high.astype(jnp.float32)
    middle = rest.astype(jnp.bfloat16)
    low = (rest - middle.astype(jnp.float32)).astype(jnp.bfloat16)
    width = rows.shape[1]
    source = lax.broadcasted_iota(jnp.int32, (width, width), 0)
    target = lax.broadcasted_iota(jnp.int32, (width, width), 1)
    upto = jnp.where(source <= target, 1.0, 0.0).astype(jnp.bfloat16)
    sums = jnp.dot(
        jnp.concatenate([high, middle, low], axis=0), upto, preferred_element_type=jnp.float32
    )
    count = rows.shape[0]
    return sums[:count] + (sums[count : 2 * count] + sums[2 * count :])


def state_kernel(
    k_ref, decay_ref, v_hbm, keep_ref, send_ref, local_ref, sums_ref, totals_ref, v_ref, held, arrived
):
    heads, tokens = decay_ref.shape
    head_width = v_ref.shape[1] // heads
    spans = tokens // SPAN
    rows_of = [slice(span * SPAN, (span + 1) * SPAN) for span in range(spans)]
    copies = [
        pltpu.make_async_copy(v_hbm.at[rows], v_ref.at[rows], arrived.at[span])
        for span, rows in enumerate(rows_of)
    ]
    for copy in copies:
        copy.start()
    within = running_sums(jnp.concatenate([decay_ref[:, rows] for rows in rows_of], axis=0))
    run = jnp.zeros((heads, 128), jnp.float32)
    fades, wholes = [], []
    for span, rows in enumerate(rows_of):
        here = within[span * heads : (span + 1) * heads]
        last = here[:, SPAN - 1 :]
        total = spread_lanes(last, 128)
        sums_ref[0, :, rows] = here
        sums_ref[1, :, rows] = here + spread_lanes(run[:, :1], SPAN)
        totals_ref[span] = total
        run = run + total
        fades.append(jnp.exp(spread_lanes(last, SPAN) - here))
        wholes.append(jnp.exp(total))
    across = [k_ref[rows].astype(jnp.float32).T for rows in rows_of]
    for copy in copies:
        copy.wait()
    for head in range(heads):
        columns = slice(head * head_width, (head + 1) * head_width)
        states = []
        for span, rows in enumerate(rows_of):
            faded = (across[span] * fades[span][head : head + 1]).astype(jnp.bfloat16)
            states.append(
                jnp.dot(faded, v_ref[rows, columns], preferred_element_type=jnp.float32)
            )
        at = 0
        size = 1
        while size < spans:
            for first in range(0, spans, 2 * size):
                group = states[first]
                for span in range(first + 1, first + size):
                    group = group * wholes[span][head : head + 1] + states[span]
                local_ref[at, :, columns] = group.astype(jnp.bfloat16)
                at += 1
            size *= 2
        group = states[0]
        for span in range(1, spans):
            group = group * wholes[span][head : head + 1] + states[span]
        held[columns] = group.T
    half = held.shape[0] // 2
    core = bit_of(place(), 0)
    keep_ref[:half] = held[pl.ds(core * half, half)]
    send_ref[:half] = held[pl.ds((1 - core) * half, half)]
    keep_ref[half:] = run
    send_ref[half:] = run


def make_states(keys, values, log_decay):
    tokens, key_width = keys.shape
    heads = log_decay.shape[0]
    width = values.shape[1]
    spans = tokens // SPAN
    message = jax.ShapeDtypeStruct((width // 2 + heads, key_width), jnp.float32)
    return pl.pallas_call(
        state_kernel,
        in_specs=[whole(keys), whole(log_decay), ANYWHERE],
        out_shape=[
            message,
            message,
            jax.ShapeDtypeStruct((spans - 1, key_width, width), jnp.bfloat16),
            jax.ShapeDtypeStruct((2, heads, tokens), jnp.float32),
            jax.ShapeDtypeStruct((spans, heads, 128), jnp.float32),
        ],
        scratch_shapes=[
            pltpu.VMEM((tokens, width), jnp.bfloat16),
            pltpu.VMEM((width, key_width), jnp.float32),
            pltpu.SemaphoreType.DMA((spans,)),
        ],
        compiler_params=PARAMS,
        name="states",
    )(keys, log_decay, values)


def local_kernel(
    first_span, spans, q_ref, k_ref, v_ref, sums_ref, totals_ref, weight_ref, local_ref, *refs
):
    mixed_ref, done_ref = refs[-2:]
    span = pl.program_id(0) + first_span
    heads = weight_ref.shape[1]
    head_width = v_ref.shape[1] // heads
    local_bits = weight_ref.shape[0] - 1
    half = SPAN // 2
    done_ref[...] = jnp.zeros_like(done_ref)
    queries = q_ref[...]
    scores = lax.dot_general(k_ref[...], queries, NT, preferred_element_type=jnp.float32)
    within = sums_ref[0]
    within_down = within.T
    values_across = v_ref[...].T
    source = lax.broadcasted_iota(jnp.int32, (half, half), 0)
    target = lax.broadcasted_iota(jnp.int32, (half, half), 1)
    causal = source <= target
    empty = jnp.zeros((half, half), jnp.bfloat16)

    def mix(head, low, high, masked):
        rows = slice(low * half, (low + 1) * half)
        columns = slice(high * half, (high + 1) * half)
        gap = within[head : head + 1, columns] - within_down[rows, head : head + 1]
        if masked:
            gap = jnp.where(causal, gap, -1e30)
        mixing = scores[rows, columns] * jnp.exp(gap) * weight_ref[0, head : head + 1, columns]
        return mixing.astype(jnp.bfloat16)

    for head in range(heads):
        rows = slice(head * head_width, (head + 1) * head_width)
        mixing = jnp.concatenate(
            [
                jnp.concatenate([mix(head, 0, 0, True), mix(head, 0, 1, False)], axis=1),
                jnp.concatenate([empty, mix(head, 1, 1, True)], axis=1),
            ],
            axis=0,
        )
        mixed_ref[rows] = jnp.dot(
            values_across[rows], mixing, preferred_element_type=jnp.float32
        )
    offset = 0
    for bit in range(local_bits):
        since = jnp.zeros((heads, 128), jnp.float32)
        for back in range(1, 2**bit):
            inside = jnp.bitwise_and(span, 2**bit - 1) >= back
            since = since + jnp.where(inside, totals_ref[jnp.maximum(span - back, 0)], 0.0)

        @pl.when(bit_of(span, bit) == 1)
        def _():
            level = local_ref[offset + jnp.right_shift(span, bit + 1)].T
            found = lax.dot_general(level, queries, NT, preferred_element_type=jnp.float32)
            scale = jnp.exp(within + spread_lanes(since[:, :1], SPAN)) * weight_ref[1 + bit]
            for head in range(heads):
                rows = slice(head * head_width, (head + 1) * head_width)
                mixed_ref[rows] += found[rows] * scale[head : head + 1]

        offset = offset + (spans >> (bit + 1))


def mix_local(first, count, queries, keys, values, sums, totals, level_weight, local, mixed):
    tokens, key_width = keys.shape
    heads = level_weight.shape[1]
    width = values.shape[1]
    spans = tokens // SPAN
    local_bits = spans.bit_length() - 1
    rest = [] if mixed is None else [mixed]
    return pl.pallas_call(
        functools.partial(local_kernel, first, spans),
        grid=(count,),
        in_specs=[
            pl.BlockSpec((SPAN, key_width), lambda c: (c + first, 0)),
            pl.BlockSpec((SPAN, key_width), lambda c: (c + first, 0)),
            pl.BlockSpec((SPAN, width), lambda c: (c + first, 0)),
            pl.BlockSpec((2, heads, SPAN), lambda c: (0, 0, c + first)),
            whole(totals),
            pl.BlockSpec((1 + local_bits, heads, SPAN), lambda c: (0, 0, c + first)),
            whole(local),
            *[ANYWHERE for _ in rest],
        ],
        out_specs=[
            pl.BlockSpec((width, SPAN), lambda c: (0, c + first)),
            pl.BlockSpec((8, 128), lambda c: (0, 0)),
        ],
        out_shape=[
            jax.ShapeDtypeStruct((width, tokens), jnp.float32),
            jax.ShapeDtypeStruct((8, 128), jnp.float32),
        ],
        input_output_aliases={7: 0} if rest else {},
        compiler_params=PARAMS,
        name=f"local{first}",
    )(queries, keys, values, sums, totals, level_weight, local, *rest)


def join(upper, mine, mine_total, other, other_total):
    fade = jnp.exp(jnp.where(upper, mine_total, other_total))
    return jnp.where(upper, other * fade + mine, mine * fade + other)


def chip_kernel(mine_ref, other_ref, *refs):
    chip_ref, prefix_ref, *message_refs = refs
    heads = prefix_ref.shape[0]
    half = chip_ref.shape[0]
    held = heads // 2
    per = half // held
    here = place()
    core = bit_of(here, 0)
    chip = jnp.bitwise_and(jnp.right_shift(here, 1), held - 1)
    upper = core == 1
    mine_total = mine_ref[half:]
    other_total = other_ref[half:]
    total = mine_total + other_total
    prefix_ref[...] = jnp.where(upper, other_total, 0.0)
    for slot in range(held):
        rows = slice(slot * per, (slot + 1) * per)
        mine_row = jnp.where(upper, mine_total[held + slot][None], mine_total[slot][None])
        other_row = jnp.where(upper, other_total[held + slot][None], other_total[slot][None])
        chip_ref[rows] = join(upper, mine_ref[rows], mine_row, other_ref[rows], other_row)
    for mask, message_ref in enumerate(message_refs):
        slot = jnp.bitwise_xor(chip, mask)
        message_ref[:per] = chip_ref[pl.ds(slot * per, per)]
        message_ref[per:] = total


def make_chip(mine, other, heads):
    half = mine.shape[0] - heads
    held = heads // 2
    message = jax.ShapeDtypeStruct((half // held + heads, mine.shape[1]), jnp.float32)
    return pl.pallas_call(
        chip_kernel,
        out_shape=[
            jax.ShapeDtypeStruct((half, mine.shape[1]), jnp.float32),
            jax.ShapeDtypeStruct((heads, mine.shape[1]), jnp.float32),
            *[message] * held,
        ],
        compiler_params=PARAMS,
        name="chip",
    )(mine, other)


def own_row(ref, per, heads):
    here = place()
    held = heads // 2
    chip = jnp.bitwise_and(jnp.right_shift(here, 1), held - 1)
    return ref[pl.ds(per + bit_of(here, 0) * held + chip, 1)]


def group_kernel(bits, *refs):
    part_refs = refs[: 2**bits]
    prefix_ref = refs[2**bits]
    group_ref = refs[-2 - (bits - 1)]
    lower_refs = refs[-1 - (bits - 1) : -1]
    prefixes_ref = refs[-1]
    heads = prefix_ref.shape[0]
    per = group_ref.shape[0] - heads
    here = place()
    states = [ref[:per] for ref in part_refs]
    totals = [ref[per:] for ref in part_refs]
    rows = [own_row(ref, per, heads) for ref in part_refs]
    prefix = prefix_ref[...]
    for bit in range(bits):
        upper = bit_of(here, bit + 1) == 1
        half = len(states) // 2
        if bit > 0:
            lower_refs[bit - 1][...] = jnp.where(upper, states[1], states[0])
        prefix = prefix + jnp.where(upper, totals[1], 0.0)
        prefixes_ref[bit] = prefix
        states = [
            join(upper, states[2 * at], rows[2 * at], states[2 * at + 1], rows[2 * at + 1])
            for at in range(half)
        ]
        totals = [totals[2 * at] + totals[2 * at + 1] for at in range(half)]
        rows = [rows[2 * at] + rows[2 * at + 1] for at in range(half)]
    group_ref[:per] = states[0]
    group_ref[per:] = totals[0]


def make_group(parts, prefix, token):
    heads, lanes = prefix.shape
    bits = len(parts).bit_length() - 1
    per = parts[0].shape[0] - heads
    state = jax.ShapeDtypeStruct((per, lanes), jnp.float32)
    return pl.pallas_call(
        functools.partial(group_kernel, bits),
        in_specs=[*[whole(part) for part in parts], whole(prefix), ANYWHERE],
        out_shape=[
            jax.ShapeDtypeStruct(parts[0].shape, jnp.float32),
            *[state] * (bits - 1),
            jax.ShapeDtypeStruct((bits, heads, lanes), jnp.float32),
        ],
        compiler_params=PARAMS,
        name="group",
    )(*parts, prefix, token)


def merge_kernel(bit, mine_ref, other_ref, prefix_ref, token_ref, merged_ref, next_ref):
    upper = bit_of(place(), bit) == 1
    heads = next_ref.shape[1]
    per = merged_ref.shape[0] - heads
    mine_row = own_row(mine_ref, per, heads)
    other_row = own_row(other_ref, per, heads)
    merged_ref[:per] = join(upper, mine_ref[:per], mine_row, other_ref[:per], other_row)
    other_total = other_ref[per:]
    merged_ref[per:] = mine_ref[per:] + other_total
    last = prefix_ref.shape[0] - 1
    next_ref[0] = prefix_ref[last] + jnp.where(upper, other_total, 0.0)


def merge(bit, mine, other, prefixes, token):
    _, heads, lanes = prefixes.shape
    return pl.pallas_call(
        functools.partial(merge_kernel, bit),
        in_specs=[whole(mine), whole(other), whole(prefixes), ANYWHERE],
        out_shape=[
            jax.ShapeDtypeStruct(mine.shape, jnp.float32),
            jax.ShapeDtypeStruct((1, heads, lanes), jnp.float32),
        ],
        compiler_params=PARAMS,
        name=f"merge{bit}",
    )(mine, other, prefixes, token)


def reach_kernel(plan, last, first_level, *refs):
    mixed_ref, q_ref, sums_ref, weight_ref, gain_ref = refs[:5]
    prefix_refs = refs[5 : 5 + len(plan)]
    part_refs = refs[5 + len(plan) : -2]
    out_ref, levels = refs[-2:]
    heads = weight_ref.shape[1]
    head_width = mixed_ref.shape[0] // heads
    held = heads // 2
    here = place()
    core = bit_of(here, 0)
    chip = jnp.bitwise_and(jnp.right_shift(here, 1), held - 1)

    @pl.when(pl.program_id(0) == 0)
    def _():
        at = 0
        for slot, (_, _, count) in enumerate(plan):
            for part in range(count):
                ref = part_refs[at]
                at += 1
                if count == 2:
                    side = core if part == 0 else 1 - core
                    first = side * held * head_width
                    rows = held * head_width
                else:
                    side = core if part < held else 1 - core
                    mask = part % held
                    first = (side * held + jnp.bitwise_xor(chip, mask)) * head_width
                    rows = head_width
                levels[slot, pl.ds(pl.multiple_of(first, 128), rows)] = ref[:rows].astype(
                    jnp.bfloat16
                )

    queries = q_ref[...]
    since = sums_ref[1]
    scales = []
    for slot, (bit, at, _) in enumerate(plan):
        active = jnp.where(bit_of(here, bit) == 1, 1.0, 0.0)
        reach = jnp.exp(since + spread_lanes(prefix_refs[slot][at][:, :1], SPAN))
        scales.append(reach * weight_ref[first_level + bit] * active)
    if last:
        gain_down = gain_ref[...].T
    for head in range(heads):
        rows = slice(head * head_width, (head + 1) * head_width)
        mixed = mixed_ref[rows]
        for slot in range(len(plan)):
            found = lax.dot_general(
                levels[slot, rows], queries, NT, preferred_element_type=jnp.float32
            )
            mixed = mixed + found * scales[slot][head : head + 1]
        if last:
            square = jnp.mean(mixed * mixed, axis=0, keepdims=True)
            normed = mixed * lax.rsqrt(square + EPS) * gain_down[:, head : head + 1]
            out_ref[:, rows] = normed.astype(jnp.bfloat16).T
        else:
            out_ref[rows] = mixed


def add_levels(mixed, queries, sums, level_weight, gain, levels, first_level, last):
    width, tokens = mixed.shape
    key_width = queries.shape[1]
    level_count, heads, _ = level_weight.shape
    spans = tokens // SPAN
    plan = [(bit, at, len(parts)) for bit, _, at, parts in levels]
    prefixes = [prefix for _, prefix, _, _ in levels]
    flat = [part for level in levels for part in level[3]]
    across = pl.BlockSpec((width, SPAN), lambda c: (0, c))
    return pl.pallas_call(
        functools.partial(reach_kernel, plan, last, first_level),
        grid=(spans,),
        in_specs=[
            across,
            pl.BlockSpec((SPAN, key_width), lambda c: (c, 0)),
            pl.BlockSpec((2, heads, SPAN), lambda c: (0, 0, c)),
            pl.BlockSpec((level_count, heads, SPAN), lambda c: (0, 0, c)),
            whole(gain),
            *[whole(array) for array in prefixes],
            *[whole(array) for array in flat],
        ],
        out_specs=pl.BlockSpec((SPAN, width), lambda c: (c, 0)) if last else across,
        out_shape=(
            jax.ShapeDtypeStruct((tokens, width), jnp.bfloat16)
            if last
            else jax.ShapeDtypeStruct(mixed.shape, jnp.float32)
        ),
        input_output_aliases={} if last else {0: 0},
        scratch_shapes=[pltpu.VMEM((len(plan), width, key_width), jnp.bfloat16)],
        compiler_params=PARAMS,
        name="finish" if last else "reach",
    )(mixed, queries, sums, level_weight, gain, *prefixes, *flat)


def trade(value, mask, senders=lambda source: True):
    wide, narrow = lax.axis_size("wide"), lax.axis_size("narrow")

    def ranked(index):
        return index % narrow * wide + index // narrow

    pairs = [
        (ranked(source), ranked(source ^ mask))
        for source in range(wide * narrow)
        if senders(source)
    ]
    return lax.ppermute(value, AXES, pairs)


def gather(own, bit, heads):
    parts = [own]
    for mask in range(1, heads // 2):
        parts.append(trade(own, 2 * mask, lambda source: ((source ^ 2 * mask) >> bit) & 1 == 1))
    needed = lambda source: (source >> bit) & 1 == 1
    return parts + [trade(part, 1, needed) for part in parts]


def per_device(queries, keys, values, log_decay, level_weight, norm_gain):
    heads = log_decay.shape[0]
    tokens, width = values.shape
    spans = tokens // SPAN
    bits = (lax.axis_size("wide") * lax.axis_size("narrow")).bit_length() - 1
    group_bits = heads.bit_length() - 1
    first_level = level_weight.shape[0] - bits
    keep, send, local, sums, totals = make_states(keys, values, log_decay)
    shared = (queries, keys, values, sums, totals, level_weight, local)
    other = trade(send, 1)
    chip, prefix, *messages = make_chip(keep, other, heads)
    levels = []
    zero = jnp.zeros((1, heads, 128), jnp.float32)
    levels.append((0, zero, 0, [other, trade(keep, 1, lambda source: source & 1 == 0)]))
    parts = [messages[0]]
    for mask in range(1, heads // 2):
        parts.append(trade(messages[mask], 2 * mask))
    mixed, token = mix_local(0, spans // 2, *shared, None)
    group, lower, prefixes = make_group(parts, prefix, token)
    near = trade(chip, 2, lambda source: (source >> 1) & 1 == 0)
    upper = lambda source: (source >> 1) & 1 == 1
    levels.append((1, prefix[None], 0, [near, trade(near, 1, upper)]))
    levels.append((2, prefixes, 0, gather(lower, 2, heads)))
    at = spans // 2
    for bit in range(group_bits, bits):
        other = trade(group, 2**bit)
        levels.append((bit, prefixes, prefixes.shape[0] - 1, gather(other, bit, heads)))
        if at < spans:
            mixed, token = mix_local(at, 1, *shared, mixed)
            at += 1
        if bit + 1 < bits:
            group, prefixes = merge(bit, group, other, prefixes, token)
    if at < spans:
        mixed, token = mix_local(at, spans - at, *shared, mixed)
    gain = norm_gain.reshape(heads, width // heads)
    rest = (queries, sums, level_weight, gain)
    mixed = add_levels(mixed, *rest, levels[:-1], first_level, False)
    return add_levels(mixed, *rest, levels[-1:], first_level, True)


def solution(mesh):
    placed = (
        P(("wide", "narrow"), None),
        P(("wide", "narrow"), None),
        P(("wide", "narrow"), None),
        P(None, ("wide", "narrow")),
        P(None, None, ("wide", "narrow")),
        P(),
    )
    return jax.shard_map(
        per_device,
        mesh=mesh,
        in_specs=placed,
        out_specs=P(("wide", "narrow"), None),
        check_vma=False,
    )
```

time: 77.8 us -> 104 us (1.34)
  the two profiles are of different devices: /device:TPU:0 before, /device:TPU:31 now
where the time goes in v2:
time: 104 us; the launch traced here: 102 us
  starting transfers between devices  61.1 us (59%)
  Pallas kernels  34.5 us (33%)
  waiting for transfers between devices  3.3 us (3%)
  local copies, waits for them, and re-layouts  2.77 us (3%)
    ppermute x30, starting transfers between devices, trade(): return lax.ppermute(value, AXES, pairs)  61.1 us
    pallas_call x2, Pallas kernels, add_levels(): pl.pallas_call(functools.partial(reach_kernel, plan, last, first_level),...  13.4 us
    pallas_call x3, Pallas kernels, mix_local(): pl.pallas_call(functools.partial(local_kernel, first, spans), grid=(count...  11.4 us
    pallas_call x1, Pallas kernels, make_states(): pl.pallas_call(state_kernel, in_specs=[whole(keys), whole(log_decay), ANY...  4.53 us
    ppermute x30, waiting for transfers between devices, trade(): return lax.ppermute(value, AXES, pairs)  3.3 us
    unnamed x60, local copies, waits for them, and re-layouts  2.12 us
  transfers between devices with their start and end apart: 30, of which 3 were waited for; matrix products, arithmetic and copies ran while one was open for 1% of the time, Pallas kernels for 23%

profile of v2, /device:TPU:31, one launch (start us, length us, event | category | flops | bytes accessed | tf_op | source)
XLA Modules:
  0.0 102.4 jit_solution(6219927560027207017)
XLA Ops:
  0.0 4.5 %states.1 = (f32[520,128]{1,0:T(8,128)}, f32[520,128]{1,0:T(8,128)}, bf16[3,128,1024]{2,1,0:T(8,128)(2,1)}, f32[2,8,1024]{2,1,0:T(8,128)}, f32[4,8,128]{2,1,0:T(8,128)}) custom-call(bf16[1024,128]{1,0:T(8,128)(2,1)} %k_ref.7, f32[8,1024]{1,0:T(8,128)} %decay_ref.1, bf16[1024,1024]{1,0:T(8,128)(2,1)} %v_ref.5), custom_call_target="tpu_custom_call" | custom-call | tf_op jit(solution)/shard_map/states/pallas_call | solution.py:118
  10.6 2.2 %collective-permute-start.1 = (f32[136,128]{1,0:T(8,128)}, f32[136,128]{1,0:T(8,128)S(1)}, u32[]{:S(2)}, u32[]{:S(2)}) collective-permute-start(f32[136,128]{1,0:T(8,128)} %get-tuple-element.36), channel_id=1, source_target_pairs={{0,16},{8,24},{16,0},{24,8},{1,17},{9,25},{17,1},{25,9},{2,18},{10... | collective-permute-start | bytes 208904 | tf_op jit(solution)/shard_map/ppermute | solution.py:462
  14.0 4.4 %local0.1 = (f32[1024,1024]{1,0:T(8,128)}, f32[8,128]{1,0:T(8,128)}) custom-call(bf16[1024,128]{1,0:T(8,128)(2,1)} %refs_1_.3, bf16[1024,128]{1,0:T(8,128)(2,1)} %k_ref.7, bf16[1024,1024]{1,0:T(8,128)(2,1)} %v_ref.5, f32[2,8,1024]{2,1,0:T(8,128)} %get-tuple-element.26.sums_ref.refs_2_, f32[4,8,128]{2,1,0:T(8,128)} %get-tuple-element.27.totals_ref, ...), custom_call_target="tpu_custom_call" | custom-call | tf_op jit(solution)/shard_map/local0/pallas_call | solution.py:205
  18.4 2.7 %collective-permute-done.1.refs_1_ = f32[136,128]{1,0:T(8,128)S(1)} collective-permute-done((f32[136,128]{1,0:T(8,128)}, f32[136,128]{1,0:T(8,128)S(1)}, u32[]{:S(2)}, u32[]{:S(2)}) %collective-permute-start.1) | collective-permute-done | bytes 69664 | tf_op jit(solution)/shard_map/ppermute | solution.py:462
  28.7 5.0 %collective-permute-start.10 = (f32[128,128]{1,0:T(8,128)}, f32[128,128]{1,0:T(8,128)S(1)}, u32[]{:S(2)}, u32[]{:S(2)}) collective-permute-start(f32[128,128]{1,0:T(8,128)} %get-tuple-element.42.refs_13_), channel_id=1, source_target_pairs={{1,9},{9,1},{17,25},{25,17},{3,11},{11,3},{19,27},{27,19},{5,13},{... | collective-permute-start | bytes 196616 | tf_op jit(solution)/shard_map/ppermute | solution.py:462
  33.7 2.6 %collective-permute-start.11 = (f32[128,128]{1,0:T(8,128)S(1)}, f32[128,128]{1,0:T(8,128)S(1)}, u32[]{:S(2)}, u32[]{:S(2)}) collective-permute-start(f32[128,128]{1,0:T(8,128)S(1)} %collective-permute-done.7.refs_14_), channel_id=1, source_target_pairs={{1,9},{9,1},{17,25},{25,17},{3,11},{11,3},{19,27},{27,19},{5,13},{... | collective-permute-start | bytes 196616 | tf_op jit(solution)/shard_map/ppermute | solution.py:462
  36.3 2.1 %collective-permute-start.12 = (f32[128,128]{1,0:T(8,128)S(1)}, f32[128,128]{1,0:T(8,128)S(1)}, u32[]{:S(2)}, u32[]{:S(2)}) collective-permute-start(f32[128,128]{1,0:T(8,128)S(1)} %collective-permute-done.8.refs_15_), channel_id=1, source_target_pairs={{1,9},{9,1},{17,25},{25,17},{3,11},{11,3},{19,27},{27,19},{5,13},{... | collective-permute-start | bytes 196616 | tf_op jit(solution)/shard_map/ppermute | solution.py:462
  38.4 3.1 %collective-permute-start.15 = (f32[136,128]{1,0:T(8,128)S(1)}, f32[136,128]{1,0:T(8,128)S(1)}, u32[]{:S(2)}, u32[]{:S(2)}) collective-permute-start(f32[136,128]{1,0:T(8,128)S(1)} %collective-permute-done.14.refs_21_.other_ref), channel_id=1, source_target_pairs={{2,18},{10,26},{18,2},{26,10},{3,19},{11,27},{19,3},{27,11},{6,22}... | collective-permute-start | bytes 208904 | tf_op jit(solution)/shard_map/ppermute | solution.py:462
  41.5 1.9 %collective-permute-start.16 = (f32[136,128]{1,0:T(8,128)S(1)}, f32[136,128]{1,0:T(8,128)S(1)}, u32[]{:S(2)}, u32[]{:S(2)}) collective-permute-start(f32[136,128]{1,0:T(8,128)S(1)} %collective-permute-done.14.refs_21_.other_ref), channel_id=1, source_target_pairs={{2,3},{10,11},{18,19},{26,27},{3,2},{11,10},{19,18},{27,26},{6,7},... | collective-permute-start | bytes 208904 | tf_op jit(solution)/shard_map/ppermute | solution.py:462
  43.5 3.4 %collective-permute-start.17 = (f32[136,128]{1,0:T(8,128)S(1)}, f32[136,128]{1,0:T(8,128)S(1)}, u32[]{:S(2)}, u32[]{:S(2)}) collective-permute-start(f32[136,128]{1,0:T(8,128)S(1)} %collective-permute-done.14.refs_21_.other_ref), channel_id=1, source_target_pairs={{2,19},{10,27},{18,3},{26,11},{3,18},{11,26},{19,2},{27,10},{6,23}... | collective-permute-start | bytes 208904 | tf_op jit(solution)/shard_map/ppermute | solution.py:462
  46.9 3.1 %collective-permute-start.13 = (f32[128,128]{1,0:T(8,128)S(1)}, f32[128,128]{1,0:T(8,128)S(1)}, u32[]{:S(2)}, u32[]{:S(2)}) collective-permute-start(f32[128,128]{1,0:T(8,128)S(1)} %collective-permute-done.9.refs_16_), channel_id=1, source_target_pairs={{1,9},{9,1},{17,25},{25,17},{3,11},{11,3},{19,27},{27,19},{5,13},{... | collective-permute-start | bytes 196616 | tf_op jit(solution)/shard_map/ppermute | solution.py:462
  50.0 1.9 %collective-permute-start.6 = (f32[512,128]{1,0:T(8,128)S(1)}, f32[512,128]{1,0:T(8,128)S(1)}, u32[]{:S(2)}, u32[]{:S(2)}) collective-permute-start(f32[512,128]{1,0:T(8,128)S(1)} %collective-permute-done.5.refs_11_), channel_id=1, source_target_pairs={{16,24},{24,16},{17,25},{25,17},{18,26},{26,18},{19,27},{27,19},{2... | collective-permute-start | bytes 786440 | tf_op jit(solution)/shard_map/ppermute | solution.py:462
  51.9 3.4 %local2.1 = (f32[1024,1024]{1,0:T(8,128)}, f32[8,128]{1,0:T(8,128)}) custom-call(bf16[1024,128]{1,0:T(8,128)(2,1)} %refs_1_.3, bf16[1024,128]{1,0:T(8,128)(2,1)} %k_ref.7, bf16[1024,1024]{1,0:T(8,128)(2,1)} %v_ref.5, f32[2,8,1024]{2,1,0:T(8,128)} %get-tuple-element.26.sums_ref.refs_2_, ...), custom_call_target="tpu_custom_call", output_to_operand_aliasing={{0}: (7, {})} | custom-call | tf_op jit(solution)/shard_map/local2/pallas_call | solution.py:205
  56.9 2.4 %collective-permute-start.18 = (f32[136,128]{1,0:T(8,128)}, f32[136,128]{1,0:T(8,128)S(1)}, u32[]{:S(2)}, u32[]{:S(2)}) collective-permute-start(f32[136,128]{1,0:T(8,128)} %copy-done.1), channel_id=1, source_target_pairs={{2,10},{10,2},{18,26},{26,18},{3,11},{11,3},{19,27},{27,19},{6,14}... | collective-permute-start | bytes 208904 | tf_op jit(solution)/shard_map/ppermute | solution.py:462
  59.5 2.2 %collective-permute-start.19 = (f32[136,128]{1,0:T(8,128)S(1)}, f32[136,128]{1,0:T(8,128)S(1)}, u32[]{:S(2)}, u32[]{:S(2)}) collective-permute-start(f32[136,128]{1,0:T(8,128)S(1)} %collective-permute-done.15.refs_22_), channel_id=1, source_target_pairs={{2,10},{10,2},{18,26},{26,18},{3,11},{11,3},{19,27},{27,19},{6,14}... | collective-permute-start | bytes 208904 | tf_op jit(solution)/shard_map/ppermute | solution.py:462
  61.7 2.1 %collective-permute-start.20 = (f32[136,128]{1,0:T(8,128)S(1)}, f32[136,128]{1,0:T(8,128)S(1)}, u32[]{:S(2)}, u32[]{:S(2)}) collective-permute-start(f32[136,128]{1,0:T(8,128)S(1)} %collective-permute-done.16.refs_23_), channel_id=1, source_target_pairs={{2,10},{10,2},{18,26},{26,18},{3,11},{11,3},{19,27},{27,19},{6,14}... | collective-permute-start | bytes 208904 | tf_op jit(solution)/shard_map/ppermute | solution.py:462
  63.9 2.2 %collective-permute-start.21 = (f32[136,128]{1,0:T(8,128)S(1)}, f32[136,128]{1,0:T(8,128)S(1)}, u32[]{:S(2)}, u32[]{:S(2)}) collective-permute-start(f32[136,128]{1,0:T(8,128)S(1)} %collective-permute-done.17.refs_24_), channel_id=1, source_target_pairs={{2,10},{10,2},{18,26},{26,18},{3,11},{11,3},{19,27},{27,19},{6,14}... | collective-permute-start | bytes 208904 | tf_op jit(solution)/shard_map/ppermute | solution.py:462
  70.0 4.5 %collective-permute-start.25 = (f32[136,128]{1,0:T(8,128)S(1)}, f32[136,128]{1,0:T(8,128)S(1)}, u32[]{:S(2)}, u32[]{:S(2)}) collective-permute-start(f32[136,128]{1,0:T(8,128)S(1)} %collective-permute-done.22.refs_6_), channel_id=1, source_target_pairs={{4,21},{12,29},{20,5},{28,13},{5,20},{13,28},{21,4},{29,12},{6,23}... | collective-permute-start | bytes 208904 | tf_op jit(solution)/shard_map/ppermute | solution.py:462
  74.5 3.0 %collective-permute-start.26 = (f32[136,128]{1,0:T(8,128)S(1)}, f32[136,128]{1,0:T(8,128)S(1)}, u32[]{:S(2)}, u32[]{:S(2)}) collective-permute-start(f32[136,128]{1,0:T(8,128)S(1)} %collective-permute-done.22.refs_6_), channel_id=1, source_target_pairs={{4,12},{12,4},{20,28},{28,20},{5,13},{13,5},{21,29},{29,21},{6,14}... | collective-permute-start | bytes 208904 | tf_op jit(solution)/shard_map/ppermute | solution.py:462
  77.5 1.9 %collective-permute-start.27 = (f32[136,128]{1,0:T(8,128)S(1)}, f32[136,128]{1,0:T(8,128)S(1)}, u32[]{:S(2)}, u32[]{:S(2)}) collective-permute-start(f32[136,128]{1,0:T(8,128)S(1)} %collective-permute-done.23.refs_7_), channel_id=1, source_target_pairs={{4,12},{12,4},{20,28},{28,20},{5,13},{13,5},{21,29},{29,21},{6,14}... | collective-permute-start | bytes 208904 | tf_op jit(solution)/shard_map/ppermute | solution.py:462
  79.5 2.4 %collective-permute-start.28 = (f32[136,128]{1,0:T(8,128)S(1)}, f32[136,128]{1,0:T(8,128)S(1)}, u32[]{:S(2)}, u32[]{:S(2)}) collective-permute-start(f32[136,128]{1,0:T(8,128)S(1)} %collective-permute-done.24.refs_8_), channel_id=1, source_target_pairs={{4,12},{12,4},{20,28},{28,20},{5,13},{13,5},{21,29},{29,21},{6,14}... | collective-permute-start | bytes 208904 | tf_op jit(solution)/shard_map/ppermute | solution.py:462
  83.8 3.6 %local3.1 = (f32[1024,1024]{1,0:T(8,128)}, f32[8,128]{1,0:T(8,128)}) custom-call(bf16[1024,128]{1,0:T(8,128)(2,1)} %refs_1_.3, bf16[1024,128]{1,0:T(8,128)(2,1)} %k_ref.7, bf16[1024,1024]{1,0:T(8,128)(2,1)} %v_ref.5, f32[2,8,1024]{2,1,0:T(8,128)} %get-tuple-element.26.sums_ref.refs_2_, ...), custom_call_target="tpu_custom_call", output_to_operand_aliasing={{0}: (7, {})} | custom-call | tf_op jit(solution)/shard_map/local3/pallas_call | solution.py:205
  88.2 7.3 %reach.1.refs_0_ = f32[1024,1024]{1,0:T(8,128)} custom-call(f32[1024,1024]{1,0:T(8,128)} %get-tuple-element.31.refs_0_, bf16[1024,128]{1,0:T(8,128)(2,1)} %refs_1_.3, f32[2,8,1024]{2,1,0:T(8,128)} %get-tuple-element.26.sums_ref.refs_2_, f32[8,8,1024]{2,1,0:T(8,128)} %refs_3_.3, f32[8,128]{1,0:T(8,128)} %bitcast.2, ...), custom_call_target="tpu_custom_call", output_to_operand_aliasing={{}: (0, {})} | custom-call | tf_op jit(solution)/shard_map/reach/pallas_call | solution.py:426
  96.3 6.1 %finish.1 = bf16[1024,1024]{1,0:T(8,128)(2,1)} custom-call(f32[1024,1024]{1,0:T(8,128)} %reach.1.refs_0_, bf16[1024,128]{1,0:T(8,128)(2,1)} %refs_1_.3, f32[2,8,1024]{2,1,0:T(8,128)} %get-tuple-element.26.sums_ref.refs_2_, f32[8,8,1024]{2,1,0:T(8,128)} %refs_3_.3, f32[8,128]{1,0:T(8,128)} %bitcast.3, f32[1,8,128]{2,1,0:T(8,128)} %get-tuple-element.45.refs_5_, ...), custom_call_target="tpu_custom_call" | custom-call | tf_op jit(solution)/shard_map/finish/pallas_call | solution.py:426
  (106 shorter events, 23.7 us)
Async XLA Ops:
  5.3 22.7 %collective-permute-start.4 = (f32[520,128]{1,0:T(8,128)}, f32[520,128]{1,0:T(8,128)S(1)}, u32[]{:S(2)}, u32[]{:S(2)}) collective-permute-start(f32[520,128]{1,0:T(8,128)} %get-tuple-element.32.mine_ref), channel_id=1, source_target_pairs={{0,8},{16,24},{1,9},{17,25},{2,10},{18,26},{3,11},{19,27},{4,12},{... | collective-permute-start | bytes 798728 | tf_op jit(solution)/shard_map/ppermute | solution.py:462
  9.3 40.7 %collective-permute-start.5 = (f32[512,128]{1,0:T(8,128)}, f32[512,128]{1,0:T(8,128)S(1)}, u32[]{:S(2)}, u32[]{:S(2)}) collective-permute-start(f32[512,128]{1,0:T(8,128)} %get-tuple-element.41), channel_id=1, source_target_pairs={{0,16},{8,24},{1,17},{9,25},{2,18},{10,26},{3,19},{11,27},{4,20},{... | collective-permute-start | bytes 786440 | tf_op jit(solution)/shard_map/ppermute | solution.py:462
  10.6 10.5 %collective-permute-start.1 = (f32[136,128]{1,0:T(8,128)}, f32[136,128]{1,0:T(8,128)S(1)}, u32[]{:S(2)}, u32[]{:S(2)}) collective-permute-start(f32[136,128]{1,0:T(8,128)} %get-tuple-element.36), channel_id=1, source_target_pairs={{0,16},{8,24},{16,0},{24,8},{1,17},{9,25},{17,1},{25,9},{2,18},{10... | collective-permute-start | bytes 208904 | tf_op jit(solution)/shard_map/ppermute | solution.py:462
  12.7 8.4 %collective-permute-start.2 = (f32[136,128]{1,0:T(8,128)}, f32[136,128]{1,0:T(8,128)S(1)}, u32[]{:S(2)}, u32[]{:S(2)}) collective-permute-start(f32[136,128]{1,0:T(8,128)} %get-tuple-element.37), channel_id=1, source_target_pairs={{0,1},{8,9},{16,17},{24,25},{1,0},{9,8},{17,16},{25,24},{2,3},{10,... | collective-permute-start | bytes 208904 | tf_op jit(solution)/shard_map/ppermute | solution.py:462
  25.4 8.3 %collective-permute-start.8 = (f32[128,128]{1,0:T(8,128)}, f32[128,128]{1,0:T(8,128)S(1)}, u32[]{:S(2)}, u32[]{:S(2)}) collective-permute-start(f32[128,128]{1,0:T(8,128)} %get-tuple-element.42.refs_13_), channel_id=1, source_target_pairs={{0,1},{8,9},{16,17},{24,25},{2,3},{10,11},{18,19},{26,27},{4,5},{1... | collective-permute-start | bytes 196616 | tf_op jit(solution)/shard_map/ppermute | solution.py:462
  26.7 9.6 %collective-permute-start.9 = (f32[128,128]{1,0:T(8,128)}, f32[128,128]{1,0:T(8,128)S(1)}, u32[]{:S(2)}, u32[]{:S(2)}) collective-permute-start(f32[128,128]{1,0:T(8,128)} %get-tuple-element.42.refs_13_), channel_id=1, source_target_pairs={{0,17},{8,25},{16,1},{24,9},{2,19},{10,27},{18,3},{26,11},{4,21},{... | collective-permute-start | bytes 196616 | tf_op jit(solution)/shard_map/ppermute | solution.py:462
  28.0 10.4 %collective-permute-start.14 = (f32[136,128]{1,0:T(8,128)}, f32[136,128]{1,0:T(8,128)S(1)}, u32[]{:S(2)}, u32[]{:S(2)}) collective-permute-start(f32[136,128]{1,0:T(8,128)} %get-tuple-element.43.mine_ref), channel_id=1, source_target_pairs={{0,2},{8,10},{16,18},{24,26},{1,3},{9,11},{17,19},{25,27},{2,0},{1... | collective-permute-start | bytes 208904 | tf_op jit(solution)/shard_map/ppermute | solution.py:462
  28.7 12.8 %collective-permute-start.10 = (f32[128,128]{1,0:T(8,128)}, f32[128,128]{1,0:T(8,128)S(1)}, u32[]{:S(2)}, u32[]{:S(2)}) collective-permute-start(f32[128,128]{1,0:T(8,128)} %get-tuple-element.42.refs_13_), channel_id=1, source_target_pairs={{1,9},{9,1},{17,25},{25,17},{3,11},{11,3},{19,27},{27,19},{5,13},{... | collective-permute-start | bytes 196616 | tf_op jit(solution)/shard_map/ppermute | solution.py:462
  33.7 9.7 %collective-permute-start.11 = (f32[128,128]{1,0:T(8,128)S(1)}, f32[128,128]{1,0:T(8,128)S(1)}, u32[]{:S(2)}, u32[]{:S(2)}) collective-permute-start(f32[128,128]{1,0:T(8,128)S(1)} %collective-permute-done.7.refs_14_), channel_id=1, source_target_pairs={{1,9},{9,1},{17,25},{25,17},{3,11},{11,3},{19,27},{27,19},{5,13},{... | collective-permute-start | bytes 196616 | tf_op jit(solution)/shard_map/ppermute | solution.py:462
  36.3 10.5 %collective-permute-start.12 = (f32[128,128]{1,0:T(8,128)S(1)}, f32[128,128]{1,0:T(8,128)S(1)}, u32[]{:S(2)}, u32[]{:S(2)}) collective-permute-start(f32[128,128]{1,0:T(8,128)S(1)} %collective-permute-done.8.refs_15_), channel_id=1, source_target_pairs={{1,9},{9,1},{17,25},{25,17},{3,11},{11,3},{19,27},{27,19},{5,13},{... | collective-permute-start | bytes 196616 | tf_op jit(solution)/shard_map/ppermute | solution.py:462
  38.4 20.9 %collective-permute-start.15 = (f32[136,128]{1,0:T(8,128)S(1)}, f32[136,128]{1,0:T(8,128)S(1)}, u32[]{:S(2)}, u32[]{:S(2)}) collective-permute-start(f32[136,128]{1,0:T(8,128)S(1)} %collective-permute-done.14.refs_21_.other_ref), channel_id=1, source_target_pairs={{2,18},{10,26},{18,2},{26,10},{3,19},{11,27},{19,3},{27,11},{6,22}... | collective-permute-start | bytes 208904 | tf_op jit(solution)/shard_map/ppermute | solution.py:462
  41.5 18.0 %collective-permute-start.16 = (f32[136,128]{1,0:T(8,128)S(1)}, f32[136,128]{1,0:T(8,128)S(1)}, u32[]{:S(2)}, u32[]{:S(2)}) collective-permute-start(f32[136,128]{1,0:T(8,128)S(1)} %collective-permute-done.14.refs_21_.other_ref), channel_id=1, source_target_pairs={{2,3},{10,11},{18,19},{26,27},{3,2},{11,10},{19,18},{27,26},{6,7},... | collective-permute-start | bytes 208904 | tf_op jit(solution)/shard_map/ppermute | solution.py:462
  43.5 18.2 %collective-permute-start.17 = (f32[136,128]{1,0:T(8,128)S(1)}, f32[136,128]{1,0:T(8,128)S(1)}, u32[]{:S(2)}, u32[]{:S(2)}) collective-permute-start(f32[136,128]{1,0:T(8,128)S(1)} %collective-permute-done.14.refs_21_.other_ref), channel_id=1, source_target_pairs={{2,19},{10,27},{18,3},{26,11},{3,18},{11,26},{19,2},{27,10},{6,23}... | collective-permute-start | bytes 208904 | tf_op jit(solution)/shard_map/ppermute | solution.py:462
  46.9 10.1 %collective-permute-start.13 = (f32[128,128]{1,0:T(8,128)S(1)}, f32[128,128]{1,0:T(8,128)S(1)}, u32[]{:S(2)}, u32[]{:S(2)}) collective-permute-start(f32[128,128]{1,0:T(8,128)S(1)} %collective-permute-done.9.refs_16_), channel_id=1, source_target_pairs={{1,9},{9,1},{17,25},{25,17},{3,11},{11,3},{19,27},{27,19},{5,13},{... | collective-permute-start | bytes 196616 | tf_op jit(solution)/shard_map/ppermute | solution.py:462
  50.0 37.5 %collective-permute-start.6 = (f32[512,128]{1,0:T(8,128)S(1)}, f32[512,128]{1,0:T(8,128)S(1)}, u32[]{:S(2)}, u32[]{:S(2)}) collective-permute-start(f32[512,128]{1,0:T(8,128)S(1)} %collective-permute-done.5.refs_11_), channel_id=1, source_target_pairs={{16,24},{24,16},{17,25},{25,17},{18,26},{26,18},{19,27},{27,19},{2... | collective-permute-start | bytes 786440 | tf_op jit(solution)/shard_map/ppermute | solution.py:462
  59.5 8.5 %collective-permute-start.19 = (f32[136,128]{1,0:T(8,128)S(1)}, f32[136,128]{1,0:T(8,128)S(1)}, u32[]{:S(2)}, u32[]{:S(2)}) collective-permute-start(f32[136,128]{1,0:T(8,128)S(1)} %collective-permute-done.15.refs_22_), channel_id=1, source_target_pairs={{2,10},{10,2},{18,26},{26,18},{3,11},{11,3},{19,27},{27,19},{6,14}... | collective-permute-start | bytes 208904 | tf_op jit(solution)/shard_map/ppermute | solution.py:462
  63.9 10.7 %collective-permute-start.21 = (f32[136,128]{1,0:T(8,128)S(1)}, f32[136,128]{1,0:T(8,128)S(1)}, u32[]{:S(2)}, u32[]{:S(2)}) collective-permute-start(f32[136,128]{1,0:T(8,128)S(1)} %collective-permute-done.17.refs_24_), channel_id=1, source_target_pairs={{2,10},{10,2},{18,26},{26,18},{3,11},{11,3},{19,27},{27,19},{6,14}... | collective-permute-start | bytes 208904 | tf_op jit(solution)/shard_map/ppermute | solution.py:462
  66.1 11.4 %collective-permute-start.23 = (f32[136,128]{1,0:T(8,128)S(1)}, f32[136,128]{1,0:T(8,128)S(1)}, u32[]{:S(2)}, u32[]{:S(2)}) collective-permute-start(f32[136,128]{1,0:T(8,128)S(1)} %collective-permute-done.22.refs_6_), channel_id=1, source_target_pairs={{4,20},{12,28},{20,4},{28,12},{5,21},{13,29},{21,5},{29,13},{6,22}... | collective-permute-start | bytes 208904 | tf_op jit(solution)/shard_map/ppermute | solution.py:462
  68.0 11.4 %collective-permute-start.24 = (f32[136,128]{1,0:T(8,128)S(1)}, f32[136,128]{1,0:T(8,128)S(1)}, u32[]{:S(2)}, u32[]{:S(2)}) collective-permute-start(f32[136,128]{1,0:T(8,128)S(1)} %collective-permute-done.22.refs_6_), channel_id=1, source_target_pairs={{4,5},{12,13},{20,21},{28,29},{5,4},{13,12},{21,20},{29,28},{6,7},... | collective-permute-start | bytes 208904 | tf_op jit(solution)/shard_map/ppermute | solution.py:462
  70.0 11.9 %collective-permute-start.25 = (f32[136,128]{1,0:T(8,128)S(1)}, f32[136,128]{1,0:T(8,128)S(1)}, u32[]{:S(2)}, u32[]{:S(2)}) collective-permute-start(f32[136,128]{1,0:T(8,128)S(1)} %collective-permute-done.22.refs_6_), channel_id=1, source_target_pairs={{4,21},{12,29},{20,5},{28,13},{5,20},{13,28},{21,4},{29,12},{6,23}... | collective-permute-start | bytes 208904 | tf_op jit(solution)/shard_map/ppermute | solution.py:462
  74.5 21.0 %collective-permute-start.26 = (f32[136,128]{1,0:T(8,128)S(1)}, f32[136,128]{1,0:T(8,128)S(1)}, u32[]{:S(2)}, u32[]{:S(2)}) collective-permute-start(f32[136,128]{1,0:T(8,128)S(1)} %collective-permute-done.22.refs_6_), channel_id=1, source_target_pairs={{4,12},{12,4},{20,28},{28,20},{5,13},{13,5},{21,29},{29,21},{6,14}... | collective-permute-start | bytes 208904 | tf_op jit(solution)/shard_map/ppermute | solution.py:462
  77.5 18.1 %collective-permute-start.27 = (f32[136,128]{1,0:T(8,128)S(1)}, f32[136,128]{1,0:T(8,128)S(1)}, u32[]{:S(2)}, u32[]{:S(2)}) collective-permute-start(f32[136,128]{1,0:T(8,128)S(1)} %collective-permute-done.23.refs_7_), channel_id=1, source_target_pairs={{4,12},{12,4},{20,28},{28,20},{5,13},{13,5},{21,29},{29,21},{6,14}... | collective-permute-start | bytes 208904 | tf_op jit(solution)/shard_map/ppermute | solution.py:462
  79.5 16.1 %collective-permute-start.28 = (f32[136,128]{1,0:T(8,128)S(1)}, f32[136,128]{1,0:T(8,128)S(1)}, u32[]{:S(2)}, u32[]{:S(2)}) collective-permute-start(f32[136,128]{1,0:T(8,128)S(1)} %collective-permute-done.24.refs_8_), channel_id=1, source_target_pairs={{4,12},{12,4},{20,28},{28,20},{5,13},{13,5},{21,29},{29,21},{6,14}... | collective-permute-start | bytes 208904 | tf_op jit(solution)/shard_map/ppermute | solution.py:462
  81.9 13.7 %collective-permute-start.29 = (f32[136,128]{1,0:T(8,128)S(1)}, f32[136,128]{1,0:T(8,128)S(1)}, u32[]{:S(2)}, u32[]{:S(2)}) collective-permute-start(f32[136,128]{1,0:T(8,128)S(1)} %collective-permute-done.25.refs_9_), channel_id=1, source_target_pairs={{4,12},{12,4},{20,28},{28,20},{5,13},{13,5},{21,29},{29,21},{6,14}... | collective-permute-start | bytes 208904 | tf_op jit(solution)/shard_map/ppermute | solution.py:462
  (36 other events, 720.2 us)

commit v3 on v2

v3 whole, which is shorter than its diff:
```python
import functools

import jax
import jax.numpy as jnp
from jax import lax
from jax.experimental import pallas as pl
from jax.experimental.pallas import tpu as pltpu
from jax.sharding import PartitionSpec as P

SPAN = 256
EPS = 1e-05
NT = (((1,), (1,)), ((), ()))
VMEM = 56 * 1024 * 1024
PARAMS = pltpu.CompilerParams(vmem_limit_bytes=VMEM)


def place():
    inner = lax.axis_index("low") * lax.axis_size("narrow") + lax.axis_index("narrow")
    return lax.axis_index("high") * lax.axis_size("low") * lax.axis_size("narrow") + inner


def bit_of(value, bit):
    return jnp.bitwise_and(jnp.right_shift(value, bit), 1)


def spread_lanes(column, width):
    return jnp.broadcast_to(column, (column.shape[0], width))


def whole(array):
    return pl.BlockSpec(array.shape, lambda *_: (0,) * len(array.shape))


ANYWHERE = pl.BlockSpec(memory_space=pl.ANY)


def running_sums(rows):
    high = rows.astype(jnp.bfloat16)
    rest = rows - high.astype(jnp.float32)
    middle = rest.astype(jnp.bfloat16)
    low = (rest - middle.astype(jnp.float32)).astype(jnp.bfloat16)
    width = rows.shape[1]
    source = lax.broadcasted_iota(jnp.int32, (width, width), 0)
    target = lax.broadcasted_iota(jnp.int32, (width, width), 1)
    upto = jnp.where(source <= target, 1.0, 0.0).astype(jnp.bfloat16)
    sums = jnp.dot(
        jnp.concatenate([high, middle, low], axis=0), upto, preferred_element_type=jnp.float32
    )
    count = rows.shape[0]
    return sums[:count] + (sums[count : 2 * count] + sums[2 * count :])


def state_kernel(
    k_ref, decay_ref, v_hbm, message_ref, local_ref, sums_ref, totals_ref, v_ref, arrived
):
    heads, tokens = decay_ref.shape
    head_width = v_ref.shape[1] // heads
    spans = tokens // SPAN
    rows_of = [slice(span * SPAN, (span + 1) * SPAN) for span in range(spans)]
    copies = [
        pltpu.make_async_copy(v_hbm.at[rows], v_ref.at[rows], arrived.at[span])
        for span, rows in enumerate(rows_of)
    ]
    for copy in copies:
        copy.start()
    within = running_sums(jnp.concatenate([decay_ref[:, rows] for rows in rows_of], axis=0))
    run = jnp.zeros((heads, 128), jnp.float32)
    fades, wholes = [], []
    for span, rows in enumerate(rows_of):
        here = within[span * heads : (span + 1) * heads]
        last = here[:, SPAN - 1 :]
        total = spread_lanes(last, 128)
        sums_ref[0, :, rows] = here
        sums_ref[1, :, rows] = here + spread_lanes(run[:, :1], SPAN)
        totals_ref[span] = total
        run = run + total
        fades.append(jnp.exp(spread_lanes(last, SPAN) - here))
        wholes.append(jnp.exp(total))
    across = [k_ref[rows].astype(jnp.float32).T for rows in rows_of]
    for copy in copies:
        copy.wait()
    for head in range(heads):
        columns = slice(head * head_width, (head + 1) * head_width)
        states = []
        for span, rows in enumerate(rows_of):
            faded = (across[span] * fades[span][head : head + 1]).astype(jnp.bfloat16)
            states.append(
                jnp.dot(faded, v_ref[rows, columns], preferred_element_type=jnp.float32)
            )
        at = 0
        size = 1
        while size < spans:
            for first in range(0, spans, 2 * size):
                group = states[first]
                for span in range(first + 1, first + size):
                    group = group * wholes[span][head : head + 1] + states[span]
                local_ref[at, :, columns] = group.astype(jnp.bfloat16)
                at += 1
            size *= 2
        group = states[0]
        for span in range(1, spans):
            group = group * wholes[span][head : head + 1] + states[span]
        message_ref[head, :head_width] = group.T
        message_ref[head, head_width:] = run


def make_states(keys, values, log_decay):
    tokens, key_width = keys.shape
    heads = log_decay.shape[0]
    width = values.shape[1]
    spans = tokens // SPAN
    return pl.pallas_call(
        state_kernel,
        in_specs=[whole(keys), whole(log_decay), ANYWHERE],
        out_shape=[
            jax.ShapeDtypeStruct((heads, width // heads + heads, key_width), jnp.float32),
            jax.ShapeDtypeStruct((spans - 1, key_width, width), jnp.bfloat16),
            jax.ShapeDtypeStruct((2, heads, tokens), jnp.float32),
            jax.ShapeDtypeStruct((spans, heads, 128), jnp.float32),
        ],
        scratch_shapes=[
            pltpu.VMEM((tokens, width), jnp.bfloat16),
            pltpu.SemaphoreType.DMA((spans,)),
        ],
        compiler_params=PARAMS,
        name="states",
    )(keys, log_decay, values)


def local_kernel(
    first_span, spans, q_ref, k_ref, v_ref, sums_ref, totals_ref, weight_ref, local_ref, *refs
):
    mixed_ref, done_ref = refs[-2:]
    span = pl.program_id(0) + first_span
    heads = weight_ref.shape[1]
    head_width = v_ref.shape[1] // heads
    local_bits = weight_ref.shape[0] - 1
    half = SPAN // 2
    done_ref[...] = jnp.zeros_like(done_ref)
    queries = q_ref[...]
    scores = lax.dot_general(k_ref[...], queries, NT, preferred_element_type=jnp.float32)
    within = sums_ref[0]
    within_down = within.T
    values_across = v_ref[...].T
    source = lax.broadcasted_iota(jnp.int32, (half, half), 0)
    target = lax.broadcasted_iota(jnp.int32, (half, half), 1)
    causal = source <= target
    empty = jnp.zeros((half, half), jnp.bfloat16)

    def mix(head, low, high, masked):
        rows = slice(low * half, (low + 1) * half)
        columns = slice(high * half, (high + 1) * half)
        gap = within[head : head + 1, columns] - within_down[rows, head : head + 1]
        if masked:
            gap = jnp.where(causal, gap, -1e30)
        mixing = scores[rows, columns] * jnp.exp(gap) * weight_ref[0, head : head + 1, columns]
        return mixing.astype(jnp.bfloat16)

    for head in range(heads):
        rows = slice(head * head_width, (head + 1) * head_width)
        mixing = jnp.concatenate(
            [
                jnp.concatenate([mix(head, 0, 0, True), mix(head, 0, 1, False)], axis=1),
                jnp.concatenate([empty, mix(head, 1, 1, True)], axis=1),
            ],
            axis=0,
        )
        mixed_ref[rows] = jnp.dot(
            values_across[rows], mixing, preferred_element_type=jnp.float32
        )
    offset = 0
    for bit in range(local_bits):
        since = jnp.zeros((heads, 128), jnp.float32)
        for back in range(1, 2**bit):
            inside = jnp.bitwise_and(span, 2**bit - 1) >= back
            since = since + jnp.where(inside, totals_ref[jnp.maximum(span - back, 0)], 0.0)

        @pl.when(bit_of(span, bit) == 1)
        def _():
            level = local_ref[offset + jnp.right_shift(span, bit + 1)].T
            found = lax.dot_general(level, queries, NT, preferred_element_type=jnp.float32)
            scale = jnp.exp(within + spread_lanes(since[:, :1], SPAN)) * weight_ref[1 + bit]
            for head in range(heads):
                rows = slice(head * head_width, (head + 1) * head_width)
                mixed_ref[rows] += found[rows] * scale[head : head + 1]

        offset = offset + (spans >> (bit + 1))


def mix_local(first, count, queries, keys, values, sums, totals, level_weight, local, mixed):
    tokens, key_width = keys.shape
    heads = level_weight.shape[1]
    width = values.shape[1]
    spans = tokens // SPAN
    local_bits = spans.bit_length() - 1
    rest = [] if mixed is None else [mixed]
    return pl.pallas_call(
        functools.partial(local_kernel, first, spans),
        grid=(count,),
        in_specs=[
            pl.BlockSpec((SPAN, key_width), lambda c: (c + first, 0)),
            pl.BlockSpec((SPAN, key_width), lambda c: (c + first, 0)),
            pl.BlockSpec((SPAN, width), lambda c: (c + first, 0)),
            pl.BlockSpec((2, heads, SPAN), lambda c: (0, 0, c + first)),
            whole(totals),
            pl.BlockSpec((1 + local_bits, heads, SPAN), lambda c: (0, 0, c + first)),
            whole(local),
            *[ANYWHERE for _ in rest],
        ],
        out_specs=[
            pl.BlockSpec((width, SPAN), lambda c: (0, c + first)),
            pl.BlockSpec((8, 128), lambda c: (0, 0)),
        ],
        out_shape=[
            jax.ShapeDtypeStruct((width, tokens), jnp.float32),
            jax.ShapeDtypeStruct((8, 128), jnp.float32),
        ],
        input_output_aliases={7: 0} if rest else {},
        compiler_params=PARAMS,
        name=f"local{first}",
    )(queries, keys, values, sums, totals, level_weight, local, *rest)


def tree(states, totals, rows):
    sizes = [(states, totals)]
    while len(states) > 1:
        states = [
            states[at] * jnp.exp(rows[at + 1]) + states[at + 1] for at in range(0, len(states), 2)
        ]
        totals = [totals[at] + totals[at + 1] for at in range(0, len(totals), 2)]
        rows = [rows[at] + rows[at + 1] for at in range(0, len(rows), 2)]
        sizes.append((states, totals))
    return sizes


def prefixes_of(sizes, here, prefix, bits):
    found = [prefix]
    for bit in range(bits):
        for at in range(0, len(sizes[bit][1]), 2):
            inside = jnp.right_shift(here, bit) == at + 1
            prefix = prefix + jnp.where(inside, sizes[bit][1][at], 0.0)
        found.append(prefix)
    return found


def pick(sizes, here, bit):
    chosen = sizes[bit][0][0]
    for at in range(2, len(sizes[bit][0]), 2):
        chosen = jnp.where(jnp.right_shift(here, bit) == at + 1, sizes[bit][0][at], chosen)
    return chosen


def group_kernel(parts_ref, token_ref, group_ref, lower_ref, prefixes_ref):
    members = parts_ref.shape[0]
    per = lower_ref.shape[1]
    bits = members.bit_length() - 1
    mine = jnp.bitwise_and(place(), members - 1)
    states = [parts_ref[member, :per] for member in range(members)]
    totals = [parts_ref[member, per:] for member in range(members)]
    rows = [parts_ref[member, pl.ds(per + mine, 1)] for member in range(members)]
    sizes = tree(states, totals, rows)
    at = 0
    for bit in range(1, bits):
        for first in range(0, members >> bit, 2):
            lower_ref[at] = sizes[bit][0][first]
            at += 1
    for bit, prefix in enumerate(prefixes_of(sizes, mine, jnp.zeros_like(totals[0]), bits)):
        prefixes_ref[bit] = prefix
    group_ref[:per] = sizes[bits][0][0]
    group_ref[per:] = sizes[bits][1][0]


def make_group(parts, token):
    members, rows, lanes = parts.shape
    bits = members.bit_length() - 1
    per = rows - members
    kinds = sum(members >> (bit + 1) for bit in range(1, bits))
    return pl.pallas_call(
        group_kernel,
        in_specs=[whole(parts), ANYWHERE],
        out_shape=[
            jax.ShapeDtypeStruct((rows, lanes), jnp.float32),
            jax.ShapeDtypeStruct((kinds, per, lanes), jnp.float32),
            jax.ShapeDtypeStruct((bits + 1, members, lanes), jnp.float32),
        ],
        compiler_params=PARAMS,
        name="group",
    )(parts, token)


def upper_kernel(parts_ref, prefix_ref, token_ref, lower_ref, prefixes_ref):
    groups = parts_ref.shape[0]
    per = lower_ref.shape[1]
    heads = prefix_ref.shape[1]
    bits = groups.bit_length() - 1
    here = place()
    mine = jnp.bitwise_and(here, heads - 1)
    high = jnp.right_shift(here, heads.bit_length() - 1)
    states = [parts_ref[group, :per] for group in range(groups)]
    totals = [parts_ref[group, per:] for group in range(groups)]
    rows = [parts_ref[group, pl.ds(per + mine, 1)] for group in range(groups)]
    sizes = tree(states, totals, rows)
    last = prefix_ref.shape[0] - 1
    found = prefixes_of(sizes, high, prefix_ref[last], bits)
    for bit in range(bits):
        lower_ref[bit] = pick(sizes, high, bit)
        prefixes_ref[bit] = found[bit]


def make_upper(parts, prefixes, token):
    groups, rows, lanes = parts.shape
    bits = groups.bit_length() - 1
    heads = prefixes.shape[1]
    return pl.pallas_call(
        upper_kernel,
        in_specs=[whole(parts), whole(prefixes), ANYWHERE],
        out_shape=[
            jax.ShapeDtypeStruct((bits, rows - heads, lanes), jnp.float32),
            jax.ShapeDtypeStruct((bits, heads, lanes), jnp.float32),
        ],
        compiler_params=PARAMS,
        name="upper",
    )(parts, prefixes, token)


def reach_kernel(plan, last, first_level, *refs):
    mixed_ref, q_ref, sums_ref, weight_ref, gain_ref = refs[:5]
    prefix_refs = refs[5 : 5 + len(plan)]
    part_refs = refs[5 + len(plan) : -2]
    out_ref, levels = refs[-2:]
    heads = weight_ref.shape[1]
    head_width = mixed_ref.shape[0] // heads
    here = place()
    mine = jnp.bitwise_and(here, heads - 1)

    @pl.when(pl.program_id(0) == 0)
    def _():
        for slot, (bit, _, kinds) in enumerate(plan):
            ref = part_refs[slot]
            kind = kinds(jnp.right_shift(mine, bit))
            for head in range(heads):
                rows = slice(head * head_width, (head + 1) * head_width)
                if kind is None:
                    level = ref[head, :head_width]
                else:
                    level = ref[head, kind]
                levels[slot, rows] = level.astype(jnp.bfloat16)

    queries = q_ref[...]
    since = sums_ref[1]
    scales = []
    for slot, (bit, at, _) in enumerate(plan):
        active = jnp.where(bit_of(here, bit) == 1, 1.0, 0.0)
        reach = jnp.exp(since + spread_lanes(prefix_refs[slot][at][:, :1], SPAN))
        scales.append(reach * weight_ref[first_level + bit] * active)
    if last:
        gain_down = gain_ref[...].T
    for head in range(heads):
        rows = slice(head * head_width, (head + 1) * head_width)
        mixed = mixed_ref[rows]
        for slot in range(len(plan)):
            found = lax.dot_general(
                levels[slot, rows], queries, NT, preferred_element_type=jnp.float32
            )
            mixed = mixed + found * scales[slot][head : head + 1]
        if last:
            square = jnp.mean(mixed * mixed, axis=0, keepdims=True)
            normed = mixed * lax.rsqrt(square + EPS) * gain_down[:, head : head + 1]
            out_ref[:, rows] = normed.astype(jnp.bfloat16).T
        else:
            out_ref[rows] = mixed


def add_levels(mixed, queries, sums, level_weight, gain, levels, first_level, last):
    width, tokens = mixed.shape
    key_width = queries.shape[1]
    level_count, heads, _ = level_weight.shape
    spans = tokens // SPAN
    plan = [(bit, at, kinds) for bit, _, at, _, kinds in levels]
    prefixes = [level[1] for level in levels]
    flat = [level[3] for level in levels]
    across = pl.BlockSpec((width, SPAN), lambda c: (0, c))
    return pl.pallas_call(
        functools.partial(reach_kernel, plan, last, first_level),
        grid=(spans,),
        in_specs=[
            across,
            pl.BlockSpec((SPAN, key_width), lambda c: (c, 0)),
            pl.BlockSpec((2, heads, SPAN), lambda c: (0, 0, c)),
            pl.BlockSpec((level_count, heads, SPAN), lambda c: (0, 0, c)),
            whole(gain),
            *[whole(array) for array in prefixes],
            *[whole(array) for array in flat],
        ],
        out_specs=pl.BlockSpec((SPAN, width), lambda c: (c, 0)) if last else across,
        out_shape=(
            jax.ShapeDtypeStruct((tokens, width), jnp.bfloat16)
            if last
            else jax.ShapeDtypeStruct(mixed.shape, jnp.float32)
        ),
        input_output_aliases={} if last else {0: 0},
        scratch_shapes=[pltpu.VMEM((len(plan), width, key_width), jnp.bfloat16)],
        compiler_params=PARAMS,
        name="finish" if last else "reach",
    )(mixed, queries, sums, level_weight, gain, *prefixes, *flat)


def per_device(queries, keys, values, log_decay, level_weight, norm_gain):
    heads = log_decay.shape[0]
    tokens, width = values.shape
    spans = tokens // SPAN
    group_bits = heads.bit_length() - 1
    high_bits = lax.axis_size("high").bit_length() - 1
    first_level = level_weight.shape[0] - group_bits - high_bits
    message, local, sums, totals = make_states(keys, values, log_decay)
    shared = (queries, keys, values, sums, totals, level_weight, local)
    inner = lax.axis_size("narrow")
    parts = lax.all_to_all(message, ("low", "narrow"), 0, 0)
    partner = lax.ppermute(message, "narrow", [(at, at + 1) for at in range(0, inner, 2)])
    mixed, token = mix_local(0, spans // 2, *shared, None)
    group, lower, prefixes = make_group(parts, token)
    groups = lax.all_gather(group, "high")
    near = lax.all_gather(lower, ("low", "narrow"))
    mixed, token = mix_local(spans // 2, spans - spans // 2, *shared, mixed)
    upper, upper_prefixes = make_upper(groups, prefixes, token)
    far = lax.all_gather(upper, ("low", "narrow"))
    levels = [(0, prefixes, 0, partner, lambda group: None)]
    at = 0
    for bit in range(1, group_bits):
        levels.append(
            (bit, prefixes, bit, near, lambda group, at=at: at + jnp.right_shift(group, 1))
        )
        at += heads >> (bit + 1)
    gain = norm_gain.reshape(heads, width // heads)
    rest = (queries, sums, level_weight, gain)
    mixed = add_levels(mixed, *rest, levels, first_level, False)
    levels = [
        (group_bits + bit, upper_prefixes, bit, far, lambda group, bit=bit: bit)
        for bit in range(high_bits)
    ]
    return add_levels(mixed, *rest, levels, first_level, True)


def solution(mesh):
    narrow, wide = mesh.shape["narrow"], mesh.shape["wide"]
    along = ("high", "low", "narrow")
    placed = (P(along), P(along), P(along), P(None, along), P(None, None, along), P())

    def run(*inputs):
        low = inputs[3].shape[0] // narrow
        split = jax.sharding.Mesh(
            mesh.devices.reshape(narrow, wide // low, low), ("narrow", "high", "low")
        )
        return jax.shard_map(
            per_device, mesh=split, in_specs=placed, out_specs=P(along), check_vma=False
        )(*inputs)

    return run
```

time: 104 us -> 93.4 us (0.90)
  the two profiles are of different devices: /device:TPU:31 before, /device:TPU:0 now
where the time goes in v3:
time: 93.4 us; the launch traced here: 92.9 us
  Pallas kernels  31.5 us (34%)
  waiting for transfers between devices  25.6 us (27%)
  blocking collectives  15 us (16%)
  between operations  13.4 us (14%)
  starting transfers between devices  6.58 us (7%)
    all_gather x1, waiting for transfers between devices, per_device(): far = lax.all_gather(upper, ('low', 'narrow'))  17.9 us
    all_gather x1, blocking collectives, per_device(): groups = lax.all_gather(group, 'high')  15 us
    pallas_call x2, Pallas kernels, add_levels(): pl.pallas_call(functools.partial(reach_kernel, plan, last, first_level),...  14.1 us
    pallas_call x2, Pallas kernels, mix_local(): pl.pallas_call(functools.partial(local_kernel, first, spans), grid=(count...  9.63 us
    all_to_all x1, starting transfers between devices, per_device(): parts = lax.all_to_all(message, ('low', 'narrow'), 0, 0)  5.17 us
    all_to_all x1, waiting for transfers between devices, per_device(): parts = lax.all_to_all(message, ('low', 'narrow'), 0, 0)  4.67 us
    pallas_call x1, Pallas kernels, make_states(): pl.pallas_call(state_kernel, in_specs=[whole(keys), whole(log_decay), ANY...  4.38 us
  transfers between devices with their start and end apart: 4, of which 4 were waited for; matrix products, arithmetic and copies ran while one was open for 0% of the time, Pallas kernels for 20%

profile of v3, /device:TPU:0, one launch (start us, length us, event | category | flops | bytes accessed | tf_op | source)
XLA Modules:
  0.0 92.9 jit_solution(17056535618198933070)
XLA Ops:
  6.5 4.4 %states.1 = (f32[8,136,128]{2,1,0:T(8,128)}, bf16[3,128,1024]{2,1,0:T(8,128)(2,1)}, f32[2,8,1024]{2,1,0:T(8,128)}, f32[4,8,128]{2,1,0:T(8,128)}) custom-call(bf16[1024,128]{1,0:T(8,128)(2,1)} %k_ref.5, f32[8,1024]{1,0:T(8,128)} %decay_ref.1, bf16[1024,1024]{1,0:T(8,128)(2,1)} %v_ref.3), custom_call_target="tpu_custom_call" | custom-call | tf_op jit(solution)/shard_map/states/pallas_call | solution.py:112
  10.9 5.2 %all-to-all-start = ((f32[8,136,128]{2,1,0:T(8,128)}), f32[8,136,128]{2,1,0:T(8,128)S(1)}, u32[]{:S(2)}, u32[]{:S(2)}) async-start(f32[8,136,128]{2,1,0:T(8,128)} %get-tuple-element.23), calls=%async_computation | async-start | bytes 1114112 | tf_op jit(solution)/shard_map/all_to_all | solution.py:418
  16.1 0.0 all-gather.6.cloned.1.call-start
  16.1 4.5 %local0.1 = (f32[1024,1024]{1,0:T(8,128)}, f32[8,128]{1,0:T(8,128)}) custom-call(bf16[1024,128]{1,0:T(8,128)(2,1)} %refs_1_.3, bf16[1024,128]{1,0:T(8,128)(2,1)} %k_ref.5, bf16[1024,1024]{1,0:T(8,128)(2,1)} %v_ref.3, f32[2,8,1024]{2,1,0:T(8,128)} %get-tuple-element.18.sums_ref.refs_2_, f32[4,8,128]{2,1,0:T(8,128)} %get-tuple-element.19.totals_ref, ...), custom_call_target="tpu_custom_call" | custom-call | tf_op jit(solution)/shard_map/local0/pallas_call | solution.py:197
  20.6 4.7 %all-to-all-done.parts_ref = f32[8,136,128]{2,1,0:T(8,128)S(1)} async-done(((f32[8,136,128]{2,1,0:T(8,128)}), f32[8,136,128]{2,1,0:T(8,128)S(1)}, u32[]{:S(2)}, u32[]{:S(2)}) %all-to-all-start) | async-done | bytes 557088 | tf_op jit(solution)/shard_map/all_to_all | solution.py:418
  25.3 0.0 copy-start
  25.3 0.8 copy-done
  26.1 1.8 %group.1 = (f32[136,128]{1,0:T(8,128)}, f32[3,128,128]{2,1,0:T(8,128)}, f32[4,8,128]{2,1,0:T(8,128)}) custom-call(f32[8,136,128]{2,1,0:T(8,128)} %copy-done, f32[8,128]{1,0:T(8,128)} %get-tuple-element.24.token_ref), custom_call_target="tpu_custom_call" | custom-call | tf_op jit(solution)/shard_map/group/pallas_call | solution.py:278
  27.9 0.0 all-gather.6.cloned.1.call-update
  27.9 0.0 all-gather.8.cloned.1.call-start
  28.0 0.0 copy-start.2
  28.0 5.1 %local2.1 = (f32[1024,1024]{1,0:T(8,128)}, f32[8,128]{1,0:T(8,128)}) custom-call(bf16[1024,128]{1,0:T(8,128)(2,1)} %refs_1_.3, bf16[1024,128]{1,0:T(8,128)(2,1)} %k_ref.5, bf16[1024,1024]{1,0:T(8,128)(2,1)} %v_ref.3, f32[2,8,1024]{2,1,0:T(8,128)} %get-tuple-element.18.sums_ref.refs_2_, ...), custom_call_target="tpu_custom_call", output_to_operand_aliasing={{0}: (7, {})} | custom-call | tf_op jit(solution)/shard_map/local2/pallas_call | solution.py:197
  33.1 0.0 copy-done.3
  33.1 15.0 %all-gather.1 = f32[544,128]{1,0:T(8,128)} all-gather(f32[136,128]{1,0:T(8,128)S(1)} %copy-done.3), channel_id=3, replica_groups=mesh['narrow'=4,'high'=4,'low'=2] {'high'}, dimensions={0}, use_global_device_ids=true | all-gather | bytes 348160 | tf_op jit(solution)/shard_map/all_gather | solution.py:422
  48.1 1.6 %upper.1 = (f32[2,128,128]{2,1,0:T(8,128)}, f32[2,8,128]{2,1,0:T(8,128)}) custom-call(f32[4,136,128]{2,1,0:T(8,128)} %bitcast.8, f32[4,8,128]{2,1,0:T(8,128)} %get-tuple-element.25.refs_5_.refs_6_.refs_7_.prefix_ref, f32[8,128]{1,0:T(8,128)} %get-tuple-element.28.token_ref), custom_call_target="tpu_custom_call" | custom-call | tf_op jit(solution)/shard_map/upper/pallas_call | solution.py:314
  49.7 0.0 all-gather.8.cloned.1.call-update
  49.7 0.0 copy-done.2
  49.8 1.3 %collective-permute-start = (f32[8,136,128]{2,1,0:T(8,128)S(1)}, f32[8,136,128]{2,1,0:T(8,128)S(1)}, u32[]{:S(2)}, u32[]{:S(2)}) collective-permute-start(f32[8,136,128]{2,1,0:T(8,128)S(1)} %copy-done.2), channel_id=1, source_target_pairs={{0,8},{16,24},{1,9},{17,25},{2,10},{18,26},{3,11},{19,27},{4,12},{... | collective-permute-start | bytes 1671176 | tf_op jit(solution)/shard_map/ppermute | solution.py:419
  51.1 1.6 %collective-permute-done.refs_8_ = f32[8,136,128]{2,1,0:T(8,128)S(1)} collective-permute-done((f32[8,136,128]{2,1,0:T(8,128)S(1)}, f32[8,136,128]{2,1,0:T(8,128)S(1)}, u32[]{:S(2)}, u32[]{:S(2)}) %collective-permute-start) | collective-permute-done | bytes 557088 | tf_op jit(solution)/shard_map/ppermute | solution.py:419
  52.7 1.4 %all-gather.6.cloned.1.call-done = f32[24,128,128]{2,1,0:T(8,128)} async-done(((f32[3,128,128]{2,1,0:T(8,128)}), f32[24,128,128]{2,1,0:T(8,128)}) %all-gather.6.cloned.1.call-update) | async-done | bytes 1572880 | tf_op jit(solution)/shard_map/all_gather | solution.py:423
  54.1 0.0 copy-done.1
  54.1 7.5 %reach.1.refs_0_ = f32[1024,1024]{1,0:T(8,128)} custom-call(f32[1024,1024]{1,0:T(8,128)} %get-tuple-element.22.refs_0_, bf16[1024,128]{1,0:T(8,128)(2,1)} %refs_1_.3, f32[2,8,1024]{2,1,0:T(8,128)} %get-tuple-element.18.sums_ref.refs_2_, f32[8,8,1024]{2,1,0:T(8,128)} %refs_3_.3, f32[8,128]{1,0:T(8,128)} %bitcast.9, ...), custom_call_target="tpu_custom_call", output_to_operand_aliasing={{}: (0, {})} | custom-call | tf_op jit(solution)/shard_map/reach/pallas_call | solution.py:383
  61.5 17.9 %all-gather.8.cloned.1.call-done = f32[16,128,128]{2,1,0:T(8,128)} async-done(((f32[2,128,128]{2,1,0:T(8,128)}), f32[16,128,128]{2,1,0:T(8,128)}) %all-gather.8.cloned.1.call-update) | async-done | bytes 1048592 | tf_op jit(solution)/shard_map/all_gather | solution.py:426
  79.5 6.6 %finish.1 = bf16[1024,1024]{1,0:T(8,128)(2,1)} custom-call(f32[1024,1024]{1,0:T(8,128)} %reach.1.refs_0_, bf16[1024,128]{1,0:T(8,128)(2,1)} %refs_1_.3, f32[2,8,1024]{2,1,0:T(8,128)} %get-tuple-element.18.sums_ref.refs_2_, f32[8,8,1024]{2,1,0:T(8,128)} %refs_3_.3, f32[8,128]{1,0:T(8,128)} %bitcast.10, f32[2,8,128]{2,1,0:T(8,128)} %get-tuple-element.29.refs_5_.refs_6_, ...), custom_call_target="tpu_custom_call" | custom-call | tf_op jit(solution)/shard_map/finish/pallas_call | solution.py:383
  (2 shorter events, 0.0 us)
Async XLA Ops:
  10.9 14.4 %all-to-all-start = ((f32[8,136,128]{2,1,0:T(8,128)}), f32[8,136,128]{2,1,0:T(8,128)S(1)}, u32[]{:S(2)}, u32[]{:S(2)}) async-start(f32[8,136,128]{2,1,0:T(8,128)} %get-tuple-element.23), calls=%async_computation | async-start | bytes 1114112 | tf_op jit(solution)/shard_map/all_to_all | solution.py:418
  16.1 38.0 %all-gather.6.cloned.1.call-start = ((), (), s32[]{:S(2)}) async-start(), calls=%async_computation.1 | async-start | bytes 1769472 | tf_op jit(solution)/shard_map/all_gather | solution.py:423
  25.3 0.8 copy-start
  27.9 5.2 %copy-start.3 = (f32[136,128]{1,0:T(8,128)S(1)}, f32[136,128]{1,0:T(8,128)}, u32[]{:S(2)}) copy-start(f32[136,128]{1,0:T(8,128)} %get-tuple-element.27) | copy-start | bytes 208900
  27.9 51.5 %all-gather.8.cloned.1.call-start = ((), (), s32[]{:S(2)}) async-start(), calls=%async_computation.2 | async-start | bytes 1179648 | tf_op jit(solution)/shard_map/all_gather | solution.py:426
  28.0 21.8 %copy-start.2 = (f32[8,136,128]{2,1,0:T(8,128)S(1)}, f32[8,136,128]{2,1,0:T(8,128)}, u32[]{:S(2)}) copy-start(f32[8,136,128]{2,1,0:T(8,128)} %get-tuple-element.23) | copy-start | bytes 1671172
  49.8 2.9 %collective-permute-start = (f32[8,136,128]{2,1,0:T(8,128)S(1)}, f32[8,136,128]{2,1,0:T(8,128)S(1)}, u32[]{:S(2)}, u32[]{:S(2)}) collective-permute-start(f32[8,136,128]{2,1,0:T(8,128)S(1)} %copy-done.2), channel_id=1, source_target_pairs={{0,8},{16,24},{1,9},{17,25},{2,10},{18,26},{3,11},{19,27},{4,12},{... | collective-permute-start | bytes 1671176 | tf_op jit(solution)/shard_map/ppermute | solution.py:419
  52.7 1.4 %copy-start.1 = (f32[8,136,128]{2,1,0:T(8,128)}, f32[8,136,128]{2,1,0:T(8,128)S(1)}, u32[]{:S(2)}) copy-start(f32[8,136,128]{2,1,0:T(8,128)S(1)} %collective-permute-done.refs_8_) | copy-start | bytes 1671172
Sparse Core Ops, SparseCore 0:
  28.0 25.9 all-gather.5
  55.9 23.4 all-gather.7

commit v4 on v0

v4 whole, which is shorter than its diff:
```python
import functools

import jax
import jax.numpy as jnp
from jax import lax
from jax.experimental import pallas as pl
from jax.experimental.pallas import tpu as pltpu
from jax.sharding import PartitionSpec as P

SPAN = 256
EPS = 1e-05
AXES = ("narrow", "wide")
NT = (((1,), (1,)), ((), ()))
PARAMS = pltpu.CompilerParams(vmem_limit_bytes=32 * 1024 * 1024)
HELD = pl.BlockSpec(memory_space=pltpu.VMEM)


def place():
    return lax.axis_index("wide") * lax.axis_size("narrow") + lax.axis_index("narrow")


def bit_of(value, bit):
    return jnp.bitwise_and(jnp.right_shift(value, bit), 1)


def spread_lanes(column, width):
    return jnp.broadcast_to(column, (column.shape[0], width))


ANYWHERE = pl.BlockSpec(memory_space=pl.ANY)


def hold(array):
    return pltpu.with_memory_space_constraint(array, pltpu.VMEM)


def call(kernel, name, inputs, outputs, scratch=(), in_specs=None, aliases=None):
    specs = in_specs or [HELD] * len(inputs)
    inputs = [hold(array) if spec is HELD else array for array, spec in zip(inputs, specs)]
    return pl.pallas_call(
        kernel,
        in_specs=specs,
        out_specs=[HELD] * len(outputs),
        out_shape=[pltpu.VMEM(shape, dtype) for shape, dtype in outputs],
        scratch_shapes=list(scratch),
        input_output_aliases=aliases or {},
        compiler_params=PARAMS,
        name=name,
    )(*inputs)


def running_sums(rows):
    high = rows.astype(jnp.bfloat16)
    rest = rows - high.astype(jnp.float32)
    middle = rest.astype(jnp.bfloat16)
    low = (rest - middle.astype(jnp.float32)).astype(jnp.bfloat16)
    width = rows.shape[1]
    source = lax.broadcasted_iota(jnp.int32, (width, width), 0)
    target = lax.broadcasted_iota(jnp.int32, (width, width), 1)
    upto = jnp.where(source <= target, 1.0, 0.0).astype(jnp.bfloat16)
    sums = jnp.dot(
        jnp.concatenate([high, middle, low], axis=0), upto, preferred_element_type=jnp.float32
    )
    count = rows.shape[0]
    return sums[:count] + (sums[count : 2 * count] + sums[2 * count :])


def state_kernel(
    k_ref, decay_ref, v_hbm, keep_ref, send_ref, local_ref, sums_ref, totals_ref, v_ref, held, arrived
):
    heads, tokens = decay_ref.shape
    head_width = v_ref.shape[1] // heads
    spans = tokens // SPAN
    rows_of = [slice(span * SPAN, (span + 1) * SPAN) for span in range(spans)]
    copies = [
        pltpu.make_async_copy(v_hbm.at[rows], v_ref.at[rows], arrived.at[span])
        for span, rows in enumerate(rows_of)
    ]
    for copy in copies:
        copy.start()
    within = running_sums(jnp.concatenate([decay_ref[:, rows] for rows in rows_of], axis=0))
    run = jnp.zeros((heads, 128), jnp.float32)
    fades, wholes = [], []
    for span, rows in enumerate(rows_of):
        here = within[span * heads : (span + 1) * heads]
        last = here[:, SPAN - 1 :]
        total = spread_lanes(last, 128)
        sums_ref[0, :, rows] = here
        sums_ref[1, :, rows] = here + spread_lanes(run[:, :1], SPAN)
        totals_ref[span] = total
        run = run + total
        fades.append(jnp.exp(spread_lanes(last, SPAN) - here))
        wholes.append(jnp.exp(total))
    across = [k_ref[rows].astype(jnp.float32).T for rows in rows_of]
    for copy in copies:
        copy.wait()
    for head in range(heads):
        columns = slice(head * head_width, (head + 1) * head_width)
        states = []
        for span, rows in enumerate(rows_of):
            faded = (across[span] * fades[span][head : head + 1]).astype(jnp.bfloat16)
            states.append(
                jnp.dot(faded, v_ref[rows, columns], preferred_element_type=jnp.float32)
            )
        at = 0
        size = 1
        while size < spans:
            for first in range(0, spans, 2 * size):
                group = states[first]
                for span in range(first + 1, first + size):
                    group = group * wholes[span][head : head + 1] + states[span]
                local_ref[at, :, columns] = group.astype(jnp.bfloat16)
                at += 1
            size *= 2
        group = states[0]
        for span in range(1, spans):
            group = group * wholes[span][head : head + 1] + states[span]
        held[columns] = group.T
    half = held.shape[0] // 2
    core = bit_of(place(), 0)
    keep_ref[:half] = held[pl.ds(core * half, half)]
    send_ref[:half] = held[pl.ds((1 - core) * half, half)]
    keep_ref[half:] = run
    send_ref[half:] = run


def make_states(keys, values, log_decay):
    tokens, key_width = keys.shape
    heads = log_decay.shape[0]
    width = values.shape[1]
    spans = tokens // SPAN
    message = ((width // 2 + heads, key_width), jnp.float32)
    plain = pl.BlockSpec()
    return call(
        state_kernel,
        "states",
        [keys, log_decay, values],
        [
            message,
            message,
            ((spans - 1, key_width, width), jnp.bfloat16),
            ((2, heads, tokens), jnp.float32),
            ((spans, heads, 128), jnp.float32),
            ((tokens, width), jnp.bfloat16),
        ],
        [pltpu.VMEM((width, key_width), jnp.float32), pltpu.SemaphoreType.DMA((spans,))],
        [plain, plain, ANYWHERE],
    )


def local_kernel(first, last, *refs):
    q_ref, k_ref, v_ref, sums_ref, totals_ref, weight_ref, local_ref = refs[:7]
    mixed_ref, done_ref = refs[-2:]
    heads = weight_ref.shape[1]
    head_width = v_ref.shape[1] // heads
    spans = totals_ref.shape[0]
    local_bits = spans.bit_length() - 1
    half = SPAN // 2
    done_ref[...] = jnp.zeros_like(done_ref)
    source = lax.broadcasted_iota(jnp.int32, (half, half), 0)
    target = lax.broadcasted_iota(jnp.int32, (half, half), 1)
    causal = source <= target
    empty = jnp.zeros((half, half), jnp.bfloat16)

    for span in range(first, last):
        tokens = slice(span * SPAN, (span + 1) * SPAN)
        queries = q_ref[tokens]
        scores = lax.dot_general(
            k_ref[tokens], queries, NT, preferred_element_type=jnp.float32
        )
        within = sums_ref[0, :, tokens]
        within_down = within.T
        weight = weight_ref[0, :, tokens]
        values_across = v_ref[tokens].T

        def mix(head, low, high):
            rows = slice(low * half, (low + 1) * half)
            columns = slice(high * half, (high + 1) * half)
            gap = within[head : head + 1, columns] - within_down[rows, head : head + 1]
            if low == high:
                gap = jnp.where(causal, gap, -1e30)
            mixing = scores[rows, columns] * jnp.exp(gap) * weight[head : head + 1, columns]
            return mixing.astype(jnp.bfloat16)

        levels = []
        offset = 0
        for bit in range(local_bits):
            if span >> bit & 1:
                since = within
                for back in range(1, span % 2**bit + 1):
                    since = since + spread_lanes(totals_ref[span - back][:, :1], SPAN)
                scale = jnp.exp(since) * weight_ref[1 + bit, :, tokens]
                levels.append((local_ref[offset + (span >> (bit + 1))].T, scale))
            offset += spans >> (bit + 1)
        for head in range(heads):
            rows = slice(head * head_width, (head + 1) * head_width)
            mixing = jnp.concatenate(
                [
                    jnp.concatenate([mix(head, 0, 0), mix(head, 0, 1)], axis=1),
                    jnp.concatenate([empty, mix(head, 1, 1)], axis=1),
                ],
                axis=0,
            )
            mixed = jnp.dot(values_across[rows], mixing, preferred_element_type=jnp.float32)
            for level, scale in levels:
                found = lax.dot_general(
                    level[rows], queries, NT, preferred_element_type=jnp.float32
                )
                mixed = mixed + found * scale[head : head + 1]
            mixed_ref[rows, tokens] = mixed


def mix_local(first, last, shared, mixed):
    queries, keys, values, sums, totals, level_weight, local = shared
    rest = [] if mixed is None else [mixed]
    return call(
        functools.partial(local_kernel, first, last),
        f"local{first}",
        [*shared, *rest],
        [(values.shape[::-1], jnp.float32), ((8, 128), jnp.float32)],
        aliases={7: 0} if rest else None,
    )


def join(upper, mine, mine_total, other, other_total):
    fade = jnp.exp(jnp.where(upper, mine_total, other_total))
    return jnp.where(upper, other * fade + mine, mine * fade + other)


def fade_row(ref, state_rows, head):
    return ref[pl.ds(state_rows + head, 1)]


def chip_kernel(mine_ref, other_ref, stay_ref, give_ref, prefix_ref, chip_ref):
    heads = prefix_ref.shape[0]
    half = chip_ref.shape[0]
    held = heads // 2
    per = half // held
    here = place()
    core = bit_of(here, 0)
    upper = core == 1
    for slot in range(held):
        rows = slice(slot * per, (slot + 1) * per)
        head = core * held + slot
        chip_ref[rows] = join(
            upper,
            mine_ref[rows],
            fade_row(mine_ref, half, head),
            other_ref[rows],
            fade_row(other_ref, half, head),
        )
    other_total = other_ref[half:]
    total = mine_ref[half:] + other_total
    prefix_ref[...] = jnp.where(upper, other_total, 0.0)
    quarter = half // 2
    side = bit_of(here, 1)
    stay_ref[:quarter] = chip_ref[pl.ds(side * quarter, quarter)]
    give_ref[:quarter] = chip_ref[pl.ds((1 - side) * quarter, quarter)]
    stay_ref[quarter:] = total
    give_ref[quarter:] = total


def make_chip(mine, other, heads):
    rows, lanes = mine.shape
    half = rows - heads
    message = ((half // 2 + heads, lanes), jnp.float32)
    return call(
        chip_kernel,
        "chip",
        [mine, other],
        [message, message, ((heads, lanes), jnp.float32)],
        [pltpu.VMEM((half, lanes), jnp.float32)],
    )


def merge_kernel(bit, mine_ref, other_ref, prefix_ref, token_ref, merged_ref, next_ref):
    here = place()
    upper = bit_of(here, bit) == 1
    heads = next_ref.shape[0]
    count = heads // 4
    quarter = merged_ref.shape[0] - heads
    per = quarter // count
    for slot in range(count):
        rows = slice(slot * per, (slot + 1) * per)
        head = bit_of(here, 0) * (heads // 2) + bit_of(here, 1) * count + slot
        merged_ref[rows] = join(
            upper,
            mine_ref[rows],
            fade_row(mine_ref, quarter, head),
            other_ref[rows],
            fade_row(other_ref, quarter, head),
        )
    other_total = other_ref[quarter:]
    merged_ref[quarter:] = mine_ref[quarter:] + other_total
    next_ref[...] = prefix_ref[...] + jnp.where(upper, other_total, 0.0)


def merge(bit, mine, other, prefix, token):
    return call(
        functools.partial(merge_kernel, bit),
        f"merge{bit}",
        [mine, other, prefix, token],
        [(mine.shape, jnp.float32), (prefix.shape, jnp.float32)],
    )


def level_scale(bit, first_level, prefix_ref, sums_ref, weight_ref, tokens):
    active = jnp.where(bit_of(place(), bit) == 1, 1.0, 0.0)
    reach = jnp.exp(sums_ref[1, :, tokens] + spread_lanes(prefix_ref[:, :1], SPAN))
    return reach * weight_ref[first_level + bit, :, tokens] * active


def take_levels(plan, part_refs, levels, heads):
    here = place()
    per = levels.shape[1] // heads
    for slot, pieces in enumerate(plan):
        for index, row, far_core, far_side, count in pieces:
            core = jnp.bitwise_xor(bit_of(here, 0), far_core)
            side = jnp.bitwise_xor(bit_of(here, 1), far_side)
            head = core * (heads // 2)
            if count < heads // 2:
                head = head + side * count
            rows = count * per
            start = pl.multiple_of(head * per, 128)
            levels[slot, pl.ds(start, rows)] = part_refs[index][row : row + rows].astype(
                jnp.bfloat16
            )


def reach_kernel(plan, bits, first_level, *refs):
    mixed_ref, q_ref, sums_ref, weight_ref = refs[:4]
    prefix_refs = refs[4 : 4 + len(bits)]
    part_refs = refs[4 + len(bits) : -2]
    out_ref, levels = refs[-2:]
    heads = weight_ref.shape[1]
    head_width = mixed_ref.shape[0] // heads
    take_levels(plan, part_refs, levels, heads)
    for span in range(q_ref.shape[0] // SPAN):
        tokens = slice(span * SPAN, (span + 1) * SPAN)
        queries = q_ref[tokens]
        scales = [
            level_scale(bit, first_level, prefix_ref, sums_ref, weight_ref, tokens)
            for bit, prefix_ref in zip(bits, prefix_refs)
        ]
        for head in range(heads):
            rows = slice(head * head_width, (head + 1) * head_width)
            mixed = mixed_ref[rows, tokens]
            for slot, scale in enumerate(scales):
                found = lax.dot_general(
                    levels[slot, rows], queries, NT, preferred_element_type=jnp.float32
                )
                mixed = mixed + found * scale[head : head + 1]
            out_ref[rows, tokens] = mixed


def add_levels(mixed, queries, sums, level_weight, levels, parts, first_level):
    width = mixed.shape[0]
    bits = [bit for bit, _, _ in levels]
    plan = [pieces for _, _, pieces in levels]
    return call(
        functools.partial(reach_kernel, plan, bits, first_level),
        "reach",
        [mixed, queries, sums, level_weight, *[prefix for _, prefix, _ in levels], *parts],
        [(mixed.shape, jnp.float32)],
        [pltpu.VMEM((len(bits), width, queries.shape[1]), jnp.bfloat16)],
        aliases={0: 0},
    )[0]


def finish_kernel(pieces, bit, first_level, *refs):
    mixed_ref, q_ref, sums_ref, weight_ref, gain_ref, prefix_ref = refs[:6]
    part_refs = refs[6:-4]
    out_hbm, levels, out_ref, sent = refs[-4:]
    heads = weight_ref.shape[1]
    head_width = mixed_ref.shape[0] // heads
    take_levels([pieces], part_refs, levels, heads)
    gain_down = gain_ref[...].T
    copies = []
    for span in range(q_ref.shape[0] // SPAN):
        tokens = slice(span * SPAN, (span + 1) * SPAN)
        queries = q_ref[tokens]
        scale = level_scale(bit, first_level, prefix_ref, sums_ref, weight_ref, tokens)
        for head in range(heads):
            rows = slice(head * head_width, (head + 1) * head_width)
            found = lax.dot_general(
                levels[0, rows], queries, NT, preferred_element_type=jnp.float32
            )
            mixed = mixed_ref[rows, tokens] + found * scale[head : head + 1]
            square = jnp.mean(mixed * mixed, axis=0, keepdims=True)
            normed = mixed * lax.rsqrt(square + EPS) * gain_down[:, head : head + 1]
            out_ref[tokens, rows] = normed.astype(jnp.bfloat16).T
        copy = pltpu.make_async_copy(out_ref.at[tokens], out_hbm.at[tokens], sent.at[span])
        copy.start()
        copies.append(copy)
    for copy in copies:
        copy.wait()


def finish(mixed, queries, sums, level_weight, gain, prefix, pieces, bit, parts, first_level):
    width, tokens = mixed.shape
    inputs = [mixed, queries, sums, level_weight, gain, prefix, *parts]
    return pl.pallas_call(
        functools.partial(finish_kernel, pieces, bit, first_level),
        in_specs=[HELD] * len(inputs),
        out_specs=ANYWHERE,
        out_shape=jax.ShapeDtypeStruct((tokens, width), jnp.bfloat16),
        scratch_shapes=[
            pltpu.VMEM((1, width, queries.shape[1]), jnp.bfloat16),
            pltpu.VMEM((tokens, width), jnp.bfloat16),
            pltpu.SemaphoreType.DMA((tokens // SPAN,)),
        ],
        compiler_params=PARAMS,
        name="finish",
    )(*[hold(array) for array in inputs])


def trade(value, mask, senders=lambda source: True):
    wide, narrow = lax.axis_size("wide"), lax.axis_size("narrow")

    def ranked(index):
        return index % narrow * wide + index // narrow

    pairs = [
        (ranked(source), ranked(source ^ mask))
        for source in range(wide * narrow)
        if senders(source)
    ]
    return lax.ppermute(value, AXES, pairs)


def per_device(queries, keys, values, log_decay, level_weight, norm_gain):
    heads = log_decay.shape[0]
    tokens, width = values.shape
    spans = tokens // SPAN
    half, quarter = width // 2, width // 4
    bits = (lax.axis_size("wide") * lax.axis_size("narrow")).bit_length() - 1
    first_level = level_weight.shape[0] - bits
    keep, send, local, sums, totals, held_values = make_states(keys, values, log_decay)
    shared = (queries, keys, held_values, sums, totals, level_weight, local)
    near = trade(send, 1)
    stay, give, prefix = make_chip(keep, near, heads)
    got = trade(give, 2)
    near_rest = trade(keep, 1, lambda source: source & 1 == 0)
    got_rest = trade(stay, 2, lambda source: source & 2 == 0)
    prefixes = [jnp.zeros((heads, 128), jnp.float32), prefix]
    mixed, at = None, 0
    found = [got]
    for bit in range(1, bits):
        if bit > 1:
            found.append(trade(group, 2**bit))
        mine = group if bit > 1 else stay
        if at < spans and bit < bits - 1:
            mixed, token = mix_local(at, at + 1, shared, mixed)
            at += 1
        if bit < bits - 1:
            group, prefix = merge(bit, mine, found[-1], prefixes[-1], token)
            prefixes.append(prefix)
    if at < spans:
        mixed, token = mix_local(at, spans, shared, mixed)
    middle = jnp.concatenate([state[:quarter] for state in found[1:-1]], axis=0)
    middle_far = trade(middle, 2)
    packed = jnp.concatenate([got[:quarter], got_rest[:quarter], middle, middle_far], axis=0)
    packed_far = trade(packed, 1)
    last = found[-1]
    last_side = trade(last, 2)
    last_parts = [last, last_side, trade(last, 1), trade(last_side, 1)]
    two = heads // 4
    levels = [(0, prefixes[0], [(0, 0, 0, 0, 2 * two), (1, 0, 1, 0, 2 * two)])]
    levels.append(
        (1, prefixes[1], [(2 + far, side * quarter, far, side, two) for far in (0, 1) for side in (0, 1)])
    )
    for bit in range(2, bits - 1):
        row = half + (bit - 2) * quarter
        step = (bits - 3) * quarter
        levels.append(
            (
                bit,
                prefixes[bit],
                [(2 + far, row + side * step, far, side, two) for far in (0, 1) for side in (0, 1)],
            )
        )
    parts = [near, near_rest, packed, packed_far]
    mixed = add_levels(mixed, queries, sums, level_weight, levels, parts, first_level)
    gain = norm_gain.reshape(heads, width // heads)
    pieces = [(0, 0, 0, 0, two), (1, 0, 0, 1, two), (2, 0, 1, 0, two), (3, 0, 1, 1, two)]
    return finish(
        mixed, queries, sums, level_weight, gain, prefixes[bits - 1], pieces, bits - 1, last_parts, first_level
    )


def solution(mesh):
    placed = (
        P(("wide", "narrow"), None),
        P(("wide", "narrow"), None),
        P(("wide", "narrow"), None),
        P(None, ("wide", "narrow")),
        P(None, None, ("wide", "narrow")),
        P(),
    )
    return jax.shard_map(
        per_device,
        mesh=mesh,
        in_specs=placed,
        out_specs=P(("wide", "narrow"), None),
        check_vma=False,
    )
```

time: 134 us -> 56.8 us (0.42)
  matrix products: 52.9 us -> 0 us
  other arithmetic: 12.4 us -> 0.02 us
  waiting for transfers between devices: 36.2 us -> 24.6 us
  Pallas kernels: 0 us -> 11.1 us
  local copies, waits for them, and re-layouts: 16.8 us -> 6.29 us
    dot_general x12 -> x0, matrix products: 52.9 us -> none  [the longest x5 24.7 us: add_level(): jnp.einsum('cin,chnp->chip', query_blocks, per_block, preferred_element_t...]
    ppermute x9 -> x12, waiting for transfers between devices: 36.2 us -> 24.6 us  [trade(): return lax.ppermute(value, AXES, pairs)]
    pallas_call x0 -> x11, Pallas kernels: none -> 11.1 us  [the longest x10 8.42 us: call(): pl.pallas_call(kernel, in_specs=specs, out_specs=[HELD] * len(outputs), o...]
    another operation x8 -> x0, other arithmetic: 8.76 us -> none  [the longest x5 4.54 us: doubling(): levels_found = jnp.stack(found)]
    mul x11 -> x0, local copies, waits for them, and re-layouts: 5.38 us -> none  [the longest x5 3.81 us: add_level(): return running + level_scale[:, :, :, None] * projected]
    convert_element_type x2 -> x0, local copies, waits for them, and re-layouts: 3.26 us -> none  [the longest x1 3.12 us: per_device(): normed.transpose(0, 2, 1, 3).reshape(tokens_here, heads * head_width)]
    convert_element_type x1 -> x0, other arithmetic: 1.85 us -> none  [per_device(): normed.transpose(0, 2, 1, 3).reshape(tokens_here, heads * head_width)]
    ppermute x9 -> x12, starting transfers between devices: 13.9 us -> 14.2 us  [trade(): return lax.ppermute(value, AXES, pairs)]
  transfers between devices with their start and end apart: 9 -> 12, of which waited for: 6 -> 7; matrix products, arithmetic and copies ran while one was open for 22% -> 0% of each run, Pallas kernels for 0% -> 12%
where the time goes in v4:
time: 56.8 us; the launch traced here: 56.4 us
  waiting for transfers between devices  24.6 us (43%)
  starting transfers between devices  14.2 us (25%)
  Pallas kernels  11.1 us (20%)
  local copies, waits for them, and re-layouts  6.29 us (11%)
    ppermute x12, waiting for transfers between devices, trade(): return lax.ppermute(value, AXES, pairs)  24.6 us
    ppermute x12, starting transfers between devices, trade(): return lax.ppermute(value, AXES, pairs)  14.2 us
    pallas_call x10, Pallas kernels, call(): pl.pallas_call(kernel, in_specs=specs, out_specs=[HELD] * len(outputs), o...  8.42 us
    unnamed x22, local copies, waits for them, and re-layouts  6.23 us
    pallas_call x1, Pallas kernels, finish(): pl.pallas_call(functools.partial(finish_kernel, pieces, bit, first_level)...  2.73 us
  transfers between devices with their start and end apart: 12, of which 7 were waited for; matrix products, arithmetic and copies ran while one was open for 0% of the time, Pallas kernels for 12%

profile of v4, /device:TPU:0, one launch (start us, length us, event | category | flops | bytes accessed | tf_op | source)
XLA Modules:
  0.0 56.4 jit_solution(361674206567291615)
XLA Ops:
  0.0 1.0 %copy-done.4 = bf16[1024,128]{1,0:T(8,128)(2,1)S(1)} copy-done((bf16[1024,128]{1,0:T(8,128)(2,1)S(1)}, bf16[1024,128]{1,0:T(8,128)(2,1)}, u32[]{:S(2)}) %copy-start.4) | copy-done | bytes 262168
  1.0 1.6 %copy-done.7 = bf16[1024,1024]{1,0:T(8,128)(2,1)S(1)} copy-done((bf16[1024,1024]{1,0:T(8,128)(2,1)S(1)}, bf16[1024,1024]{1,0:T(8,128)(2,1)}, u32[]{:S(2)}) %copy-start.7) | copy-done | bytes 2097176
  3.3 1.6 %states.1 = (f32[520,128]{1,0:T(8,128)S(1)}, f32[520,128]{1,0:T(8,128)S(1)}, bf16[3,128,1024]{2,1,0:T(8,128)(2,1)S(1)}, f32[2,8,1024]{2,1,0:T(8,128)S(1)}, f32[4...) custom-call(bf16[1024,128]{1,0:T(8,128)(2,1)S(1)} %copy-done.4, f32[8,1024]{1,0:T(8,128)S(1)} %copy-done.8, ...), custom_call_target="tpu_custom_call" | custom-call | tf_op jit(solution)/shard_map/states/pallas_call | solution.py:40
  5.4 1.2 %collective-permute-done.other_ref.refs_8_ = f32[520,128]{1,0:T(8,128)S(1)} collective-permute-done((f32[520,128]{1,0:T(8,128)S(1)}, f32[520,128]{1,0:T(8,128)S(1)}, u32[]{:S(2)}, u32[]{:S(2)}) %collective-permute-start) | collective-permute-done | bytes 266272 | tf_op jit(solution)/shard_map/ppermute | solution.py:428
  6.7 3.0 %collective-permute-start.1 = (f32[264,128]{1,0:T(8,128)S(1)}, f32[264,128]{1,0:T(8,128)S(1)}, u32[]{:S(2)}, u32[]{:S(2)}) collective-permute-start(f32[264,128]{1,0:T(8,128)S(1)} %get-tuple-element.39), channel_id=1, source_target_pairs={{0,16},{8,24},{16,0},{24,8},{1,17},{9,25},{17,1},{25,9},{2,18},{10... | collective-permute-start | bytes 405512 | tf_op jit(solution)/shard_map/ppermute | solution.py:428
  9.6 0.9 %copy-done = bf16[1024,128]{1,0:T(8,128)(2,1)S(1)} copy-done((bf16[1024,128]{1,0:T(8,128)(2,1)S(1)}, bf16[1024,128]{1,0:T(8,128)(2,1)}, u32[]{:S(2)}) %copy-start) | copy-done | bytes 262168
  10.6 0.9 %copy-done.2 = f32[8,8,1024]{2,1,0:T(8,128)S(1)} copy-done((f32[8,8,1024]{2,1,0:T(8,128)S(1)}, f32[8,8,1024]{2,1,0:T(8,128)}, u32[]{:S(2)}) %copy-start.2) | copy-done | bytes 262168
  11.5 0.9 %copy-done.5 = bf16[1024,128]{1,0:T(8,128)(2,1)S(1)} copy-done((bf16[1024,128]{1,0:T(8,128)(2,1)S(1)}, bf16[1024,128]{1,0:T(8,128)(2,1)}, u32[]{:S(2)}) %copy-start.5) | copy-done | bytes 262168
  13.3 0.9 %local1.1 = (f32[1024,1024]{1,0:T(8,128)S(1)}, f32[8,128]{1,0:T(8,128)S(1)}) custom-call(bf16[1024,128]{1,0:T(8,128)(2,1)S(1)} %copy-done, bf16[1024,128]{1,0:T(8,128)(2,1)S(1)} %copy-done.5, bf16[1024,1024]{1,0:T(8,128)(2,1)S(1)} %get-tuple-element.27.refs_2_, f32[2,8,1024]{2,1,0:T(8,128)S(1)} %get-tuple-element.28.refs_3_.refs_2_, ...), custom_call_target="tpu_custom_call", output_to_operand_aliasing={{0}: (7, {})} | custom-call | tf_op jit(solution)/shard_map/local1/pallas_call | solution.py:40
  14.2 1.9 %collective-permute-start.4 = (f32[264,128]{1,0:T(8,128)S(1)}, f32[264,128]{1,0:T(8,128)S(1)}, u32[]{:S(2)}, u32[]{:S(2)}) collective-permute-start(f32[264,128]{1,0:T(8,128)S(1)} %get-tuple-element.38.mine_ref), channel_id=1, source_target_pairs={{0,16},{8,24},{1,17},{9,25},{2,18},{10,26},{3,19},{11,27},{4,20},{... | collective-permute-start | bytes 405512 | tf_op jit(solution)/shard_map/ppermute | solution.py:428
  16.2 2.0 %collective-permute-start.2 = (f32[264,128]{1,0:T(8,128)S(1)}, f32[264,128]{1,0:T(8,128)S(1)}, u32[]{:S(2)}, u32[]{:S(2)}) collective-permute-start(f32[264,128]{1,0:T(8,128)S(1)} %get-tuple-element.42.mine_ref), channel_id=1, source_target_pairs={{0,1},{8,9},{16,17},{24,25},{1,0},{9,8},{17,16},{25,24},{2,3},{10,... | collective-permute-start | bytes 405512 | tf_op jit(solution)/shard_map/ppermute | solution.py:428
  18.3 1.0 %collective-permute-done.4 = f32[264,128]{1,0:T(8,128)S(1)} collective-permute-done((f32[264,128]{1,0:T(8,128)S(1)}, f32[264,128]{1,0:T(8,128)S(1)}, u32[]{:S(2)}, u32[]{:S(2)}) %collective-permute-start.4) | collective-permute-done | bytes 135200 | tf_op jit(solution)/shard_map/ppermute | solution.py:428
  19.3 2.3 %collective-permute-done.2.other_ref = f32[264,128]{1,0:T(8,128)S(1)} collective-permute-done((f32[264,128]{1,0:T(8,128)S(1)}, f32[264,128]{1,0:T(8,128)S(1)}, u32[]{:S(2)}, u32[]{:S(2)}) %collective-permute-start.2) | collective-permute-done | bytes 135200 | tf_op jit(solution)/shard_map/ppermute | solution.py:428
  21.7 1.8 %collective-permute-start.5 = (f32[264,128]{1,0:T(8,128)S(1)}, f32[264,128]{1,0:T(8,128)S(1)}, u32[]{:S(2)}, u32[]{:S(2)}) collective-permute-start(f32[264,128]{1,0:T(8,128)S(1)} %get-tuple-element.45.mine_ref), channel_id=1, source_target_pairs={{0,2},{8,10},{16,18},{24,26},{1,3},{9,11},{17,19},{25,27},{2,0},{1... | collective-permute-start | bytes 405512 | tf_op jit(solution)/shard_map/ppermute | solution.py:428
  23.5 3.2 %collective-permute-done.5.other_ref = f32[264,128]{1,0:T(8,128)S(1)} collective-permute-done((f32[264,128]{1,0:T(8,128)S(1)}, f32[264,128]{1,0:T(8,128)S(1)}, u32[]{:S(2)}, u32[]{:S(2)}) %collective-permute-start.5) | collective-permute-done | bytes 135200 | tf_op jit(solution)/shard_map/ppermute | solution.py:428
  27.0 6.2 %collective-permute-done.6 = f32[512,128]{1,0:T(8,128)S(1)} collective-permute-done((f32[512,128]{1,0:T(8,128)S(1)}, f32[512,128]{1,0:T(8,128)S(1)}, u32[]{:S(2)}, u32[]{:S(2)}) %collective-permute-start.6) | collective-permute-done | bytes 262176 | tf_op jit(solution)/shard_map/ppermute | solution.py:428
  33.4 0.9 %local2.1 = (f32[1024,1024]{1,0:T(8,128)S(1)}, f32[8,128]{1,0:T(8,128)S(1)}) custom-call(bf16[1024,128]{1,0:T(8,128)(2,1)S(1)} %copy-done.1, bf16[1024,128]{1,0:T(8,128)(2,1)S(1)} %copy-done.6, bf16[1024,1024]{1,0:T(8,128)(2,1)S(1)} %get-tuple-element.27.refs_2_, ...), custom_call_target="tpu_custom_call", output_to_operand_aliasing={{0}: (7, {})} | custom-call | tf_op jit(solution)/shard_map/local2/pallas_call | solution.py:40
  34.3 2.9 %collective-permute-start.8 = (f32[264,128]{1,0:T(8,128)S(1)}, f32[264,128]{1,0:T(8,128)S(1)}, u32[]{:S(2)}, u32[]{:S(2)}) collective-permute-start(f32[264,128]{1,0:T(8,128)S(1)} %get-tuple-element.48), channel_id=1, source_target_pairs={{0,4},{8,12},{16,20},{24,28},{1,5},{9,13},{17,21},{25,29},{2,6},{1... | collective-permute-start | bytes 405512 | tf_op jit(solution)/shard_map/ppermute | solution.py:428
  37.2 7.1 %collective-permute-done.8.refs_6_ = f32[264,128]{1,0:T(8,128)S(1)} collective-permute-done((f32[264,128]{1,0:T(8,128)S(1)}, f32[264,128]{1,0:T(8,128)S(1)}, u32[]{:S(2)}, u32[]{:S(2)}) %collective-permute-start.8) | collective-permute-done | bytes 135200 | tf_op jit(solution)/shard_map/ppermute | solution.py:428
  44.5 1.5 %collective-permute-start.3 = (f32[520,128]{1,0:T(8,128)S(1)}, f32[520,128]{1,0:T(8,128)S(1)}, u32[]{:S(2)}, u32[]{:S(2)}) collective-permute-start(f32[520,128]{1,0:T(8,128)S(1)} %get-tuple-element.35.mine_ref), channel_id=1, source_target_pairs={{0,8},{16,24},{1,9},{17,25},{2,10},{18,26},{3,11},{19,27},{4,12},{... | collective-permute-start | bytes 798728 | tf_op jit(solution)/shard_map/ppermute | solution.py:428
  46.1 3.5 %collective-permute-done.9.refs_7_ = f32[264,128]{1,0:T(8,128)S(1)} collective-permute-done((f32[264,128]{1,0:T(8,128)S(1)}, f32[264,128]{1,0:T(8,128)S(1)}, u32[]{:S(2)}, u32[]{:S(2)}) %collective-permute-start.9) | collective-permute-done | bytes 135200 | tf_op jit(solution)/shard_map/ppermute | solution.py:428
  49.6 1.6 %local3.1 = (f32[1024,1024]{1,0:T(8,128)S(1)}, f32[8,128]{1,0:T(8,128)}) custom-call(bf16[1024,128]{1,0:T(8,128)(2,1)S(1)} %copy-done.1, bf16[1024,128]{1,0:T(8,128)(2,1)S(1)} %copy-done.6, bf16[1024,1024]{1,0:T(8,128)(2,1)S(1)} %get-tuple-element.27.refs_2_, f32[2,8,1024]{2,1,0:T(8,128)S(1)} %get-tuple-element.28.refs_3_.refs_2_, ...), custom_call_target="tpu_custom_call", output_to_operand_aliasing={{0}: (7, {})} | custom-call | tf_op jit(solution)/shard_map/local3/pallas_call | solution.py:40
  51.1 2.5 %reach.1.refs_0_ = f32[1024,1024]{1,0:T(8,128)S(1)} custom-call(f32[1024,1024]{1,0:T(8,128)S(1)} %get-tuple-element.34.refs_0_, bf16[1024,128]{1,0:T(8,128)(2,1)S(1)} %copy-done.1, f32[2,8,1024]{2,1,0:T(8,128)S(1)} %get-tuple-element.28.refs_3_.refs_2_, f32[8,8,1024]{2,1,0:T(8,128)S(1)} %copy-done.3, ...), custom_call_target="tpu_custom_call", output_to_operand_aliasing={{}: (0, {})} | custom-call | tf_op jit(solution)/shard_map/reach/pallas_call | solution.py:40
  53.7 2.7 %finish.1 = bf16[1024,1024]{1,0:T(8,128)(2,1)} custom-call(f32[1024,1024]{1,0:T(8,128)S(1)} %reach.1.refs_0_, bf16[1024,128]{1,0:T(8,128)(2,1)S(1)} %copy-done.1, f32[2,8,1024]{2,1,0:T(8,128)S(1)} %get-tuple-element.28.refs_3_.refs_2_, f32[8,8,1024]{2,1,0:T(8,128)S(1)} %copy-done.3, f32[8,128]{1,0:T(8,128)S(1)} %bitcast.1, ...), custom_call_target="tpu_custom_call" | custom-call | tf_op jit(solution)/shard_map/finish/pallas_call | solution.py:402
  (38 shorter events, 2.9 us)
Async XLA Ops:
  0.0 13.3 %copy-start.3 = (f32[8,8,1024]{2,1,0:T(8,128)S(1)}, f32[8,8,1024]{2,1,0:T(8,128)}, u32[]{:S(2)}) copy-start(f32[8,8,1024]{2,1,0:T(8,128)} %refs_3_.3) | copy-start | bytes 786436
  0.0 1.0 %copy-start.4 = (bf16[1024,128]{1,0:T(8,128)(2,1)S(1)}, bf16[1024,128]{1,0:T(8,128)(2,1)}, u32[]{:S(2)}) copy-start(bf16[1024,128]{1,0:T(8,128)(2,1)} %refs_1_.9) | copy-start | bytes 786436
  1.0 1.6 %copy-start.7 = (bf16[1024,1024]{1,0:T(8,128)(2,1)S(1)}, bf16[1024,1024]{1,0:T(8,128)(2,1)}, u32[]{:S(2)}) copy-start(bf16[1024,1024]{1,0:T(8,128)(2,1)} %v_hbm.1) | copy-start | bytes 6291460
  2.6 0.8 %copy-start.8 = (f32[8,1024]{1,0:T(8,128)S(1)}, f32[8,1024]{1,0:T(8,128)}, u32[]{:S(2)}) copy-start(f32[8,1024]{1,0:T(8,128)} %decay_ref.1) | copy-start | bytes 98308
  4.9 1.7 %collective-permute-start = (f32[520,128]{1,0:T(8,128)S(1)}, f32[520,128]{1,0:T(8,128)S(1)}, u32[]{:S(2)}, u32[]{:S(2)}) collective-permute-start(f32[520,128]{1,0:T(8,128)S(1)} %get-tuple-element.36), channel_id=1, source_target_pairs={{0,8},{8,0},{16,24},{24,16},{1,9},{9,1},{17,25},{25,17},{2,10},{10... | collective-permute-start | bytes 798728 | tf_op jit(solution)/shard_map/ppermute | solution.py:428
  6.7 9.5 %collective-permute-start.1 = (f32[264,128]{1,0:T(8,128)S(1)}, f32[264,128]{1,0:T(8,128)S(1)}, u32[]{:S(2)}, u32[]{:S(2)}) collective-permute-start(f32[264,128]{1,0:T(8,128)S(1)} %get-tuple-element.39), channel_id=1, source_target_pairs={{0,16},{8,24},{16,0},{24,8},{1,17},{9,25},{17,1},{25,9},{2,18},{10... | collective-permute-start | bytes 405512 | tf_op jit(solution)/shard_map/ppermute | solution.py:428
  9.6 0.9 %copy-start = (bf16[1024,128]{1,0:T(8,128)(2,1)S(1)}, bf16[1024,128]{1,0:T(8,128)(2,1)}, u32[]{:S(2)}) copy-start(bf16[1024,128]{1,0:T(8,128)(2,1)} %refs_1_.11) | copy-start | bytes 786436
  10.6 0.9 %copy-start.2 = (f32[8,8,1024]{2,1,0:T(8,128)S(1)}, f32[8,8,1024]{2,1,0:T(8,128)}, u32[]{:S(2)}) copy-start(f32[8,8,1024]{2,1,0:T(8,128)} %refs_3_.3) | copy-start | bytes 786436
  11.5 0.9 %copy-start.5 = (bf16[1024,128]{1,0:T(8,128)(2,1)S(1)}, bf16[1024,128]{1,0:T(8,128)(2,1)}, u32[]{:S(2)}) copy-start(bf16[1024,128]{1,0:T(8,128)(2,1)} %refs_1_.9) | copy-start | bytes 786436
  13.3 20.0 %copy-start.1 = (bf16[1024,128]{1,0:T(8,128)(2,1)S(1)}, bf16[1024,128]{1,0:T(8,128)(2,1)}, u32[]{:S(2)}) copy-start(bf16[1024,128]{1,0:T(8,128)(2,1)} %refs_1_.11) | copy-start | bytes 786436
  13.3 20.0 %copy-start.6 = (bf16[1024,128]{1,0:T(8,128)(2,1)S(1)}, bf16[1024,128]{1,0:T(8,128)(2,1)}, u32[]{:S(2)}) copy-start(bf16[1024,128]{1,0:T(8,128)(2,1)} %refs_1_.9) | copy-start | bytes 786436
  14.2 5.1 %collective-permute-start.4 = (f32[264,128]{1,0:T(8,128)S(1)}, f32[264,128]{1,0:T(8,128)S(1)}, u32[]{:S(2)}, u32[]{:S(2)}) collective-permute-start(f32[264,128]{1,0:T(8,128)S(1)} %get-tuple-element.38.mine_ref), channel_id=1, source_target_pairs={{0,16},{8,24},{1,17},{9,25},{2,18},{10,26},{3,19},{11,27},{4,20},{... | collective-permute-start | bytes 405512 | tf_op jit(solution)/shard_map/ppermute | solution.py:428
  16.2 5.4 %collective-permute-start.2 = (f32[264,128]{1,0:T(8,128)S(1)}, f32[264,128]{1,0:T(8,128)S(1)}, u32[]{:S(2)}, u32[]{:S(2)}) collective-permute-start(f32[264,128]{1,0:T(8,128)S(1)} %get-tuple-element.42.mine_ref), channel_id=1, source_target_pairs={{0,1},{8,9},{16,17},{24,25},{1,0},{9,8},{17,16},{25,24},{2,3},{10,... | collective-permute-start | bytes 405512 | tf_op jit(solution)/shard_map/ppermute | solution.py:428
  21.7 5.1 %collective-permute-start.5 = (f32[264,128]{1,0:T(8,128)S(1)}, f32[264,128]{1,0:T(8,128)S(1)}, u32[]{:S(2)}, u32[]{:S(2)}) collective-permute-start(f32[264,128]{1,0:T(8,128)S(1)} %get-tuple-element.45.mine_ref), channel_id=1, source_target_pairs={{0,2},{8,10},{16,18},{24,26},{1,3},{9,11},{17,19},{25,27},{2,0},{1... | collective-permute-start | bytes 405512 | tf_op jit(solution)/shard_map/ppermute | solution.py:428
  26.8 6.4 %collective-permute-start.6 = (f32[512,128]{1,0:T(8,128)S(1)}, f32[512,128]{1,0:T(8,128)S(1)}, u32[]{:S(2)}, u32[]{:S(2)}) collective-permute-start(f32[512,128]{1,0:T(8,128)S(1)} %pad_maximum_fusion), channel_id=1, source_target_pairs={{0,16},{8,24},{16,0},{24,8},{1,17},{9,25},{17,1},{25,9},{2,18},{10... | collective-permute-start | bytes 786440 | tf_op jit(solution)/shard_map/ppermute | solution.py:428
  33.3 17.9 %collective-permute-start.7 = (f32[1536,128]{1,0:T(8,128)S(1)}, f32[1536,128]{1,0:T(8,128)S(1)}, u32[]{:S(2)}, u32[]{:S(2)}) collective-permute-start(f32[1536,128]{1,0:T(8,128)S(1)} %constant_dynamic-update-slice_fusion.refs_10_), channel_id=1, source_target_pairs={{0,8},{8,0},{16,24},{24,16},{1,9},{9,1},{17,25},{25,17},{2,10},{10... | collective-permute-start | bytes 2359304 | tf_op jit(solution)/shard_map/ppermute | solution.py:428
  34.3 10.0 %collective-permute-start.8 = (f32[264,128]{1,0:T(8,128)S(1)}, f32[264,128]{1,0:T(8,128)S(1)}, u32[]{:S(2)}, u32[]{:S(2)}) collective-permute-start(f32[264,128]{1,0:T(8,128)S(1)} %get-tuple-element.48), channel_id=1, source_target_pairs={{0,4},{8,12},{16,20},{24,28},{1,5},{9,13},{17,21},{25,29},{2,6},{1... | collective-permute-start | bytes 405512 | tf_op jit(solution)/shard_map/ppermute | solution.py:428
  44.3 5.3 %collective-permute-start.9 = (f32[264,128]{1,0:T(8,128)S(1)}, f32[264,128]{1,0:T(8,128)S(1)}, u32[]{:S(2)}, u32[]{:S(2)}) collective-permute-start(f32[264,128]{1,0:T(8,128)S(1)} %collective-permute-done.8.refs_6_), channel_id=1, source_target_pairs={{0,16},{8,24},{16,0},{24,8},{1,17},{9,25},{17,1},{25,9},{2,18},{10... | collective-permute-start | bytes 405512 | tf_op jit(solution)/shard_map/ppermute | solution.py:428
  44.5 6.7 %collective-permute-start.3 = (f32[520,128]{1,0:T(8,128)S(1)}, f32[520,128]{1,0:T(8,128)S(1)}, u32[]{:S(2)}, u32[]{:S(2)}) collective-permute-start(f32[520,128]{1,0:T(8,128)S(1)} %get-tuple-element.35.mine_ref), channel_id=1, source_target_pairs={{0,8},{16,24},{1,9},{17,25},{2,10},{18,26},{3,11},{19,27},{4,12},{... | collective-permute-start | bytes 798728 | tf_op jit(solution)/shard_map/ppermute | solution.py:428
  46.0 7.7 %collective-permute-start.10 = (f32[264,128]{1,0:T(8,128)S(1)}, f32[264,128]{1,0:T(8,128)S(1)}, u32[]{:S(2)}, u32[]{:S(2)}) collective-permute-start(f32[264,128]{1,0:T(8,128)S(1)} %collective-permute-done.8.refs_6_), channel_id=1, source_target_pairs={{0,8},{8,0},{16,24},{24,16},{1,9},{9,1},{17,25},{25,17},{2,10},{10... | collective-permute-start | bytes 405512 | tf_op jit(solution)/shard_map/ppermute | solution.py:428
  49.6 4.1 %collective-permute-start.11 = (f32[264,128]{1,0:T(8,128)S(1)}, f32[264,128]{1,0:T(8,128)S(1)}, u32[]{:S(2)}, u32[]{:S(2)}) collective-permute-start(f32[264,128]{1,0:T(8,128)S(1)} %collective-permute-done.9.refs_7_), channel_id=1, source_target_pairs={{0,8},{8,0},{16,24},{24,16},{1,9},{9,1},{17,25},{25,17},{2,10},{10... | collective-permute-start | bytes 405512 | tf_op jit(solution)/shard_map/ppermute | solution.py:428
  51.1 2.6 %copy-start.9 = (f32[1024]{0:T(1024)S(1)}, f32[1024]{0:T(1024)}, u32[]{:S(2)}) copy-start(f32[1024]{0:T(1024)} %param.11) | copy-start | bytes 12292

commit v5 on v4

--- a/solution.py
+++ b/solution.py
@@ -65,19 +65,24 @@
     return sums[:count] + (sums[count : 2 * count] + sums[2 * count :])
 
 
-def state_kernel(
-    k_ref, decay_ref, v_hbm, keep_ref, send_ref, local_ref, sums_ref, totals_ref, v_ref, held, arrived
-):
+def state_kernel(*refs):
+    q_hbm, k_hbm, v_hbm, decay_hbm, weight_hbm, gain_hbm = refs[:6]
+    keep_ref, send_ref, local_ref, sums_ref, totals_ref = refs[6:11]
+    q_ref, k_ref, v_ref, weight_ref, gain_ref, decay_ref, held, arrived = refs[11:]
     heads, tokens = decay_ref.shape
     head_width = v_ref.shape[1] // heads
     spans = tokens // SPAN
     rows_of = [slice(span * SPAN, (span + 1) * SPAN) for span in range(spans)]
+    loads = [(decay_hbm, decay_ref), (k_hbm, k_ref)]
+    loads += [(v_hbm.at[rows], v_ref.at[rows]) for rows in rows_of]
+    loads += [(q_hbm, q_ref), (weight_hbm, weight_ref), (gain_hbm, gain_ref)]
     copies = [
-        pltpu.make_async_copy(v_hbm.at[rows], v_ref.at[rows], arrived.at[span])
-        for span, rows in enumerate(rows_of)
+        pltpu.make_async_copy(source, target, arrived.at[at])
+        for at, (source, target) in enumerate(loads)
     ]
     for copy in copies:
         copy.start()
+    copies[0].wait()
     within = running_sums(jnp.concatenate([decay_ref[:, rows] for rows in rows_of], axis=0))
     run = jnp.zeros((heads, 128), jnp.float32)
     fades, wholes = [], []
@@ -91,8 +96,9 @@
         run = run + total
         fades.append(jnp.exp(spread_lanes(last, SPAN) - here))
         wholes.append(jnp.exp(total))
+    copies[1].wait()
     across = [k_ref[rows].astype(jnp.float32).T for rows in rows_of]
-    for copy in copies:
+    for copy in copies[2 : 2 + spans]:
         copy.wait()
     for head in range(heads):
         columns = slice(head * head_width, (head + 1) * head_width)
@@ -122,29 +128,36 @@
     send_ref[:half] = held[pl.ds((1 - core) * half, half)]
     keep_ref[half:] = run
     send_ref[half:] = run
-
-
-def make_states(keys, values, log_decay):
+    for copy in copies[2 + spans :]:
+        copy.wait()
+
+
+def make_states(queries, keys, values, log_decay, level_weight, gain):
     tokens, key_width = keys.shape
     heads = log_decay.shape[0]
     width = values.shape[1]
     spans = tokens // SPAN
     message = ((width // 2 + heads, key_width), jnp.float32)
-    plain = pl.BlockSpec()
+    inputs = [queries, keys, values, log_decay, level_weight, gain]
+    kept = [queries, keys, values, level_weight, gain]
     return call(
         state_kernel,
         "states",
-        [keys, log_decay, values],
+        [pltpu.with_memory_space_constraint(array, pltpu.HBM) for array in inputs],
         [
             message,
             message,
             ((spans - 1, key_width, width), jnp.bfloat16),
             ((2, heads, tokens), jnp.float32),
             ((spans, heads, 128), jnp.float32),
-            ((tokens, width), jnp.bfloat16),
+            *[(array.shape, array.dtype) for array in kept],
         ],
-        [pltpu.VMEM((width, key_width), jnp.float32), pltpu.SemaphoreType.DMA((spans,))],
-        [plain, plain, ANYWHERE],
+        [
+            pltpu.VMEM(log_decay.shape, jnp.float32),
+            pltpu.VMEM((width, key_width), jnp.float32),
+            pltpu.SemaphoreType.DMA((spans + 5,)),
+        ],
+        [pl.BlockSpec(memory_space=pltpu.HBM)] * len(inputs),
     )
 
 
@@ -227,81 +240,83 @@
     return jnp.where(upper, other * fade + mine, mine * fade + other)
 
 
-def fade_row(ref, state_rows, head):
-    return ref[pl.ds(state_rows + head, 1)]
-
-
-def chip_kernel(mine_ref, other_ref, stay_ref, give_ref, prefix_ref, chip_ref):
+def first_head(far, heads):
+    here = place()
+    first = 0
+    for bit, flip in enumerate(far):
+        first = first + jnp.bitwise_xor(bit_of(here, bit), flip) * (heads >> (bit + 1))
+    return first
+
+
+def merge_kernel(bit, near, split, *refs):
+    mine_ref, other_ref, prefix_ref = refs[:3]
+    whole_ref = refs[-1]
+    next_ref = refs[-2]
     heads = prefix_ref.shape[0]
-    half = chip_ref.shape[0]
-    held = heads // 2
-    per = half // held
-    here = place()
-    core = bit_of(here, 0)
-    upper = core == 1
-    for slot in range(held):
-        rows = slice(slot * per, (slot + 1) * per)
-        head = core * held + slot
-        chip_ref[rows] = join(
-            upper,
-            mine_ref[rows],
-            fade_row(mine_ref, half, head),
-            other_ref[rows],
-            fade_row(other_ref, half, head),
+    rows = mine_ref.shape[0] - heads
+    count = heads >> near
+    per = rows // count
+    upper = bit_of(place(), bit) == 1
+    first = first_head((0,) * near, heads)
+    for slot in range(count):
+        part = slice(slot * per, (slot + 1) * per)
+        total = pl.ds(rows + first + slot, 1)
+        whole_ref[part] = join(
+            upper, mine_ref[part], mine_ref[total], other_ref[part], other_ref[total]
         )
-    other_total = other_ref[half:]
-    total = mine_ref[half:] + other_total
-    prefix_ref[...] = jnp.where(upper, other_total, 0.0)
-    quarter = half // 2
-    side = bit_of(here, 1)
-    stay_ref[:quarter] = chip_ref[pl.ds(side * quarter, quarter)]
-    give_ref[:quarter] = chip_ref[pl.ds((1 - side) * quarter, quarter)]
-    stay_ref[quarter:] = total
-    give_ref[quarter:] = total
-
-
-def make_chip(mine, other, heads):
-    rows, lanes = mine.shape
-    half = rows - heads
-    message = ((half // 2 + heads, lanes), jnp.float32)
+    other_total = other_ref[rows:]
+    total = mine_ref[rows:] + other_total
+    next_ref[...] = prefix_ref[...] + jnp.where(upper, other_total, 0.0)
+    if split:
+        stay_ref, give_ref = refs[-4:-2]
+        half = rows // 2
+        side = bit_of(place(), bit + 1)
+        stay_ref[:half] = whole_ref[pl.ds(side * half, half)]
+        give_ref[:half] = whole_ref[pl.ds((1 - side) * half, half)]
+        stay_ref[half:] = total
+        give_ref[half:] = total
+    else:
+        merged_ref = refs[-3]
+        merged_ref[:rows] = whole_ref[...]
+        merged_ref[rows:] = total
+
+
+def merge(bit, mine, other, prefix, tokens=()):
+    heads, lanes = prefix.shape
+    group_bits = heads.bit_length() - 1
+    near = min(bit + 1, group_bits)
+    split = bit + 1 < group_bits
+    rows = mine.shape[0] - heads
+    if split:
+        messages = [((rows // 2 + heads, lanes), jnp.float32)] * 2
+    else:
+        messages = [(mine.shape, jnp.float32)]
     return call(
-        chip_kernel,
-        "chip",
-        [mine, other],
-        [message, message, ((heads, lanes), jnp.float32)],
-        [pltpu.VMEM((half, lanes), jnp.float32)],
-    )
-
-
-def merge_kernel(bit, mine_ref, other_ref, prefix_ref, token_ref, merged_ref, next_ref):
-    here = place()
-    upper = bit_of(here, bit) == 1
-    heads = next_ref.shape[0]
-    count = heads // 4
-    quarter = merged_ref.shape[0] - heads
-    per = quarter // count
-    for slot in range(count):
-        rows = slice(slot * per, (slot + 1) * per)
-        head = bit_of(here, 0) * (heads // 2) + bit_of(here, 1) * count + slot
-        merged_ref[rows] = join(
-            upper,
-            mine_ref[rows],
-            fade_row(mine_ref, quarter, head),
-            other_ref[rows],
-            fade_row(other_ref, quarter, head),
-        )
-    other_total = other_ref[quarter:]
-    merged_ref[quarter:] = mine_ref[quarter:] + other_total
-    next_ref[...] = prefix_ref[...] + jnp.where(upper, other_total, 0.0)
-
-
-def merge(bit, mine, other, prefix, token):
+        functools.partial(merge_kernel, bit, near, split),
+        f"merge{bit}",
+        [mine, other, prefix, *tokens],
+        [*messages, (prefix.shape, jnp.float32)],
+        [pltpu.VMEM((rows, lanes), jnp.float32)],
+    )
+
+
+def pack_kernel(takes, *refs):
+    out_ref = refs[-1]
+    at = 0
+    for ref, rows in zip(refs, takes):
+        out_ref[at : at + rows] = ref[:rows]
+        at += rows
+
+
+def pack(name, pieces, tokens=()):
+    takes = [rows for _, rows in pieces]
+    lanes = pieces[0][0].shape[1]
     return call(
-        functools.partial(merge_kernel, bit),
-        f"merge{bit}",
-        [mine, other, prefix, token],
-        [(mine.shape, jnp.float32), (prefix.shape, jnp.float32)],
-    )
+        functools.partial(pack_kernel, takes),
+        name,
+        [*[array for array, _ in pieces], *tokens],
+        [((sum(takes), lanes), jnp.float32)],
+    )[0]
 
 
 def level_scale(bit, first_level, prefix_ref, sums_ref, weight_ref, tokens):
@@ -311,17 +326,11 @@
 
 
 def take_levels(plan, part_refs, levels, heads):
-    here = place()
     per = levels.shape[1] // heads
     for slot, pieces in enumerate(plan):
-        for index, row, far_core, far_side, count in pieces:
-            core = jnp.bitwise_xor(bit_of(here, 0), far_core)
-            side = jnp.bitwise_xor(bit_of(here, 1), far_side)
-            head = core * (heads // 2)
-            if count < heads // 2:
-                head = head + side * count
-            rows = count * per
-            start = pl.multiple_of(head * per, 128)
+        for index, row, far in pieces:
+            rows = (heads >> len(far)) * per
+            start = pl.multiple_of(first_head(far, heads) * per, 128)
             levels[slot, pl.ds(start, rows)] = part_refs[index][row : row + rows].astype(
                 jnp.bfloat16
             )
@@ -367,51 +376,72 @@
     )[0]
 
 
-def finish_kernel(pieces, bit, first_level, *refs):
-    mixed_ref, q_ref, sums_ref, weight_ref, gain_ref, prefix_ref = refs[:6]
-    part_refs = refs[6:-4]
-    out_hbm, levels, out_ref, sent = refs[-4:]
+def finish_kernel(far, bit, first_level, *refs):
+    mixed_ref, q_ref, sums_ref, weight_ref, gain_ref, prefix_ref, state_ref = refs[:7]
+    out_hbm, out_ref, level, scale_ref, sent = refs[-5:]
     heads = weight_ref.shape[1]
     head_width = mixed_ref.shape[0] // heads
-    take_levels([pieces], part_refs, levels, heads)
-    gain_down = gain_ref[...].T
+    half = heads // 2
+    first = first_head((far,), heads)
+    flips = half.bit_length() - 1
+    for slot in range(half):
+        beyond = tuple(slot >> (flips - 1 - bit) & 1 for bit in range(flips))
+        start = pl.multiple_of((first_head((far, *beyond), heads) - first) * head_width, 128)
+        rows = slice(slot * head_width, (slot + 1) * head_width)
+        level[pl.ds(start, head_width)] = state_ref[rows].astype(jnp.bfloat16)
+    gains = []
+    for slot in range(half):
+        row = jnp.broadcast_to(gain_ref[pl.ds(first + slot, 1)], (8, head_width))
+        gains.append(row.T[:, :1])
+    columns = pl.ds(pl.multiple_of(first * head_width, 128), half * head_width)
     copies = []
     for span in range(q_ref.shape[0] // SPAN):
         tokens = slice(span * SPAN, (span + 1) * SPAN)
         queries = q_ref[tokens]
-        scale = level_scale(bit, first_level, prefix_ref, sums_ref, weight_ref, tokens)
-        for head in range(heads):
-            rows = slice(head * head_width, (head + 1) * head_width)
-            found = lax.dot_general(
-                levels[0, rows], queries, NT, preferred_element_type=jnp.float32
-            )
-            mixed = mixed_ref[rows, tokens] + found * scale[head : head + 1]
+        scale_ref[...] = level_scale(bit, first_level, prefix_ref, sums_ref, weight_ref, tokens)
+        for slot in range(half):
+            rows = slice(slot * head_width, (slot + 1) * head_width)
+            found = lax.dot_general(level[rows], queries, NT, preferred_element_type=jnp.float32)
+            start = pl.multiple_of((first + slot) * head_width, 128)
+            mixed = mixed_ref[pl.ds(start, head_width), tokens]
+            mixed = mixed + found * scale_ref[pl.ds(first + slot, 1)]
             square = jnp.mean(mixed * mixed, axis=0, keepdims=True)
-            normed = mixed * lax.rsqrt(square + EPS) * gain_down[:, head : head + 1]
+            normed = mixed * lax.rsqrt(square + EPS) * gains[slot]
             out_ref[tokens, rows] = normed.astype(jnp.bfloat16).T
-        copy = pltpu.make_async_copy(out_ref.at[tokens], out_hbm.at[tokens], sent.at[span])
+        copy = pltpu.make_async_copy(
+            out_ref.at[tokens], out_hbm.at[tokens, columns], sent.at[span]
+        )
         copy.start()
         copies.append(copy)
     for copy in copies:
         copy.wait()
 
 
-def finish(mixed, queries, sums, level_weight, gain, prefix, pieces, bit, parts, first_level):
+def finish(far, bit, first_level, mixed, queries, sums, level_weight, gain, prefix, state, begun):
     width, tokens = mixed.shape
-    inputs = [mixed, queries, sums, level_weight, gain, prefix, *parts]
+    heads = level_weight.shape[1]
+    inputs = [mixed, queries, sums, level_weight, gain, prefix, state]
+    specs = [HELD] * len(inputs)
+    inputs = [hold(array) for array in inputs]
+    out = pl.BlockSpec(memory_space=pltpu.HBM)
+    if begun is not None:
+        specs.append(out)
+        inputs.append(begun)
     return pl.pallas_call(
-        functools.partial(finish_kernel, pieces, bit, first_level),
-        in_specs=[HELD] * len(inputs),
-        out_specs=ANYWHERE,
+        functools.partial(finish_kernel, far, bit, first_level),
+        in_specs=specs,
+        out_specs=out,
         out_shape=jax.ShapeDtypeStruct((tokens, width), jnp.bfloat16),
         scratch_shapes=[
-            pltpu.VMEM((1, width, queries.shape[1]), jnp.bfloat16),
-            pltpu.VMEM((tokens, width), jnp.bfloat16),
+            pltpu.VMEM((tokens, width // 2), jnp.bfloat16),
+            pltpu.VMEM(state.shape, jnp.bfloat16),
+            pltpu.VMEM((heads, SPAN), jnp.float32),
             pltpu.SemaphoreType.DMA((tokens // SPAN,)),
         ],
+        input_output_aliases={} if begun is None else {7: 0},
         compiler_params=PARAMS,
-        name="finish",
-    )(*[hold(array) for array in inputs])
+        name=f"finish{far}",
+    )(*inputs)
 
 
 def trade(value, mask, senders=lambda source: True):
@@ -431,61 +461,74 @@
 def per_device(queries, keys, values, log_decay, level_weight, norm_gain):
     heads = log_decay.shape[0]
     tokens, width = values.shape
+    per = width // heads
     spans = tokens // SPAN
-    half, quarter = width // 2, width // 4
+    group_bits = heads.bit_length() - 1
     bits = (lax.axis_size("wide") * lax.axis_size("narrow")).bit_length() - 1
     first_level = level_weight.shape[0] - bits
-    keep, send, local, sums, totals, held_values = make_states(keys, values, log_decay)
-    shared = (queries, keys, held_values, sums, totals, level_weight, local)
-    near = trade(send, 1)
-    stay, give, prefix = make_chip(keep, near, heads)
-    got = trade(give, 2)
-    near_rest = trade(keep, 1, lambda source: source & 1 == 0)
-    got_rest = trade(stay, 2, lambda source: source & 2 == 0)
-    prefixes = [jnp.zeros((heads, 128), jnp.float32), prefix]
-    mixed, at = None, 0
-    found = [got]
-    for bit in range(1, bits):
-        if bit > 1:
-            found.append(trade(group, 2**bit))
-        mine = group if bit > 1 else stay
-        if at < spans and bit < bits - 1:
-            mixed, token = mix_local(at, at + 1, shared, mixed)
-            at += 1
-        if bit < bits - 1:
-            group, prefix = merge(bit, mine, found[-1], prefixes[-1], token)
-            prefixes.append(prefix)
-    if at < spans:
-        mixed, token = mix_local(at, spans, shared, mixed)
-    middle = jnp.concatenate([state[:quarter] for state in found[1:-1]], axis=0)
-    middle_far = trade(middle, 2)
-    packed = jnp.concatenate([got[:quarter], got_rest[:quarter], middle, middle_far], axis=0)
-    packed_far = trade(packed, 1)
-    last = found[-1]
-    last_side = trade(last, 2)
-    last_parts = [last, last_side, trade(last, 1), trade(last_side, 1)]
-    two = heads // 4
-    levels = [(0, prefixes[0], [(0, 0, 0, 0, 2 * two), (1, 0, 1, 0, 2 * two)])]
+    gain = norm_gain.reshape(heads, per)
+    mine, give, local, sums, totals, queries, keys, values, level_weight, gain = make_states(
+        queries, keys, values, log_decay, level_weight, gain
+    )
+    shared = (queries, keys, values, sums, totals, level_weight, local)
+
+    prefix = jnp.zeros((heads, 128), jnp.float32)
+    prefixes, found, rests = [], [], []
+    mixed, at, tokens_done = None, 0, ()
+    for bit in range(bits):
+        lower = lambda source, bit=bit: (source >> bit) & 1 == 0
+        sent = give if bit < group_bits else mine
+        both = bit < bits - 1
+        found.append(trade(sent, 2**bit) if both else trade(sent, 2**bit, lower))
+        prefixes.append(prefix)
+        if bit < group_bits:
+            rests.append(trade(mine, 2**bit, lower))
+        if 0 < bit and at < spans:
+            stop = spans if bit == bits - 2 else at + 1
+            mixed, token = mix_local(at, stop, shared, mixed)
+            at, tokens_done = stop, (token,)
+        if both:
+            *messages, prefix = merge(bit, mine, found[bit], prefix, tokens_done)
+            mine, give = messages if len(messages) == 2 else (messages[0], None)
+    after = (mine,)
+
+    early = range(group_bits, bits - 1)
+    ahead = pack("ahead", [(found[bit], per) for bit in early], after)
+    beside = trade(ahead, 4)
+    pieces = [(found[2], per), (rests[2], per)]
+    for slot, bit in enumerate(early):
+        pieces += [(ahead[slot * per : (slot + 1) * per], per), (beside[slot * per : (slot + 1) * per], per)]
+    quarter = pack("quarter", pieces)
+    across = trade(quarter, 2)
+    step = quarter.shape[0]
+    near = pack(
+        "near", [(found[1], 2 * per), (rests[1], 2 * per), (quarter, step), (across, step)]
+    )
+    far = trade(near, 1)
+    levels = [(0, prefixes[0], [(0, 0, (0,)), (1, 0, (1,))])]
     levels.append(
-        (1, prefixes[1], [(2 + far, side * quarter, far, side, two) for far in (0, 1) for side in (0, 1)])
-    )
-    for bit in range(2, bits - 1):
-        row = half + (bit - 2) * quarter
-        step = (bits - 3) * quarter
-        levels.append(
-            (
-                bit,
-                prefixes[bit],
-                [(2 + far, row + side * step, far, side, two) for far in (0, 1) for side in (0, 1)],
-            )
-        )
-    parts = [near, near_rest, packed, packed_far]
+        (1, prefixes[1], [(2 + core, side * 2 * per, (core, side)) for core in (0, 1) for side in (0, 1)])
+    )
+    for slot, bit in enumerate(range(2, bits - 1)):
+        row = 4 * per + slot * 2 * per
+        taken = [
+            (2 + core, row + side * step + last * per, (core, side, last))
+            for core in (0, 1)
+            for side in (0, 1)
+            for last in (0, 1)
+        ]
+        levels.append((bit, prefixes[bit], taken))
+    parts = [found[0], rests[0], near, far]
     mixed = add_levels(mixed, queries, sums, level_weight, levels, parts, first_level)
-    gain = norm_gain.reshape(heads, width // heads)
-    pieces = [(0, 0, 0, 0, two), (1, 0, 0, 1, two), (2, 0, 1, 0, two), (3, 0, 1, 1, two)]
-    return finish(
-        mixed, queries, sums, level_weight, gain, prefixes[bits - 1], pieces, bits - 1, last_parts, first_level
-    )
+
+    last = bits - 1
+    needed = lambda source: (source >> last) & 1 == 1
+    state = pack("last1", [(found[last], per), (trade(found[last], 4, needed), per)])
+    state = pack("last2", [(state, 2 * per), (trade(state, 2, needed), 2 * per)])
+    other = trade(state, 1, needed)
+    rest = (mixed, queries, sums, level_weight, gain, prefixes[last])
+    begun = finish(0, last, first_level, *rest, state, None)
+    return finish(1, last, first_level, *rest, other, begun)
 
 
 def solution(mesh):

time: 56.8 us -> 63.8 us (1.12)
  the two profiles are of different devices: /device:TPU:0 before, /device:TPU:29 now
where the time goes in v5:
time: 63.8 us; the launch traced here: 63.6 us
  starting transfers between devices  26.9 us (42%)
  waiting for transfers between devices  23.7 us (37%)
  Pallas kernels  12.7 us (20%)
    ppermute x14, starting transfers between devices, trade(): return lax.ppermute(value, AXES, pairs)  26.9 us
    ppermute x14, waiting for transfers between devices, trade(): return lax.ppermute(value, AXES, pairs)  23.7 us
    pallas_call x14, Pallas kernels, call(): pl.pallas_call(kernel, in_specs=specs, out_specs=[HELD] * len(outputs), o...  8.93 us
    pallas_call x2, Pallas kernels, finish(): pl.pallas_call(functools.partial(finish_kernel, far, bit, first_level), i...  3.79 us
  transfers between devices with their start and end apart: 14, of which 8 were waited for; matrix products, arithmetic and copies ran while one was open for 0% of the time, Pallas kernels for 12%

profile of v5, /device:TPU:29, one launch (start us, length us, event | category | flops | bytes accessed | tf_op | source)
XLA Modules:
  0.0 63.6 jit_solution(1957104086806702230)
XLA Ops:
  0.0 2.8 %states.1 = (f32[520,128]{1,0:T(8,128)S(1)}, f32[520,128]{1,0:T(8,128)S(1)}, bf16[3,128,1024]{2,1,0:T(8,128)(2,1)S(1)}, f32[2,8,1024]{2,1,0:T(8,128)S(1)}, f32[4...) custom-call(bf16[1024,128]{1,0:T(8,128)(2,1)} %refs_0_.1, ...), custom_call_target="tpu_custom_call" | custom-call | tf_op jit(solution)/shard_map/states/pallas_call | solution.py:40
  3.5 1.2 %collective-permute-done.refs_1_.refs_8_ = f32[520,128]{1,0:T(8,128)S(1)} collective-permute-done((f32[520,128]{1,0:T(8,128)S(1)}, f32[520,128]{1,0:T(8,128)S(1)}, u32[]{:S(2)}, u32[]{:S(2)}) %collective-permute-start) | collective-permute-done | bytes 266272 | tf_op jit(solution)/shard_map/ppermute | solution.py:458
  5.1 0.8 %local0.1 = (f32[1024,1024]{1,0:T(8,128)S(1)}, f32[8,128]{1,0:T(8,128)S(1)}) custom-call(bf16[1024,128]{1,0:T(8,128)(2,1)S(1)} %get-tuple-element.31.refs_0_.refs_1_, bf16[1024,128]{1,0:T(8,128)(2,1)S(1)} %get-tuple-element.32.refs_1_, bf16[1024,1024]{1,0:T(8,128)(2,1)S(1)} %get-tuple-element.33.refs_2_, ...), custom_call_target="tpu_custom_call" | custom-call | tf_op jit(solution)/shard_map/local0/pallas_call | solution.py:40
  5.9 3.8 %collective-permute-done.1.refs_1_.refs_0_ = f32[264,128]{1,0:T(8,128)S(1)} collective-permute-done((f32[264,128]{1,0:T(8,128)S(1)}, f32[264,128]{1,0:T(8,128)S(1)}, u32[]{:S(2)}, u32[]{:S(2)}) %collective-permute-start.1) | collective-permute-done | bytes 135200 | tf_op jit(solution)/shard_map/ppermute | solution.py:458
  9.7 1.3 %collective-permute-start.2 = (f32[136,128]{1,0:T(8,128)S(1)}, f32[136,128]{1,0:T(8,128)S(1)}, u32[]{:S(2)}, u32[]{:S(2)}) collective-permute-start(f32[136,128]{1,0:T(8,128)S(1)} %get-tuple-element.49), channel_id=1, source_target_pairs={{0,1},{8,9},{16,17},{24,25},{1,0},{9,8},{17,16},{25,24},{2,3},{10,... | collective-permute-start | bytes 208904 | tf_op jit(solution)/shard_map/ppermute | solution.py:458
  11.0 0.9 %local1.1 = (f32[1024,1024]{1,0:T(8,128)S(1)}, f32[8,128]{1,0:T(8,128)S(1)}) custom-call(bf16[1024,128]{1,0:T(8,128)(2,1)S(1)} %get-tuple-element.31.refs_0_.refs_1_, bf16[1024,128]{1,0:T(8,128)(2,1)S(1)} %get-tuple-element.32.refs_1_, bf16[1024,1024]{1,0:T(8,128)(2,1)S(1)} %get-tuple-element.33.refs_2_, ...), custom_call_target="tpu_custom_call", output_to_operand_aliasing={{0}: (7, {})} | custom-call | tf_op jit(solution)/shard_map/local1/pallas_call | solution.py:40
  11.8 1.1 %collective-permute-done.2.refs_1_.refs_0_ = f32[136,128]{1,0:T(8,128)S(1)} collective-permute-done((f32[136,128]{1,0:T(8,128)S(1)}, f32[136,128]{1,0:T(8,128)S(1)}, u32[]{:S(2)}, u32[]{:S(2)}) %collective-permute-start.2) | collective-permute-done | bytes 69664 | tf_op jit(solution)/shard_map/ppermute | solution.py:458
  13.2 3.1 %collective-permute-start.5 = (f32[136,128]{1,0:T(8,128)S(1)}, f32[136,128]{1,0:T(8,128)S(1)}, u32[]{:S(2)}, u32[]{:S(2)}) collective-permute-start(f32[136,128]{1,0:T(8,128)S(1)} %get-tuple-element.48.refs_0_), channel_id=1, source_target_pairs={{0,1},{8,9},{16,17},{24,25},{2,3},{10,11},{18,19},{26,27},{4,5},{1... | collective-permute-start | bytes 208904 | tf_op jit(solution)/shard_map/ppermute | solution.py:458
  16.3 1.7 %local2.1 = (f32[1024,1024]{1,0:T(8,128)S(1)}, f32[8,128]{1,0:T(8,128)S(1)}) custom-call(bf16[1024,128]{1,0:T(8,128)(2,1)S(1)} %get-tuple-element.31.refs_0_.refs_1_, bf16[1024,128]{1,0:T(8,128)(2,1)S(1)} %get-tuple-element.32.refs_1_, bf16[1024,1024]{1,0:T(8,128)(2,1)S(1)} %get-tuple-element.33.refs_2_, ...), custom_call_target="tpu_custom_call", output_to_operand_aliasing={{0}: (7, {})} | custom-call | tf_op jit(solution)/shard_map/local2/pallas_call | solution.py:40
  18.1 3.1 %collective-permute-done.7.refs_3_ = f32[128,128]{1,0:T(8,128)S(1)} collective-permute-done((f32[128,128]{1,0:T(8,128)S(1)}, f32[128,128]{1,0:T(8,128)S(1)}, u32[]{:S(2)}, u32[]{:S(2)}) %collective-permute-start.7) | collective-permute-done | bytes 65568 | tf_op jit(solution)/shard_map/ppermute | solution.py:458
  21.5 1.3 %collective-permute-start.4 = (f32[264,128]{1,0:T(8,128)S(1)}, f32[264,128]{1,0:T(8,128)S(1)}, u32[]{:S(2)}, u32[]{:S(2)}) collective-permute-start(f32[264,128]{1,0:T(8,128)S(1)} %get-tuple-element.44.refs_0_), channel_id=1, source_target_pairs={{0,16},{8,24},{1,17},{9,25},{2,18},{10,26},{3,19},{11,27},{4,20},{... | collective-permute-start | bytes 405512 | tf_op jit(solution)/shard_map/ppermute | solution.py:458
  22.8 5.2 %collective-permute-done.4.refs_1_ = f32[264,128]{1,0:T(8,128)S(1)} collective-permute-done((f32[264,128]{1,0:T(8,128)S(1)}, f32[264,128]{1,0:T(8,128)S(1)}, u32[]{:S(2)}, u32[]{:S(2)}) %collective-permute-start.4) | collective-permute-done | bytes 135200 | tf_op jit(solution)/shard_map/ppermute | solution.py:458
  28.0 5.3 %collective-permute-start.9 = (f32[1536,128]{1,0:T(8,128)S(1)}, f32[1536,128]{1,0:T(8,128)S(1)}, u32[]{:S(2)}, u32[]{:S(2)}) collective-permute-start(f32[1536,128]{1,0:T(8,128)S(1)} %near.1.refs_10_), channel_id=1, source_target_pairs={{0,8},{8,0},{16,24},{24,16},{1,9},{9,1},{17,25},{25,17},{2,10},{10... | collective-permute-start | bytes 2359304 | tf_op jit(solution)/shard_map/ppermute | solution.py:458
  33.3 1.3 %collective-permute-start.10 = (f32[136,128]{1,0:T(8,128)S(1)}, f32[136,128]{1,0:T(8,128)S(1)}, u32[]{:S(2)}, u32[]{:S(2)}) collective-permute-start(f32[136,128]{1,0:T(8,128)S(1)} %get-tuple-element.54.refs_1_), channel_id=1, source_target_pairs={{0,4},{8,12},{16,20},{24,28},{1,5},{9,13},{17,21},{25,29},{2,6},{1... | collective-permute-start | bytes 208904 | tf_op jit(solution)/shard_map/ppermute | solution.py:458
  34.6 5.3 %collective-permute-done.10.refs_0_ = f32[136,128]{1,0:T(8,128)S(1)} collective-permute-done((f32[136,128]{1,0:T(8,128)S(1)}, f32[136,128]{1,0:T(8,128)S(1)}, u32[]{:S(2)}, u32[]{:S(2)}) %collective-permute-start.10) | collective-permute-done | bytes 69664 | tf_op jit(solution)/shard_map/ppermute | solution.py:458
  39.9 3.4 %collective-permute-start.11 = (f32[136,128]{1,0:T(8,128)S(1)}, f32[136,128]{1,0:T(8,128)S(1)}, u32[]{:S(2)}, u32[]{:S(2)}) collective-permute-start(f32[136,128]{1,0:T(8,128)S(1)} %collective-permute-done.10.refs_0_), channel_id=1, source_target_pairs={{4,5},{12,13},{20,21},{28,29},{5,4},{13,12},{21,20},{29,28},{6,7},... | collective-permute-start | bytes 208904 | tf_op jit(solution)/shard_map/ppermute | solution.py:458
  43.3 1.7 %collective-permute-done.11.refs_1_ = f32[136,128]{1,0:T(8,128)S(1)} collective-permute-done((f32[136,128]{1,0:T(8,128)S(1)}, f32[136,128]{1,0:T(8,128)S(1)}, u32[]{:S(2)}, u32[]{:S(2)}) %collective-permute-start.11) | collective-permute-done | bytes 69664 | tf_op jit(solution)/shard_map/ppermute | solution.py:458
  45.0 1.9 %collective-permute-start.12 = (f32[256,128]{1,0:T(8,128)S(1)}, f32[256,128]{1,0:T(8,128)S(1)}, u32[]{:S(2)}, u32[]{:S(2)}) collective-permute-start(f32[256,128]{1,0:T(8,128)S(1)} %last1.1.refs_0_), channel_id=1, source_target_pairs={{4,20},{12,28},{20,4},{28,12},{5,21},{13,29},{21,5},{29,13},{6,22}... | collective-permute-start | bytes 393224 | tf_op jit(solution)/shard_map/ppermute | solution.py:458
  46.9 1.3 %collective-permute-start.3 = (f32[520,128]{1,0:T(8,128)S(1)}, f32[520,128]{1,0:T(8,128)S(1)}, u32[]{:S(2)}, u32[]{:S(2)}) collective-permute-start(f32[520,128]{1,0:T(8,128)S(1)} %get-tuple-element.41.refs_0_), channel_id=1, source_target_pairs={{0,8},{16,24},{1,9},{17,25},{2,10},{18,26},{3,11},{19,27},{4,12},{... | collective-permute-start | bytes 798728 | tf_op jit(solution)/shard_map/ppermute | solution.py:458
  48.2 2.5 %collective-permute-done.12.refs_1_ = f32[256,128]{1,0:T(8,128)S(1)} collective-permute-done((f32[256,128]{1,0:T(8,128)S(1)}, f32[256,128]{1,0:T(8,128)S(1)}, u32[]{:S(2)}, u32[]{:S(2)}) %collective-permute-start.12) | collective-permute-done | bytes 131104 | tf_op jit(solution)/shard_map/ppermute | solution.py:458
  50.7 6.5 %collective-permute-start.13 = (f32[512,128]{1,0:T(8,128)S(1)}, f32[512,128]{1,0:T(8,128)S(1)}, u32[]{:S(2)}, u32[]{:S(2)}) collective-permute-start(f32[512,128]{1,0:T(8,128)S(1)} %last2.1.refs_6_), channel_id=1, source_target_pairs={{4,12},{12,4},{20,28},{28,20},{5,13},{13,5},{21,29},{29,21},{6,14}... | collective-permute-start | bytes 786440 | tf_op jit(solution)/shard_map/ppermute | solution.py:458
  57.2 2.5 %reach.1.refs_0_ = f32[1024,1024]{1,0:T(8,128)S(1)} custom-call(f32[1024,1024]{1,0:T(8,128)S(1)} %get-tuple-element.40.refs_0_, bf16[1024,128]{1,0:T(8,128)(2,1)S(1)} %get-tuple-element.31.refs_0_.refs_1_, f32[2,8,1024]{2,1,0:T(8,128)S(1)} %get-tuple-element.34.refs_3_.refs_2_, ...), custom_call_target="tpu_custom_call", output_to_operand_aliasing={{}: (0, {})} | custom-call | tf_op jit(solution)/shard_map/reach/pallas_call | solution.py:40
  59.8 1.9 %finish0.1.refs_7_ = bf16[1024,1024]{1,0:T(8,128)(2,1)} custom-call(f32[1024,1024]{1,0:T(8,128)S(1)} %reach.1.refs_0_, bf16[1024,128]{1,0:T(8,128)(2,1)S(1)} %get-tuple-element.31.refs_0_.refs_1_, f32[2,8,1024]{2,1,0:T(8,128)S(1)} %get-tuple-element.34.refs_3_.refs_2_, f32[8,8,1024]{2,1,0:T(8,128)S(1)} %get-tuple-element.36.refs_5_.refs_3_, ...), custom_call_target="tpu_custom_call" | custom-call | tf_op jit(solution)/shard_map/finish0/pallas_call | solution.py:430
  61.7 1.9 %finish1.1 = bf16[1024,1024]{1,0:T(8,128)(2,1)} custom-call(f32[1024,1024]{1,0:T(8,128)S(1)} %reach.1.refs_0_, bf16[1024,128]{1,0:T(8,128)(2,1)S(1)} %get-tuple-element.31.refs_0_.refs_1_, f32[2,8,1024]{2,1,0:T(8,128)S(1)} %get-tuple-element.34.refs_3_.refs_2_, f32[8,8,1024]{2,1,0:T(8,128)S(1)} %get-tuple-element.36.refs_5_.refs_3_, ...), custom_call_target="tpu_custom_call", output_to_operand_aliasing={{}: (7, {})} | custom-call | tf_op jit(solution)/shard_map/finish1/pallas_call | solution.py:430
  (21 shorter events, 1.9 us)
Async XLA Ops:
  2.8 1.9 %collective-permute-start = (f32[520,128]{1,0:T(8,128)S(1)}, f32[520,128]{1,0:T(8,128)S(1)}, u32[]{:S(2)}, u32[]{:S(2)}) collective-permute-start(f32[520,128]{1,0:T(8,128)S(1)} %get-tuple-element.42), channel_id=1, source_target_pairs={{0,8},{8,0},{16,24},{24,16},{1,9},{9,1},{17,25},{25,17},{2,10},{10... | collective-permute-start | bytes 798728 | tf_op jit(solution)/shard_map/ppermute | solution.py:458
  4.8 4.9 %collective-permute-start.1 = (f32[264,128]{1,0:T(8,128)S(1)}, f32[264,128]{1,0:T(8,128)S(1)}, u32[]{:S(2)}, u32[]{:S(2)}) collective-permute-start(f32[264,128]{1,0:T(8,128)S(1)} %get-tuple-element.45), channel_id=1, source_target_pairs={{0,16},{8,24},{16,0},{24,8},{1,17},{9,25},{17,1},{25,9},{2,18},{10... | collective-permute-start | bytes 405512 | tf_op jit(solution)/shard_map/ppermute | solution.py:458
  9.7 3.2 %collective-permute-start.2 = (f32[136,128]{1,0:T(8,128)S(1)}, f32[136,128]{1,0:T(8,128)S(1)}, u32[]{:S(2)}, u32[]{:S(2)}) collective-permute-start(f32[136,128]{1,0:T(8,128)S(1)} %get-tuple-element.49), channel_id=1, source_target_pairs={{0,1},{8,9},{16,17},{24,25},{1,0},{9,8},{17,16},{25,24},{2,3},{10,... | collective-permute-start | bytes 208904 | tf_op jit(solution)/shard_map/ppermute | solution.py:458
  12.9 5.0 %collective-permute-start.6 = (f32[136,128]{1,0:T(8,128)S(1)}, f32[136,128]{1,0:T(8,128)S(1)}, u32[]{:S(2)}, u32[]{:S(2)}) collective-permute-start(f32[136,128]{1,0:T(8,128)S(1)} %get-tuple-element.52.refs_0_), channel_id=1, source_target_pairs={{0,2},{8,10},{16,18},{24,26},{1,3},{9,11},{17,19},{25,27},{2,0},{1... | collective-permute-start | bytes 208904 | tf_op jit(solution)/shard_map/ppermute | solution.py:458
  13.2 4.9 %collective-permute-start.5 = (f32[136,128]{1,0:T(8,128)S(1)}, f32[136,128]{1,0:T(8,128)S(1)}, u32[]{:S(2)}, u32[]{:S(2)}) collective-permute-start(f32[136,128]{1,0:T(8,128)S(1)} %get-tuple-element.48.refs_0_), channel_id=1, source_target_pairs={{0,1},{8,9},{16,17},{24,25},{2,3},{10,11},{18,19},{26,27},{4,5},{1... | collective-permute-start | bytes 208904 | tf_op jit(solution)/shard_map/ppermute | solution.py:458
  18.0 3.2 %collective-permute-start.7 = (f32[128,128]{1,0:T(8,128)S(1)}, f32[128,128]{1,0:T(8,128)S(1)}, u32[]{:S(2)}, u32[]{:S(2)}) collective-permute-start(f32[128,128]{1,0:T(8,128)S(1)} %ahead.1.refs_2_), channel_id=1, source_target_pairs={{0,1},{8,9},{16,17},{24,25},{1,0},{9,8},{17,16},{25,24},{2,3},{10,... | collective-permute-start | bytes 196616 | tf_op jit(solution)/shard_map/ppermute | solution.py:458
  21.2 6.7 %collective-permute-start.8 = (f32[512,128]{1,0:T(8,128)S(1)}, f32[512,128]{1,0:T(8,128)S(1)}, u32[]{:S(2)}, u32[]{:S(2)}) collective-permute-start(f32[512,128]{1,0:T(8,128)S(1)} %quarter.1.refs_2_), channel_id=1, source_target_pairs={{0,16},{8,24},{16,0},{24,8},{1,17},{9,25},{17,1},{25,9},{2,18},{10... | collective-permute-start | bytes 786440 | tf_op jit(solution)/shard_map/ppermute | solution.py:458
  21.5 6.4 %collective-permute-start.4 = (f32[264,128]{1,0:T(8,128)S(1)}, f32[264,128]{1,0:T(8,128)S(1)}, u32[]{:S(2)}, u32[]{:S(2)}) collective-permute-start(f32[264,128]{1,0:T(8,128)S(1)} %get-tuple-element.44.refs_0_), channel_id=1, source_target_pairs={{0,16},{8,24},{1,17},{9,25},{2,18},{10,26},{3,19},{11,27},{4,20},{... | collective-permute-start | bytes 405512 | tf_op jit(solution)/shard_map/ppermute | solution.py:458
  28.0 29.2 %collective-permute-start.9 = (f32[1536,128]{1,0:T(8,128)S(1)}, f32[1536,128]{1,0:T(8,128)S(1)}, u32[]{:S(2)}, u32[]{:S(2)}) collective-permute-start(f32[1536,128]{1,0:T(8,128)S(1)} %near.1.refs_10_), channel_id=1, source_target_pairs={{0,8},{8,0},{16,24},{24,16},{1,9},{9,1},{17,25},{25,17},{2,10},{10... | collective-permute-start | bytes 2359304 | tf_op jit(solution)/shard_map/ppermute | solution.py:458
  33.3 6.6 %collective-permute-start.10 = (f32[136,128]{1,0:T(8,128)S(1)}, f32[136,128]{1,0:T(8,128)S(1)}, u32[]{:S(2)}, u32[]{:S(2)}) collective-permute-start(f32[136,128]{1,0:T(8,128)S(1)} %get-tuple-element.54.refs_1_), channel_id=1, source_target_pairs={{0,4},{8,12},{16,20},{24,28},{1,5},{9,13},{17,21},{25,29},{2,6},{1... | collective-permute-start | bytes 208904 | tf_op jit(solution)/shard_map/ppermute | solution.py:458
  39.9 5.1 %collective-permute-start.11 = (f32[136,128]{1,0:T(8,128)S(1)}, f32[136,128]{1,0:T(8,128)S(1)}, u32[]{:S(2)}, u32[]{:S(2)}) collective-permute-start(f32[136,128]{1,0:T(8,128)S(1)} %collective-permute-done.10.refs_0_), channel_id=1, source_target_pairs={{4,5},{12,13},{20,21},{28,29},{5,4},{13,12},{21,20},{29,28},{6,7},... | collective-permute-start | bytes 208904 | tf_op jit(solution)/shard_map/ppermute | solution.py:458
  45.0 5.7 %collective-permute-start.12 = (f32[256,128]{1,0:T(8,128)S(1)}, f32[256,128]{1,0:T(8,128)S(1)}, u32[]{:S(2)}, u32[]{:S(2)}) collective-permute-start(f32[256,128]{1,0:T(8,128)S(1)} %last1.1.refs_0_), channel_id=1, source_target_pairs={{4,20},{12,28},{20,4},{28,12},{5,21},{13,29},{21,5},{29,13},{6,22}... | collective-permute-start | bytes 393224 | tf_op jit(solution)/shard_map/ppermute | solution.py:458
  46.9 10.3 %collective-permute-start.3 = (f32[520,128]{1,0:T(8,128)S(1)}, f32[520,128]{1,0:T(8,128)S(1)}, u32[]{:S(2)}, u32[]{:S(2)}) collective-permute-start(f32[520,128]{1,0:T(8,128)S(1)} %get-tuple-element.41.refs_0_), channel_id=1, source_target_pairs={{0,8},{16,24},{1,9},{17,25},{2,10},{18,26},{3,11},{19,27},{4,12},{... | collective-permute-start | bytes 798728 | tf_op jit(solution)/shard_map/ppermute | solution.py:458
  50.7 11.0 %collective-permute-start.13 = (f32[512,128]{1,0:T(8,128)S(1)}, f32[512,128]{1,0:T(8,128)S(1)}, u32[]{:S(2)}, u32[]{:S(2)}) collective-permute-start(f32[512,128]{1,0:T(8,128)S(1)} %last2.1.refs_6_), channel_id=1, source_target_pairs={{4,12},{12,4},{20,28},{28,20},{5,13},{13,5},{21,29},{29,21},{6,14}... | collective-permute-start | bytes 786440 | tf_op jit(solution)/shard_map/ppermute | solution.py:458

commit v6 on v5

--- a/solution.py
+++ b/solution.py
@@ -8,6 +8,7 @@
 from jax.sharding import PartitionSpec as P
 
 SPAN = 256
+SPLIT_BITS = 2
 EPS = 1e-05
 AXES = ("narrow", "wide")
 NT = (((1,), (1,)), ((), ()))
@@ -223,13 +224,13 @@
             mixed_ref[rows, tokens] = mixed
 
 
-def mix_local(first, last, shared, mixed):
+def mix_local(first, last, shared, mixed, tokens=()):
     queries, keys, values, sums, totals, level_weight, local = shared
     rest = [] if mixed is None else [mixed]
     return call(
         functools.partial(local_kernel, first, last),
         f"local{first}",
-        [*shared, *rest],
+        [*shared, *rest, *tokens],
         [(values.shape[::-1], jnp.float32), ((8, 128), jnp.float32)],
         aliases={7: 0} if rest else None,
     )
@@ -283,9 +284,8 @@
 
 def merge(bit, mine, other, prefix, tokens=()):
     heads, lanes = prefix.shape
-    group_bits = heads.bit_length() - 1
-    near = min(bit + 1, group_bits)
-    split = bit + 1 < group_bits
+    near = min(bit + 1, SPLIT_BITS)
+    split = bit + 1 < SPLIT_BITS
     rows = mine.shape[0] - heads
     if split:
         messages = [((rows // 2 + heads, lanes), jnp.float32)] * 2
@@ -339,8 +339,9 @@
 def reach_kernel(plan, bits, first_level, *refs):
     mixed_ref, q_ref, sums_ref, weight_ref = refs[:4]
     prefix_refs = refs[4 : 4 + len(bits)]
-    part_refs = refs[4 + len(bits) : -2]
-    out_ref, levels = refs[-2:]
+    part_refs = refs[4 + len(bits) : -3]
+    out_ref, done_ref, levels = refs[-3:]
+    done_ref[...] = jnp.zeros_like(done_ref)
     heads = weight_ref.shape[1]
     head_width = mixed_ref.shape[0] // heads
     take_levels(plan, part_refs, levels, heads)
@@ -362,18 +363,19 @@
             out_ref[rows, tokens] = mixed
 
 
-def add_levels(mixed, queries, sums, level_weight, levels, parts, first_level):
+def add_levels(mixed, queries, sums, level_weight, levels, parts, first_level, tokens=()):
     width = mixed.shape[0]
     bits = [bit for bit, _, _ in levels]
     plan = [pieces for _, _, pieces in levels]
+    prefixes = [prefix for _, prefix, _ in levels]
     return call(
         functools.partial(reach_kernel, plan, bits, first_level),
-        "reach",
-        [mixed, queries, sums, level_weight, *[prefix for _, prefix, _ in levels], *parts],
-        [(mixed.shape, jnp.float32)],
+        f"reach{bits[0]}",
+        [mixed, queries, sums, level_weight, *prefixes, *parts, *tokens],
+        [(mixed.shape, jnp.float32), ((8, 128), jnp.float32)],
         [pltpu.VMEM((len(bits), width, queries.shape[1]), jnp.bfloat16)],
         aliases={0: 0},
-    )[0]
+    )
 
 
 def finish_kernel(far, bit, first_level, *refs):
@@ -383,12 +385,11 @@
     head_width = mixed_ref.shape[0] // heads
     half = heads // 2
     first = first_head((far,), heads)
-    flips = half.bit_length() - 1
-    for slot in range(half):
-        beyond = tuple(slot >> (flips - 1 - bit) & 1 for bit in range(flips))
-        start = pl.multiple_of((first_head((far, *beyond), heads) - first) * head_width, 128)
-        rows = slice(slot * head_width, (slot + 1) * head_width)
-        level[pl.ds(start, head_width)] = state_ref[rows].astype(jnp.bfloat16)
+    size = half * head_width // 2
+    for side in range(2):
+        start = pl.multiple_of((first_head((far, side), heads) - first) * head_width, 128)
+        rows = slice(side * size, (side + 1) * size)
+        level[pl.ds(start, size)] = state_ref[rows].astype(jnp.bfloat16)
     gains = []
     for slot in range(half):
         row = jnp.broadcast_to(gain_ref[pl.ds(first + slot, 1)], (8, head_width))
@@ -472,61 +473,58 @@
     )
     shared = (queries, keys, values, sums, totals, level_weight, local)
 
+    last = bits - 1
     prefix = jnp.zeros((heads, 128), jnp.float32)
     prefixes, found, rests = [], [], []
-    mixed, at, tokens_done = None, 0, ()
+    mixed, at, waits = None, 0, ()
     for bit in range(bits):
         lower = lambda source, bit=bit: (source >> bit) & 1 == 0
-        sent = give if bit < group_bits else mine
-        both = bit < bits - 1
-        found.append(trade(sent, 2**bit) if both else trade(sent, 2**bit, lower))
         prefixes.append(prefix)
-        if bit < group_bits:
+        if bit < last:
+            found.append(trade(give if bit < SPLIT_BITS else mine, 2**bit))
+        else:
+            found.append(trade(mine, 2**bit, lower))
+        if bit < SPLIT_BITS:
             rests.append(trade(mine, 2**bit, lower))
         if 0 < bit and at < spans:
-            stop = spans if bit == bits - 2 else at + 1
-            mixed, token = mix_local(at, stop, shared, mixed)
-            at, tokens_done = stop, (token,)
-        if both:
-            *messages, prefix = merge(bit, mine, found[bit], prefix, tokens_done)
+            stop = spans if bit == last else at + 1
+            mixed, token = mix_local(at, stop, shared, mixed, (mine,))
+            at, waits = stop, (token,)
+        if 1 < bit < 2 + SPLIT_BITS:
+            waits = (*waits, rests[bit - 2])
+        if bit < last:
+            *messages, prefix = merge(bit, mine, found[bit], prefix, waits)
             mine, give = messages if len(messages) == 2 else (messages[0], None)
-    after = (mine,)
-
-    early = range(group_bits, bits - 1)
-    ahead = pack("ahead", [(found[bit], per) for bit in early], after)
-    beside = trade(ahead, 4)
-    pieces = [(found[2], per), (rests[2], per)]
-    for slot, bit in enumerate(early):
-        pieces += [(ahead[slot * per : (slot + 1) * per], per), (beside[slot * per : (slot + 1) * per], per)]
-    quarter = pack("quarter", pieces)
-    across = trade(quarter, 2)
-    step = quarter.shape[0]
+
+    rest = (queries, sums, level_weight)
+    two = 2 * per
+    middle = pack("middle", [(found[bit], two) for bit in range(2, last)], (mine,))
+    across = trade(middle, 2)
+    step = middle.shape[0]
+
+    needed = lambda source: (source >> last) & 1 == 1
+    state = found[last]
+    beside = trade(state, 2, needed)
+    levels = [(0, prefixes[0], [(0, 0, (0,)), (1, 0, (1,))])]
+    parts = [found[0], rests[0]]
+    mixed, token = add_levels(mixed, *rest, levels, parts, first_level)
+
     near = pack(
-        "near", [(found[1], 2 * per), (rests[1], 2 * per), (quarter, step), (across, step)]
+        "near", [(found[1], two), (rests[1], two), (middle, step), (across, step)], (state,)
     )
     far = trade(near, 1)
-    levels = [(0, prefixes[0], [(0, 0, (0,)), (1, 0, (1,))])]
-    levels.append(
-        (1, prefixes[1], [(2 + core, side * 2 * per, (core, side)) for core in (0, 1) for side in (0, 1)])
-    )
-    for slot, bit in enumerate(range(2, bits - 1)):
-        row = 4 * per + slot * 2 * per
-        taken = [
-            (2 + core, row + side * step + last * per, (core, side, last))
-            for core in (0, 1)
-            for side in (0, 1)
-            for last in (0, 1)
-        ]
-        levels.append((bit, prefixes[bit], taken))
-    parts = [found[0], rests[0], near, far]
-    mixed = add_levels(mixed, queries, sums, level_weight, levels, parts, first_level)
-
-    last = bits - 1
-    needed = lambda source: (source >> last) & 1 == 1
-    state = pack("last1", [(found[last], per), (trade(found[last], 4, needed), per)])
-    state = pack("last2", [(state, 2 * per), (trade(state, 2, needed), 2 * per)])
+    sides = [(core, side) for core in (0, 1) for side in (0, 1)]
+    levels = [(1, prefixes[1], [(core, side * two, (core, side)) for core, side in sides])]
+    for slot, bit in enumerate(range(2, last)):
+        row = 2 * two + slot * two
+        levels.append(
+            (bit, prefixes[bit], [(core, row + side * step, (core, side)) for core, side in sides])
+        )
+    mixed, token = add_levels(mixed, *rest, levels, [near, far], first_level)
+
+    state = pack("last", [(state, two), (beside, two)], (token,))
     other = trade(state, 1, needed)
-    rest = (mixed, queries, sums, level_weight, gain, prefixes[last])
+    rest = (mixed, *rest, gain, prefixes[last])
     begun = finish(0, last, first_level, *rest, state, None)
     return finish(1, last, first_level, *rest, other, begun)
 

time: 63.8 us -> 47.4 us (0.74)
  the two profiles are of different devices: /device:TPU:29 before, /device:TPU:25 now
where the time goes in v6:
time: 47.4 us; the launch traced here: 47.2 us
  starting transfers between devices  19.3 us (41%)
  Pallas kernels  15.6 us (33%)
  waiting for transfers between devices  12.1 us (26%)
    ppermute x11, starting transfers between devices, trade(): return lax.ppermute(value, AXES, pairs)  19.3 us
    ppermute x11, waiting for transfers between devices, trade(): return lax.ppermute(value, AXES, pairs)  12.1 us
    pallas_call x14, Pallas kernels, call(): pl.pallas_call(kernel, in_specs=specs, out_specs=[HELD] * len(outputs), o...  11.8 us
    pallas_call x2, Pallas kernels, finish(): pl.pallas_call(functools.partial(finish_kernel, far, bit, first_level), i...  3.83 us
  transfers between devices with their start and end apart: 11, of which 4 were waited for; matrix products, arithmetic and copies ran while one was open for 0% of the time, Pallas kernels for 23%

profile of v6, /device:TPU:25, one launch (start us, length us, event | category | flops | bytes accessed | tf_op | source)
XLA Modules:
  0.0 47.2 jit_solution(2934283575145897850)
XLA Ops:
  0.0 2.8 %states.1 = (f32[520,128]{1,0:T(8,128)S(1)}, f32[520,128]{1,0:T(8,128)S(1)}, bf16[3,128,1024]{2,1,0:T(8,128)(2,1)S(1)}, f32[2,8,1024]{2,1,0:T(8,128)S(1)}, f32[4...) custom-call(bf16[1024,128]{1,0:T(8,128)(2,1)} %refs_0_.1, ...), custom_call_target="tpu_custom_call" | custom-call | tf_op jit(solution)/shard_map/states/pallas_call | solution.py:41
  2.8 0.7 %collective-permute-start = (f32[520,128]{1,0:T(8,128)S(1)}, f32[520,128]{1,0:T(8,128)S(1)}, u32[]{:S(2)}, u32[]{:S(2)}) collective-permute-start(f32[520,128]{1,0:T(8,128)S(1)} %get-tuple-element.42), channel_id=1, source_target_pairs={{0,8},{8,0},{16,24},{24,16},{1,9},{9,1},{17,25},{25,17},{2,10},{10... | collective-permute-start | bytes 798728 | tf_op jit(solution)/shard_map/ppermute | solution.py:459
  3.5 1.2 %collective-permute-done.refs_1_.refs_5_ = f32[520,128]{1,0:T(8,128)S(1)} collective-permute-done((f32[520,128]{1,0:T(8,128)S(1)}, f32[520,128]{1,0:T(8,128)S(1)}, u32[]{:S(2)}, u32[]{:S(2)}) %collective-permute-start) | collective-permute-done | bytes 266272 | tf_op jit(solution)/shard_map/ppermute | solution.py:459
  4.8 1.3 %collective-permute-start.1 = (f32[264,128]{1,0:T(8,128)S(1)}, f32[264,128]{1,0:T(8,128)S(1)}, u32[]{:S(2)}, u32[]{:S(2)}) collective-permute-start(f32[264,128]{1,0:T(8,128)S(1)} %get-tuple-element.45), channel_id=1, source_target_pairs={{0,16},{8,24},{16,0},{24,8},{1,17},{9,25},{17,1},{25,9},{2,18},{10... | collective-permute-start | bytes 405512 | tf_op jit(solution)/shard_map/ppermute | solution.py:459
  6.1 1.3 %collective-permute-start.3 = (f32[520,128]{1,0:T(8,128)S(1)}, f32[520,128]{1,0:T(8,128)S(1)}, u32[]{:S(2)}, u32[]{:S(2)}) collective-permute-start(f32[520,128]{1,0:T(8,128)S(1)} %get-tuple-element.41.refs_0_), channel_id=1, source_target_pairs={{0,8},{16,24},{1,9},{17,25},{2,10},{18,26},{3,11},{19,27},{4,12},{... | collective-permute-start | bytes 798728 | tf_op jit(solution)/shard_map/ppermute | solution.py:459
  7.4 0.8 %local0.1 = (f32[1024,1024]{1,0:T(8,128)S(1)}, f32[8,128]{1,0:T(8,128)S(1)}) custom-call(bf16[1024,128]{1,0:T(8,128)(2,1)S(1)} %get-tuple-element.34.refs_0_.refs_1_, bf16[1024,128]{1,0:T(8,128)(2,1)S(1)} %get-tuple-element.35.refs_1_, bf16[1024,1024]{1,0:T(8,128)(2,1)S(1)} %get-tuple-element.36.refs_2_, ...), custom_call_target="tpu_custom_call" | custom-call | tf_op jit(solution)/shard_map/local0/pallas_call | solution.py:41
  8.2 1.5 %collective-permute-done.1.refs_1_.refs_0_ = f32[264,128]{1,0:T(8,128)S(1)} collective-permute-done((f32[264,128]{1,0:T(8,128)S(1)}, f32[264,128]{1,0:T(8,128)S(1)}, u32[]{:S(2)}, u32[]{:S(2)}) %collective-permute-start.1) | collective-permute-done | bytes 135200 | tf_op jit(solution)/shard_map/ppermute | solution.py:459
  9.7 1.3 %collective-permute-start.2 = (f32[264,128]{1,0:T(8,128)S(1)}, f32[264,128]{1,0:T(8,128)S(1)}, u32[]{:S(2)}, u32[]{:S(2)}) collective-permute-start(f32[264,128]{1,0:T(8,128)S(1)} %get-tuple-element.48.refs_8_.refs_0_), channel_id=1, source_target_pairs={{0,1},{8,9},{16,17},{24,25},{1,0},{9,8},{17,16},{25,24},{2,3},{10,... | collective-permute-start | bytes 405512 | tf_op jit(solution)/shard_map/ppermute | solution.py:459
  10.9 3.1 %collective-permute-start.5 = (f32[264,128]{1,0:T(8,128)S(1)}, f32[264,128]{1,0:T(8,128)S(1)}, u32[]{:S(2)}, u32[]{:S(2)}) collective-permute-start(f32[264,128]{1,0:T(8,128)S(1)} %get-tuple-element.43.refs_7_.refs_0_), channel_id=1, source_target_pairs={{0,16},{8,24},{1,17},{9,25},{2,18},{10,26},{3,19},{11,27},{4,20},{... | collective-permute-start | bytes 405512 | tf_op jit(solution)/shard_map/ppermute | solution.py:459
  14.1 0.9 %local1.1 = (f32[1024,1024]{1,0:T(8,128)S(1)}, f32[8,128]{1,0:T(8,128)S(1)}) custom-call(bf16[1024,128]{1,0:T(8,128)(2,1)S(1)} %get-tuple-element.34.refs_0_.refs_1_, bf16[1024,128]{1,0:T(8,128)(2,1)S(1)} %get-tuple-element.35.refs_1_, bf16[1024,1024]{1,0:T(8,128)(2,1)S(1)} %get-tuple-element.36.refs_2_, ...), custom_call_target="tpu_custom_call", output_to_operand_aliasing={{0}: (7, {})} | custom-call | tf_op jit(solution)/shard_map/local1/pallas_call | solution.py:41
  15.1 0.2 collective-permute-start.4
  15.3 0.9 %local2.1 = (f32[1024,1024]{1,0:T(8,128)S(1)}, f32[8,128]{1,0:T(8,128)S(1)}) custom-call(bf16[1024,128]{1,0:T(8,128)(2,1)S(1)} %get-tuple-element.34.refs_0_.refs_1_, bf16[1024,128]{1,0:T(8,128)(2,1)S(1)} %get-tuple-element.35.refs_1_, bf16[1024,1024]{1,0:T(8,128)(2,1)S(1)} %get-tuple-element.36.refs_2_, ...), custom_call_target="tpu_custom_call", output_to_operand_aliasing={{0}: (7, {})} | custom-call | tf_op jit(solution)/shard_map/local2/pallas_call | solution.py:41
  16.2 2.8 %collective-permute-done.4.refs_1_ = f32[264,128]{1,0:T(8,128)S(1)} collective-permute-done((f32[264,128]{1,0:T(8,128)S(1)}, f32[264,128]{1,0:T(8,128)S(1)}, u32[]{:S(2)}, u32[]{:S(2)}) %collective-permute-start.4) | collective-permute-done | bytes 135200 | tf_op jit(solution)/shard_map/ppermute | solution.py:459
  19.1 0.2 collective-permute-start.6
  19.3 1.3 %collective-permute-start.7 = (f32[264,128]{1,0:T(8,128)S(1)}, f32[264,128]{1,0:T(8,128)S(1)}, u32[]{:S(2)}, u32[]{:S(2)}) collective-permute-start(f32[264,128]{1,0:T(8,128)S(1)} %get-tuple-element.56.refs_8_.refs_2_), channel_id=1, source_target_pairs={{0,4},{8,12},{16,20},{24,28},{1,5},{9,13},{17,21},{25,29},{2,6},{1... | collective-permute-start | bytes 405512 | tf_op jit(solution)/shard_map/ppermute | solution.py:459
  20.5 6.7 %collective-permute-done.7.refs_4_.refs_0_ = f32[264,128]{1,0:T(8,128)S(1)} collective-permute-done((f32[264,128]{1,0:T(8,128)S(1)}, f32[264,128]{1,0:T(8,128)S(1)}, u32[]{:S(2)}, u32[]{:S(2)}) %collective-permute-start.7) | collective-permute-done | bytes 135200 | tf_op jit(solution)/shard_map/ppermute | solution.py:459
  27.3 4.7 %collective-permute-start.8 = (f32[1536,128]{1,0:T(8,128)S(1)}, f32[1536,128]{1,0:T(8,128)S(1)}, u32[]{:S(2)}, u32[]{:S(2)}) collective-permute-start(f32[1536,128]{1,0:T(8,128)S(1)} %near.1.refs_7_), channel_id=1, source_target_pairs={{0,8},{8,0},{16,24},{24,16},{1,9},{9,1},{17,25},{25,17},{2,10},{10... | collective-permute-start | bytes 2359304 | tf_op jit(solution)/shard_map/ppermute | solution.py:459
  32.0 2.9 %collective-permute-start.9 = (f32[264,128]{1,0:T(8,128)S(1)}, f32[264,128]{1,0:T(8,128)S(1)}, u32[]{:S(2)}, u32[]{:S(2)}) collective-permute-start(f32[264,128]{1,0:T(8,128)S(1)} %collective-permute-done.7.refs_4_.refs_0_), channel_id=1, source_target_pairs={{4,20},{12,28},{20,4},{28,12},{5,21},{13,29},{21,5},{29,13},{6,22}... | collective-permute-start | bytes 405512 | tf_op jit(solution)/shard_map/ppermute | solution.py:459
  34.9 1.6 %local3.1 = (f32[1024,1024]{1,0:T(8,128)S(1)}, f32[8,128]{1,0:T(8,128)}) custom-call(bf16[1024,128]{1,0:T(8,128)(2,1)S(1)} %get-tuple-element.34.refs_0_.refs_1_, bf16[1024,128]{1,0:T(8,128)(2,1)S(1)} %get-tuple-element.35.refs_1_, bf16[1024,1024]{1,0:T(8,128)(2,1)S(1)} %get-tuple-element.36.refs_2_, ...), custom_call_target="tpu_custom_call", output_to_operand_aliasing={{0}: (7, {})} | custom-call | tf_op jit(solution)/shard_map/local3/pallas_call | solution.py:41
  36.5 1.8 %reach0.1 = (f32[1024,1024]{1,0:T(8,128)S(1)}, f32[8,128]{1,0:T(8,128)}) custom-call(f32[1024,1024]{1,0:T(8,128)S(1)} %get-tuple-element.57.refs_0_, bf16[1024,128]{1,0:T(8,128)(2,1)S(1)} %get-tuple-element.34.refs_0_.refs_1_, f32[2,8,1024]{2,1,0:T(8,128)S(1)} %get-tuple-element.37.refs_3_.refs_2_, ...), custom_call_target="tpu_custom_call", output_to_operand_aliasing={{0}: (0, {})} | custom-call | tf_op jit(solution)/shard_map/reach0/pallas_call | solution.py:41
  38.3 2.8 %reach1.1 = (f32[1024,1024]{1,0:T(8,128)S(1)}, f32[8,128]{1,0:T(8,128)S(1)}) custom-call(f32[1024,1024]{1,0:T(8,128)S(1)} %get-tuple-element.58.refs_0_, bf16[1024,128]{1,0:T(8,128)(2,1)S(1)} %get-tuple-element.34.refs_0_.refs_1_, f32[2,8,1024]{2,1,0:T(8,128)S(1)} %get-tuple-element.37.refs_3_.refs_2_, ...), custom_call_target="tpu_custom_call", output_to_operand_aliasing={{0}: (0, {})} | custom-call | tf_op jit(solution)/shard_map/reach1/pallas_call | solution.py:41
  41.2 2.2 %collective-permute-start.10 = (f32[512,128]{1,0:T(8,128)S(1)}, f32[512,128]{1,0:T(8,128)S(1)}, u32[]{:S(2)}, u32[]{:S(2)}) collective-permute-start(f32[512,128]{1,0:T(8,128)S(1)} %last.1.refs_6_), channel_id=1, source_target_pairs={{4,12},{12,4},{20,28},{28,20},{5,13},{13,5},{21,29},{29,21},{6,14}... | collective-permute-start | bytes 786440 | tf_op jit(solution)/shard_map/ppermute | solution.py:459
  43.4 1.9 %finish0.1.refs_7_ = bf16[1024,1024]{1,0:T(8,128)(2,1)} custom-call(f32[1024,1024]{1,0:T(8,128)S(1)} %get-tuple-element.59.refs_0_, bf16[1024,128]{1,0:T(8,128)(2,1)S(1)} %get-tuple-element.34.refs_0_.refs_1_, f32[2,8,1024]{2,1,0:T(8,128)S(1)} %get-tuple-element.37.refs_3_.refs_2_, f32[8,8,1024]{2,1,0:T(8,128)S(1)} %get-tuple-element.39.refs_5_.refs_3_, ...), custom_call_target="tpu_custom_call" | custom-call | tf_op jit(solution)/shard_map/finish0/pallas_call | solution.py:431
  45.3 1.9 %finish1.1 = bf16[1024,1024]{1,0:T(8,128)(2,1)} custom-call(f32[1024,1024]{1,0:T(8,128)S(1)} %get-tuple-element.59.refs_0_, bf16[1024,128]{1,0:T(8,128)(2,1)S(1)} %get-tuple-element.34.refs_0_.refs_1_, f32[2,8,1024]{2,1,0:T(8,128)S(1)} %get-tuple-element.37.refs_3_.refs_2_, ...), custom_call_target="tpu_custom_call", output_to_operand_aliasing={{}: (7, {})} | custom-call | tf_op jit(solution)/shard_map/finish1/pallas_call | solution.py:431
  (15 shorter events, 0.3 us)
Async XLA Ops:
  2.8 1.9 %collective-permute-start = (f32[520,128]{1,0:T(8,128)S(1)}, f32[520,128]{1,0:T(8,128)S(1)}, u32[]{:S(2)}, u32[]{:S(2)}) collective-permute-start(f32[520,128]{1,0:T(8,128)S(1)} %get-tuple-element.42), channel_id=1, source_target_pairs={{0,8},{8,0},{16,24},{24,16},{1,9},{9,1},{17,25},{25,17},{2,10},{10... | collective-permute-start | bytes 798728 | tf_op jit(solution)/shard_map/ppermute | solution.py:459
  4.8 4.9 %collective-permute-start.1 = (f32[264,128]{1,0:T(8,128)S(1)}, f32[264,128]{1,0:T(8,128)S(1)}, u32[]{:S(2)}, u32[]{:S(2)}) collective-permute-start(f32[264,128]{1,0:T(8,128)S(1)} %get-tuple-element.45), channel_id=1, source_target_pairs={{0,16},{8,24},{16,0},{24,8},{1,17},{9,25},{17,1},{25,9},{2,18},{10... | collective-permute-start | bytes 405512 | tf_op jit(solution)/shard_map/ppermute | solution.py:459
  6.1 8.9 %collective-permute-start.3 = (f32[520,128]{1,0:T(8,128)S(1)}, f32[520,128]{1,0:T(8,128)S(1)}, u32[]{:S(2)}, u32[]{:S(2)}) collective-permute-start(f32[520,128]{1,0:T(8,128)S(1)} %get-tuple-element.41.refs_0_), channel_id=1, source_target_pairs={{0,8},{16,24},{1,9},{17,25},{2,10},{18,26},{3,11},{19,27},{4,12},{... | collective-permute-start | bytes 798728 | tf_op jit(solution)/shard_map/ppermute | solution.py:459
  9.7 5.3 %collective-permute-start.2 = (f32[264,128]{1,0:T(8,128)S(1)}, f32[264,128]{1,0:T(8,128)S(1)}, u32[]{:S(2)}, u32[]{:S(2)}) collective-permute-start(f32[264,128]{1,0:T(8,128)S(1)} %get-tuple-element.48.refs_8_.refs_0_), channel_id=1, source_target_pairs={{0,1},{8,9},{16,17},{24,25},{1,0},{9,8},{17,16},{25,24},{2,3},{10,... | collective-permute-start | bytes 405512 | tf_op jit(solution)/shard_map/ppermute | solution.py:459
  10.9 5.2 %collective-permute-start.5 = (f32[264,128]{1,0:T(8,128)S(1)}, f32[264,128]{1,0:T(8,128)S(1)}, u32[]{:S(2)}, u32[]{:S(2)}) collective-permute-start(f32[264,128]{1,0:T(8,128)S(1)} %get-tuple-element.43.refs_7_.refs_0_), channel_id=1, source_target_pairs={{0,16},{8,24},{1,17},{9,25},{2,18},{10,26},{3,19},{11,27},{4,20},{... | collective-permute-start | bytes 405512 | tf_op jit(solution)/shard_map/ppermute | solution.py:459
  15.1 3.9 %collective-permute-start.4 = (f32[264,128]{1,0:T(8,128)S(1)}, f32[264,128]{1,0:T(8,128)S(1)}, u32[]{:S(2)}, u32[]{:S(2)}) collective-permute-start(f32[264,128]{1,0:T(8,128)S(1)} %get-tuple-element.52.refs_8_.refs_0_), channel_id=1, source_target_pairs={{0,2},{8,10},{16,18},{24,26},{1,3},{9,11},{17,19},{25,27},{2,0},{1... | collective-permute-start | bytes 405512 | tf_op jit(solution)/shard_map/ppermute | solution.py:459
  19.1 8.2 %collective-permute-start.6 = (f32[512,128]{1,0:T(8,128)S(1)}, f32[512,128]{1,0:T(8,128)S(1)}, u32[]{:S(2)}, u32[]{:S(2)}) collective-permute-start(f32[512,128]{1,0:T(8,128)S(1)} %middle.1.refs_2_), channel_id=1, source_target_pairs={{0,16},{8,24},{16,0},{24,8},{1,17},{9,25},{17,1},{25,9},{2,18},{10... | collective-permute-start | bytes 786440 | tf_op jit(solution)/shard_map/ppermute | solution.py:459
  19.3 8.0 %collective-permute-start.7 = (f32[264,128]{1,0:T(8,128)S(1)}, f32[264,128]{1,0:T(8,128)S(1)}, u32[]{:S(2)}, u32[]{:S(2)}) collective-permute-start(f32[264,128]{1,0:T(8,128)S(1)} %get-tuple-element.56.refs_8_.refs_2_), channel_id=1, source_target_pairs={{0,4},{8,12},{16,20},{24,28},{1,5},{9,13},{17,21},{25,29},{2,6},{1... | collective-permute-start | bytes 405512 | tf_op jit(solution)/shard_map/ppermute | solution.py:459
  27.3 11.0 %collective-permute-start.8 = (f32[1536,128]{1,0:T(8,128)S(1)}, f32[1536,128]{1,0:T(8,128)S(1)}, u32[]{:S(2)}, u32[]{:S(2)}) collective-permute-start(f32[1536,128]{1,0:T(8,128)S(1)} %near.1.refs_7_), channel_id=1, source_target_pairs={{0,8},{8,0},{16,24},{24,16},{1,9},{9,1},{17,25},{25,17},{2,10},{10... | collective-permute-start | bytes 2359304 | tf_op jit(solution)/shard_map/ppermute | solution.py:459
  32.0 9.1 %collective-permute-start.9 = (f32[264,128]{1,0:T(8,128)S(1)}, f32[264,128]{1,0:T(8,128)S(1)}, u32[]{:S(2)}, u32[]{:S(2)}) collective-permute-start(f32[264,128]{1,0:T(8,128)S(1)} %collective-permute-done.7.refs_4_.refs_0_), channel_id=1, source_target_pairs={{4,20},{12,28},{20,4},{28,12},{5,21},{13,29},{21,5},{29,13},{6,22}... | collective-permute-start | bytes 405512 | tf_op jit(solution)/shard_map/ppermute | solution.py:459
  41.2 4.1 %collective-permute-start.10 = (f32[512,128]{1,0:T(8,128)S(1)}, f32[512,128]{1,0:T(8,128)S(1)}, u32[]{:S(2)}, u32[]{:S(2)}) collective-permute-start(f32[512,128]{1,0:T(8,128)S(1)} %last.1.refs_6_), channel_id=1, source_target_pairs={{4,12},{12,4},{20,28},{28,20},{5,13},{13,5},{21,29},{29,21},{6,14}... | collective-permute-start | bytes 786440 | tf_op jit(solution)/shard_map/ppermute | solution.py:459

commit v7 on v6

--- a/solution.py
+++ b/solution.py
@@ -383,24 +383,20 @@
     out_hbm, out_ref, level, scale_ref, sent = refs[-5:]
     heads = weight_ref.shape[1]
     head_width = mixed_ref.shape[0] // heads
-    half = heads // 2
-    first = first_head((far,), heads)
-    size = half * head_width // 2
-    for side in range(2):
-        start = pl.multiple_of((first_head((far, side), heads) - first) * head_width, 128)
-        rows = slice(side * size, (side + 1) * size)
-        level[pl.ds(start, size)] = state_ref[rows].astype(jnp.bfloat16)
+    count = heads >> len(far)
+    first = first_head(far, heads)
+    level[...] = state_ref[: level.shape[0]].astype(jnp.bfloat16)
     gains = []
-    for slot in range(half):
+    for slot in range(count):
         row = jnp.broadcast_to(gain_ref[pl.ds(first + slot, 1)], (8, head_width))
         gains.append(row.T[:, :1])
-    columns = pl.ds(pl.multiple_of(first * head_width, 128), half * head_width)
+    columns = pl.ds(pl.multiple_of(first * head_width, 128), count * head_width)
     copies = []
     for span in range(q_ref.shape[0] // SPAN):
         tokens = slice(span * SPAN, (span + 1) * SPAN)
         queries = q_ref[tokens]
         scale_ref[...] = level_scale(bit, first_level, prefix_ref, sums_ref, weight_ref, tokens)
-        for slot in range(half):
+        for slot in range(count):
             rows = slice(slot * head_width, (slot + 1) * head_width)
             found = lax.dot_general(level[rows], queries, NT, preferred_element_type=jnp.float32)
             start = pl.multiple_of((first + slot) * head_width, 128)
@@ -434,28 +430,24 @@
         out_specs=out,
         out_shape=jax.ShapeDtypeStruct((tokens, width), jnp.bfloat16),
         scratch_shapes=[
-            pltpu.VMEM((tokens, width // 2), jnp.bfloat16),
-            pltpu.VMEM(state.shape, jnp.bfloat16),
+            pltpu.VMEM((tokens, width >> len(far)), jnp.bfloat16),
+            pltpu.VMEM((width >> len(far), queries.shape[1]), jnp.bfloat16),
             pltpu.VMEM((heads, SPAN), jnp.float32),
             pltpu.SemaphoreType.DMA((tokens // SPAN,)),
         ],
         input_output_aliases={} if begun is None else {7: 0},
         compiler_params=PARAMS,
-        name=f"finish{far}",
+        name=f"finish{far[0]}{far[1]}",
     )(*inputs)
 
 
-def trade(value, mask, senders=lambda source: True):
+def trade(value, mask):
     wide, narrow = lax.axis_size("wide"), lax.axis_size("narrow")
 
     def ranked(index):
         return index % narrow * wide + index // narrow
 
-    pairs = [
-        (ranked(source), ranked(source ^ mask))
-        for source in range(wide * narrow)
-        if senders(source)
-    ]
+    pairs = [(ranked(source), ranked(source ^ mask)) for source in range(wide * narrow)]
     return lax.ppermute(value, AXES, pairs)
 
 
@@ -474,18 +466,16 @@
     shared = (queries, keys, values, sums, totals, level_weight, local)
 
     last = bits - 1
+    two = 2 * per
+    sides = [(core, side) for core in (0, 1) for side in (0, 1)]
     prefix = jnp.zeros((heads, 128), jnp.float32)
-    prefixes, found, rests = [], [], []
+    prefixes, found, rests, across = [], [], [], {}
     mixed, at, waits = None, 0, ()
     for bit in range(bits):
-        lower = lambda source, bit=bit: (source >> bit) & 1 == 0
         prefixes.append(prefix)
-        if bit < last:
-            found.append(trade(give if bit < SPLIT_BITS else mine, 2**bit))
-        else:
-            found.append(trade(mine, 2**bit, lower))
+        found.append(trade(give if bit < SPLIT_BITS else mine, 2**bit))
         if bit < SPLIT_BITS:
-            rests.append(trade(mine, 2**bit, lower))
+            rests.append(trade(mine, 2**bit))
         if 0 < bit and at < spans:
             stop = spans if bit == last else at + 1
             mixed, token = mix_local(at, stop, shared, mixed, (mine,))
@@ -495,38 +485,43 @@
         if bit < last:
             *messages, prefix = merge(bit, mine, found[bit], prefix, waits)
             mine, give = messages if len(messages) == 2 else (messages[0], None)
+        if 1 < bit < last:
+            found[bit] = pack(f"found{bit}", [(found[bit], two)], (mine,))
+            across[bit] = trade(found[bit], 2)
 
     rest = (queries, sums, level_weight)
-    two = 2 * per
-    middle = pack("middle", [(found[bit], two) for bit in range(2, last)], (mine,))
-    across = trade(middle, 2)
-    step = middle.shape[0]
-
-    needed = lambda source: (source >> last) & 1 == 1
-    state = found[last]
-    beside = trade(state, 2, needed)
+    near = pack("near1", [(found[1], two), (rests[1], two)])
+    far = trade(near, 1)
     levels = [(0, prefixes[0], [(0, 0, (0,)), (1, 0, (1,))])]
-    parts = [found[0], rests[0]]
+    levels.append((1, prefixes[1], [(2 + core, side * two, (core, side)) for core, side in sides]))
+    parts = [found[0], rests[0], near, far]
     mixed, token = add_levels(mixed, *rest, levels, parts, first_level)
-
-    near = pack(
-        "near", [(found[1], two), (rests[1], two), (middle, step), (across, step)], (state,)
-    )
+    state = pack("state", [(found[last], two)], (token,))
+
+    pieces = []
+    for bit in range(2, last - 1):
+        pieces += [(found[bit], two), (across[bit], two)]
+    near = pack("near2", [*pieces, (found[last - 1], two)], (mine,))
     far = trade(near, 1)
-    sides = [(core, side) for core in (0, 1) for side in (0, 1)]
-    levels = [(1, prefixes[1], [(core, side * two, (core, side)) for core, side in sides])]
+    near_side, far_side = across[last - 1], trade(across[last - 1], 1)
+    levels = []
     for slot, bit in enumerate(range(2, last)):
-        row = 2 * two + slot * two
-        levels.append(
-            (bit, prefixes[bit], [(core, row + side * step, (core, side)) for core, side in sides])
-        )
-    mixed, token = add_levels(mixed, *rest, levels, [near, far], first_level)
-
-    state = pack("last", [(state, two), (beside, two)], (token,))
-    other = trade(state, 1, needed)
-    rest = (mixed, *rest, gain, prefixes[last])
-    begun = finish(0, last, first_level, *rest, state, None)
-    return finish(1, last, first_level, *rest, other, begun)
+        taken = [
+            (core if bit < last - 1 or side == 0 else 2 + core, (2 * slot + side) * two, (core, side))
+            for core, side in sides
+        ]
+        if bit == last - 1:
+            taken = [(at, row if at < 2 else 0, far_bits) for at, row, far_bits in taken]
+        levels.append((bit, prefixes[bit], taken))
+    parts = [near, far, near_side, far_side]
+    mixed, token = add_levels(mixed, *rest, levels, parts, first_level, (state,))
+
+    rest = (last, first_level, mixed, *rest, gain, prefixes[last])
+    beside = pack("beside", [(trade(state, 2), two)], (token,))
+    out = finish((0, 0), *rest, state, None)
+    out = finish((1, 0), *rest, trade(state, 1), out)
+    out = finish((0, 1), *rest, beside, out)
+    return finish((1, 1), *rest, trade(beside, 1), out)
 
 
 def solution(mesh):

time: 47.4 us -> 44.3 us (0.935)
  the two profiles are of different devices: /device:TPU:25 before, /device:TPU:0 now
where the time goes in v7:
time: 44.3 us; the launch traced here: 44.1 us
  Pallas kernels  17.7 us (40%)
  starting transfers between devices  16.2 us (37%)
  waiting for transfers between devices  9.94 us (22%)
    ppermute x15, starting transfers between devices, trade(): return lax.ppermute(value, AXES, pairs)  16.2 us
    pallas_call x17, Pallas kernels, call(): pl.pallas_call(kernel, in_specs=specs, out_specs=[HELD] * len(outputs), o...  12.5 us
    ppermute x15, waiting for transfers between devices, trade(): return lax.ppermute(value, AXES, pairs)  9.94 us
    pallas_call x4, Pallas kernels, finish(): pl.pallas_call(functools.partial(finish_kernel, far, bit, first_level), i...  5.21 us
  transfers between devices with their start and end apart: 15, of which 7 were waited for; matrix products, arithmetic and copies ran while one was open for 0% of the time, Pallas kernels for 31%

profile of v7, /device:TPU:0, one launch (start us, length us, event | category | flops | bytes accessed | tf_op | source)
XLA Modules:
  0.0 44.1 jit_solution(3729346858418560830)
XLA Ops:
  0.0 2.8 %states.1 = (f32[520,128]{1,0:T(8,128)S(1)}, f32[520,128]{1,0:T(8,128)S(1)}, bf16[3,128,1024]{2,1,0:T(8,128)(2,1)S(1)}, f32[2,8,1024]{2,1,0:T(8,128)S(1)}, f32[4...) custom-call(bf16[1024,128]{1,0:T(8,128)(2,1)} %refs_0_.1, ...), custom_call_target="tpu_custom_call" | custom-call | tf_op jit(solution)/shard_map/states/pallas_call | solution.py:41
  3.3 1.2 %collective-permute-done.refs_1_.refs_6_ = f32[520,128]{1,0:T(8,128)S(1)} collective-permute-done((f32[520,128]{1,0:T(8,128)S(1)}, f32[520,128]{1,0:T(8,128)S(1)}, u32[]{:S(2)}, u32[]{:S(2)}) %collective-permute-start) | collective-permute-done | bytes 266272 | tf_op jit(solution)/shard_map/ppermute | solution.py:451
  4.6 2.9 %collective-permute-start.1 = (f32[264,128]{1,0:T(8,128)S(1)}, f32[264,128]{1,0:T(8,128)S(1)}, u32[]{:S(2)}, u32[]{:S(2)}) collective-permute-start(f32[264,128]{1,0:T(8,128)S(1)} %get-tuple-element.46), channel_id=1, source_target_pairs={{0,16},{8,24},{16,0},{24,8},{1,17},{9,25},{17,1},{25,9},{2,18},{10... | collective-permute-start | bytes 405512 | tf_op jit(solution)/shard_map/ppermute | solution.py:451
  8.3 3.1 %collective-permute-done.1.refs_1_.refs_0_ = f32[264,128]{1,0:T(8,128)S(1)} collective-permute-done((f32[264,128]{1,0:T(8,128)S(1)}, f32[264,128]{1,0:T(8,128)S(1)}, u32[]{:S(2)}, u32[]{:S(2)}) %collective-permute-start.1) | collective-permute-done | bytes 135200 | tf_op jit(solution)/shard_map/ppermute | solution.py:451
  11.4 1.8 %collective-permute-start.2 = (f32[264,128]{1,0:T(8,128)S(1)}, f32[264,128]{1,0:T(8,128)S(1)}, u32[]{:S(2)}, u32[]{:S(2)}) collective-permute-start(f32[264,128]{1,0:T(8,128)S(1)} %get-tuple-element.49.refs_8_.refs_0_), channel_id=1, source_target_pairs={{0,1},{8,9},{16,17},{24,25},{1,0},{9,8},{17,16},{25,24},{2,3},{10,... | collective-permute-start | bytes 405512 | tf_op jit(solution)/shard_map/ppermute | solution.py:451
  13.2 1.5 %collective-permute-start.5 = (f32[264,128]{1,0:T(8,128)S(1)}, f32[264,128]{1,0:T(8,128)S(1)}, u32[]{:S(2)}, u32[]{:S(2)}) collective-permute-start(f32[264,128]{1,0:T(8,128)S(1)} %get-tuple-element.44.refs_7_.refs_0_), channel_id=1, source_target_pairs={{0,16},{8,24},{16,0},{24,8},{1,17},{9,25},{17,1},{25,9},{2,18},{10... | collective-permute-start | bytes 405512 | tf_op jit(solution)/shard_map/ppermute | solution.py:451
  14.7 0.9 %local1.1 = (f32[1024,1024]{1,0:T(8,128)S(1)}, f32[8,128]{1,0:T(8,128)S(1)}) custom-call(bf16[1024,128]{1,0:T(8,128)(2,1)S(1)} %get-tuple-element.35.refs_0_.refs_1_, bf16[1024,128]{1,0:T(8,128)(2,1)S(1)} %get-tuple-element.36.refs_1_, bf16[1024,1024]{1,0:T(8,128)(2,1)S(1)} %get-tuple-element.37.refs_2_, ...), custom_call_target="tpu_custom_call", output_to_operand_aliasing={{0}: (7, {})} | custom-call | tf_op jit(solution)/shard_map/local1/pallas_call | solution.py:41
  15.6 1.0 %collective-permute-done.2.refs_1_.refs_0_ = f32[264,128]{1,0:T(8,128)S(1)} collective-permute-done((f32[264,128]{1,0:T(8,128)S(1)}, f32[264,128]{1,0:T(8,128)S(1)}, u32[]{:S(2)}, u32[]{:S(2)}) %collective-permute-start.2) | collective-permute-done | bytes 135200 | tf_op jit(solution)/shard_map/ppermute | solution.py:451
  16.7 1.8 %collective-permute-start.4 = (f32[264,128]{1,0:T(8,128)S(1)}, f32[264,128]{1,0:T(8,128)S(1)}, u32[]{:S(2)}, u32[]{:S(2)}) collective-permute-start(f32[264,128]{1,0:T(8,128)S(1)} %get-tuple-element.53.refs_8_.refs_0_.refs_1_), channel_id=1, source_target_pairs={{0,2},{8,10},{16,18},{24,26},{1,3},{9,11},{17,19},{25,27},{2,0},{1... | collective-permute-start | bytes 405512 | tf_op jit(solution)/shard_map/ppermute | solution.py:451
  18.4 1.6 %collective-permute-start.7 = (f32[256,128]{1,0:T(8,128)S(1)}, f32[256,128]{1,0:T(8,128)S(1)}, u32[]{:S(2)}, u32[]{:S(2)}) collective-permute-start(f32[256,128]{1,0:T(8,128)S(1)} %found2.1.refs_0_), channel_id=1, source_target_pairs={{0,16},{8,24},{16,0},{24,8},{1,17},{9,25},{17,1},{25,9},{2,18},{10... | collective-permute-start | bytes 393224 | tf_op jit(solution)/shard_map/ppermute | solution.py:451
  20.1 0.9 %local2.1 = (f32[1024,1024]{1,0:T(8,128)S(1)}, f32[8,128]{1,0:T(8,128)S(1)}) custom-call(bf16[1024,128]{1,0:T(8,128)(2,1)S(1)} %get-tuple-element.35.refs_0_.refs_1_, bf16[1024,128]{1,0:T(8,128)(2,1)S(1)} %get-tuple-element.36.refs_1_, bf16[1024,1024]{1,0:T(8,128)(2,1)S(1)} %get-tuple-element.37.refs_2_, ...), custom_call_target="tpu_custom_call", output_to_operand_aliasing={{0}: (7, {})} | custom-call | tf_op jit(solution)/shard_map/local2/pallas_call | solution.py:41
  21.8 1.7 %collective-permute-done.7.refs_1_ = f32[256,128]{1,0:T(8,128)S(1)} collective-permute-done((f32[256,128]{1,0:T(8,128)S(1)}, f32[256,128]{1,0:T(8,128)S(1)}, u32[]{:S(2)}, u32[]{:S(2)}) %collective-permute-start.7) | collective-permute-done | bytes 131104 | tf_op jit(solution)/shard_map/ppermute | solution.py:451
  23.6 2.7 %collective-permute-start.11 = (f32[264,128]{1,0:T(8,128)S(1)}, f32[264,128]{1,0:T(8,128)S(1)}, u32[]{:S(2)}, u32[]{:S(2)}) collective-permute-start(f32[264,128]{1,0:T(8,128)S(1)} %get-tuple-element.57.refs_8_.refs_1_.refs_3_), channel_id=1, source_target_pairs={{0,4},{8,12},{16,20},{24,28},{1,5},{9,13},{17,21},{25,29},{2,6},{1... | collective-permute-start | bytes 405512 | tf_op jit(solution)/shard_map/ppermute | solution.py:451
  26.2 1.5 %collective-permute-start.9 = (f32[256,128]{1,0:T(8,128)S(1)}, f32[256,128]{1,0:T(8,128)S(1)}, u32[]{:S(2)}, u32[]{:S(2)}) collective-permute-start(f32[256,128]{1,0:T(8,128)S(1)} %found3.1.refs_2_), channel_id=1, source_target_pairs={{0,16},{8,24},{16,0},{24,8},{1,17},{9,25},{17,1},{25,9},{2,18},{10... | collective-permute-start | bytes 393224 | tf_op jit(solution)/shard_map/ppermute | solution.py:451
  27.7 1.6 %local3.1 = (f32[1024,1024]{1,0:T(8,128)S(1)}, f32[8,128]{1,0:T(8,128)}) custom-call(bf16[1024,128]{1,0:T(8,128)(2,1)S(1)} %get-tuple-element.35.refs_0_.refs_1_, bf16[1024,128]{1,0:T(8,128)(2,1)S(1)} %get-tuple-element.36.refs_1_, bf16[1024,1024]{1,0:T(8,128)(2,1)S(1)} %get-tuple-element.37.refs_2_, ...), custom_call_target="tpu_custom_call", output_to_operand_aliasing={{0}: (7, {})} | custom-call | tf_op jit(solution)/shard_map/local3/pallas_call | solution.py:41
  29.3 2.7 %reach0.1 = (f32[1024,1024]{1,0:T(8,128)S(1)}, f32[8,128]{1,0:T(8,128)S(1)}) custom-call(f32[1024,1024]{1,0:T(8,128)S(1)} %get-tuple-element.58.refs_0_, bf16[1024,128]{1,0:T(8,128)(2,1)S(1)} %get-tuple-element.35.refs_0_.refs_1_, f32[2,8,1024]{2,1,0:T(8,128)S(1)} %get-tuple-element.38.refs_3_.refs_2_, ...), custom_call_target="tpu_custom_call", output_to_operand_aliasing={{0}: (0, {})} | custom-call | tf_op jit(solution)/shard_map/reach0/pallas_call | solution.py:41
  32.1 1.1 %collective-permute-done.11.refs_0_ = f32[264,128]{1,0:T(8,128)S(1)} collective-permute-done((f32[264,128]{1,0:T(8,128)S(1)}, f32[264,128]{1,0:T(8,128)S(1)}, u32[]{:S(2)}, u32[]{:S(2)}) %collective-permute-start.11) | collective-permute-done | bytes 135200 | tf_op jit(solution)/shard_map/ppermute | solution.py:451
  33.2 1.7 %collective-permute-start.12 = (f32[256,128]{1,0:T(8,128)S(1)}, f32[256,128]{1,0:T(8,128)S(1)}, u32[]{:S(2)}, u32[]{:S(2)}) collective-permute-start(f32[256,128]{1,0:T(8,128)S(1)} %state.1.refs_10_.refs_6_), channel_id=1, source_target_pairs={{0,16},{8,24},{16,0},{24,8},{1,17},{9,25},{17,1},{25,9},{2,18},{10... | collective-permute-start | bytes 393224 | tf_op jit(solution)/shard_map/ppermute | solution.py:451
  34.9 2.7 %reach2.1 = (f32[1024,1024]{1,0:T(8,128)S(1)}, f32[8,128]{1,0:T(8,128)S(1)}) custom-call(f32[1024,1024]{1,0:T(8,128)S(1)} %get-tuple-element.59.refs_0_, bf16[1024,128]{1,0:T(8,128)(2,1)S(1)} %get-tuple-element.35.refs_0_.refs_1_, f32[2,8,1024]{2,1,0:T(8,128)S(1)} %get-tuple-element.38.refs_3_.refs_2_, ...), custom_call_target="tpu_custom_call", output_to_operand_aliasing={{0}: (0, {})} | custom-call | tf_op jit(solution)/shard_map/reach2/pallas_call | solution.py:41
  37.5 1.2 %collective-permute-done.12.refs_0_ = f32[256,128]{1,0:T(8,128)S(1)} collective-permute-done((f32[256,128]{1,0:T(8,128)S(1)}, f32[256,128]{1,0:T(8,128)S(1)}, u32[]{:S(2)}, u32[]{:S(2)}) %collective-permute-start.12) | collective-permute-done | bytes 131104 | tf_op jit(solution)/shard_map/ppermute | solution.py:451
  38.8 1.3 %finish00.1.refs_7_ = bf16[1024,1024]{1,0:T(8,128)(2,1)} custom-call(f32[1024,1024]{1,0:T(8,128)S(1)} %get-tuple-element.61.refs_0_, bf16[1024,128]{1,0:T(8,128)(2,1)S(1)} %get-tuple-element.35.refs_0_.refs_1_, f32[2,8,1024]{2,1,0:T(8,128)S(1)} %get-tuple-element.38.refs_3_.refs_2_, f32[8,8,1024]{2,1,0:T(8,128)S(1)} %get-tuple-element.40.refs_5_.refs_3_, ...), custom_call_target="tpu_custom_call" | custom-call | tf_op jit(solution)/shard_map/finish00/pallas_call | solution.py:427
  40.1 1.3 %finish10.1.refs_7_ = bf16[1024,1024]{1,0:T(8,128)(2,1)} custom-call(f32[1024,1024]{1,0:T(8,128)S(1)} %get-tuple-element.61.refs_0_, bf16[1024,128]{1,0:T(8,128)(2,1)S(1)} %get-tuple-element.35.refs_0_.refs_1_, f32[2,8,1024]{2,1,0:T(8,128)S(1)} %get-tuple-element.38.refs_3_.refs_2_, ...), custom_call_target="tpu_custom_call", output_to_operand_aliasing={{}: (7, {})} | custom-call | tf_op jit(solution)/shard_map/finish10/pallas_call | solution.py:427
  41.4 1.3 %finish01.1.refs_7_ = bf16[1024,1024]{1,0:T(8,128)(2,1)} custom-call(f32[1024,1024]{1,0:T(8,128)S(1)} %get-tuple-element.61.refs_0_, bf16[1024,128]{1,0:T(8,128)(2,1)S(1)} %get-tuple-element.35.refs_0_.refs_1_, f32[2,8,1024]{2,1,0:T(8,128)S(1)} %get-tuple-element.38.refs_3_.refs_2_, ...), custom_call_target="tpu_custom_call", output_to_operand_aliasing={{}: (7, {})} | custom-call | tf_op jit(solution)/shard_map/finish01/pallas_call | solution.py:427
  42.8 1.3 %finish11.1 = bf16[1024,1024]{1,0:T(8,128)(2,1)} custom-call(f32[1024,1024]{1,0:T(8,128)S(1)} %get-tuple-element.61.refs_0_, bf16[1024,128]{1,0:T(8,128)(2,1)S(1)} %get-tuple-element.35.refs_0_.refs_1_, f32[2,8,1024]{2,1,0:T(8,128)S(1)} %get-tuple-element.38.refs_3_.refs_2_, ...), custom_call_target="tpu_custom_call", output_to_operand_aliasing={{}: (7, {})} | custom-call | tf_op jit(solution)/shard_map/finish11/pallas_call | solution.py:427
  (28 shorter events, 2.6 us)
Async XLA Ops:
  2.8 1.7 %collective-permute-start = (f32[520,128]{1,0:T(8,128)S(1)}, f32[520,128]{1,0:T(8,128)S(1)}, u32[]{:S(2)}, u32[]{:S(2)}) collective-permute-start(f32[520,128]{1,0:T(8,128)S(1)} %get-tuple-element.43), channel_id=1, source_target_pairs={{0,8},{8,0},{16,24},{24,16},{1,9},{9,1},{17,25},{25,17},{2,10},{10... | collective-permute-start | bytes 798728 | tf_op jit(solution)/shard_map/ppermute | solution.py:451
  4.6 6.8 %collective-permute-start.1 = (f32[264,128]{1,0:T(8,128)S(1)}, f32[264,128]{1,0:T(8,128)S(1)}, u32[]{:S(2)}, u32[]{:S(2)}) collective-permute-start(f32[264,128]{1,0:T(8,128)S(1)} %get-tuple-element.46), channel_id=1, source_target_pairs={{0,16},{8,24},{16,0},{24,8},{1,17},{9,25},{17,1},{25,9},{2,18},{10... | collective-permute-start | bytes 405512 | tf_op jit(solution)/shard_map/ppermute | solution.py:451
  7.5 8.1 %collective-permute-start.3 = (f32[520,128]{1,0:T(8,128)S(1)}, f32[520,128]{1,0:T(8,128)S(1)}, u32[]{:S(2)}, u32[]{:S(2)}) collective-permute-start(f32[520,128]{1,0:T(8,128)S(1)} %get-tuple-element.42.refs_0_), channel_id=1, source_target_pairs={{0,8},{8,0},{16,24},{24,16},{1,9},{9,1},{17,25},{25,17},{2,10},{10... | collective-permute-start | bytes 798728 | tf_op jit(solution)/shard_map/ppermute | solution.py:451
  11.4 5.2 %collective-permute-start.2 = (f32[264,128]{1,0:T(8,128)S(1)}, f32[264,128]{1,0:T(8,128)S(1)}, u32[]{:S(2)}, u32[]{:S(2)}) collective-permute-start(f32[264,128]{1,0:T(8,128)S(1)} %get-tuple-element.49.refs_8_.refs_0_), channel_id=1, source_target_pairs={{0,1},{8,9},{16,17},{24,25},{1,0},{9,8},{17,16},{25,24},{2,3},{10,... | collective-permute-start | bytes 405512 | tf_op jit(solution)/shard_map/ppermute | solution.py:451
  13.2 6.8 %collective-permute-start.5 = (f32[264,128]{1,0:T(8,128)S(1)}, f32[264,128]{1,0:T(8,128)S(1)}, u32[]{:S(2)}, u32[]{:S(2)}) collective-permute-start(f32[264,128]{1,0:T(8,128)S(1)} %get-tuple-element.44.refs_7_.refs_0_), channel_id=1, source_target_pairs={{0,16},{8,24},{16,0},{24,8},{1,17},{9,25},{17,1},{25,9},{2,18},{10... | collective-permute-start | bytes 405512 | tf_op jit(solution)/shard_map/ppermute | solution.py:451
  16.7 5.1 %collective-permute-start.4 = (f32[264,128]{1,0:T(8,128)S(1)}, f32[264,128]{1,0:T(8,128)S(1)}, u32[]{:S(2)}, u32[]{:S(2)}) collective-permute-start(f32[264,128]{1,0:T(8,128)S(1)} %get-tuple-element.53.refs_8_.refs_0_.refs_1_), channel_id=1, source_target_pairs={{0,2},{8,10},{16,18},{24,26},{1,3},{9,11},{17,19},{25,27},{2,0},{1... | collective-permute-start | bytes 405512 | tf_op jit(solution)/shard_map/ppermute | solution.py:451
  18.4 5.0 %collective-permute-start.7 = (f32[256,128]{1,0:T(8,128)S(1)}, f32[256,128]{1,0:T(8,128)S(1)}, u32[]{:S(2)}, u32[]{:S(2)}) collective-permute-start(f32[256,128]{1,0:T(8,128)S(1)} %found2.1.refs_0_), channel_id=1, source_target_pairs={{0,16},{8,24},{16,0},{24,8},{1,17},{9,25},{17,1},{25,9},{2,18},{10... | collective-permute-start | bytes 393224 | tf_op jit(solution)/shard_map/ppermute | solution.py:451
  20.0 9.3 %collective-permute-start.6 = (f32[512,128]{1,0:T(8,128)S(1)}, f32[512,128]{1,0:T(8,128)S(1)}, u32[]{:S(2)}, u32[]{:S(2)}) collective-permute-start(f32[512,128]{1,0:T(8,128)S(1)} %near1.1.refs_8_), channel_id=1, source_target_pairs={{0,8},{8,0},{16,24},{24,16},{1,9},{9,1},{17,25},{25,17},{2,10},{10... | collective-permute-start | bytes 786440 | tf_op jit(solution)/shard_map/ppermute | solution.py:451
  23.5 11.4 %collective-permute-start.8 = (f32[768,128]{1,0:T(8,128)S(1)}, f32[768,128]{1,0:T(8,128)S(1)}, u32[]{:S(2)}, u32[]{:S(2)}) collective-permute-start(f32[768,128]{1,0:T(8,128)S(1)} %near2.1.refs_6_), channel_id=1, source_target_pairs={{0,8},{8,0},{16,24},{24,16},{1,9},{9,1},{17,25},{25,17},{2,10},{10... | collective-permute-start | bytes 1179656 | tf_op jit(solution)/shard_map/ppermute | solution.py:451
  23.6 9.6 %collective-permute-start.11 = (f32[264,128]{1,0:T(8,128)S(1)}, f32[264,128]{1,0:T(8,128)S(1)}, u32[]{:S(2)}, u32[]{:S(2)}) collective-permute-start(f32[264,128]{1,0:T(8,128)S(1)} %get-tuple-element.57.refs_8_.refs_1_.refs_3_), channel_id=1, source_target_pairs={{0,4},{8,12},{16,20},{24,28},{1,5},{9,13},{17,21},{25,29},{2,6},{1... | collective-permute-start | bytes 405512 | tf_op jit(solution)/shard_map/ppermute | solution.py:451
  26.2 5.8 %collective-permute-start.9 = (f32[256,128]{1,0:T(8,128)S(1)}, f32[256,128]{1,0:T(8,128)S(1)}, u32[]{:S(2)}, u32[]{:S(2)}) collective-permute-start(f32[256,128]{1,0:T(8,128)S(1)} %found3.1.refs_2_), channel_id=1, source_target_pairs={{0,16},{8,24},{16,0},{24,8},{1,17},{9,25},{17,1},{25,9},{2,18},{10... | collective-permute-start | bytes 393224 | tf_op jit(solution)/shard_map/ppermute | solution.py:451
  32.0 2.9 %collective-permute-start.10 = (f32[256,128]{1,0:T(8,128)S(1)}, f32[256,128]{1,0:T(8,128)S(1)}, u32[]{:S(2)}, u32[]{:S(2)}) collective-permute-start(f32[256,128]{1,0:T(8,128)S(1)} %collective-permute-done.9.refs_8_), channel_id=1, source_target_pairs={{0,8},{8,0},{16,24},{24,16},{1,9},{9,1},{17,25},{25,17},{2,10},{10... | collective-permute-start | bytes 393224 | tf_op jit(solution)/shard_map/ppermute | solution.py:451
  33.2 5.5 %collective-permute-start.12 = (f32[256,128]{1,0:T(8,128)S(1)}, f32[256,128]{1,0:T(8,128)S(1)}, u32[]{:S(2)}, u32[]{:S(2)}) collective-permute-start(f32[256,128]{1,0:T(8,128)S(1)} %state.1.refs_10_.refs_6_), channel_id=1, source_target_pairs={{0,16},{8,24},{16,0},{24,8},{1,17},{9,25},{17,1},{25,9},{2,18},{10... | collective-permute-start | bytes 393224 | tf_op jit(solution)/shard_map/ppermute | solution.py:451
  34.9 5.3 %collective-permute-start.14 = (f32[256,128]{1,0:T(8,128)S(1)}, f32[256,128]{1,0:T(8,128)S(1)}, u32[]{:S(2)}, u32[]{:S(2)}) collective-permute-start(f32[256,128]{1,0:T(8,128)S(1)} %state.1.refs_10_.refs_6_), channel_id=1, source_target_pairs={{0,8},{8,0},{16,24},{24,16},{1,9},{9,1},{17,25},{25,17},{2,10},{10... | collective-permute-start | bytes 393224 | tf_op jit(solution)/shard_map/ppermute | solution.py:451
  38.7 4.0 %collective-permute-start.13 = (f32[256,128]{1,0:T(8,128)S(1)}, f32[256,128]{1,0:T(8,128)S(1)}, u32[]{:S(2)}, u32[]{:S(2)}) collective-permute-start(f32[256,128]{1,0:T(8,128)S(1)} %beside.1.refs_6_), channel_id=1, source_target_pairs={{0,8},{8,0},{16,24},{24,16},{1,9},{9,1},{17,25},{25,17},{2,10},{10... | collective-permute-start | bytes 393224 | tf_op jit(solution)/shard_map/ppermute | solution.py:451

commit v8 on v7

--- a/solution.py
+++ b/solution.py
@@ -249,17 +249,17 @@
     return first
 
 
-def merge_kernel(bit, near, split, *refs):
+def merge_kernel(bit, offset, mode, *refs):
     mine_ref, other_ref, prefix_ref = refs[:3]
     whole_ref = refs[-1]
     next_ref = refs[-2]
     heads = prefix_ref.shape[0]
+    near = min(bit + 1, SPLIT_BITS)
     rows = mine_ref.shape[0] - heads
-    count = heads >> near
-    per = rows // count
+    per = mine_ref.shape[1]
     upper = bit_of(place(), bit) == 1
-    first = first_head((0,) * near, heads)
-    for slot in range(count):
+    first = first_head((0,) * near, heads) + offset
+    for slot in range(rows // per):
         part = slice(slot * per, (slot + 1) * per)
         total = pl.ds(rows + first + slot, 1)
         whole_ref[part] = join(
@@ -268,36 +268,35 @@
     other_total = other_ref[rows:]
     total = mine_ref[rows:] + other_total
     next_ref[...] = prefix_ref[...] + jnp.where(upper, other_total, 0.0)
-    if split:
-        stay_ref, give_ref = refs[-4:-2]
-        half = rows // 2
-        side = bit_of(place(), bit + 1)
-        stay_ref[:half] = whole_ref[pl.ds(side * half, half)]
-        give_ref[:half] = whole_ref[pl.ds((1 - side) * half, half)]
-        stay_ref[half:] = total
-        give_ref[half:] = total
-    else:
+    if mode == "whole":
         merged_ref = refs[-3]
         merged_ref[:rows] = whole_ref[...]
         merged_ref[rows:] = total
-
-
-def merge(bit, mine, other, prefix, tokens=()):
+    else:
+        first_ref, second_ref = refs[-4:-2]
+        half = rows // 2
+        side = bit_of(place(), bit + 1) if mode == "side" else 0
+        first_ref[:half] = whole_ref[pl.ds(side * half, half)]
+        second_ref[:half] = whole_ref[pl.ds((1 - side) * half, half)]
+        first_ref[half:] = total
+        second_ref[half:] = total
+
+
+def merge(bit, mine, other, prefix, mode, offset, tokens=()):
     heads, lanes = prefix.shape
-    near = min(bit + 1, SPLIT_BITS)
-    split = bit + 1 < SPLIT_BITS
     rows = mine.shape[0] - heads
-    if split:
+    if mode == "whole":
+        messages = [(mine.shape, jnp.float32)]
+    else:
         messages = [((rows // 2 + heads, lanes), jnp.float32)] * 2
-    else:
-        messages = [(mine.shape, jnp.float32)]
-    return call(
-        functools.partial(merge_kernel, bit, near, split),
-        f"merge{bit}",
+    *messages, prefix = call(
+        functools.partial(merge_kernel, bit, offset, mode),
+        f"merge{bit}{offset}",
         [mine, other, prefix, *tokens],
         [*messages, (prefix.shape, jnp.float32)],
         [pltpu.VMEM((rows, lanes), jnp.float32)],
     )
+    return messages, prefix
 
 
 def pack_kernel(takes, *refs):
@@ -345,6 +344,8 @@
     heads = weight_ref.shape[1]
     head_width = mixed_ref.shape[0] // heads
     take_levels(plan, part_refs, levels, heads)
+    parts = [slice(head * head_width, (head + 1) * head_width) for head in range(heads)]
+    states = [[levels[slot, rows] for slot in range(len(bits))] for rows in parts]
     for span in range(q_ref.shape[0] // SPAN):
         tokens = slice(span * SPAN, (span + 1) * SPAN)
         queries = q_ref[tokens]
@@ -352,15 +353,13 @@
             level_scale(bit, first_level, prefix_ref, sums_ref, weight_ref, tokens)
             for bit, prefix_ref in zip(bits, prefix_refs)
         ]
+        mixed = [mixed_ref[rows, tokens] for rows in parts]
         for head in range(heads):
-            rows = slice(head * head_width, (head + 1) * head_width)
-            mixed = mixed_ref[rows, tokens]
-            for slot, scale in enumerate(scales):
-                found = lax.dot_general(
-                    levels[slot, rows], queries, NT, preferred_element_type=jnp.float32
-                )
-                mixed = mixed + found * scale[head : head + 1]
-            out_ref[rows, tokens] = mixed
+            for state, scale in zip(states[head], scales):
+                found = lax.dot_general(state, queries, NT, preferred_element_type=jnp.float32)
+                mixed[head] = mixed[head] + found * scale[head : head + 1]
+        for head, rows in enumerate(parts):
+            out_ref[rows, tokens] = mixed[head]
 
 
 def add_levels(mixed, queries, sums, level_weight, levels, parts, first_level, tokens=()):
@@ -380,7 +379,8 @@
 
 def finish_kernel(far, bit, first_level, *refs):
     mixed_ref, q_ref, sums_ref, weight_ref, gain_ref, prefix_ref, state_ref = refs[:7]
-    out_hbm, out_ref, level, scale_ref, sent = refs[-5:]
+    out_hbm, done_ref, out_ref, level, sent = refs[-5:]
+    done_ref[...] = jnp.zeros_like(done_ref)
     heads = weight_ref.shape[1]
     head_width = mixed_ref.shape[0] // heads
     count = heads >> len(far)
@@ -391,32 +391,42 @@
         row = jnp.broadcast_to(gain_ref[pl.ds(first + slot, 1)], (8, head_width))
         gains.append(row.T[:, :1])
     columns = pl.ds(pl.multiple_of(first * head_width, 128), count * head_width)
+    spans = q_ref.shape[0] // SPAN
+    states = [level[slot * head_width : (slot + 1) * head_width] for slot in range(count)]
     copies = []
-    for span in range(q_ref.shape[0] // SPAN):
-        tokens = slice(span * SPAN, (span + 1) * SPAN)
-        queries = q_ref[tokens]
-        scale_ref[...] = level_scale(bit, first_level, prefix_ref, sums_ref, weight_ref, tokens)
-        for slot in range(count):
-            rows = slice(slot * head_width, (slot + 1) * head_width)
-            found = lax.dot_general(level[rows], queries, NT, preferred_element_type=jnp.float32)
-            start = pl.multiple_of((first + slot) * head_width, 128)
-            mixed = mixed_ref[pl.ds(start, head_width), tokens]
-            mixed = mixed + found * scale_ref[pl.ds(first + slot, 1)]
-            square = jnp.mean(mixed * mixed, axis=0, keepdims=True)
-            normed = mixed * lax.rsqrt(square + EPS) * gains[slot]
-            out_ref[tokens, rows] = normed.astype(jnp.bfloat16).T
-        copy = pltpu.make_async_copy(
-            out_ref.at[tokens], out_hbm.at[tokens, columns], sent.at[span]
-        )
-        copy.start()
-        copies.append(copy)
+    for begin in range(0, spans, 2):
+        batch = [slice(span * SPAN, (span + 1) * SPAN) for span in range(begin, min(begin + 2, spans))]
+        results = []
+        for tokens in batch:
+            queries = q_ref[tokens]
+            active = jnp.where(bit_of(place(), bit) == 1, 1.0, 0.0)
+            for slot in range(count):
+                row = pl.ds(first + slot, 1)
+                reach = jnp.exp(sums_ref[1, row, tokens] + prefix_ref[row][:, :1])
+                scale = reach * weight_ref[first_level + bit, row, tokens] * active
+                found = lax.dot_general(
+                    states[slot], queries, NT, preferred_element_type=jnp.float32
+                )
+                start = pl.multiple_of((first + slot) * head_width, 128)
+                mixed = mixed_ref[pl.ds(start, head_width), tokens] + found * scale
+                square = jnp.mean(mixed * mixed, axis=0, keepdims=True)
+                normed = mixed * lax.rsqrt(square + EPS) * gains[slot]
+                rows = slice(slot * head_width, (slot + 1) * head_width)
+                results.append((tokens, rows, normed.astype(jnp.bfloat16).T))
+        for tokens, rows, result in results:
+            out_ref[tokens, rows] = result
+        for tokens in batch:
+            copy = pltpu.make_async_copy(
+                out_ref.at[tokens], out_hbm.at[tokens, columns], sent.at[len(copies)]
+            )
+            copy.start()
+            copies.append(copy)
     for copy in copies:
         copy.wait()
 
 
 def finish(far, bit, first_level, mixed, queries, sums, level_weight, gain, prefix, state, begun):
     width, tokens = mixed.shape
-    heads = level_weight.shape[1]
     inputs = [mixed, queries, sums, level_weight, gain, prefix, state]
     specs = [HELD] * len(inputs)
     inputs = [hold(array) for array in inputs]
@@ -427,12 +437,14 @@
     return pl.pallas_call(
         functools.partial(finish_kernel, far, bit, first_level),
         in_specs=specs,
-        out_specs=out,
-        out_shape=jax.ShapeDtypeStruct((tokens, width), jnp.bfloat16),
+        out_specs=[out, HELD],
+        out_shape=[
+            jax.ShapeDtypeStruct((tokens, width), jnp.bfloat16),
+            pltpu.VMEM((8, 128), jnp.float32),
+        ],
         scratch_shapes=[
             pltpu.VMEM((tokens, width >> len(far)), jnp.bfloat16),
             pltpu.VMEM((width >> len(far), queries.shape[1]), jnp.bfloat16),
-            pltpu.VMEM((heads, SPAN), jnp.float32),
             pltpu.SemaphoreType.DMA((tokens // SPAN,)),
         ],
         input_output_aliases={} if begun is None else {7: 0},
@@ -471,23 +483,35 @@
     prefix = jnp.zeros((heads, 128), jnp.float32)
     prefixes, found, rests, across = [], [], [], {}
     mixed, at, waits = None, 0, ()
+    chunks = [mine]
     for bit in range(bits):
         prefixes.append(prefix)
-        found.append(trade(give if bit < SPLIT_BITS else mine, 2**bit))
+        sent = [give] if bit < SPLIT_BITS else chunks
+        found.append([trade(chunk, 2**bit) for chunk in sent])
         if bit < SPLIT_BITS:
-            rests.append(trade(mine, 2**bit))
+            rests.append(trade(chunks[0], 2**bit))
         if 0 < bit and at < spans:
             stop = spans if bit == last else at + 1
-            mixed, token = mix_local(at, stop, shared, mixed, (mine,))
+            mixed, token = mix_local(at, stop, shared, mixed, (chunks[0],))
             at, waits = stop, (token,)
         if 1 < bit < 2 + SPLIT_BITS:
             waits = (*waits, rests[bit - 2])
         if bit < last:
-            *messages, prefix = merge(bit, mine, found[bit], prefix, waits)
-            mine, give = messages if len(messages) == 2 else (messages[0], None)
+            mode = "side" if bit + 1 < SPLIT_BITS else "whole"
+            merged = [
+                merge(bit, chunk, other, prefix, mode, offset, waits)
+                for offset, (chunk, other) in enumerate(zip(chunks, found[bit]))
+            ]
+            prefix = merged[0][1]
+            chunks = [message for messages, _ in merged for message in messages]
+            if mode == "side":
+                chunks, give = chunks[:1], chunks[1]
         if 1 < bit < last:
-            found[bit] = pack(f"found{bit}", [(found[bit], two)], (mine,))
-            across[bit] = trade(found[bit], 2)
+            pieces = [(state, two // len(found[bit])) for state in found[bit]]
+            found[bit] = [pack(f"found{bit}", pieces, (chunks[0],))]
+            across[bit] = trade(found[bit][0], 2)
+    ends = found[last]
+    found = [states[0] for states in found]
 
     rest = (queries, sums, level_weight)
     near = pack("near1", [(found[1], two), (rests[1], two)])
@@ -496,12 +520,12 @@
     levels.append((1, prefixes[1], [(2 + core, side * two, (core, side)) for core, side in sides]))
     parts = [found[0], rests[0], near, far]
     mixed, token = add_levels(mixed, *rest, levels, parts, first_level)
-    state = pack("state", [(found[last], two)], (token,))
+    state = pack("state", [(ends[0], two)], (token,))
 
     pieces = []
     for bit in range(2, last - 1):
         pieces += [(found[bit], two), (across[bit], two)]
-    near = pack("near2", [*pieces, (found[last - 1], two)], (mine,))
+    near = pack("near2", [*pieces, (found[last - 1], two)], (chunks[0],))
     far = trade(near, 1)
     near_side, far_side = across[last - 1], trade(across[last - 1], 1)
     levels = []
@@ -517,11 +541,12 @@
     mixed, token = add_levels(mixed, *rest, levels, parts, first_level, (state,))
 
     rest = (last, first_level, mixed, *rest, gain, prefixes[last])
-    beside = pack("beside", [(trade(state, 2), two)], (token,))
-    out = finish((0, 0), *rest, state, None)
-    out = finish((1, 0), *rest, trade(state, 1), out)
-    out = finish((0, 1), *rest, beside, out)
-    return finish((1, 1), *rest, trade(beside, 1), out)
+    beside = [(trade(state, 2), two)]
+    out, _ = finish((0, 0), *rest, state, None)
+    out, token = finish((1, 0), *rest, trade(state, 1), out)
+    beside = pack("beside", beside, (token,))
+    out, _ = finish((0, 1), *rest, beside, out)
+    return finish((1, 1), *rest, trade(beside, 1), out)[0]
 
 
 def solution(mesh):

time: 44.3 us -> 48.9 us (1.10)
  Pallas kernels: 17.7 us -> 20.1 us
  waiting for transfers between devices: 9.94 us -> 11.4 us
  starting transfers between devices: 16.2 us -> 17 us
    pallas_call x4, Pallas kernels: 5.21 us -> 7.16 us  [finish(): pl.pallas_call(functools.partial(finish_kernel, far, bit, first_level), i...]
    ppermute x15, waiting for transfers between devices: 9.94 us -> 11.4 us  [trade(): return lax.ppermute(value, AXES, pairs)]
    ppermute x15, starting transfers between devices: 16.2 us -> 17 us  [trade(): return lax.ppermute(value, AXES, pairs)]
  transfers between devices with their start and end apart: 15 -> 15, of which waited for: 7 -> 6; matrix products, arithmetic and copies ran while one was open for 0% -> 0% of each run, Pallas kernels for 31% -> 31%
where the time goes in v8:
time: 48.9 us; the launch traced here: 48.7 us
  Pallas kernels  20.1 us (41%)
  starting transfers between devices  17 us (35%)
  waiting for transfers between devices  11.4 us (23%)
    ppermute x15, starting transfers between devices, trade(): return lax.ppermute(value, AXES, pairs)  17 us
    pallas_call x17, Pallas kernels, call(): pl.pallas_call(kernel, in_specs=specs, out_specs=[HELD] * len(outputs), o...  13 us
    ppermute x15, waiting for transfers between devices, trade(): return lax.ppermute(value, AXES, pairs)  11.4 us
    pallas_call x4, Pallas kernels, finish(): pl.pallas_call(functools.partial(finish_kernel, far, bit, first_level), i...  7.16 us
  transfers between devices with their start and end apart: 15, of which 6 were waited for; matrix products, arithmetic and copies ran while one was open for 0% of the time, Pallas kernels for 31%

profile of v8, /device:TPU:0, one launch (start us, length us, event | category | flops | bytes accessed | tf_op | source)
XLA Modules:
  0.0 48.7 jit_solution(5228566473852520931)
XLA Ops:
  0.0 2.8 %states.1 = (f32[520,128]{1,0:T(8,128)S(1)}, f32[520,128]{1,0:T(8,128)S(1)}, bf16[3,128,1024]{2,1,0:T(8,128)(2,1)S(1)}, f32[2,8,1024]{2,1,0:T(8,128)S(1)}, f32[4...) custom-call(bf16[1024,128]{1,0:T(8,128)(2,1)} %refs_0_.1, ...), custom_call_target="tpu_custom_call" | custom-call | tf_op jit(solution)/shard_map/states/pallas_call | solution.py:41
  3.3 1.2 %collective-permute-done.refs_1_.refs_6_ = f32[520,128]{1,0:T(8,128)S(1)} collective-permute-done((f32[520,128]{1,0:T(8,128)S(1)}, f32[520,128]{1,0:T(8,128)S(1)}, u32[]{:S(2)}, u32[]{:S(2)}) %collective-permute-start) | collective-permute-done | bytes 266272 | tf_op jit(solution)/shard_map/ppermute | solution.py:463
  4.6 2.9 %collective-permute-start.1 = (f32[264,128]{1,0:T(8,128)S(1)}, f32[264,128]{1,0:T(8,128)S(1)}, u32[]{:S(2)}, u32[]{:S(2)}) collective-permute-start(f32[264,128]{1,0:T(8,128)S(1)} %get-tuple-element.50), channel_id=1, source_target_pairs={{0,16},{8,24},{16,0},{24,8},{1,17},{9,25},{17,1},{25,9},{2,18},{10... | collective-permute-start | bytes 405512 | tf_op jit(solution)/shard_map/ppermute | solution.py:463
  8.3 3.1 %collective-permute-done.1.refs_1_.refs_0_ = f32[264,128]{1,0:T(8,128)S(1)} collective-permute-done((f32[264,128]{1,0:T(8,128)S(1)}, f32[264,128]{1,0:T(8,128)S(1)}, u32[]{:S(2)}, u32[]{:S(2)}) %collective-permute-start.1) | collective-permute-done | bytes 135200 | tf_op jit(solution)/shard_map/ppermute | solution.py:463
  11.4 1.8 %collective-permute-start.2 = (f32[264,128]{1,0:T(8,128)S(1)}, f32[264,128]{1,0:T(8,128)S(1)}, u32[]{:S(2)}, u32[]{:S(2)}) collective-permute-start(f32[264,128]{1,0:T(8,128)S(1)} %get-tuple-element.53.refs_8_.refs_0_), channel_id=1, source_target_pairs={{0,1},{8,9},{16,17},{24,25},{1,0},{9,8},{17,16},{25,24},{2,3},{10,... | collective-permute-start | bytes 405512 | tf_op jit(solution)/shard_map/ppermute | solution.py:463
  13.2 1.5 %collective-permute-start.5 = (f32[264,128]{1,0:T(8,128)S(1)}, f32[264,128]{1,0:T(8,128)S(1)}, u32[]{:S(2)}, u32[]{:S(2)}) collective-permute-start(f32[264,128]{1,0:T(8,128)S(1)} %get-tuple-element.48.refs_7_.refs_0_), channel_id=1, source_target_pairs={{0,16},{8,24},{16,0},{24,8},{1,17},{9,25},{17,1},{25,9},{2,18},{10... | collective-permute-start | bytes 405512 | tf_op jit(solution)/shard_map/ppermute | solution.py:463
  14.7 0.9 %local1.1 = (f32[1024,1024]{1,0:T(8,128)S(1)}, f32[8,128]{1,0:T(8,128)S(1)}) custom-call(bf16[1024,128]{1,0:T(8,128)(2,1)S(1)} %get-tuple-element.39.refs_0_.refs_1_, bf16[1024,128]{1,0:T(8,128)(2,1)S(1)} %get-tuple-element.40.refs_1_, bf16[1024,1024]{1,0:T(8,128)(2,1)S(1)} %get-tuple-element.41.refs_2_, ...), custom_call_target="tpu_custom_call", output_to_operand_aliasing={{0}: (7, {})} | custom-call | tf_op jit(solution)/shard_map/local1/pallas_call | solution.py:41
  15.6 1.0 %collective-permute-done.2.refs_1_.refs_0_ = f32[264,128]{1,0:T(8,128)S(1)} collective-permute-done((f32[264,128]{1,0:T(8,128)S(1)}, f32[264,128]{1,0:T(8,128)S(1)}, u32[]{:S(2)}, u32[]{:S(2)}) %collective-permute-start.2) | collective-permute-done | bytes 135200 | tf_op jit(solution)/shard_map/ppermute | solution.py:463
  16.7 1.8 %collective-permute-start.4 = (f32[264,128]{1,0:T(8,128)S(1)}, f32[264,128]{1,0:T(8,128)S(1)}, u32[]{:S(2)}, u32[]{:S(2)}) collective-permute-start(f32[264,128]{1,0:T(8,128)S(1)} %get-tuple-element.57.refs_8_.refs_0_.refs_1_), channel_id=1, source_target_pairs={{0,2},{8,10},{16,18},{24,26},{1,3},{9,11},{17,19},{25,27},{2,0},{1... | collective-permute-start | bytes 405512 | tf_op jit(solution)/shard_map/ppermute | solution.py:463
  18.4 1.6 %collective-permute-start.7 = (f32[256,128]{1,0:T(8,128)S(1)}, f32[256,128]{1,0:T(8,128)S(1)}, u32[]{:S(2)}, u32[]{:S(2)}) collective-permute-start(f32[256,128]{1,0:T(8,128)S(1)} %found2.1.refs_0_), channel_id=1, source_target_pairs={{0,16},{8,24},{16,0},{24,8},{1,17},{9,25},{17,1},{25,9},{2,18},{10... | collective-permute-start | bytes 393224 | tf_op jit(solution)/shard_map/ppermute | solution.py:463
  20.0 0.9 %local2.1 = (f32[1024,1024]{1,0:T(8,128)S(1)}, f32[8,128]{1,0:T(8,128)S(1)}) custom-call(bf16[1024,128]{1,0:T(8,128)(2,1)S(1)} %get-tuple-element.39.refs_0_.refs_1_, bf16[1024,128]{1,0:T(8,128)(2,1)S(1)} %get-tuple-element.40.refs_1_, bf16[1024,1024]{1,0:T(8,128)(2,1)S(1)} %get-tuple-element.41.refs_2_, ...), custom_call_target="tpu_custom_call", output_to_operand_aliasing={{0}: (7, {})} | custom-call | tf_op jit(solution)/shard_map/local2/pallas_call | solution.py:41
  20.9 0.8 %collective-permute-done.4.refs_1_.refs_0_ = f32[264,128]{1,0:T(8,128)S(1)} collective-permute-done((f32[264,128]{1,0:T(8,128)S(1)}, f32[264,128]{1,0:T(8,128)S(1)}, u32[]{:S(2)}, u32[]{:S(2)}) %collective-permute-start.4) | collective-permute-done | bytes 135200 | tf_op jit(solution)/shard_map/ppermute | solution.py:463
  21.8 1.7 %collective-permute-done.7.refs_1_ = f32[256,128]{1,0:T(8,128)S(1)} collective-permute-done((f32[256,128]{1,0:T(8,128)S(1)}, f32[256,128]{1,0:T(8,128)S(1)}, u32[]{:S(2)}, u32[]{:S(2)}) %collective-permute-start.7) | collective-permute-done | bytes 131104 | tf_op jit(solution)/shard_map/ppermute | solution.py:463
  24.1 2.6 %collective-permute-start.11 = (f32[264,128]{1,0:T(8,128)S(1)}, f32[264,128]{1,0:T(8,128)S(1)}, u32[]{:S(2)}, u32[]{:S(2)}) collective-permute-start(f32[264,128]{1,0:T(8,128)S(1)} %get-tuple-element.61.refs_8_.refs_1_.refs_3_), channel_id=1, source_target_pairs={{0,4},{8,12},{16,20},{24,28},{1,5},{9,13},{17,21},{25,29},{2,6},{1... | collective-permute-start | bytes 405512 | tf_op jit(solution)/shard_map/ppermute | solution.py:463
  26.7 1.5 %collective-permute-start.9 = (f32[256,128]{1,0:T(8,128)S(1)}, f32[256,128]{1,0:T(8,128)S(1)}, u32[]{:S(2)}, u32[]{:S(2)}) collective-permute-start(f32[256,128]{1,0:T(8,128)S(1)} %found3.1.refs_2_), channel_id=1, source_target_pairs={{0,16},{8,24},{16,0},{24,8},{1,17},{9,25},{17,1},{25,9},{2,18},{10... | collective-permute-start | bytes 393224 | tf_op jit(solution)/shard_map/ppermute | solution.py:463
  28.2 3.7 %collective-permute-done.9.refs_8_ = f32[256,128]{1,0:T(8,128)S(1)} collective-permute-done((f32[256,128]{1,0:T(8,128)S(1)}, f32[256,128]{1,0:T(8,128)S(1)}, u32[]{:S(2)}, u32[]{:S(2)}) %collective-permute-start.9) | collective-permute-done | bytes 131104 | tf_op jit(solution)/shard_map/ppermute | solution.py:463
  31.9 1.6 %local3.1 = (f32[1024,1024]{1,0:T(8,128)S(1)}, f32[8,128]{1,0:T(8,128)}) custom-call(bf16[1024,128]{1,0:T(8,128)(2,1)S(1)} %get-tuple-element.39.refs_0_.refs_1_, bf16[1024,128]{1,0:T(8,128)(2,1)S(1)} %get-tuple-element.40.refs_1_, bf16[1024,1024]{1,0:T(8,128)(2,1)S(1)} %get-tuple-element.41.refs_2_, ...), custom_call_target="tpu_custom_call", output_to_operand_aliasing={{0}: (7, {})} | custom-call | tf_op jit(solution)/shard_map/local3/pallas_call | solution.py:41
  33.4 2.7 %reach0.1 = (f32[1024,1024]{1,0:T(8,128)S(1)}, f32[8,128]{1,0:T(8,128)S(1)}) custom-call(f32[1024,1024]{1,0:T(8,128)S(1)} %get-tuple-element.62.refs_0_, bf16[1024,128]{1,0:T(8,128)(2,1)S(1)} %get-tuple-element.39.refs_0_.refs_1_, f32[2,8,1024]{2,1,0:T(8,128)S(1)} %get-tuple-element.42.refs_3_.refs_2_, ...), custom_call_target="tpu_custom_call", output_to_operand_aliasing={{0}: (0, {})} | custom-call | tf_op jit(solution)/shard_map/reach0/pallas_call | solution.py:41
  36.7 1.5 %collective-permute-start.12 = (f32[256,128]{1,0:T(8,128)S(1)}, f32[256,128]{1,0:T(8,128)S(1)}, u32[]{:S(2)}, u32[]{:S(2)}) collective-permute-start(f32[256,128]{1,0:T(8,128)S(1)} %state.1.refs_10_.refs_6_), channel_id=1, source_target_pairs={{0,16},{8,24},{16,0},{24,8},{1,17},{9,25},{17,1},{25,9},{2,18},{10... | collective-permute-start | bytes 393224 | tf_op jit(solution)/shard_map/ppermute | solution.py:463
  38.2 3.1 %reach2.1 = (f32[1024,1024]{1,0:T(8,128)S(1)}, f32[8,128]{1,0:T(8,128)}) custom-call(f32[1024,1024]{1,0:T(8,128)S(1)} %get-tuple-element.63.refs_0_, bf16[1024,128]{1,0:T(8,128)(2,1)S(1)} %get-tuple-element.39.refs_0_.refs_1_, f32[2,8,1024]{2,1,0:T(8,128)S(1)} %get-tuple-element.42.refs_3_.refs_2_, ...), custom_call_target="tpu_custom_call", output_to_operand_aliasing={{0}: (0, {})} | custom-call | tf_op jit(solution)/shard_map/reach2/pallas_call | solution.py:41
  41.4 1.9 %finish00.1 = (bf16[1024,1024]{1,0:T(8,128)(2,1)}, f32[8,128]{1,0:T(8,128)}) custom-call(f32[1024,1024]{1,0:T(8,128)S(1)} %get-tuple-element.65.refs_0_, bf16[1024,128]{1,0:T(8,128)(2,1)S(1)} %get-tuple-element.39.refs_0_.refs_1_, f32[2,8,1024]{2,1,0:T(8,128)S(1)} %get-tuple-element.42.refs_3_.refs_2_, f32[8,8,1024]{2,1,0:T(8,128)S(1)} %get-tuple-element.44.refs_5_.refs_3_, ...), custom_call_target="tpu_custom_call" | custom-call | tf_op jit(solution)/shard_map/finish00/pallas_call | solution.py:437
  43.3 1.3 %finish10.1 = (bf16[1024,1024]{1,0:T(8,128)(2,1)}, f32[8,128]{1,0:T(8,128)S(1)}) custom-call(f32[1024,1024]{1,0:T(8,128)S(1)} %get-tuple-element.65.refs_0_, bf16[1024,128]{1,0:T(8,128)(2,1)S(1)} %get-tuple-element.39.refs_0_.refs_1_, f32[2,8,1024]{2,1,0:T(8,128)S(1)} %get-tuple-element.42.refs_3_.refs_2_, ...), custom_call_target="tpu_custom_call", output_to_operand_aliasing={{0}: (7, {})} | custom-call | tf_op jit(solution)/shard_map/finish10/pallas_call | solution.py:437
  44.8 1.9 %finish01.1 = (bf16[1024,1024]{1,0:T(8,128)(2,1)}, f32[8,128]{1,0:T(8,128)}) custom-call(f32[1024,1024]{1,0:T(8,128)S(1)} %get-tuple-element.65.refs_0_, bf16[1024,128]{1,0:T(8,128)(2,1)S(1)} %get-tuple-element.39.refs_0_.refs_1_, f32[2,8,1024]{2,1,0:T(8,128)S(1)} %get-tuple-element.42.refs_3_.refs_2_, ...), custom_call_target="tpu_custom_call", output_to_operand_aliasing={{0}: (7, {})} | custom-call | tf_op jit(solution)/shard_map/finish01/pallas_call | solution.py:437
  46.7 1.9 %finish11.1 = (bf16[1024,1024]{1,0:T(8,128)(2,1)}, f32[8,128]{1,0:T(8,128)}) custom-call(f32[1024,1024]{1,0:T(8,128)S(1)} %get-tuple-element.65.refs_0_, bf16[1024,128]{1,0:T(8,128)(2,1)S(1)} %get-tuple-element.39.refs_0_.refs_1_, f32[2,8,1024]{2,1,0:T(8,128)S(1)} %get-tuple-element.42.refs_3_.refs_2_, ...), custom_call_target="tpu_custom_call", output_to_operand_aliasing={{0}: (7, {})} | custom-call | tf_op jit(solution)/shard_map/finish11/pallas_call | solution.py:437
  (28 shorter events, 2.8 us)
Async XLA Ops:
  2.8 1.7 %collective-permute-start = (f32[520,128]{1,0:T(8,128)S(1)}, f32[520,128]{1,0:T(8,128)S(1)}, u32[]{:S(2)}, u32[]{:S(2)}) collective-permute-start(f32[520,128]{1,0:T(8,128)S(1)} %get-tuple-element.47), channel_id=1, source_target_pairs={{0,8},{8,0},{16,24},{24,16},{1,9},{9,1},{17,25},{25,17},{2,10},{10... | collective-permute-start | bytes 798728 | tf_op jit(solution)/shard_map/ppermute | solution.py:463
  4.6 6.8 %collective-permute-start.1 = (f32[264,128]{1,0:T(8,128)S(1)}, f32[264,128]{1,0:T(8,128)S(1)}, u32[]{:S(2)}, u32[]{:S(2)}) collective-permute-start(f32[264,128]{1,0:T(8,128)S(1)} %get-tuple-element.50), channel_id=1, source_target_pairs={{0,16},{8,24},{16,0},{24,8},{1,17},{9,25},{17,1},{25,9},{2,18},{10... | collective-permute-start | bytes 405512 | tf_op jit(solution)/shard_map/ppermute | solution.py:463
  7.5 8.1 %collective-permute-start.3 = (f32[520,128]{1,0:T(8,128)S(1)}, f32[520,128]{1,0:T(8,128)S(1)}, u32[]{:S(2)}, u32[]{:S(2)}) collective-permute-start(f32[520,128]{1,0:T(8,128)S(1)} %get-tuple-element.46.refs_0_), channel_id=1, source_target_pairs={{0,8},{8,0},{16,24},{24,16},{1,9},{9,1},{17,25},{25,17},{2,10},{10... | collective-permute-start | bytes 798728 | tf_op jit(solution)/shard_map/ppermute | solution.py:463
  11.4 5.2 %collective-permute-start.2 = (f32[264,128]{1,0:T(8,128)S(1)}, f32[264,128]{1,0:T(8,128)S(1)}, u32[]{:S(2)}, u32[]{:S(2)}) collective-permute-start(f32[264,128]{1,0:T(8,128)S(1)} %get-tuple-element.53.refs_8_.refs_0_), channel_id=1, source_target_pairs={{0,1},{8,9},{16,17},{24,25},{1,0},{9,8},{17,16},{25,24},{2,3},{10,... | collective-permute-start | bytes 405512 | tf_op jit(solution)/shard_map/ppermute | solution.py:463
  13.2 6.8 %collective-permute-start.5 = (f32[264,128]{1,0:T(8,128)S(1)}, f32[264,128]{1,0:T(8,128)S(1)}, u32[]{:S(2)}, u32[]{:S(2)}) collective-permute-start(f32[264,128]{1,0:T(8,128)S(1)} %get-tuple-element.48.refs_7_.refs_0_), channel_id=1, source_target_pairs={{0,16},{8,24},{16,0},{24,8},{1,17},{9,25},{17,1},{25,9},{2,18},{10... | collective-permute-start | bytes 405512 | tf_op jit(solution)/shard_map/ppermute | solution.py:463
  16.7 5.1 %collective-permute-start.4 = (f32[264,128]{1,0:T(8,128)S(1)}, f32[264,128]{1,0:T(8,128)S(1)}, u32[]{:S(2)}, u32[]{:S(2)}) collective-permute-start(f32[264,128]{1,0:T(8,128)S(1)} %get-tuple-element.57.refs_8_.refs_0_.refs_1_), channel_id=1, source_target_pairs={{0,2},{8,10},{16,18},{24,26},{1,3},{9,11},{17,19},{25,27},{2,0},{1... | collective-permute-start | bytes 405512 | tf_op jit(solution)/shard_map/ppermute | solution.py:463
  18.4 5.0 %collective-permute-start.7 = (f32[256,128]{1,0:T(8,128)S(1)}, f32[256,128]{1,0:T(8,128)S(1)}, u32[]{:S(2)}, u32[]{:S(2)}) collective-permute-start(f32[256,128]{1,0:T(8,128)S(1)} %found2.1.refs_0_), channel_id=1, source_target_pairs={{0,16},{8,24},{16,0},{24,8},{1,17},{9,25},{17,1},{25,9},{2,18},{10... | collective-permute-start | bytes 393224 | tf_op jit(solution)/shard_map/ppermute | solution.py:463
  23.5 14.7 %collective-permute-start.8 = (f32[768,128]{1,0:T(8,128)S(1)}, f32[768,128]{1,0:T(8,128)S(1)}, u32[]{:S(2)}, u32[]{:S(2)}) collective-permute-start(f32[768,128]{1,0:T(8,128)S(1)} %near2.1.refs_6_), channel_id=1, source_target_pairs={{0,8},{8,0},{16,24},{24,16},{1,9},{9,1},{17,25},{25,17},{2,10},{10... | collective-permute-start | bytes 1179656 | tf_op jit(solution)/shard_map/ppermute | solution.py:463
  23.6 9.9 %collective-permute-start.6 = (f32[512,128]{1,0:T(8,128)S(1)}, f32[512,128]{1,0:T(8,128)S(1)}, u32[]{:S(2)}, u32[]{:S(2)}) collective-permute-start(f32[512,128]{1,0:T(8,128)S(1)} %near1.1.refs_8_), channel_id=1, source_target_pairs={{0,8},{8,0},{16,24},{24,16},{1,9},{9,1},{17,25},{25,17},{2,10},{10... | collective-permute-start | bytes 786440 | tf_op jit(solution)/shard_map/ppermute | solution.py:463
  24.1 12.0 %collective-permute-start.11 = (f32[264,128]{1,0:T(8,128)S(1)}, f32[264,128]{1,0:T(8,128)S(1)}, u32[]{:S(2)}, u32[]{:S(2)}) collective-permute-start(f32[264,128]{1,0:T(8,128)S(1)} %get-tuple-element.61.refs_8_.refs_1_.refs_3_), channel_id=1, source_target_pairs={{0,4},{8,12},{16,20},{24,28},{1,5},{9,13},{17,21},{25,29},{2,6},{1... | collective-permute-start | bytes 405512 | tf_op jit(solution)/shard_map/ppermute | solution.py:463
  26.7 5.2 %collective-permute-start.9 = (f32[256,128]{1,0:T(8,128)S(1)}, f32[256,128]{1,0:T(8,128)S(1)}, u32[]{:S(2)}, u32[]{:S(2)}) collective-permute-start(f32[256,128]{1,0:T(8,128)S(1)} %found3.1.refs_2_), channel_id=1, source_target_pairs={{0,16},{8,24},{16,0},{24,8},{1,17},{9,25},{17,1},{25,9},{2,18},{10... | collective-permute-start | bytes 393224 | tf_op jit(solution)/shard_map/ppermute | solution.py:463
  31.9 6.4 %collective-permute-start.10 = (f32[256,128]{1,0:T(8,128)S(1)}, f32[256,128]{1,0:T(8,128)S(1)}, u32[]{:S(2)}, u32[]{:S(2)}) collective-permute-start(f32[256,128]{1,0:T(8,128)S(1)} %collective-permute-done.9.refs_8_), channel_id=1, source_target_pairs={{0,8},{8,0},{16,24},{24,16},{1,9},{9,1},{17,25},{25,17},{2,10},{10... | collective-permute-start | bytes 393224 | tf_op jit(solution)/shard_map/ppermute | solution.py:463
  36.1 7.2 %collective-permute-start.13 = (f32[256,128]{1,0:T(8,128)S(1)}, f32[256,128]{1,0:T(8,128)S(1)}, u32[]{:S(2)}, u32[]{:S(2)}) collective-permute-start(f32[256,128]{1,0:T(8,128)S(1)} %state.1.refs_10_.refs_6_), channel_id=1, source_target_pairs={{0,8},{8,0},{16,24},{24,16},{1,9},{9,1},{17,25},{25,17},{2,10},{10... | collective-permute-start | bytes 393224 | tf_op jit(solution)/shard_map/ppermute | solution.py:463
  36.7 8.0 %collective-permute-start.12 = (f32[256,128]{1,0:T(8,128)S(1)}, f32[256,128]{1,0:T(8,128)S(1)}, u32[]{:S(2)}, u32[]{:S(2)}) collective-permute-start(f32[256,128]{1,0:T(8,128)S(1)} %state.1.refs_10_.refs_6_), channel_id=1, source_target_pairs={{0,16},{8,24},{16,0},{24,8},{1,17},{9,25},{17,1},{25,9},{2,18},{10... | collective-permute-start | bytes 393224 | tf_op jit(solution)/shard_map/ppermute | solution.py:463
  44.7 2.0 %collective-permute-start.14 = (f32[256,128]{1,0:T(8,128)S(1)}, f32[256,128]{1,0:T(8,128)S(1)}, u32[]{:S(2)}, u32[]{:S(2)}) collective-permute-start(f32[256,128]{1,0:T(8,128)S(1)} %beside.1.refs_6_), channel_id=1, source_target_pairs={{0,8},{8,0},{16,24},{24,16},{1,9},{9,1},{17,25},{25,17},{2,10},{10... | collective-permute-start | bytes 393224 | tf_op jit(solution)/shard_map/ppermute | solution.py:463

commit v9 on v8

--- a/solution.py
+++ b/solution.py
@@ -344,8 +344,6 @@
     heads = weight_ref.shape[1]
     head_width = mixed_ref.shape[0] // heads
     take_levels(plan, part_refs, levels, heads)
-    parts = [slice(head * head_width, (head + 1) * head_width) for head in range(heads)]
-    states = [[levels[slot, rows] for slot in range(len(bits))] for rows in parts]
     for span in range(q_ref.shape[0] // SPAN):
         tokens = slice(span * SPAN, (span + 1) * SPAN)
         queries = q_ref[tokens]
@@ -353,13 +351,15 @@
             level_scale(bit, first_level, prefix_ref, sums_ref, weight_ref, tokens)
             for bit, prefix_ref in zip(bits, prefix_refs)
         ]
-        mixed = [mixed_ref[rows, tokens] for rows in parts]
         for head in range(heads):
-            for state, scale in zip(states[head], scales):
-                found = lax.dot_general(state, queries, NT, preferred_element_type=jnp.float32)
-                mixed[head] = mixed[head] + found * scale[head : head + 1]
-        for head, rows in enumerate(parts):
-            out_ref[rows, tokens] = mixed[head]
+            rows = slice(head * head_width, (head + 1) * head_width)
+            mixed = mixed_ref[rows, tokens]
+            for slot, scale in enumerate(scales):
+                found = lax.dot_general(
+                    levels[slot, rows], queries, NT, preferred_element_type=jnp.float32
+                )
+                mixed = mixed + found * scale[head : head + 1]
+            out_ref[rows, tokens] = mixed
 
 
 def add_levels(mixed, queries, sums, level_weight, levels, parts, first_level, tokens=()):
@@ -379,7 +379,7 @@
 
 def finish_kernel(far, bit, first_level, *refs):
     mixed_ref, q_ref, sums_ref, weight_ref, gain_ref, prefix_ref, state_ref = refs[:7]
-    out_hbm, done_ref, out_ref, level, sent = refs[-5:]
+    out_hbm, done_ref, out_ref, level, scale_ref, sent = refs[-6:]
     done_ref[...] = jnp.zeros_like(done_ref)
     heads = weight_ref.shape[1]
     head_width = mixed_ref.shape[0] // heads
@@ -391,36 +391,25 @@
         row = jnp.broadcast_to(gain_ref[pl.ds(first + slot, 1)], (8, head_width))
         gains.append(row.T[:, :1])
     columns = pl.ds(pl.multiple_of(first * head_width, 128), count * head_width)
-    spans = q_ref.shape[0] // SPAN
-    states = [level[slot * head_width : (slot + 1) * head_width] for slot in range(count)]
     copies = []
-    for begin in range(0, spans, 2):
-        batch = [slice(span * SPAN, (span + 1) * SPAN) for span in range(begin, min(begin + 2, spans))]
-        results = []
-        for tokens in batch:
-            queries = q_ref[tokens]
-            active = jnp.where(bit_of(place(), bit) == 1, 1.0, 0.0)
-            for slot in range(count):
-                row = pl.ds(first + slot, 1)
-                reach = jnp.exp(sums_ref[1, row, tokens] + prefix_ref[row][:, :1])
-                scale = reach * weight_ref[first_level + bit, row, tokens] * active
-                found = lax.dot_general(
-                    states[slot], queries, NT, preferred_element_type=jnp.float32
-                )
-                start = pl.multiple_of((first + slot) * head_width, 128)
-                mixed = mixed_ref[pl.ds(start, head_width), tokens] + found * scale
-                square = jnp.mean(mixed * mixed, axis=0, keepdims=True)
-                normed = mixed * lax.rsqrt(square + EPS) * gains[slot]
-                rows = slice(slot * head_width, (slot + 1) * head_width)
-                results.append((tokens, rows, normed.astype(jnp.bfloat16).T))
-        for tokens, rows, result in results:
-            out_ref[tokens, rows] = result
-        for tokens in batch:
-            copy = pltpu.make_async_copy(
-                out_ref.at[tokens], out_hbm.at[tokens, columns], sent.at[len(copies)]
-            )
-            copy.start()
-            copies.append(copy)
+    for span in range(q_ref.shape[0] // SPAN):
+        tokens = slice(span * SPAN, (span + 1) * SPAN)
+        queries = q_ref[tokens]
+        scale_ref[...] = level_scale(bit, first_level, prefix_ref, sums_ref, weight_ref, tokens)
+        for slot in range(count):
+            rows = slice(slot * head_width, (slot + 1) * head_width)
+            found = lax.dot_general(level[rows], queries, NT, preferred_element_type=jnp.float32)
+            start = pl.multiple_of((first + slot) * head_width, 128)
+            mixed = mixed_ref[pl.ds(start, head_width), tokens]
+            mixed = mixed + found * scale_ref[pl.ds(first + slot, 1)]
+            square = jnp.mean(mixed * mixed, axis=0, keepdims=True)
+            normed = mixed * lax.rsqrt(square + EPS) * gains[slot]
+            out_ref[tokens, rows] = normed.astype(jnp.bfloat16).T
+        copy = pltpu.make_async_copy(
+            out_ref.at[tokens], out_hbm.at[tokens, columns], sent.at[span]
+        )
+        copy.start()
+        copies.append(copy)
     for copy in copies:
         copy.wait()
 
@@ -445,6 +434,7 @@
         scratch_shapes=[
             pltpu.VMEM((tokens, width >> len(far)), jnp.bfloat16),
             pltpu.VMEM((width >> len(far), queries.shape[1]), jnp.bfloat16),
+            pltpu.VMEM((level_weight.shape[1], SPAN), jnp.float32),
             pltpu.SemaphoreType.DMA((tokens // SPAN,)),
         ],
         input_output_aliases={} if begun is None else {7: 0},
@@ -527,7 +517,8 @@
         pieces += [(found[bit], two), (across[bit], two)]
     near = pack("near2", [*pieces, (found[last - 1], two)], (chunks[0],))
     far = trade(near, 1)
-    near_side, far_side = across[last - 1], trade(across[last - 1], 1)
+    near_side = pack("side", [(across[last - 1], two)], (token,))
+    far_side = trade(near_side, 1)
     levels = []
     for slot, bit in enumerate(range(2, last)):
         taken = [

time: 48.9 us -> 45.5 us (0.930)
  waiting for transfers between devices: 11.4 us -> 8.74 us
  starting transfers between devices: 17 us -> 16.5 us
    ppermute x15, waiting for transfers between devices: 11.4 us -> 8.74 us  [trade(): return lax.ppermute(value, AXES, pairs)]
    ppermute x15, starting transfers between devices: 17 us -> 16.5 us  [trade(): return lax.ppermute(value, AXES, pairs)]
    pallas_call x17 -> x18, Pallas kernels: 13 us -> 13 us  [call(): pl.pallas_call(kernel, in_specs=specs, out_specs=[HELD] * len(outputs), o...]
  transfers between devices with their start and end apart: 15 -> 15, of which waited for: 6 -> 6; matrix products, arithmetic and copies ran while one was open for 0% -> 0% of each run, Pallas kernels for 31% -> 34%
where the time goes in v9:
time: 45.5 us; the launch traced here: 45.4 us
  Pallas kernels  20 us (44%)
  starting transfers between devices  16.5 us (36%)
  waiting for transfers between devices  8.74 us (19%)
    ppermute x15, starting transfers between devices, trade(): return lax.ppermute(value, AXES, pairs)  16.5 us
    pallas_call x18, Pallas kernels, call(): pl.pallas_call(kernel, in_specs=specs, out_specs=[HELD] * len(outputs), o...  13 us
    ppermute x15, waiting for transfers between devices, trade(): return lax.ppermute(value, AXES, pairs)  8.74 us
    pallas_call x4, Pallas kernels, finish(): pl.pallas_call(functools.partial(finish_kernel, far, bit, first_level), i...  6.97 us
  transfers between devices with their start and end apart: 15, of which 6 were waited for; matrix products, arithmetic and copies ran while one was open for 0% of the time, Pallas kernels for 34%

profile of v9, /device:TPU:0, one launch (start us, length us, event | category | flops | bytes accessed | tf_op | source)
XLA Modules:
  0.0 45.4 jit_solution(13868723696874071211)
XLA Ops:
  0.0 2.8 %states.1 = (f32[520,128]{1,0:T(8,128)S(1)}, f32[520,128]{1,0:T(8,128)S(1)}, bf16[3,128,1024]{2,1,0:T(8,128)(2,1)S(1)}, f32[2,8,1024]{2,1,0:T(8,128)S(1)}, f32[4...) custom-call(bf16[1024,128]{1,0:T(8,128)(2,1)} %refs_0_.1, ...), custom_call_target="tpu_custom_call" | custom-call | tf_op jit(solution)/shard_map/states/pallas_call | solution.py:41
  3.3 1.2 %collective-permute-done.refs_1_.refs_6_ = f32[520,128]{1,0:T(8,128)S(1)} collective-permute-done((f32[520,128]{1,0:T(8,128)S(1)}, f32[520,128]{1,0:T(8,128)S(1)}, u32[]{:S(2)}, u32[]{:S(2)}) %collective-permute-start) | collective-permute-done | bytes 266272 | tf_op jit(solution)/shard_map/ppermute | solution.py:453
  4.6 2.9 %collective-permute-start.1 = (f32[264,128]{1,0:T(8,128)S(1)}, f32[264,128]{1,0:T(8,128)S(1)}, u32[]{:S(2)}, u32[]{:S(2)}) collective-permute-start(f32[264,128]{1,0:T(8,128)S(1)} %get-tuple-element.50), channel_id=1, source_target_pairs={{0,16},{8,24},{16,0},{24,8},{1,17},{9,25},{17,1},{25,9},{2,18},{10... | collective-permute-start | bytes 405512 | tf_op jit(solution)/shard_map/ppermute | solution.py:453
  7.5 0.8 %local0.1 = (f32[1024,1024]{1,0:T(8,128)S(1)}, f32[8,128]{1,0:T(8,128)S(1)}) custom-call(bf16[1024,128]{1,0:T(8,128)(2,1)S(1)} %get-tuple-element.39.refs_0_.refs_1_, bf16[1024,128]{1,0:T(8,128)(2,1)S(1)} %get-tuple-element.40.refs_1_, bf16[1024,1024]{1,0:T(8,128)(2,1)S(1)} %get-tuple-element.41.refs_2_, ...), custom_call_target="tpu_custom_call" | custom-call | tf_op jit(solution)/shard_map/local0/pallas_call | solution.py:41
  8.3 3.1 %collective-permute-done.1.refs_1_.refs_0_ = f32[264,128]{1,0:T(8,128)S(1)} collective-permute-done((f32[264,128]{1,0:T(8,128)S(1)}, f32[264,128]{1,0:T(8,128)S(1)}, u32[]{:S(2)}, u32[]{:S(2)}) %collective-permute-start.1) | collective-permute-done | bytes 135200 | tf_op jit(solution)/shard_map/ppermute | solution.py:453
  11.4 1.8 %collective-permute-start.2 = (f32[264,128]{1,0:T(8,128)S(1)}, f32[264,128]{1,0:T(8,128)S(1)}, u32[]{:S(2)}, u32[]{:S(2)}) collective-permute-start(f32[264,128]{1,0:T(8,128)S(1)} %get-tuple-element.53.refs_8_.refs_0_), channel_id=1, source_target_pairs={{0,1},{8,9},{16,17},{24,25},{1,0},{9,8},{17,16},{25,24},{2,3},{10,... | collective-permute-start | bytes 405512 | tf_op jit(solution)/shard_map/ppermute | solution.py:453
  13.2 1.5 %collective-permute-start.5 = (f32[264,128]{1,0:T(8,128)S(1)}, f32[264,128]{1,0:T(8,128)S(1)}, u32[]{:S(2)}, u32[]{:S(2)}) collective-permute-start(f32[264,128]{1,0:T(8,128)S(1)} %get-tuple-element.48.refs_7_.refs_0_), channel_id=1, source_target_pairs={{0,16},{8,24},{16,0},{24,8},{1,17},{9,25},{17,1},{25,9},{2,18},{10... | collective-permute-start | bytes 405512 | tf_op jit(solution)/shard_map/ppermute | solution.py:453
  14.7 0.9 %local1.1 = (f32[1024,1024]{1,0:T(8,128)S(1)}, f32[8,128]{1,0:T(8,128)S(1)}) custom-call(bf16[1024,128]{1,0:T(8,128)(2,1)S(1)} %get-tuple-element.39.refs_0_.refs_1_, bf16[1024,128]{1,0:T(8,128)(2,1)S(1)} %get-tuple-element.40.refs_1_, bf16[1024,1024]{1,0:T(8,128)(2,1)S(1)} %get-tuple-element.41.refs_2_, ...), custom_call_target="tpu_custom_call", output_to_operand_aliasing={{0}: (7, {})} | custom-call | tf_op jit(solution)/shard_map/local1/pallas_call | solution.py:41
  15.6 1.0 %collective-permute-done.2.refs_1_.refs_0_ = f32[264,128]{1,0:T(8,128)S(1)} collective-permute-done((f32[264,128]{1,0:T(8,128)S(1)}, f32[264,128]{1,0:T(8,128)S(1)}, u32[]{:S(2)}, u32[]{:S(2)}) %collective-permute-start.2) | collective-permute-done | bytes 135200 | tf_op jit(solution)/shard_map/ppermute | solution.py:453
  16.7 1.8 %collective-permute-start.4 = (f32[264,128]{1,0:T(8,128)S(1)}, f32[264,128]{1,0:T(8,128)S(1)}, u32[]{:S(2)}, u32[]{:S(2)}) collective-permute-start(f32[264,128]{1,0:T(8,128)S(1)} %get-tuple-element.57.refs_8_.refs_0_.refs_1_), channel_id=1, source_target_pairs={{0,2},{8,10},{16,18},{24,26},{1,3},{9,11},{17,19},{25,27},{2,0},{1... | collective-permute-start | bytes 405512 | tf_op jit(solution)/shard_map/ppermute | solution.py:453
  18.4 1.6 %collective-permute-start.7 = (f32[256,128]{1,0:T(8,128)S(1)}, f32[256,128]{1,0:T(8,128)S(1)}, u32[]{:S(2)}, u32[]{:S(2)}) collective-permute-start(f32[256,128]{1,0:T(8,128)S(1)} %found2.1.refs_0_), channel_id=1, source_target_pairs={{0,16},{8,24},{16,0},{24,8},{1,17},{9,25},{17,1},{25,9},{2,18},{10... | collective-permute-start | bytes 393224 | tf_op jit(solution)/shard_map/ppermute | solution.py:453
  20.1 0.9 %local2.1 = (f32[1024,1024]{1,0:T(8,128)S(1)}, f32[8,128]{1,0:T(8,128)S(1)}) custom-call(bf16[1024,128]{1,0:T(8,128)(2,1)S(1)} %get-tuple-element.39.refs_0_.refs_1_, bf16[1024,128]{1,0:T(8,128)(2,1)S(1)} %get-tuple-element.40.refs_1_, bf16[1024,1024]{1,0:T(8,128)(2,1)S(1)} %get-tuple-element.41.refs_2_, ...), custom_call_target="tpu_custom_call", output_to_operand_aliasing={{0}: (7, {})} | custom-call | tf_op jit(solution)/shard_map/local2/pallas_call | solution.py:41
  21.8 1.7 %collective-permute-done.7.refs_1_ = f32[256,128]{1,0:T(8,128)S(1)} collective-permute-done((f32[256,128]{1,0:T(8,128)S(1)}, f32[256,128]{1,0:T(8,128)S(1)}, u32[]{:S(2)}, u32[]{:S(2)}) %collective-permute-start.7) | collective-permute-done | bytes 131104 | tf_op jit(solution)/shard_map/ppermute | solution.py:453
  23.6 2.7 %collective-permute-start.11 = (f32[264,128]{1,0:T(8,128)S(1)}, f32[264,128]{1,0:T(8,128)S(1)}, u32[]{:S(2)}, u32[]{:S(2)}) collective-permute-start(f32[264,128]{1,0:T(8,128)S(1)} %get-tuple-element.61.refs_8_.refs_1_.refs_3_), channel_id=1, source_target_pairs={{0,4},{8,12},{16,20},{24,28},{1,5},{9,13},{17,21},{25,29},{2,6},{1... | collective-permute-start | bytes 405512 | tf_op jit(solution)/shard_map/ppermute | solution.py:453
  26.2 1.5 %collective-permute-start.9 = (f32[256,128]{1,0:T(8,128)S(1)}, f32[256,128]{1,0:T(8,128)S(1)}, u32[]{:S(2)}, u32[]{:S(2)}) collective-permute-start(f32[256,128]{1,0:T(8,128)S(1)} %found3.1.refs_2_), channel_id=1, source_target_pairs={{0,16},{8,24},{16,0},{24,8},{1,17},{9,25},{17,1},{25,9},{2,18},{10... | collective-permute-start | bytes 393224 | tf_op jit(solution)/shard_map/ppermute | solution.py:453
  27.7 1.6 %local3.1 = (f32[1024,1024]{1,0:T(8,128)S(1)}, f32[8,128]{1,0:T(8,128)}) custom-call(bf16[1024,128]{1,0:T(8,128)(2,1)S(1)} %get-tuple-element.39.refs_0_.refs_1_, bf16[1024,128]{1,0:T(8,128)(2,1)S(1)} %get-tuple-element.40.refs_1_, bf16[1024,1024]{1,0:T(8,128)(2,1)S(1)} %get-tuple-element.41.refs_2_, ...), custom_call_target="tpu_custom_call", output_to_operand_aliasing={{0}: (7, {})} | custom-call | tf_op jit(solution)/shard_map/local3/pallas_call | solution.py:41
  29.3 2.7 %reach0.1 = (f32[1024,1024]{1,0:T(8,128)S(1)}, f32[8,128]{1,0:T(8,128)S(1)}) custom-call(f32[1024,1024]{1,0:T(8,128)S(1)} %get-tuple-element.62.refs_0_, bf16[1024,128]{1,0:T(8,128)(2,1)S(1)} %get-tuple-element.39.refs_0_.refs_1_, f32[2,8,1024]{2,1,0:T(8,128)S(1)} %get-tuple-element.42.refs_3_.refs_2_, ...), custom_call_target="tpu_custom_call", output_to_operand_aliasing={{0}: (0, {})} | custom-call | tf_op jit(solution)/shard_map/reach0/pallas_call | solution.py:41
  32.1 1.1 %collective-permute-done.11.refs_0_ = f32[264,128]{1,0:T(8,128)S(1)} collective-permute-done((f32[264,128]{1,0:T(8,128)S(1)}, f32[264,128]{1,0:T(8,128)S(1)}, u32[]{:S(2)}, u32[]{:S(2)}) %collective-permute-start.11) | collective-permute-done | bytes 135200 | tf_op jit(solution)/shard_map/ppermute | solution.py:453
  33.3 1.6 %collective-permute-start.12 = (f32[256,128]{1,0:T(8,128)S(1)}, f32[256,128]{1,0:T(8,128)S(1)}, u32[]{:S(2)}, u32[]{:S(2)}) collective-permute-start(f32[256,128]{1,0:T(8,128)S(1)} %state.1.refs_10_.refs_6_), channel_id=1, source_target_pairs={{0,16},{8,24},{16,0},{24,8},{1,17},{9,25},{17,1},{25,9},{2,18},{10... | collective-permute-start | bytes 393224 | tf_op jit(solution)/shard_map/ppermute | solution.py:453
  34.9 3.2 %reach2.1 = (f32[1024,1024]{1,0:T(8,128)S(1)}, f32[8,128]{1,0:T(8,128)}) custom-call(f32[1024,1024]{1,0:T(8,128)S(1)} %get-tuple-element.63.refs_0_, bf16[1024,128]{1,0:T(8,128)(2,1)S(1)} %get-tuple-element.39.refs_0_.refs_1_, f32[2,8,1024]{2,1,0:T(8,128)S(1)} %get-tuple-element.42.refs_3_.refs_2_, ...), custom_call_target="tpu_custom_call", output_to_operand_aliasing={{0}: (0, {})} | custom-call | tf_op jit(solution)/shard_map/reach2/pallas_call | solution.py:41
  38.1 1.9 %finish00.1 = (bf16[1024,1024]{1,0:T(8,128)(2,1)}, f32[8,128]{1,0:T(8,128)}) custom-call(f32[1024,1024]{1,0:T(8,128)S(1)} %get-tuple-element.65.refs_0_, bf16[1024,128]{1,0:T(8,128)(2,1)S(1)} %get-tuple-element.39.refs_0_.refs_1_, f32[2,8,1024]{2,1,0:T(8,128)S(1)} %get-tuple-element.42.refs_3_.refs_2_, f32[8,8,1024]{2,1,0:T(8,128)S(1)} %get-tuple-element.44.refs_5_.refs_3_, ...), custom_call_target="tpu_custom_call" | custom-call | tf_op jit(solution)/shard_map/finish00/pallas_call | solution.py:426
  40.0 1.3 %finish10.1 = (bf16[1024,1024]{1,0:T(8,128)(2,1)}, f32[8,128]{1,0:T(8,128)S(1)}) custom-call(f32[1024,1024]{1,0:T(8,128)S(1)} %get-tuple-element.65.refs_0_, bf16[1024,128]{1,0:T(8,128)(2,1)S(1)} %get-tuple-element.39.refs_0_.refs_1_, f32[2,8,1024]{2,1,0:T(8,128)S(1)} %get-tuple-element.42.refs_3_.refs_2_, ...), custom_call_target="tpu_custom_call", output_to_operand_aliasing={{0}: (7, {})} | custom-call | tf_op jit(solution)/shard_map/finish10/pallas_call | solution.py:426
  41.6 1.9 %finish01.1 = (bf16[1024,1024]{1,0:T(8,128)(2,1)}, f32[8,128]{1,0:T(8,128)}) custom-call(f32[1024,1024]{1,0:T(8,128)S(1)} %get-tuple-element.65.refs_0_, bf16[1024,128]{1,0:T(8,128)(2,1)S(1)} %get-tuple-element.39.refs_0_.refs_1_, f32[2,8,1024]{2,1,0:T(8,128)S(1)} %get-tuple-element.42.refs_3_.refs_2_, ...), custom_call_target="tpu_custom_call", output_to_operand_aliasing={{0}: (7, {})} | custom-call | tf_op jit(solution)/shard_map/finish01/pallas_call | solution.py:426
  43.5 1.9 %finish11.1 = (bf16[1024,1024]{1,0:T(8,128)(2,1)}, f32[8,128]{1,0:T(8,128)}) custom-call(f32[1024,1024]{1,0:T(8,128)S(1)} %get-tuple-element.65.refs_0_, bf16[1024,128]{1,0:T(8,128)(2,1)S(1)} %get-tuple-element.39.refs_0_.refs_1_, f32[2,8,1024]{2,1,0:T(8,128)S(1)} %get-tuple-element.42.refs_3_.refs_2_, ...), custom_call_target="tpu_custom_call", output_to_operand_aliasing={{0}: (7, {})} | custom-call | tf_op jit(solution)/shard_map/finish11/pallas_call | solution.py:426
  (29 shorter events, 2.1 us)
Async XLA Ops:
  2.8 1.7 %collective-permute-start = (f32[520,128]{1,0:T(8,128)S(1)}, f32[520,128]{1,0:T(8,128)S(1)}, u32[]{:S(2)}, u32[]{:S(2)}) collective-permute-start(f32[520,128]{1,0:T(8,128)S(1)} %get-tuple-element.47), channel_id=1, source_target_pairs={{0,8},{8,0},{16,24},{24,16},{1,9},{9,1},{17,25},{25,17},{2,10},{10... | collective-permute-start | bytes 798728 | tf_op jit(solution)/shard_map/ppermute | solution.py:453
  4.6 6.8 %collective-permute-start.1 = (f32[264,128]{1,0:T(8,128)S(1)}, f32[264,128]{1,0:T(8,128)S(1)}, u32[]{:S(2)}, u32[]{:S(2)}) collective-permute-start(f32[264,128]{1,0:T(8,128)S(1)} %get-tuple-element.50), channel_id=1, source_target_pairs={{0,16},{8,24},{16,0},{24,8},{1,17},{9,25},{17,1},{25,9},{2,18},{10... | collective-permute-start | bytes 405512 | tf_op jit(solution)/shard_map/ppermute | solution.py:453
  7.5 8.1 %collective-permute-start.3 = (f32[520,128]{1,0:T(8,128)S(1)}, f32[520,128]{1,0:T(8,128)S(1)}, u32[]{:S(2)}, u32[]{:S(2)}) collective-permute-start(f32[520,128]{1,0:T(8,128)S(1)} %get-tuple-element.46.refs_0_), channel_id=1, source_target_pairs={{0,8},{8,0},{16,24},{24,16},{1,9},{9,1},{17,25},{25,17},{2,10},{10... | collective-permute-start | bytes 798728 | tf_op jit(solution)/shard_map/ppermute | solution.py:453
  11.4 5.2 %collective-permute-start.2 = (f32[264,128]{1,0:T(8,128)S(1)}, f32[264,128]{1,0:T(8,128)S(1)}, u32[]{:S(2)}, u32[]{:S(2)}) collective-permute-start(f32[264,128]{1,0:T(8,128)S(1)} %get-tuple-element.53.refs_8_.refs_0_), channel_id=1, source_target_pairs={{0,1},{8,9},{16,17},{24,25},{1,0},{9,8},{17,16},{25,24},{2,3},{10,... | collective-permute-start | bytes 405512 | tf_op jit(solution)/shard_map/ppermute | solution.py:453
  13.2 6.8 %collective-permute-start.5 = (f32[264,128]{1,0:T(8,128)S(1)}, f32[264,128]{1,0:T(8,128)S(1)}, u32[]{:S(2)}, u32[]{:S(2)}) collective-permute-start(f32[264,128]{1,0:T(8,128)S(1)} %get-tuple-element.48.refs_7_.refs_0_), channel_id=1, source_target_pairs={{0,16},{8,24},{16,0},{24,8},{1,17},{9,25},{17,1},{25,9},{2,18},{10... | collective-permute-start | bytes 405512 | tf_op jit(solution)/shard_map/ppermute | solution.py:453
  16.7 5.1 %collective-permute-start.4 = (f32[264,128]{1,0:T(8,128)S(1)}, f32[264,128]{1,0:T(8,128)S(1)}, u32[]{:S(2)}, u32[]{:S(2)}) collective-permute-start(f32[264,128]{1,0:T(8,128)S(1)} %get-tuple-element.57.refs_8_.refs_0_.refs_1_), channel_id=1, source_target_pairs={{0,2},{8,10},{16,18},{24,26},{1,3},{9,11},{17,19},{25,27},{2,0},{1... | collective-permute-start | bytes 405512 | tf_op jit(solution)/shard_map/ppermute | solution.py:453
  18.4 5.0 %collective-permute-start.7 = (f32[256,128]{1,0:T(8,128)S(1)}, f32[256,128]{1,0:T(8,128)S(1)}, u32[]{:S(2)}, u32[]{:S(2)}) collective-permute-start(f32[256,128]{1,0:T(8,128)S(1)} %found2.1.refs_0_), channel_id=1, source_target_pairs={{0,16},{8,24},{16,0},{24,8},{1,17},{9,25},{17,1},{25,9},{2,18},{10... | collective-permute-start | bytes 393224 | tf_op jit(solution)/shard_map/ppermute | solution.py:453
  20.0 9.3 %collective-permute-start.6 = (f32[512,128]{1,0:T(8,128)S(1)}, f32[512,128]{1,0:T(8,128)S(1)}, u32[]{:S(2)}, u32[]{:S(2)}) collective-permute-start(f32[512,128]{1,0:T(8,128)S(1)} %near1.1.refs_8_), channel_id=1, source_target_pairs={{0,8},{8,0},{16,24},{24,16},{1,9},{9,1},{17,25},{25,17},{2,10},{10... | collective-permute-start | bytes 786440 | tf_op jit(solution)/shard_map/ppermute | solution.py:453
  23.5 11.4 %collective-permute-start.8 = (f32[768,128]{1,0:T(8,128)S(1)}, f32[768,128]{1,0:T(8,128)S(1)}, u32[]{:S(2)}, u32[]{:S(2)}) collective-permute-start(f32[768,128]{1,0:T(8,128)S(1)} %near2.1.refs_6_), channel_id=1, source_target_pairs={{0,8},{8,0},{16,24},{24,16},{1,9},{9,1},{17,25},{25,17},{2,10},{10... | collective-permute-start | bytes 1179656 | tf_op jit(solution)/shard_map/ppermute | solution.py:453
  23.6 9.6 %collective-permute-start.11 = (f32[264,128]{1,0:T(8,128)S(1)}, f32[264,128]{1,0:T(8,128)S(1)}, u32[]{:S(2)}, u32[]{:S(2)}) collective-permute-start(f32[264,128]{1,0:T(8,128)S(1)} %get-tuple-element.61.refs_8_.refs_1_.refs_3_), channel_id=1, source_target_pairs={{0,4},{8,12},{16,20},{24,28},{1,5},{9,13},{17,21},{25,29},{2,6},{1... | collective-permute-start | bytes 405512 | tf_op jit(solution)/shard_map/ppermute | solution.py:453
  26.2 5.8 %collective-permute-start.9 = (f32[256,128]{1,0:T(8,128)S(1)}, f32[256,128]{1,0:T(8,128)S(1)}, u32[]{:S(2)}, u32[]{:S(2)}) collective-permute-start(f32[256,128]{1,0:T(8,128)S(1)} %found3.1.refs_2_), channel_id=1, source_target_pairs={{0,16},{8,24},{16,0},{24,8},{1,17},{9,25},{17,1},{25,9},{2,18},{10... | collective-permute-start | bytes 393224 | tf_op jit(solution)/shard_map/ppermute | solution.py:453
  32.0 2.9 %collective-permute-start.10 = (f32[256,128]{1,0:T(8,128)S(1)}, f32[256,128]{1,0:T(8,128)S(1)}, u32[]{:S(2)}, u32[]{:S(2)}) collective-permute-start(f32[256,128]{1,0:T(8,128)S(1)} %side.1.refs_8_), channel_id=1, source_target_pairs={{0,8},{8,0},{16,24},{24,16},{1,9},{9,1},{17,25},{25,17},{2,10},{10... | collective-permute-start | bytes 393224 | tf_op jit(solution)/shard_map/ppermute | solution.py:453
  33.2 6.8 %collective-permute-start.13 = (f32[256,128]{1,0:T(8,128)S(1)}, f32[256,128]{1,0:T(8,128)S(1)}, u32[]{:S(2)}, u32[]{:S(2)}) collective-permute-start(f32[256,128]{1,0:T(8,128)S(1)} %state.1.refs_10_.refs_6_), channel_id=1, source_target_pairs={{0,8},{8,0},{16,24},{24,16},{1,9},{9,1},{17,25},{25,17},{2,10},{10... | collective-permute-start | bytes 393224 | tf_op jit(solution)/shard_map/ppermute | solution.py:453
  33.3 8.0 %collective-permute-start.12 = (f32[256,128]{1,0:T(8,128)S(1)}, f32[256,128]{1,0:T(8,128)S(1)}, u32[]{:S(2)}, u32[]{:S(2)}) collective-permute-start(f32[256,128]{1,0:T(8,128)S(1)} %state.1.refs_10_.refs_6_), channel_id=1, source_target_pairs={{0,16},{8,24},{16,0},{24,8},{1,17},{9,25},{17,1},{25,9},{2,18},{10... | collective-permute-start | bytes 393224 | tf_op jit(solution)/shard_map/ppermute | solution.py:453
  41.3 2.1 %collective-permute-start.14 = (f32[256,128]{1,0:T(8,128)S(1)}, f32[256,128]{1,0:T(8,128)S(1)}, u32[]{:S(2)}, u32[]{:S(2)}) collective-permute-start(f32[256,128]{1,0:T(8,128)S(1)} %beside.1.refs_6_), channel_id=1, source_target_pairs={{0,8},{8,0},{16,24},{24,16},{1,9},{9,1},{17,25},{25,17},{2,10},{10... | collective-permute-start | bytes 393224 | tf_op jit(solution)/shard_map/ppermute | solution.py:453

commit v10 on v9

--- a/solution.py
+++ b/solution.py
@@ -162,15 +162,18 @@
     )
 
 
-def local_kernel(first, last, *refs):
+def local_kernel(first, last, has_token, *refs):
     q_ref, k_ref, v_ref, sums_ref, totals_ref, weight_ref, local_ref = refs[:7]
-    mixed_ref, done_ref = refs[-2:]
+    if has_token:
+        mixed_ref, done_ref = refs[-2:]
+        done_ref[...] = jnp.zeros_like(done_ref)
+    else:
+        mixed_ref = refs[-1]
     heads = weight_ref.shape[1]
     head_width = v_ref.shape[1] // heads
     spans = totals_ref.shape[0]
     local_bits = spans.bit_length() - 1
     half = SPAN // 2
-    done_ref[...] = jnp.zeros_like(done_ref)
     source = lax.broadcasted_iota(jnp.int32, (half, half), 0)
     target = lax.broadcasted_iota(jnp.int32, (half, half), 1)
     causal = source <= target
@@ -224,14 +227,14 @@
             mixed_ref[rows, tokens] = mixed
 
 
-def mix_local(first, last, shared, mixed, tokens=()):
+def mix_local(first, last, shared, mixed, tokens, has_token):
     queries, keys, values, sums, totals, level_weight, local = shared
     rest = [] if mixed is None else [mixed]
     return call(
-        functools.partial(local_kernel, first, last),
+        functools.partial(local_kernel, first, last, has_token),
         f"local{first}",
         [*shared, *rest, *tokens],
-        [(values.shape[::-1], jnp.float32), ((8, 128), jnp.float32)],
+        [(values.shape[::-1], jnp.float32), ((8, 128), jnp.float32)][: 1 + has_token],
         aliases={7: 0} if rest else None,
     )
 
@@ -377,69 +380,88 @@
     )
 
 
-def finish_kernel(far, bit, first_level, *refs):
-    mixed_ref, q_ref, sums_ref, weight_ref, gain_ref, prefix_ref, state_ref = refs[:7]
-    out_hbm, done_ref, out_ref, level, scale_ref, sent = refs[-6:]
-    done_ref[...] = jnp.zeros_like(done_ref)
+def finish_kernel(quarters, first_level, bits, has_token, *refs):
+    mixed_ref, q_ref, sums_ref, weight_ref, gain_ref = refs[:5]
+    prefix_refs = refs[5 : 5 + len(bits)]
+    part_refs = refs[5 + len(bits) :]
+    out_ref, scale_ref, sent = refs[-3:]
+    out_hbm = refs[-5] if has_token else refs[-4]
+    if has_token:
+        refs[-4][...] = jnp.zeros_like(refs[-4])
     heads = weight_ref.shape[1]
     head_width = mixed_ref.shape[0] // heads
-    count = heads >> len(far)
-    first = first_head(far, heads)
-    level[...] = state_ref[: level.shape[0]].astype(jnp.bfloat16)
-    gains = []
-    for slot in range(count):
-        row = jnp.broadcast_to(gain_ref[pl.ds(first + slot, 1)], (8, head_width))
-        gains.append(row.T[:, :1])
-    columns = pl.ds(pl.multiple_of(first * head_width, 128), count * head_width)
+    count = heads // 4
+    work = []
+    for at, (far, pieces) in enumerate(quarters):
+        first = first_head(far, heads)
+        for slot in range(count):
+            row = jnp.broadcast_to(gain_ref[pl.ds(first + slot, 1)], (8, head_width))
+            states = []
+            for index, start in pieces:
+                rows = slice(start + slot * head_width, start + (slot + 1) * head_width)
+                states.append(part_refs[index][rows].astype(jnp.bfloat16))
+            work.append((first + slot, at * count + slot, row.T[:, :1], states))
     copies = []
     for span in range(q_ref.shape[0] // SPAN):
         tokens = slice(span * SPAN, (span + 1) * SPAN)
         queries = q_ref[tokens]
-        scale_ref[...] = level_scale(bit, first_level, prefix_ref, sums_ref, weight_ref, tokens)
-        for slot in range(count):
-            rows = slice(slot * head_width, (slot + 1) * head_width)
-            found = lax.dot_general(level[rows], queries, NT, preferred_element_type=jnp.float32)
-            start = pl.multiple_of((first + slot) * head_width, 128)
+        for level, (bit, prefix_ref) in enumerate(zip(bits, prefix_refs)):
+            scale_ref[level] = level_scale(
+                bit, first_level, prefix_ref, sums_ref, weight_ref, tokens
+            )
+        for head, place_out, gain_column, states in work:
+            start = pl.multiple_of(head * head_width, 128)
             mixed = mixed_ref[pl.ds(start, head_width), tokens]
-            mixed = mixed + found * scale_ref[pl.ds(first + slot, 1)]
+            for level, state in enumerate(states):
+                found = lax.dot_general(state, queries, NT, preferred_element_type=jnp.float32)
+                mixed = mixed + found * scale_ref[level, pl.ds(head, 1)]
             square = jnp.mean(mixed * mixed, axis=0, keepdims=True)
-            normed = mixed * lax.rsqrt(square + EPS) * gains[slot]
-            out_ref[tokens, rows] = normed.astype(jnp.bfloat16).T
-        copy = pltpu.make_async_copy(
-            out_ref.at[tokens], out_hbm.at[tokens, columns], sent.at[span]
-        )
-        copy.start()
-        copies.append(copy)
+            normed = mixed * lax.rsqrt(square + EPS) * gain_column
+            columns = slice(place_out * head_width, (place_out + 1) * head_width)
+            out_ref[tokens, columns] = normed.astype(jnp.bfloat16).T
+        for at, (far, _) in enumerate(quarters):
+            size = count * head_width
+            columns = pl.ds(pl.multiple_of(first_head(far, heads) * head_width, 128), size)
+            copy = pltpu.make_async_copy(
+                out_ref.at[tokens, at * size : (at + 1) * size],
+                out_hbm.at[tokens, columns],
+                sent.at[len(copies)],
+            )
+            copy.start()
+            copies.append(copy)
     for copy in copies:
         copy.wait()
 
 
-def finish(far, bit, first_level, mixed, queries, sums, level_weight, gain, prefix, state, begun):
+def finish(quarters, first_level, bits, shared, prefixes, parts, begun, has_token):
+    mixed, queries, sums, level_weight, gain = shared
     width, tokens = mixed.shape
-    inputs = [mixed, queries, sums, level_weight, gain, prefix, state]
+    heads = level_weight.shape[1]
+    inputs = [*shared, *prefixes, *parts]
     specs = [HELD] * len(inputs)
     inputs = [hold(array) for array in inputs]
     out = pl.BlockSpec(memory_space=pltpu.HBM)
+    aliases = {}
     if begun is not None:
+        aliases = {len(inputs): 0}
         specs.append(out)
         inputs.append(begun)
+    shapes = [jax.ShapeDtypeStruct((tokens, width), jnp.bfloat16)]
+    if has_token:
+        shapes.append(pltpu.VMEM((8, 128), jnp.float32))
     return pl.pallas_call(
-        functools.partial(finish_kernel, far, bit, first_level),
+        functools.partial(finish_kernel, quarters, first_level, bits, has_token),
         in_specs=specs,
-        out_specs=[out, HELD],
-        out_shape=[
-            jax.ShapeDtypeStruct((tokens, width), jnp.bfloat16),
-            pltpu.VMEM((8, 128), jnp.float32),
+        out_specs=[out, HELD][: len(shapes)],
+        out_shape=shapes,
+        scratch_shapes=[
+            pltpu.VMEM((tokens, len(quarters) * width // 4), jnp.bfloat16),
+            pltpu.VMEM((len(bits), heads, SPAN), jnp.float32),
+            pltpu.SemaphoreType.DMA((len(quarters) * (tokens // SPAN),)),
         ],
-        scratch_shapes=[
-            pltpu.VMEM((tokens, width >> len(far)), jnp.bfloat16),
-            pltpu.VMEM((width >> len(far), queries.shape[1]), jnp.bfloat16),
-            pltpu.VMEM((level_weight.shape[1], SPAN), jnp.float32),
-            pltpu.SemaphoreType.DMA((tokens // SPAN,)),
-        ],
-        input_output_aliases={} if begun is None else {7: 0},
+        input_output_aliases=aliases,
         compiler_params=PARAMS,
-        name=f"finish{far[0]}{far[1]}",
+        name="finish" + "".join(f"{core}{side}" for (core, side), _ in quarters),
     )(*inputs)
 
 
@@ -482,8 +504,8 @@
             rests.append(trade(chunks[0], 2**bit))
         if 0 < bit and at < spans:
             stop = spans if bit == last else at + 1
-            mixed, token = mix_local(at, stop, shared, mixed, (chunks[0],))
-            at, waits = stop, (token,)
+            mixed, *waits = mix_local(at, stop, shared, mixed, (chunks[0],), bit < last)
+            at = stop
         if 1 < bit < 2 + SPLIT_BITS:
             waits = (*waits, rests[bit - 2])
         if bit < last:
@@ -519,25 +541,23 @@
     far = trade(near, 1)
     near_side = pack("side", [(across[last - 1], two)], (token,))
     far_side = trade(near_side, 1)
-    levels = []
-    for slot, bit in enumerate(range(2, last)):
-        taken = [
-            (core if bit < last - 1 or side == 0 else 2 + core, (2 * slot + side) * two, (core, side))
-            for core, side in sides
-        ]
-        if bit == last - 1:
-            taken = [(at, row if at < 2 else 0, far_bits) for at, row, far_bits in taken]
-        levels.append((bit, prefixes[bit], taken))
+    late = list(range(2, bits))
+    where = {}
+    for core, side in sides:
+        where[core, side] = [(core, (2 * slot + side) * two) for slot in range(len(late) - 2)]
+        top = (core, 2 * (len(late) - 2) * two) if side == 0 else (2 + core, 0)
+        where[core, side].append(top)
     parts = [near, far, near_side, far_side]
-    mixed, token = add_levels(mixed, *rest, levels, parts, first_level, (state,))
-
-    rest = (last, first_level, mixed, *rest, gain, prefixes[last])
+    shared = (mixed, queries, sums, level_weight, gain)
+    rest = (first_level, late, shared, [prefixes[bit] for bit in late])
     beside = [(trade(state, 2), two)]
-    out, _ = finish((0, 0), *rest, state, None)
-    out, token = finish((1, 0), *rest, trade(state, 1), out)
+    quarters = [((core, 0), [*where[core, 0], (4 + core, 0)]) for core in (0, 1)]
+    out, token = finish(quarters, *rest, [*parts, state, trade(state, 1)], None, True)
     beside = pack("beside", beside, (token,))
-    out, _ = finish((0, 1), *rest, beside, out)
-    return finish((1, 1), *rest, trade(beside, 1), out)[0]
+    quarters = [((0, 1), [*where[0, 1], (4, 0)])]
+    (out,) = finish(quarters, *rest, [*parts, beside], out, False)
+    quarters = [((1, 1), [*where[1, 1], (4, 0)])]
+    return finish(quarters, *rest, [*parts, trade(beside, 1)], out, False)[0]
 
 
 def solution(mesh):

time: 45.5 us -> 42.4 us (0.932)
  Pallas kernels: 20 us -> 14.4 us
  waiting for transfers between devices: 8.74 us -> 11.3 us
    pallas_call x18 -> x17, Pallas kernels: 13 us -> 9.33 us  [call(): pl.pallas_call(kernel, in_specs=specs, out_specs=[HELD] * len(outputs), o...]
    ppermute x15, waiting for transfers between devices: 8.74 us -> 11.3 us  [trade(): return lax.ppermute(value, AXES, pairs)]
    pallas_call x4 -> x3, Pallas kernels: 6.97 us -> 5.08 us  [finish(): pl.pallas_call(functools.partial(finish_kernel, quarters, first_level, bi...]
  transfers between devices with their start and end apart: 15 -> 15, of which waited for: 6 -> 8; matrix products, arithmetic and copies ran while one was open for 0% -> 0% of each run, Pallas kernels for 34% -> 24%
where the time goes in v10:
time: 42.4 us; the launch traced here: 42.3 us
  starting transfers between devices  16.3 us (38%)
  Pallas kernels  14.4 us (34%)
  waiting for transfers between devices  11.3 us (27%)
    ppermute x15, starting transfers between devices, trade(): return lax.ppermute(value, AXES, pairs)  16.3 us
    ppermute x15, waiting for transfers between devices, trade(): return lax.ppermute(value, AXES, pairs)  11.3 us
    pallas_call x17, Pallas kernels, call(): pl.pallas_call(kernel, in_specs=specs, out_specs=[HELD] * len(outputs), o...  9.33 us
    pallas_call x3, Pallas kernels, finish(): pl.pallas_call(functools.partial(finish_kernel, quarters, first_level, bi...  5.08 us
  transfers between devices with their start and end apart: 15, of which 8 were waited for; matrix products, arithmetic and copies ran while one was open for 0% of the time, Pallas kernels for 24%

profile of v10, /device:TPU:0, one launch (start us, length us, event | category | flops | bytes accessed | tf_op | source)
XLA Modules:
  0.0 42.3 jit_solution(14001474931537064427)
XLA Ops:
  0.0 2.8 %states.1 = (f32[520,128]{1,0:T(8,128)S(1)}, f32[520,128]{1,0:T(8,128)S(1)}, bf16[3,128,1024]{2,1,0:T(8,128)(2,1)S(1)}, f32[2,8,1024]{2,1,0:T(8,128)S(1)}, f32[4...) custom-call(bf16[1024,128]{1,0:T(8,128)(2,1)} %refs_0_.1, ...), custom_call_target="tpu_custom_call" | custom-call | tf_op jit(solution)/shard_map/states/pallas_call | solution.py:41
  3.3 1.2 %collective-permute-done.refs_1_.refs_6_ = f32[520,128]{1,0:T(8,128)S(1)} collective-permute-done((f32[520,128]{1,0:T(8,128)S(1)}, f32[520,128]{1,0:T(8,128)S(1)}, u32[]{:S(2)}, u32[]{:S(2)}) %collective-permute-start) | collective-permute-done | bytes 266272 | tf_op jit(solution)/shard_map/ppermute | solution.py:475
  4.5 2.9 %collective-permute-start.1 = (f32[264,128]{1,0:T(8,128)S(1)}, f32[264,128]{1,0:T(8,128)S(1)}, u32[]{:S(2)}, u32[]{:S(2)}) collective-permute-start(f32[264,128]{1,0:T(8,128)S(1)} %get-tuple-element.45), channel_id=1, source_target_pairs={{0,16},{8,24},{16,0},{24,8},{1,17},{9,25},{17,1},{25,9},{2,18},{10... | collective-permute-start | bytes 405512 | tf_op jit(solution)/shard_map/ppermute | solution.py:475
  7.5 0.8 %local0.1 = (f32[1024,1024]{1,0:T(8,128)S(1)}, f32[8,128]{1,0:T(8,128)S(1)}) custom-call(bf16[1024,128]{1,0:T(8,128)(2,1)S(1)} %get-tuple-element.34.refs_0_.refs_1_, bf16[1024,128]{1,0:T(8,128)(2,1)S(1)} %get-tuple-element.35.refs_1_, bf16[1024,1024]{1,0:T(8,128)(2,1)S(1)} %get-tuple-element.36.refs_2_, ...), custom_call_target="tpu_custom_call" | custom-call | tf_op jit(solution)/shard_map/local0/pallas_call | solution.py:41
  8.3 3.1 %collective-permute-done.1.refs_1_.refs_0_ = f32[264,128]{1,0:T(8,128)S(1)} collective-permute-done((f32[264,128]{1,0:T(8,128)S(1)}, f32[264,128]{1,0:T(8,128)S(1)}, u32[]{:S(2)}, u32[]{:S(2)}) %collective-permute-start.1) | collective-permute-done | bytes 135200 | tf_op jit(solution)/shard_map/ppermute | solution.py:475
  11.4 1.8 %collective-permute-start.2 = (f32[264,128]{1,0:T(8,128)S(1)}, f32[264,128]{1,0:T(8,128)S(1)}, u32[]{:S(2)}, u32[]{:S(2)}) collective-permute-start(f32[264,128]{1,0:T(8,128)S(1)} %get-tuple-element.48.refs_8_.refs_0_), channel_id=1, source_target_pairs={{0,1},{8,9},{16,17},{24,25},{1,0},{9,8},{17,16},{25,24},{2,3},{10,... | collective-permute-start | bytes 405512 | tf_op jit(solution)/shard_map/ppermute | solution.py:475
  13.2 1.5 %collective-permute-start.5 = (f32[264,128]{1,0:T(8,128)S(1)}, f32[264,128]{1,0:T(8,128)S(1)}, u32[]{:S(2)}, u32[]{:S(2)}) collective-permute-start(f32[264,128]{1,0:T(8,128)S(1)} %get-tuple-element.43.refs_7_.refs_0_), channel_id=1, source_target_pairs={{0,16},{8,24},{16,0},{24,8},{1,17},{9,25},{17,1},{25,9},{2,18},{10... | collective-permute-start | bytes 405512 | tf_op jit(solution)/shard_map/ppermute | solution.py:475
  14.7 0.9 %local1.1 = (f32[1024,1024]{1,0:T(8,128)S(1)}, f32[8,128]{1,0:T(8,128)S(1)}) custom-call(bf16[1024,128]{1,0:T(8,128)(2,1)S(1)} %get-tuple-element.34.refs_0_.refs_1_, bf16[1024,128]{1,0:T(8,128)(2,1)S(1)} %get-tuple-element.35.refs_1_, bf16[1024,1024]{1,0:T(8,128)(2,1)S(1)} %get-tuple-element.36.refs_2_, ...), custom_call_target="tpu_custom_call", output_to_operand_aliasing={{0}: (7, {})} | custom-call | tf_op jit(solution)/shard_map/local1/pallas_call | solution.py:41
  15.6 1.0 %collective-permute-done.2.refs_1_.refs_0_ = f32[264,128]{1,0:T(8,128)S(1)} collective-permute-done((f32[264,128]{1,0:T(8,128)S(1)}, f32[264,128]{1,0:T(8,128)S(1)}, u32[]{:S(2)}, u32[]{:S(2)}) %collective-permute-start.2) | collective-permute-done | bytes 135200 | tf_op jit(solution)/shard_map/ppermute | solution.py:475
  16.7 1.8 %collective-permute-start.4 = (f32[264,128]{1,0:T(8,128)S(1)}, f32[264,128]{1,0:T(8,128)S(1)}, u32[]{:S(2)}, u32[]{:S(2)}) collective-permute-start(f32[264,128]{1,0:T(8,128)S(1)} %get-tuple-element.52.refs_8_.refs_0_.refs_1_), channel_id=1, source_target_pairs={{0,2},{8,10},{16,18},{24,26},{1,3},{9,11},{17,19},{25,27},{2,0},{1... | collective-permute-start | bytes 405512 | tf_op jit(solution)/shard_map/ppermute | solution.py:475
  18.4 1.6 %collective-permute-start.7 = (f32[256,128]{1,0:T(8,128)S(1)}, f32[256,128]{1,0:T(8,128)S(1)}, u32[]{:S(2)}, u32[]{:S(2)}) collective-permute-start(f32[256,128]{1,0:T(8,128)S(1)} %found2.1.refs_0_), channel_id=1, source_target_pairs={{0,16},{8,24},{16,0},{24,8},{1,17},{9,25},{17,1},{25,9},{2,18},{10... | collective-permute-start | bytes 393224 | tf_op jit(solution)/shard_map/ppermute | solution.py:475
  20.1 0.9 %local2.1 = (f32[1024,1024]{1,0:T(8,128)S(1)}, f32[8,128]{1,0:T(8,128)S(1)}) custom-call(bf16[1024,128]{1,0:T(8,128)(2,1)S(1)} %get-tuple-element.34.refs_0_.refs_1_, bf16[1024,128]{1,0:T(8,128)(2,1)S(1)} %get-tuple-element.35.refs_1_, bf16[1024,1024]{1,0:T(8,128)(2,1)S(1)} %get-tuple-element.36.refs_2_, ...), custom_call_target="tpu_custom_call", output_to_operand_aliasing={{0}: (7, {})} | custom-call | tf_op jit(solution)/shard_map/local2/pallas_call | solution.py:41
  21.0 0.7 %collective-permute-done.4.refs_1_.refs_0_ = f32[264,128]{1,0:T(8,128)S(1)} collective-permute-done((f32[264,128]{1,0:T(8,128)S(1)}, f32[264,128]{1,0:T(8,128)S(1)}, u32[]{:S(2)}, u32[]{:S(2)}) %collective-permute-start.4) | collective-permute-done | bytes 135200 | tf_op jit(solution)/shard_map/ppermute | solution.py:475
  21.8 1.7 %collective-permute-done.7.refs_1_ = f32[256,128]{1,0:T(8,128)S(1)} collective-permute-done((f32[256,128]{1,0:T(8,128)S(1)}, f32[256,128]{1,0:T(8,128)S(1)}, u32[]{:S(2)}, u32[]{:S(2)}) %collective-permute-start.7) | collective-permute-done | bytes 131104 | tf_op jit(solution)/shard_map/ppermute | solution.py:475
  23.6 2.7 %collective-permute-start.11 = (f32[264,128]{1,0:T(8,128)S(1)}, f32[264,128]{1,0:T(8,128)S(1)}, u32[]{:S(2)}, u32[]{:S(2)}) collective-permute-start(f32[264,128]{1,0:T(8,128)S(1)} %get-tuple-element.56.refs_8_.refs_1_.refs_3_), channel_id=1, source_target_pairs={{0,4},{8,12},{16,20},{24,28},{1,5},{9,13},{17,21},{25,29},{2,6},{1... | collective-permute-start | bytes 405512 | tf_op jit(solution)/shard_map/ppermute | solution.py:475
  26.2 1.5 %collective-permute-start.9 = (f32[256,128]{1,0:T(8,128)S(1)}, f32[256,128]{1,0:T(8,128)S(1)}, u32[]{:S(2)}, u32[]{:S(2)}) collective-permute-start(f32[256,128]{1,0:T(8,128)S(1)} %found3.1.refs_2_), channel_id=1, source_target_pairs={{0,16},{8,24},{16,0},{24,8},{1,17},{9,25},{17,1},{25,9},{2,18},{10... | collective-permute-start | bytes 393224 | tf_op jit(solution)/shard_map/ppermute | solution.py:475
  27.7 1.1 %local3.1.refs_0_ = f32[1024,1024]{1,0:T(8,128)S(1)} custom-call(bf16[1024,128]{1,0:T(8,128)(2,1)S(1)} %get-tuple-element.34.refs_0_.refs_1_, bf16[1024,128]{1,0:T(8,128)(2,1)S(1)} %get-tuple-element.35.refs_1_, bf16[1024,1024]{1,0:T(8,128)(2,1)S(1)} %get-tuple-element.36.refs_2_, ...), custom_call_target="tpu_custom_call", output_to_operand_aliasing={{}: (7, {})} | custom-call | tf_op jit(solution)/shard_map/local3/pallas_call | solution.py:41
  28.8 2.7 %reach0.1 = (f32[1024,1024]{1,0:T(8,128)S(1)}, f32[8,128]{1,0:T(8,128)S(1)}) custom-call(f32[1024,1024]{1,0:T(8,128)S(1)} %local3.1.refs_0_, bf16[1024,128]{1,0:T(8,128)(2,1)S(1)} %get-tuple-element.34.refs_0_.refs_1_, f32[2,8,1024]{2,1,0:T(8,128)S(1)} %get-tuple-element.37.refs_3_.refs_2_, ...), custom_call_target="tpu_custom_call", output_to_operand_aliasing={{0}: (0, {})} | custom-call | tf_op jit(solution)/shard_map/reach0/pallas_call | solution.py:41
  31.9 1.3 %collective-permute-done.11.refs_0_ = f32[264,128]{1,0:T(8,128)S(1)} collective-permute-done((f32[264,128]{1,0:T(8,128)S(1)}, f32[264,128]{1,0:T(8,128)S(1)}, u32[]{:S(2)}, u32[]{:S(2)}) %collective-permute-start.11) | collective-permute-done | bytes 135200 | tf_op jit(solution)/shard_map/ppermute | solution.py:475
  33.3 1.6 %collective-permute-start.12 = (f32[256,128]{1,0:T(8,128)S(1)}, f32[256,128]{1,0:T(8,128)S(1)}, u32[]{:S(2)}, u32[]{:S(2)}) collective-permute-start(f32[256,128]{1,0:T(8,128)S(1)} %state.1.refs_12_), channel_id=1, source_target_pairs={{0,16},{8,24},{16,0},{24,8},{1,17},{9,25},{17,1},{25,9},{2,18},{10... | collective-permute-start | bytes 393224 | tf_op jit(solution)/shard_map/ppermute | solution.py:475
  34.9 2.1 %finish0010.1 = (bf16[1024,1024]{1,0:T(8,128)(2,1)}, f32[8,128]{1,0:T(8,128)S(1)}) custom-call(f32[1024,1024]{1,0:T(8,128)S(1)} %get-tuple-element.57.refs_0_, bf16[1024,128]{1,0:T(8,128)(2,1)S(1)} %get-tuple-element.34.refs_0_.refs_1_, f32[2,8,1024]{2,1,0:T(8,128)S(1)} %get-tuple-element.37.refs_3_.refs_2_, ...), custom_call_target="tpu_custom_call" | custom-call | tf_op jit(solution)/shard_map/finish0010/pallas_call | solution.py:452
  37.1 2.1 %collective-permute-done.12.refs_0_ = f32[256,128]{1,0:T(8,128)S(1)} collective-permute-done((f32[256,128]{1,0:T(8,128)S(1)}, f32[256,128]{1,0:T(8,128)S(1)}, u32[]{:S(2)}, u32[]{:S(2)}) %collective-permute-start.12) | collective-permute-done | bytes 131104 | tf_op jit(solution)/shard_map/ppermute | solution.py:475
  39.3 1.5 %finish01.1.refs_13_ = bf16[1024,1024]{1,0:T(8,128)(2,1)} custom-call(f32[1024,1024]{1,0:T(8,128)S(1)} %get-tuple-element.57.refs_0_, bf16[1024,128]{1,0:T(8,128)(2,1)S(1)} %get-tuple-element.34.refs_0_.refs_1_, f32[2,8,1024]{2,1,0:T(8,128)S(1)} %get-tuple-element.37.refs_3_.refs_2_, ...), custom_call_target="tpu_custom_call", output_to_operand_aliasing={{}: (13, {})} | custom-call | tf_op jit(solution)/shard_map/finish01/pallas_call | solution.py:452
  40.8 1.5 %finish11.1 = bf16[1024,1024]{1,0:T(8,128)(2,1)} custom-call(f32[1024,1024]{1,0:T(8,128)S(1)} %get-tuple-element.57.refs_0_, bf16[1024,128]{1,0:T(8,128)(2,1)S(1)} %get-tuple-element.34.refs_0_.refs_1_, f32[2,8,1024]{2,1,0:T(8,128)S(1)} %get-tuple-element.37.refs_3_.refs_2_, ...), custom_call_target="tpu_custom_call", output_to_operand_aliasing={{}: (13, {})} | custom-call | tf_op jit(solution)/shard_map/finish11/pallas_call | solution.py:452
  (27 shorter events, 1.5 us)
Async XLA Ops:
  2.8 1.7 %collective-permute-start = (f32[520,128]{1,0:T(8,128)S(1)}, f32[520,128]{1,0:T(8,128)S(1)}, u32[]{:S(2)}, u32[]{:S(2)}) collective-permute-start(f32[520,128]{1,0:T(8,128)S(1)} %get-tuple-element.42), channel_id=1, source_target_pairs={{0,8},{8,0},{16,24},{24,16},{1,9},{9,1},{17,25},{25,17},{2,10},{10... | collective-permute-start | bytes 798728 | tf_op jit(solution)/shard_map/ppermute | solution.py:475
  4.5 6.8 %collective-permute-start.1 = (f32[264,128]{1,0:T(8,128)S(1)}, f32[264,128]{1,0:T(8,128)S(1)}, u32[]{:S(2)}, u32[]{:S(2)}) collective-permute-start(f32[264,128]{1,0:T(8,128)S(1)} %get-tuple-element.45), channel_id=1, source_target_pairs={{0,16},{8,24},{16,0},{24,8},{1,17},{9,25},{17,1},{25,9},{2,18},{10... | collective-permute-start | bytes 405512 | tf_op jit(solution)/shard_map/ppermute | solution.py:475
  7.5 8.1 %collective-permute-start.3 = (f32[520,128]{1,0:T(8,128)S(1)}, f32[520,128]{1,0:T(8,128)S(1)}, u32[]{:S(2)}, u32[]{:S(2)}) collective-permute-start(f32[520,128]{1,0:T(8,128)S(1)} %get-tuple-element.41.refs_0_), channel_id=1, source_target_pairs={{0,8},{8,0},{16,24},{24,16},{1,9},{9,1},{17,25},{25,17},{2,10},{10... | collective-permute-start | bytes 798728 | tf_op jit(solution)/shard_map/ppermute | solution.py:475
  11.4 5.2 %collective-permute-start.2 = (f32[264,128]{1,0:T(8,128)S(1)}, f32[264,128]{1,0:T(8,128)S(1)}, u32[]{:S(2)}, u32[]{:S(2)}) collective-permute-start(f32[264,128]{1,0:T(8,128)S(1)} %get-tuple-element.48.refs_8_.refs_0_), channel_id=1, source_target_pairs={{0,1},{8,9},{16,17},{24,25},{1,0},{9,8},{17,16},{25,24},{2,3},{10,... | collective-permute-start | bytes 405512 | tf_op jit(solution)/shard_map/ppermute | solution.py:475
  13.2 6.8 %collective-permute-start.5 = (f32[264,128]{1,0:T(8,128)S(1)}, f32[264,128]{1,0:T(8,128)S(1)}, u32[]{:S(2)}, u32[]{:S(2)}) collective-permute-start(f32[264,128]{1,0:T(8,128)S(1)} %get-tuple-element.43.refs_7_.refs_0_), channel_id=1, source_target_pairs={{0,16},{8,24},{16,0},{24,8},{1,17},{9,25},{17,1},{25,9},{2,18},{10... | collective-permute-start | bytes 405512 | tf_op jit(solution)/shard_map/ppermute | solution.py:475
  16.7 5.1 %collective-permute-start.4 = (f32[264,128]{1,0:T(8,128)S(1)}, f32[264,128]{1,0:T(8,128)S(1)}, u32[]{:S(2)}, u32[]{:S(2)}) collective-permute-start(f32[264,128]{1,0:T(8,128)S(1)} %get-tuple-element.52.refs_8_.refs_0_.refs_1_), channel_id=1, source_target_pairs={{0,2},{8,10},{16,18},{24,26},{1,3},{9,11},{17,19},{25,27},{2,0},{1... | collective-permute-start | bytes 405512 | tf_op jit(solution)/shard_map/ppermute | solution.py:475
  18.4 5.0 %collective-permute-start.7 = (f32[256,128]{1,0:T(8,128)S(1)}, f32[256,128]{1,0:T(8,128)S(1)}, u32[]{:S(2)}, u32[]{:S(2)}) collective-permute-start(f32[256,128]{1,0:T(8,128)S(1)} %found2.1.refs_0_), channel_id=1, source_target_pairs={{0,16},{8,24},{16,0},{24,8},{1,17},{9,25},{17,1},{25,9},{2,18},{10... | collective-permute-start | bytes 393224 | tf_op jit(solution)/shard_map/ppermute | solution.py:475
  20.0 8.8 %collective-permute-start.6 = (f32[512,128]{1,0:T(8,128)S(1)}, f32[512,128]{1,0:T(8,128)S(1)}, u32[]{:S(2)}, u32[]{:S(2)}) collective-permute-start(f32[512,128]{1,0:T(8,128)S(1)} %near1.1.refs_8_), channel_id=1, source_target_pairs={{0,8},{8,0},{16,24},{24,16},{1,9},{9,1},{17,25},{25,17},{2,10},{10... | collective-permute-start | bytes 786440 | tf_op jit(solution)/shard_map/ppermute | solution.py:475
  23.5 11.4 %collective-permute-start.8 = (f32[768,128]{1,0:T(8,128)S(1)}, f32[768,128]{1,0:T(8,128)S(1)}, u32[]{:S(2)}, u32[]{:S(2)}) collective-permute-start(f32[768,128]{1,0:T(8,128)S(1)} %near2.1.refs_8_), channel_id=1, source_target_pairs={{0,8},{8,0},{16,24},{24,16},{1,9},{9,1},{17,25},{25,17},{2,10},{10... | collective-permute-start | bytes 1179656 | tf_op jit(solution)/shard_map/ppermute | solution.py:475
  23.6 9.6 %collective-permute-start.11 = (f32[264,128]{1,0:T(8,128)S(1)}, f32[264,128]{1,0:T(8,128)S(1)}, u32[]{:S(2)}, u32[]{:S(2)}) collective-permute-start(f32[264,128]{1,0:T(8,128)S(1)} %get-tuple-element.56.refs_8_.refs_1_.refs_3_), channel_id=1, source_target_pairs={{0,4},{8,12},{16,20},{24,28},{1,5},{9,13},{17,21},{25,29},{2,6},{1... | collective-permute-start | bytes 405512 | tf_op jit(solution)/shard_map/ppermute | solution.py:475
  26.2 5.6 %collective-permute-start.9 = (f32[256,128]{1,0:T(8,128)S(1)}, f32[256,128]{1,0:T(8,128)S(1)}, u32[]{:S(2)}, u32[]{:S(2)}) collective-permute-start(f32[256,128]{1,0:T(8,128)S(1)} %found3.1.refs_2_), channel_id=1, source_target_pairs={{0,16},{8,24},{16,0},{24,8},{1,17},{9,25},{17,1},{25,9},{2,18},{10... | collective-permute-start | bytes 393224 | tf_op jit(solution)/shard_map/ppermute | solution.py:475
  31.8 3.1 %collective-permute-start.10 = (f32[256,128]{1,0:T(8,128)S(1)}, f32[256,128]{1,0:T(8,128)S(1)}, u32[]{:S(2)}, u32[]{:S(2)}) collective-permute-start(f32[256,128]{1,0:T(8,128)S(1)} %side.1.refs_10_), channel_id=1, source_target_pairs={{0,8},{8,0},{16,24},{24,16},{1,9},{9,1},{17,25},{25,17},{2,10},{10... | collective-permute-start | bytes 393224 | tf_op jit(solution)/shard_map/ppermute | solution.py:475
  33.2 1.7 %collective-permute-start.13 = (f32[256,128]{1,0:T(8,128)S(1)}, f32[256,128]{1,0:T(8,128)S(1)}, u32[]{:S(2)}, u32[]{:S(2)}) collective-permute-start(f32[256,128]{1,0:T(8,128)S(1)} %state.1.refs_12_), channel_id=1, source_target_pairs={{0,8},{8,0},{16,24},{24,16},{1,9},{9,1},{17,25},{25,17},{2,10},{10... | collective-permute-start | bytes 393224 | tf_op jit(solution)/shard_map/ppermute | solution.py:475
  33.3 5.9 %collective-permute-start.12 = (f32[256,128]{1,0:T(8,128)S(1)}, f32[256,128]{1,0:T(8,128)S(1)}, u32[]{:S(2)}, u32[]{:S(2)}) collective-permute-start(f32[256,128]{1,0:T(8,128)S(1)} %state.1.refs_12_), channel_id=1, source_target_pairs={{0,16},{8,24},{16,0},{24,8},{1,17},{9,25},{17,1},{25,9},{2,18},{10... | collective-permute-start | bytes 393224 | tf_op jit(solution)/shard_map/ppermute | solution.py:475
  39.2 1.6 %collective-permute-start.14 = (f32[256,128]{1,0:T(8,128)S(1)}, f32[256,128]{1,0:T(8,128)S(1)}, u32[]{:S(2)}, u32[]{:S(2)}) collective-permute-start(f32[256,128]{1,0:T(8,128)S(1)} %beside.1.refs_12_), channel_id=1, source_target_pairs={{0,8},{8,0},{16,24},{24,16},{1,9},{9,1},{17,25},{25,17},{2,10},{10... | collective-permute-start | bytes 393224 | tf_op jit(solution)/shard_map/ppermute | solution.py:475

commit v11 on v10

--- a/solution.py
+++ b/solution.py
@@ -9,6 +9,7 @@
 
 SPAN = 256
 SPLIT_BITS = 2
+CUTS = 2
 EPS = 1e-05
 AXES = ("narrow", "wide")
 NT = (((1,), (1,)), ((), ()))
@@ -68,8 +69,8 @@
 
 def state_kernel(*refs):
     q_hbm, k_hbm, v_hbm, decay_hbm, weight_hbm, gain_hbm = refs[:6]
-    keep_ref, send_ref, local_ref, sums_ref, totals_ref = refs[6:11]
-    q_ref, k_ref, v_ref, weight_ref, gain_ref, decay_ref, held, arrived = refs[11:]
+    message_ref, local_ref, sums_ref, totals_ref = refs[6:10]
+    q_ref, k_ref, v_ref, weight_ref, gain_ref, decay_ref, arrived = refs[10:]
     heads, tokens = decay_ref.shape
     head_width = v_ref.shape[1] // heads
     spans = tokens // SPAN
@@ -122,13 +123,8 @@
         group = states[0]
         for span in range(1, spans):
             group = group * wholes[span][head : head + 1] + states[span]
-        held[columns] = group.T
-    half = held.shape[0] // 2
-    core = bit_of(place(), 0)
-    keep_ref[:half] = held[pl.ds(core * half, half)]
-    send_ref[:half] = held[pl.ds((1 - core) * half, half)]
-    keep_ref[half:] = run
-    send_ref[half:] = run
+        message_ref[columns] = group.T
+    message_ref[heads * head_width :] = run
     for copy in copies[2 + spans :]:
         copy.wait()
 
@@ -138,7 +134,6 @@
     heads = log_decay.shape[0]
     width = values.shape[1]
     spans = tokens // SPAN
-    message = ((width // 2 + heads, key_width), jnp.float32)
     inputs = [queries, keys, values, log_decay, level_weight, gain]
     kept = [queries, keys, values, level_weight, gain]
     return call(
@@ -146,8 +141,7 @@
         "states",
         [pltpu.with_memory_space_constraint(array, pltpu.HBM) for array in inputs],
         [
-            message,
-            message,
+            ((width + heads, key_width), jnp.float32),
             ((spans - 1, key_width, width), jnp.bfloat16),
             ((2, heads, tokens), jnp.float32),
             ((spans, heads, 128), jnp.float32),
@@ -155,7 +149,6 @@
         ],
         [
             pltpu.VMEM(log_decay.shape, jnp.float32),
-            pltpu.VMEM((width, key_width), jnp.float32),
             pltpu.SemaphoreType.DMA((spans + 5,)),
         ],
         [pl.BlockSpec(memory_space=pltpu.HBM)] * len(inputs),
@@ -252,54 +245,76 @@
     return first
 
 
-def merge_kernel(bit, offset, mode, *refs):
+def chip_kernel(mine_ref, other_ref, *refs):
+    *message_refs, next_ref, whole_ref = refs
+    heads = next_ref.shape[0]
+    width = mine_ref.shape[0] - heads
+    per = width // heads
+    held = whole_ref.shape[0] // per
+    here = place()
+    upper = bit_of(here, 0) == 1
+    first = first_head((0,), heads)
+    for slot in range(held):
+        part = pl.ds(pl.multiple_of((first + slot) * per, 8), per)
+        total = pl.ds(width + first + slot, 1)
+        whole_ref[slot * per : (slot + 1) * per] = join(
+            upper, mine_ref[part], mine_ref[total], other_ref[part], other_ref[total]
+        )
+    other_total = other_ref[width:]
+    total = mine_ref[width:] + other_total
+    next_ref[...] = jnp.where(upper, other_total, 0.0)
+    half = held * per // 2
+    side = bit_of(here, 1)
+    cuts = len(message_refs) // 2
+    size = half // cuts
+    for at, ref in enumerate(message_refs):
+        start = (side if at < cuts else 1 - side) * half + at % cuts * size
+        ref[:size] = whole_ref[pl.ds(pl.multiple_of(start, 8), size)]
+        ref[size:] = total
+
+
+def make_chip(mine, other, heads, cuts):
+    rows, lanes = mine.shape
+    half = (rows - heads) // 2
+    *messages, prefix = call(
+        chip_kernel,
+        "chip",
+        [mine, other],
+        [
+            *[((half // 2 // cuts + heads, lanes), jnp.float32)] * (2 * cuts),
+            ((heads, lanes), jnp.float32),
+        ],
+        [pltpu.VMEM((half, lanes), jnp.float32)],
+    )
+    return messages[:cuts], messages[cuts:], prefix
+
+
+def merge_kernel(bit, offset, *refs):
     mine_ref, other_ref, prefix_ref = refs[:3]
-    whole_ref = refs[-1]
-    next_ref = refs[-2]
+    merged_ref, next_ref = refs[-2:]
     heads = prefix_ref.shape[0]
-    near = min(bit + 1, SPLIT_BITS)
     rows = mine_ref.shape[0] - heads
     per = mine_ref.shape[1]
     upper = bit_of(place(), bit) == 1
-    first = first_head((0,) * near, heads) + offset
+    first = first_head((0,) * SPLIT_BITS, heads) + offset
     for slot in range(rows // per):
         part = slice(slot * per, (slot + 1) * per)
         total = pl.ds(rows + first + slot, 1)
-        whole_ref[part] = join(
+        merged_ref[part] = join(
             upper, mine_ref[part], mine_ref[total], other_ref[part], other_ref[total]
         )
     other_total = other_ref[rows:]
-    total = mine_ref[rows:] + other_total
+    merged_ref[rows:] = mine_ref[rows:] + other_total
     next_ref[...] = prefix_ref[...] + jnp.where(upper, other_total, 0.0)
-    if mode == "whole":
-        merged_ref = refs[-3]
-        merged_ref[:rows] = whole_ref[...]
-        merged_ref[rows:] = total
-    else:
-        first_ref, second_ref = refs[-4:-2]
-        half = rows // 2
-        side = bit_of(place(), bit + 1) if mode == "side" else 0
-        first_ref[:half] = whole_ref[pl.ds(side * half, half)]
-        second_ref[:half] = whole_ref[pl.ds((1 - side) * half, half)]
-        first_ref[half:] = total
-        second_ref[half:] = total
-
-
-def merge(bit, mine, other, prefix, mode, offset, tokens=()):
-    heads, lanes = prefix.shape
-    rows = mine.shape[0] - heads
-    if mode == "whole":
-        messages = [(mine.shape, jnp.float32)]
-    else:
-        messages = [((rows // 2 + heads, lanes), jnp.float32)] * 2
-    *messages, prefix = call(
-        functools.partial(merge_kernel, bit, offset, mode),
+
+
+def merge(bit, offset, mine, other, prefix, tokens=()):
+    return call(
+        functools.partial(merge_kernel, bit, offset),
         f"merge{bit}{offset}",
         [mine, other, prefix, *tokens],
-        [*messages, (prefix.shape, jnp.float32)],
-        [pltpu.VMEM((rows, lanes), jnp.float32)],
-    )
-    return messages, prefix
+        [(mine.shape, jnp.float32), (prefix.shape, jnp.float32)],
+    )
 
 
 def pack_kernel(takes, *refs):
@@ -327,55 +342,60 @@
     return reach * weight_ref[first_level + bit, :, tokens] * active
 
 
-def take_levels(plan, part_refs, levels, heads):
-    per = levels.shape[1] // heads
-    for slot, pieces in enumerate(plan):
-        for index, row, far in pieces:
-            rows = (heads >> len(far)) * per
-            start = pl.multiple_of(first_head(far, heads) * per, 128)
-            levels[slot, pl.ds(start, rows)] = part_refs[index][row : row + rows].astype(
-                jnp.bfloat16
-            )
-
-
-def reach_kernel(plan, bits, first_level, *refs):
+def gather_work(quarters, part_refs, heads, per):
+    work = []
+    for far, pieces in quarters:
+        first = first_head(far, heads)
+        for slot in range(heads // 4):
+            states = []
+            for level, index, start in pieces:
+                if start is None:
+                    rows = pl.ds(pl.multiple_of((first + slot) * per, 128), per)
+                else:
+                    rows = slice(start + slot * per, start + (slot + 1) * per)
+                states.append((level, part_refs[index][rows].astype(jnp.bfloat16)))
+            work.append((first + slot, states))
+    return work
+
+
+def add_found(mixed, queries, head, states, scale_ref):
+    for level, state in states:
+        found = lax.dot_general(state, queries, NT, preferred_element_type=jnp.float32)
+        mixed = mixed + found * scale_ref[level, pl.ds(head, 1)]
+    return mixed
+
+
+def reach_kernel(quarters, first_level, bits, *refs):
     mixed_ref, q_ref, sums_ref, weight_ref = refs[:4]
     prefix_refs = refs[4 : 4 + len(bits)]
-    part_refs = refs[4 + len(bits) : -3]
-    out_ref, done_ref, levels = refs[-3:]
+    part_refs = refs[4 + len(bits) :]
+    out_ref, done_ref, scale_ref = refs[-3:]
     done_ref[...] = jnp.zeros_like(done_ref)
     heads = weight_ref.shape[1]
     head_width = mixed_ref.shape[0] // heads
-    take_levels(plan, part_refs, levels, heads)
+    work = gather_work(quarters, part_refs, heads, head_width)
     for span in range(q_ref.shape[0] // SPAN):
         tokens = slice(span * SPAN, (span + 1) * SPAN)
         queries = q_ref[tokens]
-        scales = [
-            level_scale(bit, first_level, prefix_ref, sums_ref, weight_ref, tokens)
-            for bit, prefix_ref in zip(bits, prefix_refs)
-        ]
-        for head in range(heads):
-            rows = slice(head * head_width, (head + 1) * head_width)
-            mixed = mixed_ref[rows, tokens]
-            for slot, scale in enumerate(scales):
-                found = lax.dot_general(
-                    levels[slot, rows], queries, NT, preferred_element_type=jnp.float32
-                )
-                mixed = mixed + found * scale[head : head + 1]
-            out_ref[rows, tokens] = mixed
-
-
-def add_levels(mixed, queries, sums, level_weight, levels, parts, first_level, tokens=()):
-    width = mixed.shape[0]
-    bits = [bit for bit, _, _ in levels]
-    plan = [pieces for _, _, pieces in levels]
-    prefixes = [prefix for _, prefix, _ in levels]
+        for level, (bit, prefix_ref) in enumerate(zip(bits, prefix_refs)):
+            scale_ref[level] = level_scale(
+                bit, first_level, prefix_ref, sums_ref, weight_ref, tokens
+            )
+        for head, states in work:
+            rows = pl.ds(pl.multiple_of(head * head_width, 128), head_width)
+            out_ref[rows, tokens] = add_found(
+                mixed_ref[rows, tokens], queries, head, states, scale_ref
+            )
+
+
+def add_levels(quarters, first_level, bits, shared, prefixes, parts):
+    mixed, _, _, level_weight = shared
     return call(
-        functools.partial(reach_kernel, plan, bits, first_level),
-        f"reach{bits[0]}",
-        [mixed, queries, sums, level_weight, *prefixes, *parts, *tokens],
+        functools.partial(reach_kernel, quarters, first_level, bits),
+        "reach",
+        [*shared, *prefixes, *parts],
         [(mixed.shape, jnp.float32), ((8, 128), jnp.float32)],
-        [pltpu.VMEM((len(bits), width, queries.shape[1]), jnp.bfloat16)],
+        [pltpu.VMEM((len(bits), level_weight.shape[1], SPAN), jnp.float32)],
         aliases={0: 0},
     )
 
@@ -391,16 +411,12 @@
     heads = weight_ref.shape[1]
     head_width = mixed_ref.shape[0] // heads
     count = heads // 4
-    work = []
-    for at, (far, pieces) in enumerate(quarters):
-        first = first_head(far, heads)
-        for slot in range(count):
-            row = jnp.broadcast_to(gain_ref[pl.ds(first + slot, 1)], (8, head_width))
-            states = []
-            for index, start in pieces:
-                rows = slice(start + slot * head_width, start + (slot + 1) * head_width)
-                states.append(part_refs[index][rows].astype(jnp.bfloat16))
-            work.append((first + slot, at * count + slot, row.T[:, :1], states))
+    size = count * head_width
+    work = gather_work(quarters, part_refs, heads, head_width)
+    gains = []
+    for head, _ in work:
+        row = jnp.broadcast_to(gain_ref[pl.ds(head, 1)], (8, head_width))
+        gains.append(row.T[:, :1])
     copies = []
     for span in range(q_ref.shape[0] // SPAN):
         tokens = slice(span * SPAN, (span + 1) * SPAN)
@@ -409,18 +425,14 @@
             scale_ref[level] = level_scale(
                 bit, first_level, prefix_ref, sums_ref, weight_ref, tokens
             )
-        for head, place_out, gain_column, states in work:
-            start = pl.multiple_of(head * head_width, 128)
-            mixed = mixed_ref[pl.ds(start, head_width), tokens]
-            for level, state in enumerate(states):
-                found = lax.dot_general(state, queries, NT, preferred_element_type=jnp.float32)
-                mixed = mixed + found * scale_ref[level, pl.ds(head, 1)]
+        for at, (head, states) in enumerate(work):
+            rows = pl.ds(pl.multiple_of(head * head_width, 128), head_width)
+            mixed = add_found(mixed_ref[rows, tokens], queries, head, states, scale_ref)
             square = jnp.mean(mixed * mixed, axis=0, keepdims=True)
-            normed = mixed * lax.rsqrt(square + EPS) * gain_column
-            columns = slice(place_out * head_width, (place_out + 1) * head_width)
+            normed = mixed * lax.rsqrt(square + EPS) * gains[at]
+            columns = slice(at * head_width, (at + 1) * head_width)
             out_ref[tokens, columns] = normed.astype(jnp.bfloat16).T
         for at, (far, _) in enumerate(quarters):
-            size = count * head_width
             columns = pl.ds(pl.multiple_of(first_head(far, heads) * head_width, 128), size)
             copy = pltpu.make_async_copy(
                 out_ref.at[tokens, at * size : (at + 1) * size],
@@ -484,80 +496,77 @@
     bits = (lax.axis_size("wide") * lax.axis_size("narrow")).bit_length() - 1
     first_level = level_weight.shape[0] - bits
     gain = norm_gain.reshape(heads, per)
-    mine, give, local, sums, totals, queries, keys, values, level_weight, gain = make_states(
+    message, local, sums, totals, queries, keys, values, level_weight, gain = make_states(
         queries, keys, values, log_decay, level_weight, gain
     )
     shared = (queries, keys, values, sums, totals, level_weight, local)
-
     last = bits - 1
     two = 2 * per
+    size = two // CUTS
     sides = [(core, side) for core in (0, 1) for side in (0, 1)]
-    prefix = jnp.zeros((heads, 128), jnp.float32)
-    prefixes, found, rests, across = [], [], [], {}
-    mixed, at, waits = None, 0, ()
-    chunks = [mine]
-    for bit in range(bits):
-        prefixes.append(prefix)
-        sent = [give] if bit < SPLIT_BITS else chunks
-        found.append([trade(chunk, 2**bit) for chunk in sent])
-        if bit < SPLIT_BITS:
-            rests.append(trade(chunks[0], 2**bit))
-        if 0 < bit and at < spans:
+    other = trade(message, 1)
+    zero = jnp.zeros((heads, 128), jnp.float32)
+    chunks, give, prefix = make_chip(message, other, heads, CUTS)
+    prefixes = [zero, prefix]
+    found, across = {}, {}
+    mixed, at = None, 0
+
+    def both(name, messages, tokens=()):
+        return pack(name, [(state, size) for state in messages], tokens)
+
+    for bit in range(1, bits):
+        found[bit] = [trade(chunk, 2**bit) for chunk in (give if bit == 1 else chunks)]
+        if bit == 1:
+            rest = trade(both("rest", chunks), 2)
+        waits = ()
+        if at < spans:
             stop = spans if bit == last else at + 1
-            mixed, *waits = mix_local(at, stop, shared, mixed, (chunks[0],), bit < last)
+            mixed, *waits = mix_local(at, stop, shared, mixed, chunks[-1:], bit < last)
             at = stop
-        if 1 < bit < 2 + SPLIT_BITS:
-            waits = (*waits, rests[bit - 2])
         if bit < last:
-            mode = "side" if bit + 1 < SPLIT_BITS else "whole"
-            merged = [
-                merge(bit, chunk, other, prefix, mode, offset, waits)
-                for offset, (chunk, other) in enumerate(zip(chunks, found[bit]))
-            ]
-            prefix = merged[0][1]
-            chunks = [message for messages, _ in merged for message in messages]
-            if mode == "side":
-                chunks, give = chunks[:1], chunks[1]
-        if 1 < bit < last:
-            pieces = [(state, two // len(found[bit])) for state in found[bit]]
-            found[bit] = [pack(f"found{bit}", pieces, (chunks[0],))]
-            across[bit] = trade(found[bit][0], 2)
-    ends = found[last]
-    found = [states[0] for states in found]
-
-    rest = (queries, sums, level_weight)
-    near = pack("near1", [(found[1], two), (rests[1], two)])
+            merged, tokens_of = [], ()
+            for offset, (chunk, state) in enumerate(zip(chunks, found[bit])):
+                tokens_of = (*tokens_of, *waits) if offset == CUTS - 1 else tokens_of
+                chunk, prefix = merge(
+                    bit, offset * two // CUTS // per, chunk, state, prefixes[bit], tokens_of
+                )
+                merged.append(chunk)
+                tokens_of = (chunk,)
+            chunks = merged
+            prefixes.append(prefix)
+            found[bit] = both(f"found{bit}", found[bit], chunks[-1:])
+            if bit > 1:
+                across[bit] = trade(found[bit], 2)
+
+    quarters = [((core, side), [(0, 0, None)]) for core, side in sides]
+    shared = (mixed, queries, sums, level_weight)
+    mixed, token = add_levels(quarters, first_level, [0], shared, [zero], [other])
+    ended = token
+    ended = pack("ended0", [(ended, 8)], found[last])
+    ended = pack("ended1", [(ended, 8)])
+    ended = pack("ended2", [(ended, 8)])
+    early = list(range(2, last))
+    pieces = [(found[1], two), (rest, two)]
+    for bit in early:
+        pieces += [(found[bit], two), (across[bit], two)]
+    near = pack("near", pieces, (ended,))
     far = trade(near, 1)
-    levels = [(0, prefixes[0], [(0, 0, (0,)), (1, 0, (1,))])]
-    levels.append((1, prefixes[1], [(2 + core, side * two, (core, side)) for core, side in sides]))
-    parts = [found[0], rests[0], near, far]
-    mixed, token = add_levels(mixed, *rest, levels, parts, first_level)
-    state = pack("state", [(ends[0], two)], (token,))
-
-    pieces = []
-    for bit in range(2, last - 1):
-        pieces += [(found[bit], two), (across[bit], two)]
-    near = pack("near2", [*pieces, (found[last - 1], two)], (chunks[0],))
-    far = trade(near, 1)
-    near_side = pack("side", [(across[last - 1], two)], (token,))
-    far_side = trade(near_side, 1)
-    late = list(range(2, bits))
-    where = {}
-    for core, side in sides:
-        where[core, side] = [(core, (2 * slot + side) * two) for slot in range(len(late) - 2)]
-        top = (core, 2 * (len(late) - 2) * two) if side == 0 else (2 + core, 0)
-        where[core, side].append(top)
-    parts = [near, far, near_side, far_side]
+    middle = [1, *early]
+    ahead = [prefixes[bit] for bit in middle]
+
+    def states_of(side, index, first):
+        return [(first + slot, index, (2 * slot + side) * two) for slot in range(len(middle))]
+
     shared = (mixed, queries, sums, level_weight, gain)
-    rest = (first_level, late, shared, [prefixes[bit] for bit in late])
-    beside = [(trade(state, 2), two)]
-    quarters = [((core, 0), [*where[core, 0], (4 + core, 0)]) for core in (0, 1)]
-    out, token = finish(quarters, *rest, [*parts, state, trade(state, 1)], None, True)
-    beside = pack("beside", beside, (token,))
-    quarters = [((0, 1), [*where[0, 1], (4, 0)])]
-    (out,) = finish(quarters, *rest, [*parts, beside], out, False)
-    quarters = [((1, 1), [*where[1, 1], (4, 0)])]
-    return finish(quarters, *rest, [*parts, trade(beside, 1)], out, False)[0]
+    every = (first_level, [last, *middle], shared, [prefixes[last], *ahead])
+    state = both("state", found[last])
+    beside = trade(state, 2)
+    quarters = {(core, side): [(0, 0, 0), *states_of(side, 1, 1)] for core, side in sides}
+    (out,) = finish([((0, 0), quarters[0, 0])], *every, [state, near], None, False)
+    out, token = finish([((1, 0), quarters[1, 0])], *every, [trade(state, 1), far], out, True)
+    beside = pack("beside", [(beside, two)], (token,))
+    (out,) = finish([((0, 1), quarters[0, 1])], *every, [beside, near], out, False)
+    return finish([((1, 1), quarters[1, 1])], *every, [trade(beside, 1), far], out, False)[0]
 
 
 def solution(mesh):

time: 42.4 us -> 43 us (1.014)
  waiting for transfers between devices: 11.3 us -> 9.69 us
  Pallas kernels: 14.4 us -> 15.7 us
  starting transfers between devices: 16.3 us -> 17.1 us
    ppermute x15 -> x16, waiting for transfers between devices: 11.3 us -> 9.69 us  [trade(): return lax.ppermute(value, AXES, pairs)]
    pallas_call x3 -> x4, Pallas kernels: 5.08 us -> 6.28 us  [finish(): pl.pallas_call(functools.partial(finish_kernel, quarters, first_level, bi...]
    ppermute x15 -> x16, starting transfers between devices: 16.3 us -> 17.1 us  [trade(): return lax.ppermute(value, AXES, pairs)]
    pallas_call x17 -> x23, Pallas kernels: 9.33 us -> 9.47 us  [call(): pl.pallas_call(kernel, in_specs=specs, out_specs=[HELD] * len(outputs), o...]
  transfers between devices with their start and end apart: 15 -> 16, of which waited for: 8 -> 6; matrix products, arithmetic and copies ran while one was open for 0% -> 0% of each run, Pallas kernels for 24% -> 27%
where the time goes in v11:
time: 43 us; the launch traced here: 42.8 us
  starting transfers between devices  17.1 us (40%)
  Pallas kernels  15.7 us (37%)
  waiting for transfers between devices  9.69 us (23%)
    ppermute x16, starting transfers between devices, trade(): return lax.ppermute(value, AXES, pairs)  17.1 us
    ppermute x16, waiting for transfers between devices, trade(): return lax.ppermute(value, AXES, pairs)  9.69 us
    pallas_call x23, Pallas kernels, call(): pl.pallas_call(kernel, in_specs=specs, out_specs=[HELD] * len(outputs), o...  9.47 us
    pallas_call x4, Pallas kernels, finish(): pl.pallas_call(functools.partial(finish_kernel, quarters, first_level, bi...  6.28 us
  transfers between devices with their start and end apart: 16, of which 6 were waited for; matrix products, arithmetic and copies ran while one was open for 0% of the time, Pallas kernels for 27%

profile of v11, /device:TPU:0, one launch (start us, length us, event | category | flops | bytes accessed | tf_op | source)
XLA Modules:
  0.0 42.8 jit_solution(14699272447471633138)
XLA Ops:
  0.0 2.7 %states.1 = (f32[1032,128]{1,0:T(8,128)S(1)}, bf16[3,128,1024]{2,1,0:T(8,128)(2,1)S(1)}, f32[2,8,1024]{2,1,0:T(8,128)S(1)}, f32[4,8,128]{2,1,0:T(8,128)S(1)}, bf...) custom-call(bf16[1024,128]{1,0:T(8,128)(2,1)} %refs_0_.1, ...), custom_call_target="tpu_custom_call" | custom-call | tf_op jit(solution)/shard_map/states/pallas_call | solution.py:42
  3.2 1.5 %collective-permute-done.other_ref.refs_5_ = f32[1032,128]{1,0:T(8,128)S(1)} collective-permute-done((f32[1032,128]{1,0:T(8,128)S(1)}, f32[1032,128]{1,0:T(8,128)S(1)}, u32[]{:S(2)}, u32[]{:S(2)}) %collective-permute-start) | collective-permute-done | bytes 528416 | tf_op jit(solution)/shard_map/ppermute | solution.py:487
  4.8 3.0 %collective-permute-start.2 = (f32[136,128]{1,0:T(8,128)S(1)}, f32[136,128]{1,0:T(8,128)S(1)}, u32[]{:S(2)}, u32[]{:S(2)}) collective-permute-start(f32[136,128]{1,0:T(8,128)S(1)} %get-tuple-element.51), channel_id=1, source_target_pairs={{0,16},{8,24},{16,0},{24,8},{1,17},{9,25},{17,1},{25,9},{2,18},{10... | collective-permute-start | bytes 208904 | tf_op jit(solution)/shard_map/ppermute | solution.py:487
  7.9 0.8 %local0.1 = (f32[1024,1024]{1,0:T(8,128)S(1)}, f32[8,128]{1,0:T(8,128)S(1)}) custom-call(bf16[1024,128]{1,0:T(8,128)(2,1)S(1)} %get-tuple-element.38.refs_0_.refs_1_, bf16[1024,128]{1,0:T(8,128)(2,1)S(1)} %get-tuple-element.39.refs_1_, bf16[1024,1024]{1,0:T(8,128)(2,1)S(1)} %get-tuple-element.40.refs_2_, ...), custom_call_target="tpu_custom_call" | custom-call | tf_op jit(solution)/shard_map/local0/pallas_call | solution.py:42
  8.7 1.6 %collective-permute-done.2.refs_1_.refs_0_ = f32[136,128]{1,0:T(8,128)S(1)} collective-permute-done((f32[136,128]{1,0:T(8,128)S(1)}, f32[136,128]{1,0:T(8,128)S(1)}, u32[]{:S(2)}, u32[]{:S(2)}) %collective-permute-start.2) | collective-permute-done | bytes 69664 | tf_op jit(solution)/shard_map/ppermute | solution.py:487
  10.3 0.6 %merge10.1 = (f32[136,128]{1,0:T(8,128)S(1)}, f32[8,128]{1,0:T(8,128)}) custom-call(f32[136,128]{1,0:T(8,128)S(1)} %get-tuple-element.50.refs_0_, f32[136,128]{1,0:T(8,128)S(1)} %collective-permute-done.2.refs_1_.refs_0_, f32[8,128]{1,0:T(8,128)S(1)} %get-tuple-element.49.refs_2_.refs_6_), custom_call_target="tpu_custom_call" | custom-call | tf_op jit(solution)/shard_map/merge10/pallas_call | solution.py:42
  10.9 2.2 %collective-permute-start.4 = (f32[136,128]{1,0:T(8,128)S(1)}, f32[136,128]{1,0:T(8,128)S(1)}, u32[]{:S(2)}, u32[]{:S(2)}) collective-permute-start(f32[136,128]{1,0:T(8,128)S(1)} %get-tuple-element.52.refs_3_.refs_0_), channel_id=1, source_target_pairs={{0,1},{8,9},{16,17},{24,25},{1,0},{9,8},{17,16},{25,24},{2,3},{10,... | collective-permute-start | bytes 208904 | tf_op jit(solution)/shard_map/ppermute | solution.py:487
  13.7 0.9 %local1.1 = (f32[1024,1024]{1,0:T(8,128)S(1)}, f32[8,128]{1,0:T(8,128)S(1)}) custom-call(bf16[1024,128]{1,0:T(8,128)(2,1)S(1)} %get-tuple-element.38.refs_0_.refs_1_, bf16[1024,128]{1,0:T(8,128)(2,1)S(1)} %get-tuple-element.39.refs_1_, bf16[1024,1024]{1,0:T(8,128)(2,1)S(1)} %get-tuple-element.40.refs_2_, ...), custom_call_target="tpu_custom_call", output_to_operand_aliasing={{0}: (7, {})} | custom-call | tf_op jit(solution)/shard_map/local1/pallas_call | solution.py:42
  14.6 1.0 %collective-permute-done.4.refs_1_.refs_0_ = f32[136,128]{1,0:T(8,128)S(1)} collective-permute-done((f32[136,128]{1,0:T(8,128)S(1)}, f32[136,128]{1,0:T(8,128)S(1)}, u32[]{:S(2)}, u32[]{:S(2)}) %collective-permute-start.4) | collective-permute-done | bytes 69664 | tf_op jit(solution)/shard_map/ppermute | solution.py:487
  16.2 1.9 %collective-permute-start.6 = (f32[136,128]{1,0:T(8,128)S(1)}, f32[136,128]{1,0:T(8,128)S(1)}, u32[]{:S(2)}, u32[]{:S(2)}) collective-permute-start(f32[136,128]{1,0:T(8,128)S(1)} %get-tuple-element.57.refs_3_.refs_0_), channel_id=1, source_target_pairs={{0,2},{8,10},{16,18},{24,26},{1,3},{9,11},{17,19},{25,27},{2,0},{1... | collective-permute-start | bytes 208904 | tf_op jit(solution)/shard_map/ppermute | solution.py:487
  18.1 1.1 %collective-permute-start.5 = (f32[136,128]{1,0:T(8,128)S(1)}, f32[136,128]{1,0:T(8,128)S(1)}, u32[]{:S(2)}, u32[]{:S(2)}) collective-permute-start(f32[136,128]{1,0:T(8,128)S(1)} %get-tuple-element.59.refs_8_.refs_0_.refs_2_), channel_id=1, source_target_pairs={{0,2},{8,10},{16,18},{24,26},{1,3},{9,11},{17,19},{25,27},{2,0},{1... | collective-permute-start | bytes 208904 | tf_op jit(solution)/shard_map/ppermute | solution.py:487
  19.2 1.8 %collective-permute-start.11 = (f32[256,128]{1,0:T(8,128)S(1)}, f32[256,128]{1,0:T(8,128)S(1)}, u32[]{:S(2)}, u32[]{:S(2)}) collective-permute-start(f32[256,128]{1,0:T(8,128)S(1)} %rest.1), channel_id=1, source_target_pairs={{0,16},{8,24},{16,0},{24,8},{1,17},{9,25},{17,1},{25,9},{2,18},{10... | collective-permute-start | bytes 393224 | tf_op jit(solution)/shard_map/ppermute | solution.py:487
  21.0 0.9 %local2.1 = (f32[1024,1024]{1,0:T(8,128)S(1)}, f32[8,128]{1,0:T(8,128)S(1)}) custom-call(bf16[1024,128]{1,0:T(8,128)(2,1)S(1)} %get-tuple-element.38.refs_0_.refs_1_, bf16[1024,128]{1,0:T(8,128)(2,1)S(1)} %get-tuple-element.39.refs_1_, bf16[1024,1024]{1,0:T(8,128)(2,1)S(1)} %get-tuple-element.40.refs_2_, ...), custom_call_target="tpu_custom_call", output_to_operand_aliasing={{0}: (7, {})} | custom-call | tf_op jit(solution)/shard_map/local2/pallas_call | solution.py:42
  22.9 1.8 %collective-permute-start.13 = (f32[256,128]{1,0:T(8,128)S(1)}, f32[256,128]{1,0:T(8,128)S(1)}, u32[]{:S(2)}, u32[]{:S(2)}) collective-permute-start(f32[256,128]{1,0:T(8,128)S(1)} %found3.1.refs_4_), channel_id=1, source_target_pairs={{0,16},{8,24},{16,0},{24,8},{1,17},{9,25},{17,1},{25,9},{2,18},{10... | collective-permute-start | bytes 393224 | tf_op jit(solution)/shard_map/ppermute | solution.py:487
  24.7 2.6 %collective-permute-start.7 = (f32[136,128]{1,0:T(8,128)S(1)}, f32[136,128]{1,0:T(8,128)S(1)}, u32[]{:S(2)}, u32[]{:S(2)}) collective-permute-start(f32[136,128]{1,0:T(8,128)S(1)} %get-tuple-element.62.refs_3_), channel_id=1, source_target_pairs={{0,4},{8,12},{16,20},{24,28},{1,5},{9,13},{17,21},{25,29},{2,6},{1... | collective-permute-start | bytes 208904 | tf_op jit(solution)/shard_map/ppermute | solution.py:487
  27.7 1.1 %local3.1.refs_0_ = f32[1024,1024]{1,0:T(8,128)S(1)} custom-call(bf16[1024,128]{1,0:T(8,128)(2,1)S(1)} %get-tuple-element.38.refs_0_.refs_1_, bf16[1024,128]{1,0:T(8,128)(2,1)S(1)} %get-tuple-element.39.refs_1_, bf16[1024,1024]{1,0:T(8,128)(2,1)S(1)} %get-tuple-element.40.refs_2_, ...), custom_call_target="tpu_custom_call", output_to_operand_aliasing={{}: (7, {})} | custom-call | tf_op jit(solution)/shard_map/local3/pallas_call | solution.py:42
  28.8 1.1 %reach.1 = (f32[1024,1024]{1,0:T(8,128)S(1)}, f32[8,128]{1,0:T(8,128)S(1)}) custom-call(f32[1024,1024]{1,0:T(8,128)S(1)} %local3.1.refs_0_, bf16[1024,128]{1,0:T(8,128)(2,1)S(1)} %get-tuple-element.38.refs_0_.refs_1_, f32[2,8,1024]{2,1,0:T(8,128)S(1)} %get-tuple-element.41.refs_3_.refs_2_, ...), custom_call_target="tpu_custom_call", output_to_operand_aliasing={{0}: (0, {})} | custom-call | tf_op jit(solution)/shard_map/reach/pallas_call | solution.py:42
  29.9 0.8 %collective-permute-done.7.refs_0_.refs_1_ = f32[136,128]{1,0:T(8,128)S(1)} collective-permute-done((f32[136,128]{1,0:T(8,128)S(1)}, f32[136,128]{1,0:T(8,128)S(1)}, u32[]{:S(2)}, u32[]{:S(2)}) %collective-permute-start.7) | collective-permute-done | bytes 69664 | tf_op jit(solution)/shard_map/ppermute | solution.py:487
  30.7 2.6 %collective-permute-done.8.refs_1_.refs_2_ = f32[136,128]{1,0:T(8,128)S(1)} collective-permute-done((f32[136,128]{1,0:T(8,128)S(1)}, f32[136,128]{1,0:T(8,128)S(1)}, u32[]{:S(2)}, u32[]{:S(2)}) %collective-permute-start.8) | collective-permute-done | bytes 69664 | tf_op jit(solution)/shard_map/ppermute | solution.py:487
  34.3 1.6 %finish00.1.refs_11_ = bf16[1024,1024]{1,0:T(8,128)(2,1)} custom-call(f32[1024,1024]{1,0:T(8,128)S(1)} %get-tuple-element.65.refs_0_, bf16[1024,128]{1,0:T(8,128)(2,1)S(1)} %get-tuple-element.38.refs_0_.refs_1_, f32[2,8,1024]{2,1,0:T(8,128)S(1)} %get-tuple-element.41.refs_3_.refs_2_, f32[8,8,1024]{2,1,0:T(8,128)S(1)} %get-tuple-element.43.refs_5_.refs_3_, ...), custom_call_target="tpu_custom_call" | custom-call | tf_op jit(solution)/shard_map/finish00/pallas_call | solution.py:464
  35.9 1.6 %finish10.1 = (bf16[1024,1024]{1,0:T(8,128)(2,1)}, f32[8,128]{1,0:T(8,128)S(1)}) custom-call(f32[1024,1024]{1,0:T(8,128)S(1)} %get-tuple-element.65.refs_0_, bf16[1024,128]{1,0:T(8,128)(2,1)S(1)} %get-tuple-element.38.refs_0_.refs_1_, f32[2,8,1024]{2,1,0:T(8,128)S(1)} %get-tuple-element.41.refs_3_.refs_2_, ...), custom_call_target="tpu_custom_call", output_to_operand_aliasing={{0}: (11, {})} | custom-call | tf_op jit(solution)/shard_map/finish10/pallas_call | solution.py:464
  37.5 2.0 %collective-permute-done.9.refs_0_ = f32[256,128]{1,0:T(8,128)S(1)} collective-permute-done((f32[256,128]{1,0:T(8,128)S(1)}, f32[256,128]{1,0:T(8,128)S(1)}, u32[]{:S(2)}, u32[]{:S(2)}) %collective-permute-start.9) | collective-permute-done | bytes 131104 | tf_op jit(solution)/shard_map/ppermute | solution.py:487
  39.6 1.6 %finish01.1.refs_11_ = bf16[1024,1024]{1,0:T(8,128)(2,1)} custom-call(f32[1024,1024]{1,0:T(8,128)S(1)} %get-tuple-element.65.refs_0_, bf16[1024,128]{1,0:T(8,128)(2,1)S(1)} %get-tuple-element.38.refs_0_.refs_1_, f32[2,8,1024]{2,1,0:T(8,128)S(1)} %get-tuple-element.41.refs_3_.refs_2_, ...), custom_call_target="tpu_custom_call", output_to_operand_aliasing={{}: (11, {})} | custom-call | tf_op jit(solution)/shard_map/finish01/pallas_call | solution.py:464
  41.2 1.6 %finish11.1 = bf16[1024,1024]{1,0:T(8,128)(2,1)} custom-call(f32[1024,1024]{1,0:T(8,128)S(1)} %get-tuple-element.65.refs_0_, bf16[1024,128]{1,0:T(8,128)(2,1)S(1)} %get-tuple-element.38.refs_0_.refs_1_, f32[2,8,1024]{2,1,0:T(8,128)S(1)} %get-tuple-element.41.refs_3_.refs_2_, ...), custom_call_target="tpu_custom_call", output_to_operand_aliasing={{}: (11, {})} | custom-call | tf_op jit(solution)/shard_map/finish11/pallas_call | solution.py:464
  (36 shorter events, 4.4 us)
Async XLA Ops:
  2.7 2.1 %collective-permute-start = (f32[1032,128]{1,0:T(8,128)S(1)}, f32[1032,128]{1,0:T(8,128)S(1)}, u32[]{:S(2)}, u32[]{:S(2)}) collective-permute-start(f32[1032,128]{1,0:T(8,128)S(1)} %get-tuple-element.45.mine_ref), channel_id=1, source_target_pairs={{0,8},{8,0},{16,24},{24,16},{1,9},{9,1},{17,25},{25,17},{2,10},{10... | collective-permute-start | bytes 1585160 | tf_op jit(solution)/shard_map/ppermute | solution.py:487
  4.8 5.5 %collective-permute-start.2 = (f32[136,128]{1,0:T(8,128)S(1)}, f32[136,128]{1,0:T(8,128)S(1)}, u32[]{:S(2)}, u32[]{:S(2)}) collective-permute-start(f32[136,128]{1,0:T(8,128)S(1)} %get-tuple-element.51), channel_id=1, source_target_pairs={{0,16},{8,24},{16,0},{24,8},{1,17},{9,25},{17,1},{25,9},{2,18},{10... | collective-permute-start | bytes 208904 | tf_op jit(solution)/shard_map/ppermute | solution.py:487
  7.8 5.3 %collective-permute-start.1 = (f32[136,128]{1,0:T(8,128)S(1)}, f32[136,128]{1,0:T(8,128)S(1)}, u32[]{:S(2)}, u32[]{:S(2)}) collective-permute-start(f32[136,128]{1,0:T(8,128)S(1)} %get-tuple-element.48), channel_id=1, source_target_pairs={{0,16},{8,24},{16,0},{24,8},{1,17},{9,25},{17,1},{25,9},{2,18},{10... | collective-permute-start | bytes 208904 | tf_op jit(solution)/shard_map/ppermute | solution.py:487
  10.9 4.7 %collective-permute-start.4 = (f32[136,128]{1,0:T(8,128)S(1)}, f32[136,128]{1,0:T(8,128)S(1)}, u32[]{:S(2)}, u32[]{:S(2)}) collective-permute-start(f32[136,128]{1,0:T(8,128)S(1)} %get-tuple-element.52.refs_3_.refs_0_), channel_id=1, source_target_pairs={{0,1},{8,9},{16,17},{24,25},{1,0},{9,8},{17,16},{25,24},{2,3},{10,... | collective-permute-start | bytes 208904 | tf_op jit(solution)/shard_map/ppermute | solution.py:487
  13.1 5.0 %collective-permute-start.3 = (f32[136,128]{1,0:T(8,128)S(1)}, f32[136,128]{1,0:T(8,128)S(1)}, u32[]{:S(2)}, u32[]{:S(2)}) collective-permute-start(f32[136,128]{1,0:T(8,128)S(1)} %get-tuple-element.54.refs_8_.refs_0_.refs_2_), channel_id=1, source_target_pairs={{0,1},{8,9},{16,17},{24,25},{1,0},{9,8},{17,16},{25,24},{2,3},{10,... | collective-permute-start | bytes 208904 | tf_op jit(solution)/shard_map/ppermute | solution.py:487
  16.2 6.1 %collective-permute-start.6 = (f32[136,128]{1,0:T(8,128)S(1)}, f32[136,128]{1,0:T(8,128)S(1)}, u32[]{:S(2)}, u32[]{:S(2)}) collective-permute-start(f32[136,128]{1,0:T(8,128)S(1)} %get-tuple-element.57.refs_3_.refs_0_), channel_id=1, source_target_pairs={{0,2},{8,10},{16,18},{24,26},{1,3},{9,11},{17,19},{25,27},{2,0},{1... | collective-permute-start | bytes 208904 | tf_op jit(solution)/shard_map/ppermute | solution.py:487
  18.1 4.7 %collective-permute-start.5 = (f32[136,128]{1,0:T(8,128)S(1)}, f32[136,128]{1,0:T(8,128)S(1)}, u32[]{:S(2)}, u32[]{:S(2)}) collective-permute-start(f32[136,128]{1,0:T(8,128)S(1)} %get-tuple-element.59.refs_8_.refs_0_.refs_2_), channel_id=1, source_target_pairs={{0,2},{8,10},{16,18},{24,26},{1,3},{9,11},{17,19},{25,27},{2,0},{1... | collective-permute-start | bytes 208904 | tf_op jit(solution)/shard_map/ppermute | solution.py:487
  19.2 14.1 %collective-permute-start.11 = (f32[256,128]{1,0:T(8,128)S(1)}, f32[256,128]{1,0:T(8,128)S(1)}, u32[]{:S(2)}, u32[]{:S(2)}) collective-permute-start(f32[256,128]{1,0:T(8,128)S(1)} %rest.1), channel_id=1, source_target_pairs={{0,16},{8,24},{16,0},{24,8},{1,17},{9,25},{17,1},{25,9},{2,18},{10... | collective-permute-start | bytes 393224 | tf_op jit(solution)/shard_map/ppermute | solution.py:487
  21.9 11.4 %collective-permute-start.12 = (f32[256,128]{1,0:T(8,128)S(1)}, f32[256,128]{1,0:T(8,128)S(1)}, u32[]{:S(2)}, u32[]{:S(2)}) collective-permute-start(f32[256,128]{1,0:T(8,128)S(1)} %found2.1.refs_2_), channel_id=1, source_target_pairs={{0,16},{8,24},{16,0},{24,8},{1,17},{9,25},{17,1},{25,9},{2,18},{10... | collective-permute-start | bytes 393224 | tf_op jit(solution)/shard_map/ppermute | solution.py:487
  22.9 10.4 %collective-permute-start.13 = (f32[256,128]{1,0:T(8,128)S(1)}, f32[256,128]{1,0:T(8,128)S(1)}, u32[]{:S(2)}, u32[]{:S(2)}) collective-permute-start(f32[256,128]{1,0:T(8,128)S(1)} %found3.1.refs_4_), channel_id=1, source_target_pairs={{0,16},{8,24},{16,0},{24,8},{1,17},{9,25},{17,1},{25,9},{2,18},{10... | collective-permute-start | bytes 393224 | tf_op jit(solution)/shard_map/ppermute | solution.py:487
  24.7 6.0 %collective-permute-start.7 = (f32[136,128]{1,0:T(8,128)S(1)}, f32[136,128]{1,0:T(8,128)S(1)}, u32[]{:S(2)}, u32[]{:S(2)}) collective-permute-start(f32[136,128]{1,0:T(8,128)S(1)} %get-tuple-element.62.refs_3_), channel_id=1, source_target_pairs={{0,4},{8,12},{16,20},{24,28},{1,5},{9,13},{17,21},{25,29},{2,6},{1... | collective-permute-start | bytes 208904 | tf_op jit(solution)/shard_map/ppermute | solution.py:487
  27.3 6.0 %collective-permute-start.8 = (f32[136,128]{1,0:T(8,128)S(1)}, f32[136,128]{1,0:T(8,128)S(1)}, u32[]{:S(2)}, u32[]{:S(2)}) collective-permute-start(f32[136,128]{1,0:T(8,128)S(1)} %get-tuple-element.64.refs_8_.refs_2_), channel_id=1, source_target_pairs={{0,4},{8,12},{16,20},{24,28},{1,5},{9,13},{17,21},{25,29},{2,6},{1... | collective-permute-start | bytes 208904 | tf_op jit(solution)/shard_map/ppermute | solution.py:487
  33.4 2.5 %collective-permute-start.14 = (f32[1536,128]{1,0:T(8,128)S(1)}, f32[1536,128]{1,0:T(8,128)S(1)}, u32[]{:S(2)}, u32[]{:S(2)}) collective-permute-start(f32[1536,128]{1,0:T(8,128)S(1)} %near.1.refs_10_), channel_id=1, source_target_pairs={{0,8},{8,0},{16,24},{24,16},{1,9},{9,1},{17,25},{25,17},{2,10},{10... | collective-permute-start | bytes 2359304 | tf_op jit(solution)/shard_map/ppermute | solution.py:487
  33.5 2.4 %collective-permute-start.10 = (f32[256,128]{1,0:T(8,128)S(1)}, f32[256,128]{1,0:T(8,128)S(1)}, u32[]{:S(2)}, u32[]{:S(2)}) collective-permute-start(f32[256,128]{1,0:T(8,128)S(1)} %state.1.refs_9_), channel_id=1, source_target_pairs={{0,8},{8,0},{16,24},{24,16},{1,9},{9,1},{17,25},{25,17},{2,10},{10... | collective-permute-start | bytes 393224 | tf_op jit(solution)/shard_map/ppermute | solution.py:487
  34.0 5.5 %collective-permute-start.9 = (f32[256,128]{1,0:T(8,128)S(1)}, f32[256,128]{1,0:T(8,128)S(1)}, u32[]{:S(2)}, u32[]{:S(2)}) collective-permute-start(f32[256,128]{1,0:T(8,128)S(1)} %state.1.refs_9_), channel_id=1, source_target_pairs={{0,16},{8,24},{16,0},{24,8},{1,17},{9,25},{17,1},{25,9},{2,18},{10... | collective-permute-start | bytes 393224 | tf_op jit(solution)/shard_map/ppermute | solution.py:487
  39.5 1.7 %collective-permute-start.15 = (f32[256,128]{1,0:T(8,128)S(1)}, f32[256,128]{1,0:T(8,128)S(1)}, u32[]{:S(2)}, u32[]{:S(2)}) collective-permute-start(f32[256,128]{1,0:T(8,128)S(1)} %beside.1.refs_9_), channel_id=1, source_target_pairs={{0,8},{8,0},{16,24},{24,16},{1,9},{9,1},{17,25},{25,17},{2,10},{10... | collective-permute-start | bytes 393224 | tf_op jit(solution)/shard_map/ppermute | solution.py:487

commit v12 on v11

--- a/solution.py
+++ b/solution.py
@@ -289,9 +289,9 @@
     return messages[:cuts], messages[cuts:], prefix
 
 
-def merge_kernel(bit, offset, *refs):
+def merge_kernel(bit, offset, has_prefix, *refs):
     mine_ref, other_ref, prefix_ref = refs[:3]
-    merged_ref, next_ref = refs[-2:]
+    merged_ref = refs[-2] if has_prefix else refs[-1]
     heads = prefix_ref.shape[0]
     rows = mine_ref.shape[0] - heads
     per = mine_ref.shape[1]
@@ -305,15 +305,16 @@
         )
     other_total = other_ref[rows:]
     merged_ref[rows:] = mine_ref[rows:] + other_total
-    next_ref[...] = prefix_ref[...] + jnp.where(upper, other_total, 0.0)
-
-
-def merge(bit, offset, mine, other, prefix, tokens=()):
+    if has_prefix:
+        refs[-1][...] = prefix_ref[...] + jnp.where(upper, other_total, 0.0)
+
+
+def merge(bit, offset, has_prefix, mine, other, prefix, tokens=()):
     return call(
-        functools.partial(merge_kernel, bit, offset),
+        functools.partial(merge_kernel, bit, offset, has_prefix),
         f"merge{bit}{offset}",
         [mine, other, prefix, *tokens],
-        [(mine.shape, jnp.float32), (prefix.shape, jnp.float32)],
+        [(mine.shape, jnp.float32), (prefix.shape, jnp.float32)][: 1 + has_prefix],
     )
 
 
@@ -518,22 +519,24 @@
         found[bit] = [trade(chunk, 2**bit) for chunk in (give if bit == 1 else chunks)]
         if bit == 1:
             rest = trade(both("rest", chunks), 2)
-        waits = ()
-        if at < spans:
+        waits = []
+        if bit < 3 or bit == last:
             stop = spans if bit == last else at + 1
             mixed, *waits = mix_local(at, stop, shared, mixed, chunks[-1:], bit < last)
             at = stop
+        if bit == 3:
+            waits.append(rest)
         if bit < last:
-            merged, tokens_of = [], ()
+            merged = []
             for offset, (chunk, state) in enumerate(zip(chunks, found[bit])):
-                tokens_of = (*tokens_of, *waits) if offset == CUTS - 1 else tokens_of
-                chunk, prefix = merge(
-                    bit, offset * two // CUTS // per, chunk, state, prefixes[bit], tokens_of
+                ending = offset == CUTS - 1
+                tokens_of = [*merged[-1:], *(waits if ending else ())]
+                chunk, *after = merge(
+                    bit, offset, ending, chunk, state, prefixes[bit], tokens_of
                 )
                 merged.append(chunk)
-                tokens_of = (chunk,)
             chunks = merged
-            prefixes.append(prefix)
+            prefixes += after
             found[bit] = both(f"found{bit}", found[bit], chunks[-1:])
             if bit > 1:
                 across[bit] = trade(found[bit], 2)

time: 43 us -> 41 us (0.953)
  starting transfers between devices: 17.1 us -> 19.3 us
  waiting for transfers between devices: 9.69 us -> 7.51 us
  Pallas kernels: 15.7 us -> 13.8 us
    ppermute x16, waiting for transfers between devices: 9.69 us -> 7.51 us  [trade(): return lax.ppermute(value, AXES, pairs)]
    ppermute x16, starting transfers between devices: 17.1 us -> 19.3 us  [trade(): return lax.ppermute(value, AXES, pairs)]
    pallas_call x23 -> x22, Pallas kernels: 9.47 us -> 7.5 us  [call(): pl.pallas_call(kernel, in_specs=specs, out_specs=[HELD] * len(outputs), o...]
  transfers between devices with their start and end apart: 16 -> 16, of which waited for: 6 -> 5; matrix products, arithmetic and copies ran while one was open for 0% -> 0% of each run, Pallas kernels for 27% -> 23%
where the time goes in v12:
time: 41 us; the launch traced here: 40.9 us
  starting transfers between devices  19.3 us (47%)
  Pallas kernels  13.8 us (34%)
  waiting for transfers between devices  7.51 us (18%)
    ppermute x16, starting transfers between devices, trade(): return lax.ppermute(value, AXES, pairs)  19.3 us
    ppermute x16, waiting for transfers between devices, trade(): return lax.ppermute(value, AXES, pairs)  7.51 us
    pallas_call x22, Pallas kernels, call(): pl.pallas_call(kernel, in_specs=specs, out_specs=[HELD] * len(outputs), o...  7.5 us
    pallas_call x4, Pallas kernels, finish(): pl.pallas_call(functools.partial(finish_kernel, quarters, first_level, bi...  6.29 us
  transfers between devices with their start and end apart: 16, of which 5 were waited for; matrix products, arithmetic and copies ran while one was open for 0% of the time, Pallas kernels for 23%

profile of v12, /device:TPU:0, one launch (start us, length us, event | category | flops | bytes accessed | tf_op | source)
XLA Modules:
  0.0 40.9 jit_solution(6917404650557762962)
XLA Ops:
  0.0 2.7 %states.1 = (f32[1032,128]{1,0:T(8,128)S(1)}, bf16[3,128,1024]{2,1,0:T(8,128)(2,1)S(1)}, f32[2,8,1024]{2,1,0:T(8,128)S(1)}, f32[4,8,128]{2,1,0:T(8,128)S(1)}, bf...) custom-call(bf16[1024,128]{1,0:T(8,128)(2,1)} %refs_0_.1, ...), custom_call_target="tpu_custom_call" | custom-call | tf_op jit(solution)/shard_map/states/pallas_call | solution.py:42
  3.2 1.5 %collective-permute-done.other_ref.refs_5_ = f32[1032,128]{1,0:T(8,128)S(1)} collective-permute-done((f32[1032,128]{1,0:T(8,128)S(1)}, f32[1032,128]{1,0:T(8,128)S(1)}, u32[]{:S(2)}, u32[]{:S(2)}) %collective-permute-start) | collective-permute-done | bytes 528416 | tf_op jit(solution)/shard_map/ppermute | solution.py:488
  4.8 3.0 %collective-permute-start.2 = (f32[136,128]{1,0:T(8,128)S(1)}, f32[136,128]{1,0:T(8,128)S(1)}, u32[]{:S(2)}, u32[]{:S(2)}) collective-permute-start(f32[136,128]{1,0:T(8,128)S(1)} %get-tuple-element.46), channel_id=1, source_target_pairs={{0,16},{8,24},{16,0},{24,8},{1,17},{9,25},{17,1},{25,9},{2,18},{10... | collective-permute-start | bytes 208904 | tf_op jit(solution)/shard_map/ppermute | solution.py:488
  7.9 0.8 %local0.1 = (f32[1024,1024]{1,0:T(8,128)S(1)}, f32[8,128]{1,0:T(8,128)S(1)}) custom-call(bf16[1024,128]{1,0:T(8,128)(2,1)S(1)} %get-tuple-element.33.refs_0_.refs_1_, bf16[1024,128]{1,0:T(8,128)(2,1)S(1)} %get-tuple-element.34.refs_1_, bf16[1024,1024]{1,0:T(8,128)(2,1)S(1)} %get-tuple-element.35.refs_2_, ...), custom_call_target="tpu_custom_call" | custom-call | tf_op jit(solution)/shard_map/local0/pallas_call | solution.py:42
  8.7 1.6 %collective-permute-done.2.refs_1_.refs_0_ = f32[136,128]{1,0:T(8,128)S(1)} collective-permute-done((f32[136,128]{1,0:T(8,128)S(1)}, f32[136,128]{1,0:T(8,128)S(1)}, u32[]{:S(2)}, u32[]{:S(2)}) %collective-permute-start.2) | collective-permute-done | bytes 69664 | tf_op jit(solution)/shard_map/ppermute | solution.py:488
  10.3 2.2 %collective-permute-start.4 = (f32[136,128]{1,0:T(8,128)S(1)}, f32[136,128]{1,0:T(8,128)S(1)}, u32[]{:S(2)}, u32[]{:S(2)}) collective-permute-start(f32[136,128]{1,0:T(8,128)S(1)} %merge10.1.refs_3_.refs_0_), channel_id=1, source_target_pairs={{0,1},{8,9},{16,17},{24,25},{1,0},{9,8},{17,16},{25,24},{2,3},{10,... | collective-permute-start | bytes 208904 | tf_op jit(solution)/shard_map/ppermute | solution.py:488
  12.6 1.1 %collective-permute-start.3 = (f32[136,128]{1,0:T(8,128)S(1)}, f32[136,128]{1,0:T(8,128)S(1)}, u32[]{:S(2)}, u32[]{:S(2)}) collective-permute-start(f32[136,128]{1,0:T(8,128)S(1)} %get-tuple-element.48.refs_8_.refs_0_.refs_2_), channel_id=1, source_target_pairs={{0,1},{8,9},{16,17},{24,25},{1,0},{9,8},{17,16},{25,24},{2,3},{10,... | collective-permute-start | bytes 208904 | tf_op jit(solution)/shard_map/ppermute | solution.py:488
  13.7 1.5 %collective-permute-start.7 = (f32[256,128]{1,0:T(8,128)S(1)}, f32[256,128]{1,0:T(8,128)S(1)}, u32[]{:S(2)}, u32[]{:S(2)}) collective-permute-start(f32[256,128]{1,0:T(8,128)S(1)} %rest.1), channel_id=1, source_target_pairs={{0,16},{8,24},{16,0},{24,8},{1,17},{9,25},{17,1},{25,9},{2,18},{10... | collective-permute-start | bytes 393224 | tf_op jit(solution)/shard_map/ppermute | solution.py:488
  15.2 0.9 %local1.1 = (f32[1024,1024]{1,0:T(8,128)S(1)}, f32[8,128]{1,0:T(8,128)S(1)}) custom-call(bf16[1024,128]{1,0:T(8,128)(2,1)S(1)} %get-tuple-element.33.refs_0_.refs_1_, bf16[1024,128]{1,0:T(8,128)(2,1)S(1)} %get-tuple-element.34.refs_1_, bf16[1024,1024]{1,0:T(8,128)(2,1)S(1)} %get-tuple-element.35.refs_2_, ...), custom_call_target="tpu_custom_call", output_to_operand_aliasing={{0}: (7, {})} | custom-call | tf_op jit(solution)/shard_map/local1/pallas_call | solution.py:42
  16.1 1.6 %collective-permute-start.6 = (f32[136,128]{1,0:T(8,128)S(1)}, f32[136,128]{1,0:T(8,128)S(1)}, u32[]{:S(2)}, u32[]{:S(2)}) collective-permute-start(f32[136,128]{1,0:T(8,128)S(1)} %merge20.1.refs_3_.refs_0_), channel_id=1, source_target_pairs={{0,2},{8,10},{16,18},{24,26},{1,3},{9,11},{17,19},{25,27},{2,0},{1... | collective-permute-start | bytes 208904 | tf_op jit(solution)/shard_map/ppermute | solution.py:488
  17.8 0.9 %collective-permute-start.5 = (f32[136,128]{1,0:T(8,128)S(1)}, f32[136,128]{1,0:T(8,128)S(1)}, u32[]{:S(2)}, u32[]{:S(2)}) collective-permute-start(f32[136,128]{1,0:T(8,128)S(1)} %get-tuple-element.52.refs_0_.refs_2_), channel_id=1, source_target_pairs={{0,2},{8,10},{16,18},{24,26},{1,3},{9,11},{17,19},{25,27},{2,0},{1... | collective-permute-start | bytes 208904 | tf_op jit(solution)/shard_map/ppermute | solution.py:488
  18.7 1.8 %collective-permute-start.12 = (f32[256,128]{1,0:T(8,128)S(1)}, f32[256,128]{1,0:T(8,128)S(1)}, u32[]{:S(2)}, u32[]{:S(2)}) collective-permute-start(f32[256,128]{1,0:T(8,128)S(1)} %found2.1.refs_2_), channel_id=1, source_target_pairs={{0,16},{8,24},{16,0},{24,8},{1,17},{9,25},{17,1},{25,9},{2,18},{10... | collective-permute-start | bytes 393224 | tf_op jit(solution)/shard_map/ppermute | solution.py:488
  20.6 1.6 %collective-permute-done.5.refs_1_ = f32[136,128]{1,0:T(8,128)S(1)} collective-permute-done((f32[136,128]{1,0:T(8,128)S(1)}, f32[136,128]{1,0:T(8,128)S(1)}, u32[]{:S(2)}, u32[]{:S(2)}) %collective-permute-start.5) | collective-permute-done | bytes 69664 | tf_op jit(solution)/shard_map/ppermute | solution.py:488
  22.2 1.2 %collective-permute-start.13 = (f32[256,128]{1,0:T(8,128)S(1)}, f32[256,128]{1,0:T(8,128)S(1)}, u32[]{:S(2)}, u32[]{:S(2)}) collective-permute-start(f32[256,128]{1,0:T(8,128)S(1)} %found3.1.refs_4_), channel_id=1, source_target_pairs={{0,16},{8,24},{16,0},{24,8},{1,17},{9,25},{17,1},{25,9},{2,18},{10... | collective-permute-start | bytes 393224 | tf_op jit(solution)/shard_map/ppermute | solution.py:488
  23.4 2.7 %collective-permute-start.8 = (f32[136,128]{1,0:T(8,128)S(1)}, f32[136,128]{1,0:T(8,128)S(1)}, u32[]{:S(2)}, u32[]{:S(2)}) collective-permute-start(f32[136,128]{1,0:T(8,128)S(1)} %merge30.1.refs_3_), channel_id=1, source_target_pairs={{0,4},{8,12},{16,20},{24,28},{1,5},{9,13},{17,21},{25,29},{2,6},{1... | collective-permute-start | bytes 208904 | tf_op jit(solution)/shard_map/ppermute | solution.py:488
  26.3 1.7 %local2.1.refs_0_ = f32[1024,1024]{1,0:T(8,128)S(1)} custom-call(bf16[1024,128]{1,0:T(8,128)(2,1)S(1)} %get-tuple-element.33.refs_0_.refs_1_, bf16[1024,128]{1,0:T(8,128)(2,1)S(1)} %get-tuple-element.34.refs_1_, bf16[1024,1024]{1,0:T(8,128)(2,1)S(1)} %get-tuple-element.35.refs_2_, ...), custom_call_target="tpu_custom_call", output_to_operand_aliasing={{}: (7, {})} | custom-call | tf_op jit(solution)/shard_map/local2/pallas_call | solution.py:42
  28.0 1.1 %reach.1 = (f32[1024,1024]{1,0:T(8,128)S(1)}, f32[8,128]{1,0:T(8,128)S(1)}) custom-call(f32[1024,1024]{1,0:T(8,128)S(1)} %local2.1.refs_0_, bf16[1024,128]{1,0:T(8,128)(2,1)S(1)} %get-tuple-element.33.refs_0_.refs_1_, f32[2,8,1024]{2,1,0:T(8,128)S(1)} %get-tuple-element.36.refs_3_.refs_2_, ...), custom_call_target="tpu_custom_call", output_to_operand_aliasing={{0}: (0, {})} | custom-call | tf_op jit(solution)/shard_map/reach/pallas_call | solution.py:42
  29.1 2.1 %collective-permute-done.9.refs_1_.refs_2_ = f32[136,128]{1,0:T(8,128)S(1)} collective-permute-done((f32[136,128]{1,0:T(8,128)S(1)}, f32[136,128]{1,0:T(8,128)S(1)}, u32[]{:S(2)}, u32[]{:S(2)}) %collective-permute-start.9) | collective-permute-done | bytes 69664 | tf_op jit(solution)/shard_map/ppermute | solution.py:488
  32.0 1.9 %collective-permute-start.10 = (f32[256,128]{1,0:T(8,128)S(1)}, f32[256,128]{1,0:T(8,128)S(1)}, u32[]{:S(2)}, u32[]{:S(2)}) collective-permute-start(f32[256,128]{1,0:T(8,128)S(1)} %state.1.refs_9_), channel_id=1, source_target_pairs={{0,16},{8,24},{16,0},{24,8},{1,17},{9,25},{17,1},{25,9},{2,18},{10... | collective-permute-start | bytes 393224 | tf_op jit(solution)/shard_map/ppermute | solution.py:488
  33.8 1.6 %finish00.1.refs_11_ = bf16[1024,1024]{1,0:T(8,128)(2,1)} custom-call(f32[1024,1024]{1,0:T(8,128)S(1)} %get-tuple-element.55.refs_0_, bf16[1024,128]{1,0:T(8,128)(2,1)S(1)} %get-tuple-element.33.refs_0_.refs_1_, f32[2,8,1024]{2,1,0:T(8,128)S(1)} %get-tuple-element.36.refs_3_.refs_2_, f32[8,8,1024]{2,1,0:T(8,128)S(1)} %get-tuple-element.38.refs_5_.refs_3_, ...), custom_call_target="tpu_custom_call" | custom-call | tf_op jit(solution)/shard_map/finish00/pallas_call | solution.py:465
  35.4 1.6 %finish10.1 = (bf16[1024,1024]{1,0:T(8,128)(2,1)}, f32[8,128]{1,0:T(8,128)S(1)}) custom-call(f32[1024,1024]{1,0:T(8,128)S(1)} %get-tuple-element.55.refs_0_, bf16[1024,128]{1,0:T(8,128)(2,1)S(1)} %get-tuple-element.33.refs_0_.refs_1_, f32[2,8,1024]{2,1,0:T(8,128)S(1)} %get-tuple-element.36.refs_3_.refs_2_, ...), custom_call_target="tpu_custom_call", output_to_operand_aliasing={{0}: (11, {})} | custom-call | tf_op jit(solution)/shard_map/finish10/pallas_call | solution.py:465
  37.0 0.6 %collective-permute-done.10.refs_0_ = f32[256,128]{1,0:T(8,128)S(1)} collective-permute-done((f32[256,128]{1,0:T(8,128)S(1)}, f32[256,128]{1,0:T(8,128)S(1)}, u32[]{:S(2)}, u32[]{:S(2)}) %collective-permute-start.10) | collective-permute-done | bytes 131104 | tf_op jit(solution)/shard_map/ppermute | solution.py:488
  37.7 1.6 %finish01.1.refs_11_ = bf16[1024,1024]{1,0:T(8,128)(2,1)} custom-call(f32[1024,1024]{1,0:T(8,128)S(1)} %get-tuple-element.55.refs_0_, bf16[1024,128]{1,0:T(8,128)(2,1)S(1)} %get-tuple-element.33.refs_0_.refs_1_, f32[2,8,1024]{2,1,0:T(8,128)S(1)} %get-tuple-element.36.refs_3_.refs_2_, ...), custom_call_target="tpu_custom_call", output_to_operand_aliasing={{}: (11, {})} | custom-call | tf_op jit(solution)/shard_map/finish01/pallas_call | solution.py:465
  39.3 1.6 %finish11.1 = bf16[1024,1024]{1,0:T(8,128)(2,1)} custom-call(f32[1024,1024]{1,0:T(8,128)S(1)} %get-tuple-element.55.refs_0_, bf16[1024,128]{1,0:T(8,128)(2,1)S(1)} %get-tuple-element.33.refs_0_.refs_1_, f32[2,8,1024]{2,1,0:T(8,128)S(1)} %get-tuple-element.36.refs_3_.refs_2_, ...), custom_call_target="tpu_custom_call", output_to_operand_aliasing={{}: (11, {})} | custom-call | tf_op jit(solution)/shard_map/finish11/pallas_call | solution.py:465
  (35 shorter events, 1.9 us)
Async XLA Ops:
  2.7 2.1 %collective-permute-start = (f32[1032,128]{1,0:T(8,128)S(1)}, f32[1032,128]{1,0:T(8,128)S(1)}, u32[]{:S(2)}, u32[]{:S(2)}) collective-permute-start(f32[1032,128]{1,0:T(8,128)S(1)} %get-tuple-element.40.mine_ref), channel_id=1, source_target_pairs={{0,8},{8,0},{16,24},{24,16},{1,9},{9,1},{17,25},{25,17},{2,10},{10... | collective-permute-start | bytes 1585160 | tf_op jit(solution)/shard_map/ppermute | solution.py:488
  4.8 5.5 %collective-permute-start.2 = (f32[136,128]{1,0:T(8,128)S(1)}, f32[136,128]{1,0:T(8,128)S(1)}, u32[]{:S(2)}, u32[]{:S(2)}) collective-permute-start(f32[136,128]{1,0:T(8,128)S(1)} %get-tuple-element.46), channel_id=1, source_target_pairs={{0,16},{8,24},{16,0},{24,8},{1,17},{9,25},{17,1},{25,9},{2,18},{10... | collective-permute-start | bytes 208904 | tf_op jit(solution)/shard_map/ppermute | solution.py:488
  7.8 4.8 %collective-permute-start.1 = (f32[136,128]{1,0:T(8,128)S(1)}, f32[136,128]{1,0:T(8,128)S(1)}, u32[]{:S(2)}, u32[]{:S(2)}) collective-permute-start(f32[136,128]{1,0:T(8,128)S(1)} %get-tuple-element.43), channel_id=1, source_target_pairs={{0,16},{8,24},{16,0},{24,8},{1,17},{9,25},{17,1},{25,9},{2,18},{10... | collective-permute-start | bytes 208904 | tf_op jit(solution)/shard_map/ppermute | solution.py:488
  10.3 5.7 %collective-permute-start.4 = (f32[136,128]{1,0:T(8,128)S(1)}, f32[136,128]{1,0:T(8,128)S(1)}, u32[]{:S(2)}, u32[]{:S(2)}) collective-permute-start(f32[136,128]{1,0:T(8,128)S(1)} %merge10.1.refs_3_.refs_0_), channel_id=1, source_target_pairs={{0,1},{8,9},{16,17},{24,25},{1,0},{9,8},{17,16},{25,24},{2,3},{10,... | collective-permute-start | bytes 208904 | tf_op jit(solution)/shard_map/ppermute | solution.py:488
  12.6 5.1 %collective-permute-start.3 = (f32[136,128]{1,0:T(8,128)S(1)}, f32[136,128]{1,0:T(8,128)S(1)}, u32[]{:S(2)}, u32[]{:S(2)}) collective-permute-start(f32[136,128]{1,0:T(8,128)S(1)} %get-tuple-element.48.refs_8_.refs_0_.refs_2_), channel_id=1, source_target_pairs={{0,1},{8,9},{16,17},{24,25},{1,0},{9,8},{17,16},{25,24},{2,3},{10,... | collective-permute-start | bytes 208904 | tf_op jit(solution)/shard_map/ppermute | solution.py:488
  13.7 6.8 %collective-permute-start.7 = (f32[256,128]{1,0:T(8,128)S(1)}, f32[256,128]{1,0:T(8,128)S(1)}, u32[]{:S(2)}, u32[]{:S(2)}) collective-permute-start(f32[256,128]{1,0:T(8,128)S(1)} %rest.1), channel_id=1, source_target_pairs={{0,16},{8,24},{16,0},{24,8},{1,17},{9,25},{17,1},{25,9},{2,18},{10... | collective-permute-start | bytes 393224 | tf_op jit(solution)/shard_map/ppermute | solution.py:488
  16.1 4.4 %collective-permute-start.6 = (f32[136,128]{1,0:T(8,128)S(1)}, f32[136,128]{1,0:T(8,128)S(1)}, u32[]{:S(2)}, u32[]{:S(2)}) collective-permute-start(f32[136,128]{1,0:T(8,128)S(1)} %merge20.1.refs_3_.refs_0_), channel_id=1, source_target_pairs={{0,2},{8,10},{16,18},{24,26},{1,3},{9,11},{17,19},{25,27},{2,0},{1... | collective-permute-start | bytes 208904 | tf_op jit(solution)/shard_map/ppermute | solution.py:488
  17.8 4.4 %collective-permute-start.5 = (f32[136,128]{1,0:T(8,128)S(1)}, f32[136,128]{1,0:T(8,128)S(1)}, u32[]{:S(2)}, u32[]{:S(2)}) collective-permute-start(f32[136,128]{1,0:T(8,128)S(1)} %get-tuple-element.52.refs_0_.refs_2_), channel_id=1, source_target_pairs={{0,2},{8,10},{16,18},{24,26},{1,3},{9,11},{17,19},{25,27},{2,0},{1... | collective-permute-start | bytes 208904 | tf_op jit(solution)/shard_map/ppermute | solution.py:488
  18.7 12.6 %collective-permute-start.12 = (f32[256,128]{1,0:T(8,128)S(1)}, f32[256,128]{1,0:T(8,128)S(1)}, u32[]{:S(2)}, u32[]{:S(2)}) collective-permute-start(f32[256,128]{1,0:T(8,128)S(1)} %found2.1.refs_2_), channel_id=1, source_target_pairs={{0,16},{8,24},{16,0},{24,8},{1,17},{9,25},{17,1},{25,9},{2,18},{10... | collective-permute-start | bytes 393224 | tf_op jit(solution)/shard_map/ppermute | solution.py:488
  22.2 9.1 %collective-permute-start.13 = (f32[256,128]{1,0:T(8,128)S(1)}, f32[256,128]{1,0:T(8,128)S(1)}, u32[]{:S(2)}, u32[]{:S(2)}) collective-permute-start(f32[256,128]{1,0:T(8,128)S(1)} %found3.1.refs_4_), channel_id=1, source_target_pairs={{0,16},{8,24},{16,0},{24,8},{1,17},{9,25},{17,1},{25,9},{2,18},{10... | collective-permute-start | bytes 393224 | tf_op jit(solution)/shard_map/ppermute | solution.py:488
  23.4 5.8 %collective-permute-start.8 = (f32[136,128]{1,0:T(8,128)S(1)}, f32[136,128]{1,0:T(8,128)S(1)}, u32[]{:S(2)}, u32[]{:S(2)}) collective-permute-start(f32[136,128]{1,0:T(8,128)S(1)} %merge30.1.refs_3_), channel_id=1, source_target_pairs={{0,4},{8,12},{16,20},{24,28},{1,5},{9,13},{17,21},{25,29},{2,6},{1... | collective-permute-start | bytes 208904 | tf_op jit(solution)/shard_map/ppermute | solution.py:488
  26.0 5.2 %collective-permute-start.9 = (f32[136,128]{1,0:T(8,128)S(1)}, f32[136,128]{1,0:T(8,128)S(1)}, u32[]{:S(2)}, u32[]{:S(2)}) collective-permute-start(f32[136,128]{1,0:T(8,128)S(1)} %get-tuple-element.54.refs_8_.refs_2_), channel_id=1, source_target_pairs={{0,4},{8,12},{16,20},{24,28},{1,5},{9,13},{17,21},{25,29},{2,6},{1... | collective-permute-start | bytes 208904 | tf_op jit(solution)/shard_map/ppermute | solution.py:488
  31.3 4.1 %collective-permute-start.14 = (f32[1536,128]{1,0:T(8,128)S(1)}, f32[1536,128]{1,0:T(8,128)S(1)}, u32[]{:S(2)}, u32[]{:S(2)}) collective-permute-start(f32[1536,128]{1,0:T(8,128)S(1)} %near.1.refs_10_), channel_id=1, source_target_pairs={{0,8},{8,0},{16,24},{24,16},{1,9},{9,1},{17,25},{25,17},{2,10},{10... | collective-permute-start | bytes 2359304 | tf_op jit(solution)/shard_map/ppermute | solution.py:488
  31.4 4.0 %collective-permute-start.11 = (f32[256,128]{1,0:T(8,128)S(1)}, f32[256,128]{1,0:T(8,128)S(1)}, u32[]{:S(2)}, u32[]{:S(2)}) collective-permute-start(f32[256,128]{1,0:T(8,128)S(1)} %state.1.refs_9_), channel_id=1, source_target_pairs={{0,8},{8,0},{16,24},{24,16},{1,9},{9,1},{17,25},{25,17},{2,10},{10... | collective-permute-start | bytes 393224 | tf_op jit(solution)/shard_map/ppermute | solution.py:488
  32.0 5.6 %collective-permute-start.10 = (f32[256,128]{1,0:T(8,128)S(1)}, f32[256,128]{1,0:T(8,128)S(1)}, u32[]{:S(2)}, u32[]{:S(2)}) collective-permute-start(f32[256,128]{1,0:T(8,128)S(1)} %state.1.refs_9_), channel_id=1, source_target_pairs={{0,16},{8,24},{16,0},{24,8},{1,17},{9,25},{17,1},{25,9},{2,18},{10... | collective-permute-start | bytes 393224 | tf_op jit(solution)/shard_map/ppermute | solution.py:488
  37.6 1.7 %collective-permute-start.15 = (f32[256,128]{1,0:T(8,128)S(1)}, f32[256,128]{1,0:T(8,128)S(1)}, u32[]{:S(2)}, u32[]{:S(2)}) collective-permute-start(f32[256,128]{1,0:T(8,128)S(1)} %beside.1.refs_9_), channel_id=1, source_target_pairs={{0,8},{8,0},{16,24},{24,16},{1,9},{9,1},{17,25},{25,17},{2,10},{10... | collective-permute-start | bytes 393224 | tf_op jit(solution)/shard_map/ppermute | solution.py:488

commit v13 on v12

--- a/solution.py
+++ b/solution.py
@@ -13,6 +13,7 @@
 EPS = 1e-05
 AXES = ("narrow", "wide")
 NT = (((1,), (1,)), ((), ()))
+COST = pl.CostEstimate(flops=2_000_000_000, transcendentals=0, bytes_accessed=1_000_000)
 PARAMS = pltpu.CompilerParams(vmem_limit_bytes=32 * 1024 * 1024)
 HELD = pl.BlockSpec(memory_space=pltpu.VMEM)
 
@@ -47,6 +48,7 @@
         scratch_shapes=list(scratch),
         input_output_aliases=aliases or {},
         compiler_params=PARAMS,
+        cost_estimate=COST,
         name=name,
     )(*inputs)
 
@@ -69,8 +71,8 @@
 
 def state_kernel(*refs):
     q_hbm, k_hbm, v_hbm, decay_hbm, weight_hbm, gain_hbm = refs[:6]
-    message_ref, local_ref, sums_ref, totals_ref = refs[6:10]
-    q_ref, k_ref, v_ref, weight_ref, gain_ref, decay_ref, arrived = refs[10:]
+    keep_ref, send_ref, local_ref, sums_ref, totals_ref = refs[6:11]
+    q_ref, k_ref, v_ref, weight_ref, gain_ref, decay_ref, held, arrived = refs[11:]
     heads, tokens = decay_ref.shape
     head_width = v_ref.shape[1] // heads
     spans = tokens // SPAN
@@ -123,8 +125,13 @@
         group = states[0]
         for span in range(1, spans):
             group = group * wholes[span][head : head + 1] + states[span]
-        message_ref[columns] = group.T
-    message_ref[heads * head_width :] = run
+        held[columns] = group.T
+    half = held.shape[0] // 2
+    core = bit_of(place(), 0)
+    keep_ref[:half] = held[pl.ds(pl.multiple_of(core * half, 8), half)]
+    send_ref[:half] = held[pl.ds(pl.multiple_of((1 - core) * half, 8), half)]
+    keep_ref[half:] = run
+    send_ref[half:] = run
     for copy in copies[2 + spans :]:
         copy.wait()
 
@@ -141,7 +148,8 @@
         "states",
         [pltpu.with_memory_space_constraint(array, pltpu.HBM) for array in inputs],
         [
-            ((width + heads, key_width), jnp.float32),
+            ((width // 2 + heads, key_width), jnp.float32),
+            ((width // 2 + heads, key_width), jnp.float32),
             ((spans - 1, key_width, width), jnp.bfloat16),
             ((2, heads, tokens), jnp.float32),
             ((spans, heads, 128), jnp.float32),
@@ -149,6 +157,7 @@
         ],
         [
             pltpu.VMEM(log_decay.shape, jnp.float32),
+            pltpu.VMEM((width, key_width), jnp.float32),
             pltpu.SemaphoreType.DMA((spans + 5,)),
         ],
         [pl.BlockSpec(memory_space=pltpu.HBM)] * len(inputs),
@@ -248,22 +257,22 @@
 def chip_kernel(mine_ref, other_ref, *refs):
     *message_refs, next_ref, whole_ref = refs
     heads = next_ref.shape[0]
-    width = mine_ref.shape[0] - heads
-    per = width // heads
-    held = whole_ref.shape[0] // per
+    width = whole_ref.shape[0]
+    held = heads // 2
+    per = width // held
     here = place()
     upper = bit_of(here, 0) == 1
     first = first_head((0,), heads)
     for slot in range(held):
-        part = pl.ds(pl.multiple_of((first + slot) * per, 8), per)
+        part = slice(slot * per, (slot + 1) * per)
         total = pl.ds(width + first + slot, 1)
-        whole_ref[slot * per : (slot + 1) * per] = join(
+        whole_ref[part] = join(
             upper, mine_ref[part], mine_ref[total], other_ref[part], other_ref[total]
         )
     other_total = other_ref[width:]
     total = mine_ref[width:] + other_total
     next_ref[...] = jnp.where(upper, other_total, 0.0)
-    half = held * per // 2
+    half = width // 2
     side = bit_of(here, 1)
     cuts = len(message_refs) // 2
     size = half // cuts
@@ -275,7 +284,7 @@
 
 def make_chip(mine, other, heads, cuts):
     rows, lanes = mine.shape
-    half = (rows - heads) // 2
+    half = rows - heads
     *messages, prefix = call(
         chip_kernel,
         "chip",
@@ -347,13 +356,10 @@
     work = []
     for far, pieces in quarters:
         first = first_head(far, heads)
-        for slot in range(heads // 4):
+        for slot in range(heads >> len(far)):
             states = []
             for level, index, start in pieces:
-                if start is None:
-                    rows = pl.ds(pl.multiple_of((first + slot) * per, 128), per)
-                else:
-                    rows = slice(start + slot * per, start + (slot + 1) * per)
+                rows = slice(start + slot * per, start + (slot + 1) * per)
                 states.append((level, part_refs[index][rows].astype(jnp.bfloat16)))
             work.append((first + slot, states))
     return work
@@ -474,6 +480,7 @@
         ],
         input_output_aliases=aliases,
         compiler_params=PARAMS,
+        cost_estimate=COST,
         name="finish" + "".join(f"{core}{side}" for (core, side), _ in quarters),
     )(*inputs)
 
@@ -497,7 +504,7 @@
     bits = (lax.axis_size("wide") * lax.axis_size("narrow")).bit_length() - 1
     first_level = level_weight.shape[0] - bits
     gain = norm_gain.reshape(heads, per)
-    message, local, sums, totals, queries, keys, values, level_weight, gain = make_states(
+    keep, send, local, sums, totals, queries, keys, values, level_weight, gain = make_states(
         queries, keys, values, log_decay, level_weight, gain
     )
     shared = (queries, keys, values, sums, totals, level_weight, local)
@@ -505,9 +512,10 @@
     two = 2 * per
     size = two // CUTS
     sides = [(core, side) for core in (0, 1) for side in (0, 1)]
-    other = trade(message, 1)
+    other = trade(send, 1)
     zero = jnp.zeros((heads, 128), jnp.float32)
-    chunks, give, prefix = make_chip(message, other, heads, CUTS)
+    chunks, give, prefix = make_chip(keep, other, heads, CUTS)
+    other_rest = trade(pack("kept", [(keep, width // 2)], chunks[:1]), 1)
     prefixes = [zero, prefix]
     found, across = {}, {}
     mixed, at = None, 0
@@ -517,12 +525,12 @@
 
     for bit in range(1, bits):
         found[bit] = [trade(chunk, 2**bit) for chunk in (give if bit == 1 else chunks)]
-        if bit == 1:
-            rest = trade(both("rest", chunks), 2)
+        stays = chunks if bit == 1 else stays
         waits = []
         if bit < 3 or bit == last:
             stop = spans if bit == last else at + 1
-            mixed, *waits = mix_local(at, stop, shared, mixed, chunks[-1:], bit < last)
+            begun = [*chunks[-1:], *([other_rest] if bit == 1 else [])]
+            mixed, *waits = mix_local(at, stop, shared, mixed, begun, bit < last)
             at = stop
         if bit == 3:
             waits.append(rest)
@@ -540,20 +548,17 @@
             found[bit] = both(f"found{bit}", found[bit], chunks[-1:])
             if bit > 1:
                 across[bit] = trade(found[bit], 2)
-
-    quarters = [((core, side), [(0, 0, None)]) for core, side in sides]
+            else:
+                rest = trade(both("rest", stays, chunks[-1:]), 2)
+
+    halves = [((core,), [(0, core, 0)]) for core in (0, 1)]
     shared = (mixed, queries, sums, level_weight)
-    mixed, token = add_levels(quarters, first_level, [0], shared, [zero], [other])
-    ended = token
-    ended = pack("ended0", [(ended, 8)], found[last])
-    ended = pack("ended1", [(ended, 8)])
-    ended = pack("ended2", [(ended, 8)])
+    mixed, token = add_levels(halves, first_level, [0], shared, [zero], [other, other_rest])
     early = list(range(2, last))
     pieces = [(found[1], two), (rest, two)]
     for bit in early:
         pieces += [(found[bit], two), (across[bit], two)]
-    near = pack("near", pieces, (ended,))
-    far = trade(near, 1)
+    near = pack("near", pieces, (token,))
     middle = [1, *early]
     ahead = [prefixes[bit] for bit in middle]
 
@@ -565,11 +570,14 @@
     state = both("state", found[last])
     beside = trade(state, 2)
     quarters = {(core, side): [(0, 0, 0), *states_of(side, 1, 1)] for core, side in sides}
-    (out,) = finish([((0, 0), quarters[0, 0])], *every, [state, near], None, False)
-    out, token = finish([((1, 0), quarters[1, 0])], *every, [trade(state, 1), far], out, True)
+    out, token = finish([((0, 0), quarters[0, 0])], *every, [state, near], None, True)
+    far = trade(near, 1)
     beside = pack("beside", [(beside, two)], (token,))
     (out,) = finish([((0, 1), quarters[0, 1])], *every, [beside, near], out, False)
-    return finish([((1, 1), quarters[1, 1])], *every, [trade(beside, 1), far], out, False)[0]
+    state_far, beside_far = trade(state, 1), trade(beside, 1)
+    pairs = [((1, 0), quarters[1, 0])]
+    pairs.append(((1, 1), [(0, 2, 0), *states_of(1, 1, 1)]))
+    return finish(pairs, *every, [state_far, far, beside_far], out, False)[0]
 
 
 def solution(mesh):

time: 41 us -> 45.4 us (1.11)
  starting transfers between devices: 19.3 us -> 22.1 us
  waiting for transfers between devices: 7.51 us -> 9.71 us
  Pallas kernels: 13.8 us -> 13.2 us
    ppermute x16 -> x17, starting transfers between devices: 19.3 us -> 22.1 us  [trade(): return lax.ppermute(value, AXES, pairs)]
    ppermute x16 -> x17, waiting for transfers between devices: 7.51 us -> 9.71 us  [trade(): return lax.ppermute(value, AXES, pairs)]
    pallas_call x4 -> x3, Pallas kernels: 6.29 us -> 5.52 us  [finish(): pl.pallas_call(functools.partial(finish_kernel, quarters, first_level, bi...]
    pallas_call x22 -> x20, Pallas kernels: 7.5 us -> 7.72 us  [call(): pl.pallas_call(kernel, in_specs=specs, out_specs=[HELD] * len(outputs), o...]
  transfers between devices with their start and end apart: 16 -> 17, of which waited for: 5 -> 7; matrix products, arithmetic and copies ran while one was open for 0% -> 0% of each run, Pallas kernels for 23% -> 18%
where the time goes in v13:
time: 45.4 us; the launch traced here: 45.3 us
  starting transfers between devices  22.1 us (49%)
  Pallas kernels  13.2 us (29%)
  waiting for transfers between devices  9.71 us (21%)
    ppermute x17, starting transfers between devices, trade(): return lax.ppermute(value, AXES, pairs)  22.1 us
    ppermute x17, waiting for transfers between devices, trade(): return lax.ppermute(value, AXES, pairs)  9.71 us
    pallas_call x20, Pallas kernels, call(): pl.pallas_call(kernel, in_specs=specs, out_specs=[HELD] * len(outputs), o...  7.72 us
    pallas_call x3, Pallas kernels, finish(): pl.pallas_call(functools.partial(finish_kernel, quarters, first_level, bi...  5.52 us
  transfers between devices with their start and end apart: 17, of which 7 were waited for; matrix products, arithmetic and copies ran while one was open for 0% of the time, Pallas kernels for 18%

profile of v13, /device:TPU:0, one launch (start us, length us, event | category | flops | bytes accessed | tf_op | source)
XLA Modules:
  0.0 45.3 jit_solution(415358616698861622)
XLA Ops:
  0.0 2.8 %states.1 = (f32[520,128]{1,0:T(8,128)S(1)}, f32[520,128]{1,0:T(8,128)S(1)}, bf16[3,128,1024]{2,1,0:T(8,128)(2,1)S(1)}, f32[2,8,1024]{2,1,0:T(8,128)S(1)}, f32[4...) custom-call(bf16[1024,128]{1,0:T(8,128)(2,1)} %refs_0_.1, ...), custom_call_target="tpu_custom_call" | custom-call | flops 2000000000 | bytes 1000000 | tf_op jit(solution)/shard_map/states/pallas_call | solution.py:43
  2.8 0.5 %collective-permute-start = (f32[520,128]{1,0:T(8,128)S(1)}, f32[520,128]{1,0:T(8,128)S(1)}, u32[]{:S(2)}, u32[]{:S(2)}) collective-permute-start(f32[520,128]{1,0:T(8,128)S(1)} %get-tuple-element.42), channel_id=1, source_target_pairs={{0,8},{8,0},{16,24},{24,16},{1,9},{9,1},{17,25},{25,17},{2,10},{10... | collective-permute-start | bytes 798728 | tf_op jit(solution)/shard_map/ppermute | solution.py:495
  3.3 1.2 %collective-permute-done.other_ref.refs_5_ = f32[520,128]{1,0:T(8,128)S(1)} collective-permute-done((f32[520,128]{1,0:T(8,128)S(1)}, f32[520,128]{1,0:T(8,128)S(1)}, u32[]{:S(2)}, u32[]{:S(2)}) %collective-permute-start) | collective-permute-done | bytes 266272 | tf_op jit(solution)/shard_map/ppermute | solution.py:495
  4.6 0.4 collective-permute-start.1
  5.0 2.7 %collective-permute-start.3 = (f32[136,128]{1,0:T(8,128)S(1)}, f32[136,128]{1,0:T(8,128)S(1)}, u32[]{:S(2)}, u32[]{:S(2)}) collective-permute-start(f32[136,128]{1,0:T(8,128)S(1)} %get-tuple-element.48), channel_id=1, source_target_pairs={{0,16},{8,24},{16,0},{24,8},{1,17},{9,25},{17,1},{25,9},{2,18},{10... | collective-permute-start | bytes 208904 | tf_op jit(solution)/shard_map/ppermute | solution.py:495
  7.7 2.7 %collective-permute-done.3.refs_1_.refs_0_ = f32[136,128]{1,0:T(8,128)S(1)} collective-permute-done((f32[136,128]{1,0:T(8,128)S(1)}, f32[136,128]{1,0:T(8,128)S(1)}, u32[]{:S(2)}, u32[]{:S(2)}) %collective-permute-start.3) | collective-permute-done | bytes 69664 | tf_op jit(solution)/shard_map/ppermute | solution.py:495
  10.4 2.1 %collective-permute-start.5 = (f32[136,128]{1,0:T(8,128)S(1)}, f32[136,128]{1,0:T(8,128)S(1)}, u32[]{:S(2)}, u32[]{:S(2)}) collective-permute-start(f32[136,128]{1,0:T(8,128)S(1)} %merge10.1.refs_3_.refs_0_), channel_id=1, source_target_pairs={{0,1},{8,9},{16,17},{24,25},{1,0},{9,8},{17,16},{25,24},{2,3},{10,... | collective-permute-start | bytes 208904 | tf_op jit(solution)/shard_map/ppermute | solution.py:495
  12.5 0.8 %local0.1 = (f32[1024,1024]{1,0:T(8,128)S(1)}, f32[8,128]{1,0:T(8,128)S(1)}) custom-call(bf16[1024,128]{1,0:T(8,128)(2,1)S(1)} %get-tuple-element.34.refs_0_.refs_1_, bf16[1024,128]{1,0:T(8,128)(2,1)S(1)} %get-tuple-element.35.refs_1_, bf16[1024,1024]{1,0:T(8,128)(2,1)S(1)} %get-tuple-element.36.refs_2_, ...), custom_call_target="tpu_custom_call" | custom-call | flops 2000000000 | bytes 1000000 | tf_op jit(solution)/shard_map/local0/pallas_call | solution.py:43
  13.7 0.9 %local1.1 = (f32[1024,1024]{1,0:T(8,128)S(1)}, f32[8,128]{1,0:T(8,128)S(1)}) custom-call(bf16[1024,128]{1,0:T(8,128)(2,1)S(1)} %get-tuple-element.34.refs_0_.refs_1_, bf16[1024,128]{1,0:T(8,128)(2,1)S(1)} %get-tuple-element.35.refs_1_, bf16[1024,1024]{1,0:T(8,128)(2,1)S(1)} %get-tuple-element.36.refs_2_, ...), custom_call_target="tpu_custom_call", output_to_operand_aliasing={{0}: (7, {})} | custom-call | flops 2000000000 | bytes 1000000 | tf_op jit(solution)/shard_map/local1/pallas_call | solution.py:43
  14.8 2.5 %collective-permute-start.7 = (f32[136,128]{1,0:T(8,128)S(1)}, f32[136,128]{1,0:T(8,128)S(1)}, u32[]{:S(2)}, u32[]{:S(2)}) collective-permute-start(f32[136,128]{1,0:T(8,128)S(1)} %merge20.1.refs_3_.refs_0_), channel_id=1, source_target_pairs={{0,2},{8,10},{16,18},{24,26},{1,3},{9,11},{17,19},{25,27},{2,0},{1... | collective-permute-start | bytes 208904 | tf_op jit(solution)/shard_map/ppermute | solution.py:495
  17.4 1.9 %collective-permute-start.8 = (f32[256,128]{1,0:T(8,128)S(1)}, f32[256,128]{1,0:T(8,128)S(1)}, u32[]{:S(2)}, u32[]{:S(2)}) collective-permute-start(f32[256,128]{1,0:T(8,128)S(1)} %rest.1), channel_id=1, source_target_pairs={{0,16},{8,24},{16,0},{24,8},{1,17},{9,25},{17,1},{25,9},{2,18},{10... | collective-permute-start | bytes 393224 | tf_op jit(solution)/shard_map/ppermute | solution.py:495
  19.7 3.4 %collective-permute-start.9 = (f32[136,128]{1,0:T(8,128)S(1)}, f32[136,128]{1,0:T(8,128)S(1)}, u32[]{:S(2)}, u32[]{:S(2)}) collective-permute-start(f32[136,128]{1,0:T(8,128)S(1)} %merge30.1.refs_3_), channel_id=1, source_target_pairs={{0,4},{8,12},{16,20},{24,28},{1,5},{9,13},{17,21},{25,29},{2,6},{1... | collective-permute-start | bytes 208904 | tf_op jit(solution)/shard_map/ppermute | solution.py:495
  23.1 1.3 %collective-permute-start.6 = (f32[136,128]{1,0:T(8,128)S(1)}, f32[136,128]{1,0:T(8,128)S(1)}, u32[]{:S(2)}, u32[]{:S(2)}) collective-permute-start(f32[136,128]{1,0:T(8,128)S(1)} %get-tuple-element.54.refs_0_.refs_2_), channel_id=1, source_target_pairs={{0,2},{8,10},{16,18},{24,26},{1,3},{9,11},{17,19},{25,27},{2,0},{1... | collective-permute-start | bytes 208904 | tf_op jit(solution)/shard_map/ppermute | solution.py:495
  24.4 2.4 %collective-permute-start.12 = (f32[256,128]{1,0:T(8,128)S(1)}, f32[256,128]{1,0:T(8,128)S(1)}, u32[]{:S(2)}, u32[]{:S(2)}) collective-permute-start(f32[256,128]{1,0:T(8,128)S(1)} %found2.1.refs_2_), channel_id=1, source_target_pairs={{0,16},{8,24},{16,0},{24,8},{1,17},{9,25},{17,1},{25,9},{2,18},{10... | collective-permute-start | bytes 393224 | tf_op jit(solution)/shard_map/ppermute | solution.py:495
  26.8 1.2 %collective-permute-done.6.refs_1_ = f32[136,128]{1,0:T(8,128)S(1)} collective-permute-done((f32[136,128]{1,0:T(8,128)S(1)}, f32[136,128]{1,0:T(8,128)S(1)}, u32[]{:S(2)}, u32[]{:S(2)}) %collective-permute-start.6) | collective-permute-done | bytes 69664 | tf_op jit(solution)/shard_map/ppermute | solution.py:495
  28.1 1.7 %local2.1.refs_0_ = f32[1024,1024]{1,0:T(8,128)S(1)} custom-call(bf16[1024,128]{1,0:T(8,128)(2,1)S(1)} %get-tuple-element.34.refs_0_.refs_1_, bf16[1024,128]{1,0:T(8,128)(2,1)S(1)} %get-tuple-element.35.refs_1_, bf16[1024,1024]{1,0:T(8,128)(2,1)S(1)} %get-tuple-element.36.refs_2_, ...), custom_call_target="tpu_custom_call", output_to_operand_aliasing={{}: (7, {})} | custom-call | flops 2000000000 | bytes 1000000 | tf_op jit(solution)/shard_map/local2/pallas_call | solution.py:43
  29.9 2.0 %collective-permute-start.13 = (f32[256,128]{1,0:T(8,128)S(1)}, f32[256,128]{1,0:T(8,128)S(1)}, u32[]{:S(2)}, u32[]{:S(2)}) collective-permute-start(f32[256,128]{1,0:T(8,128)S(1)} %found3.1.refs_4_), channel_id=1, source_target_pairs={{0,16},{8,24},{16,0},{24,8},{1,17},{9,25},{17,1},{25,9},{2,18},{10... | collective-permute-start | bytes 393224 | tf_op jit(solution)/shard_map/ppermute | solution.py:495
  31.8 1.2 %reach.1 = (f32[1024,1024]{1,0:T(8,128)S(1)}, f32[8,128]{1,0:T(8,128)S(1)}) custom-call(f32[1024,1024]{1,0:T(8,128)S(1)} %local2.1.refs_0_, bf16[1024,128]{1,0:T(8,128)(2,1)S(1)} %get-tuple-element.34.refs_0_.refs_1_, f32[2,8,1024]{2,1,0:T(8,128)S(1)} %get-tuple-element.37.refs_3_.refs_2_, ...), custom_call_target="tpu_custom_call", output_to_operand_aliasing={{0}: (0, {})} | custom-call | flops 2000000000 | bytes 1000000 | tf_op jit(solution)/shard_map/reach/pallas_call | solution.py:43
  33.1 1.8 %collective-permute-done.13.refs_5_ = f32[256,128]{1,0:T(8,128)S(1)} collective-permute-done((f32[256,128]{1,0:T(8,128)S(1)}, f32[256,128]{1,0:T(8,128)S(1)}, u32[]{:S(2)}, u32[]{:S(2)}) %collective-permute-start.13) | collective-permute-done | bytes 131104 | tf_op jit(solution)/shard_map/ppermute | solution.py:495
  35.1 2.0 %collective-permute-start.15 = (f32[256,128]{1,0:T(8,128)S(1)}, f32[256,128]{1,0:T(8,128)S(1)}, u32[]{:S(2)}, u32[]{:S(2)}) collective-permute-start(f32[256,128]{1,0:T(8,128)S(1)} %state.1.refs_9_), channel_id=1, source_target_pairs={{0,16},{8,24},{16,0},{24,8},{1,17},{9,25},{17,1},{25,9},{2,18},{10... | collective-permute-start | bytes 393224 | tf_op jit(solution)/shard_map/ppermute | solution.py:495
  37.3 1.6 %finish00.1 = (bf16[1024,1024]{1,0:T(8,128)(2,1)}, f32[8,128]{1,0:T(8,128)S(1)}) custom-call(f32[1024,1024]{1,0:T(8,128)S(1)} %get-tuple-element.57.refs_0_, bf16[1024,128]{1,0:T(8,128)(2,1)S(1)} %get-tuple-element.34.refs_0_.refs_1_, f32[2,8,1024]{2,1,0:T(8,128)S(1)} %get-tuple-element.37.refs_3_.refs_2_, ...), custom_call_target="tpu_custom_call" | custom-call | flops 2000000000 | bytes 1000000 | tf_op jit(solution)/shard_map/finish00/pallas_call | solution.py:471
  38.8 2.4 %collective-permute-done.15.refs_0_ = f32[256,128]{1,0:T(8,128)S(1)} collective-permute-done((f32[256,128]{1,0:T(8,128)S(1)}, f32[256,128]{1,0:T(8,128)S(1)}, u32[]{:S(2)}, u32[]{:S(2)}) %collective-permute-start.15) | collective-permute-done | bytes 131104 | tf_op jit(solution)/shard_map/ppermute | solution.py:495
  41.3 1.6 %finish01.1.refs_12_ = bf16[1024,1024]{1,0:T(8,128)(2,1)} custom-call(f32[1024,1024]{1,0:T(8,128)S(1)} %get-tuple-element.57.refs_0_, bf16[1024,128]{1,0:T(8,128)(2,1)S(1)} %get-tuple-element.34.refs_0_.refs_1_, f32[2,8,1024]{2,1,0:T(8,128)S(1)} %get-tuple-element.37.refs_3_.refs_2_, ...), custom_call_target="tpu_custom_call", output_to_operand_aliasing={{}: (11, {})} | custom-call | flops 2000000000 | bytes 1000000 | tf_op jit(solution)/shard_map/finish01/pallas_call | solution.py:471
  42.9 2.4 %finish1011.1 = bf16[1024,1024]{1,0:T(8,128)(2,1)} custom-call(f32[1024,1024]{1,0:T(8,128)S(1)} %get-tuple-element.57.refs_0_, bf16[1024,128]{1,0:T(8,128)(2,1)S(1)} %get-tuple-element.34.refs_0_.refs_1_, f32[2,8,1024]{2,1,0:T(8,128)S(1)} %get-tuple-element.37.refs_3_.refs_2_, ...), custom_call_target="tpu_custom_call", output_to_operand_aliasing={{}: (12, {})} | custom-call | flops 2000000000 | bytes 1000000 | tf_op jit(solution)/shard_map/finish1011/pallas_call | solution.py:471
  (34 shorter events, 1.7 us)
Async XLA Ops:
  2.8 1.7 %collective-permute-start = (f32[520,128]{1,0:T(8,128)S(1)}, f32[520,128]{1,0:T(8,128)S(1)}, u32[]{:S(2)}, u32[]{:S(2)}) collective-permute-start(f32[520,128]{1,0:T(8,128)S(1)} %get-tuple-element.42), channel_id=1, source_target_pairs={{0,8},{8,0},{16,24},{24,16},{1,9},{9,1},{17,25},{25,17},{2,10},{10... | collective-permute-start | bytes 798728 | tf_op jit(solution)/shard_map/ppermute | solution.py:495
  4.6 7.9 %collective-permute-start.1 = (f32[512,128]{1,0:T(8,128)S(1)}, f32[512,128]{1,0:T(8,128)S(1)}, u32[]{:S(2)}, u32[]{:S(2)}) collective-permute-start(f32[512,128]{1,0:T(8,128)S(1)} %kept.1), channel_id=1, source_target_pairs={{0,8},{8,0},{16,24},{24,16},{1,9},{9,1},{17,25},{25,17},{2,10},{10... | collective-permute-start | bytes 786440 | tf_op jit(solution)/shard_map/ppermute | solution.py:495
  5.0 5.4 %collective-permute-start.3 = (f32[136,128]{1,0:T(8,128)S(1)}, f32[136,128]{1,0:T(8,128)S(1)}, u32[]{:S(2)}, u32[]{:S(2)}) collective-permute-start(f32[136,128]{1,0:T(8,128)S(1)} %get-tuple-element.48), channel_id=1, source_target_pairs={{0,16},{8,24},{16,0},{24,8},{1,17},{9,25},{17,1},{25,9},{2,18},{10... | collective-permute-start | bytes 208904 | tf_op jit(solution)/shard_map/ppermute | solution.py:495
  7.7 5.6 %collective-permute-start.2 = (f32[136,128]{1,0:T(8,128)S(1)}, f32[136,128]{1,0:T(8,128)S(1)}, u32[]{:S(2)}, u32[]{:S(2)}) collective-permute-start(f32[136,128]{1,0:T(8,128)S(1)} %get-tuple-element.46), channel_id=1, source_target_pairs={{0,16},{8,24},{16,0},{24,8},{1,17},{9,25},{17,1},{25,9},{2,18},{10... | collective-permute-start | bytes 208904 | tf_op jit(solution)/shard_map/ppermute | solution.py:495
  10.4 4.4 %collective-permute-start.5 = (f32[136,128]{1,0:T(8,128)S(1)}, f32[136,128]{1,0:T(8,128)S(1)}, u32[]{:S(2)}, u32[]{:S(2)}) collective-permute-start(f32[136,128]{1,0:T(8,128)S(1)} %merge10.1.refs_3_.refs_0_), channel_id=1, source_target_pairs={{0,1},{8,9},{16,17},{24,25},{1,0},{9,8},{17,16},{25,24},{2,3},{10,... | collective-permute-start | bytes 208904 | tf_op jit(solution)/shard_map/ppermute | solution.py:495
  13.4 6.0 %collective-permute-start.4 = (f32[136,128]{1,0:T(8,128)S(1)}, f32[136,128]{1,0:T(8,128)S(1)}, u32[]{:S(2)}, u32[]{:S(2)}) collective-permute-start(f32[136,128]{1,0:T(8,128)S(1)} %get-tuple-element.50.refs_8_.refs_0_.refs_2_), channel_id=1, source_target_pairs={{0,1},{8,9},{16,17},{24,25},{1,0},{9,8},{17,16},{25,24},{2,3},{10,... | collective-permute-start | bytes 208904 | tf_op jit(solution)/shard_map/ppermute | solution.py:495
  14.8 4.8 %collective-permute-start.7 = (f32[136,128]{1,0:T(8,128)S(1)}, f32[136,128]{1,0:T(8,128)S(1)}, u32[]{:S(2)}, u32[]{:S(2)}) collective-permute-start(f32[136,128]{1,0:T(8,128)S(1)} %merge20.1.refs_3_.refs_0_), channel_id=1, source_target_pairs={{0,2},{8,10},{16,18},{24,26},{1,3},{9,11},{17,19},{25,27},{2,0},{1... | collective-permute-start | bytes 208904 | tf_op jit(solution)/shard_map/ppermute | solution.py:495
  17.4 9.4 %collective-permute-start.8 = (f32[256,128]{1,0:T(8,128)S(1)}, f32[256,128]{1,0:T(8,128)S(1)}, u32[]{:S(2)}, u32[]{:S(2)}) collective-permute-start(f32[256,128]{1,0:T(8,128)S(1)} %rest.1), channel_id=1, source_target_pairs={{0,16},{8,24},{16,0},{24,8},{1,17},{9,25},{17,1},{25,9},{2,18},{10... | collective-permute-start | bytes 393224 | tf_op jit(solution)/shard_map/ppermute | solution.py:495
  19.7 15.3 %collective-permute-start.9 = (f32[136,128]{1,0:T(8,128)S(1)}, f32[136,128]{1,0:T(8,128)S(1)}, u32[]{:S(2)}, u32[]{:S(2)}) collective-permute-start(f32[136,128]{1,0:T(8,128)S(1)} %merge30.1.refs_3_), channel_id=1, source_target_pairs={{0,4},{8,12},{16,20},{24,28},{1,5},{9,13},{17,21},{25,29},{2,6},{1... | collective-permute-start | bytes 208904 | tf_op jit(solution)/shard_map/ppermute | solution.py:495
  23.1 5.0 %collective-permute-start.6 = (f32[136,128]{1,0:T(8,128)S(1)}, f32[136,128]{1,0:T(8,128)S(1)}, u32[]{:S(2)}, u32[]{:S(2)}) collective-permute-start(f32[136,128]{1,0:T(8,128)S(1)} %get-tuple-element.54.refs_0_.refs_2_), channel_id=1, source_target_pairs={{0,2},{8,10},{16,18},{24,26},{1,3},{9,11},{17,19},{25,27},{2,0},{1... | collective-permute-start | bytes 208904 | tf_op jit(solution)/shard_map/ppermute | solution.py:495
  24.4 8.7 %collective-permute-start.12 = (f32[256,128]{1,0:T(8,128)S(1)}, f32[256,128]{1,0:T(8,128)S(1)}, u32[]{:S(2)}, u32[]{:S(2)}) collective-permute-start(f32[256,128]{1,0:T(8,128)S(1)} %found2.1.refs_2_), channel_id=1, source_target_pairs={{0,16},{8,24},{16,0},{24,8},{1,17},{9,25},{17,1},{25,9},{2,18},{10... | collective-permute-start | bytes 393224 | tf_op jit(solution)/shard_map/ppermute | solution.py:495
  28.0 7.0 %collective-permute-start.10 = (f32[136,128]{1,0:T(8,128)S(1)}, f32[136,128]{1,0:T(8,128)S(1)}, u32[]{:S(2)}, u32[]{:S(2)}) collective-permute-start(f32[136,128]{1,0:T(8,128)S(1)} %get-tuple-element.56.refs_8_.refs_2_), channel_id=1, source_target_pairs={{0,4},{8,12},{16,20},{24,28},{1,5},{9,13},{17,21},{25,29},{2,6},{1... | collective-permute-start | bytes 208904 | tf_op jit(solution)/shard_map/ppermute | solution.py:495
  29.9 5.0 %collective-permute-start.13 = (f32[256,128]{1,0:T(8,128)S(1)}, f32[256,128]{1,0:T(8,128)S(1)}, u32[]{:S(2)}, u32[]{:S(2)}) collective-permute-start(f32[256,128]{1,0:T(8,128)S(1)} %found3.1.refs_4_), channel_id=1, source_target_pairs={{0,16},{8,24},{16,0},{24,8},{1,17},{9,25},{17,1},{25,9},{2,18},{10... | collective-permute-start | bytes 393224 | tf_op jit(solution)/shard_map/ppermute | solution.py:495
  34.9 8.0 %collective-permute-start.14 = (f32[1536,128]{1,0:T(8,128)S(1)}, f32[1536,128]{1,0:T(8,128)S(1)}, u32[]{:S(2)}, u32[]{:S(2)}) collective-permute-start(f32[1536,128]{1,0:T(8,128)S(1)} %near.1.refs_10_), channel_id=1, source_target_pairs={{0,8},{8,0},{16,24},{24,16},{1,9},{9,1},{17,25},{25,17},{2,10},{10... | collective-permute-start | bytes 2359304 | tf_op jit(solution)/shard_map/ppermute | solution.py:495
  35.1 6.1 %collective-permute-start.15 = (f32[256,128]{1,0:T(8,128)S(1)}, f32[256,128]{1,0:T(8,128)S(1)}, u32[]{:S(2)}, u32[]{:S(2)}) collective-permute-start(f32[256,128]{1,0:T(8,128)S(1)} %state.1.refs_9_), channel_id=1, source_target_pairs={{0,16},{8,24},{16,0},{24,8},{1,17},{9,25},{17,1},{25,9},{2,18},{10... | collective-permute-start | bytes 393224 | tf_op jit(solution)/shard_map/ppermute | solution.py:495
  37.1 5.8 %collective-permute-start.11 = (f32[256,128]{1,0:T(8,128)S(1)}, f32[256,128]{1,0:T(8,128)S(1)}, u32[]{:S(2)}, u32[]{:S(2)}) collective-permute-start(f32[256,128]{1,0:T(8,128)S(1)} %state.1.refs_9_), channel_id=1, source_target_pairs={{0,8},{8,0},{16,24},{24,16},{1,9},{9,1},{17,25},{25,17},{2,10},{10... | collective-permute-start | bytes 393224 | tf_op jit(solution)/shard_map/ppermute | solution.py:495
  41.2 1.7 %collective-permute-start.16 = (f32[256,128]{1,0:T(8,128)S(1)}, f32[256,128]{1,0:T(8,128)S(1)}, u32[]{:S(2)}, u32[]{:S(2)}) collective-permute-start(f32[256,128]{1,0:T(8,128)S(1)} %beside.1.refs_9_), channel_id=1, source_target_pairs={{0,8},{8,0},{16,24},{24,16},{1,9},{9,1},{17,25},{25,17},{2,10},{10... | collective-permute-start | bytes 393224 | tf_op jit(solution)/shard_map/ppermute | solution.py:495

commit v14 on v13

--- a/solution.py
+++ b/solution.py
@@ -13,8 +13,14 @@
 EPS = 1e-05
 AXES = ("narrow", "wide")
 NT = (((1,), (1,)), ((), ()))
-COST = pl.CostEstimate(flops=2_000_000_000, transcendentals=0, bytes_accessed=1_000_000)
+
+
+def cost(flops):
+    return pl.CostEstimate(flops=flops, transcendentals=0, bytes_accessed=1_000_000)
+
+
 PARAMS = pltpu.CompilerParams(vmem_limit_bytes=32 * 1024 * 1024)
+COSTS = {"finish00": 1000, "finish01": 20000000000}
 HELD = pl.BlockSpec(memory_space=pltpu.VMEM)
 
 
@@ -48,7 +54,7 @@
         scratch_shapes=list(scratch),
         input_output_aliases=aliases or {},
         compiler_params=PARAMS,
-        cost_estimate=COST,
+        cost_estimate=cost(COSTS.get(name, 2_000_000_000)),
         name=name,
     )(*inputs)
 
@@ -465,6 +471,7 @@
         aliases = {len(inputs): 0}
         specs.append(out)
         inputs.append(begun)
+    name = "finish" + "".join(f"{core}{side}" for (core, side), _ in quarters)
     shapes = [jax.ShapeDtypeStruct((tokens, width), jnp.bfloat16)]
     if has_token:
         shapes.append(pltpu.VMEM((8, 128), jnp.float32))
@@ -480,8 +487,8 @@
         ],
         input_output_aliases=aliases,
         compiler_params=PARAMS,
-        cost_estimate=COST,
-        name="finish" + "".join(f"{core}{side}" for (core, side), _ in quarters),
+        cost_estimate=cost(COSTS.get(name, 2_000_000_000)),
+        name=name,
     )(*inputs)
 
 
@@ -515,7 +522,7 @@
     other = trade(send, 1)
     zero = jnp.zeros((heads, 128), jnp.float32)
     chunks, give, prefix = make_chip(keep, other, heads, CUTS)
-    other_rest = trade(pack("kept", [(keep, width // 2)], chunks[:1]), 1)
+    other_rest = trade(keep, 1)
     prefixes = [zero, prefix]
     found, across = {}, {}
     mixed, at = None, 0
@@ -554,11 +561,13 @@
     halves = [((core,), [(0, core, 0)]) for core in (0, 1)]
     shared = (mixed, queries, sums, level_weight)
     mixed, token = add_levels(halves, first_level, [0], shared, [zero], [other, other_rest])
+    state = both("state", found[last], (token,))
+    beside = trade(state, 2)
     early = list(range(2, last))
     pieces = [(found[1], two), (rest, two)]
     for bit in early:
         pieces += [(found[bit], two), (across[bit], two)]
-    near = pack("near", pieces, (token,))
+    near = pack("near", pieces, (state,))
     middle = [1, *early]
     ahead = [prefixes[bit] for bit in middle]
 
@@ -567,8 +576,6 @@
 
     shared = (mixed, queries, sums, level_weight, gain)
     every = (first_level, [last, *middle], shared, [prefixes[last], *ahead])
-    state = both("state", found[last])
-    beside = trade(state, 2)
     quarters = {(core, side): [(0, 0, 0), *states_of(side, 1, 1)] for core, side in sides}
     out, token = finish([((0, 0), quarters[0, 0])], *every, [state, near], None, True)
     far = trade(near, 1)

time: 45.4 us -> 39.7 us (0.87)
  waiting for transfers between devices: 9.71 us -> 6.04 us
  starting transfers between devices: 22.1 us -> 20.1 us
    ppermute x17, waiting for transfers between devices: 9.71 us -> 6.04 us  [trade(): return lax.ppermute(value, AXES, pairs)]
    ppermute x17, starting transfers between devices: 22.1 us -> 20.1 us  [trade(): return lax.ppermute(value, AXES, pairs)]
    pallas_call x20 -> x19, Pallas kernels: 7.72 us -> 7.68 us  [call(): pl.pallas_call(kernel, in_specs=specs, out_specs=[HELD] * len(outputs), o...]
  transfers between devices with their start and end apart: 17 -> 17, of which waited for: 7 -> 3; matrix products, arithmetic and copies ran while one was open for 0% -> 0% of each run, Pallas kernels for 18% -> 20%
where the time goes in v14:
time: 39.7 us; the launch traced here: 39.5 us
  starting transfers between devices  20.1 us (51%)
  Pallas kernels  13.2 us (33%)
  waiting for transfers between devices  6.04 us (15%)
    ppermute x17, starting transfers between devices, trade(): return lax.ppermute(value, AXES, pairs)  20.1 us
    pallas_call x19, Pallas kernels, call(): pl.pallas_call(kernel, in_specs=specs, out_specs=[HELD] * len(outputs), o...  7.68 us
    ppermute x17, waiting for transfers between devices, trade(): return lax.ppermute(value, AXES, pairs)  6.04 us
    pallas_call x3, Pallas kernels, finish(): pl.pallas_call(functools.partial(finish_kernel, quarters, first_level, bi...  5.5 us
  transfers between devices with their start and end apart: 17, of which 3 were waited for; matrix products, arithmetic and copies ran while one was open for 0% of the time, Pallas kernels for 20%

profile of v14, /device:TPU:0, one launch (start us, length us, event | category | flops | bytes accessed | tf_op | source)
XLA Modules:
  0.0 39.5 jit_solution(7669199931371604155)
XLA Ops:
  0.0 2.8 %states.1 = (f32[520,128]{1,0:T(8,128)S(1)}, f32[520,128]{1,0:T(8,128)S(1)}, bf16[3,128,1024]{2,1,0:T(8,128)(2,1)S(1)}, f32[2,8,1024]{2,1,0:T(8,128)S(1)}, f32[4...) custom-call(bf16[1024,128]{1,0:T(8,128)(2,1)} %refs_0_.1, ...), custom_call_target="tpu_custom_call" | custom-call | flops 2000000000 | bytes 1000000 | tf_op jit(solution)/shard_map/states/pallas_call | solution.py:49
  2.8 0.5 %collective-permute-start = (f32[520,128]{1,0:T(8,128)S(1)}, f32[520,128]{1,0:T(8,128)S(1)}, u32[]{:S(2)}, u32[]{:S(2)}) collective-permute-start(f32[520,128]{1,0:T(8,128)S(1)} %get-tuple-element.42), channel_id=1, source_target_pairs={{0,8},{8,0},{16,24},{24,16},{1,9},{9,1},{17,25},{25,17},{2,10},{10... | collective-permute-start | bytes 798728 | tf_op jit(solution)/shard_map/ppermute | solution.py:502
  3.4 1.1 %collective-permute-done.other_ref.refs_5_ = f32[520,128]{1,0:T(8,128)S(1)} collective-permute-done((f32[520,128]{1,0:T(8,128)S(1)}, f32[520,128]{1,0:T(8,128)S(1)}, u32[]{:S(2)}, u32[]{:S(2)}) %collective-permute-start) | collective-permute-done | bytes 266272 | tf_op jit(solution)/shard_map/ppermute | solution.py:502
  4.5 2.9 %collective-permute-start.2 = (f32[136,128]{1,0:T(8,128)S(1)}, f32[136,128]{1,0:T(8,128)S(1)}, u32[]{:S(2)}, u32[]{:S(2)}) collective-permute-start(f32[136,128]{1,0:T(8,128)S(1)} %get-tuple-element.45), channel_id=1, source_target_pairs={{0,16},{8,24},{16,0},{24,8},{1,17},{9,25},{17,1},{25,9},{2,18},{10... | collective-permute-start | bytes 208904 | tf_op jit(solution)/shard_map/ppermute | solution.py:502
  7.6 0.8 %local0.1 = (f32[1024,1024]{1,0:T(8,128)S(1)}, f32[8,128]{1,0:T(8,128)S(1)}) custom-call(bf16[1024,128]{1,0:T(8,128)(2,1)S(1)} %get-tuple-element.34.refs_0_.refs_1_, bf16[1024,128]{1,0:T(8,128)(2,1)S(1)} %get-tuple-element.35.refs_1_, bf16[1024,1024]{1,0:T(8,128)(2,1)S(1)} %get-tuple-element.36.refs_2_, ...), custom_call_target="tpu_custom_call" | custom-call | flops 2000000000 | bytes 1000000 | tf_op jit(solution)/shard_map/local0/pallas_call | solution.py:49
  8.4 3.4 %collective-permute-done.3.refs_1_.refs_0_ = f32[136,128]{1,0:T(8,128)S(1)} collective-permute-done((f32[136,128]{1,0:T(8,128)S(1)}, f32[136,128]{1,0:T(8,128)S(1)}, u32[]{:S(2)}, u32[]{:S(2)}) %collective-permute-start.3) | collective-permute-done | bytes 69664 | tf_op jit(solution)/shard_map/ppermute | solution.py:502
  11.8 1.6 %collective-permute-start.5 = (f32[136,128]{1,0:T(8,128)S(1)}, f32[136,128]{1,0:T(8,128)S(1)}, u32[]{:S(2)}, u32[]{:S(2)}) collective-permute-start(f32[136,128]{1,0:T(8,128)S(1)} %merge10.1.refs_3_.refs_0_), channel_id=1, source_target_pairs={{0,1},{8,9},{16,17},{24,25},{1,0},{9,8},{17,16},{25,24},{2,3},{10,... | collective-permute-start | bytes 208904 | tf_op jit(solution)/shard_map/ppermute | solution.py:502
  13.5 0.6 %collective-permute-start.4 = (f32[136,128]{1,0:T(8,128)S(1)}, f32[136,128]{1,0:T(8,128)S(1)}, u32[]{:S(2)}, u32[]{:S(2)}) collective-permute-start(f32[136,128]{1,0:T(8,128)S(1)} %get-tuple-element.50.refs_8_.refs_0_.refs_2_), channel_id=1, source_target_pairs={{0,1},{8,9},{16,17},{24,25},{1,0},{9,8},{17,16},{25,24},{2,3},{10,... | collective-permute-start | bytes 208904 | tf_op jit(solution)/shard_map/ppermute | solution.py:502
  14.1 0.9 %local1.1 = (f32[1024,1024]{1,0:T(8,128)S(1)}, f32[8,128]{1,0:T(8,128)S(1)}) custom-call(bf16[1024,128]{1,0:T(8,128)(2,1)S(1)} %get-tuple-element.34.refs_0_.refs_1_, bf16[1024,128]{1,0:T(8,128)(2,1)S(1)} %get-tuple-element.35.refs_1_, bf16[1024,1024]{1,0:T(8,128)(2,1)S(1)} %get-tuple-element.36.refs_2_, ...), custom_call_target="tpu_custom_call", output_to_operand_aliasing={{0}: (7, {})} | custom-call | flops 2000000000 | bytes 1000000 | tf_op jit(solution)/shard_map/local1/pallas_call | solution.py:49
  15.0 1.4 %collective-permute-start.8 = (f32[256,128]{1,0:T(8,128)S(1)}, f32[256,128]{1,0:T(8,128)S(1)}, u32[]{:S(2)}, u32[]{:S(2)}) collective-permute-start(f32[256,128]{1,0:T(8,128)S(1)} %rest.1), channel_id=1, source_target_pairs={{0,16},{8,24},{16,0},{24,8},{1,17},{9,25},{17,1},{25,9},{2,18},{10... | collective-permute-start | bytes 393224 | tf_op jit(solution)/shard_map/ppermute | solution.py:502
  16.5 1.6 %collective-permute-start.7 = (f32[136,128]{1,0:T(8,128)S(1)}, f32[136,128]{1,0:T(8,128)S(1)}, u32[]{:S(2)}, u32[]{:S(2)}) collective-permute-start(f32[136,128]{1,0:T(8,128)S(1)} %merge20.1.refs_3_.refs_0_), channel_id=1, source_target_pairs={{0,2},{8,10},{16,18},{24,26},{1,3},{9,11},{17,19},{25,27},{2,0},{1... | collective-permute-start | bytes 208904 | tf_op jit(solution)/shard_map/ppermute | solution.py:502
  18.1 1.4 %collective-permute-start.6 = (f32[136,128]{1,0:T(8,128)S(1)}, f32[136,128]{1,0:T(8,128)S(1)}, u32[]{:S(2)}, u32[]{:S(2)}) collective-permute-start(f32[136,128]{1,0:T(8,128)S(1)} %get-tuple-element.54.refs_0_.refs_2_), channel_id=1, source_target_pairs={{0,2},{8,10},{16,18},{24,26},{1,3},{9,11},{17,19},{25,27},{2,0},{1... | collective-permute-start | bytes 208904 | tf_op jit(solution)/shard_map/ppermute | solution.py:502
  19.5 1.5 %collective-permute-start.12 = (f32[256,128]{1,0:T(8,128)S(1)}, f32[256,128]{1,0:T(8,128)S(1)}, u32[]{:S(2)}, u32[]{:S(2)}) collective-permute-start(f32[256,128]{1,0:T(8,128)S(1)} %found2.1.refs_2_), channel_id=1, source_target_pairs={{0,16},{8,24},{16,0},{24,8},{1,17},{9,25},{17,1},{25,9},{2,18},{10... | collective-permute-start | bytes 393224 | tf_op jit(solution)/shard_map/ppermute | solution.py:502
  21.0 2.7 %collective-permute-start.9 = (f32[136,128]{1,0:T(8,128)S(1)}, f32[136,128]{1,0:T(8,128)S(1)}, u32[]{:S(2)}, u32[]{:S(2)}) collective-permute-start(f32[136,128]{1,0:T(8,128)S(1)} %merge30.1.refs_3_), channel_id=1, source_target_pairs={{0,4},{8,12},{16,20},{24,28},{1,5},{9,13},{17,21},{25,29},{2,6},{1... | collective-permute-start | bytes 208904 | tf_op jit(solution)/shard_map/ppermute | solution.py:502
  23.7 1.5 %collective-permute-start.10 = (f32[136,128]{1,0:T(8,128)S(1)}, f32[136,128]{1,0:T(8,128)S(1)}, u32[]{:S(2)}, u32[]{:S(2)}) collective-permute-start(f32[136,128]{1,0:T(8,128)S(1)} %get-tuple-element.56.refs_8_.refs_2_), channel_id=1, source_target_pairs={{0,4},{8,12},{16,20},{24,28},{1,5},{9,13},{17,21},{25,29},{2,6},{1... | collective-permute-start | bytes 208904 | tf_op jit(solution)/shard_map/ppermute | solution.py:502
  25.2 1.7 %local2.1.refs_0_ = f32[1024,1024]{1,0:T(8,128)S(1)} custom-call(bf16[1024,128]{1,0:T(8,128)(2,1)S(1)} %get-tuple-element.34.refs_0_.refs_1_, bf16[1024,128]{1,0:T(8,128)(2,1)S(1)} %get-tuple-element.35.refs_1_, bf16[1024,1024]{1,0:T(8,128)(2,1)S(1)} %get-tuple-element.36.refs_2_, ...), custom_call_target="tpu_custom_call", output_to_operand_aliasing={{}: (7, {})} | custom-call | flops 2000000000 | bytes 1000000 | tf_op jit(solution)/shard_map/local2/pallas_call | solution.py:49
  26.9 1.6 %collective-permute-start.13 = (f32[256,128]{1,0:T(8,128)S(1)}, f32[256,128]{1,0:T(8,128)S(1)}, u32[]{:S(2)}, u32[]{:S(2)}) collective-permute-start(f32[256,128]{1,0:T(8,128)S(1)} %found3.1.refs_4_), channel_id=1, source_target_pairs={{0,16},{8,24},{16,0},{24,8},{1,17},{9,25},{17,1},{25,9},{2,18},{10... | collective-permute-start | bytes 393224 | tf_op jit(solution)/shard_map/ppermute | solution.py:502
  28.6 1.2 %reach.1 = (f32[1024,1024]{1,0:T(8,128)S(1)}, f32[8,128]{1,0:T(8,128)S(1)}) custom-call(f32[1024,1024]{1,0:T(8,128)S(1)} %local2.1.refs_0_, bf16[1024,128]{1,0:T(8,128)(2,1)S(1)} %get-tuple-element.34.refs_0_.refs_1_, f32[2,8,1024]{2,1,0:T(8,128)S(1)} %get-tuple-element.37.refs_3_.refs_2_, ...), custom_call_target="tpu_custom_call", output_to_operand_aliasing={{0}: (0, {})} | custom-call | flops 2000000000 | bytes 1000000 | tf_op jit(solution)/shard_map/reach/pallas_call | solution.py:49
  29.8 2.0 %collective-permute-start.15 = (f32[256,128]{1,0:T(8,128)S(1)}, f32[256,128]{1,0:T(8,128)S(1)}, u32[]{:S(2)}, u32[]{:S(2)}) collective-permute-start(f32[256,128]{1,0:T(8,128)S(1)} %state.1.refs_6_.refs_9_), channel_id=1, source_target_pairs={{0,16},{8,24},{16,0},{24,8},{1,17},{9,25},{17,1},{25,9},{2,18},{10... | collective-permute-start | bytes 393224 | tf_op jit(solution)/shard_map/ppermute | solution.py:502
  31.8 1.5 %collective-permute-done.13.refs_5_ = f32[256,128]{1,0:T(8,128)S(1)} collective-permute-done((f32[256,128]{1,0:T(8,128)S(1)}, f32[256,128]{1,0:T(8,128)S(1)}, u32[]{:S(2)}, u32[]{:S(2)}) %collective-permute-start.13) | collective-permute-done | bytes 131104 | tf_op jit(solution)/shard_map/ppermute | solution.py:502
  33.4 1.6 %finish00.1 = (bf16[1024,1024]{1,0:T(8,128)(2,1)}, f32[8,128]{1,0:T(8,128)S(1)}) custom-call(f32[1024,1024]{1,0:T(8,128)S(1)} %get-tuple-element.57.refs_0_, bf16[1024,128]{1,0:T(8,128)(2,1)S(1)} %get-tuple-element.34.refs_0_.refs_1_, f32[2,8,1024]{2,1,0:T(8,128)S(1)} %get-tuple-element.37.refs_3_.refs_2_, ...), custom_call_target="tpu_custom_call" | custom-call | flops 1000 | bytes 1000000 | tf_op jit(solution)/shard_map/finish00/pallas_call | solution.py:478
  35.0 0.6 %collective-permute-start.16 = (f32[256,128]{1,0:T(8,128)S(1)}, f32[256,128]{1,0:T(8,128)S(1)}, u32[]{:S(2)}, u32[]{:S(2)}) collective-permute-start(f32[256,128]{1,0:T(8,128)S(1)} %beside.1.refs_9_), channel_id=1, source_target_pairs={{0,8},{8,0},{16,24},{24,16},{1,9},{9,1},{17,25},{25,17},{2,10},{10... | collective-permute-start | bytes 393224 | tf_op jit(solution)/shard_map/ppermute | solution.py:502
  35.6 1.6 %finish01.1.refs_12_ = bf16[1024,1024]{1,0:T(8,128)(2,1)} custom-call(f32[1024,1024]{1,0:T(8,128)S(1)} %get-tuple-element.57.refs_0_, bf16[1024,128]{1,0:T(8,128)(2,1)S(1)} %get-tuple-element.34.refs_0_.refs_1_, f32[2,8,1024]{2,1,0:T(8,128)S(1)} %get-tuple-element.37.refs_3_.refs_2_, ...), custom_call_target="tpu_custom_call", output_to_operand_aliasing={{}: (11, {})} | custom-call | flops 20000000000 | bytes 1000000 | tf_op jit(solution)/shard_map/finish01/pallas_call | solution.py:478
  37.2 2.4 %finish1011.1 = bf16[1024,1024]{1,0:T(8,128)(2,1)} custom-call(f32[1024,1024]{1,0:T(8,128)S(1)} %get-tuple-element.57.refs_0_, bf16[1024,128]{1,0:T(8,128)(2,1)S(1)} %get-tuple-element.34.refs_0_.refs_1_, f32[2,8,1024]{2,1,0:T(8,128)S(1)} %get-tuple-element.37.refs_3_.refs_2_, ...), custom_call_target="tpu_custom_call", output_to_operand_aliasing={{}: (12, {})} | custom-call | flops 2000000000 | bytes 1000000 | tf_op jit(solution)/shard_map/finish1011/pallas_call | solution.py:478
  (33 shorter events, 0.6 us)
Async XLA Ops:
  2.8 1.7 %collective-permute-start = (f32[520,128]{1,0:T(8,128)S(1)}, f32[520,128]{1,0:T(8,128)S(1)}, u32[]{:S(2)}, u32[]{:S(2)}) collective-permute-start(f32[520,128]{1,0:T(8,128)S(1)} %get-tuple-element.42), channel_id=1, source_target_pairs={{0,8},{8,0},{16,24},{24,16},{1,9},{9,1},{17,25},{25,17},{2,10},{10... | collective-permute-start | bytes 798728 | tf_op jit(solution)/shard_map/ppermute | solution.py:502
  3.3 4.3 %collective-permute-start.1 = (f32[520,128]{1,0:T(8,128)S(1)}, f32[520,128]{1,0:T(8,128)S(1)}, u32[]{:S(2)}, u32[]{:S(2)}) collective-permute-start(f32[520,128]{1,0:T(8,128)S(1)} %get-tuple-element.41.mine_ref), channel_id=1, source_target_pairs={{0,8},{8,0},{16,24},{24,16},{1,9},{9,1},{17,25},{25,17},{2,10},{10... | collective-permute-start | bytes 798728 | tf_op jit(solution)/shard_map/ppermute | solution.py:502
  4.5 8.9 %collective-permute-start.2 = (f32[136,128]{1,0:T(8,128)S(1)}, f32[136,128]{1,0:T(8,128)S(1)}, u32[]{:S(2)}, u32[]{:S(2)}) collective-permute-start(f32[136,128]{1,0:T(8,128)S(1)} %get-tuple-element.45), channel_id=1, source_target_pairs={{0,16},{8,24},{16,0},{24,8},{1,17},{9,25},{17,1},{25,9},{2,18},{10... | collective-permute-start | bytes 208904 | tf_op jit(solution)/shard_map/ppermute | solution.py:502
  7.5 4.3 %collective-permute-start.3 = (f32[136,128]{1,0:T(8,128)S(1)}, f32[136,128]{1,0:T(8,128)S(1)}, u32[]{:S(2)}, u32[]{:S(2)}) collective-permute-start(f32[136,128]{1,0:T(8,128)S(1)} %get-tuple-element.48), channel_id=1, source_target_pairs={{0,16},{8,24},{16,0},{24,8},{1,17},{9,25},{17,1},{25,9},{2,18},{10... | collective-permute-start | bytes 208904 | tf_op jit(solution)/shard_map/ppermute | solution.py:502
  11.8 4.6 %collective-permute-start.5 = (f32[136,128]{1,0:T(8,128)S(1)}, f32[136,128]{1,0:T(8,128)S(1)}, u32[]{:S(2)}, u32[]{:S(2)}) collective-permute-start(f32[136,128]{1,0:T(8,128)S(1)} %merge10.1.refs_3_.refs_0_), channel_id=1, source_target_pairs={{0,1},{8,9},{16,17},{24,25},{1,0},{9,8},{17,16},{25,24},{2,3},{10,... | collective-permute-start | bytes 208904 | tf_op jit(solution)/shard_map/ppermute | solution.py:502
  13.5 4.7 %collective-permute-start.4 = (f32[136,128]{1,0:T(8,128)S(1)}, f32[136,128]{1,0:T(8,128)S(1)}, u32[]{:S(2)}, u32[]{:S(2)}) collective-permute-start(f32[136,128]{1,0:T(8,128)S(1)} %get-tuple-element.50.refs_8_.refs_0_.refs_2_), channel_id=1, source_target_pairs={{0,1},{8,9},{16,17},{24,25},{1,0},{9,8},{17,16},{25,24},{2,3},{10,... | collective-permute-start | bytes 208904 | tf_op jit(solution)/shard_map/ppermute | solution.py:502
  15.0 8.8 %collective-permute-start.8 = (f32[256,128]{1,0:T(8,128)S(1)}, f32[256,128]{1,0:T(8,128)S(1)}, u32[]{:S(2)}, u32[]{:S(2)}) collective-permute-start(f32[256,128]{1,0:T(8,128)S(1)} %rest.1), channel_id=1, source_target_pairs={{0,16},{8,24},{16,0},{24,8},{1,17},{9,25},{17,1},{25,9},{2,18},{10... | collective-permute-start | bytes 393224 | tf_op jit(solution)/shard_map/ppermute | solution.py:502
  16.5 4.5 %collective-permute-start.7 = (f32[136,128]{1,0:T(8,128)S(1)}, f32[136,128]{1,0:T(8,128)S(1)}, u32[]{:S(2)}, u32[]{:S(2)}) collective-permute-start(f32[136,128]{1,0:T(8,128)S(1)} %merge20.1.refs_3_.refs_0_), channel_id=1, source_target_pairs={{0,2},{8,10},{16,18},{24,26},{1,3},{9,11},{17,19},{25,27},{2,0},{1... | collective-permute-start | bytes 208904 | tf_op jit(solution)/shard_map/ppermute | solution.py:502
  18.1 5.6 %collective-permute-start.6 = (f32[136,128]{1,0:T(8,128)S(1)}, f32[136,128]{1,0:T(8,128)S(1)}, u32[]{:S(2)}, u32[]{:S(2)}) collective-permute-start(f32[136,128]{1,0:T(8,128)S(1)} %get-tuple-element.54.refs_0_.refs_2_), channel_id=1, source_target_pairs={{0,2},{8,10},{16,18},{24,26},{1,3},{9,11},{17,19},{25,27},{2,0},{1... | collective-permute-start | bytes 208904 | tf_op jit(solution)/shard_map/ppermute | solution.py:502
  19.5 12.3 %collective-permute-start.12 = (f32[256,128]{1,0:T(8,128)S(1)}, f32[256,128]{1,0:T(8,128)S(1)}, u32[]{:S(2)}, u32[]{:S(2)}) collective-permute-start(f32[256,128]{1,0:T(8,128)S(1)} %found2.1.refs_2_), channel_id=1, source_target_pairs={{0,16},{8,24},{16,0},{24,8},{1,17},{9,25},{17,1},{25,9},{2,18},{10... | collective-permute-start | bytes 393224 | tf_op jit(solution)/shard_map/ppermute | solution.py:502
  21.0 8.8 %collective-permute-start.9 = (f32[136,128]{1,0:T(8,128)S(1)}, f32[136,128]{1,0:T(8,128)S(1)}, u32[]{:S(2)}, u32[]{:S(2)}) collective-permute-start(f32[136,128]{1,0:T(8,128)S(1)} %merge30.1.refs_3_), channel_id=1, source_target_pairs={{0,4},{8,12},{16,20},{24,28},{1,5},{9,13},{17,21},{25,29},{2,6},{1... | collective-permute-start | bytes 208904 | tf_op jit(solution)/shard_map/ppermute | solution.py:502
  23.7 6.0 %collective-permute-start.10 = (f32[136,128]{1,0:T(8,128)S(1)}, f32[136,128]{1,0:T(8,128)S(1)}, u32[]{:S(2)}, u32[]{:S(2)}) collective-permute-start(f32[136,128]{1,0:T(8,128)S(1)} %get-tuple-element.56.refs_8_.refs_2_), channel_id=1, source_target_pairs={{0,4},{8,12},{16,20},{24,28},{1,5},{9,13},{17,21},{25,29},{2,6},{1... | collective-permute-start | bytes 208904 | tf_op jit(solution)/shard_map/ppermute | solution.py:502
  26.9 6.3 %collective-permute-start.13 = (f32[256,128]{1,0:T(8,128)S(1)}, f32[256,128]{1,0:T(8,128)S(1)}, u32[]{:S(2)}, u32[]{:S(2)}) collective-permute-start(f32[256,128]{1,0:T(8,128)S(1)} %found3.1.refs_4_), channel_id=1, source_target_pairs={{0,16},{8,24},{16,0},{24,8},{1,17},{9,25},{17,1},{25,9},{2,18},{10... | collective-permute-start | bytes 393224 | tf_op jit(solution)/shard_map/ppermute | solution.py:502
  29.8 5.2 %collective-permute-start.15 = (f32[256,128]{1,0:T(8,128)S(1)}, f32[256,128]{1,0:T(8,128)S(1)}, u32[]{:S(2)}, u32[]{:S(2)}) collective-permute-start(f32[256,128]{1,0:T(8,128)S(1)} %state.1.refs_6_.refs_9_), channel_id=1, source_target_pairs={{0,16},{8,24},{16,0},{24,8},{1,17},{9,25},{17,1},{25,9},{2,18},{10... | collective-permute-start | bytes 393224 | tf_op jit(solution)/shard_map/ppermute | solution.py:502
  31.8 5.4 %collective-permute-start.11 = (f32[256,128]{1,0:T(8,128)S(1)}, f32[256,128]{1,0:T(8,128)S(1)}, u32[]{:S(2)}, u32[]{:S(2)}) collective-permute-start(f32[256,128]{1,0:T(8,128)S(1)} %state.1.refs_6_.refs_9_), channel_id=1, source_target_pairs={{0,8},{8,0},{16,24},{24,16},{1,9},{9,1},{17,25},{25,17},{2,10},{10... | collective-permute-start | bytes 393224 | tf_op jit(solution)/shard_map/ppermute | solution.py:502
  33.3 3.9 %collective-permute-start.14 = (f32[1536,128]{1,0:T(8,128)S(1)}, f32[1536,128]{1,0:T(8,128)S(1)}, u32[]{:S(2)}, u32[]{:S(2)}) collective-permute-start(f32[1536,128]{1,0:T(8,128)S(1)} %near.1.refs_10_), channel_id=1, source_target_pairs={{0,8},{8,0},{16,24},{24,16},{1,9},{9,1},{17,25},{25,17},{2,10},{10... | collective-permute-start | bytes 2359304 | tf_op jit(solution)/shard_map/ppermute | solution.py:502
  35.0 2.2 %collective-permute-start.16 = (f32[256,128]{1,0:T(8,128)S(1)}, f32[256,128]{1,0:T(8,128)S(1)}, u32[]{:S(2)}, u32[]{:S(2)}) collective-permute-start(f32[256,128]{1,0:T(8,128)S(1)} %beside.1.refs_9_), channel_id=1, source_target_pairs={{0,8},{8,0},{16,24},{24,16},{1,9},{9,1},{17,25},{25,17},{2,10},{10... | collective-permute-start | bytes 393224 | tf_op jit(solution)/shard_map/ppermute | solution.py:502

commit v15 on v12

--- a/solution.py
+++ b/solution.py
@@ -13,6 +13,14 @@
 EPS = 1e-05
 AXES = ("narrow", "wide")
 NT = (((1,), (1,)), ((), ()))
+COSTS = {"finish00": 20000000000, "finish10": 1000, "finish01": 20000000000, "local2": 1000, "reach": 1000}
+
+
+def cost(name):
+    flops = COSTS.get(name, 2000000000)
+    return pl.CostEstimate(flops=flops, transcendentals=0, bytes_accessed=1_000_000)
+
+
 PARAMS = pltpu.CompilerParams(vmem_limit_bytes=32 * 1024 * 1024)
 HELD = pl.BlockSpec(memory_space=pltpu.VMEM)
 
@@ -47,6 +55,7 @@
         scratch_shapes=list(scratch),
         input_output_aliases=aliases or {},
         compiler_params=PARAMS,
+        cost_estimate=cost(name),
         name=name,
     )(*inputs)
 
@@ -70,7 +79,7 @@
 def state_kernel(*refs):
     q_hbm, k_hbm, v_hbm, decay_hbm, weight_hbm, gain_hbm = refs[:6]
     message_ref, local_ref, sums_ref, totals_ref = refs[6:10]
-    q_ref, k_ref, v_ref, weight_ref, gain_ref, decay_ref, arrived = refs[10:]
+    q_ref, k_ref, v_ref, weight_ref, gain_ref, decay_ref, held, arrived = refs[10:]
     heads, tokens = decay_ref.shape
     head_width = v_ref.shape[1] // heads
     spans = tokens // SPAN
@@ -100,30 +109,28 @@
         wholes.append(jnp.exp(total))
     copies[1].wait()
     across = [k_ref[rows].astype(jnp.float32).T for rows in rows_of]
-    for copy in copies[2 : 2 + spans]:
-        copy.wait()
-    for head in range(heads):
-        columns = slice(head * head_width, (head + 1) * head_width)
-        states = []
-        for span, rows in enumerate(rows_of):
+    local_bits = spans.bit_length() - 1
+    for span, rows in enumerate(rows_of):
+        copies[2 + span].wait()
+        for head in range(heads):
+            columns = slice(head * head_width, (head + 1) * head_width)
             faded = (across[span] * fades[span][head : head + 1]).astype(jnp.bfloat16)
-            states.append(
-                jnp.dot(faded, v_ref[rows, columns], preferred_element_type=jnp.float32)
-            )
-        at = 0
-        size = 1
-        while size < spans:
-            for first in range(0, spans, 2 * size):
-                group = states[first]
-                for span in range(first + 1, first + size):
-                    group = group * wholes[span][head : head + 1] + states[span]
-                local_ref[at, :, columns] = group.astype(jnp.bfloat16)
-                at += 1
-            size *= 2
-        group = states[0]
-        for span in range(1, spans):
-            group = group * wholes[span][head : head + 1] + states[span]
-        message_ref[columns] = group.T
+            state = jnp.dot(faded, v_ref[rows, columns], preferred_element_type=jnp.float32)
+            at = 0
+            for bit in range(local_bits + 1):
+                if span >> bit & 1 == 0 or bit == local_bits:
+                    group = state
+                    if span % 2**bit > 0:
+                        group = held[bit - 1, head] * wholes[span][head : head + 1] + state
+                    if (span + 1) % 2**bit > 0:
+                        held[bit - 1, head] = group
+                    elif bit < local_bits:
+                        local_ref[at + (span >> (bit + 1)), :, columns] = group.astype(
+                            jnp.bfloat16
+                        )
+                    else:
+                        message_ref[columns] = group.T
+                at += spans >> (bit + 1)
     message_ref[heads * head_width :] = run
     for copy in copies[2 + spans :]:
         copy.wait()
@@ -149,6 +156,7 @@
         ],
         [
             pltpu.VMEM(log_decay.shape, jnp.float32),
+            pltpu.VMEM((spans.bit_length() - 1, heads, key_width, width // heads), jnp.float32),
             pltpu.SemaphoreType.DMA((spans + 5,)),
         ],
         [pl.BlockSpec(memory_space=pltpu.HBM)] * len(inputs),
@@ -459,6 +467,7 @@
         aliases = {len(inputs): 0}
         specs.append(out)
         inputs.append(begun)
+    name = "finish" + "".join(f"{core}{side}" for (core, side), _ in quarters)
     shapes = [jax.ShapeDtypeStruct((tokens, width), jnp.bfloat16)]
     if has_token:
         shapes.append(pltpu.VMEM((8, 128), jnp.float32))
@@ -474,7 +483,8 @@
         ],
         input_output_aliases=aliases,
         compiler_params=PARAMS,
-        name="finish" + "".join(f"{core}{side}" for (core, side), _ in quarters),
+        cost_estimate=cost(name),
+        name=name,
     )(*inputs)
 
 
@@ -517,12 +527,12 @@
 
     for bit in range(1, bits):
         found[bit] = [trade(chunk, 2**bit) for chunk in (give if bit == 1 else chunks)]
-        if bit == 1:
-            rest = trade(both("rest", chunks), 2)
+        stays = chunks if bit == 1 else stays
         waits = []
         if bit < 3 or bit == last:
             stop = spans if bit == last else at + 1
-            mixed, *waits = mix_local(at, stop, shared, mixed, chunks[-1:], bit < last)
+            begun = [*chunks[-1:], *([found[bit - 1]] if bit == last else [])]
+            mixed, *waits = mix_local(at, stop, shared, mixed, begun, bit < last)
             at = stop
         if bit == 3:
             waits.append(rest)
@@ -540,19 +550,19 @@
             found[bit] = both(f"found{bit}", found[bit], chunks[-1:])
             if bit > 1:
                 across[bit] = trade(found[bit], 2)
+            else:
+                rest = trade(both("rest", stays, chunks[-1:]), 2)
 
     quarters = [((core, side), [(0, 0, None)]) for core, side in sides]
     shared = (mixed, queries, sums, level_weight)
     mixed, token = add_levels(quarters, first_level, [0], shared, [zero], [other])
-    ended = token
-    ended = pack("ended0", [(ended, 8)], found[last])
-    ended = pack("ended1", [(ended, 8)])
-    ended = pack("ended2", [(ended, 8)])
+    state = both("state", found[last], (token,))
+    beside = trade(state, 2)
     early = list(range(2, last))
     pieces = [(found[1], two), (rest, two)]
     for bit in early:
         pieces += [(found[bit], two), (across[bit], two)]
-    near = pack("near", pieces, (ended,))
+    near = pack("near", pieces, (state,))
     far = trade(near, 1)
     middle = [1, *early]
     ahead = [prefixes[bit] for bit in middle]
@@ -562,11 +572,10 @@
 
     shared = (mixed, queries, sums, level_weight, gain)
     every = (first_level, [last, *middle], shared, [prefixes[last], *ahead])
-    state = both("state", found[last])
-    beside = trade(state, 2)
     quarters = {(core, side): [(0, 0, 0), *states_of(side, 1, 1)] for core, side in sides}
+    state_far = trade(pack("shared", [(state, two)], (near,)), 1)
     (out,) = finish([((0, 0), quarters[0, 0])], *every, [state, near], None, False)
-    out, token = finish([((1, 0), quarters[1, 0])], *every, [trade(state, 1), far], out, True)
+    out, token = finish([((1, 0), quarters[1, 0])], *every, [state_far, far], out, True)
     beside = pack("beside", [(beside, two)], (token,))
     (out,) = finish([((0, 1), quarters[0, 1])], *every, [beside, near], out, False)
     return finish([((1, 1), quarters[1, 1])], *every, [trade(beside, 1), far], out, False)[0]

time: 41 us -> 39.7 us (0.968)
  waiting for transfers between devices: 7.51 us -> 5.38 us
  starting transfers between devices: 19.3 us -> 20.2 us
    ppermute x16, waiting for transfers between devices: 7.51 us -> 5.38 us  [trade(): return lax.ppermute(value, AXES, pairs)]
    ppermute x16, starting transfers between devices: 19.3 us -> 20.2 us  [trade(): return lax.ppermute(value, AXES, pairs)]
    pallas_call x22 -> x20, Pallas kernels: 7.5 us -> 7.39 us  [call(): pl.pallas_call(kernel, in_specs=specs, out_specs=[HELD] * len(outputs), o...]
  transfers between devices with their start and end apart: 16 -> 16, of which waited for: 5 -> 3; matrix products, arithmetic and copies ran while one was open for 0% -> 0% of each run, Pallas kernels for 23% -> 24%
where the time goes in v15:
time: 39.7 us; the launch traced here: 39.5 us
  starting transfers between devices  20.2 us (51%)
  Pallas kernels  13.7 us (35%)
  waiting for transfers between devices  5.38 us (14%)
    ppermute x16, starting transfers between devices, trade(): return lax.ppermute(value, AXES, pairs)  20.2 us
    pallas_call x20, Pallas kernels, call(): pl.pallas_call(kernel, in_specs=specs, out_specs=[HELD] * len(outputs), o...  7.39 us
    pallas_call x4, Pallas kernels, finish(): pl.pallas_call(functools.partial(finish_kernel, quarters, first_level, bi...  6.31 us
    ppermute x16, waiting for transfers between devices, trade(): return lax.ppermute(value, AXES, pairs)  5.38 us
  transfers between devices with their start and end apart: 16, of which 3 were waited for; matrix products, arithmetic and copies ran while one was open for 0% of the time, Pallas kernels for 24%

profile of v15, /device:TPU:0, one launch (start us, length us, event | category | flops | bytes accessed | tf_op | source)
XLA Modules:
  0.0 39.5 jit_solution(10460299735300645134)
XLA Ops:
  0.0 2.6 %states.1 = (f32[1032,128]{1,0:T(8,128)S(1)}, bf16[3,128,1024]{2,1,0:T(8,128)(2,1)S(1)}, f32[2,8,1024]{2,1,0:T(8,128)S(1)}, f32[4,8,128]{2,1,0:T(8,128)S(1)}, bf...) custom-call(bf16[1024,128]{1,0:T(8,128)(2,1)} %refs_0_.1, ...), custom_call_target="tpu_custom_call" | custom-call | flops 2000000000 | bytes 1000000 | tf_op jit(solution)/shard_map/states/pallas_call | solution.py:50
  2.6 0.5 %collective-permute-start = (f32[1032,128]{1,0:T(8,128)S(1)}, f32[1032,128]{1,0:T(8,128)S(1)}, u32[]{:S(2)}, u32[]{:S(2)}) collective-permute-start(f32[1032,128]{1,0:T(8,128)S(1)} %get-tuple-element.40.mine_ref), channel_id=1, source_target_pairs={{0,8},{8,0},{16,24},{24,16},{1,9},{9,1},{17,25},{25,17},{2,10},{10... | collective-permute-start | bytes 1585160 | tf_op jit(solution)/shard_map/ppermute | solution.py:498
  3.1 1.5 %collective-permute-done.other_ref.refs_5_ = f32[1032,128]{1,0:T(8,128)S(1)} collective-permute-done((f32[1032,128]{1,0:T(8,128)S(1)}, f32[1032,128]{1,0:T(8,128)S(1)}, u32[]{:S(2)}, u32[]{:S(2)}) %collective-permute-start) | collective-permute-done | bytes 528416 | tf_op jit(solution)/shard_map/ppermute | solution.py:498
  4.7 3.0 %collective-permute-start.1 = (f32[136,128]{1,0:T(8,128)S(1)}, f32[136,128]{1,0:T(8,128)S(1)}, u32[]{:S(2)}, u32[]{:S(2)}) collective-permute-start(f32[136,128]{1,0:T(8,128)S(1)} %get-tuple-element.43), channel_id=1, source_target_pairs={{0,16},{8,24},{16,0},{24,8},{1,17},{9,25},{17,1},{25,9},{2,18},{10... | collective-permute-start | bytes 208904 | tf_op jit(solution)/shard_map/ppermute | solution.py:498
  7.7 0.8 %local0.1 = (f32[1024,1024]{1,0:T(8,128)S(1)}, f32[8,128]{1,0:T(8,128)S(1)}) custom-call(bf16[1024,128]{1,0:T(8,128)(2,1)S(1)} %get-tuple-element.33.refs_0_.refs_1_, bf16[1024,128]{1,0:T(8,128)(2,1)S(1)} %get-tuple-element.34.refs_1_, bf16[1024,1024]{1,0:T(8,128)(2,1)S(1)} %get-tuple-element.35.refs_2_, ...), custom_call_target="tpu_custom_call" | custom-call | flops 2000000000 | bytes 1000000 | tf_op jit(solution)/shard_map/local0/pallas_call | solution.py:50
  8.5 3.4 %collective-permute-done.2.refs_1_.refs_0_ = f32[136,128]{1,0:T(8,128)S(1)} collective-permute-done((f32[136,128]{1,0:T(8,128)S(1)}, f32[136,128]{1,0:T(8,128)S(1)}, u32[]{:S(2)}, u32[]{:S(2)}) %collective-permute-start.2) | collective-permute-done | bytes 69664 | tf_op jit(solution)/shard_map/ppermute | solution.py:498
  12.0 1.6 %collective-permute-start.4 = (f32[136,128]{1,0:T(8,128)S(1)}, f32[136,128]{1,0:T(8,128)S(1)}, u32[]{:S(2)}, u32[]{:S(2)}) collective-permute-start(f32[136,128]{1,0:T(8,128)S(1)} %merge10.1.refs_3_.refs_0_), channel_id=1, source_target_pairs={{0,1},{8,9},{16,17},{24,25},{1,0},{9,8},{17,16},{25,24},{2,3},{10,... | collective-permute-start | bytes 208904 | tf_op jit(solution)/shard_map/ppermute | solution.py:498
  13.6 0.6 %collective-permute-start.3 = (f32[136,128]{1,0:T(8,128)S(1)}, f32[136,128]{1,0:T(8,128)S(1)}, u32[]{:S(2)}, u32[]{:S(2)}) collective-permute-start(f32[136,128]{1,0:T(8,128)S(1)} %get-tuple-element.48.refs_8_.refs_0_.refs_2_), channel_id=1, source_target_pairs={{0,1},{8,9},{16,17},{24,25},{1,0},{9,8},{17,16},{25,24},{2,3},{10,... | collective-permute-start | bytes 208904 | tf_op jit(solution)/shard_map/ppermute | solution.py:498
  14.2 0.9 %local1.1 = (f32[1024,1024]{1,0:T(8,128)S(1)}, f32[8,128]{1,0:T(8,128)S(1)}) custom-call(bf16[1024,128]{1,0:T(8,128)(2,1)S(1)} %get-tuple-element.33.refs_0_.refs_1_, bf16[1024,128]{1,0:T(8,128)(2,1)S(1)} %get-tuple-element.34.refs_1_, bf16[1024,1024]{1,0:T(8,128)(2,1)S(1)} %get-tuple-element.35.refs_2_, ...), custom_call_target="tpu_custom_call", output_to_operand_aliasing={{0}: (7, {})} | custom-call | flops 2000000000 | bytes 1000000 | tf_op jit(solution)/shard_map/local1/pallas_call | solution.py:50
  15.1 1.5 %collective-permute-start.7 = (f32[256,128]{1,0:T(8,128)S(1)}, f32[256,128]{1,0:T(8,128)S(1)}, u32[]{:S(2)}, u32[]{:S(2)}) collective-permute-start(f32[256,128]{1,0:T(8,128)S(1)} %rest.1), channel_id=1, source_target_pairs={{0,16},{8,24},{16,0},{24,8},{1,17},{9,25},{17,1},{25,9},{2,18},{10... | collective-permute-start | bytes 393224 | tf_op jit(solution)/shard_map/ppermute | solution.py:498
  16.6 1.6 %collective-permute-start.6 = (f32[136,128]{1,0:T(8,128)S(1)}, f32[136,128]{1,0:T(8,128)S(1)}, u32[]{:S(2)}, u32[]{:S(2)}) collective-permute-start(f32[136,128]{1,0:T(8,128)S(1)} %merge20.1.refs_3_.refs_0_), channel_id=1, source_target_pairs={{0,2},{8,10},{16,18},{24,26},{1,3},{9,11},{17,19},{25,27},{2,0},{1... | collective-permute-start | bytes 208904 | tf_op jit(solution)/shard_map/ppermute | solution.py:498
  18.3 1.4 %collective-permute-start.5 = (f32[136,128]{1,0:T(8,128)S(1)}, f32[136,128]{1,0:T(8,128)S(1)}, u32[]{:S(2)}, u32[]{:S(2)}) collective-permute-start(f32[136,128]{1,0:T(8,128)S(1)} %get-tuple-element.52.refs_0_.refs_2_), channel_id=1, source_target_pairs={{0,2},{8,10},{16,18},{24,26},{1,3},{9,11},{17,19},{25,27},{2,0},{1... | collective-permute-start | bytes 208904 | tf_op jit(solution)/shard_map/ppermute | solution.py:498
  19.7 1.5 %collective-permute-start.11 = (f32[256,128]{1,0:T(8,128)S(1)}, f32[256,128]{1,0:T(8,128)S(1)}, u32[]{:S(2)}, u32[]{:S(2)}) collective-permute-start(f32[256,128]{1,0:T(8,128)S(1)} %found2.1.refs_2_), channel_id=1, source_target_pairs={{0,16},{8,24},{16,0},{24,8},{1,17},{9,25},{17,1},{25,9},{2,18},{10... | collective-permute-start | bytes 393224 | tf_op jit(solution)/shard_map/ppermute | solution.py:498
  21.2 2.7 %collective-permute-start.8 = (f32[136,128]{1,0:T(8,128)S(1)}, f32[136,128]{1,0:T(8,128)S(1)}, u32[]{:S(2)}, u32[]{:S(2)}) collective-permute-start(f32[136,128]{1,0:T(8,128)S(1)} %merge30.1.refs_3_), channel_id=1, source_target_pairs={{0,4},{8,12},{16,20},{24,28},{1,5},{9,13},{17,21},{25,29},{2,6},{1... | collective-permute-start | bytes 208904 | tf_op jit(solution)/shard_map/ppermute | solution.py:498
  23.9 1.5 %collective-permute-start.9 = (f32[136,128]{1,0:T(8,128)S(1)}, f32[136,128]{1,0:T(8,128)S(1)}, u32[]{:S(2)}, u32[]{:S(2)}) collective-permute-start(f32[136,128]{1,0:T(8,128)S(1)} %get-tuple-element.54.refs_2_.refs_8_), channel_id=1, source_target_pairs={{0,4},{8,12},{16,20},{24,28},{1,5},{9,13},{17,21},{25,29},{2,6},{1... | collective-permute-start | bytes 208904 | tf_op jit(solution)/shard_map/ppermute | solution.py:498
  25.4 1.7 %collective-permute-start.12 = (f32[256,128]{1,0:T(8,128)S(1)}, f32[256,128]{1,0:T(8,128)S(1)}, u32[]{:S(2)}, u32[]{:S(2)}) collective-permute-start(f32[256,128]{1,0:T(8,128)S(1)} %found3.1.refs_9_.refs_4_), channel_id=1, source_target_pairs={{0,16},{8,24},{16,0},{24,8},{1,17},{9,25},{17,1},{25,9},{2,18},{10... | collective-permute-start | bytes 393224 | tf_op jit(solution)/shard_map/ppermute | solution.py:498
  27.1 1.7 %local2.1.refs_0_ = f32[1024,1024]{1,0:T(8,128)S(1)} custom-call(bf16[1024,128]{1,0:T(8,128)(2,1)S(1)} %get-tuple-element.33.refs_0_.refs_1_, bf16[1024,128]{1,0:T(8,128)(2,1)S(1)} %get-tuple-element.34.refs_1_, bf16[1024,1024]{1,0:T(8,128)(2,1)S(1)} %get-tuple-element.35.refs_2_, ...), custom_call_target="tpu_custom_call", output_to_operand_aliasing={{}: (7, {})} | custom-call | flops 1000 | bytes 1000000 | tf_op jit(solution)/shard_map/local2/pallas_call | solution.py:50
  28.8 1.1 %reach.1 = (f32[1024,1024]{1,0:T(8,128)S(1)}, f32[8,128]{1,0:T(8,128)S(1)}) custom-call(f32[1024,1024]{1,0:T(8,128)S(1)} %local2.1.refs_0_, bf16[1024,128]{1,0:T(8,128)(2,1)S(1)} %get-tuple-element.33.refs_0_.refs_1_, f32[2,8,1024]{2,1,0:T(8,128)S(1)} %get-tuple-element.36.refs_3_.refs_2_, ...), custom_call_target="tpu_custom_call", output_to_operand_aliasing={{0}: (0, {})} | custom-call | flops 1000 | bytes 1000000 | tf_op jit(solution)/shard_map/reach/pallas_call | solution.py:50
  29.9 2.0 %collective-permute-start.10 = (f32[256,128]{1,0:T(8,128)S(1)}, f32[256,128]{1,0:T(8,128)S(1)}, u32[]{:S(2)}, u32[]{:S(2)}) collective-permute-start(f32[256,128]{1,0:T(8,128)S(1)} %state.1.refs_6_.refs_0_.refs_9_), channel_id=1, source_target_pairs={{0,16},{8,24},{16,0},{24,8},{1,17},{9,25},{17,1},{25,9},{2,18},{10... | collective-permute-start | bytes 393224 | tf_op jit(solution)/shard_map/ppermute | solution.py:498
  32.1 0.5 %collective-permute-start.13 = (f32[256,128]{1,0:T(8,128)S(1)}, f32[256,128]{1,0:T(8,128)S(1)}, u32[]{:S(2)}, u32[]{:S(2)}) collective-permute-start(f32[256,128]{1,0:T(8,128)S(1)} %shared.1), channel_id=1, source_target_pairs={{0,8},{8,0},{16,24},{24,16},{1,9},{9,1},{17,25},{25,17},{2,10},{10... | collective-permute-start | bytes 393224 | tf_op jit(solution)/shard_map/ppermute | solution.py:498
  32.6 1.6 %finish00.1.refs_11_ = bf16[1024,1024]{1,0:T(8,128)(2,1)} custom-call(f32[1024,1024]{1,0:T(8,128)S(1)} %get-tuple-element.55.refs_0_, bf16[1024,128]{1,0:T(8,128)(2,1)S(1)} %get-tuple-element.33.refs_0_.refs_1_, f32[2,8,1024]{2,1,0:T(8,128)S(1)} %get-tuple-element.36.refs_3_.refs_2_, f32[8,8,1024]{2,1,0:T(8,128)S(1)} %get-tuple-element.38.refs_5_.refs_3_, ...), custom_call_target="tpu_custom_call" | custom-call | flops 20000000000 | bytes 1000000 | tf_op jit(solution)/shard_map/finish00/pallas_call | solution.py:474
  34.6 1.6 %finish10.1 = (bf16[1024,1024]{1,0:T(8,128)(2,1)}, f32[8,128]{1,0:T(8,128)S(1)}) custom-call(f32[1024,1024]{1,0:T(8,128)S(1)} %get-tuple-element.55.refs_0_, bf16[1024,128]{1,0:T(8,128)(2,1)S(1)} %get-tuple-element.33.refs_0_.refs_1_, f32[2,8,1024]{2,1,0:T(8,128)S(1)} %get-tuple-element.36.refs_3_.refs_2_, ...), custom_call_target="tpu_custom_call", output_to_operand_aliasing={{0}: (11, {})} | custom-call | flops 1000 | bytes 1000000 | tf_op jit(solution)/shard_map/finish10/pallas_call | solution.py:474
  36.4 1.6 %finish01.1.refs_11_ = bf16[1024,1024]{1,0:T(8,128)(2,1)} custom-call(f32[1024,1024]{1,0:T(8,128)S(1)} %get-tuple-element.55.refs_0_, bf16[1024,128]{1,0:T(8,128)(2,1)S(1)} %get-tuple-element.33.refs_0_.refs_1_, f32[2,8,1024]{2,1,0:T(8,128)S(1)} %get-tuple-element.36.refs_3_.refs_2_, ...), custom_call_target="tpu_custom_call", output_to_operand_aliasing={{}: (11, {})} | custom-call | flops 20000000000 | bytes 1000000 | tf_op jit(solution)/shard_map/finish01/pallas_call | solution.py:474
  38.0 1.6 %finish11.1 = bf16[1024,1024]{1,0:T(8,128)(2,1)} custom-call(f32[1024,1024]{1,0:T(8,128)S(1)} %get-tuple-element.55.refs_0_, bf16[1024,128]{1,0:T(8,128)(2,1)S(1)} %get-tuple-element.33.refs_0_.refs_1_, f32[2,8,1024]{2,1,0:T(8,128)S(1)} %get-tuple-element.36.refs_3_.refs_2_, ...), custom_call_target="tpu_custom_call", output_to_operand_aliasing={{}: (11, {})} | custom-call | flops 2000000000 | bytes 1000000 | tf_op jit(solution)/shard_map/finish11/pallas_call | solution.py:474
  (33 shorter events, 1.1 us)
Async XLA Ops:
  2.6 2.1 %collective-permute-start = (f32[1032,128]{1,0:T(8,128)S(1)}, f32[1032,128]{1,0:T(8,128)S(1)}, u32[]{:S(2)}, u32[]{:S(2)}) collective-permute-start(f32[1032,128]{1,0:T(8,128)S(1)} %get-tuple-element.40.mine_ref), channel_id=1, source_target_pairs={{0,8},{8,0},{16,24},{24,16},{1,9},{9,1},{17,25},{25,17},{2,10},{10... | collective-permute-start | bytes 1585160 | tf_op jit(solution)/shard_map/ppermute | solution.py:498
  4.7 8.9 %collective-permute-start.1 = (f32[136,128]{1,0:T(8,128)S(1)}, f32[136,128]{1,0:T(8,128)S(1)}, u32[]{:S(2)}, u32[]{:S(2)}) collective-permute-start(f32[136,128]{1,0:T(8,128)S(1)} %get-tuple-element.43), channel_id=1, source_target_pairs={{0,16},{8,24},{16,0},{24,8},{1,17},{9,25},{17,1},{25,9},{2,18},{10... | collective-permute-start | bytes 208904 | tf_op jit(solution)/shard_map/ppermute | solution.py:498
  7.7 4.3 %collective-permute-start.2 = (f32[136,128]{1,0:T(8,128)S(1)}, f32[136,128]{1,0:T(8,128)S(1)}, u32[]{:S(2)}, u32[]{:S(2)}) collective-permute-start(f32[136,128]{1,0:T(8,128)S(1)} %get-tuple-element.46), channel_id=1, source_target_pairs={{0,16},{8,24},{16,0},{24,8},{1,17},{9,25},{17,1},{25,9},{2,18},{10... | collective-permute-start | bytes 208904 | tf_op jit(solution)/shard_map/ppermute | solution.py:498
  12.0 4.6 %collective-permute-start.4 = (f32[136,128]{1,0:T(8,128)S(1)}, f32[136,128]{1,0:T(8,128)S(1)}, u32[]{:S(2)}, u32[]{:S(2)}) collective-permute-start(f32[136,128]{1,0:T(8,128)S(1)} %merge10.1.refs_3_.refs_0_), channel_id=1, source_target_pairs={{0,1},{8,9},{16,17},{24,25},{1,0},{9,8},{17,16},{25,24},{2,3},{10,... | collective-permute-start | bytes 208904 | tf_op jit(solution)/shard_map/ppermute | solution.py:498
  13.6 4.7 %collective-permute-start.3 = (f32[136,128]{1,0:T(8,128)S(1)}, f32[136,128]{1,0:T(8,128)S(1)}, u32[]{:S(2)}, u32[]{:S(2)}) collective-permute-start(f32[136,128]{1,0:T(8,128)S(1)} %get-tuple-element.48.refs_8_.refs_0_.refs_2_), channel_id=1, source_target_pairs={{0,1},{8,9},{16,17},{24,25},{1,0},{9,8},{17,16},{25,24},{2,3},{10,... | collective-permute-start | bytes 208904 | tf_op jit(solution)/shard_map/ppermute | solution.py:498
  15.1 8.7 %collective-permute-start.7 = (f32[256,128]{1,0:T(8,128)S(1)}, f32[256,128]{1,0:T(8,128)S(1)}, u32[]{:S(2)}, u32[]{:S(2)}) collective-permute-start(f32[256,128]{1,0:T(8,128)S(1)} %rest.1), channel_id=1, source_target_pairs={{0,16},{8,24},{16,0},{24,8},{1,17},{9,25},{17,1},{25,9},{2,18},{10... | collective-permute-start | bytes 393224 | tf_op jit(solution)/shard_map/ppermute | solution.py:498
  16.6 4.5 %collective-permute-start.6 = (f32[136,128]{1,0:T(8,128)S(1)}, f32[136,128]{1,0:T(8,128)S(1)}, u32[]{:S(2)}, u32[]{:S(2)}) collective-permute-start(f32[136,128]{1,0:T(8,128)S(1)} %merge20.1.refs_3_.refs_0_), channel_id=1, source_target_pairs={{0,2},{8,10},{16,18},{24,26},{1,3},{9,11},{17,19},{25,27},{2,0},{1... | collective-permute-start | bytes 208904 | tf_op jit(solution)/shard_map/ppermute | solution.py:498
  18.3 5.5 %collective-permute-start.5 = (f32[136,128]{1,0:T(8,128)S(1)}, f32[136,128]{1,0:T(8,128)S(1)}, u32[]{:S(2)}, u32[]{:S(2)}) collective-permute-start(f32[136,128]{1,0:T(8,128)S(1)} %get-tuple-element.52.refs_0_.refs_2_), channel_id=1, source_target_pairs={{0,2},{8,10},{16,18},{24,26},{1,3},{9,11},{17,19},{25,27},{2,0},{1... | collective-permute-start | bytes 208904 | tf_op jit(solution)/shard_map/ppermute | solution.py:498
  19.7 12.2 %collective-permute-start.11 = (f32[256,128]{1,0:T(8,128)S(1)}, f32[256,128]{1,0:T(8,128)S(1)}, u32[]{:S(2)}, u32[]{:S(2)}) collective-permute-start(f32[256,128]{1,0:T(8,128)S(1)} %found2.1.refs_2_), channel_id=1, source_target_pairs={{0,16},{8,24},{16,0},{24,8},{1,17},{9,25},{17,1},{25,9},{2,18},{10... | collective-permute-start | bytes 393224 | tf_op jit(solution)/shard_map/ppermute | solution.py:498
  21.2 8.7 %collective-permute-start.8 = (f32[136,128]{1,0:T(8,128)S(1)}, f32[136,128]{1,0:T(8,128)S(1)}, u32[]{:S(2)}, u32[]{:S(2)}) collective-permute-start(f32[136,128]{1,0:T(8,128)S(1)} %merge30.1.refs_3_), channel_id=1, source_target_pairs={{0,4},{8,12},{16,20},{24,28},{1,5},{9,13},{17,21},{25,29},{2,6},{1... | collective-permute-start | bytes 208904 | tf_op jit(solution)/shard_map/ppermute | solution.py:498
  23.9 6.0 %collective-permute-start.9 = (f32[136,128]{1,0:T(8,128)S(1)}, f32[136,128]{1,0:T(8,128)S(1)}, u32[]{:S(2)}, u32[]{:S(2)}) collective-permute-start(f32[136,128]{1,0:T(8,128)S(1)} %get-tuple-element.54.refs_2_.refs_8_), channel_id=1, source_target_pairs={{0,4},{8,12},{16,20},{24,28},{1,5},{9,13},{17,21},{25,29},{2,6},{1... | collective-permute-start | bytes 208904 | tf_op jit(solution)/shard_map/ppermute | solution.py:498
  25.4 6.5 %collective-permute-start.12 = (f32[256,128]{1,0:T(8,128)S(1)}, f32[256,128]{1,0:T(8,128)S(1)}, u32[]{:S(2)}, u32[]{:S(2)}) collective-permute-start(f32[256,128]{1,0:T(8,128)S(1)} %found3.1.refs_9_.refs_4_), channel_id=1, source_target_pairs={{0,16},{8,24},{16,0},{24,8},{1,17},{9,25},{17,1},{25,9},{2,18},{10... | collective-permute-start | bytes 393224 | tf_op jit(solution)/shard_map/ppermute | solution.py:498
  29.9 6.2 %collective-permute-start.10 = (f32[256,128]{1,0:T(8,128)S(1)}, f32[256,128]{1,0:T(8,128)S(1)}, u32[]{:S(2)}, u32[]{:S(2)}) collective-permute-start(f32[256,128]{1,0:T(8,128)S(1)} %state.1.refs_6_.refs_0_.refs_9_), channel_id=1, source_target_pairs={{0,16},{8,24},{16,0},{24,8},{1,17},{9,25},{17,1},{25,9},{2,18},{10... | collective-permute-start | bytes 393224 | tf_op jit(solution)/shard_map/ppermute | solution.py:498
  32.0 2.5 %collective-permute-start.14 = (f32[1536,128]{1,0:T(8,128)S(1)}, f32[1536,128]{1,0:T(8,128)S(1)}, u32[]{:S(2)}, u32[]{:S(2)}) collective-permute-start(f32[1536,128]{1,0:T(8,128)S(1)} %near.1.refs_1_.refs_10_), channel_id=1, source_target_pairs={{0,8},{8,0},{16,24},{24,16},{1,9},{9,1},{17,25},{25,17},{2,10},{10... | collective-permute-start | bytes 2359304 | tf_op jit(solution)/shard_map/ppermute | solution.py:498
  32.1 2.5 %collective-permute-start.13 = (f32[256,128]{1,0:T(8,128)S(1)}, f32[256,128]{1,0:T(8,128)S(1)}, u32[]{:S(2)}, u32[]{:S(2)}) collective-permute-start(f32[256,128]{1,0:T(8,128)S(1)} %shared.1), channel_id=1, source_target_pairs={{0,8},{8,0},{16,24},{24,16},{1,9},{9,1},{17,25},{25,17},{2,10},{10... | collective-permute-start | bytes 393224 | tf_op jit(solution)/shard_map/ppermute | solution.py:498
  36.2 1.8 %collective-permute-start.15 = (f32[256,128]{1,0:T(8,128)S(1)}, f32[256,128]{1,0:T(8,128)S(1)}, u32[]{:S(2)}, u32[]{:S(2)}) collective-permute-start(f32[256,128]{1,0:T(8,128)S(1)} %beside.1.refs_9_), channel_id=1, source_target_pairs={{0,8},{8,0},{16,24},{24,16},{1,9},{9,1},{17,25},{25,17},{2,10},{10... | collective-permute-start | bytes 393224 | tf_op jit(solution)/shard_map/ppermute | solution.py:498

commit v16 on v15

--- a/solution.py
+++ b/solution.py
@@ -409,24 +409,34 @@
     )
 
 
-def finish_kernel(quarters, first_level, bits, has_token, *refs):
+def finish_kernel(quarters, first_level, bits, stays, carried, *refs):
     mixed_ref, q_ref, sums_ref, weight_ref, gain_ref = refs[:5]
     prefix_refs = refs[5 : 5 + len(bits)]
     part_refs = refs[5 + len(bits) :]
-    out_ref, scale_ref, sent = refs[-3:]
-    out_hbm = refs[-5] if has_token else refs[-4]
-    if has_token:
-        refs[-4][...] = jnp.zeros_like(refs[-4])
+    out_refs, (own_ref, scale_ref, sent) = refs[-3 - FINISH_OUTS[stays, carried] : -3], refs[-3:]
+    if stays:
+        own_ref = out_refs[-1]
     heads = weight_ref.shape[1]
     head_width = mixed_ref.shape[0] // heads
-    count = heads // 4
-    size = count * head_width
+    size = heads // 4 * head_width
+    copies = []
+
+    def send(block, far, rows):
+        columns = pl.ds(pl.multiple_of(first_head(far, heads) * head_width, 128), size)
+        copy = pltpu.make_async_copy(
+            block.at[rows], out_refs[0].at[rows, columns], sent.at[len(copies)]
+        )
+        copy.start()
+        copies.append(copy)
+
+    if carried is not None:
+        index, far = carried
+        send(part_refs[index], far, slice(0, q_ref.shape[0]))
     work = gather_work(quarters, part_refs, heads, head_width)
     gains = []
     for head, _ in work:
         row = jnp.broadcast_to(gain_ref[pl.ds(head, 1)], (8, head_width))
         gains.append(row.T[:, :1])
-    copies = []
     for span in range(q_ref.shape[0] // SPAN):
         tokens = slice(span * SPAN, (span + 1) * SPAN)
         queries = q_ref[tokens]
@@ -440,46 +450,48 @@
             square = jnp.mean(mixed * mixed, axis=0, keepdims=True)
             normed = mixed * lax.rsqrt(square + EPS) * gains[at]
             columns = slice(at * head_width, (at + 1) * head_width)
-            out_ref[tokens, columns] = normed.astype(jnp.bfloat16).T
-        for at, (far, _) in enumerate(quarters):
-            columns = pl.ds(pl.multiple_of(first_head(far, heads) * head_width, 128), size)
-            copy = pltpu.make_async_copy(
-                out_ref.at[tokens, at * size : (at + 1) * size],
-                out_hbm.at[tokens, columns],
-                sent.at[len(copies)],
-            )
-            copy.start()
-            copies.append(copy)
+            own_ref[tokens, columns] = normed.astype(jnp.bfloat16).T
+        if not stays:
+            send(own_ref, quarters[0][0], tokens)
     for copy in copies:
         copy.wait()
 
 
-def finish(quarters, first_level, bits, shared, prefixes, parts, begun, has_token):
+FINISH_OUTS = {}
+
+
+def finish(quarters, first_level, bits, shared, prefixes, parts, begun, stays, carried):
     mixed, queries, sums, level_weight, gain = shared
     width, tokens = mixed.shape
     heads = level_weight.shape[1]
     inputs = [*shared, *prefixes, *parts]
     specs = [HELD] * len(inputs)
     inputs = [hold(array) for array in inputs]
-    out = pl.BlockSpec(memory_space=pltpu.HBM)
+    hbm = pl.BlockSpec(memory_space=pltpu.HBM)
     aliases = {}
     if begun is not None:
         aliases = {len(inputs): 0}
-        specs.append(out)
+        specs.append(hbm)
         inputs.append(begun)
     name = "finish" + "".join(f"{core}{side}" for (core, side), _ in quarters)
-    shapes = [jax.ShapeDtypeStruct((tokens, width), jnp.bfloat16)]
-    if has_token:
-        shapes.append(pltpu.VMEM((8, 128), jnp.float32))
+    block = (tokens, width // 4)
+    out_specs, shapes = [], []
+    if carried is not None or not stays:
+        out_specs.append(hbm)
+        shapes.append(jax.ShapeDtypeStruct((tokens, width), jnp.bfloat16))
+    if stays:
+        out_specs.append(HELD)
+        shapes.append(pltpu.VMEM(block, jnp.bfloat16))
+    FINISH_OUTS[stays, carried] = len(shapes)
     return pl.pallas_call(
-        functools.partial(finish_kernel, quarters, first_level, bits, has_token),
+        functools.partial(finish_kernel, quarters, first_level, bits, stays, carried),
         in_specs=specs,
-        out_specs=[out, HELD][: len(shapes)],
+        out_specs=out_specs,
         out_shape=shapes,
         scratch_shapes=[
-            pltpu.VMEM((tokens, len(quarters) * width // 4), jnp.bfloat16),
+            pltpu.VMEM((8, 128) if stays else block, jnp.bfloat16),
             pltpu.VMEM((len(bits), heads, SPAN), jnp.float32),
-            pltpu.SemaphoreType.DMA((len(quarters) * (tokens // SPAN),)),
+            pltpu.SemaphoreType.DMA((1 + tokens // SPAN,)),
         ],
         input_output_aliases=aliases,
         compiler_params=PARAMS,
@@ -537,21 +549,22 @@
         if bit == 3:
             waits.append(rest)
         if bit < last:
-            merged = []
-            for offset, (chunk, state) in enumerate(zip(chunks, found[bit])):
-                ending = offset == CUTS - 1
-                tokens_of = [*merged[-1:], *(waits if ending else ())]
-                chunk, *after = merge(
-                    bit, offset, ending, chunk, state, prefixes[bit], tokens_of
+            merged = {}
+            order = list(reversed(range(CUTS)))
+            for offset in order:
+                ending = offset == order[-1]
+                tokens_of = [*merged.values(), *(waits if ending else ())]
+                merged[offset], *after = merge(
+                    bit, offset, ending, chunks[offset], found[bit][offset], prefixes[bit], tokens_of
                 )
-                merged.append(chunk)
-            chunks = merged
+            chunks = [merged[offset] for offset in range(CUTS)]
+            newest = merged[order[-1]]
             prefixes += after
             found[bit] = both(f"found{bit}", found[bit], chunks[-1:])
             if bit > 1:
                 across[bit] = trade(found[bit], 2)
             else:
-                rest = trade(both("rest", stays, chunks[-1:]), 2)
+                rest = trade(both("rest", stays, (newest,)), 2)
 
     quarters = [((core, side), [(0, 0, None)]) for core, side in sides]
     shared = (mixed, queries, sums, level_weight)
@@ -574,11 +587,16 @@
     every = (first_level, [last, *middle], shared, [prefixes[last], *ahead])
     quarters = {(core, side): [(0, 0, 0), *states_of(side, 1, 1)] for core, side in sides}
     state_far = trade(pack("shared", [(state, two)], (near,)), 1)
-    (out,) = finish([((0, 0), quarters[0, 0])], *every, [state, near], None, False)
-    out, token = finish([((1, 0), quarters[1, 0])], *every, [state_far, far], out, True)
-    beside = pack("beside", [(beside, two)], (token,))
-    (out,) = finish([((0, 1), quarters[0, 1])], *every, [beside, near], out, False)
-    return finish([((1, 1), quarters[1, 1])], *every, [trade(beside, 1), far], out, False)[0]
+    (block,) = finish([((0, 0), quarters[0, 0])], *every, [state, near], None, True, None)
+    out, block = finish(
+        [((1, 0), quarters[1, 0])], *every, [state_far, far, block], None, True, (2, (0, 0))
+    )
+    beside = pack("beside", [(beside, two)], (block,))
+    (out,) = finish(
+        [((0, 1), quarters[0, 1])], *every, [beside, near, block], out, False, (2, (1, 0))
+    )
+    beside_far = trade(beside, 1)
+    return finish([((1, 1), quarters[1, 1])], *every, [beside_far, far], out, False, None)[0]
 
 
 def solution(mesh):

time: 39.7 us -> 38.5 us (0.970)
  waiting for transfers between devices: 5.38 us -> 4.87 us
  Pallas kernels: 13.7 us -> 13.2 us
    pallas_call x4, Pallas kernels: 6.31 us -> 5.77 us  [finish(): pl.pallas_call(functools.partial(finish_kernel, quarters, first_level, bi...]
    ppermute x16, waiting for transfers between devices: 5.38 us -> 4.87 us  [trade(): return lax.ppermute(value, AXES, pairs)]
  transfers between devices with their start and end apart: 16 -> 16, of which waited for: 3 -> 4; matrix products, arithmetic and copies ran while one was open for 0% -> 0% of each run, Pallas kernels for 24% -> 23%
where the time goes in v16:
time: 38.5 us; the launch traced here: 38.4 us
  starting transfers between devices  20.1 us (52%)
  Pallas kernels  13.2 us (34%)
  waiting for transfers between devices  4.87 us (13%)
    ppermute x16, starting transfers between devices, trade(): return lax.ppermute(value, AXES, pairs)  20.1 us
    pallas_call x20, Pallas kernels, call(): pl.pallas_call(kernel, in_specs=specs, out_specs=[HELD] * len(outputs), o...  7.39 us
    pallas_call x4, Pallas kernels, finish(): pl.pallas_call(functools.partial(finish_kernel, quarters, first_level, bi...  5.77 us
    ppermute x16, waiting for transfers between devices, trade(): return lax.ppermute(value, AXES, pairs)  4.87 us
  transfers between devices with their start and end apart: 16, of which 4 were waited for; matrix products, arithmetic and copies ran while one was open for 0% of the time, Pallas kernels for 23%

profile of v16, /device:TPU:0, one launch (start us, length us, event | category | flops | bytes accessed | tf_op | source)
XLA Modules:
  0.0 38.4 jit_solution(17772973754671570522)
XLA Ops:
  0.0 2.6 %states.1 = (f32[1032,128]{1,0:T(8,128)S(1)}, bf16[3,128,1024]{2,1,0:T(8,128)(2,1)S(1)}, f32[2,8,1024]{2,1,0:T(8,128)S(1)}, f32[4,8,128]{2,1,0:T(8,128)S(1)}, bf...) custom-call(bf16[1024,128]{1,0:T(8,128)(2,1)} %refs_0_.1, ...), custom_call_target="tpu_custom_call" | custom-call | flops 2000000000 | bytes 1000000 | tf_op jit(solution)/shard_map/states/pallas_call | solution.py:50
  3.1 1.5 %collective-permute-done.other_ref.refs_5_ = f32[1032,128]{1,0:T(8,128)S(1)} collective-permute-done((f32[1032,128]{1,0:T(8,128)S(1)}, f32[1032,128]{1,0:T(8,128)S(1)}, u32[]{:S(2)}, u32[]{:S(2)}) %collective-permute-start) | collective-permute-done | bytes 528416 | tf_op jit(solution)/shard_map/ppermute | solution.py:510
  4.7 3.0 %collective-permute-start.1 = (f32[136,128]{1,0:T(8,128)S(1)}, f32[136,128]{1,0:T(8,128)S(1)}, u32[]{:S(2)}, u32[]{:S(2)}) collective-permute-start(f32[136,128]{1,0:T(8,128)S(1)} %get-tuple-element.43), channel_id=1, source_target_pairs={{0,16},{8,24},{16,0},{24,8},{1,17},{9,25},{17,1},{25,9},{2,18},{10... | collective-permute-start | bytes 208904 | tf_op jit(solution)/shard_map/ppermute | solution.py:510
  7.7 0.8 %local0.1 = (f32[1024,1024]{1,0:T(8,128)S(1)}, f32[8,128]{1,0:T(8,128)S(1)}) custom-call(bf16[1024,128]{1,0:T(8,128)(2,1)S(1)} %get-tuple-element.33.refs_0_.refs_1_, bf16[1024,128]{1,0:T(8,128)(2,1)S(1)} %get-tuple-element.34.refs_1_, bf16[1024,1024]{1,0:T(8,128)(2,1)S(1)} %get-tuple-element.35.refs_2_, ...), custom_call_target="tpu_custom_call" | custom-call | flops 2000000000 | bytes 1000000 | tf_op jit(solution)/shard_map/local0/pallas_call | solution.py:50
  8.5 1.6 %collective-permute-done.1.refs_1_ = f32[136,128]{1,0:T(8,128)S(1)} collective-permute-done((f32[136,128]{1,0:T(8,128)S(1)}, f32[136,128]{1,0:T(8,128)S(1)}, u32[]{:S(2)}, u32[]{:S(2)}) %collective-permute-start.1) | collective-permute-done | bytes 69664 | tf_op jit(solution)/shard_map/ppermute | solution.py:510
  10.2 2.2 %collective-permute-start.2 = (f32[136,128]{1,0:T(8,128)S(1)}, f32[136,128]{1,0:T(8,128)S(1)}, u32[]{:S(2)}, u32[]{:S(2)}) collective-permute-start(f32[136,128]{1,0:T(8,128)S(1)} %merge11.1.refs_8_.refs_3_.refs_0_.refs_2_), channel_id=1, source_target_pairs={{0,1},{8,9},{16,17},{24,25},{1,0},{9,8},{17,16},{25,24},{2,3},{10,... | collective-permute-start | bytes 208904 | tf_op jit(solution)/shard_map/ppermute | solution.py:510
  12.5 1.1 %collective-permute-start.5 = (f32[136,128]{1,0:T(8,128)S(1)}, f32[136,128]{1,0:T(8,128)S(1)}, u32[]{:S(2)}, u32[]{:S(2)}) collective-permute-start(f32[136,128]{1,0:T(8,128)S(1)} %get-tuple-element.50.refs_0_.refs_2_), channel_id=1, source_target_pairs={{0,1},{8,9},{16,17},{24,25},{1,0},{9,8},{17,16},{25,24},{2,3},{10,... | collective-permute-start | bytes 208904 | tf_op jit(solution)/shard_map/ppermute | solution.py:510
  13.6 0.9 %local1.1 = (f32[1024,1024]{1,0:T(8,128)S(1)}, f32[8,128]{1,0:T(8,128)S(1)}) custom-call(bf16[1024,128]{1,0:T(8,128)(2,1)S(1)} %get-tuple-element.33.refs_0_.refs_1_, bf16[1024,128]{1,0:T(8,128)(2,1)S(1)} %get-tuple-element.34.refs_1_, bf16[1024,1024]{1,0:T(8,128)(2,1)S(1)} %get-tuple-element.35.refs_2_, ...), custom_call_target="tpu_custom_call", output_to_operand_aliasing={{0}: (7, {})} | custom-call | flops 2000000000 | bytes 1000000 | tf_op jit(solution)/shard_map/local1/pallas_call | solution.py:50
  14.5 1.5 %collective-permute-start.7 = (f32[256,128]{1,0:T(8,128)S(1)}, f32[256,128]{1,0:T(8,128)S(1)}, u32[]{:S(2)}, u32[]{:S(2)}) collective-permute-start(f32[256,128]{1,0:T(8,128)S(1)} %rest.1), channel_id=1, source_target_pairs={{0,16},{8,24},{16,0},{24,8},{1,17},{9,25},{17,1},{25,9},{2,18},{10... | collective-permute-start | bytes 393224 | tf_op jit(solution)/shard_map/ppermute | solution.py:510
  16.0 1.6 %collective-permute-start.4 = (f32[136,128]{1,0:T(8,128)S(1)}, f32[136,128]{1,0:T(8,128)S(1)}, u32[]{:S(2)}, u32[]{:S(2)}) collective-permute-start(f32[136,128]{1,0:T(8,128)S(1)} %merge21.1.refs_3_.refs_0_.refs_2_), channel_id=1, source_target_pairs={{0,2},{8,10},{16,18},{24,26},{1,3},{9,11},{17,19},{25,27},{2,0},{1... | collective-permute-start | bytes 208904 | tf_op jit(solution)/shard_map/ppermute | solution.py:510
  17.7 0.9 %collective-permute-start.6 = (f32[136,128]{1,0:T(8,128)S(1)}, f32[136,128]{1,0:T(8,128)S(1)}, u32[]{:S(2)}, u32[]{:S(2)}) collective-permute-start(f32[136,128]{1,0:T(8,128)S(1)} %get-tuple-element.53.refs_0_), channel_id=1, source_target_pairs={{0,2},{8,10},{16,18},{24,26},{1,3},{9,11},{17,19},{25,27},{2,0},{1... | collective-permute-start | bytes 208904 | tf_op jit(solution)/shard_map/ppermute | solution.py:510
  18.6 1.8 %collective-permute-start.11 = (f32[256,128]{1,0:T(8,128)S(1)}, f32[256,128]{1,0:T(8,128)S(1)}, u32[]{:S(2)}, u32[]{:S(2)}) collective-permute-start(f32[256,128]{1,0:T(8,128)S(1)} %found2.1.refs_2_), channel_id=1, source_target_pairs={{0,16},{8,24},{16,0},{24,8},{1,17},{9,25},{17,1},{25,9},{2,18},{10... | collective-permute-start | bytes 393224 | tf_op jit(solution)/shard_map/ppermute | solution.py:510
  20.4 2.7 %collective-permute-start.9 = (f32[136,128]{1,0:T(8,128)S(1)}, f32[136,128]{1,0:T(8,128)S(1)}, u32[]{:S(2)}, u32[]{:S(2)}) collective-permute-start(f32[136,128]{1,0:T(8,128)S(1)} %merge31.1.refs_2_.refs_8_.refs_3_), channel_id=1, source_target_pairs={{0,4},{8,12},{16,20},{24,28},{1,5},{9,13},{17,21},{25,29},{2,6},{1... | collective-permute-start | bytes 208904 | tf_op jit(solution)/shard_map/ppermute | solution.py:510
  23.1 1.9 %collective-permute-start.8 = (f32[136,128]{1,0:T(8,128)S(1)}, f32[136,128]{1,0:T(8,128)S(1)}, u32[]{:S(2)}, u32[]{:S(2)}) collective-permute-start(f32[136,128]{1,0:T(8,128)S(1)} %get-tuple-element.57), channel_id=1, source_target_pairs={{0,4},{8,12},{16,20},{24,28},{1,5},{9,13},{17,21},{25,29},{2,6},{1... | collective-permute-start | bytes 208904 | tf_op jit(solution)/shard_map/ppermute | solution.py:510
  25.0 0.9 %collective-permute-start.12 = (f32[256,128]{1,0:T(8,128)S(1)}, f32[256,128]{1,0:T(8,128)S(1)}, u32[]{:S(2)}, u32[]{:S(2)}) collective-permute-start(f32[256,128]{1,0:T(8,128)S(1)} %found3.1.refs_9_.refs_4_), channel_id=1, source_target_pairs={{0,16},{8,24},{16,0},{24,8},{1,17},{9,25},{17,1},{25,9},{2,18},{10... | collective-permute-start | bytes 393224 | tf_op jit(solution)/shard_map/ppermute | solution.py:510
  25.9 1.7 %local2.1.refs_0_ = f32[1024,1024]{1,0:T(8,128)S(1)} custom-call(bf16[1024,128]{1,0:T(8,128)(2,1)S(1)} %get-tuple-element.33.refs_0_.refs_1_, bf16[1024,128]{1,0:T(8,128)(2,1)S(1)} %get-tuple-element.34.refs_1_, bf16[1024,1024]{1,0:T(8,128)(2,1)S(1)} %get-tuple-element.35.refs_2_, ...), custom_call_target="tpu_custom_call", output_to_operand_aliasing={{}: (7, {})} | custom-call | flops 1000 | bytes 1000000 | tf_op jit(solution)/shard_map/local2/pallas_call | solution.py:50
  27.6 1.1 %reach.1 = (f32[1024,1024]{1,0:T(8,128)S(1)}, f32[8,128]{1,0:T(8,128)S(1)}) custom-call(f32[1024,1024]{1,0:T(8,128)S(1)} %local2.1.refs_0_, bf16[1024,128]{1,0:T(8,128)(2,1)S(1)} %get-tuple-element.33.refs_0_.refs_1_, f32[2,8,1024]{2,1,0:T(8,128)S(1)} %get-tuple-element.36.refs_3_.refs_2_, ...), custom_call_target="tpu_custom_call", output_to_operand_aliasing={{0}: (0, {})} | custom-call | flops 1000 | bytes 1000000 | tf_op jit(solution)/shard_map/reach/pallas_call | solution.py:50
  28.8 1.3 %collective-permute-start.10 = (f32[256,128]{1,0:T(8,128)S(1)}, f32[256,128]{1,0:T(8,128)S(1)}, u32[]{:S(2)}, u32[]{:S(2)}) collective-permute-start(f32[256,128]{1,0:T(8,128)S(1)} %state.1.refs_6_.refs_0_.refs_9_), channel_id=1, source_target_pairs={{0,16},{8,24},{16,0},{24,8},{1,17},{9,25},{17,1},{25,9},{2,18},{10... | collective-permute-start | bytes 393224 | tf_op jit(solution)/shard_map/ppermute | solution.py:510
  30.0 0.6 %collective-permute-done.12.refs_5_ = f32[256,128]{1,0:T(8,128)S(1)} collective-permute-done((f32[256,128]{1,0:T(8,128)S(1)}, f32[256,128]{1,0:T(8,128)S(1)}, u32[]{:S(2)}, u32[]{:S(2)}) %collective-permute-start.12) | collective-permute-done | bytes 131104 | tf_op jit(solution)/shard_map/ppermute | solution.py:510
  31.3 0.9 %finish00.1.refs_11_ = bf16[1024,256]{1,0:T(8,128)(2,1)S(1)} custom-call(f32[1024,1024]{1,0:T(8,128)S(1)} %get-tuple-element.54.refs_0_, bf16[1024,128]{1,0:T(8,128)(2,1)S(1)} %get-tuple-element.33.refs_0_.refs_1_, f32[2,8,1024]{2,1,0:T(8,128)S(1)} %get-tuple-element.36.refs_3_.refs_2_, f32[8,8,1024]{2,1,0:T(8,128)S(1)} %get-tuple-element.38.refs_5_.refs_3_, ...), custom_call_target="tpu_custom_call" | custom-call | flops 20000000000 | bytes 1000000 | tf_op jit(solution)/shard_map/finish00/pallas_call | solution.py:486
  32.3 1.0 %collective-permute-done.13.refs_9_ = f32[256,128]{1,0:T(8,128)S(1)} collective-permute-done((f32[256,128]{1,0:T(8,128)S(1)}, f32[256,128]{1,0:T(8,128)S(1)}, u32[]{:S(2)}, u32[]{:S(2)}) %collective-permute-start.13) | collective-permute-done | bytes 131104 | tf_op jit(solution)/shard_map/ppermute | solution.py:510
  33.3 1.6 %finish10.1 = (bf16[1024,1024]{1,0:T(8,128)(2,1)}, bf16[1024,256]{1,0:T(8,128)(2,1)S(1)}) custom-call(f32[1024,1024]{1,0:T(8,128)S(1)} %get-tuple-element.54.refs_0_, bf16[1024,128]{1,0:T(8,128)(2,1)S(1)} %get-tuple-element.33.refs_0_.refs_1_, f32[2,8,1024]{2,1,0:T(8,128)S(1)} %get-tuple-element.36.refs_3_.refs_2_, ...), custom_call_target="tpu_custom_call" | custom-call | flops 1000 | bytes 1000000 | tf_op jit(solution)/shard_map/finish10/pallas_call | solution.py:486
  35.1 1.7 %finish01.1.refs_11_ = bf16[1024,1024]{1,0:T(8,128)(2,1)} custom-call(f32[1024,1024]{1,0:T(8,128)S(1)} %get-tuple-element.54.refs_0_, bf16[1024,128]{1,0:T(8,128)(2,1)S(1)} %get-tuple-element.33.refs_0_.refs_1_, f32[2,8,1024]{2,1,0:T(8,128)S(1)} %get-tuple-element.36.refs_3_.refs_2_, ...), custom_call_target="tpu_custom_call", output_to_operand_aliasing={{}: (12, {})} | custom-call | flops 20000000000 | bytes 1000000 | tf_op jit(solution)/shard_map/finish01/pallas_call | solution.py:486
  36.8 1.6 %finish11.1 = bf16[1024,1024]{1,0:T(8,128)(2,1)} custom-call(f32[1024,1024]{1,0:T(8,128)S(1)} %get-tuple-element.54.refs_0_, bf16[1024,128]{1,0:T(8,128)(2,1)S(1)} %get-tuple-element.33.refs_0_.refs_1_, f32[2,8,1024]{2,1,0:T(8,128)S(1)} %get-tuple-element.36.refs_3_.refs_2_, ...), custom_call_target="tpu_custom_call", output_to_operand_aliasing={{}: (11, {})} | custom-call | flops 2000000000 | bytes 1000000 | tf_op jit(solution)/shard_map/finish11/pallas_call | solution.py:486
  (33 shorter events, 1.8 us)
Async XLA Ops:
  2.6 2.1 %collective-permute-start = (f32[1032,128]{1,0:T(8,128)S(1)}, f32[1032,128]{1,0:T(8,128)S(1)}, u32[]{:S(2)}, u32[]{:S(2)}) collective-permute-start(f32[1032,128]{1,0:T(8,128)S(1)} %get-tuple-element.40.mine_ref), channel_id=1, source_target_pairs={{0,8},{8,0},{16,24},{24,16},{1,9},{9,1},{17,25},{25,17},{2,10},{10... | collective-permute-start | bytes 1585160 | tf_op jit(solution)/shard_map/ppermute | solution.py:510
  4.7 5.5 %collective-permute-start.1 = (f32[136,128]{1,0:T(8,128)S(1)}, f32[136,128]{1,0:T(8,128)S(1)}, u32[]{:S(2)}, u32[]{:S(2)}) collective-permute-start(f32[136,128]{1,0:T(8,128)S(1)} %get-tuple-element.43), channel_id=1, source_target_pairs={{0,16},{8,24},{16,0},{24,8},{1,17},{9,25},{17,1},{25,9},{2,18},{10... | collective-permute-start | bytes 208904 | tf_op jit(solution)/shard_map/ppermute | solution.py:510
  7.7 4.8 %collective-permute-start.3 = (f32[136,128]{1,0:T(8,128)S(1)}, f32[136,128]{1,0:T(8,128)S(1)}, u32[]{:S(2)}, u32[]{:S(2)}) collective-permute-start(f32[136,128]{1,0:T(8,128)S(1)} %get-tuple-element.47), channel_id=1, source_target_pairs={{0,16},{8,24},{16,0},{24,8},{1,17},{9,25},{17,1},{25,9},{2,18},{10... | collective-permute-start | bytes 208904 | tf_op jit(solution)/shard_map/ppermute | solution.py:510
  10.2 5.7 %collective-permute-start.2 = (f32[136,128]{1,0:T(8,128)S(1)}, f32[136,128]{1,0:T(8,128)S(1)}, u32[]{:S(2)}, u32[]{:S(2)}) collective-permute-start(f32[136,128]{1,0:T(8,128)S(1)} %merge11.1.refs_8_.refs_3_.refs_0_.refs_2_), channel_id=1, source_target_pairs={{0,1},{8,9},{16,17},{24,25},{1,0},{9,8},{17,16},{25,24},{2,3},{10,... | collective-permute-start | bytes 208904 | tf_op jit(solution)/shard_map/ppermute | solution.py:510
  12.5 5.1 %collective-permute-start.5 = (f32[136,128]{1,0:T(8,128)S(1)}, f32[136,128]{1,0:T(8,128)S(1)}, u32[]{:S(2)}, u32[]{:S(2)}) collective-permute-start(f32[136,128]{1,0:T(8,128)S(1)} %get-tuple-element.50.refs_0_.refs_2_), channel_id=1, source_target_pairs={{0,1},{8,9},{16,17},{24,25},{1,0},{9,8},{17,16},{25,24},{2,3},{10,... | collective-permute-start | bytes 208904 | tf_op jit(solution)/shard_map/ppermute | solution.py:510
  14.5 8.6 %collective-permute-start.7 = (f32[256,128]{1,0:T(8,128)S(1)}, f32[256,128]{1,0:T(8,128)S(1)}, u32[]{:S(2)}, u32[]{:S(2)}) collective-permute-start(f32[256,128]{1,0:T(8,128)S(1)} %rest.1), channel_id=1, source_target_pairs={{0,16},{8,24},{16,0},{24,8},{1,17},{9,25},{17,1},{25,9},{2,18},{10... | collective-permute-start | bytes 393224 | tf_op jit(solution)/shard_map/ppermute | solution.py:510
  16.0 4.4 %collective-permute-start.4 = (f32[136,128]{1,0:T(8,128)S(1)}, f32[136,128]{1,0:T(8,128)S(1)}, u32[]{:S(2)}, u32[]{:S(2)}) collective-permute-start(f32[136,128]{1,0:T(8,128)S(1)} %merge21.1.refs_3_.refs_0_.refs_2_), channel_id=1, source_target_pairs={{0,2},{8,10},{16,18},{24,26},{1,3},{9,11},{17,19},{25,27},{2,0},{1... | collective-permute-start | bytes 208904 | tf_op jit(solution)/shard_map/ppermute | solution.py:510
  17.7 5.4 %collective-permute-start.6 = (f32[136,128]{1,0:T(8,128)S(1)}, f32[136,128]{1,0:T(8,128)S(1)}, u32[]{:S(2)}, u32[]{:S(2)}) collective-permute-start(f32[136,128]{1,0:T(8,128)S(1)} %get-tuple-element.53.refs_0_), channel_id=1, source_target_pairs={{0,2},{8,10},{16,18},{24,26},{1,3},{9,11},{17,19},{25,27},{2,0},{1... | collective-permute-start | bytes 208904 | tf_op jit(solution)/shard_map/ppermute | solution.py:510
  18.6 11.4 %collective-permute-start.11 = (f32[256,128]{1,0:T(8,128)S(1)}, f32[256,128]{1,0:T(8,128)S(1)}, u32[]{:S(2)}, u32[]{:S(2)}) collective-permute-start(f32[256,128]{1,0:T(8,128)S(1)} %found2.1.refs_2_), channel_id=1, source_target_pairs={{0,16},{8,24},{16,0},{24,8},{1,17},{9,25},{17,1},{25,9},{2,18},{10... | collective-permute-start | bytes 393224 | tf_op jit(solution)/shard_map/ppermute | solution.py:510
  20.4 8.3 %collective-permute-start.9 = (f32[136,128]{1,0:T(8,128)S(1)}, f32[136,128]{1,0:T(8,128)S(1)}, u32[]{:S(2)}, u32[]{:S(2)}) collective-permute-start(f32[136,128]{1,0:T(8,128)S(1)} %merge31.1.refs_2_.refs_8_.refs_3_), channel_id=1, source_target_pairs={{0,4},{8,12},{16,20},{24,28},{1,5},{9,13},{17,21},{25,29},{2,6},{1... | collective-permute-start | bytes 208904 | tf_op jit(solution)/shard_map/ppermute | solution.py:510
  23.1 5.6 %collective-permute-start.8 = (f32[136,128]{1,0:T(8,128)S(1)}, f32[136,128]{1,0:T(8,128)S(1)}, u32[]{:S(2)}, u32[]{:S(2)}) collective-permute-start(f32[136,128]{1,0:T(8,128)S(1)} %get-tuple-element.57), channel_id=1, source_target_pairs={{0,4},{8,12},{16,20},{24,28},{1,5},{9,13},{17,21},{25,29},{2,6},{1... | collective-permute-start | bytes 208904 | tf_op jit(solution)/shard_map/ppermute | solution.py:510
  25.0 5.7 %collective-permute-start.12 = (f32[256,128]{1,0:T(8,128)S(1)}, f32[256,128]{1,0:T(8,128)S(1)}, u32[]{:S(2)}, u32[]{:S(2)}) collective-permute-start(f32[256,128]{1,0:T(8,128)S(1)} %found3.1.refs_9_.refs_4_), channel_id=1, source_target_pairs={{0,16},{8,24},{16,0},{24,8},{1,17},{9,25},{17,1},{25,9},{2,18},{10... | collective-permute-start | bytes 393224 | tf_op jit(solution)/shard_map/ppermute | solution.py:510
  28.8 6.1 %collective-permute-start.10 = (f32[256,128]{1,0:T(8,128)S(1)}, f32[256,128]{1,0:T(8,128)S(1)}, u32[]{:S(2)}, u32[]{:S(2)}) collective-permute-start(f32[256,128]{1,0:T(8,128)S(1)} %state.1.refs_6_.refs_0_.refs_9_), channel_id=1, source_target_pairs={{0,16},{8,24},{16,0},{24,8},{1,17},{9,25},{17,1},{25,9},{2,18},{10... | collective-permute-start | bytes 393224 | tf_op jit(solution)/shard_map/ppermute | solution.py:510
  30.7 2.5 %collective-permute-start.14 = (f32[1536,128]{1,0:T(8,128)S(1)}, f32[1536,128]{1,0:T(8,128)S(1)}, u32[]{:S(2)}, u32[]{:S(2)}) collective-permute-start(f32[1536,128]{1,0:T(8,128)S(1)} %near.1.refs_1_.refs_10_), channel_id=1, source_target_pairs={{0,8},{8,0},{16,24},{24,16},{1,9},{9,1},{17,25},{25,17},{2,10},{10... | collective-permute-start | bytes 2359304 | tf_op jit(solution)/shard_map/ppermute | solution.py:510
  30.8 2.5 %collective-permute-start.13 = (f32[256,128]{1,0:T(8,128)S(1)}, f32[256,128]{1,0:T(8,128)S(1)}, u32[]{:S(2)}, u32[]{:S(2)}) collective-permute-start(f32[256,128]{1,0:T(8,128)S(1)} %shared.1), channel_id=1, source_target_pairs={{0,8},{8,0},{16,24},{24,16},{1,9},{9,1},{17,25},{25,17},{2,10},{10... | collective-permute-start | bytes 393224 | tf_op jit(solution)/shard_map/ppermute | solution.py:510
  34.9 1.9 %collective-permute-start.15 = (f32[256,128]{1,0:T(8,128)S(1)}, f32[256,128]{1,0:T(8,128)S(1)}, u32[]{:S(2)}, u32[]{:S(2)}) collective-permute-start(f32[256,128]{1,0:T(8,128)S(1)} %beside.1.refs_9_), channel_id=1, source_target_pairs={{0,8},{8,0},{16,24},{24,16},{1,9},{9,1},{17,25},{25,17},{2,10},{10... | collective-permute-start | bytes 393224 | tf_op jit(solution)/shard_map/ppermute | solution.py:510

commit v17 on v16

--- a/solution.py
+++ b/solution.py
@@ -164,7 +164,7 @@
 
 
 def local_kernel(first, last, has_token, *refs):
-    q_ref, k_ref, v_ref, sums_ref, totals_ref, weight_ref, local_ref = refs[:7]
+    q_ref, k_ref, v_ref, sums_ref, totals_ref, weight_ref, local_ref, near_ref = refs[:8]
     if has_token:
         mixed_ref, done_ref = refs[-2:]
         done_ref[...] = jnp.zeros_like(done_ref)
@@ -179,6 +179,8 @@
     target = lax.broadcasted_iota(jnp.int32, (half, half), 1)
     causal = source <= target
     empty = jnp.zeros((half, half), jnp.bfloat16)
+    upper = jnp.where(bit_of(place(), 0) == 1, 1.0, 0.0)
+    near = near_ref[: heads * head_width].astype(jnp.bfloat16)
 
     for span in range(first, last):
         tokens = slice(span * SPAN, (span + 1) * SPAN)
@@ -210,6 +212,8 @@
                 scale = jnp.exp(since) * weight_ref[1 + bit, :, tokens]
                 levels.append((local_ref[offset + (span >> (bit + 1))].T, scale))
             offset += spans >> (bit + 1)
+        reach = jnp.exp(sums_ref[1, :, tokens]) * weight_ref[1 + local_bits, :, tokens] * upper
+        levels.append((near, reach))
         for head in range(heads):
             rows = slice(head * head_width, (head + 1) * head_width)
             mixing = jnp.concatenate(
@@ -229,14 +233,14 @@
 
 
 def mix_local(first, last, shared, mixed, tokens, has_token):
-    queries, keys, values, sums, totals, level_weight, local = shared
+    values = shared[2]
     rest = [] if mixed is None else [mixed]
     return call(
         functools.partial(local_kernel, first, last, has_token),
         f"local{first}",
         [*shared, *rest, *tokens],
         [(values.shape[::-1], jnp.float32), ((8, 128), jnp.float32)][: 1 + has_token],
-        aliases={7: 0} if rest else None,
+        aliases={8: 0} if rest else None,
     )
 
 
@@ -374,41 +378,6 @@
     return mixed
 
 
-def reach_kernel(quarters, first_level, bits, *refs):
-    mixed_ref, q_ref, sums_ref, weight_ref = refs[:4]
-    prefix_refs = refs[4 : 4 + len(bits)]
-    part_refs = refs[4 + len(bits) :]
-    out_ref, done_ref, scale_ref = refs[-3:]
-    done_ref[...] = jnp.zeros_like(done_ref)
-    heads = weight_ref.shape[1]
-    head_width = mixed_ref.shape[0] // heads
-    work = gather_work(quarters, part_refs, heads, head_width)
-    for span in range(q_ref.shape[0] // SPAN):
-        tokens = slice(span * SPAN, (span + 1) * SPAN)
-        queries = q_ref[tokens]
-        for level, (bit, prefix_ref) in enumerate(zip(bits, prefix_refs)):
-            scale_ref[level] = level_scale(
-                bit, first_level, prefix_ref, sums_ref, weight_ref, tokens
-            )
-        for head, states in work:
-            rows = pl.ds(pl.multiple_of(head * head_width, 128), head_width)
-            out_ref[rows, tokens] = add_found(
-                mixed_ref[rows, tokens], queries, head, states, scale_ref
-            )
-
-
-def add_levels(quarters, first_level, bits, shared, prefixes, parts):
-    mixed, _, _, level_weight = shared
-    return call(
-        functools.partial(reach_kernel, quarters, first_level, bits),
-        "reach",
-        [*shared, *prefixes, *parts],
-        [(mixed.shape, jnp.float32), ((8, 128), jnp.float32)],
-        [pltpu.VMEM((len(bits), level_weight.shape[1], SPAN), jnp.float32)],
-        aliases={0: 0},
-    )
-
-
 def finish_kernel(quarters, first_level, bits, stays, carried, *refs):
     mixed_ref, q_ref, sums_ref, weight_ref, gain_ref = refs[:5]
     prefix_refs = refs[5 : 5 + len(bits)]
@@ -431,7 +400,8 @@
 
     if carried is not None:
         index, far = carried
-        send(part_refs[index], far, slice(0, q_ref.shape[0]))
+        for start in range(0, q_ref.shape[0], SPAN):
+            send(part_refs[index], far, slice(start, start + SPAN))
     work = gather_work(quarters, part_refs, heads, head_width)
     gains = []
     for head, _ in work:
@@ -452,7 +422,8 @@
             columns = slice(at * head_width, (at + 1) * head_width)
             own_ref[tokens, columns] = normed.astype(jnp.bfloat16).T
         if not stays:
-            send(own_ref, quarters[0][0], tokens)
+            for start in range(tokens.start, tokens.stop, SPAN // 2):
+                send(own_ref, quarters[0][0], slice(start, start + SPAN // 2))
     for copy in copies:
         copy.wait()
 
@@ -491,7 +462,7 @@
         scratch_shapes=[
             pltpu.VMEM((8, 128) if stays else block, jnp.bfloat16),
             pltpu.VMEM((len(bits), heads, SPAN), jnp.float32),
-            pltpu.SemaphoreType.DMA((1 + tokens // SPAN,)),
+            pltpu.SemaphoreType.DMA((3 * tokens // SPAN,)),
         ],
         input_output_aliases=aliases,
         compiler_params=PARAMS,
@@ -528,9 +499,9 @@
     size = two // CUTS
     sides = [(core, side) for core in (0, 1) for side in (0, 1)]
     other = trade(message, 1)
-    zero = jnp.zeros((heads, 128), jnp.float32)
+    shared = (*shared, other)
     chunks, give, prefix = make_chip(message, other, heads, CUTS)
-    prefixes = [zero, prefix]
+    prefixes = [None, prefix]
     found, across = {}, {}
     mixed, at = None, 0
 
@@ -541,10 +512,10 @@
         found[bit] = [trade(chunk, 2**bit) for chunk in (give if bit == 1 else chunks)]
         stays = chunks if bit == 1 else stays
         waits = []
-        if bit < 3 or bit == last:
+        if at < spans:
             stop = spans if bit == last else at + 1
             begun = [*chunks[-1:], *([found[bit - 1]] if bit == last else [])]
-            mixed, *waits = mix_local(at, stop, shared, mixed, begun, bit < last)
+            mixed, *waits = mix_local(at, stop, shared, mixed, begun, True)
             at = stop
         if bit == 3:
             waits.append(rest)
@@ -560,16 +531,13 @@
             chunks = [merged[offset] for offset in range(CUTS)]
             newest = merged[order[-1]]
             prefixes += after
-            found[bit] = both(f"found{bit}", found[bit], chunks[-1:])
+            found[bit] = both(f"found{bit}", found[bit], (newest,))
             if bit > 1:
                 across[bit] = trade(found[bit], 2)
             else:
                 rest = trade(both("rest", stays, (newest,)), 2)
 
-    quarters = [((core, side), [(0, 0, None)]) for core, side in sides]
-    shared = (mixed, queries, sums, level_weight)
-    mixed, token = add_levels(quarters, first_level, [0], shared, [zero], [other])
-    state = both("state", found[last], (token,))
+    state = both("state", found[last], waits)
     beside = trade(state, 2)
     early = list(range(2, last))
     pieces = [(found[1], two), (rest, two)]

time: 38.5 us -> 38.9 us (1.010)
  waiting for transfers between devices: 4.87 us -> 7.59 us
  starting transfers between devices: 20.1 us -> 17.9 us
    ppermute x16, waiting for transfers between devices: 4.87 us -> 7.59 us  [trade(): return lax.ppermute(value, AXES, pairs)]
    ppermute x16, starting transfers between devices: 20.1 us -> 17.9 us  [trade(): return lax.ppermute(value, AXES, pairs)]
    pallas_call x20, Pallas kernels: 7.39 us -> 6.94 us  [call(): pl.pallas_call(kernel, in_specs=specs, out_specs=[HELD] * len(outputs), o...]
  transfers between devices with their start and end apart: 16 -> 16, of which waited for: 4 -> 6; matrix products, arithmetic and copies ran while one was open for 0% -> 0% of each run, Pallas kernels for 23% -> 22%
where the time goes in v17:
time: 38.9 us; the launch traced here: 38.7 us
  starting transfers between devices  17.9 us (46%)
  Pallas kernels  13 us (33%)
  waiting for transfers between devices  7.59 us (20%)
    ppermute x16, starting transfers between devices, trade(): return lax.ppermute(value, AXES, pairs)  17.9 us
    ppermute x16, waiting for transfers between devices, trade(): return lax.ppermute(value, AXES, pairs)  7.59 us
    pallas_call x20, Pallas kernels, call(): pl.pallas_call(kernel, in_specs=specs, out_specs=[HELD] * len(outputs), o...  6.94 us
    pallas_call x4, Pallas kernels, finish(): pl.pallas_call(functools.partial(finish_kernel, quarters, first_level, bi...  6.05 us
  transfers between devices with their start and end apart: 16, of which 6 were waited for; matrix products, arithmetic and copies ran while one was open for 0% of the time, Pallas kernels for 22%

profile of v17, /device:TPU:0, one launch (start us, length us, event | category | flops | bytes accessed | tf_op | source)
XLA Modules:
  0.0 38.7 jit_solution(3930343411721945238)
XLA Ops:
  0.0 2.6 %states.1 = (f32[1032,128]{1,0:T(8,128)S(1)}, bf16[3,128,1024]{2,1,0:T(8,128)(2,1)S(1)}, f32[2,8,1024]{2,1,0:T(8,128)S(1)}, f32[4,8,128]{2,1,0:T(8,128)S(1)}, bf...) custom-call(bf16[1024,128]{1,0:T(8,128)(2,1)} %refs_0_.1, ...), custom_call_target="tpu_custom_call" | custom-call | flops 2000000000 | bytes 1000000 | tf_op jit(solution)/shard_map/states/pallas_call | solution.py:50
  3.1 1.5 %collective-permute-done.other_ref.refs_7_ = f32[1032,128]{1,0:T(8,128)S(1)} collective-permute-done((f32[1032,128]{1,0:T(8,128)S(1)}, f32[1032,128]{1,0:T(8,128)S(1)}, u32[]{:S(2)}, u32[]{:S(2)}) %collective-permute-start) | collective-permute-done | bytes 528416 | tf_op jit(solution)/shard_map/ppermute | solution.py:481
  4.7 3.0 %collective-permute-start.1 = (f32[136,128]{1,0:T(8,128)S(1)}, f32[136,128]{1,0:T(8,128)S(1)}, u32[]{:S(2)}, u32[]{:S(2)}) collective-permute-start(f32[136,128]{1,0:T(8,128)S(1)} %get-tuple-element.45), channel_id=1, source_target_pairs={{0,16},{8,24},{16,0},{24,8},{1,17},{9,25},{17,1},{25,9},{2,18},{10... | collective-permute-start | bytes 208904 | tf_op jit(solution)/shard_map/ppermute | solution.py:481
  7.7 0.8 %local0.1 = (f32[1024,1024]{1,0:T(8,128)S(1)}, f32[8,128]{1,0:T(8,128)S(1)}) custom-call(bf16[1024,128]{1,0:T(8,128)(2,1)S(1)} %get-tuple-element.35.refs_0_.refs_1_, bf16[1024,128]{1,0:T(8,128)(2,1)S(1)} %get-tuple-element.36.refs_1_, bf16[1024,1024]{1,0:T(8,128)(2,1)S(1)} %get-tuple-element.37.refs_2_, ...), custom_call_target="tpu_custom_call" | custom-call | flops 2000000000 | bytes 1000000 | tf_op jit(solution)/shard_map/local0/pallas_call | solution.py:50
  8.6 1.6 %collective-permute-done.1.refs_1_ = f32[136,128]{1,0:T(8,128)S(1)} collective-permute-done((f32[136,128]{1,0:T(8,128)S(1)}, f32[136,128]{1,0:T(8,128)S(1)}, u32[]{:S(2)}, u32[]{:S(2)}) %collective-permute-start.1) | collective-permute-done | bytes 69664 | tf_op jit(solution)/shard_map/ppermute | solution.py:481
  10.2 2.2 %collective-permute-start.2 = (f32[136,128]{1,0:T(8,128)S(1)}, f32[136,128]{1,0:T(8,128)S(1)}, u32[]{:S(2)}, u32[]{:S(2)}) collective-permute-start(f32[136,128]{1,0:T(8,128)S(1)} %merge11.1.refs_9_.refs_3_.refs_0_), channel_id=1, source_target_pairs={{0,1},{8,9},{16,17},{24,25},{1,0},{9,8},{17,16},{25,24},{2,3},{10,... | collective-permute-start | bytes 208904 | tf_op jit(solution)/shard_map/ppermute | solution.py:481
  12.5 1.1 %collective-permute-start.5 = (f32[136,128]{1,0:T(8,128)S(1)}, f32[136,128]{1,0:T(8,128)S(1)}, u32[]{:S(2)}, u32[]{:S(2)}) collective-permute-start(f32[136,128]{1,0:T(8,128)S(1)} %get-tuple-element.53.refs_0_.refs_2_), channel_id=1, source_target_pairs={{0,1},{8,9},{16,17},{24,25},{1,0},{9,8},{17,16},{25,24},{2,3},{10,... | collective-permute-start | bytes 208904 | tf_op jit(solution)/shard_map/ppermute | solution.py:481
  13.6 1.5 %collective-permute-start.7 = (f32[256,128]{1,0:T(8,128)S(1)}, f32[256,128]{1,0:T(8,128)S(1)}, u32[]{:S(2)}, u32[]{:S(2)}) collective-permute-start(f32[256,128]{1,0:T(8,128)S(1)} %rest.1), channel_id=1, source_target_pairs={{0,16},{8,24},{16,0},{24,8},{1,17},{9,25},{17,1},{25,9},{2,18},{10... | collective-permute-start | bytes 393224 | tf_op jit(solution)/shard_map/ppermute | solution.py:481
  15.1 1.0 %local1.1 = (f32[1024,1024]{1,0:T(8,128)S(1)}, f32[8,128]{1,0:T(8,128)S(1)}) custom-call(bf16[1024,128]{1,0:T(8,128)(2,1)S(1)} %get-tuple-element.35.refs_0_.refs_1_, bf16[1024,128]{1,0:T(8,128)(2,1)S(1)} %get-tuple-element.36.refs_1_, bf16[1024,1024]{1,0:T(8,128)(2,1)S(1)} %get-tuple-element.37.refs_2_, ...), custom_call_target="tpu_custom_call", output_to_operand_aliasing={{0}: (8, {})} | custom-call | flops 2000000000 | bytes 1000000 | tf_op jit(solution)/shard_map/local1/pallas_call | solution.py:50
  16.1 1.6 %collective-permute-start.4 = (f32[136,128]{1,0:T(8,128)S(1)}, f32[136,128]{1,0:T(8,128)S(1)}, u32[]{:S(2)}, u32[]{:S(2)}) collective-permute-start(f32[136,128]{1,0:T(8,128)S(1)} %merge21.1.refs_9_.refs_3_.refs_0_), channel_id=1, source_target_pairs={{0,2},{8,10},{16,18},{24,26},{1,3},{9,11},{17,19},{25,27},{2,0},{1... | collective-permute-start | bytes 208904 | tf_op jit(solution)/shard_map/ppermute | solution.py:481
  17.8 0.8 %collective-permute-start.6 = (f32[136,128]{1,0:T(8,128)S(1)}, f32[136,128]{1,0:T(8,128)S(1)}, u32[]{:S(2)}, u32[]{:S(2)}) collective-permute-start(f32[136,128]{1,0:T(8,128)S(1)} %get-tuple-element.56.refs_0_.refs_2_), channel_id=1, source_target_pairs={{0,2},{8,10},{16,18},{24,26},{1,3},{9,11},{17,19},{25,27},{2,0},{1... | collective-permute-start | bytes 208904 | tf_op jit(solution)/shard_map/ppermute | solution.py:481
  18.6 1.8 %collective-permute-start.11 = (f32[256,128]{1,0:T(8,128)S(1)}, f32[256,128]{1,0:T(8,128)S(1)}, u32[]{:S(2)}, u32[]{:S(2)}) collective-permute-start(f32[256,128]{1,0:T(8,128)S(1)} %found2.1.refs_2_), channel_id=1, source_target_pairs={{0,16},{8,24},{16,0},{24,8},{1,17},{9,25},{17,1},{25,9},{2,18},{10... | collective-permute-start | bytes 393224 | tf_op jit(solution)/shard_map/ppermute | solution.py:481
  20.4 1.0 %local2.1 = (f32[1024,1024]{1,0:T(8,128)S(1)}, f32[8,128]{1,0:T(8,128)S(1)}) custom-call(bf16[1024,128]{1,0:T(8,128)(2,1)S(1)} %get-tuple-element.35.refs_0_.refs_1_, bf16[1024,128]{1,0:T(8,128)(2,1)S(1)} %get-tuple-element.36.refs_1_, bf16[1024,1024]{1,0:T(8,128)(2,1)S(1)} %get-tuple-element.37.refs_2_, ...), custom_call_target="tpu_custom_call", output_to_operand_aliasing={{0}: (8, {})} | custom-call | flops 1000 | bytes 1000000 | tf_op jit(solution)/shard_map/local2/pallas_call | solution.py:50
  21.4 2.7 %collective-permute-start.9 = (f32[136,128]{1,0:T(8,128)S(1)}, f32[136,128]{1,0:T(8,128)S(1)}, u32[]{:S(2)}, u32[]{:S(2)}) collective-permute-start(f32[136,128]{1,0:T(8,128)S(1)} %merge31.1.refs_3_.refs_9_), channel_id=1, source_target_pairs={{0,4},{8,12},{16,20},{24,28},{1,5},{9,13},{17,21},{25,29},{2,6},{1... | collective-permute-start | bytes 208904 | tf_op jit(solution)/shard_map/ppermute | solution.py:481
  24.1 1.0 %collective-permute-start.8 = (f32[136,128]{1,0:T(8,128)S(1)}, f32[136,128]{1,0:T(8,128)S(1)}, u32[]{:S(2)}, u32[]{:S(2)}) collective-permute-start(f32[136,128]{1,0:T(8,128)S(1)} %get-tuple-element.58.refs_2_), channel_id=1, source_target_pairs={{0,4},{8,12},{16,20},{24,28},{1,5},{9,13},{17,21},{25,29},{2,6},{1... | collective-permute-start | bytes 208904 | tf_op jit(solution)/shard_map/ppermute | solution.py:481
  25.1 1.0 %collective-permute-start.12 = (f32[256,128]{1,0:T(8,128)S(1)}, f32[256,128]{1,0:T(8,128)S(1)}, u32[]{:S(2)}, u32[]{:S(2)}) collective-permute-start(f32[256,128]{1,0:T(8,128)S(1)} %found3.1.refs_10_.refs_4_), channel_id=1, source_target_pairs={{0,16},{8,24},{16,0},{24,8},{1,17},{9,25},{17,1},{25,9},{2,18},{10... | collective-permute-start | bytes 393224 | tf_op jit(solution)/shard_map/ppermute | solution.py:481
  26.2 1.2 %local3.1 = (f32[1024,1024]{1,0:T(8,128)S(1)}, f32[8,128]{1,0:T(8,128)S(1)}) custom-call(bf16[1024,128]{1,0:T(8,128)(2,1)S(1)} %get-tuple-element.35.refs_0_.refs_1_, bf16[1024,128]{1,0:T(8,128)(2,1)S(1)} %get-tuple-element.36.refs_1_, bf16[1024,1024]{1,0:T(8,128)(2,1)S(1)} %get-tuple-element.37.refs_2_, ...), custom_call_target="tpu_custom_call", output_to_operand_aliasing={{0}: (8, {})} | custom-call | flops 2000000000 | bytes 1000000 | tf_op jit(solution)/shard_map/local3/pallas_call | solution.py:50
  27.4 2.8 %collective-permute-done.8.refs_0_ = f32[136,128]{1,0:T(8,128)S(1)} collective-permute-done((f32[136,128]{1,0:T(8,128)S(1)}, f32[136,128]{1,0:T(8,128)S(1)}, u32[]{:S(2)}, u32[]{:S(2)}) %collective-permute-start.8) | collective-permute-done | bytes 69664 | tf_op jit(solution)/shard_map/ppermute | solution.py:481
  31.1 1.0 %finish00.1.refs_11_ = bf16[1024,256]{1,0:T(8,128)(2,1)S(1)} custom-call(f32[1024,1024]{1,0:T(8,128)S(1)} %get-tuple-element.59.refs_0_, bf16[1024,128]{1,0:T(8,128)(2,1)S(1)} %get-tuple-element.35.refs_0_.refs_1_, f32[2,8,1024]{2,1,0:T(8,128)S(1)} %get-tuple-element.38.refs_3_.refs_2_, f32[8,8,1024]{2,1,0:T(8,128)S(1)} %get-tuple-element.40.refs_5_.refs_3_, ...), custom_call_target="tpu_custom_call" | custom-call | flops 20000000000 | bytes 1000000 | tf_op jit(solution)/shard_map/finish00/pallas_call | solution.py:457
  32.1 0.9 %collective-permute-done.13.refs_9_ = f32[256,128]{1,0:T(8,128)S(1)} collective-permute-done((f32[256,128]{1,0:T(8,128)S(1)}, f32[256,128]{1,0:T(8,128)S(1)}, u32[]{:S(2)}, u32[]{:S(2)}) %collective-permute-start.13) | collective-permute-done | bytes 131104 | tf_op jit(solution)/shard_map/ppermute | solution.py:481
  33.0 1.6 %finish10.1 = (bf16[1024,1024]{1,0:T(8,128)(2,1)}, bf16[1024,256]{1,0:T(8,128)(2,1)S(1)}) custom-call(f32[1024,1024]{1,0:T(8,128)S(1)} %get-tuple-element.59.refs_0_, bf16[1024,128]{1,0:T(8,128)(2,1)S(1)} %get-tuple-element.35.refs_0_.refs_1_, f32[2,8,1024]{2,1,0:T(8,128)S(1)} %get-tuple-element.38.refs_3_.refs_2_, ...), custom_call_target="tpu_custom_call" | custom-call | flops 1000 | bytes 1000000 | tf_op jit(solution)/shard_map/finish10/pallas_call | solution.py:457
  34.7 0.5 %collective-permute-done.10.refs_0_ = f32[256,128]{1,0:T(8,128)S(1)} collective-permute-done((f32[256,128]{1,0:T(8,128)S(1)}, f32[256,128]{1,0:T(8,128)S(1)}, u32[]{:S(2)}, u32[]{:S(2)}) %collective-permute-start.10) | collective-permute-done | bytes 131104 | tf_op jit(solution)/shard_map/ppermute | solution.py:481
  35.3 1.7 %finish01.1.refs_11_ = bf16[1024,1024]{1,0:T(8,128)(2,1)} custom-call(f32[1024,1024]{1,0:T(8,128)S(1)} %get-tuple-element.59.refs_0_, bf16[1024,128]{1,0:T(8,128)(2,1)S(1)} %get-tuple-element.35.refs_0_.refs_1_, f32[2,8,1024]{2,1,0:T(8,128)S(1)} %get-tuple-element.38.refs_3_.refs_2_, ...), custom_call_target="tpu_custom_call", output_to_operand_aliasing={{}: (12, {})} | custom-call | flops 20000000000 | bytes 1000000 | tf_op jit(solution)/shard_map/finish01/pallas_call | solution.py:457
  37.0 1.6 %finish11.1 = bf16[1024,1024]{1,0:T(8,128)(2,1)} custom-call(f32[1024,1024]{1,0:T(8,128)S(1)} %get-tuple-element.59.refs_0_, bf16[1024,128]{1,0:T(8,128)(2,1)S(1)} %get-tuple-element.35.refs_0_.refs_1_, f32[2,8,1024]{2,1,0:T(8,128)S(1)} %get-tuple-element.38.refs_3_.refs_2_, ...), custom_call_target="tpu_custom_call", output_to_operand_aliasing={{}: (11, {})} | custom-call | flops 2000000000 | bytes 1000000 | tf_op jit(solution)/shard_map/finish11/pallas_call | solution.py:457
  (32 shorter events, 1.9 us)
Async XLA Ops:
  2.6 2.1 %collective-permute-start = (f32[1032,128]{1,0:T(8,128)S(1)}, f32[1032,128]{1,0:T(8,128)S(1)}, u32[]{:S(2)}, u32[]{:S(2)}) collective-permute-start(f32[1032,128]{1,0:T(8,128)S(1)} %get-tuple-element.42.mine_ref), channel_id=1, source_target_pairs={{0,8},{8,0},{16,24},{24,16},{1,9},{9,1},{17,25},{25,17},{2,10},{10... | collective-permute-start | bytes 1585160 | tf_op jit(solution)/shard_map/ppermute | solution.py:481
  4.7 5.5 %collective-permute-start.1 = (f32[136,128]{1,0:T(8,128)S(1)}, f32[136,128]{1,0:T(8,128)S(1)}, u32[]{:S(2)}, u32[]{:S(2)}) collective-permute-start(f32[136,128]{1,0:T(8,128)S(1)} %get-tuple-element.45), channel_id=1, source_target_pairs={{0,16},{8,24},{16,0},{24,8},{1,17},{9,25},{17,1},{25,9},{2,18},{10... | collective-permute-start | bytes 208904 | tf_op jit(solution)/shard_map/ppermute | solution.py:481
  7.7 4.8 %collective-permute-start.3 = (f32[136,128]{1,0:T(8,128)S(1)}, f32[136,128]{1,0:T(8,128)S(1)}, u32[]{:S(2)}, u32[]{:S(2)}) collective-permute-start(f32[136,128]{1,0:T(8,128)S(1)} %get-tuple-element.49), channel_id=1, source_target_pairs={{0,16},{8,24},{16,0},{24,8},{1,17},{9,25},{17,1},{25,9},{2,18},{10... | collective-permute-start | bytes 208904 | tf_op jit(solution)/shard_map/ppermute | solution.py:481
  10.2 5.8 %collective-permute-start.2 = (f32[136,128]{1,0:T(8,128)S(1)}, f32[136,128]{1,0:T(8,128)S(1)}, u32[]{:S(2)}, u32[]{:S(2)}) collective-permute-start(f32[136,128]{1,0:T(8,128)S(1)} %merge11.1.refs_9_.refs_3_.refs_0_), channel_id=1, source_target_pairs={{0,1},{8,9},{16,17},{24,25},{1,0},{9,8},{17,16},{25,24},{2,3},{10,... | collective-permute-start | bytes 208904 | tf_op jit(solution)/shard_map/ppermute | solution.py:481
  12.5 5.3 %collective-permute-start.5 = (f32[136,128]{1,0:T(8,128)S(1)}, f32[136,128]{1,0:T(8,128)S(1)}, u32[]{:S(2)}, u32[]{:S(2)}) collective-permute-start(f32[136,128]{1,0:T(8,128)S(1)} %get-tuple-element.53.refs_0_.refs_2_), channel_id=1, source_target_pairs={{0,1},{8,9},{16,17},{24,25},{1,0},{9,8},{17,16},{25,24},{2,3},{10,... | collective-permute-start | bytes 208904 | tf_op jit(solution)/shard_map/ppermute | solution.py:481
  13.6 10.5 %collective-permute-start.7 = (f32[256,128]{1,0:T(8,128)S(1)}, f32[256,128]{1,0:T(8,128)S(1)}, u32[]{:S(2)}, u32[]{:S(2)}) collective-permute-start(f32[256,128]{1,0:T(8,128)S(1)} %rest.1), channel_id=1, source_target_pairs={{0,16},{8,24},{16,0},{24,8},{1,17},{9,25},{17,1},{25,9},{2,18},{10... | collective-permute-start | bytes 393224 | tf_op jit(solution)/shard_map/ppermute | solution.py:481
  16.1 5.3 %collective-permute-start.4 = (f32[136,128]{1,0:T(8,128)S(1)}, f32[136,128]{1,0:T(8,128)S(1)}, u32[]{:S(2)}, u32[]{:S(2)}) collective-permute-start(f32[136,128]{1,0:T(8,128)S(1)} %merge21.1.refs_9_.refs_3_.refs_0_), channel_id=1, source_target_pairs={{0,2},{8,10},{16,18},{24,26},{1,3},{9,11},{17,19},{25,27},{2,0},{1... | collective-permute-start | bytes 208904 | tf_op jit(solution)/shard_map/ppermute | solution.py:481
  17.8 6.3 %collective-permute-start.6 = (f32[136,128]{1,0:T(8,128)S(1)}, f32[136,128]{1,0:T(8,128)S(1)}, u32[]{:S(2)}, u32[]{:S(2)}) collective-permute-start(f32[136,128]{1,0:T(8,128)S(1)} %get-tuple-element.56.refs_0_.refs_2_), channel_id=1, source_target_pairs={{0,2},{8,10},{16,18},{24,26},{1,3},{9,11},{17,19},{25,27},{2,0},{1... | collective-permute-start | bytes 208904 | tf_op jit(solution)/shard_map/ppermute | solution.py:481
  18.6 11.7 %collective-permute-start.11 = (f32[256,128]{1,0:T(8,128)S(1)}, f32[256,128]{1,0:T(8,128)S(1)}, u32[]{:S(2)}, u32[]{:S(2)}) collective-permute-start(f32[256,128]{1,0:T(8,128)S(1)} %found2.1.refs_2_), channel_id=1, source_target_pairs={{0,16},{8,24},{16,0},{24,8},{1,17},{9,25},{17,1},{25,9},{2,18},{10... | collective-permute-start | bytes 393224 | tf_op jit(solution)/shard_map/ppermute | solution.py:481
  21.4 8.7 %collective-permute-start.9 = (f32[136,128]{1,0:T(8,128)S(1)}, f32[136,128]{1,0:T(8,128)S(1)}, u32[]{:S(2)}, u32[]{:S(2)}) collective-permute-start(f32[136,128]{1,0:T(8,128)S(1)} %merge31.1.refs_3_.refs_9_), channel_id=1, source_target_pairs={{0,4},{8,12},{16,20},{24,28},{1,5},{9,13},{17,21},{25,29},{2,6},{1... | collective-permute-start | bytes 208904 | tf_op jit(solution)/shard_map/ppermute | solution.py:481
  24.1 6.0 %collective-permute-start.8 = (f32[136,128]{1,0:T(8,128)S(1)}, f32[136,128]{1,0:T(8,128)S(1)}, u32[]{:S(2)}, u32[]{:S(2)}) collective-permute-start(f32[136,128]{1,0:T(8,128)S(1)} %get-tuple-element.58.refs_2_), channel_id=1, source_target_pairs={{0,4},{8,12},{16,20},{24,28},{1,5},{9,13},{17,21},{25,29},{2,6},{1... | collective-permute-start | bytes 208904 | tf_op jit(solution)/shard_map/ppermute | solution.py:481
  25.1 5.3 %collective-permute-start.12 = (f32[256,128]{1,0:T(8,128)S(1)}, f32[256,128]{1,0:T(8,128)S(1)}, u32[]{:S(2)}, u32[]{:S(2)}) collective-permute-start(f32[256,128]{1,0:T(8,128)S(1)} %found3.1.refs_10_.refs_4_), channel_id=1, source_target_pairs={{0,16},{8,24},{16,0},{24,8},{1,17},{9,25},{17,1},{25,9},{2,18},{10... | collective-permute-start | bytes 393224 | tf_op jit(solution)/shard_map/ppermute | solution.py:481
  30.2 5.0 %collective-permute-start.10 = (f32[256,128]{1,0:T(8,128)S(1)}, f32[256,128]{1,0:T(8,128)S(1)}, u32[]{:S(2)}, u32[]{:S(2)}) collective-permute-start(f32[256,128]{1,0:T(8,128)S(1)} %state.1.refs_6_.refs_0_.refs_9_), channel_id=1, source_target_pairs={{0,16},{8,24},{16,0},{24,8},{1,17},{9,25},{17,1},{25,9},{2,18},{10... | collective-permute-start | bytes 393224 | tf_op jit(solution)/shard_map/ppermute | solution.py:481
  30.5 2.5 %collective-permute-start.14 = (f32[1536,128]{1,0:T(8,128)S(1)}, f32[1536,128]{1,0:T(8,128)S(1)}, u32[]{:S(2)}, u32[]{:S(2)}) collective-permute-start(f32[1536,128]{1,0:T(8,128)S(1)} %near.1.refs_1_.refs_10_), channel_id=1, source_target_pairs={{0,8},{8,0},{16,24},{24,16},{1,9},{9,1},{17,25},{25,17},{2,10},{10... | collective-permute-start | bytes 2359304 | tf_op jit(solution)/shard_map/ppermute | solution.py:481
  30.6 2.5 %collective-permute-start.13 = (f32[256,128]{1,0:T(8,128)S(1)}, f32[256,128]{1,0:T(8,128)S(1)}, u32[]{:S(2)}, u32[]{:S(2)}) collective-permute-start(f32[256,128]{1,0:T(8,128)S(1)} %shared.1), channel_id=1, source_target_pairs={{0,8},{8,0},{16,24},{24,16},{1,9},{9,1},{17,25},{25,17},{2,10},{10... | collective-permute-start | bytes 393224 | tf_op jit(solution)/shard_map/ppermute | solution.py:481
  35.2 1.8 %collective-permute-start.15 = (f32[256,128]{1,0:T(8,128)S(1)}, f32[256,128]{1,0:T(8,128)S(1)}, u32[]{:S(2)}, u32[]{:S(2)}) collective-permute-start(f32[256,128]{1,0:T(8,128)S(1)} %beside.1.refs_9_), channel_id=1, source_target_pairs={{0,8},{8,0},{16,24},{24,16},{1,9},{9,1},{17,25},{25,17},{2,10},{10... | collective-permute-start | bytes 393224 | tf_op jit(solution)/shard_map/ppermute | solution.py:481

commit v18 on v17

--- a/solution.py
+++ b/solution.py
@@ -471,13 +471,17 @@
     )(*inputs)
 
 
-def trade(value, mask):
+def trade(value, mask, sends=lambda source: True):
     wide, narrow = lax.axis_size("wide"), lax.axis_size("narrow")
 
     def ranked(index):
         return index % narrow * wide + index // narrow
 
-    pairs = [(ranked(source), ranked(source ^ mask)) for source in range(wide * narrow)]
+    pairs = [
+        (ranked(source), ranked(source ^ mask))
+        for source in range(wide * narrow)
+        if sends(source)
+    ]
     return lax.ppermute(value, AXES, pairs)
 
 
@@ -509,7 +513,9 @@
         return pack(name, [(state, size) for state in messages], tokens)
 
     for bit in range(1, bits):
-        found[bit] = [trade(chunk, 2**bit) for chunk in (give if bit == 1 else chunks)]
+        lower = lambda source: bit < last or source >> last & 1 == 0
+        sent = give if bit == 1 else chunks
+        found[bit] = [trade(chunk, 2**bit, lower) for chunk in sent]
         stays = chunks if bit == 1 else stays
         waits = []
         if at < spans:
@@ -556,15 +562,17 @@
     quarters = {(core, side): [(0, 0, 0), *states_of(side, 1, 1)] for core, side in sides}
     state_far = trade(pack("shared", [(state, two)], (near,)), 1)
     (block,) = finish([((0, 0), quarters[0, 0])], *every, [state, near], None, True, None)
-    out, block = finish(
-        [((1, 0), quarters[1, 0])], *every, [state_far, far, block], None, True, (2, (0, 0))
-    )
-    beside = pack("beside", [(beside, two)], (block,))
+    (block_far,) = finish(
+        [((1, 0), quarters[1, 0])], *every, [state_far, far, block], None, True, None
+    )
+    beside = pack("beside", [(beside, two)], (block_far,))
     (out,) = finish(
-        [((0, 1), quarters[0, 1])], *every, [beside, near, block], out, False, (2, (1, 0))
+        [((0, 1), quarters[0, 1])], *every, [beside, near, block], None, False, (2, (0, 0))
     )
     beside_far = trade(beside, 1)
-    return finish([((1, 1), quarters[1, 1])], *every, [beside_far, far], out, False, None)[0]
+    return finish(
+        [((1, 1), quarters[1, 1])], *every, [beside_far, far, block_far], out, False, (2, (1, 0))
+    )[0]
 
 
 def solution(mesh):

time: 38.9 us -> 39.9 us (1.026)
  starting transfers between devices: 17.9 us -> 21 us
  waiting for transfers between devices: 7.59 us -> 6.03 us
  Pallas kernels: 13 us -> 12.5 us
    ppermute x16, starting transfers between devices: 17.9 us -> 21 us  [trade(): return lax.ppermute(value, AXES, pairs)]
    ppermute x16, waiting for transfers between devices: 7.59 us -> 6.03 us  [trade(): return lax.ppermute(value, AXES, pairs)]
    pallas_call x4, Pallas kernels: 6.05 us -> 5.52 us  [finish(): pl.pallas_call(functools.partial(finish_kernel, quarters, first_level, bi...]
  transfers between devices with their start and end apart: 16 -> 16, of which waited for: 6 -> 5; matrix products, arithmetic and copies ran while one was open for 0% -> 0% of each run, Pallas kernels for 22% -> 20%
where the time goes in v18:
time: 39.9 us; the launch traced here: 39.7 us
  starting transfers between devices  21 us (53%)
  Pallas kernels  12.5 us (31%)
  waiting for transfers between devices  6.03 us (15%)
    ppermute x16, starting transfers between devices, trade(): return lax.ppermute(value, AXES, pairs)  21 us
    pallas_call x20, Pallas kernels, call(): pl.pallas_call(kernel, in_specs=specs, out_specs=[HELD] * len(outputs), o...  6.95 us
    ppermute x16, waiting for transfers between devices, trade(): return lax.ppermute(value, AXES, pairs)  6.03 us
    pallas_call x4, Pallas kernels, finish(): pl.pallas_call(functools.partial(finish_kernel, quarters, first_level, bi...  5.52 us
  transfers between devices with their start and end apart: 16, of which 5 were waited for; matrix products, arithmetic and copies ran while one was open for 0% of the time, Pallas kernels for 20%

profile of v18, /device:TPU:0, one launch (start us, length us, event | category | flops | bytes accessed | tf_op | source)
XLA Modules:
  0.0 39.7 jit_solution(2698231003651660130)
XLA Ops:
  0.0 2.6 %states.1 = (f32[1032,128]{1,0:T(8,128)S(1)}, bf16[3,128,1024]{2,1,0:T(8,128)(2,1)S(1)}, f32[2,8,1024]{2,1,0:T(8,128)S(1)}, f32[4,8,128]{2,1,0:T(8,128)S(1)}, bf...) custom-call(bf16[1024,128]{1,0:T(8,128)(2,1)} %refs_0_.1, ...), custom_call_target="tpu_custom_call" | custom-call | flops 2000000000 | bytes 1000000 | tf_op jit(solution)/shard_map/states/pallas_call | solution.py:50
  2.6 0.5 %collective-permute-start = (f32[1032,128]{1,0:T(8,128)S(1)}, f32[1032,128]{1,0:T(8,128)S(1)}, u32[]{:S(2)}, u32[]{:S(2)}) collective-permute-start(f32[1032,128]{1,0:T(8,128)S(1)} %get-tuple-element.40.mine_ref), channel_id=1, source_target_pairs={{0,8},{8,0},{16,24},{24,16},{1,9},{9,1},{17,25},{25,17},{2,10},{10... | collective-permute-start | bytes 1585160 | tf_op jit(solution)/shard_map/ppermute | solution.py:485
  3.1 1.5 %collective-permute-done.other_ref.refs_7_ = f32[1032,128]{1,0:T(8,128)S(1)} collective-permute-done((f32[1032,128]{1,0:T(8,128)S(1)}, f32[1032,128]{1,0:T(8,128)S(1)}, u32[]{:S(2)}, u32[]{:S(2)}) %collective-permute-start) | collective-permute-done | bytes 528416 | tf_op jit(solution)/shard_map/ppermute | solution.py:485
  4.7 3.0 %collective-permute-start.1 = (f32[136,128]{1,0:T(8,128)S(1)}, f32[136,128]{1,0:T(8,128)S(1)}, u32[]{:S(2)}, u32[]{:S(2)}) collective-permute-start(f32[136,128]{1,0:T(8,128)S(1)} %get-tuple-element.43), channel_id=1, source_target_pairs={{0,16},{8,24},{16,0},{24,8},{1,17},{9,25},{17,1},{25,9},{2,18},{10... | collective-permute-start | bytes 208904 | tf_op jit(solution)/shard_map/ppermute | solution.py:485
  7.7 0.8 %local0.1 = (f32[1024,1024]{1,0:T(8,128)S(1)}, f32[8,128]{1,0:T(8,128)S(1)}) custom-call(bf16[1024,128]{1,0:T(8,128)(2,1)S(1)} %get-tuple-element.33.refs_0_.refs_1_, bf16[1024,128]{1,0:T(8,128)(2,1)S(1)} %get-tuple-element.34.refs_1_, bf16[1024,1024]{1,0:T(8,128)(2,1)S(1)} %get-tuple-element.35.refs_2_, ...), custom_call_target="tpu_custom_call" | custom-call | flops 2000000000 | bytes 1000000 | tf_op jit(solution)/shard_map/local0/pallas_call | solution.py:50
  8.6 1.6 %collective-permute-done.1.refs_1_ = f32[136,128]{1,0:T(8,128)S(1)} collective-permute-done((f32[136,128]{1,0:T(8,128)S(1)}, f32[136,128]{1,0:T(8,128)S(1)}, u32[]{:S(2)}, u32[]{:S(2)}) %collective-permute-start.1) | collective-permute-done | bytes 69664 | tf_op jit(solution)/shard_map/ppermute | solution.py:485
  10.2 2.2 %collective-permute-start.2 = (f32[136,128]{1,0:T(8,128)S(1)}, f32[136,128]{1,0:T(8,128)S(1)}, u32[]{:S(2)}, u32[]{:S(2)}) collective-permute-start(f32[136,128]{1,0:T(8,128)S(1)} %merge11.1.refs_9_.refs_3_.refs_0_), channel_id=1, source_target_pairs={{0,1},{8,9},{16,17},{24,25},{1,0},{9,8},{17,16},{25,24},{2,3},{10,... | collective-permute-start | bytes 208904 | tf_op jit(solution)/shard_map/ppermute | solution.py:485
  12.5 1.1 %collective-permute-start.5 = (f32[136,128]{1,0:T(8,128)S(1)}, f32[136,128]{1,0:T(8,128)S(1)}, u32[]{:S(2)}, u32[]{:S(2)}) collective-permute-start(f32[136,128]{1,0:T(8,128)S(1)} %get-tuple-element.51.refs_0_.refs_2_), channel_id=1, source_target_pairs={{0,1},{8,9},{16,17},{24,25},{1,0},{9,8},{17,16},{25,24},{2,3},{10,... | collective-permute-start | bytes 208904 | tf_op jit(solution)/shard_map/ppermute | solution.py:485
  13.6 1.5 %collective-permute-start.7 = (f32[256,128]{1,0:T(8,128)S(1)}, f32[256,128]{1,0:T(8,128)S(1)}, u32[]{:S(2)}, u32[]{:S(2)}) collective-permute-start(f32[256,128]{1,0:T(8,128)S(1)} %rest.1), channel_id=1, source_target_pairs={{0,16},{8,24},{16,0},{24,8},{1,17},{9,25},{17,1},{25,9},{2,18},{10... | collective-permute-start | bytes 393224 | tf_op jit(solution)/shard_map/ppermute | solution.py:485
  15.1 1.0 %local1.1 = (f32[1024,1024]{1,0:T(8,128)S(1)}, f32[8,128]{1,0:T(8,128)S(1)}) custom-call(bf16[1024,128]{1,0:T(8,128)(2,1)S(1)} %get-tuple-element.33.refs_0_.refs_1_, bf16[1024,128]{1,0:T(8,128)(2,1)S(1)} %get-tuple-element.34.refs_1_, bf16[1024,1024]{1,0:T(8,128)(2,1)S(1)} %get-tuple-element.35.refs_2_, ...), custom_call_target="tpu_custom_call", output_to_operand_aliasing={{0}: (8, {})} | custom-call | flops 2000000000 | bytes 1000000 | tf_op jit(solution)/shard_map/local1/pallas_call | solution.py:50
  16.1 1.6 %collective-permute-start.4 = (f32[136,128]{1,0:T(8,128)S(1)}, f32[136,128]{1,0:T(8,128)S(1)}, u32[]{:S(2)}, u32[]{:S(2)}) collective-permute-start(f32[136,128]{1,0:T(8,128)S(1)} %merge21.1.refs_9_.refs_3_.refs_0_), channel_id=1, source_target_pairs={{0,2},{8,10},{16,18},{24,26},{1,3},{9,11},{17,19},{25,27},{2,0},{1... | collective-permute-start | bytes 208904 | tf_op jit(solution)/shard_map/ppermute | solution.py:485
  17.8 0.8 %collective-permute-start.6 = (f32[136,128]{1,0:T(8,128)S(1)}, f32[136,128]{1,0:T(8,128)S(1)}, u32[]{:S(2)}, u32[]{:S(2)}) collective-permute-start(f32[136,128]{1,0:T(8,128)S(1)} %get-tuple-element.54.refs_0_.refs_2_), channel_id=1, source_target_pairs={{0,2},{8,10},{16,18},{24,26},{1,3},{9,11},{17,19},{25,27},{2,0},{1... | collective-permute-start | bytes 208904 | tf_op jit(solution)/shard_map/ppermute | solution.py:485
  18.6 1.8 %collective-permute-start.11 = (f32[256,128]{1,0:T(8,128)S(1)}, f32[256,128]{1,0:T(8,128)S(1)}, u32[]{:S(2)}, u32[]{:S(2)}) collective-permute-start(f32[256,128]{1,0:T(8,128)S(1)} %found2.1.refs_2_), channel_id=1, source_target_pairs={{0,16},{8,24},{16,0},{24,8},{1,17},{9,25},{17,1},{25,9},{2,18},{10... | collective-permute-start | bytes 393224 | tf_op jit(solution)/shard_map/ppermute | solution.py:485
  20.4 1.0 %local2.1 = (f32[1024,1024]{1,0:T(8,128)S(1)}, f32[8,128]{1,0:T(8,128)S(1)}) custom-call(bf16[1024,128]{1,0:T(8,128)(2,1)S(1)} %get-tuple-element.33.refs_0_.refs_1_, bf16[1024,128]{1,0:T(8,128)(2,1)S(1)} %get-tuple-element.34.refs_1_, bf16[1024,1024]{1,0:T(8,128)(2,1)S(1)} %get-tuple-element.35.refs_2_, ...), custom_call_target="tpu_custom_call", output_to_operand_aliasing={{0}: (8, {})} | custom-call | flops 1000 | bytes 1000000 | tf_op jit(solution)/shard_map/local2/pallas_call | solution.py:50
  21.4 4.5 %collective-permute-start.9 = (f32[136,128]{1,0:T(8,128)S(1)}, f32[136,128]{1,0:T(8,128)S(1)}, u32[]{:S(2)}, u32[]{:S(2)}) collective-permute-start(f32[136,128]{1,0:T(8,128)S(1)} %merge31.1.refs_3_.refs_9_), channel_id=1, source_target_pairs={{0,4},{8,12},{16,20},{24,28},{1,5},{9,13},{17,21},{25,29},{2,6},{1... | collective-permute-start | bytes 208904 | tf_op jit(solution)/shard_map/ppermute | solution.py:485
  26.0 1.3 %collective-permute-start.8 = (f32[136,128]{1,0:T(8,128)S(1)}, f32[136,128]{1,0:T(8,128)S(1)}, u32[]{:S(2)}, u32[]{:S(2)}) collective-permute-start(f32[136,128]{1,0:T(8,128)S(1)} %get-tuple-element.56.refs_2_), channel_id=1, source_target_pairs={{0,4},{8,12},{16,20},{24,28},{1,5},{9,13},{17,21},{25,29},{2,6},{1... | collective-permute-start | bytes 208904 | tf_op jit(solution)/shard_map/ppermute | solution.py:485
  27.7 1.2 %local3.1 = (f32[1024,1024]{1,0:T(8,128)S(1)}, f32[8,128]{1,0:T(8,128)S(1)}) custom-call(bf16[1024,128]{1,0:T(8,128)(2,1)S(1)} %get-tuple-element.33.refs_0_.refs_1_, bf16[1024,128]{1,0:T(8,128)(2,1)S(1)} %get-tuple-element.34.refs_1_, bf16[1024,1024]{1,0:T(8,128)(2,1)S(1)} %get-tuple-element.35.refs_2_, ...), custom_call_target="tpu_custom_call", output_to_operand_aliasing={{0}: (8, {})} | custom-call | flops 2000000000 | bytes 1000000 | tf_op jit(solution)/shard_map/local3/pallas_call | solution.py:50
  29.3 1.5 %collective-permute-start.10 = (f32[256,128]{1,0:T(8,128)S(1)}, f32[256,128]{1,0:T(8,128)S(1)}, u32[]{:S(2)}, u32[]{:S(2)}) collective-permute-start(f32[256,128]{1,0:T(8,128)S(1)} %state.1.refs_6_.refs_0_.refs_9_), channel_id=1, source_target_pairs={{0,16},{8,24},{16,0},{24,8},{1,17},{9,25},{17,1},{25,9},{2,18},{10... | collective-permute-start | bytes 393224 | tf_op jit(solution)/shard_map/ppermute | solution.py:485
  30.7 1.6 %collective-permute-done.12.refs_5_ = f32[256,128]{1,0:T(8,128)S(1)} collective-permute-done((f32[256,128]{1,0:T(8,128)S(1)}, f32[256,128]{1,0:T(8,128)S(1)}, u32[]{:S(2)}, u32[]{:S(2)}) %collective-permute-start.12) | collective-permute-done | bytes 131104 | tf_op jit(solution)/shard_map/ppermute | solution.py:485
  33.0 1.0 %finish00.1.refs_11_ = bf16[1024,256]{1,0:T(8,128)(2,1)S(1)} custom-call(f32[1024,1024]{1,0:T(8,128)S(1)} %get-tuple-element.57.refs_0_, bf16[1024,128]{1,0:T(8,128)(2,1)S(1)} %get-tuple-element.33.refs_0_.refs_1_, f32[2,8,1024]{2,1,0:T(8,128)S(1)} %get-tuple-element.36.refs_3_.refs_2_, f32[8,8,1024]{2,1,0:T(8,128)S(1)} %get-tuple-element.38.refs_5_.refs_3_, ...), custom_call_target="tpu_custom_call" | custom-call | flops 20000000000 | bytes 1000000 | tf_op jit(solution)/shard_map/finish00/pallas_call | solution.py:457
  34.1 0.9 %collective-permute-done.13.refs_9_ = f32[256,128]{1,0:T(8,128)S(1)} collective-permute-done((f32[256,128]{1,0:T(8,128)S(1)}, f32[256,128]{1,0:T(8,128)S(1)}, u32[]{:S(2)}, u32[]{:S(2)}) %collective-permute-start.13) | collective-permute-done | bytes 131104 | tf_op jit(solution)/shard_map/ppermute | solution.py:485
  35.0 1.0 %finish10.1.refs_1_.refs_11_ = bf16[1024,256]{1,0:T(8,128)(2,1)S(1)} custom-call(f32[1024,1024]{1,0:T(8,128)S(1)} %get-tuple-element.57.refs_0_, bf16[1024,128]{1,0:T(8,128)(2,1)S(1)} %get-tuple-element.33.refs_0_.refs_1_, f32[2,8,1024]{2,1,0:T(8,128)S(1)} %get-tuple-element.36.refs_3_.refs_2_, f32[8,8,1024]{2,1,0:T(8,128)S(1)} %get-tuple-element.38.refs_5_.refs_3_, ...), custom_call_target="tpu_custom_call" | custom-call | flops 1000 | bytes 1000000 | tf_op jit(solution)/shard_map/finish10/pallas_call | solution.py:457
  36.2 1.8 %finish01.1.refs_12_ = bf16[1024,1024]{1,0:T(8,128)(2,1)} custom-call(f32[1024,1024]{1,0:T(8,128)S(1)} %get-tuple-element.57.refs_0_, bf16[1024,128]{1,0:T(8,128)(2,1)S(1)} %get-tuple-element.33.refs_0_.refs_1_, f32[2,8,1024]{2,1,0:T(8,128)S(1)} %get-tuple-element.36.refs_3_.refs_2_, f32[8,8,1024]{2,1,0:T(8,128)S(1)} %get-tuple-element.38.refs_5_.refs_3_, ...), custom_call_target="tpu_custom_call" | custom-call | flops 20000000000 | bytes 1000000 | tf_op jit(solution)/shard_map/finish01/pallas_call | solution.py:457
  38.0 1.7 %finish11.1 = bf16[1024,1024]{1,0:T(8,128)(2,1)} custom-call(f32[1024,1024]{1,0:T(8,128)S(1)} %get-tuple-element.57.refs_0_, bf16[1024,128]{1,0:T(8,128)(2,1)S(1)} %get-tuple-element.33.refs_0_.refs_1_, f32[2,8,1024]{2,1,0:T(8,128)S(1)} %get-tuple-element.36.refs_3_.refs_2_, ...), custom_call_target="tpu_custom_call", output_to_operand_aliasing={{}: (12, {})} | custom-call | flops 2000000000 | bytes 1000000 | tf_op jit(solution)/shard_map/finish11/pallas_call | solution.py:457
  (32 shorter events, 2.0 us)
Async XLA Ops:
  2.6 2.1 %collective-permute-start = (f32[1032,128]{1,0:T(8,128)S(1)}, f32[1032,128]{1,0:T(8,128)S(1)}, u32[]{:S(2)}, u32[]{:S(2)}) collective-permute-start(f32[1032,128]{1,0:T(8,128)S(1)} %get-tuple-element.40.mine_ref), channel_id=1, source_target_pairs={{0,8},{8,0},{16,24},{24,16},{1,9},{9,1},{17,25},{25,17},{2,10},{10... | collective-permute-start | bytes 1585160 | tf_op jit(solution)/shard_map/ppermute | solution.py:485
  4.7 5.5 %collective-permute-start.1 = (f32[136,128]{1,0:T(8,128)S(1)}, f32[136,128]{1,0:T(8,128)S(1)}, u32[]{:S(2)}, u32[]{:S(2)}) collective-permute-start(f32[136,128]{1,0:T(8,128)S(1)} %get-tuple-element.43), channel_id=1, source_target_pairs={{0,16},{8,24},{16,0},{24,8},{1,17},{9,25},{17,1},{25,9},{2,18},{10... | collective-permute-start | bytes 208904 | tf_op jit(solution)/shard_map/ppermute | solution.py:485
  7.7 4.8 %collective-permute-start.3 = (f32[136,128]{1,0:T(8,128)S(1)}, f32[136,128]{1,0:T(8,128)S(1)}, u32[]{:S(2)}, u32[]{:S(2)}) collective-permute-start(f32[136,128]{1,0:T(8,128)S(1)} %get-tuple-element.47), channel_id=1, source_target_pairs={{0,16},{8,24},{16,0},{24,8},{1,17},{9,25},{17,1},{25,9},{2,18},{10... | collective-permute-start | bytes 208904 | tf_op jit(solution)/shard_map/ppermute | solution.py:485
  10.2 5.8 %collective-permute-start.2 = (f32[136,128]{1,0:T(8,128)S(1)}, f32[136,128]{1,0:T(8,128)S(1)}, u32[]{:S(2)}, u32[]{:S(2)}) collective-permute-start(f32[136,128]{1,0:T(8,128)S(1)} %merge11.1.refs_9_.refs_3_.refs_0_), channel_id=1, source_target_pairs={{0,1},{8,9},{16,17},{24,25},{1,0},{9,8},{17,16},{25,24},{2,3},{10,... | collective-permute-start | bytes 208904 | tf_op jit(solution)/shard_map/ppermute | solution.py:485
  12.5 5.3 %collective-permute-start.5 = (f32[136,128]{1,0:T(8,128)S(1)}, f32[136,128]{1,0:T(8,128)S(1)}, u32[]{:S(2)}, u32[]{:S(2)}) collective-permute-start(f32[136,128]{1,0:T(8,128)S(1)} %get-tuple-element.51.refs_0_.refs_2_), channel_id=1, source_target_pairs={{0,1},{8,9},{16,17},{24,25},{1,0},{9,8},{17,16},{25,24},{2,3},{10,... | collective-permute-start | bytes 208904 | tf_op jit(solution)/shard_map/ppermute | solution.py:485
  13.6 12.4 %collective-permute-start.7 = (f32[256,128]{1,0:T(8,128)S(1)}, f32[256,128]{1,0:T(8,128)S(1)}, u32[]{:S(2)}, u32[]{:S(2)}) collective-permute-start(f32[256,128]{1,0:T(8,128)S(1)} %rest.1), channel_id=1, source_target_pairs={{0,16},{8,24},{16,0},{24,8},{1,17},{9,25},{17,1},{25,9},{2,18},{10... | collective-permute-start | bytes 393224 | tf_op jit(solution)/shard_map/ppermute | solution.py:485
  16.1 5.3 %collective-permute-start.4 = (f32[136,128]{1,0:T(8,128)S(1)}, f32[136,128]{1,0:T(8,128)S(1)}, u32[]{:S(2)}, u32[]{:S(2)}) collective-permute-start(f32[136,128]{1,0:T(8,128)S(1)} %merge21.1.refs_9_.refs_3_.refs_0_), channel_id=1, source_target_pairs={{0,2},{8,10},{16,18},{24,26},{1,3},{9,11},{17,19},{25,27},{2,0},{1... | collective-permute-start | bytes 208904 | tf_op jit(solution)/shard_map/ppermute | solution.py:485
  17.8 8.2 %collective-permute-start.6 = (f32[136,128]{1,0:T(8,128)S(1)}, f32[136,128]{1,0:T(8,128)S(1)}, u32[]{:S(2)}, u32[]{:S(2)}) collective-permute-start(f32[136,128]{1,0:T(8,128)S(1)} %get-tuple-element.54.refs_0_.refs_2_), channel_id=1, source_target_pairs={{0,2},{8,10},{16,18},{24,26},{1,3},{9,11},{17,19},{25,27},{2,0},{1... | collective-permute-start | bytes 208904 | tf_op jit(solution)/shard_map/ppermute | solution.py:485
  18.6 12.2 %collective-permute-start.11 = (f32[256,128]{1,0:T(8,128)S(1)}, f32[256,128]{1,0:T(8,128)S(1)}, u32[]{:S(2)}, u32[]{:S(2)}) collective-permute-start(f32[256,128]{1,0:T(8,128)S(1)} %found2.1.refs_2_), channel_id=1, source_target_pairs={{0,16},{8,24},{16,0},{24,8},{1,17},{9,25},{17,1},{25,9},{2,18},{10... | collective-permute-start | bytes 393224 | tf_op jit(solution)/shard_map/ppermute | solution.py:485
  21.4 7.8 %collective-permute-start.9 = (f32[136,128]{1,0:T(8,128)S(1)}, f32[136,128]{1,0:T(8,128)S(1)}, u32[]{:S(2)}, u32[]{:S(2)}) collective-permute-start(f32[136,128]{1,0:T(8,128)S(1)} %merge31.1.refs_3_.refs_9_), channel_id=1, source_target_pairs={{0,4},{8,12},{16,20},{24,28},{1,5},{9,13},{17,21},{25,29},{2,6},{1... | collective-permute-start | bytes 208904 | tf_op jit(solution)/shard_map/ppermute | solution.py:485
  26.0 3.2 %collective-permute-start.8 = (f32[136,128]{1,0:T(8,128)S(1)}, f32[136,128]{1,0:T(8,128)S(1)}, u32[]{:S(2)}, u32[]{:S(2)}) collective-permute-start(f32[136,128]{1,0:T(8,128)S(1)} %get-tuple-element.56.refs_2_), channel_id=1, source_target_pairs={{0,4},{8,12},{16,20},{24,28},{1,5},{9,13},{17,21},{25,29},{2,6},{1... | collective-permute-start | bytes 208904 | tf_op jit(solution)/shard_map/ppermute | solution.py:485
  27.3 5.0 %collective-permute-start.12 = (f32[256,128]{1,0:T(8,128)S(1)}, f32[256,128]{1,0:T(8,128)S(1)}, u32[]{:S(2)}, u32[]{:S(2)}) collective-permute-start(f32[256,128]{1,0:T(8,128)S(1)} %found3.1.refs_10_.refs_4_), channel_id=1, source_target_pairs={{0,16},{8,24},{16,0},{24,8},{1,17},{9,25},{17,1},{25,9},{2,18},{10... | collective-permute-start | bytes 393224 | tf_op jit(solution)/shard_map/ppermute | solution.py:485
  29.3 6.7 %collective-permute-start.10 = (f32[256,128]{1,0:T(8,128)S(1)}, f32[256,128]{1,0:T(8,128)S(1)}, u32[]{:S(2)}, u32[]{:S(2)}) collective-permute-start(f32[256,128]{1,0:T(8,128)S(1)} %state.1.refs_6_.refs_0_.refs_9_), channel_id=1, source_target_pairs={{0,16},{8,24},{16,0},{24,8},{1,17},{9,25},{17,1},{25,9},{2,18},{10... | collective-permute-start | bytes 393224 | tf_op jit(solution)/shard_map/ppermute | solution.py:485
  32.4 2.5 %collective-permute-start.14 = (f32[1536,128]{1,0:T(8,128)S(1)}, f32[1536,128]{1,0:T(8,128)S(1)}, u32[]{:S(2)}, u32[]{:S(2)}) collective-permute-start(f32[1536,128]{1,0:T(8,128)S(1)} %near.1.refs_1_.refs_10_), channel_id=1, source_target_pairs={{0,8},{8,0},{16,24},{24,16},{1,9},{9,1},{17,25},{25,17},{2,10},{10... | collective-permute-start | bytes 2359304 | tf_op jit(solution)/shard_map/ppermute | solution.py:485
  32.5 2.5 %collective-permute-start.13 = (f32[256,128]{1,0:T(8,128)S(1)}, f32[256,128]{1,0:T(8,128)S(1)}, u32[]{:S(2)}, u32[]{:S(2)}) collective-permute-start(f32[256,128]{1,0:T(8,128)S(1)} %shared.1), channel_id=1, source_target_pairs={{0,8},{8,0},{16,24},{24,16},{1,9},{9,1},{17,25},{25,17},{2,10},{10... | collective-permute-start | bytes 393224 | tf_op jit(solution)/shard_map/ppermute | solution.py:485
  36.0 2.0 %collective-permute-start.15 = (f32[256,128]{1,0:T(8,128)S(1)}, f32[256,128]{1,0:T(8,128)S(1)}, u32[]{:S(2)}, u32[]{:S(2)}) collective-permute-start(f32[256,128]{1,0:T(8,128)S(1)} %beside.1.refs_9_), channel_id=1, source_target_pairs={{0,8},{8,0},{16,24},{24,16},{1,9},{9,1},{17,25},{25,17},{2,10},{10... | collective-permute-start | bytes 393224 | tf_op jit(solution)/shard_map/ppermute | solution.py:485

commit v19 on v18

--- a/solution.py
+++ b/solution.py
@@ -471,17 +471,13 @@
     )(*inputs)
 
 
-def trade(value, mask, sends=lambda source: True):
+def trade(value, mask):
     wide, narrow = lax.axis_size("wide"), lax.axis_size("narrow")
 
     def ranked(index):
         return index % narrow * wide + index // narrow
 
-    pairs = [
-        (ranked(source), ranked(source ^ mask))
-        for source in range(wide * narrow)
-        if sends(source)
-    ]
+    pairs = [(ranked(source), ranked(source ^ mask)) for source in range(wide * narrow)]
     return lax.ppermute(value, AXES, pairs)
 
 
@@ -513,12 +509,10 @@
         return pack(name, [(state, size) for state in messages], tokens)
 
     for bit in range(1, bits):
-        lower = lambda source: bit < last or source >> last & 1 == 0
-        sent = give if bit == 1 else chunks
-        found[bit] = [trade(chunk, 2**bit, lower) for chunk in sent]
+        found[bit] = [trade(chunk, 2**bit) for chunk in (give if bit == 1 else chunks)]
         stays = chunks if bit == 1 else stays
         waits = []
-        if at < spans:
+        if bit < 3 or bit == last:
             stop = spans if bit == last else at + 1
             begun = [*chunks[-1:], *([found[bit - 1]] if bit == last else [])]
             mixed, *waits = mix_local(at, stop, shared, mixed, begun, True)

time: 39.9 us -> 38.3 us (0.960)
  starting transfers between devices: 21 us -> 19.8 us
    ppermute x16, starting transfers between devices: 21 us -> 19.8 us  [trade(): return lax.ppermute(value, AXES, pairs)]
    pallas_call x20 -> x19, Pallas kernels: 6.95 us -> 6.78 us  [call(): pl.pallas_call(kernel, in_specs=specs, out_specs=[HELD] * len(outputs), o...]
  transfers between devices with their start and end apart: 16 -> 16, of which waited for: 5 -> 6; matrix products, arithmetic and copies ran while one was open for 0% -> 0% of each run, Pallas kernels for 20% -> 21%
where the time goes in v19:
time: 38.3 us; the launch traced here: 38.2 us
  starting transfers between devices  19.8 us (52%)
  Pallas kernels  12.3 us (32%)
  waiting for transfers between devices  5.87 us (15%)
    ppermute x16, starting transfers between devices, trade(): return lax.ppermute(value, AXES, pairs)  19.8 us
    pallas_call x19, Pallas kernels, call(): pl.pallas_call(kernel, in_specs=specs, out_specs=[HELD] * len(outputs), o...  6.78 us
    ppermute x16, waiting for transfers between devices, trade(): return lax.ppermute(value, AXES, pairs)  5.87 us
    pallas_call x4, Pallas kernels, finish(): pl.pallas_call(functools.partial(finish_kernel, quarters, first_level, bi...  5.5 us
  transfers between devices with their start and end apart: 16, of which 6 were waited for; matrix products, arithmetic and copies ran while one was open for 0% of the time, Pallas kernels for 21%

profile of v19, /device:TPU:0, one launch (start us, length us, event | category | flops | bytes accessed | tf_op | source)
XLA Modules:
  0.0 38.2 jit_solution(17029349414044734253)
XLA Ops:
  0.0 2.6 %states.1 = (f32[1032,128]{1,0:T(8,128)S(1)}, bf16[3,128,1024]{2,1,0:T(8,128)(2,1)S(1)}, f32[2,8,1024]{2,1,0:T(8,128)S(1)}, f32[4,8,128]{2,1,0:T(8,128)S(1)}, bf...) custom-call(bf16[1024,128]{1,0:T(8,128)(2,1)} %refs_0_.1, ...), custom_call_target="tpu_custom_call" | custom-call | flops 2000000000 | bytes 1000000 | tf_op jit(solution)/shard_map/states/pallas_call | solution.py:50
  3.1 1.5 %collective-permute-done.other_ref.refs_7_ = f32[1032,128]{1,0:T(8,128)S(1)} collective-permute-done((f32[1032,128]{1,0:T(8,128)S(1)}, f32[1032,128]{1,0:T(8,128)S(1)}, u32[]{:S(2)}, u32[]{:S(2)}) %collective-permute-start) | collective-permute-done | bytes 528416 | tf_op jit(solution)/shard_map/ppermute | solution.py:481
  4.7 3.0 %collective-permute-start.1 = (f32[136,128]{1,0:T(8,128)S(1)}, f32[136,128]{1,0:T(8,128)S(1)}, u32[]{:S(2)}, u32[]{:S(2)}) collective-permute-start(f32[136,128]{1,0:T(8,128)S(1)} %get-tuple-element.41), channel_id=1, source_target_pairs={{0,16},{8,24},{16,0},{24,8},{1,17},{9,25},{17,1},{25,9},{2,18},{10... | collective-permute-start | bytes 208904 | tf_op jit(solution)/shard_map/ppermute | solution.py:481
  7.7 0.8 %local0.1 = (f32[1024,1024]{1,0:T(8,128)S(1)}, f32[8,128]{1,0:T(8,128)S(1)}) custom-call(bf16[1024,128]{1,0:T(8,128)(2,1)S(1)} %get-tuple-element.31.refs_0_.refs_1_, bf16[1024,128]{1,0:T(8,128)(2,1)S(1)} %get-tuple-element.32.refs_1_, bf16[1024,1024]{1,0:T(8,128)(2,1)S(1)} %get-tuple-element.33.refs_2_, ...), custom_call_target="tpu_custom_call" | custom-call | flops 2000000000 | bytes 1000000 | tf_op jit(solution)/shard_map/local0/pallas_call | solution.py:50
  8.6 1.6 %collective-permute-done.1.refs_1_ = f32[136,128]{1,0:T(8,128)S(1)} collective-permute-done((f32[136,128]{1,0:T(8,128)S(1)}, f32[136,128]{1,0:T(8,128)S(1)}, u32[]{:S(2)}, u32[]{:S(2)}) %collective-permute-start.1) | collective-permute-done | bytes 69664 | tf_op jit(solution)/shard_map/ppermute | solution.py:481
  10.2 2.2 %collective-permute-start.2 = (f32[136,128]{1,0:T(8,128)S(1)}, f32[136,128]{1,0:T(8,128)S(1)}, u32[]{:S(2)}, u32[]{:S(2)}) collective-permute-start(f32[136,128]{1,0:T(8,128)S(1)} %merge11.1.refs_9_.refs_3_.refs_0_), channel_id=1, source_target_pairs={{0,1},{8,9},{16,17},{24,25},{1,0},{9,8},{17,16},{25,24},{2,3},{10,... | collective-permute-start | bytes 208904 | tf_op jit(solution)/shard_map/ppermute | solution.py:481
  12.5 1.1 %collective-permute-start.5 = (f32[136,128]{1,0:T(8,128)S(1)}, f32[136,128]{1,0:T(8,128)S(1)}, u32[]{:S(2)}, u32[]{:S(2)}) collective-permute-start(f32[136,128]{1,0:T(8,128)S(1)} %get-tuple-element.48.refs_0_.refs_2_), channel_id=1, source_target_pairs={{0,1},{8,9},{16,17},{24,25},{1,0},{9,8},{17,16},{25,24},{2,3},{10,... | collective-permute-start | bytes 208904 | tf_op jit(solution)/shard_map/ppermute | solution.py:481
  13.6 1.5 %collective-permute-start.7 = (f32[256,128]{1,0:T(8,128)S(1)}, f32[256,128]{1,0:T(8,128)S(1)}, u32[]{:S(2)}, u32[]{:S(2)}) collective-permute-start(f32[256,128]{1,0:T(8,128)S(1)} %rest.1), channel_id=1, source_target_pairs={{0,16},{8,24},{16,0},{24,8},{1,17},{9,25},{17,1},{25,9},{2,18},{10... | collective-permute-start | bytes 393224 | tf_op jit(solution)/shard_map/ppermute | solution.py:481
  15.1 1.0 %local1.1 = (f32[1024,1024]{1,0:T(8,128)S(1)}, f32[8,128]{1,0:T(8,128)S(1)}) custom-call(bf16[1024,128]{1,0:T(8,128)(2,1)S(1)} %get-tuple-element.31.refs_0_.refs_1_, bf16[1024,128]{1,0:T(8,128)(2,1)S(1)} %get-tuple-element.32.refs_1_, bf16[1024,1024]{1,0:T(8,128)(2,1)S(1)} %get-tuple-element.33.refs_2_, ...), custom_call_target="tpu_custom_call", output_to_operand_aliasing={{0}: (8, {})} | custom-call | flops 2000000000 | bytes 1000000 | tf_op jit(solution)/shard_map/local1/pallas_call | solution.py:50
  16.1 1.6 %collective-permute-start.4 = (f32[136,128]{1,0:T(8,128)S(1)}, f32[136,128]{1,0:T(8,128)S(1)}, u32[]{:S(2)}, u32[]{:S(2)}) collective-permute-start(f32[136,128]{1,0:T(8,128)S(1)} %merge21.1.refs_3_.refs_0_), channel_id=1, source_target_pairs={{0,2},{8,10},{16,18},{24,26},{1,3},{9,11},{17,19},{25,27},{2,0},{1... | collective-permute-start | bytes 208904 | tf_op jit(solution)/shard_map/ppermute | solution.py:481
  17.8 0.8 %collective-permute-start.6 = (f32[136,128]{1,0:T(8,128)S(1)}, f32[136,128]{1,0:T(8,128)S(1)}, u32[]{:S(2)}, u32[]{:S(2)}) collective-permute-start(f32[136,128]{1,0:T(8,128)S(1)} %get-tuple-element.51.refs_0_.refs_2_), channel_id=1, source_target_pairs={{0,2},{8,10},{16,18},{24,26},{1,3},{9,11},{17,19},{25,27},{2,0},{1... | collective-permute-start | bytes 208904 | tf_op jit(solution)/shard_map/ppermute | solution.py:481
  18.6 1.8 %collective-permute-start.11 = (f32[256,128]{1,0:T(8,128)S(1)}, f32[256,128]{1,0:T(8,128)S(1)}, u32[]{:S(2)}, u32[]{:S(2)}) collective-permute-start(f32[256,128]{1,0:T(8,128)S(1)} %found2.1.refs_2_), channel_id=1, source_target_pairs={{0,16},{8,24},{16,0},{24,8},{1,17},{9,25},{17,1},{25,9},{2,18},{10... | collective-permute-start | bytes 393224 | tf_op jit(solution)/shard_map/ppermute | solution.py:481
  20.5 2.7 %collective-permute-start.9 = (f32[136,128]{1,0:T(8,128)S(1)}, f32[136,128]{1,0:T(8,128)S(1)}, u32[]{:S(2)}, u32[]{:S(2)}) collective-permute-start(f32[136,128]{1,0:T(8,128)S(1)} %merge31.1.refs_3_.refs_9_), channel_id=1, source_target_pairs={{0,4},{8,12},{16,20},{24,28},{1,5},{9,13},{17,21},{25,29},{2,6},{1... | collective-permute-start | bytes 208904 | tf_op jit(solution)/shard_map/ppermute | solution.py:481
  23.2 1.9 %collective-permute-start.8 = (f32[136,128]{1,0:T(8,128)S(1)}, f32[136,128]{1,0:T(8,128)S(1)}, u32[]{:S(2)}, u32[]{:S(2)}) collective-permute-start(f32[136,128]{1,0:T(8,128)S(1)} %get-tuple-element.52.refs_2_), channel_id=1, source_target_pairs={{0,4},{8,12},{16,20},{24,28},{1,5},{9,13},{17,21},{25,29},{2,6},{1... | collective-permute-start | bytes 208904 | tf_op jit(solution)/shard_map/ppermute | solution.py:481
  25.1 0.8 %collective-permute-start.12 = (f32[256,128]{1,0:T(8,128)S(1)}, f32[256,128]{1,0:T(8,128)S(1)}, u32[]{:S(2)}, u32[]{:S(2)}) collective-permute-start(f32[256,128]{1,0:T(8,128)S(1)} %found3.1.refs_10_.refs_4_), channel_id=1, source_target_pairs={{0,16},{8,24},{16,0},{24,8},{1,17},{9,25},{17,1},{25,9},{2,18},{10... | collective-permute-start | bytes 393224 | tf_op jit(solution)/shard_map/ppermute | solution.py:481
  25.9 2.0 %local2.1 = (f32[1024,1024]{1,0:T(8,128)S(1)}, f32[8,128]{1,0:T(8,128)S(1)}) custom-call(bf16[1024,128]{1,0:T(8,128)(2,1)S(1)} %get-tuple-element.31.refs_0_.refs_1_, bf16[1024,128]{1,0:T(8,128)(2,1)S(1)} %get-tuple-element.32.refs_1_, bf16[1024,1024]{1,0:T(8,128)(2,1)S(1)} %get-tuple-element.33.refs_2_, ...), custom_call_target="tpu_custom_call", output_to_operand_aliasing={{0}: (8, {})} | custom-call | flops 1000 | bytes 1000000 | tf_op jit(solution)/shard_map/local2/pallas_call | solution.py:50
  27.9 0.6 %collective-permute-done.8.refs_0_ = f32[136,128]{1,0:T(8,128)S(1)} collective-permute-done((f32[136,128]{1,0:T(8,128)S(1)}, f32[136,128]{1,0:T(8,128)S(1)}, u32[]{:S(2)}, u32[]{:S(2)}) %collective-permute-start.8) | collective-permute-done | bytes 69664 | tf_op jit(solution)/shard_map/ppermute | solution.py:481
  28.5 1.2 %collective-permute-start.10 = (f32[256,128]{1,0:T(8,128)S(1)}, f32[256,128]{1,0:T(8,128)S(1)}, u32[]{:S(2)}, u32[]{:S(2)}) collective-permute-start(f32[256,128]{1,0:T(8,128)S(1)} %state.1.refs_6_.refs_0_.refs_9_), channel_id=1, source_target_pairs={{0,16},{8,24},{16,0},{24,8},{1,17},{9,25},{17,1},{25,9},{2,18},{10... | collective-permute-start | bytes 393224 | tf_op jit(solution)/shard_map/ppermute | solution.py:481
  29.7 1.1 %collective-permute-done.12.refs_5_ = f32[256,128]{1,0:T(8,128)S(1)} collective-permute-done((f32[256,128]{1,0:T(8,128)S(1)}, f32[256,128]{1,0:T(8,128)S(1)}, u32[]{:S(2)}, u32[]{:S(2)}) %collective-permute-start.12) | collective-permute-done | bytes 131104 | tf_op jit(solution)/shard_map/ppermute | solution.py:481
  31.6 1.0 %finish00.1.refs_11_ = bf16[1024,256]{1,0:T(8,128)(2,1)S(1)} custom-call(f32[1024,1024]{1,0:T(8,128)S(1)} %get-tuple-element.53.refs_0_, bf16[1024,128]{1,0:T(8,128)(2,1)S(1)} %get-tuple-element.31.refs_0_.refs_1_, f32[2,8,1024]{2,1,0:T(8,128)S(1)} %get-tuple-element.34.refs_3_.refs_2_, f32[8,8,1024]{2,1,0:T(8,128)S(1)} %get-tuple-element.36.refs_5_.refs_3_, ...), custom_call_target="tpu_custom_call" | custom-call | flops 20000000000 | bytes 1000000 | tf_op jit(solution)/shard_map/finish00/pallas_call | solution.py:457
  32.6 0.9 %collective-permute-done.13.refs_9_ = f32[256,128]{1,0:T(8,128)S(1)} collective-permute-done((f32[256,128]{1,0:T(8,128)S(1)}, f32[256,128]{1,0:T(8,128)S(1)}, u32[]{:S(2)}, u32[]{:S(2)}) %collective-permute-start.13) | collective-permute-done | bytes 131104 | tf_op jit(solution)/shard_map/ppermute | solution.py:481
  33.4 1.0 %finish10.1.refs_1_.refs_11_ = bf16[1024,256]{1,0:T(8,128)(2,1)S(1)} custom-call(f32[1024,1024]{1,0:T(8,128)S(1)} %get-tuple-element.53.refs_0_, bf16[1024,128]{1,0:T(8,128)(2,1)S(1)} %get-tuple-element.31.refs_0_.refs_1_, f32[2,8,1024]{2,1,0:T(8,128)S(1)} %get-tuple-element.34.refs_3_.refs_2_, f32[8,8,1024]{2,1,0:T(8,128)S(1)} %get-tuple-element.36.refs_5_.refs_3_, ...), custom_call_target="tpu_custom_call" | custom-call | flops 1000 | bytes 1000000 | tf_op jit(solution)/shard_map/finish10/pallas_call | solution.py:457
  34.7 1.7 %finish01.1.refs_12_ = bf16[1024,1024]{1,0:T(8,128)(2,1)} custom-call(f32[1024,1024]{1,0:T(8,128)S(1)} %get-tuple-element.53.refs_0_, bf16[1024,128]{1,0:T(8,128)(2,1)S(1)} %get-tuple-element.31.refs_0_.refs_1_, f32[2,8,1024]{2,1,0:T(8,128)S(1)} %get-tuple-element.34.refs_3_.refs_2_, f32[8,8,1024]{2,1,0:T(8,128)S(1)} %get-tuple-element.36.refs_5_.refs_3_, ...), custom_call_target="tpu_custom_call" | custom-call | flops 20000000000 | bytes 1000000 | tf_op jit(solution)/shard_map/finish01/pallas_call | solution.py:457
  36.4 1.8 %finish11.1 = bf16[1024,1024]{1,0:T(8,128)(2,1)} custom-call(f32[1024,1024]{1,0:T(8,128)S(1)} %get-tuple-element.53.refs_0_, bf16[1024,128]{1,0:T(8,128)(2,1)S(1)} %get-tuple-element.31.refs_0_.refs_1_, f32[2,8,1024]{2,1,0:T(8,128)S(1)} %get-tuple-element.34.refs_3_.refs_2_, ...), custom_call_target="tpu_custom_call", output_to_operand_aliasing={{}: (12, {})} | custom-call | flops 2000000000 | bytes 1000000 | tf_op jit(solution)/shard_map/finish11/pallas_call | solution.py:457
  (31 shorter events, 1.9 us)
Async XLA Ops:
  2.6 2.1 %collective-permute-start = (f32[1032,128]{1,0:T(8,128)S(1)}, f32[1032,128]{1,0:T(8,128)S(1)}, u32[]{:S(2)}, u32[]{:S(2)}) collective-permute-start(f32[1032,128]{1,0:T(8,128)S(1)} %get-tuple-element.38.mine_ref), channel_id=1, source_target_pairs={{0,8},{8,0},{16,24},{24,16},{1,9},{9,1},{17,25},{25,17},{2,10},{10... | collective-permute-start | bytes 1585160 | tf_op jit(solution)/shard_map/ppermute | solution.py:481
  4.7 5.5 %collective-permute-start.1 = (f32[136,128]{1,0:T(8,128)S(1)}, f32[136,128]{1,0:T(8,128)S(1)}, u32[]{:S(2)}, u32[]{:S(2)}) collective-permute-start(f32[136,128]{1,0:T(8,128)S(1)} %get-tuple-element.41), channel_id=1, source_target_pairs={{0,16},{8,24},{16,0},{24,8},{1,17},{9,25},{17,1},{25,9},{2,18},{10... | collective-permute-start | bytes 208904 | tf_op jit(solution)/shard_map/ppermute | solution.py:481
  7.7 4.8 %collective-permute-start.3 = (f32[136,128]{1,0:T(8,128)S(1)}, f32[136,128]{1,0:T(8,128)S(1)}, u32[]{:S(2)}, u32[]{:S(2)}) collective-permute-start(f32[136,128]{1,0:T(8,128)S(1)} %get-tuple-element.45), channel_id=1, source_target_pairs={{0,16},{8,24},{16,0},{24,8},{1,17},{9,25},{17,1},{25,9},{2,18},{10... | collective-permute-start | bytes 208904 | tf_op jit(solution)/shard_map/ppermute | solution.py:481
  10.2 5.8 %collective-permute-start.2 = (f32[136,128]{1,0:T(8,128)S(1)}, f32[136,128]{1,0:T(8,128)S(1)}, u32[]{:S(2)}, u32[]{:S(2)}) collective-permute-start(f32[136,128]{1,0:T(8,128)S(1)} %merge11.1.refs_9_.refs_3_.refs_0_), channel_id=1, source_target_pairs={{0,1},{8,9},{16,17},{24,25},{1,0},{9,8},{17,16},{25,24},{2,3},{10,... | collective-permute-start | bytes 208904 | tf_op jit(solution)/shard_map/ppermute | solution.py:481
  12.5 5.3 %collective-permute-start.5 = (f32[136,128]{1,0:T(8,128)S(1)}, f32[136,128]{1,0:T(8,128)S(1)}, u32[]{:S(2)}, u32[]{:S(2)}) collective-permute-start(f32[136,128]{1,0:T(8,128)S(1)} %get-tuple-element.48.refs_0_.refs_2_), channel_id=1, source_target_pairs={{0,1},{8,9},{16,17},{24,25},{1,0},{9,8},{17,16},{25,24},{2,3},{10,... | collective-permute-start | bytes 208904 | tf_op jit(solution)/shard_map/ppermute | solution.py:481
  13.6 9.6 %collective-permute-start.7 = (f32[256,128]{1,0:T(8,128)S(1)}, f32[256,128]{1,0:T(8,128)S(1)}, u32[]{:S(2)}, u32[]{:S(2)}) collective-permute-start(f32[256,128]{1,0:T(8,128)S(1)} %rest.1), channel_id=1, source_target_pairs={{0,16},{8,24},{16,0},{24,8},{1,17},{9,25},{17,1},{25,9},{2,18},{10... | collective-permute-start | bytes 393224 | tf_op jit(solution)/shard_map/ppermute | solution.py:481
  16.1 4.4 %collective-permute-start.4 = (f32[136,128]{1,0:T(8,128)S(1)}, f32[136,128]{1,0:T(8,128)S(1)}, u32[]{:S(2)}, u32[]{:S(2)}) collective-permute-start(f32[136,128]{1,0:T(8,128)S(1)} %merge21.1.refs_3_.refs_0_), channel_id=1, source_target_pairs={{0,2},{8,10},{16,18},{24,26},{1,3},{9,11},{17,19},{25,27},{2,0},{1... | collective-permute-start | bytes 208904 | tf_op jit(solution)/shard_map/ppermute | solution.py:481
  17.8 5.4 %collective-permute-start.6 = (f32[136,128]{1,0:T(8,128)S(1)}, f32[136,128]{1,0:T(8,128)S(1)}, u32[]{:S(2)}, u32[]{:S(2)}) collective-permute-start(f32[136,128]{1,0:T(8,128)S(1)} %get-tuple-element.51.refs_0_.refs_2_), channel_id=1, source_target_pairs={{0,2},{8,10},{16,18},{24,26},{1,3},{9,11},{17,19},{25,27},{2,0},{1... | collective-permute-start | bytes 208904 | tf_op jit(solution)/shard_map/ppermute | solution.py:481
  18.6 11.1 %collective-permute-start.11 = (f32[256,128]{1,0:T(8,128)S(1)}, f32[256,128]{1,0:T(8,128)S(1)}, u32[]{:S(2)}, u32[]{:S(2)}) collective-permute-start(f32[256,128]{1,0:T(8,128)S(1)} %found2.1.refs_2_), channel_id=1, source_target_pairs={{0,16},{8,24},{16,0},{24,8},{1,17},{9,25},{17,1},{25,9},{2,18},{10... | collective-permute-start | bytes 393224 | tf_op jit(solution)/shard_map/ppermute | solution.py:481
  20.5 8.0 %collective-permute-start.9 = (f32[136,128]{1,0:T(8,128)S(1)}, f32[136,128]{1,0:T(8,128)S(1)}, u32[]{:S(2)}, u32[]{:S(2)}) collective-permute-start(f32[136,128]{1,0:T(8,128)S(1)} %merge31.1.refs_3_.refs_9_), channel_id=1, source_target_pairs={{0,4},{8,12},{16,20},{24,28},{1,5},{9,13},{17,21},{25,29},{2,6},{1... | collective-permute-start | bytes 208904 | tf_op jit(solution)/shard_map/ppermute | solution.py:481
  23.2 5.3 %collective-permute-start.8 = (f32[136,128]{1,0:T(8,128)S(1)}, f32[136,128]{1,0:T(8,128)S(1)}, u32[]{:S(2)}, u32[]{:S(2)}) collective-permute-start(f32[136,128]{1,0:T(8,128)S(1)} %get-tuple-element.52.refs_2_), channel_id=1, source_target_pairs={{0,4},{8,12},{16,20},{24,28},{1,5},{9,13},{17,21},{25,29},{2,6},{1... | collective-permute-start | bytes 208904 | tf_op jit(solution)/shard_map/ppermute | solution.py:481
  25.1 5.7 %collective-permute-start.12 = (f32[256,128]{1,0:T(8,128)S(1)}, f32[256,128]{1,0:T(8,128)S(1)}, u32[]{:S(2)}, u32[]{:S(2)}) collective-permute-start(f32[256,128]{1,0:T(8,128)S(1)} %found3.1.refs_10_.refs_4_), channel_id=1, source_target_pairs={{0,16},{8,24},{16,0},{24,8},{1,17},{9,25},{17,1},{25,9},{2,18},{10... | collective-permute-start | bytes 393224 | tf_op jit(solution)/shard_map/ppermute | solution.py:481
  28.5 5.9 %collective-permute-start.10 = (f32[256,128]{1,0:T(8,128)S(1)}, f32[256,128]{1,0:T(8,128)S(1)}, u32[]{:S(2)}, u32[]{:S(2)}) collective-permute-start(f32[256,128]{1,0:T(8,128)S(1)} %state.1.refs_6_.refs_0_.refs_9_), channel_id=1, source_target_pairs={{0,16},{8,24},{16,0},{24,8},{1,17},{9,25},{17,1},{25,9},{2,18},{10... | collective-permute-start | bytes 393224 | tf_op jit(solution)/shard_map/ppermute | solution.py:481
  30.9 2.5 %collective-permute-start.14 = (f32[1536,128]{1,0:T(8,128)S(1)}, f32[1536,128]{1,0:T(8,128)S(1)}, u32[]{:S(2)}, u32[]{:S(2)}) collective-permute-start(f32[1536,128]{1,0:T(8,128)S(1)} %near.1.refs_1_.refs_10_), channel_id=1, source_target_pairs={{0,8},{8,0},{16,24},{24,16},{1,9},{9,1},{17,25},{25,17},{2,10},{10... | collective-permute-start | bytes 2359304 | tf_op jit(solution)/shard_map/ppermute | solution.py:481
  31.0 2.4 %collective-permute-start.13 = (f32[256,128]{1,0:T(8,128)S(1)}, f32[256,128]{1,0:T(8,128)S(1)}, u32[]{:S(2)}, u32[]{:S(2)}) collective-permute-start(f32[256,128]{1,0:T(8,128)S(1)} %shared.1), channel_id=1, source_target_pairs={{0,8},{8,0},{16,24},{24,16},{1,9},{9,1},{17,25},{25,17},{2,10},{10... | collective-permute-start | bytes 393224 | tf_op jit(solution)/shard_map/ppermute | solution.py:481
  34.5 2.0 %collective-permute-start.15 = (f32[256,128]{1,0:T(8,128)S(1)}, f32[256,128]{1,0:T(8,128)S(1)}, u32[]{:S(2)}, u32[]{:S(2)}) collective-permute-start(f32[256,128]{1,0:T(8,128)S(1)} %beside.1.refs_9_), channel_id=1, source_target_pairs={{0,8},{8,0},{16,24},{24,16},{1,9},{9,1},{17,25},{25,17},{2,10},{10... | collective-permute-start | bytes 393224 | tf_op jit(solution)/shard_map/ppermute | solution.py:481

commit v20 on v19

--- a/solution.py
+++ b/solution.py
@@ -13,7 +13,7 @@
 EPS = 1e-05
 AXES = ("narrow", "wide")
 NT = (((1,), (1,)), ((), ()))
-COSTS = {"finish00": 20000000000, "finish10": 1000, "finish01": 20000000000, "local2": 1000, "reach": 1000}
+COSTS = {"local0": 1000, "finish00": 20000000000, "finish10": 1000, "finish01": 20000000000, "local2": 1000, "reach": 1000}
 
 
 def cost(name):
@@ -77,16 +77,15 @@
 
 
 def state_kernel(*refs):
-    q_hbm, k_hbm, v_hbm, decay_hbm, weight_hbm, gain_hbm = refs[:6]
-    message_ref, local_ref, sums_ref, totals_ref = refs[6:10]
-    q_ref, k_ref, v_ref, weight_ref, gain_ref, decay_ref, held, arrived = refs[10:]
+    k_hbm, v_hbm, decay_hbm = refs[:3]
+    keep_ref, send_ref, local_ref, sums_ref, totals_ref = refs[3:8]
+    k_ref, v_ref, decay_ref, held, message_ref, arrived = refs[8:]
     heads, tokens = decay_ref.shape
     head_width = v_ref.shape[1] // heads
     spans = tokens // SPAN
     rows_of = [slice(span * SPAN, (span + 1) * SPAN) for span in range(spans)]
     loads = [(decay_hbm, decay_ref), (k_hbm, k_ref)]
     loads += [(v_hbm.at[rows], v_ref.at[rows]) for rows in rows_of]
-    loads += [(q_hbm, q_ref), (weight_hbm, weight_ref), (gain_hbm, gain_ref)]
     copies = [
         pltpu.make_async_copy(source, target, arrived.at[at])
         for at, (source, target) in enumerate(loads)
@@ -131,24 +130,28 @@
                     else:
                         message_ref[columns] = group.T
                 at += spans >> (bit + 1)
-    message_ref[heads * head_width :] = run
-    for copy in copies[2 + spans :]:
-        copy.wait()
-
-
-def make_states(queries, keys, values, log_decay, level_weight, gain):
+    half = message_ref.shape[0] // 2
+    core = bit_of(place(), 0)
+    keep_ref[:half] = message_ref[pl.ds(pl.multiple_of(core * half, 8), half)]
+    send_ref[:half] = message_ref[pl.ds(pl.multiple_of((1 - core) * half, 8), half)]
+    keep_ref[half:] = run
+    send_ref[half:] = run
+
+
+def make_states(keys, values, log_decay):
     tokens, key_width = keys.shape
     heads = log_decay.shape[0]
     width = values.shape[1]
     spans = tokens // SPAN
-    inputs = [queries, keys, values, log_decay, level_weight, gain]
-    kept = [queries, keys, values, level_weight, gain]
+    inputs = [keys, values, log_decay]
+    kept = [keys, values]
     return call(
         state_kernel,
         "states",
         [pltpu.with_memory_space_constraint(array, pltpu.HBM) for array in inputs],
         [
-            ((width + heads, key_width), jnp.float32),
+            ((width // 2 + heads, key_width), jnp.float32),
+            ((width // 2 + heads, key_width), jnp.float32),
             ((spans - 1, key_width, width), jnp.bfloat16),
             ((2, heads, tokens), jnp.float32),
             ((spans, heads, 128), jnp.float32),
@@ -157,14 +160,39 @@
         [
             pltpu.VMEM(log_decay.shape, jnp.float32),
             pltpu.VMEM((spans.bit_length() - 1, heads, key_width, width // heads), jnp.float32),
-            pltpu.SemaphoreType.DMA((spans + 5,)),
+            pltpu.VMEM((width, key_width), jnp.float32),
+            pltpu.SemaphoreType.DMA((spans + 2,)),
         ],
         [pl.BlockSpec(memory_space=pltpu.HBM)] * len(inputs),
     )
 
 
+def load_kernel(count, *refs):
+    copies = [
+        pltpu.make_async_copy(source, target, refs[-1].at[at])
+        for at, (source, target) in enumerate(zip(refs[:count], refs[-1 - count : -1]))
+    ]
+    for copy in copies:
+        copy.start()
+    for copy in copies:
+        copy.wait()
+
+
+def load(arrays, token):
+    count = len(arrays)
+    hbm = pl.BlockSpec(memory_space=pltpu.HBM)
+    return call(
+        functools.partial(load_kernel, count),
+        "load",
+        [*[pltpu.with_memory_space_constraint(array, pltpu.HBM) for array in arrays], token],
+        [(array.shape, array.dtype) for array in arrays],
+        [pltpu.SemaphoreType.DMA((count,))],
+        [*[hbm] * count, HELD],
+    )
+
+
 def local_kernel(first, last, has_token, *refs):
-    q_ref, k_ref, v_ref, sums_ref, totals_ref, weight_ref, local_ref, near_ref = refs[:8]
+    q_ref, k_ref, v_ref, sums_ref, totals_ref, weight_ref, local_ref, near_ref, rest_ref = refs[:9]
     if has_token:
         mixed_ref, done_ref = refs[-2:]
         done_ref[...] = jnp.zeros_like(done_ref)
@@ -180,7 +208,12 @@
     causal = source <= target
     empty = jnp.zeros((half, half), jnp.bfloat16)
     upper = jnp.where(bit_of(place(), 0) == 1, 1.0, 0.0)
-    near = near_ref[: heads * head_width].astype(jnp.bfloat16)
+    size = heads // 2 * head_width
+    near, rest = near_ref[:size], rest_ref[:size]
+    first_core = bit_of(place(), 0) == 0
+    near = jnp.concatenate(
+        [jnp.where(first_core, near, rest), jnp.where(first_core, rest, near)], axis=0
+    ).astype(jnp.bfloat16)
 
     for span in range(first, last):
         tokens = slice(span * SPAN, (span + 1) * SPAN)
@@ -240,7 +273,7 @@
         f"local{first}",
         [*shared, *rest, *tokens],
         [(values.shape[::-1], jnp.float32), ((8, 128), jnp.float32)][: 1 + has_token],
-        aliases={8: 0} if rest else None,
+        aliases={9: 0} if rest else None,
     )
 
 
@@ -260,22 +293,22 @@
 def chip_kernel(mine_ref, other_ref, *refs):
     *message_refs, next_ref, whole_ref = refs
     heads = next_ref.shape[0]
-    width = mine_ref.shape[0] - heads
-    per = width // heads
-    held = whole_ref.shape[0] // per
+    width = whole_ref.shape[0]
+    held = heads // 2
+    per = width // held
     here = place()
     upper = bit_of(here, 0) == 1
     first = first_head((0,), heads)
     for slot in range(held):
-        part = pl.ds(pl.multiple_of((first + slot) * per, 8), per)
+        part = slice(slot * per, (slot + 1) * per)
         total = pl.ds(width + first + slot, 1)
-        whole_ref[slot * per : (slot + 1) * per] = join(
+        whole_ref[part] = join(
             upper, mine_ref[part], mine_ref[total], other_ref[part], other_ref[total]
         )
     other_total = other_ref[width:]
     total = mine_ref[width:] + other_total
     next_ref[...] = jnp.where(upper, other_total, 0.0)
-    half = held * per // 2
+    half = width // 2
     side = bit_of(here, 1)
     cuts = len(message_refs) // 2
     size = half // cuts
@@ -287,7 +320,7 @@
 
 def make_chip(mine, other, heads, cuts):
     rows, lanes = mine.shape
-    half = (rows - heads) // 2
+    half = rows - heads
     *messages, prefix = call(
         chip_kernel,
         "chip",
@@ -490,17 +523,15 @@
     bits = (lax.axis_size("wide") * lax.axis_size("narrow")).bit_length() - 1
     first_level = level_weight.shape[0] - bits
     gain = norm_gain.reshape(heads, per)
-    message, local, sums, totals, queries, keys, values, level_weight, gain = make_states(
-        queries, keys, values, log_decay, level_weight, gain
-    )
-    shared = (queries, keys, values, sums, totals, level_weight, local)
+    keep, send, local, sums, totals, keys, values = make_states(keys, values, log_decay)
     last = bits - 1
     two = 2 * per
     size = two // CUTS
     sides = [(core, side) for core in (0, 1) for side in (0, 1)]
-    other = trade(message, 1)
-    shared = (*shared, other)
-    chunks, give, prefix = make_chip(message, other, heads, CUTS)
+    other, other_rest = trade(send, 1), trade(keep, 1)
+    chunks, give, prefix = make_chip(keep, other, heads, CUTS)
+    queries, level_weight, gain = load([queries, level_weight, gain], chunks[0])
+    shared = (queries, keys, values, sums, totals, level_weight, local, other, other_rest)
     prefixes = [None, prefix]
     found, across = {}, {}
     mixed, at = None, 0

time: 38.3 us -> 38.1 us (level)
  waiting for transfers between devices: 5.87 us -> 4.44 us
  Pallas kernels: 12.3 us -> 13.5 us
    ppermute x16 -> x17, waiting for transfers between devices: 5.87 us -> 4.44 us  [trade(): return lax.ppermute(value, AXES, pairs)]
    pallas_call x19 -> x20, Pallas kernels: 6.78 us -> 8.07 us  [call(): pl.pallas_call(kernel, in_specs=specs, out_specs=[HELD] * len(outputs), o...]
    ppermute x16 -> x17, starting transfers between devices: 19.8 us -> 19.8 us  [trade(): return lax.ppermute(value, AXES, pairs)]
  transfers between devices with their start and end apart: 16 -> 17, of which waited for: 6 -> 6; matrix products, arithmetic and copies ran while one was open for 0% -> 0% of each run, Pallas kernels for 21% -> 24%
where the time goes in v20:
time: 38.1 us; the launch traced here: 37.9 us
  starting transfers between devices  19.8 us (52%)
  Pallas kernels  13.5 us (35%)
  waiting for transfers between devices  4.44 us (12%)
    ppermute x17, starting transfers between devices, trade(): return lax.ppermute(value, AXES, pairs)  19.8 us
    pallas_call x20, Pallas kernels, call(): pl.pallas_call(kernel, in_specs=specs, out_specs=[HELD] * len(outputs), o...  8.07 us
    pallas_call x4, Pallas kernels, finish(): pl.pallas_call(functools.partial(finish_kernel, quarters, first_level, bi...  5.41 us
    ppermute x17, waiting for transfers between devices, trade(): return lax.ppermute(value, AXES, pairs)  4.44 us
  transfers between devices with their start and end apart: 17, of which 6 were waited for; matrix products, arithmetic and copies ran while one was open for 0% of the time, Pallas kernels for 24%

profile of v20, /device:TPU:0, one launch (start us, length us, event | category | flops | bytes accessed | tf_op | source)
XLA Modules:
  0.0 37.9 jit_solution(377921628692938484)
XLA Ops:
  0.0 2.6 %states.1 = (f32[520,128]{1,0:T(8,128)S(1)}, f32[520,128]{1,0:T(8,128)S(1)}, bf16[3,128,1024]{2,1,0:T(8,128)(2,1)S(1)}, f32[2,8,1024]{2,1,0:T(8,128)S(1)}, f32[4...) custom-call(bf16[1024,128]{1,0:T(8,128)(2,1)} %refs_0_.2, ...), custom_call_target="tpu_custom_call" | custom-call | flops 2000000000 | bytes 1000000 | tf_op jit(solution)/shard_map/states/pallas_call | solution.py:50
  3.2 1.1 %collective-permute-done.other_ref.refs_7_ = f32[520,128]{1,0:T(8,128)S(1)} collective-permute-done((f32[520,128]{1,0:T(8,128)S(1)}, f32[520,128]{1,0:T(8,128)S(1)}, u32[]{:S(2)}, u32[]{:S(2)}) %collective-permute-start) | collective-permute-done | bytes 266272 | tf_op jit(solution)/shard_map/ppermute | solution.py:514
  4.4 3.0 %collective-permute-start.2 = (f32[136,128]{1,0:T(8,128)S(1)}, f32[136,128]{1,0:T(8,128)S(1)}, u32[]{:S(2)}, u32[]{:S(2)}) collective-permute-start(f32[136,128]{1,0:T(8,128)S(1)} %get-tuple-element.44), channel_id=1, source_target_pairs={{0,16},{8,24},{16,0},{24,8},{1,17},{9,25},{17,1},{25,9},{2,18},{10... | collective-permute-start | bytes 208904 | tf_op jit(solution)/shard_map/ppermute | solution.py:514
  7.5 1.1 %load.1 = (bf16[1024,128]{1,0:T(8,128)(2,1)S(1)}, f32[8,8,1024]{2,1,0:T(8,128)S(1)}, f32[8,128]{1,0:T(8,128)S(1)}) custom-call(bf16[1024,128]{1,0:T(8,128)(2,1)} %refs_0_.3, f32[8,8,1024]{2,1,0:T(8,128)} %refs_1_.3, f32[8,128]{1,0:T(8,128)} %bitcast.1, f32[136,128]{1,0:T(8,128)S(1)} %get-tuple-element.34.refs_3_.refs_0_), custom_call_target="tpu_custom_call" | custom-call | flops 2000000000 | bytes 1000000 | tf_op jit(solution)/shard_map/load/pallas_call | solution.py:50
  8.5 0.9 %local0.1 = (f32[1024,1024]{1,0:T(8,128)S(1)}, f32[8,128]{1,0:T(8,128)S(1)}) custom-call(bf16[1024,128]{1,0:T(8,128)(2,1)S(1)} %get-tuple-element.35.refs_0_.refs_1_, bf16[1024,128]{1,0:T(8,128)(2,1)S(1)} %get-tuple-element.36.refs_1_, bf16[1024,1024]{1,0:T(8,128)(2,1)S(1)} %get-tuple-element.37.refs_2_, ...), custom_call_target="tpu_custom_call" | custom-call | flops 1000 | bytes 1000000 | tf_op jit(solution)/shard_map/local0/pallas_call | solution.py:50
  9.9 2.2 %collective-permute-start.3 = (f32[136,128]{1,0:T(8,128)S(1)}, f32[136,128]{1,0:T(8,128)S(1)}, u32[]{:S(2)}, u32[]{:S(2)}) collective-permute-start(f32[136,128]{1,0:T(8,128)S(1)} %merge11.1.refs_10_.refs_3_.refs_0_), channel_id=1, source_target_pairs={{0,1},{8,9},{16,17},{24,25},{1,0},{9,8},{17,16},{25,24},{2,3},{10,... | collective-permute-start | bytes 208904 | tf_op jit(solution)/shard_map/ppermute | solution.py:514
  12.2 1.1 %collective-permute-start.6 = (f32[136,128]{1,0:T(8,128)S(1)}, f32[136,128]{1,0:T(8,128)S(1)}, u32[]{:S(2)}, u32[]{:S(2)}) collective-permute-start(f32[136,128]{1,0:T(8,128)S(1)} %get-tuple-element.50.refs_0_.refs_2_), channel_id=1, source_target_pairs={{0,1},{8,9},{16,17},{24,25},{1,0},{9,8},{17,16},{25,24},{2,3},{10,... | collective-permute-start | bytes 208904 | tf_op jit(solution)/shard_map/ppermute | solution.py:514
  13.3 1.5 %collective-permute-start.8 = (f32[256,128]{1,0:T(8,128)S(1)}, f32[256,128]{1,0:T(8,128)S(1)}, u32[]{:S(2)}, u32[]{:S(2)}) collective-permute-start(f32[256,128]{1,0:T(8,128)S(1)} %rest.1), channel_id=1, source_target_pairs={{0,16},{8,24},{16,0},{24,8},{1,17},{9,25},{17,1},{25,9},{2,18},{10... | collective-permute-start | bytes 393224 | tf_op jit(solution)/shard_map/ppermute | solution.py:514
  14.8 1.0 %local1.1 = (f32[1024,1024]{1,0:T(8,128)S(1)}, f32[8,128]{1,0:T(8,128)S(1)}) custom-call(bf16[1024,128]{1,0:T(8,128)(2,1)S(1)} %get-tuple-element.35.refs_0_.refs_1_, bf16[1024,128]{1,0:T(8,128)(2,1)S(1)} %get-tuple-element.36.refs_1_, bf16[1024,1024]{1,0:T(8,128)(2,1)S(1)} %get-tuple-element.37.refs_2_, ...), custom_call_target="tpu_custom_call", output_to_operand_aliasing={{0}: (9, {})} | custom-call | flops 2000000000 | bytes 1000000 | tf_op jit(solution)/shard_map/local1/pallas_call | solution.py:50
  15.9 1.6 %collective-permute-start.5 = (f32[136,128]{1,0:T(8,128)S(1)}, f32[136,128]{1,0:T(8,128)S(1)}, u32[]{:S(2)}, u32[]{:S(2)}) collective-permute-start(f32[136,128]{1,0:T(8,128)S(1)} %merge21.1.refs_3_.refs_0_), channel_id=1, source_target_pairs={{0,2},{8,10},{16,18},{24,26},{1,3},{9,11},{17,19},{25,27},{2,0},{1... | collective-permute-start | bytes 208904 | tf_op jit(solution)/shard_map/ppermute | solution.py:514
  17.5 0.7 %collective-permute-start.7 = (f32[136,128]{1,0:T(8,128)S(1)}, f32[136,128]{1,0:T(8,128)S(1)}, u32[]{:S(2)}, u32[]{:S(2)}) collective-permute-start(f32[136,128]{1,0:T(8,128)S(1)} %get-tuple-element.53.refs_0_.refs_2_), channel_id=1, source_target_pairs={{0,2},{8,10},{16,18},{24,26},{1,3},{9,11},{17,19},{25,27},{2,0},{1... | collective-permute-start | bytes 208904 | tf_op jit(solution)/shard_map/ppermute | solution.py:514
  18.3 1.8 %collective-permute-start.12 = (f32[256,128]{1,0:T(8,128)S(1)}, f32[256,128]{1,0:T(8,128)S(1)}, u32[]{:S(2)}, u32[]{:S(2)}) collective-permute-start(f32[256,128]{1,0:T(8,128)S(1)} %found2.1.refs_2_), channel_id=1, source_target_pairs={{0,16},{8,24},{16,0},{24,8},{1,17},{9,25},{17,1},{25,9},{2,18},{10... | collective-permute-start | bytes 393224 | tf_op jit(solution)/shard_map/ppermute | solution.py:514
  20.3 2.7 %collective-permute-start.10 = (f32[136,128]{1,0:T(8,128)S(1)}, f32[136,128]{1,0:T(8,128)S(1)}, u32[]{:S(2)}, u32[]{:S(2)}) collective-permute-start(f32[136,128]{1,0:T(8,128)S(1)} %merge31.1.refs_3_.refs_10_), channel_id=1, source_target_pairs={{0,4},{8,12},{16,20},{24,28},{1,5},{9,13},{17,21},{25,29},{2,6},{1... | collective-permute-start | bytes 208904 | tf_op jit(solution)/shard_map/ppermute | solution.py:514
  23.0 1.9 %collective-permute-start.9 = (f32[136,128]{1,0:T(8,128)S(1)}, f32[136,128]{1,0:T(8,128)S(1)}, u32[]{:S(2)}, u32[]{:S(2)}) collective-permute-start(f32[136,128]{1,0:T(8,128)S(1)} %get-tuple-element.54.refs_2_), channel_id=1, source_target_pairs={{0,4},{8,12},{16,20},{24,28},{1,5},{9,13},{17,21},{25,29},{2,6},{1... | collective-permute-start | bytes 208904 | tf_op jit(solution)/shard_map/ppermute | solution.py:514
  24.9 0.7 %collective-permute-start.13 = (f32[256,128]{1,0:T(8,128)S(1)}, f32[256,128]{1,0:T(8,128)S(1)}, u32[]{:S(2)}, u32[]{:S(2)}) collective-permute-start(f32[256,128]{1,0:T(8,128)S(1)} %found3.1.refs_11_.refs_4_), channel_id=1, source_target_pairs={{0,16},{8,24},{16,0},{24,8},{1,17},{9,25},{17,1},{25,9},{2,18},{10... | collective-permute-start | bytes 393224 | tf_op jit(solution)/shard_map/ppermute | solution.py:514
  25.6 2.1 %local2.1 = (f32[1024,1024]{1,0:T(8,128)S(1)}, f32[8,128]{1,0:T(8,128)S(1)}) custom-call(bf16[1024,128]{1,0:T(8,128)(2,1)S(1)} %get-tuple-element.35.refs_0_.refs_1_, bf16[1024,128]{1,0:T(8,128)(2,1)S(1)} %get-tuple-element.36.refs_1_, bf16[1024,1024]{1,0:T(8,128)(2,1)S(1)} %get-tuple-element.37.refs_2_, ...), custom_call_target="tpu_custom_call", output_to_operand_aliasing={{0}: (9, {})} | custom-call | flops 1000 | bytes 1000000 | tf_op jit(solution)/shard_map/local2/pallas_call | solution.py:50
  28.3 1.1 %collective-permute-start.11 = (f32[256,128]{1,0:T(8,128)S(1)}, f32[256,128]{1,0:T(8,128)S(1)}, u32[]{:S(2)}, u32[]{:S(2)}) collective-permute-start(f32[256,128]{1,0:T(8,128)S(1)} %state.1.refs_6_.refs_0_.refs_9_), channel_id=1, source_target_pairs={{0,16},{8,24},{16,0},{24,8},{1,17},{9,25},{17,1},{25,9},{2,18},{10... | collective-permute-start | bytes 393224 | tf_op jit(solution)/shard_map/ppermute | solution.py:514
  29.4 1.3 %collective-permute-done.13.refs_5_ = f32[256,128]{1,0:T(8,128)S(1)} collective-permute-done((f32[256,128]{1,0:T(8,128)S(1)}, f32[256,128]{1,0:T(8,128)S(1)}, u32[]{:S(2)}, u32[]{:S(2)}) %collective-permute-start.13) | collective-permute-done | bytes 131104 | tf_op jit(solution)/shard_map/ppermute | solution.py:514
  30.8 0.6 %collective-permute-start.14 = (f32[256,128]{1,0:T(8,128)S(1)}, f32[256,128]{1,0:T(8,128)S(1)}, u32[]{:S(2)}, u32[]{:S(2)}) collective-permute-start(f32[256,128]{1,0:T(8,128)S(1)} %shared.1), channel_id=1, source_target_pairs={{0,8},{8,0},{16,24},{24,16},{1,9},{9,1},{17,25},{25,17},{2,10},{10... | collective-permute-start | bytes 393224 | tf_op jit(solution)/shard_map/ppermute | solution.py:514
  31.3 1.0 %finish00.1.refs_11_ = bf16[1024,256]{1,0:T(8,128)(2,1)S(1)} custom-call(f32[1024,1024]{1,0:T(8,128)S(1)} %get-tuple-element.55.refs_0_, bf16[1024,128]{1,0:T(8,128)(2,1)S(1)} %get-tuple-element.35.refs_0_.refs_1_, f32[2,8,1024]{2,1,0:T(8,128)S(1)} %get-tuple-element.38.refs_3_.refs_2_, f32[8,8,1024]{2,1,0:T(8,128)S(1)} %get-tuple-element.40.refs_5_.refs_3_, ...), custom_call_target="tpu_custom_call" | custom-call | flops 20000000000 | bytes 1000000 | tf_op jit(solution)/shard_map/finish00/pallas_call | solution.py:490
  32.3 0.9 %collective-permute-done.14.refs_9_ = f32[256,128]{1,0:T(8,128)S(1)} collective-permute-done((f32[256,128]{1,0:T(8,128)S(1)}, f32[256,128]{1,0:T(8,128)S(1)}, u32[]{:S(2)}, u32[]{:S(2)}) %collective-permute-start.14) | collective-permute-done | bytes 131104 | tf_op jit(solution)/shard_map/ppermute | solution.py:514
  33.2 1.0 %finish10.1.refs_1_.refs_11_ = bf16[1024,256]{1,0:T(8,128)(2,1)S(1)} custom-call(f32[1024,1024]{1,0:T(8,128)S(1)} %get-tuple-element.55.refs_0_, bf16[1024,128]{1,0:T(8,128)(2,1)S(1)} %get-tuple-element.35.refs_0_.refs_1_, f32[2,8,1024]{2,1,0:T(8,128)S(1)} %get-tuple-element.38.refs_3_.refs_2_, f32[8,8,1024]{2,1,0:T(8,128)S(1)} %get-tuple-element.40.refs_5_.refs_3_, ...), custom_call_target="tpu_custom_call" | custom-call | flops 1000 | bytes 1000000 | tf_op jit(solution)/shard_map/finish10/pallas_call | solution.py:490
  34.4 1.7 %finish01.1.refs_12_ = bf16[1024,1024]{1,0:T(8,128)(2,1)} custom-call(f32[1024,1024]{1,0:T(8,128)S(1)} %get-tuple-element.55.refs_0_, bf16[1024,128]{1,0:T(8,128)(2,1)S(1)} %get-tuple-element.35.refs_0_.refs_1_, f32[2,8,1024]{2,1,0:T(8,128)S(1)} %get-tuple-element.38.refs_3_.refs_2_, f32[8,8,1024]{2,1,0:T(8,128)S(1)} %get-tuple-element.40.refs_5_.refs_3_, ...), custom_call_target="tpu_custom_call" | custom-call | flops 20000000000 | bytes 1000000 | tf_op jit(solution)/shard_map/finish01/pallas_call | solution.py:490
  36.2 1.7 %finish11.1 = bf16[1024,1024]{1,0:T(8,128)(2,1)} custom-call(f32[1024,1024]{1,0:T(8,128)S(1)} %get-tuple-element.55.refs_0_, bf16[1024,128]{1,0:T(8,128)(2,1)S(1)} %get-tuple-element.35.refs_0_.refs_1_, f32[2,8,1024]{2,1,0:T(8,128)S(1)} %get-tuple-element.38.refs_3_.refs_2_, ...), custom_call_target="tpu_custom_call", output_to_operand_aliasing={{}: (12, {})} | custom-call | flops 2000000000 | bytes 1000000 | tf_op jit(solution)/shard_map/finish11/pallas_call | solution.py:490
  (34 shorter events, 2.5 us)
Async XLA Ops:
  2.6 1.7 %collective-permute-start = (f32[520,128]{1,0:T(8,128)S(1)}, f32[520,128]{1,0:T(8,128)S(1)}, u32[]{:S(2)}, u32[]{:S(2)}) collective-permute-start(f32[520,128]{1,0:T(8,128)S(1)} %get-tuple-element.33), channel_id=1, source_target_pairs={{0,8},{8,0},{16,24},{24,16},{1,9},{9,1},{17,25},{25,17},{2,10},{10... | collective-permute-start | bytes 798728 | tf_op jit(solution)/shard_map/ppermute | solution.py:514
  3.2 5.4 %collective-permute-start.1 = (f32[520,128]{1,0:T(8,128)S(1)}, f32[520,128]{1,0:T(8,128)S(1)}, u32[]{:S(2)}, u32[]{:S(2)}) collective-permute-start(f32[520,128]{1,0:T(8,128)S(1)} %get-tuple-element.32.mine_ref), channel_id=1, source_target_pairs={{0,8},{8,0},{16,24},{24,16},{1,9},{9,1},{17,25},{25,17},{2,10},{10... | collective-permute-start | bytes 798728 | tf_op jit(solution)/shard_map/ppermute | solution.py:514
  4.4 5.5 %collective-permute-start.2 = (f32[136,128]{1,0:T(8,128)S(1)}, f32[136,128]{1,0:T(8,128)S(1)}, u32[]{:S(2)}, u32[]{:S(2)}) collective-permute-start(f32[136,128]{1,0:T(8,128)S(1)} %get-tuple-element.44), channel_id=1, source_target_pairs={{0,16},{8,24},{16,0},{24,8},{1,17},{9,25},{17,1},{25,9},{2,18},{10... | collective-permute-start | bytes 208904 | tf_op jit(solution)/shard_map/ppermute | solution.py:514
  7.4 4.8 %collective-permute-start.4 = (f32[136,128]{1,0:T(8,128)S(1)}, f32[136,128]{1,0:T(8,128)S(1)}, u32[]{:S(2)}, u32[]{:S(2)}) collective-permute-start(f32[136,128]{1,0:T(8,128)S(1)} %get-tuple-element.47), channel_id=1, source_target_pairs={{0,16},{8,24},{16,0},{24,8},{1,17},{9,25},{17,1},{25,9},{2,18},{10... | collective-permute-start | bytes 208904 | tf_op jit(solution)/shard_map/ppermute | solution.py:514
  9.9 5.9 %collective-permute-start.3 = (f32[136,128]{1,0:T(8,128)S(1)}, f32[136,128]{1,0:T(8,128)S(1)}, u32[]{:S(2)}, u32[]{:S(2)}) collective-permute-start(f32[136,128]{1,0:T(8,128)S(1)} %merge11.1.refs_10_.refs_3_.refs_0_), channel_id=1, source_target_pairs={{0,1},{8,9},{16,17},{24,25},{1,0},{9,8},{17,16},{25,24},{2,3},{10,... | collective-permute-start | bytes 208904 | tf_op jit(solution)/shard_map/ppermute | solution.py:514
  12.2 5.3 %collective-permute-start.6 = (f32[136,128]{1,0:T(8,128)S(1)}, f32[136,128]{1,0:T(8,128)S(1)}, u32[]{:S(2)}, u32[]{:S(2)}) collective-permute-start(f32[136,128]{1,0:T(8,128)S(1)} %get-tuple-element.50.refs_0_.refs_2_), channel_id=1, source_target_pairs={{0,1},{8,9},{16,17},{24,25},{1,0},{9,8},{17,16},{25,24},{2,3},{10,... | collective-permute-start | bytes 208904 | tf_op jit(solution)/shard_map/ppermute | solution.py:514
  13.3 9.6 %collective-permute-start.8 = (f32[256,128]{1,0:T(8,128)S(1)}, f32[256,128]{1,0:T(8,128)S(1)}, u32[]{:S(2)}, u32[]{:S(2)}) collective-permute-start(f32[256,128]{1,0:T(8,128)S(1)} %rest.1), channel_id=1, source_target_pairs={{0,16},{8,24},{16,0},{24,8},{1,17},{9,25},{17,1},{25,9},{2,18},{10... | collective-permute-start | bytes 393224 | tf_op jit(solution)/shard_map/ppermute | solution.py:514
  15.9 4.4 %collective-permute-start.5 = (f32[136,128]{1,0:T(8,128)S(1)}, f32[136,128]{1,0:T(8,128)S(1)}, u32[]{:S(2)}, u32[]{:S(2)}) collective-permute-start(f32[136,128]{1,0:T(8,128)S(1)} %merge21.1.refs_3_.refs_0_), channel_id=1, source_target_pairs={{0,2},{8,10},{16,18},{24,26},{1,3},{9,11},{17,19},{25,27},{2,0},{1... | collective-permute-start | bytes 208904 | tf_op jit(solution)/shard_map/ppermute | solution.py:514
  17.5 5.4 %collective-permute-start.7 = (f32[136,128]{1,0:T(8,128)S(1)}, f32[136,128]{1,0:T(8,128)S(1)}, u32[]{:S(2)}, u32[]{:S(2)}) collective-permute-start(f32[136,128]{1,0:T(8,128)S(1)} %get-tuple-element.53.refs_0_.refs_2_), channel_id=1, source_target_pairs={{0,2},{8,10},{16,18},{24,26},{1,3},{9,11},{17,19},{25,27},{2,0},{1... | collective-permute-start | bytes 208904 | tf_op jit(solution)/shard_map/ppermute | solution.py:514
  18.3 11.1 %collective-permute-start.12 = (f32[256,128]{1,0:T(8,128)S(1)}, f32[256,128]{1,0:T(8,128)S(1)}, u32[]{:S(2)}, u32[]{:S(2)}) collective-permute-start(f32[256,128]{1,0:T(8,128)S(1)} %found2.1.refs_2_), channel_id=1, source_target_pairs={{0,16},{8,24},{16,0},{24,8},{1,17},{9,25},{17,1},{25,9},{2,18},{10... | collective-permute-start | bytes 393224 | tf_op jit(solution)/shard_map/ppermute | solution.py:514
  20.3 8.0 %collective-permute-start.10 = (f32[136,128]{1,0:T(8,128)S(1)}, f32[136,128]{1,0:T(8,128)S(1)}, u32[]{:S(2)}, u32[]{:S(2)}) collective-permute-start(f32[136,128]{1,0:T(8,128)S(1)} %merge31.1.refs_3_.refs_10_), channel_id=1, source_target_pairs={{0,4},{8,12},{16,20},{24,28},{1,5},{9,13},{17,21},{25,29},{2,6},{1... | collective-permute-start | bytes 208904 | tf_op jit(solution)/shard_map/ppermute | solution.py:514
  23.0 5.3 %collective-permute-start.9 = (f32[136,128]{1,0:T(8,128)S(1)}, f32[136,128]{1,0:T(8,128)S(1)}, u32[]{:S(2)}, u32[]{:S(2)}) collective-permute-start(f32[136,128]{1,0:T(8,128)S(1)} %get-tuple-element.54.refs_2_), channel_id=1, source_target_pairs={{0,4},{8,12},{16,20},{24,28},{1,5},{9,13},{17,21},{25,29},{2,6},{1... | collective-permute-start | bytes 208904 | tf_op jit(solution)/shard_map/ppermute | solution.py:514
  24.9 5.8 %collective-permute-start.13 = (f32[256,128]{1,0:T(8,128)S(1)}, f32[256,128]{1,0:T(8,128)S(1)}, u32[]{:S(2)}, u32[]{:S(2)}) collective-permute-start(f32[256,128]{1,0:T(8,128)S(1)} %found3.1.refs_11_.refs_4_), channel_id=1, source_target_pairs={{0,16},{8,24},{16,0},{24,8},{1,17},{9,25},{17,1},{25,9},{2,18},{10... | collective-permute-start | bytes 393224 | tf_op jit(solution)/shard_map/ppermute | solution.py:514
  28.3 6.0 %collective-permute-start.11 = (f32[256,128]{1,0:T(8,128)S(1)}, f32[256,128]{1,0:T(8,128)S(1)}, u32[]{:S(2)}, u32[]{:S(2)}) collective-permute-start(f32[256,128]{1,0:T(8,128)S(1)} %state.1.refs_6_.refs_0_.refs_9_), channel_id=1, source_target_pairs={{0,16},{8,24},{16,0},{24,8},{1,17},{9,25},{17,1},{25,9},{2,18},{10... | collective-permute-start | bytes 393224 | tf_op jit(solution)/shard_map/ppermute | solution.py:514
  30.7 2.5 %collective-permute-start.15 = (f32[1536,128]{1,0:T(8,128)S(1)}, f32[1536,128]{1,0:T(8,128)S(1)}, u32[]{:S(2)}, u32[]{:S(2)}) collective-permute-start(f32[1536,128]{1,0:T(8,128)S(1)} %near.1.refs_1_.refs_10_), channel_id=1, source_target_pairs={{0,8},{8,0},{16,24},{24,16},{1,9},{9,1},{17,25},{25,17},{2,10},{10... | collective-permute-start | bytes 2359304 | tf_op jit(solution)/shard_map/ppermute | solution.py:514
  30.8 2.4 %collective-permute-start.14 = (f32[256,128]{1,0:T(8,128)S(1)}, f32[256,128]{1,0:T(8,128)S(1)}, u32[]{:S(2)}, u32[]{:S(2)}) collective-permute-start(f32[256,128]{1,0:T(8,128)S(1)} %shared.1), channel_id=1, source_target_pairs={{0,8},{8,0},{16,24},{24,16},{1,9},{9,1},{17,25},{25,17},{2,10},{10... | collective-permute-start | bytes 393224 | tf_op jit(solution)/shard_map/ppermute | solution.py:514
  34.2 1.9 %collective-permute-start.16 = (f32[256,128]{1,0:T(8,128)S(1)}, f32[256,128]{1,0:T(8,128)S(1)}, u32[]{:S(2)}, u32[]{:S(2)}) collective-permute-start(f32[256,128]{1,0:T(8,128)S(1)} %beside.1.refs_9_), channel_id=1, source_target_pairs={{0,8},{8,0},{16,24},{24,16},{1,9},{9,1},{17,25},{25,17},{2,10},{10... | collective-permute-start | bytes 393224 | tf_op jit(solution)/shard_map/ppermute | solution.py:514

commit v21 on v20

--- a/solution.py
+++ b/solution.py
@@ -93,6 +93,7 @@
     for copy in copies:
         copy.start()
     copies[0].wait()
+    copies[1].wait()
     within = running_sums(jnp.concatenate([decay_ref[:, rows] for rows in rows_of], axis=0))
     run = jnp.zeros((heads, 128), jnp.float32)
     fades, wholes = [], []
@@ -106,7 +107,6 @@
         run = run + total
         fades.append(jnp.exp(spread_lanes(last, SPAN) - here))
         wholes.append(jnp.exp(total))
-    copies[1].wait()
     across = [k_ref[rows].astype(jnp.float32).T for rows in rows_of]
     local_bits = spans.bit_length() - 1
     for span, rows in enumerate(rows_of):
@@ -540,7 +540,10 @@
         return pack(name, [(state, size) for state in messages], tokens)
 
     for bit in range(1, bits):
-        found[bit] = [trade(chunk, 2**bit) for chunk in (give if bit == 1 else chunks)]
+        sent = give if bit == 1 else chunks
+        if bit == last:
+            sent = [both("top", chunks)]
+        found[bit] = [trade(chunk, 2**bit) for chunk in sent]
         stays = chunks if bit == 1 else stays
         waits = []
         if bit < 3 or bit == last:
@@ -568,7 +571,7 @@
             else:
                 rest = trade(both("rest", stays, (newest,)), 2)
 
-    state = both("state", found[last], waits)
+    state = pack("state", [(found[last][0], two)], waits)
     beside = trade(state, 2)
     early = list(range(2, last))
     pieces = [(found[1], two), (rest, two)]

time: 38.1 us -> 38.4 us (level)
  waiting for transfers between devices: 4.44 us -> 5.39 us
  starting transfers between devices: 19.8 us -> 19.1 us
    ppermute x17 -> x16, waiting for transfers between devices: 4.44 us -> 5.39 us  [trade(): return lax.ppermute(value, AXES, pairs)]
    ppermute x17 -> x16, starting transfers between devices: 19.8 us -> 19.1 us  [trade(): return lax.ppermute(value, AXES, pairs)]
    pallas_call x20 -> x21, Pallas kernels: 8.07 us -> 8.18 us  [call(): pl.pallas_call(kernel, in_specs=specs, out_specs=[HELD] * len(outputs), o...]
  transfers between devices with their start and end apart: 17 -> 16, of which waited for: 6 -> 7; matrix products, arithmetic and copies ran while one was open for 0% -> 0% of each run, Pallas kernels for 24% -> 24%
where the time goes in v21:
time: 38.4 us; the launch traced here: 38.3 us
  starting transfers between devices  19.1 us (50%)
  Pallas kernels  13.6 us (35%)
  waiting for transfers between devices  5.39 us (14%)
    ppermute x16, starting transfers between devices, trade(): return lax.ppermute(value, AXES, pairs)  19.1 us
    pallas_call x21, Pallas kernels, call(): pl.pallas_call(kernel, in_specs=specs, out_specs=[HELD] * len(outputs), o...  8.18 us
    pallas_call x4, Pallas kernels, finish(): pl.pallas_call(functools.partial(finish_kernel, quarters, first_level, bi...  5.4 us
    ppermute x16, waiting for transfers between devices, trade(): return lax.ppermute(value, AXES, pairs)  5.39 us
  transfers between devices with their start and end apart: 16, of which 7 were waited for; matrix products, arithmetic and copies ran while one was open for 0% of the time, Pallas kernels for 24%

profile of v21, /device:TPU:0, one launch (start us, length us, event | category | flops | bytes accessed | tf_op | source)
XLA Modules:
  0.0 38.3 jit_solution(18259731499131518230)
XLA Ops:
  0.0 2.7 %states.1 = (f32[520,128]{1,0:T(8,128)S(1)}, f32[520,128]{1,0:T(8,128)S(1)}, bf16[3,128,1024]{2,1,0:T(8,128)(2,1)S(1)}, f32[2,8,1024]{2,1,0:T(8,128)S(1)}, f32[4...) custom-call(bf16[1024,128]{1,0:T(8,128)(2,1)} %refs_0_.2, ...), custom_call_target="tpu_custom_call" | custom-call | flops 2000000000 | bytes 1000000 | tf_op jit(solution)/shard_map/states/pallas_call | solution.py:50
  2.7 0.5 %collective-permute-start = (f32[520,128]{1,0:T(8,128)S(1)}, f32[520,128]{1,0:T(8,128)S(1)}, u32[]{:S(2)}, u32[]{:S(2)}) collective-permute-start(f32[520,128]{1,0:T(8,128)S(1)} %get-tuple-element.33), channel_id=1, source_target_pairs={{0,8},{8,0},{16,24},{24,16},{1,9},{9,1},{17,25},{25,17},{2,10},{10... | collective-permute-start | bytes 798728 | tf_op jit(solution)/shard_map/ppermute | solution.py:514
  3.4 1.1 %collective-permute-done.other_ref.refs_7_ = f32[520,128]{1,0:T(8,128)S(1)} collective-permute-done((f32[520,128]{1,0:T(8,128)S(1)}, f32[520,128]{1,0:T(8,128)S(1)}, u32[]{:S(2)}, u32[]{:S(2)}) %collective-permute-start) | collective-permute-done | bytes 266272 | tf_op jit(solution)/shard_map/ppermute | solution.py:514
  4.5 2.9 %collective-permute-start.2 = (f32[136,128]{1,0:T(8,128)S(1)}, f32[136,128]{1,0:T(8,128)S(1)}, u32[]{:S(2)}, u32[]{:S(2)}) collective-permute-start(f32[136,128]{1,0:T(8,128)S(1)} %get-tuple-element.44), channel_id=1, source_target_pairs={{0,16},{8,24},{16,0},{24,8},{1,17},{9,25},{17,1},{25,9},{2,18},{10... | collective-permute-start | bytes 208904 | tf_op jit(solution)/shard_map/ppermute | solution.py:514
  7.6 1.1 %load.1 = (bf16[1024,128]{1,0:T(8,128)(2,1)S(1)}, f32[8,8,1024]{2,1,0:T(8,128)S(1)}, f32[8,128]{1,0:T(8,128)S(1)}) custom-call(bf16[1024,128]{1,0:T(8,128)(2,1)} %refs_0_.3, f32[8,8,1024]{2,1,0:T(8,128)} %refs_1_.3, f32[8,128]{1,0:T(8,128)} %bitcast.1, f32[136,128]{1,0:T(8,128)S(1)} %get-tuple-element.34.refs_3_.refs_0_), custom_call_target="tpu_custom_call" | custom-call | flops 2000000000 | bytes 1000000 | tf_op jit(solution)/shard_map/load/pallas_call | solution.py:50
  8.6 0.9 %local0.1 = (f32[1024,1024]{1,0:T(8,128)S(1)}, f32[8,128]{1,0:T(8,128)S(1)}) custom-call(bf16[1024,128]{1,0:T(8,128)(2,1)S(1)} %get-tuple-element.35.refs_0_.refs_1_, bf16[1024,128]{1,0:T(8,128)(2,1)S(1)} %get-tuple-element.36.refs_1_, bf16[1024,1024]{1,0:T(8,128)(2,1)S(1)} %get-tuple-element.37.refs_2_, ...), custom_call_target="tpu_custom_call" | custom-call | flops 1000 | bytes 1000000 | tf_op jit(solution)/shard_map/local0/pallas_call | solution.py:50
  10.0 2.2 %collective-permute-start.3 = (f32[136,128]{1,0:T(8,128)S(1)}, f32[136,128]{1,0:T(8,128)S(1)}, u32[]{:S(2)}, u32[]{:S(2)}) collective-permute-start(f32[136,128]{1,0:T(8,128)S(1)} %merge11.1.refs_10_.refs_3_.refs_0_), channel_id=1, source_target_pairs={{0,1},{8,9},{16,17},{24,25},{1,0},{9,8},{17,16},{25,24},{2,3},{10,... | collective-permute-start | bytes 208904 | tf_op jit(solution)/shard_map/ppermute | solution.py:514
  12.3 1.1 %collective-permute-start.6 = (f32[136,128]{1,0:T(8,128)S(1)}, f32[136,128]{1,0:T(8,128)S(1)}, u32[]{:S(2)}, u32[]{:S(2)}) collective-permute-start(f32[136,128]{1,0:T(8,128)S(1)} %get-tuple-element.50.refs_0_.refs_2_), channel_id=1, source_target_pairs={{0,1},{8,9},{16,17},{24,25},{1,0},{9,8},{17,16},{25,24},{2,3},{10,... | collective-permute-start | bytes 208904 | tf_op jit(solution)/shard_map/ppermute | solution.py:514
  13.4 1.4 %collective-permute-start.8 = (f32[256,128]{1,0:T(8,128)S(1)}, f32[256,128]{1,0:T(8,128)S(1)}, u32[]{:S(2)}, u32[]{:S(2)}) collective-permute-start(f32[256,128]{1,0:T(8,128)S(1)} %rest.1), channel_id=1, source_target_pairs={{0,16},{8,24},{16,0},{24,8},{1,17},{9,25},{17,1},{25,9},{2,18},{10... | collective-permute-start | bytes 393224 | tf_op jit(solution)/shard_map/ppermute | solution.py:514
  14.8 1.0 %local1.1 = (f32[1024,1024]{1,0:T(8,128)S(1)}, f32[8,128]{1,0:T(8,128)S(1)}) custom-call(bf16[1024,128]{1,0:T(8,128)(2,1)S(1)} %get-tuple-element.35.refs_0_.refs_1_, bf16[1024,128]{1,0:T(8,128)(2,1)S(1)} %get-tuple-element.36.refs_1_, bf16[1024,1024]{1,0:T(8,128)(2,1)S(1)} %get-tuple-element.37.refs_2_, ...), custom_call_target="tpu_custom_call", output_to_operand_aliasing={{0}: (9, {})} | custom-call | flops 2000000000 | bytes 1000000 | tf_op jit(solution)/shard_map/local1/pallas_call | solution.py:50
  15.9 1.6 %collective-permute-start.5 = (f32[136,128]{1,0:T(8,128)S(1)}, f32[136,128]{1,0:T(8,128)S(1)}, u32[]{:S(2)}, u32[]{:S(2)}) collective-permute-start(f32[136,128]{1,0:T(8,128)S(1)} %merge21.1.refs_3_.refs_0_), channel_id=1, source_target_pairs={{0,2},{8,10},{16,18},{24,26},{1,3},{9,11},{17,19},{25,27},{2,0},{1... | collective-permute-start | bytes 208904 | tf_op jit(solution)/shard_map/ppermute | solution.py:514
  17.6 0.8 %collective-permute-start.7 = (f32[136,128]{1,0:T(8,128)S(1)}, f32[136,128]{1,0:T(8,128)S(1)}, u32[]{:S(2)}, u32[]{:S(2)}) collective-permute-start(f32[136,128]{1,0:T(8,128)S(1)} %get-tuple-element.53.refs_0_.refs_2_), channel_id=1, source_target_pairs={{0,2},{8,10},{16,18},{24,26},{1,3},{9,11},{17,19},{25,27},{2,0},{1... | collective-permute-start | bytes 208904 | tf_op jit(solution)/shard_map/ppermute | solution.py:514
  18.4 1.8 %collective-permute-start.11 = (f32[256,128]{1,0:T(8,128)S(1)}, f32[256,128]{1,0:T(8,128)S(1)}, u32[]{:S(2)}, u32[]{:S(2)}) collective-permute-start(f32[256,128]{1,0:T(8,128)S(1)} %found2.1.refs_2_), channel_id=1, source_target_pairs={{0,16},{8,24},{16,0},{24,8},{1,17},{9,25},{17,1},{25,9},{2,18},{10... | collective-permute-start | bytes 393224 | tf_op jit(solution)/shard_map/ppermute | solution.py:514
  20.3 1.6 %collective-permute-done.7.refs_1_.refs_0_ = f32[136,128]{1,0:T(8,128)S(1)} collective-permute-done((f32[136,128]{1,0:T(8,128)S(1)}, f32[136,128]{1,0:T(8,128)S(1)}, u32[]{:S(2)}, u32[]{:S(2)}) %collective-permute-start.7) | collective-permute-done | bytes 69664 | tf_op jit(solution)/shard_map/ppermute | solution.py:514
  22.0 3.4 %collective-permute-start.9 = (f32[256,128]{1,0:T(8,128)S(1)}, f32[256,128]{1,0:T(8,128)S(1)}, u32[]{:S(2)}, u32[]{:S(2)}) collective-permute-start(f32[256,128]{1,0:T(8,128)S(1)} %top.1), channel_id=1, source_target_pairs={{0,4},{8,12},{16,20},{24,28},{1,5},{9,13},{17,21},{25,29},{2,6},{1... | collective-permute-start | bytes 393224 | tf_op jit(solution)/shard_map/ppermute | solution.py:514
  25.4 1.0 %collective-permute-start.12 = (f32[256,128]{1,0:T(8,128)S(1)}, f32[256,128]{1,0:T(8,128)S(1)}, u32[]{:S(2)}, u32[]{:S(2)}) collective-permute-start(f32[256,128]{1,0:T(8,128)S(1)} %found3.1.refs_11_.refs_4_), channel_id=1, source_target_pairs={{0,16},{8,24},{16,0},{24,8},{1,17},{9,25},{17,1},{25,9},{2,18},{10... | collective-permute-start | bytes 393224 | tf_op jit(solution)/shard_map/ppermute | solution.py:514
  26.5 2.1 %local2.1 = (f32[1024,1024]{1,0:T(8,128)S(1)}, f32[8,128]{1,0:T(8,128)S(1)}) custom-call(bf16[1024,128]{1,0:T(8,128)(2,1)S(1)} %get-tuple-element.35.refs_0_.refs_1_, bf16[1024,128]{1,0:T(8,128)(2,1)S(1)} %get-tuple-element.36.refs_1_, bf16[1024,1024]{1,0:T(8,128)(2,1)S(1)} %get-tuple-element.37.refs_2_, ...), custom_call_target="tpu_custom_call", output_to_operand_aliasing={{0}: (9, {})} | custom-call | flops 1000 | bytes 1000000 | tf_op jit(solution)/shard_map/local2/pallas_call | solution.py:50
  28.6 1.0 %collective-permute-done.9.refs_0_ = f32[256,128]{1,0:T(8,128)S(1)} collective-permute-done((f32[256,128]{1,0:T(8,128)S(1)}, f32[256,128]{1,0:T(8,128)S(1)}, u32[]{:S(2)}, u32[]{:S(2)}) %collective-permute-start.9) | collective-permute-done | bytes 131104 | tf_op jit(solution)/shard_map/ppermute | solution.py:514
  29.5 1.3 %collective-permute-start.10 = (f32[256,128]{1,0:T(8,128)S(1)}, f32[256,128]{1,0:T(8,128)S(1)}, u32[]{:S(2)}, u32[]{:S(2)}) collective-permute-start(f32[256,128]{1,0:T(8,128)S(1)} %state.1.refs_6_.refs_0_.refs_9_), channel_id=1, source_target_pairs={{0,16},{8,24},{16,0},{24,8},{1,17},{9,25},{17,1},{25,9},{2,18},{10... | collective-permute-start | bytes 393224 | tf_op jit(solution)/shard_map/ppermute | solution.py:514
  31.6 1.0 %finish00.1.refs_11_ = bf16[1024,256]{1,0:T(8,128)(2,1)S(1)} custom-call(f32[1024,1024]{1,0:T(8,128)S(1)} %get-tuple-element.55.refs_0_, bf16[1024,128]{1,0:T(8,128)(2,1)S(1)} %get-tuple-element.35.refs_0_.refs_1_, f32[2,8,1024]{2,1,0:T(8,128)S(1)} %get-tuple-element.38.refs_3_.refs_2_, f32[8,8,1024]{2,1,0:T(8,128)S(1)} %get-tuple-element.40.refs_5_.refs_3_, ...), custom_call_target="tpu_custom_call" | custom-call | flops 20000000000 | bytes 1000000 | tf_op jit(solution)/shard_map/finish00/pallas_call | solution.py:490
  32.6 1.0 %collective-permute-done.13.refs_9_ = f32[256,128]{1,0:T(8,128)S(1)} collective-permute-done((f32[256,128]{1,0:T(8,128)S(1)}, f32[256,128]{1,0:T(8,128)S(1)}, u32[]{:S(2)}, u32[]{:S(2)}) %collective-permute-start.13) | collective-permute-done | bytes 131104 | tf_op jit(solution)/shard_map/ppermute | solution.py:514
  33.6 1.0 %finish10.1.refs_1_.refs_11_ = bf16[1024,256]{1,0:T(8,128)(2,1)S(1)} custom-call(f32[1024,1024]{1,0:T(8,128)S(1)} %get-tuple-element.55.refs_0_, bf16[1024,128]{1,0:T(8,128)(2,1)S(1)} %get-tuple-element.35.refs_0_.refs_1_, f32[2,8,1024]{2,1,0:T(8,128)S(1)} %get-tuple-element.38.refs_3_.refs_2_, f32[8,8,1024]{2,1,0:T(8,128)S(1)} %get-tuple-element.40.refs_5_.refs_3_, ...), custom_call_target="tpu_custom_call" | custom-call | flops 1000 | bytes 1000000 | tf_op jit(solution)/shard_map/finish10/pallas_call | solution.py:490
  34.8 1.7 %finish01.1.refs_12_ = bf16[1024,1024]{1,0:T(8,128)(2,1)} custom-call(f32[1024,1024]{1,0:T(8,128)S(1)} %get-tuple-element.55.refs_0_, bf16[1024,128]{1,0:T(8,128)(2,1)S(1)} %get-tuple-element.35.refs_0_.refs_1_, f32[2,8,1024]{2,1,0:T(8,128)S(1)} %get-tuple-element.38.refs_3_.refs_2_, f32[8,8,1024]{2,1,0:T(8,128)S(1)} %get-tuple-element.40.refs_5_.refs_3_, ...), custom_call_target="tpu_custom_call" | custom-call | flops 20000000000 | bytes 1000000 | tf_op jit(solution)/shard_map/finish01/pallas_call | solution.py:490
  36.5 1.7 %finish11.1 = bf16[1024,1024]{1,0:T(8,128)(2,1)} custom-call(f32[1024,1024]{1,0:T(8,128)S(1)} %get-tuple-element.55.refs_0_, bf16[1024,128]{1,0:T(8,128)(2,1)S(1)} %get-tuple-element.35.refs_0_.refs_1_, f32[2,8,1024]{2,1,0:T(8,128)S(1)} %get-tuple-element.38.refs_3_.refs_2_, ...), custom_call_target="tpu_custom_call", output_to_operand_aliasing={{}: (12, {})} | custom-call | flops 2000000000 | bytes 1000000 | tf_op jit(solution)/shard_map/finish11/pallas_call | solution.py:490
  (33 shorter events, 2.0 us)
Async XLA Ops:
  2.7 1.7 %collective-permute-start = (f32[520,128]{1,0:T(8,128)S(1)}, f32[520,128]{1,0:T(8,128)S(1)}, u32[]{:S(2)}, u32[]{:S(2)}) collective-permute-start(f32[520,128]{1,0:T(8,128)S(1)} %get-tuple-element.33), channel_id=1, source_target_pairs={{0,8},{8,0},{16,24},{24,16},{1,9},{9,1},{17,25},{25,17},{2,10},{10... | collective-permute-start | bytes 798728 | tf_op jit(solution)/shard_map/ppermute | solution.py:514
  3.3 5.4 %collective-permute-start.1 = (f32[520,128]{1,0:T(8,128)S(1)}, f32[520,128]{1,0:T(8,128)S(1)}, u32[]{:S(2)}, u32[]{:S(2)}) collective-permute-start(f32[520,128]{1,0:T(8,128)S(1)} %get-tuple-element.32.mine_ref), channel_id=1, source_target_pairs={{0,8},{8,0},{16,24},{24,16},{1,9},{9,1},{17,25},{25,17},{2,10},{10... | collective-permute-start | bytes 798728 | tf_op jit(solution)/shard_map/ppermute | solution.py:514
  4.5 5.5 %collective-permute-start.2 = (f32[136,128]{1,0:T(8,128)S(1)}, f32[136,128]{1,0:T(8,128)S(1)}, u32[]{:S(2)}, u32[]{:S(2)}) collective-permute-start(f32[136,128]{1,0:T(8,128)S(1)} %get-tuple-element.44), channel_id=1, source_target_pairs={{0,16},{8,24},{16,0},{24,8},{1,17},{9,25},{17,1},{25,9},{2,18},{10... | collective-permute-start | bytes 208904 | tf_op jit(solution)/shard_map/ppermute | solution.py:514
  7.5 4.8 %collective-permute-start.4 = (f32[136,128]{1,0:T(8,128)S(1)}, f32[136,128]{1,0:T(8,128)S(1)}, u32[]{:S(2)}, u32[]{:S(2)}) collective-permute-start(f32[136,128]{1,0:T(8,128)S(1)} %get-tuple-element.47), channel_id=1, source_target_pairs={{0,16},{8,24},{16,0},{24,8},{1,17},{9,25},{17,1},{25,9},{2,18},{10... | collective-permute-start | bytes 208904 | tf_op jit(solution)/shard_map/ppermute | solution.py:514
  10.0 5.8 %collective-permute-start.3 = (f32[136,128]{1,0:T(8,128)S(1)}, f32[136,128]{1,0:T(8,128)S(1)}, u32[]{:S(2)}, u32[]{:S(2)}) collective-permute-start(f32[136,128]{1,0:T(8,128)S(1)} %merge11.1.refs_10_.refs_3_.refs_0_), channel_id=1, source_target_pairs={{0,1},{8,9},{16,17},{24,25},{1,0},{9,8},{17,16},{25,24},{2,3},{10,... | collective-permute-start | bytes 208904 | tf_op jit(solution)/shard_map/ppermute | solution.py:514
  12.3 5.2 %collective-permute-start.6 = (f32[136,128]{1,0:T(8,128)S(1)}, f32[136,128]{1,0:T(8,128)S(1)}, u32[]{:S(2)}, u32[]{:S(2)}) collective-permute-start(f32[136,128]{1,0:T(8,128)S(1)} %get-tuple-element.50.refs_0_.refs_2_), channel_id=1, source_target_pairs={{0,1},{8,9},{16,17},{24,25},{1,0},{9,8},{17,16},{25,24},{2,3},{10,... | collective-permute-start | bytes 208904 | tf_op jit(solution)/shard_map/ppermute | solution.py:514
  13.4 6.9 %collective-permute-start.8 = (f32[256,128]{1,0:T(8,128)S(1)}, f32[256,128]{1,0:T(8,128)S(1)}, u32[]{:S(2)}, u32[]{:S(2)}) collective-permute-start(f32[256,128]{1,0:T(8,128)S(1)} %rest.1), channel_id=1, source_target_pairs={{0,16},{8,24},{16,0},{24,8},{1,17},{9,25},{17,1},{25,9},{2,18},{10... | collective-permute-start | bytes 393224 | tf_op jit(solution)/shard_map/ppermute | solution.py:514
  15.9 4.4 %collective-permute-start.5 = (f32[136,128]{1,0:T(8,128)S(1)}, f32[136,128]{1,0:T(8,128)S(1)}, u32[]{:S(2)}, u32[]{:S(2)}) collective-permute-start(f32[136,128]{1,0:T(8,128)S(1)} %merge21.1.refs_3_.refs_0_), channel_id=1, source_target_pairs={{0,2},{8,10},{16,18},{24,26},{1,3},{9,11},{17,19},{25,27},{2,0},{1... | collective-permute-start | bytes 208904 | tf_op jit(solution)/shard_map/ppermute | solution.py:514
  17.6 4.4 %collective-permute-start.7 = (f32[136,128]{1,0:T(8,128)S(1)}, f32[136,128]{1,0:T(8,128)S(1)}, u32[]{:S(2)}, u32[]{:S(2)}) collective-permute-start(f32[136,128]{1,0:T(8,128)S(1)} %get-tuple-element.53.refs_0_.refs_2_), channel_id=1, source_target_pairs={{0,2},{8,10},{16,18},{24,26},{1,3},{9,11},{17,19},{25,27},{2,0},{1... | collective-permute-start | bytes 208904 | tf_op jit(solution)/shard_map/ppermute | solution.py:514
  18.4 12.4 %collective-permute-start.11 = (f32[256,128]{1,0:T(8,128)S(1)}, f32[256,128]{1,0:T(8,128)S(1)}, u32[]{:S(2)}, u32[]{:S(2)}) collective-permute-start(f32[256,128]{1,0:T(8,128)S(1)} %found2.1.refs_2_), channel_id=1, source_target_pairs={{0,16},{8,24},{16,0},{24,8},{1,17},{9,25},{17,1},{25,9},{2,18},{10... | collective-permute-start | bytes 393224 | tf_op jit(solution)/shard_map/ppermute | solution.py:514
  22.0 7.5 %collective-permute-start.9 = (f32[256,128]{1,0:T(8,128)S(1)}, f32[256,128]{1,0:T(8,128)S(1)}, u32[]{:S(2)}, u32[]{:S(2)}) collective-permute-start(f32[256,128]{1,0:T(8,128)S(1)} %top.1), channel_id=1, source_target_pairs={{0,4},{8,12},{16,20},{24,28},{1,5},{9,13},{17,21},{25,29},{2,6},{1... | collective-permute-start | bytes 393224 | tf_op jit(solution)/shard_map/ppermute | solution.py:514
  25.4 5.6 %collective-permute-start.12 = (f32[256,128]{1,0:T(8,128)S(1)}, f32[256,128]{1,0:T(8,128)S(1)}, u32[]{:S(2)}, u32[]{:S(2)}) collective-permute-start(f32[256,128]{1,0:T(8,128)S(1)} %found3.1.refs_11_.refs_4_), channel_id=1, source_target_pairs={{0,16},{8,24},{16,0},{24,8},{1,17},{9,25},{17,1},{25,9},{2,18},{10... | collective-permute-start | bytes 393224 | tf_op jit(solution)/shard_map/ppermute | solution.py:514
  29.5 5.0 %collective-permute-start.10 = (f32[256,128]{1,0:T(8,128)S(1)}, f32[256,128]{1,0:T(8,128)S(1)}, u32[]{:S(2)}, u32[]{:S(2)}) collective-permute-start(f32[256,128]{1,0:T(8,128)S(1)} %state.1.refs_6_.refs_0_.refs_9_), channel_id=1, source_target_pairs={{0,16},{8,24},{16,0},{24,8},{1,17},{9,25},{17,1},{25,9},{2,18},{10... | collective-permute-start | bytes 393224 | tf_op jit(solution)/shard_map/ppermute | solution.py:514
  31.0 2.5 %collective-permute-start.14 = (f32[1536,128]{1,0:T(8,128)S(1)}, f32[1536,128]{1,0:T(8,128)S(1)}, u32[]{:S(2)}, u32[]{:S(2)}) collective-permute-start(f32[1536,128]{1,0:T(8,128)S(1)} %near.1.refs_1_.refs_10_), channel_id=1, source_target_pairs={{0,8},{8,0},{16,24},{24,16},{1,9},{9,1},{17,25},{25,17},{2,10},{10... | collective-permute-start | bytes 2359304 | tf_op jit(solution)/shard_map/ppermute | solution.py:514
  31.1 2.5 %collective-permute-start.13 = (f32[256,128]{1,0:T(8,128)S(1)}, f32[256,128]{1,0:T(8,128)S(1)}, u32[]{:S(2)}, u32[]{:S(2)}) collective-permute-start(f32[256,128]{1,0:T(8,128)S(1)} %shared.1), channel_id=1, source_target_pairs={{0,8},{8,0},{16,24},{24,16},{1,9},{9,1},{17,25},{25,17},{2,10},{10... | collective-permute-start | bytes 393224 | tf_op jit(solution)/shard_map/ppermute | solution.py:514
  34.6 1.9 %collective-permute-start.15 = (f32[256,128]{1,0:T(8,128)S(1)}, f32[256,128]{1,0:T(8,128)S(1)}, u32[]{:S(2)}, u32[]{:S(2)}) collective-permute-start(f32[256,128]{1,0:T(8,128)S(1)} %beside.1.refs_9_), channel_id=1, source_target_pairs={{0,8},{8,0},{16,24},{24,16},{1,9},{9,1},{17,25},{25,17},{2,10},{10... | collective-permute-start | bytes 393224 | tf_op jit(solution)/shard_map/ppermute | solution.py:514

commit v22 on v20

--- a/solution.py
+++ b/solution.py
@@ -10,6 +10,7 @@
 SPAN = 256
 SPLIT_BITS = 2
 CUTS = 2
+LOADS = 4
 EPS = 1e-05
 AXES = ("narrow", "wide")
 NT = (((1,), (1,)), ((), ()))
@@ -85,7 +86,9 @@
     spans = tokens // SPAN
     rows_of = [slice(span * SPAN, (span + 1) * SPAN) for span in range(spans)]
     loads = [(decay_hbm, decay_ref), (k_hbm, k_ref)]
-    loads += [(v_hbm.at[rows], v_ref.at[rows]) for rows in rows_of]
+    step = SPAN // LOADS
+    pieces = [slice(start, start + step) for start in range(0, tokens, step)]
+    loads += [(v_hbm.at[rows], v_ref.at[rows]) for rows in pieces]
     copies = [
         pltpu.make_async_copy(source, target, arrived.at[at])
         for at, (source, target) in enumerate(loads)
@@ -93,6 +96,7 @@
     for copy in copies:
         copy.start()
     copies[0].wait()
+    copies[1].wait()
     within = running_sums(jnp.concatenate([decay_ref[:, rows] for rows in rows_of], axis=0))
     run = jnp.zeros((heads, 128), jnp.float32)
     fades, wholes = [], []
@@ -106,11 +110,11 @@
         run = run + total
         fades.append(jnp.exp(spread_lanes(last, SPAN) - here))
         wholes.append(jnp.exp(total))
-    copies[1].wait()
     across = [k_ref[rows].astype(jnp.float32).T for rows in rows_of]
     local_bits = spans.bit_length() - 1
     for span, rows in enumerate(rows_of):
-        copies[2 + span].wait()
+        for copy in copies[2 + span * LOADS : 2 + (span + 1) * LOADS]:
+            copy.wait()
         for head in range(heads):
             columns = slice(head * head_width, (head + 1) * head_width)
             faded = (across[span] * fades[span][head : head + 1]).astype(jnp.bfloat16)
@@ -161,7 +165,7 @@
             pltpu.VMEM(log_decay.shape, jnp.float32),
             pltpu.VMEM((spans.bit_length() - 1, heads, key_width, width // heads), jnp.float32),
             pltpu.VMEM((width, key_width), jnp.float32),
-            pltpu.SemaphoreType.DMA((spans + 2,)),
+            pltpu.SemaphoreType.DMA((LOADS * spans + 2,)),
         ],
         [pl.BlockSpec(memory_space=pltpu.HBM)] * len(inputs),
     )
@@ -415,26 +419,22 @@
     mixed_ref, q_ref, sums_ref, weight_ref, gain_ref = refs[:5]
     prefix_refs = refs[5 : 5 + len(bits)]
     part_refs = refs[5 + len(bits) :]
-    out_refs, (own_ref, scale_ref, sent) = refs[-3 - FINISH_OUTS[stays, carried] : -3], refs[-3:]
+    out_ref, own_ref, scale_ref, sent = refs[-4:]
     if stays:
-        own_ref = out_refs[-1]
+        own_ref = out_ref
     heads = weight_ref.shape[1]
     head_width = mixed_ref.shape[0] // heads
     size = heads // 4 * head_width
     copies = []
-
-    def send(block, far, rows):
-        columns = pl.ds(pl.multiple_of(first_head(far, heads) * head_width, 128), size)
-        copy = pltpu.make_async_copy(
-            block.at[rows], out_refs[0].at[rows, columns], sent.at[len(copies)]
-        )
-        copy.start()
-        copies.append(copy)
-
-    if carried is not None:
-        index, far = carried
-        for start in range(0, q_ref.shape[0], SPAN):
-            send(part_refs[index], far, slice(start, start + SPAN))
+    far = quarters[0][0]
+    base = 0
+    if not stays:
+        side = jnp.bitwise_xor(bit_of(place(), 1), far[1])
+        base = side * size
+        left = pl.ds(pl.multiple_of((1 - side) * size, 128), size)
+        own_ref[:, left] = part_refs[carried][...]
+        half = pl.ds(pl.multiple_of(first_head(far[:1], heads) * head_width, 128), 2 * size)
+
     work = gather_work(quarters, part_refs, heads, head_width)
     gains = []
     for head, _ in work:
@@ -452,16 +452,16 @@
             mixed = add_found(mixed_ref[rows, tokens], queries, head, states, scale_ref)
             square = jnp.mean(mixed * mixed, axis=0, keepdims=True)
             normed = mixed * lax.rsqrt(square + EPS) * gains[at]
-            columns = slice(at * head_width, (at + 1) * head_width)
+            columns = pl.ds(pl.multiple_of(base + at * head_width, 128), head_width)
             own_ref[tokens, columns] = normed.astype(jnp.bfloat16).T
         if not stays:
-            for start in range(tokens.start, tokens.stop, SPAN // 2):
-                send(own_ref, quarters[0][0], slice(start, start + SPAN // 2))
+            copy = pltpu.make_async_copy(
+                own_ref.at[tokens], out_ref.at[tokens, half], sent.at[span]
+            )
+            copy.start()
+            copies.append(copy)
     for copy in copies:
         copy.wait()
-
-
-FINISH_OUTS = {}
 
 
 def finish(quarters, first_level, bits, shared, prefixes, parts, begun, stays, carried):
@@ -479,23 +479,19 @@
         inputs.append(begun)
     name = "finish" + "".join(f"{core}{side}" for (core, side), _ in quarters)
     block = (tokens, width // 4)
-    out_specs, shapes = [], []
-    if carried is not None or not stays:
-        out_specs.append(hbm)
-        shapes.append(jax.ShapeDtypeStruct((tokens, width), jnp.bfloat16))
     if stays:
-        out_specs.append(HELD)
-        shapes.append(pltpu.VMEM(block, jnp.bfloat16))
-    FINISH_OUTS[stays, carried] = len(shapes)
+        out_spec, shape = HELD, pltpu.VMEM(block, jnp.bfloat16)
+    else:
+        out_spec, shape = hbm, jax.ShapeDtypeStruct((tokens, width), jnp.bfloat16)
     return pl.pallas_call(
         functools.partial(finish_kernel, quarters, first_level, bits, stays, carried),
         in_specs=specs,
-        out_specs=out_specs,
-        out_shape=shapes,
+        out_specs=out_spec,
+        out_shape=shape,
         scratch_shapes=[
-            pltpu.VMEM((8, 128) if stays else block, jnp.bfloat16),
+            pltpu.VMEM((8, 128) if stays else (tokens, width // 2), jnp.bfloat16),
             pltpu.VMEM((len(bits), heads, SPAN), jnp.float32),
-            pltpu.SemaphoreType.DMA((3 * tokens // SPAN,)),
+            pltpu.SemaphoreType.DMA((tokens // SPAN,)),
         ],
         input_output_aliases=aliases,
         compiler_params=PARAMS,
@@ -586,18 +582,16 @@
     every = (first_level, [last, *middle], shared, [prefixes[last], *ahead])
     quarters = {(core, side): [(0, 0, 0), *states_of(side, 1, 1)] for core, side in sides}
     state_far = trade(pack("shared", [(state, two)], (near,)), 1)
-    (block,) = finish([((0, 0), quarters[0, 0])], *every, [state, near], None, True, None)
-    (block_far,) = finish(
+    block = finish([((0, 0), quarters[0, 0])], *every, [state, near], None, True, None)
+    block_far = finish(
         [((1, 0), quarters[1, 0])], *every, [state_far, far, block], None, True, None
     )
     beside = pack("beside", [(beside, two)], (block_far,))
-    (out,) = finish(
-        [((0, 1), quarters[0, 1])], *every, [beside, near, block], None, False, (2, (0, 0))
-    )
+    out = finish([((0, 1), quarters[0, 1])], *every, [beside, near, block], None, False, 2)
     beside_far = trade(beside, 1)
     return finish(
-        [((1, 1), quarters[1, 1])], *every, [beside_far, far, block_far], out, False, (2, (1, 0))
-    )[0]
+        [((1, 1), quarters[1, 1])], *every, [beside_far, far, block_far], out, False, 2
+    )
 
 
 def solution(mesh):

time: 38.1 us -> 38.2 us (level)
  no operation moved by 1% of the time
where the time goes in v22:
time: 38.2 us; the launch traced here: 38.1 us
  starting transfers between devices  19.8 us (52%)
  Pallas kernels  13.6 us (36%)
  waiting for transfers between devices  4.45 us (12%)
    ppermute x17, starting transfers between devices, trade(): return lax.ppermute(value, AXES, pairs)  19.8 us
    pallas_call x20, Pallas kernels, call(): pl.pallas_call(kernel, in_specs=specs, out_specs=[HELD] * len(outputs), o...  8.29 us
    pallas_call x4, Pallas kernels, finish(): pl.pallas_call(functools.partial(finish_kernel, quarters, first_level, bi...  5.29 us
    ppermute x17, waiting for transfers between devices, trade(): return lax.ppermute(value, AXES, pairs)  4.45 us
  transfers between devices with their start and end apart: 17, of which 6 were waited for; matrix products, arithmetic and copies ran while one was open for 0% of the time, Pallas kernels for 24%

profile of v22, /device:TPU:0, one launch (start us, length us, event | category | flops | bytes accessed | tf_op | source)
XLA Modules:
  0.0 38.1 jit_solution(6690548285766469448)
XLA Ops:
  0.0 2.9 %states.1 = (f32[520,128]{1,0:T(8,128)S(1)}, f32[520,128]{1,0:T(8,128)S(1)}, bf16[3,128,1024]{2,1,0:T(8,128)(2,1)S(1)}, f32[2,8,1024]{2,1,0:T(8,128)S(1)}, f32[4...) custom-call(bf16[1024,128]{1,0:T(8,128)(2,1)} %refs_0_.2, ...), custom_call_target="tpu_custom_call" | custom-call | flops 2000000000 | bytes 1000000 | tf_op jit(solution)/shard_map/states/pallas_call | solution.py:51
  3.5 1.1 %collective-permute-done.other_ref.refs_7_ = f32[520,128]{1,0:T(8,128)S(1)} collective-permute-done((f32[520,128]{1,0:T(8,128)S(1)}, f32[520,128]{1,0:T(8,128)S(1)}, u32[]{:S(2)}, u32[]{:S(2)}) %collective-permute-start) | collective-permute-done | bytes 266272 | tf_op jit(solution)/shard_map/ppermute | solution.py:510
  4.7 2.9 %collective-permute-start.2 = (f32[136,128]{1,0:T(8,128)S(1)}, f32[136,128]{1,0:T(8,128)S(1)}, u32[]{:S(2)}, u32[]{:S(2)}) collective-permute-start(f32[136,128]{1,0:T(8,128)S(1)} %get-tuple-element.44), channel_id=1, source_target_pairs={{0,16},{8,24},{16,0},{24,8},{1,17},{9,25},{17,1},{25,9},{2,18},{10... | collective-permute-start | bytes 208904 | tf_op jit(solution)/shard_map/ppermute | solution.py:510
  7.7 1.1 %load.1 = (bf16[1024,128]{1,0:T(8,128)(2,1)S(1)}, f32[8,8,1024]{2,1,0:T(8,128)S(1)}, f32[8,128]{1,0:T(8,128)S(1)}) custom-call(bf16[1024,128]{1,0:T(8,128)(2,1)} %refs_0_.3, f32[8,8,1024]{2,1,0:T(8,128)} %refs_1_.3, f32[8,128]{1,0:T(8,128)} %bitcast.1, f32[136,128]{1,0:T(8,128)S(1)} %get-tuple-element.34.refs_3_.refs_0_), custom_call_target="tpu_custom_call" | custom-call | flops 2000000000 | bytes 1000000 | tf_op jit(solution)/shard_map/load/pallas_call | solution.py:51
  8.8 0.9 %local0.1 = (f32[1024,1024]{1,0:T(8,128)S(1)}, f32[8,128]{1,0:T(8,128)S(1)}) custom-call(bf16[1024,128]{1,0:T(8,128)(2,1)S(1)} %get-tuple-element.35.refs_0_.refs_1_, bf16[1024,128]{1,0:T(8,128)(2,1)S(1)} %get-tuple-element.36.refs_1_, bf16[1024,1024]{1,0:T(8,128)(2,1)S(1)} %get-tuple-element.37.refs_2_, ...), custom_call_target="tpu_custom_call" | custom-call | flops 1000 | bytes 1000000 | tf_op jit(solution)/shard_map/local0/pallas_call | solution.py:51
  10.2 2.2 %collective-permute-start.3 = (f32[136,128]{1,0:T(8,128)S(1)}, f32[136,128]{1,0:T(8,128)S(1)}, u32[]{:S(2)}, u32[]{:S(2)}) collective-permute-start(f32[136,128]{1,0:T(8,128)S(1)} %merge11.1.refs_10_.refs_3_.refs_0_), channel_id=1, source_target_pairs={{0,1},{8,9},{16,17},{24,25},{1,0},{9,8},{17,16},{25,24},{2,3},{10,... | collective-permute-start | bytes 208904 | tf_op jit(solution)/shard_map/ppermute | solution.py:510
  12.4 1.1 %collective-permute-start.6 = (f32[136,128]{1,0:T(8,128)S(1)}, f32[136,128]{1,0:T(8,128)S(1)}, u32[]{:S(2)}, u32[]{:S(2)}) collective-permute-start(f32[136,128]{1,0:T(8,128)S(1)} %get-tuple-element.50.refs_0_.refs_2_), channel_id=1, source_target_pairs={{0,1},{8,9},{16,17},{24,25},{1,0},{9,8},{17,16},{25,24},{2,3},{10,... | collective-permute-start | bytes 208904 | tf_op jit(solution)/shard_map/ppermute | solution.py:510
  13.5 1.5 %collective-permute-start.8 = (f32[256,128]{1,0:T(8,128)S(1)}, f32[256,128]{1,0:T(8,128)S(1)}, u32[]{:S(2)}, u32[]{:S(2)}) collective-permute-start(f32[256,128]{1,0:T(8,128)S(1)} %rest.1), channel_id=1, source_target_pairs={{0,16},{8,24},{16,0},{24,8},{1,17},{9,25},{17,1},{25,9},{2,18},{10... | collective-permute-start | bytes 393224 | tf_op jit(solution)/shard_map/ppermute | solution.py:510
  15.0 1.0 %local1.1 = (f32[1024,1024]{1,0:T(8,128)S(1)}, f32[8,128]{1,0:T(8,128)S(1)}) custom-call(bf16[1024,128]{1,0:T(8,128)(2,1)S(1)} %get-tuple-element.35.refs_0_.refs_1_, bf16[1024,128]{1,0:T(8,128)(2,1)S(1)} %get-tuple-element.36.refs_1_, bf16[1024,1024]{1,0:T(8,128)(2,1)S(1)} %get-tuple-element.37.refs_2_, ...), custom_call_target="tpu_custom_call", output_to_operand_aliasing={{0}: (9, {})} | custom-call | flops 2000000000 | bytes 1000000 | tf_op jit(solution)/shard_map/local1/pallas_call | solution.py:51
  16.1 1.6 %collective-permute-start.5 = (f32[136,128]{1,0:T(8,128)S(1)}, f32[136,128]{1,0:T(8,128)S(1)}, u32[]{:S(2)}, u32[]{:S(2)}) collective-permute-start(f32[136,128]{1,0:T(8,128)S(1)} %merge21.1.refs_3_.refs_0_), channel_id=1, source_target_pairs={{0,2},{8,10},{16,18},{24,26},{1,3},{9,11},{17,19},{25,27},{2,0},{1... | collective-permute-start | bytes 208904 | tf_op jit(solution)/shard_map/ppermute | solution.py:510
  17.8 0.7 %collective-permute-start.7 = (f32[136,128]{1,0:T(8,128)S(1)}, f32[136,128]{1,0:T(8,128)S(1)}, u32[]{:S(2)}, u32[]{:S(2)}) collective-permute-start(f32[136,128]{1,0:T(8,128)S(1)} %get-tuple-element.53.refs_0_.refs_2_), channel_id=1, source_target_pairs={{0,2},{8,10},{16,18},{24,26},{1,3},{9,11},{17,19},{25,27},{2,0},{1... | collective-permute-start | bytes 208904 | tf_op jit(solution)/shard_map/ppermute | solution.py:510
  18.5 1.8 %collective-permute-start.12 = (f32[256,128]{1,0:T(8,128)S(1)}, f32[256,128]{1,0:T(8,128)S(1)}, u32[]{:S(2)}, u32[]{:S(2)}) collective-permute-start(f32[256,128]{1,0:T(8,128)S(1)} %found2.1.refs_2_), channel_id=1, source_target_pairs={{0,16},{8,24},{16,0},{24,8},{1,17},{9,25},{17,1},{25,9},{2,18},{10... | collective-permute-start | bytes 393224 | tf_op jit(solution)/shard_map/ppermute | solution.py:510
  20.5 2.7 %collective-permute-start.10 = (f32[136,128]{1,0:T(8,128)S(1)}, f32[136,128]{1,0:T(8,128)S(1)}, u32[]{:S(2)}, u32[]{:S(2)}) collective-permute-start(f32[136,128]{1,0:T(8,128)S(1)} %merge31.1.refs_3_.refs_10_), channel_id=1, source_target_pairs={{0,4},{8,12},{16,20},{24,28},{1,5},{9,13},{17,21},{25,29},{2,6},{1... | collective-permute-start | bytes 208904 | tf_op jit(solution)/shard_map/ppermute | solution.py:510
  23.2 1.9 %collective-permute-start.9 = (f32[136,128]{1,0:T(8,128)S(1)}, f32[136,128]{1,0:T(8,128)S(1)}, u32[]{:S(2)}, u32[]{:S(2)}) collective-permute-start(f32[136,128]{1,0:T(8,128)S(1)} %get-tuple-element.54.refs_2_), channel_id=1, source_target_pairs={{0,4},{8,12},{16,20},{24,28},{1,5},{9,13},{17,21},{25,29},{2,6},{1... | collective-permute-start | bytes 208904 | tf_op jit(solution)/shard_map/ppermute | solution.py:510
  25.1 0.7 %collective-permute-start.13 = (f32[256,128]{1,0:T(8,128)S(1)}, f32[256,128]{1,0:T(8,128)S(1)}, u32[]{:S(2)}, u32[]{:S(2)}) collective-permute-start(f32[256,128]{1,0:T(8,128)S(1)} %found3.1.refs_11_.refs_4_), channel_id=1, source_target_pairs={{0,16},{8,24},{16,0},{24,8},{1,17},{9,25},{17,1},{25,9},{2,18},{10... | collective-permute-start | bytes 393224 | tf_op jit(solution)/shard_map/ppermute | solution.py:510
  25.8 2.1 %local2.1 = (f32[1024,1024]{1,0:T(8,128)S(1)}, f32[8,128]{1,0:T(8,128)S(1)}) custom-call(bf16[1024,128]{1,0:T(8,128)(2,1)S(1)} %get-tuple-element.35.refs_0_.refs_1_, bf16[1024,128]{1,0:T(8,128)(2,1)S(1)} %get-tuple-element.36.refs_1_, bf16[1024,1024]{1,0:T(8,128)(2,1)S(1)} %get-tuple-element.37.refs_2_, ...), custom_call_target="tpu_custom_call", output_to_operand_aliasing={{0}: (9, {})} | custom-call | flops 1000 | bytes 1000000 | tf_op jit(solution)/shard_map/local2/pallas_call | solution.py:51
  28.5 1.1 %collective-permute-start.11 = (f32[256,128]{1,0:T(8,128)S(1)}, f32[256,128]{1,0:T(8,128)S(1)}, u32[]{:S(2)}, u32[]{:S(2)}) collective-permute-start(f32[256,128]{1,0:T(8,128)S(1)} %state.1.refs_6_.refs_0_.refs_9_), channel_id=1, source_target_pairs={{0,16},{8,24},{16,0},{24,8},{1,17},{9,25},{17,1},{25,9},{2,18},{10... | collective-permute-start | bytes 393224 | tf_op jit(solution)/shard_map/ppermute | solution.py:510
  29.6 1.2 %collective-permute-done.13.refs_5_ = f32[256,128]{1,0:T(8,128)S(1)} collective-permute-done((f32[256,128]{1,0:T(8,128)S(1)}, f32[256,128]{1,0:T(8,128)S(1)}, u32[]{:S(2)}, u32[]{:S(2)}) %collective-permute-start.13) | collective-permute-done | bytes 131104 | tf_op jit(solution)/shard_map/ppermute | solution.py:510
  31.0 0.6 %collective-permute-start.14 = (f32[256,128]{1,0:T(8,128)S(1)}, f32[256,128]{1,0:T(8,128)S(1)}, u32[]{:S(2)}, u32[]{:S(2)}) collective-permute-start(f32[256,128]{1,0:T(8,128)S(1)} %shared.1), channel_id=1, source_target_pairs={{0,8},{8,0},{16,24},{24,16},{1,9},{9,1},{17,25},{25,17},{2,10},{10... | collective-permute-start | bytes 393224 | tf_op jit(solution)/shard_map/ppermute | solution.py:510
  31.5 0.9 %finish00.1.refs_11_ = bf16[1024,256]{1,0:T(8,128)(2,1)S(1)} custom-call(f32[1024,1024]{1,0:T(8,128)S(1)} %get-tuple-element.55.refs_0_, bf16[1024,128]{1,0:T(8,128)(2,1)S(1)} %get-tuple-element.35.refs_0_.refs_1_, f32[2,8,1024]{2,1,0:T(8,128)S(1)} %get-tuple-element.38.refs_3_.refs_2_, f32[8,8,1024]{2,1,0:T(8,128)S(1)} %get-tuple-element.40.refs_5_.refs_3_, ...), custom_call_target="tpu_custom_call" | custom-call | flops 20000000000 | bytes 1000000 | tf_op jit(solution)/shard_map/finish00/pallas_call | solution.py:486
  32.4 1.0 %collective-permute-done.14.refs_9_ = f32[256,128]{1,0:T(8,128)S(1)} collective-permute-done((f32[256,128]{1,0:T(8,128)S(1)}, f32[256,128]{1,0:T(8,128)S(1)}, u32[]{:S(2)}, u32[]{:S(2)}) %collective-permute-start.14) | collective-permute-done | bytes 131104 | tf_op jit(solution)/shard_map/ppermute | solution.py:510
  33.4 0.9 %finish10.1.refs_1_.refs_11_ = bf16[1024,256]{1,0:T(8,128)(2,1)S(1)} custom-call(f32[1024,1024]{1,0:T(8,128)S(1)} %get-tuple-element.55.refs_0_, bf16[1024,128]{1,0:T(8,128)(2,1)S(1)} %get-tuple-element.35.refs_0_.refs_1_, f32[2,8,1024]{2,1,0:T(8,128)S(1)} %get-tuple-element.38.refs_3_.refs_2_, f32[8,8,1024]{2,1,0:T(8,128)S(1)} %get-tuple-element.40.refs_5_.refs_3_, ...), custom_call_target="tpu_custom_call" | custom-call | flops 1000 | bytes 1000000 | tf_op jit(solution)/shard_map/finish10/pallas_call | solution.py:486
  34.5 1.8 %finish01.1.refs_12_ = bf16[1024,1024]{1,0:T(8,128)(2,1)} custom-call(f32[1024,1024]{1,0:T(8,128)S(1)} %get-tuple-element.55.refs_0_, bf16[1024,128]{1,0:T(8,128)(2,1)S(1)} %get-tuple-element.35.refs_0_.refs_1_, f32[2,8,1024]{2,1,0:T(8,128)S(1)} %get-tuple-element.38.refs_3_.refs_2_, f32[8,8,1024]{2,1,0:T(8,128)S(1)} %get-tuple-element.40.refs_5_.refs_3_, ...), custom_call_target="tpu_custom_call" | custom-call | flops 20000000000 | bytes 1000000 | tf_op jit(solution)/shard_map/finish01/pallas_call | solution.py:486
  36.3 1.7 %finish11.1 = bf16[1024,1024]{1,0:T(8,128)(2,1)} custom-call(f32[1024,1024]{1,0:T(8,128)S(1)} %get-tuple-element.55.refs_0_, bf16[1024,128]{1,0:T(8,128)(2,1)S(1)} %get-tuple-element.35.refs_0_.refs_1_, f32[2,8,1024]{2,1,0:T(8,128)S(1)} %get-tuple-element.38.refs_3_.refs_2_, ...), custom_call_target="tpu_custom_call", output_to_operand_aliasing={{}: (12, {})} | custom-call | flops 2000000000 | bytes 1000000 | tf_op jit(solution)/shard_map/finish11/pallas_call | solution.py:486
  (34 shorter events, 2.5 us)
Async XLA Ops:
  2.9 1.7 %collective-permute-start = (f32[520,128]{1,0:T(8,128)S(1)}, f32[520,128]{1,0:T(8,128)S(1)}, u32[]{:S(2)}, u32[]{:S(2)}) collective-permute-start(f32[520,128]{1,0:T(8,128)S(1)} %get-tuple-element.33), channel_id=1, source_target_pairs={{0,8},{8,0},{16,24},{24,16},{1,9},{9,1},{17,25},{25,17},{2,10},{10... | collective-permute-start | bytes 798728 | tf_op jit(solution)/shard_map/ppermute | solution.py:510
  3.4 5.4 %collective-permute-start.1 = (f32[520,128]{1,0:T(8,128)S(1)}, f32[520,128]{1,0:T(8,128)S(1)}, u32[]{:S(2)}, u32[]{:S(2)}) collective-permute-start(f32[520,128]{1,0:T(8,128)S(1)} %get-tuple-element.32.mine_ref), channel_id=1, source_target_pairs={{0,8},{8,0},{16,24},{24,16},{1,9},{9,1},{17,25},{25,17},{2,10},{10... | collective-permute-start | bytes 798728 | tf_op jit(solution)/shard_map/ppermute | solution.py:510
  4.7 5.5 %collective-permute-start.2 = (f32[136,128]{1,0:T(8,128)S(1)}, f32[136,128]{1,0:T(8,128)S(1)}, u32[]{:S(2)}, u32[]{:S(2)}) collective-permute-start(f32[136,128]{1,0:T(8,128)S(1)} %get-tuple-element.44), channel_id=1, source_target_pairs={{0,16},{8,24},{16,0},{24,8},{1,17},{9,25},{17,1},{25,9},{2,18},{10... | collective-permute-start | bytes 208904 | tf_op jit(solution)/shard_map/ppermute | solution.py:510
  7.6 4.8 %collective-permute-start.4 = (f32[136,128]{1,0:T(8,128)S(1)}, f32[136,128]{1,0:T(8,128)S(1)}, u32[]{:S(2)}, u32[]{:S(2)}) collective-permute-start(f32[136,128]{1,0:T(8,128)S(1)} %get-tuple-element.47), channel_id=1, source_target_pairs={{0,16},{8,24},{16,0},{24,8},{1,17},{9,25},{17,1},{25,9},{2,18},{10... | collective-permute-start | bytes 208904 | tf_op jit(solution)/shard_map/ppermute | solution.py:510
  10.2 5.9 %collective-permute-start.3 = (f32[136,128]{1,0:T(8,128)S(1)}, f32[136,128]{1,0:T(8,128)S(1)}, u32[]{:S(2)}, u32[]{:S(2)}) collective-permute-start(f32[136,128]{1,0:T(8,128)S(1)} %merge11.1.refs_10_.refs_3_.refs_0_), channel_id=1, source_target_pairs={{0,1},{8,9},{16,17},{24,25},{1,0},{9,8},{17,16},{25,24},{2,3},{10,... | collective-permute-start | bytes 208904 | tf_op jit(solution)/shard_map/ppermute | solution.py:510
  12.4 5.3 %collective-permute-start.6 = (f32[136,128]{1,0:T(8,128)S(1)}, f32[136,128]{1,0:T(8,128)S(1)}, u32[]{:S(2)}, u32[]{:S(2)}) collective-permute-start(f32[136,128]{1,0:T(8,128)S(1)} %get-tuple-element.50.refs_0_.refs_2_), channel_id=1, source_target_pairs={{0,1},{8,9},{16,17},{24,25},{1,0},{9,8},{17,16},{25,24},{2,3},{10,... | collective-permute-start | bytes 208904 | tf_op jit(solution)/shard_map/ppermute | solution.py:510
  13.5 9.6 %collective-permute-start.8 = (f32[256,128]{1,0:T(8,128)S(1)}, f32[256,128]{1,0:T(8,128)S(1)}, u32[]{:S(2)}, u32[]{:S(2)}) collective-permute-start(f32[256,128]{1,0:T(8,128)S(1)} %rest.1), channel_id=1, source_target_pairs={{0,16},{8,24},{16,0},{24,8},{1,17},{9,25},{17,1},{25,9},{2,18},{10... | collective-permute-start | bytes 393224 | tf_op jit(solution)/shard_map/ppermute | solution.py:510
  16.1 4.4 %collective-permute-start.5 = (f32[136,128]{1,0:T(8,128)S(1)}, f32[136,128]{1,0:T(8,128)S(1)}, u32[]{:S(2)}, u32[]{:S(2)}) collective-permute-start(f32[136,128]{1,0:T(8,128)S(1)} %merge21.1.refs_3_.refs_0_), channel_id=1, source_target_pairs={{0,2},{8,10},{16,18},{24,26},{1,3},{9,11},{17,19},{25,27},{2,0},{1... | collective-permute-start | bytes 208904 | tf_op jit(solution)/shard_map/ppermute | solution.py:510
  17.8 5.4 %collective-permute-start.7 = (f32[136,128]{1,0:T(8,128)S(1)}, f32[136,128]{1,0:T(8,128)S(1)}, u32[]{:S(2)}, u32[]{:S(2)}) collective-permute-start(f32[136,128]{1,0:T(8,128)S(1)} %get-tuple-element.53.refs_0_.refs_2_), channel_id=1, source_target_pairs={{0,2},{8,10},{16,18},{24,26},{1,3},{9,11},{17,19},{25,27},{2,0},{1... | collective-permute-start | bytes 208904 | tf_op jit(solution)/shard_map/ppermute | solution.py:510
  18.5 11.1 %collective-permute-start.12 = (f32[256,128]{1,0:T(8,128)S(1)}, f32[256,128]{1,0:T(8,128)S(1)}, u32[]{:S(2)}, u32[]{:S(2)}) collective-permute-start(f32[256,128]{1,0:T(8,128)S(1)} %found2.1.refs_2_), channel_id=1, source_target_pairs={{0,16},{8,24},{16,0},{24,8},{1,17},{9,25},{17,1},{25,9},{2,18},{10... | collective-permute-start | bytes 393224 | tf_op jit(solution)/shard_map/ppermute | solution.py:510
  20.5 8.0 %collective-permute-start.10 = (f32[136,128]{1,0:T(8,128)S(1)}, f32[136,128]{1,0:T(8,128)S(1)}, u32[]{:S(2)}, u32[]{:S(2)}) collective-permute-start(f32[136,128]{1,0:T(8,128)S(1)} %merge31.1.refs_3_.refs_10_), channel_id=1, source_target_pairs={{0,4},{8,12},{16,20},{24,28},{1,5},{9,13},{17,21},{25,29},{2,6},{1... | collective-permute-start | bytes 208904 | tf_op jit(solution)/shard_map/ppermute | solution.py:510
  23.2 5.3 %collective-permute-start.9 = (f32[136,128]{1,0:T(8,128)S(1)}, f32[136,128]{1,0:T(8,128)S(1)}, u32[]{:S(2)}, u32[]{:S(2)}) collective-permute-start(f32[136,128]{1,0:T(8,128)S(1)} %get-tuple-element.54.refs_2_), channel_id=1, source_target_pairs={{0,4},{8,12},{16,20},{24,28},{1,5},{9,13},{17,21},{25,29},{2,6},{1... | collective-permute-start | bytes 208904 | tf_op jit(solution)/shard_map/ppermute | solution.py:510
  25.1 5.7 %collective-permute-start.13 = (f32[256,128]{1,0:T(8,128)S(1)}, f32[256,128]{1,0:T(8,128)S(1)}, u32[]{:S(2)}, u32[]{:S(2)}) collective-permute-start(f32[256,128]{1,0:T(8,128)S(1)} %found3.1.refs_11_.refs_4_), channel_id=1, source_target_pairs={{0,16},{8,24},{16,0},{24,8},{1,17},{9,25},{17,1},{25,9},{2,18},{10... | collective-permute-start | bytes 393224 | tf_op jit(solution)/shard_map/ppermute | solution.py:510
  28.5 5.8 %collective-permute-start.11 = (f32[256,128]{1,0:T(8,128)S(1)}, f32[256,128]{1,0:T(8,128)S(1)}, u32[]{:S(2)}, u32[]{:S(2)}) collective-permute-start(f32[256,128]{1,0:T(8,128)S(1)} %state.1.refs_6_.refs_0_.refs_9_), channel_id=1, source_target_pairs={{0,16},{8,24},{16,0},{24,8},{1,17},{9,25},{17,1},{25,9},{2,18},{10... | collective-permute-start | bytes 393224 | tf_op jit(solution)/shard_map/ppermute | solution.py:510
  30.9 2.5 %collective-permute-start.15 = (f32[1536,128]{1,0:T(8,128)S(1)}, f32[1536,128]{1,0:T(8,128)S(1)}, u32[]{:S(2)}, u32[]{:S(2)}) collective-permute-start(f32[1536,128]{1,0:T(8,128)S(1)} %near.1.refs_1_.refs_10_), channel_id=1, source_target_pairs={{0,8},{8,0},{16,24},{24,16},{1,9},{9,1},{17,25},{25,17},{2,10},{10... | collective-permute-start | bytes 2359304 | tf_op jit(solution)/shard_map/ppermute | solution.py:510
  31.0 2.4 %collective-permute-start.14 = (f32[256,128]{1,0:T(8,128)S(1)}, f32[256,128]{1,0:T(8,128)S(1)}, u32[]{:S(2)}, u32[]{:S(2)}) collective-permute-start(f32[256,128]{1,0:T(8,128)S(1)} %shared.1), channel_id=1, source_target_pairs={{0,8},{8,0},{16,24},{24,16},{1,9},{9,1},{17,25},{25,17},{2,10},{10... | collective-permute-start | bytes 393224 | tf_op jit(solution)/shard_map/ppermute | solution.py:510
  34.3 2.0 %collective-permute-start.16 = (f32[256,128]{1,0:T(8,128)S(1)}, f32[256,128]{1,0:T(8,128)S(1)}, u32[]{:S(2)}, u32[]{:S(2)}) collective-permute-start(f32[256,128]{1,0:T(8,128)S(1)} %beside.1.refs_9_), channel_id=1, source_target_pairs={{0,8},{8,0},{16,24},{24,16},{1,9},{9,1},{17,25},{25,17},{2,10},{10... | collective-permute-start | bytes 393224 | tf_op jit(solution)/shard_map/ppermute | solution.py:510

commit v23 on v20

--- a/solution.py
+++ b/solution.py
@@ -570,33 +570,27 @@
 
     state = both("state", found[last], waits)
     beside = trade(state, 2)
-    early = list(range(2, last))
-    pieces = [(found[1], two), (rest, two)]
-    for bit in early:
-        pieces += [(found[bit], two), (across[bit], two)]
-    near = pack("near", pieces, (state,))
-    far = trade(near, 1)
-    middle = [1, *early]
-    ahead = [prefixes[bit] for bit in middle]
-
-    def states_of(side, index, first):
-        return [(first + slot, index, (2 * slot + side) * two) for slot in range(len(middle))]
-
+    early = list(range(1, last))
+    ours = pack("ours", [(found[bit], two) for bit in early], ())
+    theirs = pack("theirs", [(rest if bit == 1 else across[bit], two) for bit in early], (state,))
+    joined = pack("joined", [(ours, len(early) * two), (state, two)])
+    joined_far = trade(joined, 1)
+    theirs_far = trade(theirs, 1)
+    ahead = [prefixes[bit] for bit in early]
     shared = (mixed, queries, sums, level_weight, gain)
-    every = (first_level, [last, *middle], shared, [prefixes[last], *ahead])
-    quarters = {(core, side): [(0, 0, 0), *states_of(side, 1, 1)] for core, side in sides}
-    state_far = trade(pack("shared", [(state, two)], (near,)), 1)
-    (block,) = finish([((0, 0), quarters[0, 0])], *every, [state, near], None, True, None)
-    (block_far,) = finish(
-        [((1, 0), quarters[1, 0])], *every, [state_far, far, block], None, True, None
-    )
+    every = (first_level, [*early, last], shared, [*ahead, prefixes[last]])
+    levels = [(slot, 0, slot * two) for slot in range(len(early))]
+    whole = [*levels, (len(early), 0, len(early) * two)]
+    parted = [*levels, (len(early), 1, 0)]
+    (block,) = finish([((0, 0), whole)], *every, [joined], None, True, None)
+    (block_far,) = finish([((1, 0), whole)], *every, [joined_far, block], None, True, None)
     beside = pack("beside", [(beside, two)], (block_far,))
     (out,) = finish(
-        [((0, 1), quarters[0, 1])], *every, [beside, near, block], None, False, (2, (0, 0))
+        [((0, 1), parted)], *every, [theirs, beside, block], None, False, (2, (0, 0))
     )
     beside_far = trade(beside, 1)
     return finish(
-        [((1, 1), quarters[1, 1])], *every, [beside_far, far, block_far], out, False, (2, (1, 0))
+        [((1, 1), parted)], *every, [theirs_far, beside_far, block_far], out, False, (2, (1, 0))
     )[0]
 
 

time: 38.1 us -> 37.3 us (0.979)
  waiting for transfers between devices: 4.44 us -> 3.61 us
    ppermute x17, waiting for transfers between devices: 4.44 us -> 3.61 us  [trade(): return lax.ppermute(value, AXES, pairs)]
    pallas_call x20 -> x21, Pallas kernels: 8.07 us -> 8.03 us  [call(): pl.pallas_call(kernel, in_specs=specs, out_specs=[HELD] * len(outputs), o...]
  transfers between devices with their start and end apart: 17 -> 17, of which waited for: 6 -> 7; matrix products, arithmetic and copies ran while one was open for 0% -> 0% of each run, Pallas kernels for 24% -> 25%
where the time goes in v23:
time: 37.3 us; the launch traced here: 36.9 us
  starting transfers between devices  19.6 us (53%)
  Pallas kernels  13.4 us (36%)
  waiting for transfers between devices  3.61 us (10%)
    ppermute x17, starting transfers between devices, trade(): return lax.ppermute(value, AXES, pairs)  19.6 us
    pallas_call x21, Pallas kernels, call(): pl.pallas_call(kernel, in_specs=specs, out_specs=[HELD] * len(outputs), o...  8.03 us
    pallas_call x4, Pallas kernels, finish(): pl.pallas_call(functools.partial(finish_kernel, quarters, first_level, bi...  5.42 us
    ppermute x17, waiting for transfers between devices, trade(): return lax.ppermute(value, AXES, pairs)  3.61 us
  transfers between devices with their start and end apart: 17, of which 7 were waited for; matrix products, arithmetic and copies ran while one was open for 0% of the time, Pallas kernels for 25%

profile of v23, /device:TPU:0, one launch (start us, length us, event | category | flops | bytes accessed | tf_op | source)
XLA Modules:
  0.0 36.9 jit_solution(9014056433780550213)
XLA Ops:
  0.0 2.6 %states.1 = (f32[520,128]{1,0:T(8,128)S(1)}, f32[520,128]{1,0:T(8,128)S(1)}, bf16[3,128,1024]{2,1,0:T(8,128)(2,1)S(1)}, f32[2,8,1024]{2,1,0:T(8,128)S(1)}, f32[4...) custom-call(bf16[1024,128]{1,0:T(8,128)(2,1)} %refs_0_.2, ...), custom_call_target="tpu_custom_call" | custom-call | flops 2000000000 | bytes 1000000 | tf_op jit(solution)/shard_map/states/pallas_call | solution.py:50
  2.6 0.5 %collective-permute-start = (f32[520,128]{1,0:T(8,128)S(1)}, f32[520,128]{1,0:T(8,128)S(1)}, u32[]{:S(2)}, u32[]{:S(2)}) collective-permute-start(f32[520,128]{1,0:T(8,128)S(1)} %get-tuple-element.33), channel_id=1, source_target_pairs={{0,8},{8,0},{16,24},{24,16},{1,9},{9,1},{17,25},{25,17},{2,10},{10... | collective-permute-start | bytes 798728 | tf_op jit(solution)/shard_map/ppermute | solution.py:514
  3.2 1.1 %collective-permute-done.other_ref.refs_7_ = f32[520,128]{1,0:T(8,128)S(1)} collective-permute-done((f32[520,128]{1,0:T(8,128)S(1)}, f32[520,128]{1,0:T(8,128)S(1)}, u32[]{:S(2)}, u32[]{:S(2)}) %collective-permute-start) | collective-permute-done | bytes 266272 | tf_op jit(solution)/shard_map/ppermute | solution.py:514
  4.4 3.0 %collective-permute-start.2 = (f32[136,128]{1,0:T(8,128)S(1)}, f32[136,128]{1,0:T(8,128)S(1)}, u32[]{:S(2)}, u32[]{:S(2)}) collective-permute-start(f32[136,128]{1,0:T(8,128)S(1)} %get-tuple-element.44), channel_id=1, source_target_pairs={{0,16},{8,24},{16,0},{24,8},{1,17},{9,25},{17,1},{25,9},{2,18},{10... | collective-permute-start | bytes 208904 | tf_op jit(solution)/shard_map/ppermute | solution.py:514
  7.5 1.1 %load.1 = (bf16[1024,128]{1,0:T(8,128)(2,1)S(1)}, f32[8,8,1024]{2,1,0:T(8,128)S(1)}, f32[8,128]{1,0:T(8,128)S(1)}) custom-call(bf16[1024,128]{1,0:T(8,128)(2,1)} %refs_0_.3, f32[8,8,1024]{2,1,0:T(8,128)} %refs_1_.3, f32[8,128]{1,0:T(8,128)} %bitcast.1, f32[136,128]{1,0:T(8,128)S(1)} %get-tuple-element.34.refs_3_.refs_0_), custom_call_target="tpu_custom_call" | custom-call | flops 2000000000 | bytes 1000000 | tf_op jit(solution)/shard_map/load/pallas_call | solution.py:50
  8.5 0.9 %local0.1 = (f32[1024,1024]{1,0:T(8,128)S(1)}, f32[8,128]{1,0:T(8,128)S(1)}) custom-call(bf16[1024,128]{1,0:T(8,128)(2,1)S(1)} %get-tuple-element.35.refs_0_.refs_1_, bf16[1024,128]{1,0:T(8,128)(2,1)S(1)} %get-tuple-element.36.refs_1_, bf16[1024,1024]{1,0:T(8,128)(2,1)S(1)} %get-tuple-element.37.refs_2_, ...), custom_call_target="tpu_custom_call" | custom-call | flops 1000 | bytes 1000000 | tf_op jit(solution)/shard_map/local0/pallas_call | solution.py:50
  9.9 2.2 %collective-permute-start.3 = (f32[136,128]{1,0:T(8,128)S(1)}, f32[136,128]{1,0:T(8,128)S(1)}, u32[]{:S(2)}, u32[]{:S(2)}) collective-permute-start(f32[136,128]{1,0:T(8,128)S(1)} %merge11.1.refs_10_.refs_3_.refs_0_), channel_id=1, source_target_pairs={{0,1},{8,9},{16,17},{24,25},{1,0},{9,8},{17,16},{25,24},{2,3},{10,... | collective-permute-start | bytes 208904 | tf_op jit(solution)/shard_map/ppermute | solution.py:514
  12.2 1.1 %collective-permute-start.6 = (f32[136,128]{1,0:T(8,128)S(1)}, f32[136,128]{1,0:T(8,128)S(1)}, u32[]{:S(2)}, u32[]{:S(2)}) collective-permute-start(f32[136,128]{1,0:T(8,128)S(1)} %get-tuple-element.50.refs_0_.refs_2_), channel_id=1, source_target_pairs={{0,1},{8,9},{16,17},{24,25},{1,0},{9,8},{17,16},{25,24},{2,3},{10,... | collective-permute-start | bytes 208904 | tf_op jit(solution)/shard_map/ppermute | solution.py:514
  13.3 1.5 %collective-permute-start.8 = (f32[256,128]{1,0:T(8,128)S(1)}, f32[256,128]{1,0:T(8,128)S(1)}, u32[]{:S(2)}, u32[]{:S(2)}) collective-permute-start(f32[256,128]{1,0:T(8,128)S(1)} %rest.1), channel_id=1, source_target_pairs={{0,16},{8,24},{16,0},{24,8},{1,17},{9,25},{17,1},{25,9},{2,18},{10... | collective-permute-start | bytes 393224 | tf_op jit(solution)/shard_map/ppermute | solution.py:514
  14.8 1.0 %local1.1 = (f32[1024,1024]{1,0:T(8,128)S(1)}, f32[8,128]{1,0:T(8,128)S(1)}) custom-call(bf16[1024,128]{1,0:T(8,128)(2,1)S(1)} %get-tuple-element.35.refs_0_.refs_1_, bf16[1024,128]{1,0:T(8,128)(2,1)S(1)} %get-tuple-element.36.refs_1_, bf16[1024,1024]{1,0:T(8,128)(2,1)S(1)} %get-tuple-element.37.refs_2_, ...), custom_call_target="tpu_custom_call", output_to_operand_aliasing={{0}: (9, {})} | custom-call | flops 2000000000 | bytes 1000000 | tf_op jit(solution)/shard_map/local1/pallas_call | solution.py:50
  15.8 1.6 %collective-permute-start.5 = (f32[136,128]{1,0:T(8,128)S(1)}, f32[136,128]{1,0:T(8,128)S(1)}, u32[]{:S(2)}, u32[]{:S(2)}) collective-permute-start(f32[136,128]{1,0:T(8,128)S(1)} %merge21.1.refs_3_.refs_0_), channel_id=1, source_target_pairs={{0,2},{8,10},{16,18},{24,26},{1,3},{9,11},{17,19},{25,27},{2,0},{1... | collective-permute-start | bytes 208904 | tf_op jit(solution)/shard_map/ppermute | solution.py:514
  17.5 0.8 %collective-permute-start.7 = (f32[136,128]{1,0:T(8,128)S(1)}, f32[136,128]{1,0:T(8,128)S(1)}, u32[]{:S(2)}, u32[]{:S(2)}) collective-permute-start(f32[136,128]{1,0:T(8,128)S(1)} %get-tuple-element.53.refs_0_.refs_2_), channel_id=1, source_target_pairs={{0,2},{8,10},{16,18},{24,26},{1,3},{9,11},{17,19},{25,27},{2,0},{1... | collective-permute-start | bytes 208904 | tf_op jit(solution)/shard_map/ppermute | solution.py:514
  18.3 1.8 %collective-permute-start.9 = (f32[256,128]{1,0:T(8,128)S(1)}, f32[256,128]{1,0:T(8,128)S(1)}, u32[]{:S(2)}, u32[]{:S(2)}) collective-permute-start(f32[256,128]{1,0:T(8,128)S(1)} %found2.1.refs_1_), channel_id=1, source_target_pairs={{0,16},{8,24},{16,0},{24,8},{1,17},{9,25},{17,1},{25,9},{2,18},{10... | collective-permute-start | bytes 393224 | tf_op jit(solution)/shard_map/ppermute | solution.py:514
  20.3 2.7 %collective-permute-start.12 = (f32[136,128]{1,0:T(8,128)S(1)}, f32[136,128]{1,0:T(8,128)S(1)}, u32[]{:S(2)}, u32[]{:S(2)}) collective-permute-start(f32[136,128]{1,0:T(8,128)S(1)} %merge31.1.refs_3_.refs_10_), channel_id=1, source_target_pairs={{0,4},{8,12},{16,20},{24,28},{1,5},{9,13},{17,21},{25,29},{2,6},{1... | collective-permute-start | bytes 208904 | tf_op jit(solution)/shard_map/ppermute | solution.py:514
  23.0 1.9 %collective-permute-start.11 = (f32[136,128]{1,0:T(8,128)S(1)}, f32[136,128]{1,0:T(8,128)S(1)}, u32[]{:S(2)}, u32[]{:S(2)}) collective-permute-start(f32[136,128]{1,0:T(8,128)S(1)} %get-tuple-element.54.refs_2_), channel_id=1, source_target_pairs={{0,4},{8,12},{16,20},{24,28},{1,5},{9,13},{17,21},{25,29},{2,6},{1... | collective-permute-start | bytes 208904 | tf_op jit(solution)/shard_map/ppermute | solution.py:514
  24.9 0.7 %collective-permute-start.10 = (f32[256,128]{1,0:T(8,128)S(1)}, f32[256,128]{1,0:T(8,128)S(1)}, u32[]{:S(2)}, u32[]{:S(2)}) collective-permute-start(f32[256,128]{1,0:T(8,128)S(1)} %found3.1.refs_11_.refs_2_), channel_id=1, source_target_pairs={{0,16},{8,24},{16,0},{24,8},{1,17},{9,25},{17,1},{25,9},{2,18},{10... | collective-permute-start | bytes 393224 | tf_op jit(solution)/shard_map/ppermute | solution.py:514
  25.6 2.1 %local2.1 = (f32[1024,1024]{1,0:T(8,128)S(1)}, f32[8,128]{1,0:T(8,128)S(1)}) custom-call(bf16[1024,128]{1,0:T(8,128)(2,1)S(1)} %get-tuple-element.35.refs_0_.refs_1_, bf16[1024,128]{1,0:T(8,128)(2,1)S(1)} %get-tuple-element.36.refs_1_, bf16[1024,1024]{1,0:T(8,128)(2,1)S(1)} %get-tuple-element.37.refs_2_, ...), custom_call_target="tpu_custom_call", output_to_operand_aliasing={{0}: (9, {})} | custom-call | flops 1000 | bytes 1000000 | tf_op jit(solution)/shard_map/local2/pallas_call | solution.py:50
  27.7 0.5 %collective-permute-done.11.refs_0_ = f32[136,128]{1,0:T(8,128)S(1)} collective-permute-done((f32[136,128]{1,0:T(8,128)S(1)}, f32[136,128]{1,0:T(8,128)S(1)}, u32[]{:S(2)}, u32[]{:S(2)}) %collective-permute-start.11) | collective-permute-done | bytes 69664 | tf_op jit(solution)/shard_map/ppermute | solution.py:514
  28.2 1.1 %collective-permute-start.14 = (f32[256,128]{1,0:T(8,128)S(1)}, f32[256,128]{1,0:T(8,128)S(1)}, u32[]{:S(2)}, u32[]{:S(2)}) collective-permute-start(f32[256,128]{1,0:T(8,128)S(1)} %state.1.refs_3_.refs_1_), channel_id=1, source_target_pairs={{0,16},{8,24},{16,0},{24,8},{1,17},{9,25},{17,1},{25,9},{2,18},{10... | collective-permute-start | bytes 393224 | tf_op jit(solution)/shard_map/ppermute | solution.py:514
  29.5 1.0 %finish00.1.refs_10_.refs_11_ = bf16[1024,256]{1,0:T(8,128)(2,1)S(1)} custom-call(f32[1024,1024]{1,0:T(8,128)S(1)} %get-tuple-element.55.refs_0_, bf16[1024,128]{1,0:T(8,128)(2,1)S(1)} %get-tuple-element.35.refs_0_.refs_1_, f32[2,8,1024]{2,1,0:T(8,128)S(1)} %get-tuple-element.38.refs_3_.refs_2_, f32[8,8,1024]{2,1,0:T(8,128)S(1)} %get-tuple-element.40.refs_5_.refs_3_, ...), custom_call_target="tpu_custom_call" | custom-call | flops 20000000000 | bytes 1000000 | tf_op jit(solution)/shard_map/finish00/pallas_call | solution.py:490
  31.4 1.0 %finish10.1.refs_1_.refs_11_ = bf16[1024,256]{1,0:T(8,128)(2,1)S(1)} custom-call(f32[1024,1024]{1,0:T(8,128)S(1)} %get-tuple-element.55.refs_0_, bf16[1024,128]{1,0:T(8,128)(2,1)S(1)} %get-tuple-element.35.refs_0_.refs_1_, f32[2,8,1024]{2,1,0:T(8,128)S(1)} %get-tuple-element.38.refs_3_.refs_2_, f32[8,8,1024]{2,1,0:T(8,128)S(1)} %get-tuple-element.40.refs_5_.refs_3_, ...), custom_call_target="tpu_custom_call" | custom-call | flops 1000 | bytes 1000000 | tf_op jit(solution)/shard_map/finish10/pallas_call | solution.py:490
  32.4 0.9 %collective-permute-done.14.refs_0_ = f32[256,128]{1,0:T(8,128)S(1)} collective-permute-done((f32[256,128]{1,0:T(8,128)S(1)}, f32[256,128]{1,0:T(8,128)S(1)}, u32[]{:S(2)}, u32[]{:S(2)}) %collective-permute-start.14) | collective-permute-done | bytes 131104 | tf_op jit(solution)/shard_map/ppermute | solution.py:514
  33.4 1.7 %finish01.1.refs_12_ = bf16[1024,1024]{1,0:T(8,128)(2,1)} custom-call(f32[1024,1024]{1,0:T(8,128)S(1)} %get-tuple-element.55.refs_0_, bf16[1024,128]{1,0:T(8,128)(2,1)S(1)} %get-tuple-element.35.refs_0_.refs_1_, f32[2,8,1024]{2,1,0:T(8,128)S(1)} %get-tuple-element.38.refs_3_.refs_2_, f32[8,8,1024]{2,1,0:T(8,128)S(1)} %get-tuple-element.40.refs_5_.refs_3_, ...), custom_call_target="tpu_custom_call" | custom-call | flops 20000000000 | bytes 1000000 | tf_op jit(solution)/shard_map/finish01/pallas_call | solution.py:490
  35.1 1.7 %finish11.1 = bf16[1024,1024]{1,0:T(8,128)(2,1)} custom-call(f32[1024,1024]{1,0:T(8,128)S(1)} %get-tuple-element.55.refs_0_, bf16[1024,128]{1,0:T(8,128)(2,1)S(1)} %get-tuple-element.35.refs_0_.refs_1_, f32[2,8,1024]{2,1,0:T(8,128)S(1)} %get-tuple-element.38.refs_3_.refs_2_, ...), custom_call_target="tpu_custom_call", output_to_operand_aliasing={{}: (12, {})} | custom-call | flops 2000000000 | bytes 1000000 | tf_op jit(solution)/shard_map/finish11/pallas_call | solution.py:490
  (35 shorter events, 2.2 us)
Async XLA Ops:
  2.6 1.7 %collective-permute-start = (f32[520,128]{1,0:T(8,128)S(1)}, f32[520,128]{1,0:T(8,128)S(1)}, u32[]{:S(2)}, u32[]{:S(2)}) collective-permute-start(f32[520,128]{1,0:T(8,128)S(1)} %get-tuple-element.33), channel_id=1, source_target_pairs={{0,8},{8,0},{16,24},{24,16},{1,9},{9,1},{17,25},{25,17},{2,10},{10... | collective-permute-start | bytes 798728 | tf_op jit(solution)/shard_map/ppermute | solution.py:514
  3.1 5.4 %collective-permute-start.1 = (f32[520,128]{1,0:T(8,128)S(1)}, f32[520,128]{1,0:T(8,128)S(1)}, u32[]{:S(2)}, u32[]{:S(2)}) collective-permute-start(f32[520,128]{1,0:T(8,128)S(1)} %get-tuple-element.32.mine_ref), channel_id=1, source_target_pairs={{0,8},{8,0},{16,24},{24,16},{1,9},{9,1},{17,25},{25,17},{2,10},{10... | collective-permute-start | bytes 798728 | tf_op jit(solution)/shard_map/ppermute | solution.py:514
  4.4 5.5 %collective-permute-start.2 = (f32[136,128]{1,0:T(8,128)S(1)}, f32[136,128]{1,0:T(8,128)S(1)}, u32[]{:S(2)}, u32[]{:S(2)}) collective-permute-start(f32[136,128]{1,0:T(8,128)S(1)} %get-tuple-element.44), channel_id=1, source_target_pairs={{0,16},{8,24},{16,0},{24,8},{1,17},{9,25},{17,1},{25,9},{2,18},{10... | collective-permute-start | bytes 208904 | tf_op jit(solution)/shard_map/ppermute | solution.py:514
  7.4 4.8 %collective-permute-start.4 = (f32[136,128]{1,0:T(8,128)S(1)}, f32[136,128]{1,0:T(8,128)S(1)}, u32[]{:S(2)}, u32[]{:S(2)}) collective-permute-start(f32[136,128]{1,0:T(8,128)S(1)} %get-tuple-element.47), channel_id=1, source_target_pairs={{0,16},{8,24},{16,0},{24,8},{1,17},{9,25},{17,1},{25,9},{2,18},{10... | collective-permute-start | bytes 208904 | tf_op jit(solution)/shard_map/ppermute | solution.py:514
  9.9 5.9 %collective-permute-start.3 = (f32[136,128]{1,0:T(8,128)S(1)}, f32[136,128]{1,0:T(8,128)S(1)}, u32[]{:S(2)}, u32[]{:S(2)}) collective-permute-start(f32[136,128]{1,0:T(8,128)S(1)} %merge11.1.refs_10_.refs_3_.refs_0_), channel_id=1, source_target_pairs={{0,1},{8,9},{16,17},{24,25},{1,0},{9,8},{17,16},{25,24},{2,3},{10,... | collective-permute-start | bytes 208904 | tf_op jit(solution)/shard_map/ppermute | solution.py:514
  12.2 5.3 %collective-permute-start.6 = (f32[136,128]{1,0:T(8,128)S(1)}, f32[136,128]{1,0:T(8,128)S(1)}, u32[]{:S(2)}, u32[]{:S(2)}) collective-permute-start(f32[136,128]{1,0:T(8,128)S(1)} %get-tuple-element.50.refs_0_.refs_2_), channel_id=1, source_target_pairs={{0,1},{8,9},{16,17},{24,25},{1,0},{9,8},{17,16},{25,24},{2,3},{10,... | collective-permute-start | bytes 208904 | tf_op jit(solution)/shard_map/ppermute | solution.py:514
  13.3 9.6 %collective-permute-start.8 = (f32[256,128]{1,0:T(8,128)S(1)}, f32[256,128]{1,0:T(8,128)S(1)}, u32[]{:S(2)}, u32[]{:S(2)}) collective-permute-start(f32[256,128]{1,0:T(8,128)S(1)} %rest.1), channel_id=1, source_target_pairs={{0,16},{8,24},{16,0},{24,8},{1,17},{9,25},{17,1},{25,9},{2,18},{10... | collective-permute-start | bytes 393224 | tf_op jit(solution)/shard_map/ppermute | solution.py:514
  15.8 4.4 %collective-permute-start.5 = (f32[136,128]{1,0:T(8,128)S(1)}, f32[136,128]{1,0:T(8,128)S(1)}, u32[]{:S(2)}, u32[]{:S(2)}) collective-permute-start(f32[136,128]{1,0:T(8,128)S(1)} %merge21.1.refs_3_.refs_0_), channel_id=1, source_target_pairs={{0,2},{8,10},{16,18},{24,26},{1,3},{9,11},{17,19},{25,27},{2,0},{1... | collective-permute-start | bytes 208904 | tf_op jit(solution)/shard_map/ppermute | solution.py:514
  17.5 5.4 %collective-permute-start.7 = (f32[136,128]{1,0:T(8,128)S(1)}, f32[136,128]{1,0:T(8,128)S(1)}, u32[]{:S(2)}, u32[]{:S(2)}) collective-permute-start(f32[136,128]{1,0:T(8,128)S(1)} %get-tuple-element.53.refs_0_.refs_2_), channel_id=1, source_target_pairs={{0,2},{8,10},{16,18},{24,26},{1,3},{9,11},{17,19},{25,27},{2,0},{1... | collective-permute-start | bytes 208904 | tf_op jit(solution)/shard_map/ppermute | solution.py:514
  18.3 12.2 %collective-permute-start.9 = (f32[256,128]{1,0:T(8,128)S(1)}, f32[256,128]{1,0:T(8,128)S(1)}, u32[]{:S(2)}, u32[]{:S(2)}) collective-permute-start(f32[256,128]{1,0:T(8,128)S(1)} %found2.1.refs_1_), channel_id=1, source_target_pairs={{0,16},{8,24},{16,0},{24,8},{1,17},{9,25},{17,1},{25,9},{2,18},{10... | collective-permute-start | bytes 393224 | tf_op jit(solution)/shard_map/ppermute | solution.py:514
  20.3 8.0 %collective-permute-start.12 = (f32[136,128]{1,0:T(8,128)S(1)}, f32[136,128]{1,0:T(8,128)S(1)}, u32[]{:S(2)}, u32[]{:S(2)}) collective-permute-start(f32[136,128]{1,0:T(8,128)S(1)} %merge31.1.refs_3_.refs_10_), channel_id=1, source_target_pairs={{0,4},{8,12},{16,20},{24,28},{1,5},{9,13},{17,21},{25,29},{2,6},{1... | collective-permute-start | bytes 208904 | tf_op jit(solution)/shard_map/ppermute | solution.py:514
  23.0 5.3 %collective-permute-start.11 = (f32[136,128]{1,0:T(8,128)S(1)}, f32[136,128]{1,0:T(8,128)S(1)}, u32[]{:S(2)}, u32[]{:S(2)}) collective-permute-start(f32[136,128]{1,0:T(8,128)S(1)} %get-tuple-element.54.refs_2_), channel_id=1, source_target_pairs={{0,4},{8,12},{16,20},{24,28},{1,5},{9,13},{17,21},{25,29},{2,6},{1... | collective-permute-start | bytes 208904 | tf_op jit(solution)/shard_map/ppermute | solution.py:514
  24.9 5.8 %collective-permute-start.10 = (f32[256,128]{1,0:T(8,128)S(1)}, f32[256,128]{1,0:T(8,128)S(1)}, u32[]{:S(2)}, u32[]{:S(2)}) collective-permute-start(f32[256,128]{1,0:T(8,128)S(1)} %found3.1.refs_11_.refs_2_), channel_id=1, source_target_pairs={{0,16},{8,24},{16,0},{24,8},{1,17},{9,25},{17,1},{25,9},{2,18},{10... | collective-permute-start | bytes 393224 | tf_op jit(solution)/shard_map/ppermute | solution.py:514
  28.2 5.0 %collective-permute-start.14 = (f32[256,128]{1,0:T(8,128)S(1)}, f32[256,128]{1,0:T(8,128)S(1)}, u32[]{:S(2)}, u32[]{:S(2)}) collective-permute-start(f32[256,128]{1,0:T(8,128)S(1)} %state.1.refs_3_.refs_1_), channel_id=1, source_target_pairs={{0,16},{8,24},{16,0},{24,8},{1,17},{9,25},{17,1},{25,9},{2,18},{10... | collective-permute-start | bytes 393224 | tf_op jit(solution)/shard_map/ppermute | solution.py:514
  29.4 2.0 %collective-permute-start.15 = (f32[1024,128]{1,0:T(8,128)S(1)}, f32[1024,128]{1,0:T(8,128)S(1)}, u32[]{:S(2)}, u32[]{:S(2)}) collective-permute-start(f32[1024,128]{1,0:T(8,128)S(1)} %joined.1.refs_9_), channel_id=1, source_target_pairs={{0,8},{8,0},{16,24},{24,16},{1,9},{9,1},{17,25},{25,17},{2,10},{10... | collective-permute-start | bytes 1572872 | tf_op jit(solution)/shard_map/ppermute | solution.py:514
  30.6 4.5 %collective-permute-start.13 = (f32[768,128]{1,0:T(8,128)S(1)}, f32[768,128]{1,0:T(8,128)S(1)}, u32[]{:S(2)}, u32[]{:S(2)}) collective-permute-start(f32[768,128]{1,0:T(8,128)S(1)} %theirs.1.refs_9_), channel_id=1, source_target_pairs={{0,8},{8,0},{16,24},{24,16},{1,9},{9,1},{17,25},{25,17},{2,10},{10... | collective-permute-start | bytes 1179656 | tf_op jit(solution)/shard_map/ppermute | solution.py:514
  33.3 1.8 %collective-permute-start.16 = (f32[256,128]{1,0:T(8,128)S(1)}, f32[256,128]{1,0:T(8,128)S(1)}, u32[]{:S(2)}, u32[]{:S(2)}) collective-permute-start(f32[256,128]{1,0:T(8,128)S(1)} %beside.1.refs_10_), channel_id=1, source_target_pairs={{0,8},{8,0},{16,24},{24,16},{1,9},{9,1},{17,25},{25,17},{2,10},{10... | collective-permute-start | bytes 393224 | tf_op jit(solution)/shard_map/ppermute | solution.py:514

commit v24 on v23

--- a/solution.py
+++ b/solution.py
@@ -583,14 +583,16 @@
     whole = [*levels, (len(early), 0, len(early) * two)]
     parted = [*levels, (len(early), 1, 0)]
     (block,) = finish([((0, 0), whole)], *every, [joined], None, True, None)
-    (block_far,) = finish([((1, 0), whole)], *every, [joined_far, block], None, True, None)
+    out, block_far = finish(
+        [((1, 0), whole)], *every, [joined_far, block], None, True, (1, (0, 0))
+    )
     beside = pack("beside", [(beside, two)], (block_far,))
     (out,) = finish(
-        [((0, 1), parted)], *every, [theirs, beside, block], None, False, (2, (0, 0))
+        [((0, 1), parted)], *every, [theirs, beside, block_far], out, False, (2, (1, 0))
     )
     beside_far = trade(beside, 1)
     return finish(
-        [((1, 1), parted)], *every, [theirs_far, beside_far, block_far], out, False, (2, (1, 0))
+        [((1, 1), parted)], *every, [theirs_far, beside_far], out, False, None
     )[0]
 
 

time: 37.3 us -> 37.2 us (level)
  waiting for transfers between devices: 3.61 us -> 2.97 us
  Pallas kernels: 13.4 us -> 14 us
    ppermute x17, waiting for transfers between devices: 3.61 us -> 2.97 us  [trade(): return lax.ppermute(value, AXES, pairs)]
    pallas_call x4, Pallas kernels: 5.42 us -> 5.98 us  [finish(): pl.pallas_call(functools.partial(finish_kernel, quarters, first_level, bi...]
  transfers between devices with their start and end apart: 17 -> 17, of which waited for: 7 -> 7; matrix products, arithmetic and copies ran while one was open for 0% -> 0% of each run, Pallas kernels for 25% -> 26%
where the time goes in v24:
time: 37.2 us; the launch traced here: 36.8 us
  starting transfers between devices  19.6 us (53%)
  Pallas kernels  14 us (38%)
  waiting for transfers between devices  2.97 us (8%)
    ppermute x17, starting transfers between devices, trade(): return lax.ppermute(value, AXES, pairs)  19.6 us
    pallas_call x21, Pallas kernels, call(): pl.pallas_call(kernel, in_specs=specs, out_specs=[HELD] * len(outputs), o...  8.03 us
    pallas_call x4, Pallas kernels, finish(): pl.pallas_call(functools.partial(finish_kernel, quarters, first_level, bi...  5.98 us
    ppermute x17, waiting for transfers between devices, trade(): return lax.ppermute(value, AXES, pairs)  2.97 us
  transfers between devices with their start and end apart: 17, of which 7 were waited for; matrix products, arithmetic and copies ran while one was open for 0% of the time, Pallas kernels for 26%

profile of v24, /device:TPU:0, one launch (start us, length us, event | category | flops | bytes accessed | tf_op | source)
XLA Modules:
  0.0 36.8 jit_solution(16327463607852390668)
XLA Ops:
  0.0 2.6 %states.1 = (f32[520,128]{1,0:T(8,128)S(1)}, f32[520,128]{1,0:T(8,128)S(1)}, bf16[3,128,1024]{2,1,0:T(8,128)(2,1)S(1)}, f32[2,8,1024]{2,1,0:T(8,128)S(1)}, f32[4...) custom-call(bf16[1024,128]{1,0:T(8,128)(2,1)} %refs_0_.2, ...), custom_call_target="tpu_custom_call" | custom-call | flops 2000000000 | bytes 1000000 | tf_op jit(solution)/shard_map/states/pallas_call | solution.py:50
  2.6 0.5 %collective-permute-start = (f32[520,128]{1,0:T(8,128)S(1)}, f32[520,128]{1,0:T(8,128)S(1)}, u32[]{:S(2)}, u32[]{:S(2)}) collective-permute-start(f32[520,128]{1,0:T(8,128)S(1)} %get-tuple-element.35), channel_id=1, source_target_pairs={{0,8},{8,0},{16,24},{24,16},{1,9},{9,1},{17,25},{25,17},{2,10},{10... | collective-permute-start | bytes 798728 | tf_op jit(solution)/shard_map/ppermute | solution.py:514
  3.2 1.1 %collective-permute-done.other_ref.refs_7_ = f32[520,128]{1,0:T(8,128)S(1)} collective-permute-done((f32[520,128]{1,0:T(8,128)S(1)}, f32[520,128]{1,0:T(8,128)S(1)}, u32[]{:S(2)}, u32[]{:S(2)}) %collective-permute-start) | collective-permute-done | bytes 266272 | tf_op jit(solution)/shard_map/ppermute | solution.py:514
  4.4 3.0 %collective-permute-start.2 = (f32[136,128]{1,0:T(8,128)S(1)}, f32[136,128]{1,0:T(8,128)S(1)}, u32[]{:S(2)}, u32[]{:S(2)}) collective-permute-start(f32[136,128]{1,0:T(8,128)S(1)} %get-tuple-element.46), channel_id=1, source_target_pairs={{0,16},{8,24},{16,0},{24,8},{1,17},{9,25},{17,1},{25,9},{2,18},{10... | collective-permute-start | bytes 208904 | tf_op jit(solution)/shard_map/ppermute | solution.py:514
  7.5 1.1 %load.1 = (bf16[1024,128]{1,0:T(8,128)(2,1)S(1)}, f32[8,8,1024]{2,1,0:T(8,128)S(1)}, f32[8,128]{1,0:T(8,128)S(1)}) custom-call(bf16[1024,128]{1,0:T(8,128)(2,1)} %refs_0_.3, f32[8,8,1024]{2,1,0:T(8,128)} %refs_1_.3, f32[8,128]{1,0:T(8,128)} %bitcast.1, f32[136,128]{1,0:T(8,128)S(1)} %get-tuple-element.36.refs_3_.refs_0_), custom_call_target="tpu_custom_call" | custom-call | flops 2000000000 | bytes 1000000 | tf_op jit(solution)/shard_map/load/pallas_call | solution.py:50
  8.5 0.9 %local0.1 = (f32[1024,1024]{1,0:T(8,128)S(1)}, f32[8,128]{1,0:T(8,128)S(1)}) custom-call(bf16[1024,128]{1,0:T(8,128)(2,1)S(1)} %get-tuple-element.37.refs_0_.refs_1_, bf16[1024,128]{1,0:T(8,128)(2,1)S(1)} %get-tuple-element.38.refs_1_, bf16[1024,1024]{1,0:T(8,128)(2,1)S(1)} %get-tuple-element.39.refs_2_, ...), custom_call_target="tpu_custom_call" | custom-call | flops 1000 | bytes 1000000 | tf_op jit(solution)/shard_map/local0/pallas_call | solution.py:50
  9.4 0.5 %collective-permute-done.2.refs_1_ = f32[136,128]{1,0:T(8,128)S(1)} collective-permute-done((f32[136,128]{1,0:T(8,128)S(1)}, f32[136,128]{1,0:T(8,128)S(1)}, u32[]{:S(2)}, u32[]{:S(2)}) %collective-permute-start.2) | collective-permute-done | bytes 69664 | tf_op jit(solution)/shard_map/ppermute | solution.py:514
  9.9 2.2 %collective-permute-start.3 = (f32[136,128]{1,0:T(8,128)S(1)}, f32[136,128]{1,0:T(8,128)S(1)}, u32[]{:S(2)}, u32[]{:S(2)}) collective-permute-start(f32[136,128]{1,0:T(8,128)S(1)} %merge11.1.refs_10_.refs_3_.refs_0_), channel_id=1, source_target_pairs={{0,1},{8,9},{16,17},{24,25},{1,0},{9,8},{17,16},{25,24},{2,3},{10,... | collective-permute-start | bytes 208904 | tf_op jit(solution)/shard_map/ppermute | solution.py:514
  12.2 1.1 %collective-permute-start.6 = (f32[136,128]{1,0:T(8,128)S(1)}, f32[136,128]{1,0:T(8,128)S(1)}, u32[]{:S(2)}, u32[]{:S(2)}) collective-permute-start(f32[136,128]{1,0:T(8,128)S(1)} %get-tuple-element.52.refs_0_.refs_2_), channel_id=1, source_target_pairs={{0,1},{8,9},{16,17},{24,25},{1,0},{9,8},{17,16},{25,24},{2,3},{10,... | collective-permute-start | bytes 208904 | tf_op jit(solution)/shard_map/ppermute | solution.py:514
  13.3 1.5 %collective-permute-start.8 = (f32[256,128]{1,0:T(8,128)S(1)}, f32[256,128]{1,0:T(8,128)S(1)}, u32[]{:S(2)}, u32[]{:S(2)}) collective-permute-start(f32[256,128]{1,0:T(8,128)S(1)} %rest.1), channel_id=1, source_target_pairs={{0,16},{8,24},{16,0},{24,8},{1,17},{9,25},{17,1},{25,9},{2,18},{10... | collective-permute-start | bytes 393224 | tf_op jit(solution)/shard_map/ppermute | solution.py:514
  14.8 1.0 %local1.1 = (f32[1024,1024]{1,0:T(8,128)S(1)}, f32[8,128]{1,0:T(8,128)S(1)}) custom-call(bf16[1024,128]{1,0:T(8,128)(2,1)S(1)} %get-tuple-element.37.refs_0_.refs_1_, bf16[1024,128]{1,0:T(8,128)(2,1)S(1)} %get-tuple-element.38.refs_1_, bf16[1024,1024]{1,0:T(8,128)(2,1)S(1)} %get-tuple-element.39.refs_2_, ...), custom_call_target="tpu_custom_call", output_to_operand_aliasing={{0}: (9, {})} | custom-call | flops 2000000000 | bytes 1000000 | tf_op jit(solution)/shard_map/local1/pallas_call | solution.py:50
  15.8 1.6 %collective-permute-start.5 = (f32[136,128]{1,0:T(8,128)S(1)}, f32[136,128]{1,0:T(8,128)S(1)}, u32[]{:S(2)}, u32[]{:S(2)}) collective-permute-start(f32[136,128]{1,0:T(8,128)S(1)} %merge21.1.refs_3_.refs_0_), channel_id=1, source_target_pairs={{0,2},{8,10},{16,18},{24,26},{1,3},{9,11},{17,19},{25,27},{2,0},{1... | collective-permute-start | bytes 208904 | tf_op jit(solution)/shard_map/ppermute | solution.py:514
  17.5 0.8 %collective-permute-start.7 = (f32[136,128]{1,0:T(8,128)S(1)}, f32[136,128]{1,0:T(8,128)S(1)}, u32[]{:S(2)}, u32[]{:S(2)}) collective-permute-start(f32[136,128]{1,0:T(8,128)S(1)} %get-tuple-element.55.refs_0_.refs_2_), channel_id=1, source_target_pairs={{0,2},{8,10},{16,18},{24,26},{1,3},{9,11},{17,19},{25,27},{2,0},{1... | collective-permute-start | bytes 208904 | tf_op jit(solution)/shard_map/ppermute | solution.py:514
  18.3 1.8 %collective-permute-start.9 = (f32[256,128]{1,0:T(8,128)S(1)}, f32[256,128]{1,0:T(8,128)S(1)}, u32[]{:S(2)}, u32[]{:S(2)}) collective-permute-start(f32[256,128]{1,0:T(8,128)S(1)} %found2.1.refs_1_), channel_id=1, source_target_pairs={{0,16},{8,24},{16,0},{24,8},{1,17},{9,25},{17,1},{25,9},{2,18},{10... | collective-permute-start | bytes 393224 | tf_op jit(solution)/shard_map/ppermute | solution.py:514
  20.3 2.7 %collective-permute-start.12 = (f32[136,128]{1,0:T(8,128)S(1)}, f32[136,128]{1,0:T(8,128)S(1)}, u32[]{:S(2)}, u32[]{:S(2)}) collective-permute-start(f32[136,128]{1,0:T(8,128)S(1)} %merge31.1.refs_3_.refs_10_), channel_id=1, source_target_pairs={{0,4},{8,12},{16,20},{24,28},{1,5},{9,13},{17,21},{25,29},{2,6},{1... | collective-permute-start | bytes 208904 | tf_op jit(solution)/shard_map/ppermute | solution.py:514
  23.0 1.9 %collective-permute-start.11 = (f32[136,128]{1,0:T(8,128)S(1)}, f32[136,128]{1,0:T(8,128)S(1)}, u32[]{:S(2)}, u32[]{:S(2)}) collective-permute-start(f32[136,128]{1,0:T(8,128)S(1)} %get-tuple-element.56.refs_2_), channel_id=1, source_target_pairs={{0,4},{8,12},{16,20},{24,28},{1,5},{9,13},{17,21},{25,29},{2,6},{1... | collective-permute-start | bytes 208904 | tf_op jit(solution)/shard_map/ppermute | solution.py:514
  24.9 0.7 %collective-permute-start.10 = (f32[256,128]{1,0:T(8,128)S(1)}, f32[256,128]{1,0:T(8,128)S(1)}, u32[]{:S(2)}, u32[]{:S(2)}) collective-permute-start(f32[256,128]{1,0:T(8,128)S(1)} %found3.1.refs_11_.refs_2_), channel_id=1, source_target_pairs={{0,16},{8,24},{16,0},{24,8},{1,17},{9,25},{17,1},{25,9},{2,18},{10... | collective-permute-start | bytes 393224 | tf_op jit(solution)/shard_map/ppermute | solution.py:514
  25.6 2.1 %local2.1 = (f32[1024,1024]{1,0:T(8,128)S(1)}, f32[8,128]{1,0:T(8,128)S(1)}) custom-call(bf16[1024,128]{1,0:T(8,128)(2,1)S(1)} %get-tuple-element.37.refs_0_.refs_1_, bf16[1024,128]{1,0:T(8,128)(2,1)S(1)} %get-tuple-element.38.refs_1_, bf16[1024,1024]{1,0:T(8,128)(2,1)S(1)} %get-tuple-element.39.refs_2_, ...), custom_call_target="tpu_custom_call", output_to_operand_aliasing={{0}: (9, {})} | custom-call | flops 1000 | bytes 1000000 | tf_op jit(solution)/shard_map/local2/pallas_call | solution.py:50
  27.7 0.5 %collective-permute-done.11.refs_0_ = f32[136,128]{1,0:T(8,128)S(1)} collective-permute-done((f32[136,128]{1,0:T(8,128)S(1)}, f32[136,128]{1,0:T(8,128)S(1)}, u32[]{:S(2)}, u32[]{:S(2)}) %collective-permute-start.11) | collective-permute-done | bytes 69664 | tf_op jit(solution)/shard_map/ppermute | solution.py:514
  28.2 1.1 %collective-permute-start.14 = (f32[256,128]{1,0:T(8,128)S(1)}, f32[256,128]{1,0:T(8,128)S(1)}, u32[]{:S(2)}, u32[]{:S(2)}) collective-permute-start(f32[256,128]{1,0:T(8,128)S(1)} %state.1.refs_3_.refs_1_), channel_id=1, source_target_pairs={{0,16},{8,24},{16,0},{24,8},{1,17},{9,25},{17,1},{25,9},{2,18},{10... | collective-permute-start | bytes 393224 | tf_op jit(solution)/shard_map/ppermute | solution.py:514
  29.5 1.0 %finish00.1.refs_10_ = bf16[1024,256]{1,0:T(8,128)(2,1)S(1)} custom-call(f32[1024,1024]{1,0:T(8,128)S(1)} %get-tuple-element.57.refs_0_, bf16[1024,128]{1,0:T(8,128)(2,1)S(1)} %get-tuple-element.37.refs_0_.refs_1_, f32[2,8,1024]{2,1,0:T(8,128)S(1)} %get-tuple-element.40.refs_3_.refs_2_, f32[8,8,1024]{2,1,0:T(8,128)S(1)} %get-tuple-element.42.refs_5_.refs_3_, ...), custom_call_target="tpu_custom_call" | custom-call | flops 20000000000 | bytes 1000000 | tf_op jit(solution)/shard_map/finish00/pallas_call | solution.py:490
  31.4 1.6 %finish10.1 = (bf16[1024,1024]{1,0:T(8,128)(2,1)}, bf16[1024,256]{1,0:T(8,128)(2,1)S(1)}) custom-call(f32[1024,1024]{1,0:T(8,128)S(1)} %get-tuple-element.57.refs_0_, bf16[1024,128]{1,0:T(8,128)(2,1)S(1)} %get-tuple-element.37.refs_0_.refs_1_, f32[2,8,1024]{2,1,0:T(8,128)S(1)} %get-tuple-element.40.refs_3_.refs_2_, ...), custom_call_target="tpu_custom_call" | custom-call | flops 1000 | bytes 1000000 | tf_op jit(solution)/shard_map/finish10/pallas_call | solution.py:490
  33.4 1.7 %finish01.1.refs_11_ = bf16[1024,1024]{1,0:T(8,128)(2,1)} custom-call(f32[1024,1024]{1,0:T(8,128)S(1)} %get-tuple-element.57.refs_0_, bf16[1024,128]{1,0:T(8,128)(2,1)S(1)} %get-tuple-element.37.refs_0_.refs_1_, f32[2,8,1024]{2,1,0:T(8,128)S(1)} %get-tuple-element.40.refs_3_.refs_2_, ...), custom_call_target="tpu_custom_call", output_to_operand_aliasing={{}: (12, {})} | custom-call | flops 20000000000 | bytes 1000000 | tf_op jit(solution)/shard_map/finish01/pallas_call | solution.py:490
  35.1 1.6 %finish11.1 = bf16[1024,1024]{1,0:T(8,128)(2,1)} custom-call(f32[1024,1024]{1,0:T(8,128)S(1)} %get-tuple-element.57.refs_0_, bf16[1024,128]{1,0:T(8,128)(2,1)S(1)} %get-tuple-element.37.refs_0_.refs_1_, f32[2,8,1024]{2,1,0:T(8,128)S(1)} %get-tuple-element.40.refs_3_.refs_2_, ...), custom_call_target="tpu_custom_call", output_to_operand_aliasing={{}: (11, {})} | custom-call | flops 2000000000 | bytes 1000000 | tf_op jit(solution)/shard_map/finish11/pallas_call | solution.py:490
  (35 shorter events, 2.0 us)
Async XLA Ops:
  2.6 1.7 %collective-permute-start = (f32[520,128]{1,0:T(8,128)S(1)}, f32[520,128]{1,0:T(8,128)S(1)}, u32[]{:S(2)}, u32[]{:S(2)}) collective-permute-start(f32[520,128]{1,0:T(8,128)S(1)} %get-tuple-element.35), channel_id=1, source_target_pairs={{0,8},{8,0},{16,24},{24,16},{1,9},{9,1},{17,25},{25,17},{2,10},{10... | collective-permute-start | bytes 798728 | tf_op jit(solution)/shard_map/ppermute | solution.py:514
  3.1 5.4 %collective-permute-start.1 = (f32[520,128]{1,0:T(8,128)S(1)}, f32[520,128]{1,0:T(8,128)S(1)}, u32[]{:S(2)}, u32[]{:S(2)}) collective-permute-start(f32[520,128]{1,0:T(8,128)S(1)} %get-tuple-element.34.mine_ref), channel_id=1, source_target_pairs={{0,8},{8,0},{16,24},{24,16},{1,9},{9,1},{17,25},{25,17},{2,10},{10... | collective-permute-start | bytes 798728 | tf_op jit(solution)/shard_map/ppermute | solution.py:514
  4.4 5.5 %collective-permute-start.2 = (f32[136,128]{1,0:T(8,128)S(1)}, f32[136,128]{1,0:T(8,128)S(1)}, u32[]{:S(2)}, u32[]{:S(2)}) collective-permute-start(f32[136,128]{1,0:T(8,128)S(1)} %get-tuple-element.46), channel_id=1, source_target_pairs={{0,16},{8,24},{16,0},{24,8},{1,17},{9,25},{17,1},{25,9},{2,18},{10... | collective-permute-start | bytes 208904 | tf_op jit(solution)/shard_map/ppermute | solution.py:514
  7.4 4.8 %collective-permute-start.4 = (f32[136,128]{1,0:T(8,128)S(1)}, f32[136,128]{1,0:T(8,128)S(1)}, u32[]{:S(2)}, u32[]{:S(2)}) collective-permute-start(f32[136,128]{1,0:T(8,128)S(1)} %get-tuple-element.49), channel_id=1, source_target_pairs={{0,16},{8,24},{16,0},{24,8},{1,17},{9,25},{17,1},{25,9},{2,18},{10... | collective-permute-start | bytes 208904 | tf_op jit(solution)/shard_map/ppermute | solution.py:514
  9.9 5.9 %collective-permute-start.3 = (f32[136,128]{1,0:T(8,128)S(1)}, f32[136,128]{1,0:T(8,128)S(1)}, u32[]{:S(2)}, u32[]{:S(2)}) collective-permute-start(f32[136,128]{1,0:T(8,128)S(1)} %merge11.1.refs_10_.refs_3_.refs_0_), channel_id=1, source_target_pairs={{0,1},{8,9},{16,17},{24,25},{1,0},{9,8},{17,16},{25,24},{2,3},{10,... | collective-permute-start | bytes 208904 | tf_op jit(solution)/shard_map/ppermute | solution.py:514
  12.2 5.3 %collective-permute-start.6 = (f32[136,128]{1,0:T(8,128)S(1)}, f32[136,128]{1,0:T(8,128)S(1)}, u32[]{:S(2)}, u32[]{:S(2)}) collective-permute-start(f32[136,128]{1,0:T(8,128)S(1)} %get-tuple-element.52.refs_0_.refs_2_), channel_id=1, source_target_pairs={{0,1},{8,9},{16,17},{24,25},{1,0},{9,8},{17,16},{25,24},{2,3},{10,... | collective-permute-start | bytes 208904 | tf_op jit(solution)/shard_map/ppermute | solution.py:514
  13.3 9.6 %collective-permute-start.8 = (f32[256,128]{1,0:T(8,128)S(1)}, f32[256,128]{1,0:T(8,128)S(1)}, u32[]{:S(2)}, u32[]{:S(2)}) collective-permute-start(f32[256,128]{1,0:T(8,128)S(1)} %rest.1), channel_id=1, source_target_pairs={{0,16},{8,24},{16,0},{24,8},{1,17},{9,25},{17,1},{25,9},{2,18},{10... | collective-permute-start | bytes 393224 | tf_op jit(solution)/shard_map/ppermute | solution.py:514
  15.8 4.4 %collective-permute-start.5 = (f32[136,128]{1,0:T(8,128)S(1)}, f32[136,128]{1,0:T(8,128)S(1)}, u32[]{:S(2)}, u32[]{:S(2)}) collective-permute-start(f32[136,128]{1,0:T(8,128)S(1)} %merge21.1.refs_3_.refs_0_), channel_id=1, source_target_pairs={{0,2},{8,10},{16,18},{24,26},{1,3},{9,11},{17,19},{25,27},{2,0},{1... | collective-permute-start | bytes 208904 | tf_op jit(solution)/shard_map/ppermute | solution.py:514
  17.5 5.4 %collective-permute-start.7 = (f32[136,128]{1,0:T(8,128)S(1)}, f32[136,128]{1,0:T(8,128)S(1)}, u32[]{:S(2)}, u32[]{:S(2)}) collective-permute-start(f32[136,128]{1,0:T(8,128)S(1)} %get-tuple-element.55.refs_0_.refs_2_), channel_id=1, source_target_pairs={{0,2},{8,10},{16,18},{24,26},{1,3},{9,11},{17,19},{25,27},{2,0},{1... | collective-permute-start | bytes 208904 | tf_op jit(solution)/shard_map/ppermute | solution.py:514
  18.3 12.2 %collective-permute-start.9 = (f32[256,128]{1,0:T(8,128)S(1)}, f32[256,128]{1,0:T(8,128)S(1)}, u32[]{:S(2)}, u32[]{:S(2)}) collective-permute-start(f32[256,128]{1,0:T(8,128)S(1)} %found2.1.refs_1_), channel_id=1, source_target_pairs={{0,16},{8,24},{16,0},{24,8},{1,17},{9,25},{17,1},{25,9},{2,18},{10... | collective-permute-start | bytes 393224 | tf_op jit(solution)/shard_map/ppermute | solution.py:514
  20.3 8.0 %collective-permute-start.12 = (f32[136,128]{1,0:T(8,128)S(1)}, f32[136,128]{1,0:T(8,128)S(1)}, u32[]{:S(2)}, u32[]{:S(2)}) collective-permute-start(f32[136,128]{1,0:T(8,128)S(1)} %merge31.1.refs_3_.refs_10_), channel_id=1, source_target_pairs={{0,4},{8,12},{16,20},{24,28},{1,5},{9,13},{17,21},{25,29},{2,6},{1... | collective-permute-start | bytes 208904 | tf_op jit(solution)/shard_map/ppermute | solution.py:514
  23.0 5.3 %collective-permute-start.11 = (f32[136,128]{1,0:T(8,128)S(1)}, f32[136,128]{1,0:T(8,128)S(1)}, u32[]{:S(2)}, u32[]{:S(2)}) collective-permute-start(f32[136,128]{1,0:T(8,128)S(1)} %get-tuple-element.56.refs_2_), channel_id=1, source_target_pairs={{0,4},{8,12},{16,20},{24,28},{1,5},{9,13},{17,21},{25,29},{2,6},{1... | collective-permute-start | bytes 208904 | tf_op jit(solution)/shard_map/ppermute | solution.py:514
  24.9 5.8 %collective-permute-start.10 = (f32[256,128]{1,0:T(8,128)S(1)}, f32[256,128]{1,0:T(8,128)S(1)}, u32[]{:S(2)}, u32[]{:S(2)}) collective-permute-start(f32[256,128]{1,0:T(8,128)S(1)} %found3.1.refs_11_.refs_2_), channel_id=1, source_target_pairs={{0,16},{8,24},{16,0},{24,8},{1,17},{9,25},{17,1},{25,9},{2,18},{10... | collective-permute-start | bytes 393224 | tf_op jit(solution)/shard_map/ppermute | solution.py:514
  28.2 5.0 %collective-permute-start.14 = (f32[256,128]{1,0:T(8,128)S(1)}, f32[256,128]{1,0:T(8,128)S(1)}, u32[]{:S(2)}, u32[]{:S(2)}) collective-permute-start(f32[256,128]{1,0:T(8,128)S(1)} %state.1.refs_3_.refs_1_), channel_id=1, source_target_pairs={{0,16},{8,24},{16,0},{24,8},{1,17},{9,25},{17,1},{25,9},{2,18},{10... | collective-permute-start | bytes 393224 | tf_op jit(solution)/shard_map/ppermute | solution.py:514
  29.4 2.0 %collective-permute-start.15 = (f32[1024,128]{1,0:T(8,128)S(1)}, f32[1024,128]{1,0:T(8,128)S(1)}, u32[]{:S(2)}, u32[]{:S(2)}) collective-permute-start(f32[1024,128]{1,0:T(8,128)S(1)} %joined.1.refs_9_), channel_id=1, source_target_pairs={{0,8},{8,0},{16,24},{24,16},{1,9},{9,1},{17,25},{25,17},{2,10},{10... | collective-permute-start | bytes 1572872 | tf_op jit(solution)/shard_map/ppermute | solution.py:514
  30.6 4.5 %collective-permute-start.13 = (f32[768,128]{1,0:T(8,128)S(1)}, f32[768,128]{1,0:T(8,128)S(1)}, u32[]{:S(2)}, u32[]{:S(2)}) collective-permute-start(f32[768,128]{1,0:T(8,128)S(1)} %theirs.1.refs_9_), channel_id=1, source_target_pairs={{0,8},{8,0},{16,24},{24,16},{1,9},{9,1},{17,25},{25,17},{2,10},{10... | collective-permute-start | bytes 1179656 | tf_op jit(solution)/shard_map/ppermute | solution.py:514
  33.3 1.8 %collective-permute-start.16 = (f32[256,128]{1,0:T(8,128)S(1)}, f32[256,128]{1,0:T(8,128)S(1)}, u32[]{:S(2)}, u32[]{:S(2)}) collective-permute-start(f32[256,128]{1,0:T(8,128)S(1)} %beside.1.refs_10_), channel_id=1, source_target_pairs={{0,8},{8,0},{16,24},{24,16},{1,9},{9,1},{17,25},{25,17},{2,10},{10... | collective-permute-start | bytes 393224 | tf_op jit(solution)/shard_map/ppermute | solution.py:514

commit v25 on v24

--- a/solution.py
+++ b/solution.py
@@ -562,11 +562,13 @@
             chunks = [merged[offset] for offset in range(CUTS)]
             newest = merged[order[-1]]
             prefixes += after
-            found[bit] = both(f"found{bit}", found[bit], (newest,))
-            if bit > 1:
-                across[bit] = trade(found[bit], 2)
-            else:
+            if bit == 1:
+                found[bit] = both("found1", found[bit], (newest,))
                 rest = trade(both("rest", stays, (newest,)), 2)
+            if bit == last - 1:
+                for level in range(2, last):
+                    found[level] = both(f"found{level}", found[level], (newest,))
+                    across[level] = trade(found[level], 2)
 
     state = both("state", found[last], waits)
     beside = trade(state, 2)

time: 37.2 us -> 38 us (1.022)
  waiting for transfers between devices: 2.97 us -> 4.87 us
  starting transfers between devices: 19.6 us -> 18.8 us
    ppermute x17, waiting for transfers between devices: 2.97 us -> 4.87 us  [trade(): return lax.ppermute(value, AXES, pairs)]
    ppermute x17, starting transfers between devices: 19.6 us -> 18.8 us  [trade(): return lax.ppermute(value, AXES, pairs)]
  transfers between devices with their start and end apart: 17 -> 17, of which waited for: 7 -> 5; matrix products, arithmetic and copies ran while one was open for 0% -> 0% of each run, Pallas kernels for 26% -> 26%
where the time goes in v25:
time: 38 us; the launch traced here: 37.9 us
  starting transfers between devices  18.8 us (49%)
  Pallas kernels  14 us (37%)
  waiting for transfers between devices  4.87 us (13%)
    ppermute x17, starting transfers between devices, trade(): return lax.ppermute(value, AXES, pairs)  18.8 us
    pallas_call x21, Pallas kernels, call(): pl.pallas_call(kernel, in_specs=specs, out_specs=[HELD] * len(outputs), o...  8.03 us
    pallas_call x4, Pallas kernels, finish(): pl.pallas_call(functools.partial(finish_kernel, quarters, first_level, bi...  5.95 us
    ppermute x17, waiting for transfers between devices, trade(): return lax.ppermute(value, AXES, pairs)  4.87 us
  transfers between devices with their start and end apart: 17, of which 5 were waited for; matrix products, arithmetic and copies ran while one was open for 0% of the time, Pallas kernels for 26%

profile of v25, /device:TPU:0, one launch (start us, length us, event | category | flops | bytes accessed | tf_op | source)
XLA Modules:
  0.0 37.9 jit_solution(1142454168604528958)
XLA Ops:
  0.0 2.6 %states.1 = (f32[520,128]{1,0:T(8,128)S(1)}, f32[520,128]{1,0:T(8,128)S(1)}, bf16[3,128,1024]{2,1,0:T(8,128)(2,1)S(1)}, f32[2,8,1024]{2,1,0:T(8,128)S(1)}, f32[4...) custom-call(bf16[1024,128]{1,0:T(8,128)(2,1)} %refs_0_.2, ...), custom_call_target="tpu_custom_call" | custom-call | flops 2000000000 | bytes 1000000 | tf_op jit(solution)/shard_map/states/pallas_call | solution.py:50
  2.6 0.5 %collective-permute-start = (f32[520,128]{1,0:T(8,128)S(1)}, f32[520,128]{1,0:T(8,128)S(1)}, u32[]{:S(2)}, u32[]{:S(2)}) collective-permute-start(f32[520,128]{1,0:T(8,128)S(1)} %get-tuple-element.35), channel_id=1, source_target_pairs={{0,8},{8,0},{16,24},{24,16},{1,9},{9,1},{17,25},{25,17},{2,10},{10... | collective-permute-start | bytes 798728 | tf_op jit(solution)/shard_map/ppermute | solution.py:514
  3.2 1.1 %collective-permute-done.other_ref.refs_7_ = f32[520,128]{1,0:T(8,128)S(1)} collective-permute-done((f32[520,128]{1,0:T(8,128)S(1)}, f32[520,128]{1,0:T(8,128)S(1)}, u32[]{:S(2)}, u32[]{:S(2)}) %collective-permute-start) | collective-permute-done | bytes 266272 | tf_op jit(solution)/shard_map/ppermute | solution.py:514
  4.4 3.0 %collective-permute-start.2 = (f32[136,128]{1,0:T(8,128)S(1)}, f32[136,128]{1,0:T(8,128)S(1)}, u32[]{:S(2)}, u32[]{:S(2)}) collective-permute-start(f32[136,128]{1,0:T(8,128)S(1)} %get-tuple-element.46), channel_id=1, source_target_pairs={{0,16},{8,24},{16,0},{24,8},{1,17},{9,25},{17,1},{25,9},{2,18},{10... | collective-permute-start | bytes 208904 | tf_op jit(solution)/shard_map/ppermute | solution.py:514
  7.5 1.1 %load.1 = (bf16[1024,128]{1,0:T(8,128)(2,1)S(1)}, f32[8,8,1024]{2,1,0:T(8,128)S(1)}, f32[8,128]{1,0:T(8,128)S(1)}) custom-call(bf16[1024,128]{1,0:T(8,128)(2,1)} %refs_0_.3, f32[8,8,1024]{2,1,0:T(8,128)} %refs_1_.3, f32[8,128]{1,0:T(8,128)} %bitcast.1, f32[136,128]{1,0:T(8,128)S(1)} %get-tuple-element.36.refs_3_.refs_0_), custom_call_target="tpu_custom_call" | custom-call | flops 2000000000 | bytes 1000000 | tf_op jit(solution)/shard_map/load/pallas_call | solution.py:50
  8.5 0.9 %local0.1 = (f32[1024,1024]{1,0:T(8,128)S(1)}, f32[8,128]{1,0:T(8,128)S(1)}) custom-call(bf16[1024,128]{1,0:T(8,128)(2,1)S(1)} %get-tuple-element.37.refs_0_.refs_1_, bf16[1024,128]{1,0:T(8,128)(2,1)S(1)} %get-tuple-element.38.refs_1_, bf16[1024,1024]{1,0:T(8,128)(2,1)S(1)} %get-tuple-element.39.refs_2_, ...), custom_call_target="tpu_custom_call" | custom-call | flops 1000 | bytes 1000000 | tf_op jit(solution)/shard_map/local0/pallas_call | solution.py:50
  9.9 2.2 %collective-permute-start.3 = (f32[136,128]{1,0:T(8,128)S(1)}, f32[136,128]{1,0:T(8,128)S(1)}, u32[]{:S(2)}, u32[]{:S(2)}) collective-permute-start(f32[136,128]{1,0:T(8,128)S(1)} %merge11.1.refs_10_.refs_3_.refs_0_), channel_id=1, source_target_pairs={{0,1},{8,9},{16,17},{24,25},{1,0},{9,8},{17,16},{25,24},{2,3},{10,... | collective-permute-start | bytes 208904 | tf_op jit(solution)/shard_map/ppermute | solution.py:514
  12.2 1.1 %collective-permute-start.6 = (f32[136,128]{1,0:T(8,128)S(1)}, f32[136,128]{1,0:T(8,128)S(1)}, u32[]{:S(2)}, u32[]{:S(2)}) collective-permute-start(f32[136,128]{1,0:T(8,128)S(1)} %get-tuple-element.52.refs_0_.refs_2_), channel_id=1, source_target_pairs={{0,1},{8,9},{16,17},{24,25},{1,0},{9,8},{17,16},{25,24},{2,3},{10,... | collective-permute-start | bytes 208904 | tf_op jit(solution)/shard_map/ppermute | solution.py:514
  13.3 1.4 %collective-permute-start.8 = (f32[256,128]{1,0:T(8,128)S(1)}, f32[256,128]{1,0:T(8,128)S(1)}, u32[]{:S(2)}, u32[]{:S(2)}) collective-permute-start(f32[256,128]{1,0:T(8,128)S(1)} %rest.1), channel_id=1, source_target_pairs={{0,16},{8,24},{16,0},{24,8},{1,17},{9,25},{17,1},{25,9},{2,18},{10... | collective-permute-start | bytes 393224 | tf_op jit(solution)/shard_map/ppermute | solution.py:514
  14.7 1.0 %local1.1 = (f32[1024,1024]{1,0:T(8,128)S(1)}, f32[8,128]{1,0:T(8,128)S(1)}) custom-call(bf16[1024,128]{1,0:T(8,128)(2,1)S(1)} %get-tuple-element.37.refs_0_.refs_1_, bf16[1024,128]{1,0:T(8,128)(2,1)S(1)} %get-tuple-element.38.refs_1_, bf16[1024,1024]{1,0:T(8,128)(2,1)S(1)} %get-tuple-element.39.refs_2_, ...), custom_call_target="tpu_custom_call", output_to_operand_aliasing={{0}: (9, {})} | custom-call | flops 2000000000 | bytes 1000000 | tf_op jit(solution)/shard_map/local1/pallas_call | solution.py:50
  15.8 1.6 %collective-permute-start.5 = (f32[136,128]{1,0:T(8,128)S(1)}, f32[136,128]{1,0:T(8,128)S(1)}, u32[]{:S(2)}, u32[]{:S(2)}) collective-permute-start(f32[136,128]{1,0:T(8,128)S(1)} %merge21.1.refs_3_.refs_0_), channel_id=1, source_target_pairs={{0,2},{8,10},{16,18},{24,26},{1,3},{9,11},{17,19},{25,27},{2,0},{1... | collective-permute-start | bytes 208904 | tf_op jit(solution)/shard_map/ppermute | solution.py:514
  17.5 0.8 %collective-permute-start.7 = (f32[136,128]{1,0:T(8,128)S(1)}, f32[136,128]{1,0:T(8,128)S(1)}, u32[]{:S(2)}, u32[]{:S(2)}) collective-permute-start(f32[136,128]{1,0:T(8,128)S(1)} %get-tuple-element.55.refs_0_), channel_id=1, source_target_pairs={{0,2},{8,10},{16,18},{24,26},{1,3},{9,11},{17,19},{25,27},{2,0},{1... | collective-permute-start | bytes 208904 | tf_op jit(solution)/shard_map/ppermute | solution.py:514
  18.3 1.9 %collective-permute-done.5.refs_1_ = f32[136,128]{1,0:T(8,128)S(1)} collective-permute-done((f32[136,128]{1,0:T(8,128)S(1)}, f32[136,128]{1,0:T(8,128)S(1)}, u32[]{:S(2)}, u32[]{:S(2)}) %collective-permute-start.5) | collective-permute-done | bytes 69664 | tf_op jit(solution)/shard_map/ppermute | solution.py:514
  20.2 2.7 %collective-permute-start.12 = (f32[136,128]{1,0:T(8,128)S(1)}, f32[136,128]{1,0:T(8,128)S(1)}, u32[]{:S(2)}, u32[]{:S(2)}) collective-permute-start(f32[136,128]{1,0:T(8,128)S(1)} %merge31.1.refs_3_.refs_10_), channel_id=1, source_target_pairs={{0,4},{8,12},{16,20},{24,28},{1,5},{9,13},{17,21},{25,29},{2,6},{1... | collective-permute-start | bytes 208904 | tf_op jit(solution)/shard_map/ppermute | solution.py:514
  22.9 1.9 %collective-permute-start.11 = (f32[136,128]{1,0:T(8,128)S(1)}, f32[136,128]{1,0:T(8,128)S(1)}, u32[]{:S(2)}, u32[]{:S(2)}) collective-permute-start(f32[136,128]{1,0:T(8,128)S(1)} %get-tuple-element.56.refs_2_), channel_id=1, source_target_pairs={{0,4},{8,12},{16,20},{24,28},{1,5},{9,13},{17,21},{25,29},{2,6},{1... | collective-permute-start | bytes 208904 | tf_op jit(solution)/shard_map/ppermute | solution.py:514
  24.8 0.8 %collective-permute-start.9 = (f32[256,128]{1,0:T(8,128)S(1)}, f32[256,128]{1,0:T(8,128)S(1)}, u32[]{:S(2)}, u32[]{:S(2)}) collective-permute-start(f32[256,128]{1,0:T(8,128)S(1)} %found2.1.refs_1_), channel_id=1, source_target_pairs={{0,16},{8,24},{16,0},{24,8},{1,17},{9,25},{17,1},{25,9},{2,18},{10... | collective-permute-start | bytes 393224 | tf_op jit(solution)/shard_map/ppermute | solution.py:514
  25.6 1.4 %collective-permute-start.10 = (f32[256,128]{1,0:T(8,128)S(1)}, f32[256,128]{1,0:T(8,128)S(1)}, u32[]{:S(2)}, u32[]{:S(2)}) collective-permute-start(f32[256,128]{1,0:T(8,128)S(1)} %found3.1.refs_11_.refs_2_), channel_id=1, source_target_pairs={{0,16},{8,24},{16,0},{24,8},{1,17},{9,25},{17,1},{25,9},{2,18},{10... | collective-permute-start | bytes 393224 | tf_op jit(solution)/shard_map/ppermute | solution.py:514
  27.0 2.1 %local2.1 = (f32[1024,1024]{1,0:T(8,128)S(1)}, f32[8,128]{1,0:T(8,128)S(1)}) custom-call(bf16[1024,128]{1,0:T(8,128)(2,1)S(1)} %get-tuple-element.37.refs_0_.refs_1_, bf16[1024,128]{1,0:T(8,128)(2,1)S(1)} %get-tuple-element.38.refs_1_, bf16[1024,1024]{1,0:T(8,128)(2,1)S(1)} %get-tuple-element.39.refs_2_, ...), custom_call_target="tpu_custom_call", output_to_operand_aliasing={{0}: (9, {})} | custom-call | flops 1000 | bytes 1000000 | tf_op jit(solution)/shard_map/local2/pallas_call | solution.py:50
  29.1 0.8 %collective-permute-start.14 = (f32[256,128]{1,0:T(8,128)S(1)}, f32[256,128]{1,0:T(8,128)S(1)}, u32[]{:S(2)}, u32[]{:S(2)}) collective-permute-start(f32[256,128]{1,0:T(8,128)S(1)} %state.1.refs_3_.refs_1_), channel_id=1, source_target_pairs={{0,16},{8,24},{16,0},{24,8},{1,17},{9,25},{17,1},{25,9},{2,18},{10... | collective-permute-start | bytes 393224 | tf_op jit(solution)/shard_map/ppermute | solution.py:514
  30.0 1.0 %finish00.1.refs_10_ = bf16[1024,256]{1,0:T(8,128)(2,1)S(1)} custom-call(f32[1024,1024]{1,0:T(8,128)S(1)} %get-tuple-element.57.refs_0_, bf16[1024,128]{1,0:T(8,128)(2,1)S(1)} %get-tuple-element.37.refs_0_.refs_1_, f32[2,8,1024]{2,1,0:T(8,128)S(1)} %get-tuple-element.40.refs_3_.refs_2_, f32[8,8,1024]{2,1,0:T(8,128)S(1)} %get-tuple-element.42.refs_5_.refs_3_, ...), custom_call_target="tpu_custom_call" | custom-call | flops 20000000000 | bytes 1000000 | tf_op jit(solution)/shard_map/finish00/pallas_call | solution.py:490
  31.0 1.2 %collective-permute-done.10.refs_2_ = f32[256,128]{1,0:T(8,128)S(1)} collective-permute-done((f32[256,128]{1,0:T(8,128)S(1)}, f32[256,128]{1,0:T(8,128)S(1)}, u32[]{:S(2)}, u32[]{:S(2)}) %collective-permute-start.10) | collective-permute-done | bytes 131104 | tf_op jit(solution)/shard_map/ppermute | solution.py:514
  32.3 1.6 %finish10.1 = (bf16[1024,1024]{1,0:T(8,128)(2,1)}, bf16[1024,256]{1,0:T(8,128)(2,1)S(1)}) custom-call(f32[1024,1024]{1,0:T(8,128)S(1)} %get-tuple-element.57.refs_0_, bf16[1024,128]{1,0:T(8,128)(2,1)S(1)} %get-tuple-element.37.refs_0_.refs_1_, f32[2,8,1024]{2,1,0:T(8,128)S(1)} %get-tuple-element.40.refs_3_.refs_2_, ...), custom_call_target="tpu_custom_call" | custom-call | flops 1000 | bytes 1000000 | tf_op jit(solution)/shard_map/finish10/pallas_call | solution.py:490
  34.5 1.7 %finish01.1.refs_11_ = bf16[1024,1024]{1,0:T(8,128)(2,1)} custom-call(f32[1024,1024]{1,0:T(8,128)S(1)} %get-tuple-element.57.refs_0_, bf16[1024,128]{1,0:T(8,128)(2,1)S(1)} %get-tuple-element.37.refs_0_.refs_1_, f32[2,8,1024]{2,1,0:T(8,128)S(1)} %get-tuple-element.40.refs_3_.refs_2_, ...), custom_call_target="tpu_custom_call", output_to_operand_aliasing={{}: (12, {})} | custom-call | flops 20000000000 | bytes 1000000 | tf_op jit(solution)/shard_map/finish01/pallas_call | solution.py:490
  36.2 1.6 %finish11.1 = bf16[1024,1024]{1,0:T(8,128)(2,1)} custom-call(f32[1024,1024]{1,0:T(8,128)S(1)} %get-tuple-element.57.refs_0_, bf16[1024,128]{1,0:T(8,128)(2,1)S(1)} %get-tuple-element.37.refs_0_.refs_1_, f32[2,8,1024]{2,1,0:T(8,128)S(1)} %get-tuple-element.40.refs_3_.refs_2_, ...), custom_call_target="tpu_custom_call", output_to_operand_aliasing={{}: (11, {})} | custom-call | flops 2000000000 | bytes 1000000 | tf_op jit(solution)/shard_map/finish11/pallas_call | solution.py:490
  (35 shorter events, 1.8 us)
Async XLA Ops:
  2.6 1.7 %collective-permute-start = (f32[520,128]{1,0:T(8,128)S(1)}, f32[520,128]{1,0:T(8,128)S(1)}, u32[]{:S(2)}, u32[]{:S(2)}) collective-permute-start(f32[520,128]{1,0:T(8,128)S(1)} %get-tuple-element.35), channel_id=1, source_target_pairs={{0,8},{8,0},{16,24},{24,16},{1,9},{9,1},{17,25},{25,17},{2,10},{10... | collective-permute-start | bytes 798728 | tf_op jit(solution)/shard_map/ppermute | solution.py:514
  3.1 5.4 %collective-permute-start.1 = (f32[520,128]{1,0:T(8,128)S(1)}, f32[520,128]{1,0:T(8,128)S(1)}, u32[]{:S(2)}, u32[]{:S(2)}) collective-permute-start(f32[520,128]{1,0:T(8,128)S(1)} %get-tuple-element.34.mine_ref), channel_id=1, source_target_pairs={{0,8},{8,0},{16,24},{24,16},{1,9},{9,1},{17,25},{25,17},{2,10},{10... | collective-permute-start | bytes 798728 | tf_op jit(solution)/shard_map/ppermute | solution.py:514
  4.4 5.5 %collective-permute-start.2 = (f32[136,128]{1,0:T(8,128)S(1)}, f32[136,128]{1,0:T(8,128)S(1)}, u32[]{:S(2)}, u32[]{:S(2)}) collective-permute-start(f32[136,128]{1,0:T(8,128)S(1)} %get-tuple-element.46), channel_id=1, source_target_pairs={{0,16},{8,24},{16,0},{24,8},{1,17},{9,25},{17,1},{25,9},{2,18},{10... | collective-permute-start | bytes 208904 | tf_op jit(solution)/shard_map/ppermute | solution.py:514
  7.4 4.8 %collective-permute-start.4 = (f32[136,128]{1,0:T(8,128)S(1)}, f32[136,128]{1,0:T(8,128)S(1)}, u32[]{:S(2)}, u32[]{:S(2)}) collective-permute-start(f32[136,128]{1,0:T(8,128)S(1)} %get-tuple-element.49), channel_id=1, source_target_pairs={{0,16},{8,24},{16,0},{24,8},{1,17},{9,25},{17,1},{25,9},{2,18},{10... | collective-permute-start | bytes 208904 | tf_op jit(solution)/shard_map/ppermute | solution.py:514
  9.9 5.8 %collective-permute-start.3 = (f32[136,128]{1,0:T(8,128)S(1)}, f32[136,128]{1,0:T(8,128)S(1)}, u32[]{:S(2)}, u32[]{:S(2)}) collective-permute-start(f32[136,128]{1,0:T(8,128)S(1)} %merge11.1.refs_10_.refs_3_.refs_0_), channel_id=1, source_target_pairs={{0,1},{8,9},{16,17},{24,25},{1,0},{9,8},{17,16},{25,24},{2,3},{10,... | collective-permute-start | bytes 208904 | tf_op jit(solution)/shard_map/ppermute | solution.py:514
  12.2 5.2 %collective-permute-start.6 = (f32[136,128]{1,0:T(8,128)S(1)}, f32[136,128]{1,0:T(8,128)S(1)}, u32[]{:S(2)}, u32[]{:S(2)}) collective-permute-start(f32[136,128]{1,0:T(8,128)S(1)} %get-tuple-element.52.refs_0_.refs_2_), channel_id=1, source_target_pairs={{0,1},{8,9},{16,17},{24,25},{1,0},{9,8},{17,16},{25,24},{2,3},{10,... | collective-permute-start | bytes 208904 | tf_op jit(solution)/shard_map/ppermute | solution.py:514
  13.3 9.6 %collective-permute-start.8 = (f32[256,128]{1,0:T(8,128)S(1)}, f32[256,128]{1,0:T(8,128)S(1)}, u32[]{:S(2)}, u32[]{:S(2)}) collective-permute-start(f32[256,128]{1,0:T(8,128)S(1)} %rest.1), channel_id=1, source_target_pairs={{0,16},{8,24},{16,0},{24,8},{1,17},{9,25},{17,1},{25,9},{2,18},{10... | collective-permute-start | bytes 393224 | tf_op jit(solution)/shard_map/ppermute | solution.py:514
  15.8 4.4 %collective-permute-start.5 = (f32[136,128]{1,0:T(8,128)S(1)}, f32[136,128]{1,0:T(8,128)S(1)}, u32[]{:S(2)}, u32[]{:S(2)}) collective-permute-start(f32[136,128]{1,0:T(8,128)S(1)} %merge21.1.refs_3_.refs_0_), channel_id=1, source_target_pairs={{0,2},{8,10},{16,18},{24,26},{1,3},{9,11},{17,19},{25,27},{2,0},{1... | collective-permute-start | bytes 208904 | tf_op jit(solution)/shard_map/ppermute | solution.py:514
  17.5 5.4 %collective-permute-start.7 = (f32[136,128]{1,0:T(8,128)S(1)}, f32[136,128]{1,0:T(8,128)S(1)}, u32[]{:S(2)}, u32[]{:S(2)}) collective-permute-start(f32[136,128]{1,0:T(8,128)S(1)} %get-tuple-element.55.refs_0_), channel_id=1, source_target_pairs={{0,2},{8,10},{16,18},{24,26},{1,3},{9,11},{17,19},{25,27},{2,0},{1... | collective-permute-start | bytes 208904 | tf_op jit(solution)/shard_map/ppermute | solution.py:514
  20.2 8.9 %collective-permute-start.12 = (f32[136,128]{1,0:T(8,128)S(1)}, f32[136,128]{1,0:T(8,128)S(1)}, u32[]{:S(2)}, u32[]{:S(2)}) collective-permute-start(f32[136,128]{1,0:T(8,128)S(1)} %merge31.1.refs_3_.refs_10_), channel_id=1, source_target_pairs={{0,4},{8,12},{16,20},{24,28},{1,5},{9,13},{17,21},{25,29},{2,6},{1... | collective-permute-start | bytes 208904 | tf_op jit(solution)/shard_map/ppermute | solution.py:514
  22.9 6.2 %collective-permute-start.11 = (f32[136,128]{1,0:T(8,128)S(1)}, f32[136,128]{1,0:T(8,128)S(1)}, u32[]{:S(2)}, u32[]{:S(2)}) collective-permute-start(f32[136,128]{1,0:T(8,128)S(1)} %get-tuple-element.56.refs_2_), channel_id=1, source_target_pairs={{0,4},{8,12},{16,20},{24,28},{1,5},{9,13},{17,21},{25,29},{2,6},{1... | collective-permute-start | bytes 208904 | tf_op jit(solution)/shard_map/ppermute | solution.py:514
  24.8 6.2 %collective-permute-start.9 = (f32[256,128]{1,0:T(8,128)S(1)}, f32[256,128]{1,0:T(8,128)S(1)}, u32[]{:S(2)}, u32[]{:S(2)}) collective-permute-start(f32[256,128]{1,0:T(8,128)S(1)} %found2.1.refs_1_), channel_id=1, source_target_pairs={{0,16},{8,24},{16,0},{24,8},{1,17},{9,25},{17,1},{25,9},{2,18},{10... | collective-permute-start | bytes 393224 | tf_op jit(solution)/shard_map/ppermute | solution.py:514
  25.6 6.6 %collective-permute-start.10 = (f32[256,128]{1,0:T(8,128)S(1)}, f32[256,128]{1,0:T(8,128)S(1)}, u32[]{:S(2)}, u32[]{:S(2)}) collective-permute-start(f32[256,128]{1,0:T(8,128)S(1)} %found3.1.refs_11_.refs_2_), channel_id=1, source_target_pairs={{0,16},{8,24},{16,0},{24,8},{1,17},{9,25},{17,1},{25,9},{2,18},{10... | collective-permute-start | bytes 393224 | tf_op jit(solution)/shard_map/ppermute | solution.py:514
  29.1 5.0 %collective-permute-start.14 = (f32[256,128]{1,0:T(8,128)S(1)}, f32[256,128]{1,0:T(8,128)S(1)}, u32[]{:S(2)}, u32[]{:S(2)}) collective-permute-start(f32[256,128]{1,0:T(8,128)S(1)} %state.1.refs_3_.refs_1_), channel_id=1, source_target_pairs={{0,16},{8,24},{16,0},{24,8},{1,17},{9,25},{17,1},{25,9},{2,18},{10... | collective-permute-start | bytes 393224 | tf_op jit(solution)/shard_map/ppermute | solution.py:514
  29.9 2.3 %collective-permute-start.15 = (f32[1024,128]{1,0:T(8,128)S(1)}, f32[1024,128]{1,0:T(8,128)S(1)}, u32[]{:S(2)}, u32[]{:S(2)}) collective-permute-start(f32[1024,128]{1,0:T(8,128)S(1)} %joined.1.refs_9_), channel_id=1, source_target_pairs={{0,8},{8,0},{16,24},{24,16},{1,9},{9,1},{17,25},{25,17},{2,10},{10... | collective-permute-start | bytes 1572872 | tf_op jit(solution)/shard_map/ppermute | solution.py:514
  32.2 4.0 %collective-permute-start.13 = (f32[768,128]{1,0:T(8,128)S(1)}, f32[768,128]{1,0:T(8,128)S(1)}, u32[]{:S(2)}, u32[]{:S(2)}) collective-permute-start(f32[768,128]{1,0:T(8,128)S(1)} %theirs.1.refs_9_), channel_id=1, source_target_pairs={{0,8},{8,0},{16,24},{24,16},{1,9},{9,1},{17,25},{25,17},{2,10},{10... | collective-permute-start | bytes 1179656 | tf_op jit(solution)/shard_map/ppermute | solution.py:514
  34.2 2.1 %collective-permute-start.16 = (f32[256,128]{1,0:T(8,128)S(1)}, f32[256,128]{1,0:T(8,128)S(1)}, u32[]{:S(2)}, u32[]{:S(2)}) collective-permute-start(f32[256,128]{1,0:T(8,128)S(1)} %beside.1.refs_10_), channel_id=1, source_target_pairs={{0,8},{8,0},{16,24},{24,16},{1,9},{9,1},{17,25},{25,17},{2,10},{10... | collective-permute-start | bytes 393224 | tf_op jit(solution)/shard_map/ppermute | solution.py:514

commit v26 on v24

--- a/solution.py
+++ b/solution.py
@@ -388,27 +388,14 @@
     return reach * weight_ref[first_level + bit, :, tokens] * active
 
 
-def gather_work(quarters, part_refs, heads, per):
-    work = []
-    for far, pieces in quarters:
-        first = first_head(far, heads)
-        for slot in range(heads // 4):
-            states = []
-            for level, index, start in pieces:
-                if start is None:
-                    rows = pl.ds(pl.multiple_of((first + slot) * per, 128), per)
-                else:
-                    rows = slice(start + slot * per, start + (slot + 1) * per)
-                states.append((level, part_refs[index][rows].astype(jnp.bfloat16)))
-            work.append((first + slot, states))
-    return work
-
-
-def add_found(mixed, queries, head, states, scale_ref):
-    for level, state in states:
-        found = lax.dot_general(state, queries, NT, preferred_element_type=jnp.float32)
-        mixed = mixed + found * scale_ref[level, pl.ds(head, 1)]
-    return mixed
+def gather_work(quarter, part_refs, heads, per):
+    far, pieces = quarter
+    rows = heads // 4 * per
+    states = [
+        (level, part_refs[index][start : start + rows].astype(jnp.bfloat16))
+        for level, index, start in pieces
+    ]
+    return first_head(far, heads), states
 
 
 def finish_kernel(quarters, first_level, bits, stays, carried, *refs):
@@ -435,10 +422,10 @@
         index, far = carried
         for start in range(0, q_ref.shape[0], SPAN):
             send(part_refs[index], far, slice(start, start + SPAN))
-    work = gather_work(quarters, part_refs, heads, head_width)
+    first, states = gather_work(quarters[0], part_refs, heads, head_width)
     gains = []
-    for head, _ in work:
-        row = jnp.broadcast_to(gain_ref[pl.ds(head, 1)], (8, head_width))
+    for slot in range(heads // 4):
+        row = jnp.broadcast_to(gain_ref[pl.ds(first + slot, 1)], (8, head_width))
         gains.append(row.T[:, :1])
     for span in range(q_ref.shape[0] // SPAN):
         tokens = slice(span * SPAN, (span + 1) * SPAN)
@@ -447,9 +434,16 @@
             scale_ref[level] = level_scale(
                 bit, first_level, prefix_ref, sums_ref, weight_ref, tokens
             )
-        for at, (head, states) in enumerate(work):
-            rows = pl.ds(pl.multiple_of(head * head_width, 128), head_width)
-            mixed = add_found(mixed_ref[rows, tokens], queries, head, states, scale_ref)
+        founds = [
+            (level, lax.dot_general(state, queries, NT, preferred_element_type=jnp.float32))
+            for level, state in states
+        ]
+        for at in range(heads // 4):
+            rows = pl.ds(pl.multiple_of((first + at) * head_width, 128), head_width)
+            mixed = mixed_ref[rows, tokens]
+            for level, found in founds:
+                part = found[at * head_width : (at + 1) * head_width]
+                mixed = mixed + part * scale_ref[level, pl.ds(first + at, 1)]
             square = jnp.mean(mixed * mixed, axis=0, keepdims=True)
             normed = mixed * lax.rsqrt(square + EPS) * gains[at]
             columns = slice(at * head_width, (at + 1) * head_width)

time: 37.2 us -> 37.2 us (level)
  no operation moved by 1% of the time
where the time goes in v26:
time: 37.2 us; the launch traced here: 36.8 us
  starting transfers between devices  19.6 us (53%)
  Pallas kernels  14 us (38%)
  waiting for transfers between devices  2.97 us (8%)
    ppermute x17, starting transfers between devices, trade(): return lax.ppermute(value, AXES, pairs)  19.6 us
    pallas_call x21, Pallas kernels, call(): pl.pallas_call(kernel, in_specs=specs, out_specs=[HELD] * len(outputs), o...  8.03 us
    pallas_call x4, Pallas kernels, finish(): pl.pallas_call(functools.partial(finish_kernel, quarters, first_level, bi...  5.98 us
    ppermute x17, waiting for transfers between devices, trade(): return lax.ppermute(value, AXES, pairs)  2.97 us
  transfers between devices with their start and end apart: 17, of which 7 were waited for; matrix products, arithmetic and copies ran while one was open for 0% of the time, Pallas kernels for 26%

profile of v26, /device:TPU:0, one launch (start us, length us, event | category | flops | bytes accessed | tf_op | source)
XLA Modules:
  0.0 36.8 jit_solution(10339005534502670669)
XLA Ops:
  0.0 2.6 %states.1 = (f32[520,128]{1,0:T(8,128)S(1)}, f32[520,128]{1,0:T(8,128)S(1)}, bf16[3,128,1024]{2,1,0:T(8,128)(2,1)S(1)}, f32[2,8,1024]{2,1,0:T(8,128)S(1)}, f32[4...) custom-call(bf16[1024,128]{1,0:T(8,128)(2,1)} %refs_0_.2, ...), custom_call_target="tpu_custom_call" | custom-call | flops 2000000000 | bytes 1000000 | tf_op jit(solution)/shard_map/states/pallas_call | solution.py:50
  2.6 0.5 %collective-permute-start = (f32[520,128]{1,0:T(8,128)S(1)}, f32[520,128]{1,0:T(8,128)S(1)}, u32[]{:S(2)}, u32[]{:S(2)}) collective-permute-start(f32[520,128]{1,0:T(8,128)S(1)} %get-tuple-element.35), channel_id=1, source_target_pairs={{0,8},{8,0},{16,24},{24,16},{1,9},{9,1},{17,25},{25,17},{2,10},{10... | collective-permute-start | bytes 798728 | tf_op jit(solution)/shard_map/ppermute | solution.py:508
  3.2 1.1 %collective-permute-done.other_ref.refs_7_ = f32[520,128]{1,0:T(8,128)S(1)} collective-permute-done((f32[520,128]{1,0:T(8,128)S(1)}, f32[520,128]{1,0:T(8,128)S(1)}, u32[]{:S(2)}, u32[]{:S(2)}) %collective-permute-start) | collective-permute-done | bytes 266272 | tf_op jit(solution)/shard_map/ppermute | solution.py:508
  4.4 3.0 %collective-permute-start.2 = (f32[136,128]{1,0:T(8,128)S(1)}, f32[136,128]{1,0:T(8,128)S(1)}, u32[]{:S(2)}, u32[]{:S(2)}) collective-permute-start(f32[136,128]{1,0:T(8,128)S(1)} %get-tuple-element.46), channel_id=1, source_target_pairs={{0,16},{8,24},{16,0},{24,8},{1,17},{9,25},{17,1},{25,9},{2,18},{10... | collective-permute-start | bytes 208904 | tf_op jit(solution)/shard_map/ppermute | solution.py:508
  7.5 1.1 %load.1 = (bf16[1024,128]{1,0:T(8,128)(2,1)S(1)}, f32[8,8,1024]{2,1,0:T(8,128)S(1)}, f32[8,128]{1,0:T(8,128)S(1)}) custom-call(bf16[1024,128]{1,0:T(8,128)(2,1)} %refs_0_.3, f32[8,8,1024]{2,1,0:T(8,128)} %refs_1_.3, f32[8,128]{1,0:T(8,128)} %bitcast.1, f32[136,128]{1,0:T(8,128)S(1)} %get-tuple-element.36.refs_3_.refs_0_), custom_call_target="tpu_custom_call" | custom-call | flops 2000000000 | bytes 1000000 | tf_op jit(solution)/shard_map/load/pallas_call | solution.py:50
  8.5 0.9 %local0.1 = (f32[1024,1024]{1,0:T(8,128)S(1)}, f32[8,128]{1,0:T(8,128)S(1)}) custom-call(bf16[1024,128]{1,0:T(8,128)(2,1)S(1)} %get-tuple-element.37.refs_0_.refs_1_, bf16[1024,128]{1,0:T(8,128)(2,1)S(1)} %get-tuple-element.38.refs_1_, bf16[1024,1024]{1,0:T(8,128)(2,1)S(1)} %get-tuple-element.39.refs_2_, ...), custom_call_target="tpu_custom_call" | custom-call | flops 1000 | bytes 1000000 | tf_op jit(solution)/shard_map/local0/pallas_call | solution.py:50
  9.4 0.5 %collective-permute-done.2.refs_1_ = f32[136,128]{1,0:T(8,128)S(1)} collective-permute-done((f32[136,128]{1,0:T(8,128)S(1)}, f32[136,128]{1,0:T(8,128)S(1)}, u32[]{:S(2)}, u32[]{:S(2)}) %collective-permute-start.2) | collective-permute-done | bytes 69664 | tf_op jit(solution)/shard_map/ppermute | solution.py:508
  9.9 2.2 %collective-permute-start.3 = (f32[136,128]{1,0:T(8,128)S(1)}, f32[136,128]{1,0:T(8,128)S(1)}, u32[]{:S(2)}, u32[]{:S(2)}) collective-permute-start(f32[136,128]{1,0:T(8,128)S(1)} %merge11.1.refs_10_.refs_3_.refs_0_), channel_id=1, source_target_pairs={{0,1},{8,9},{16,17},{24,25},{1,0},{9,8},{17,16},{25,24},{2,3},{10,... | collective-permute-start | bytes 208904 | tf_op jit(solution)/shard_map/ppermute | solution.py:508
  12.2 1.1 %collective-permute-start.6 = (f32[136,128]{1,0:T(8,128)S(1)}, f32[136,128]{1,0:T(8,128)S(1)}, u32[]{:S(2)}, u32[]{:S(2)}) collective-permute-start(f32[136,128]{1,0:T(8,128)S(1)} %get-tuple-element.52.refs_0_.refs_2_), channel_id=1, source_target_pairs={{0,1},{8,9},{16,17},{24,25},{1,0},{9,8},{17,16},{25,24},{2,3},{10,... | collective-permute-start | bytes 208904 | tf_op jit(solution)/shard_map/ppermute | solution.py:508
  13.3 1.5 %collective-permute-start.8 = (f32[256,128]{1,0:T(8,128)S(1)}, f32[256,128]{1,0:T(8,128)S(1)}, u32[]{:S(2)}, u32[]{:S(2)}) collective-permute-start(f32[256,128]{1,0:T(8,128)S(1)} %rest.1), channel_id=1, source_target_pairs={{0,16},{8,24},{16,0},{24,8},{1,17},{9,25},{17,1},{25,9},{2,18},{10... | collective-permute-start | bytes 393224 | tf_op jit(solution)/shard_map/ppermute | solution.py:508
  14.8 1.0 %local1.1 = (f32[1024,1024]{1,0:T(8,128)S(1)}, f32[8,128]{1,0:T(8,128)S(1)}) custom-call(bf16[1024,128]{1,0:T(8,128)(2,1)S(1)} %get-tuple-element.37.refs_0_.refs_1_, bf16[1024,128]{1,0:T(8,128)(2,1)S(1)} %get-tuple-element.38.refs_1_, bf16[1024,1024]{1,0:T(8,128)(2,1)S(1)} %get-tuple-element.39.refs_2_, ...), custom_call_target="tpu_custom_call", output_to_operand_aliasing={{0}: (9, {})} | custom-call | flops 2000000000 | bytes 1000000 | tf_op jit(solution)/shard_map/local1/pallas_call | solution.py:50
  15.8 1.6 %collective-permute-start.5 = (f32[136,128]{1,0:T(8,128)S(1)}, f32[136,128]{1,0:T(8,128)S(1)}, u32[]{:S(2)}, u32[]{:S(2)}) collective-permute-start(f32[136,128]{1,0:T(8,128)S(1)} %merge21.1.refs_3_.refs_0_), channel_id=1, source_target_pairs={{0,2},{8,10},{16,18},{24,26},{1,3},{9,11},{17,19},{25,27},{2,0},{1... | collective-permute-start | bytes 208904 | tf_op jit(solution)/shard_map/ppermute | solution.py:508
  17.5 0.8 %collective-permute-start.7 = (f32[136,128]{1,0:T(8,128)S(1)}, f32[136,128]{1,0:T(8,128)S(1)}, u32[]{:S(2)}, u32[]{:S(2)}) collective-permute-start(f32[136,128]{1,0:T(8,128)S(1)} %get-tuple-element.55.refs_0_.refs_2_), channel_id=1, source_target_pairs={{0,2},{8,10},{16,18},{24,26},{1,3},{9,11},{17,19},{25,27},{2,0},{1... | collective-permute-start | bytes 208904 | tf_op jit(solution)/shard_map/ppermute | solution.py:508
  18.3 1.8 %collective-permute-start.9 = (f32[256,128]{1,0:T(8,128)S(1)}, f32[256,128]{1,0:T(8,128)S(1)}, u32[]{:S(2)}, u32[]{:S(2)}) collective-permute-start(f32[256,128]{1,0:T(8,128)S(1)} %found2.1.refs_1_), channel_id=1, source_target_pairs={{0,16},{8,24},{16,0},{24,8},{1,17},{9,25},{17,1},{25,9},{2,18},{10... | collective-permute-start | bytes 393224 | tf_op jit(solution)/shard_map/ppermute | solution.py:508
  20.3 2.7 %collective-permute-start.12 = (f32[136,128]{1,0:T(8,128)S(1)}, f32[136,128]{1,0:T(8,128)S(1)}, u32[]{:S(2)}, u32[]{:S(2)}) collective-permute-start(f32[136,128]{1,0:T(8,128)S(1)} %merge31.1.refs_3_.refs_10_), channel_id=1, source_target_pairs={{0,4},{8,12},{16,20},{24,28},{1,5},{9,13},{17,21},{25,29},{2,6},{1... | collective-permute-start | bytes 208904 | tf_op jit(solution)/shard_map/ppermute | solution.py:508
  23.0 1.9 %collective-permute-start.11 = (f32[136,128]{1,0:T(8,128)S(1)}, f32[136,128]{1,0:T(8,128)S(1)}, u32[]{:S(2)}, u32[]{:S(2)}) collective-permute-start(f32[136,128]{1,0:T(8,128)S(1)} %get-tuple-element.56.refs_2_), channel_id=1, source_target_pairs={{0,4},{8,12},{16,20},{24,28},{1,5},{9,13},{17,21},{25,29},{2,6},{1... | collective-permute-start | bytes 208904 | tf_op jit(solution)/shard_map/ppermute | solution.py:508
  24.9 0.7 %collective-permute-start.10 = (f32[256,128]{1,0:T(8,128)S(1)}, f32[256,128]{1,0:T(8,128)S(1)}, u32[]{:S(2)}, u32[]{:S(2)}) collective-permute-start(f32[256,128]{1,0:T(8,128)S(1)} %found3.1.refs_11_.refs_2_), channel_id=1, source_target_pairs={{0,16},{8,24},{16,0},{24,8},{1,17},{9,25},{17,1},{25,9},{2,18},{10... | collective-permute-start | bytes 393224 | tf_op jit(solution)/shard_map/ppermute | solution.py:508
  25.6 2.1 %local2.1 = (f32[1024,1024]{1,0:T(8,128)S(1)}, f32[8,128]{1,0:T(8,128)S(1)}) custom-call(bf16[1024,128]{1,0:T(8,128)(2,1)S(1)} %get-tuple-element.37.refs_0_.refs_1_, bf16[1024,128]{1,0:T(8,128)(2,1)S(1)} %get-tuple-element.38.refs_1_, bf16[1024,1024]{1,0:T(8,128)(2,1)S(1)} %get-tuple-element.39.refs_2_, ...), custom_call_target="tpu_custom_call", output_to_operand_aliasing={{0}: (9, {})} | custom-call | flops 1000 | bytes 1000000 | tf_op jit(solution)/shard_map/local2/pallas_call | solution.py:50
  27.7 0.5 %collective-permute-done.11.refs_0_ = f32[136,128]{1,0:T(8,128)S(1)} collective-permute-done((f32[136,128]{1,0:T(8,128)S(1)}, f32[136,128]{1,0:T(8,128)S(1)}, u32[]{:S(2)}, u32[]{:S(2)}) %collective-permute-start.11) | collective-permute-done | bytes 69664 | tf_op jit(solution)/shard_map/ppermute | solution.py:508
  28.2 1.1 %collective-permute-start.14 = (f32[256,128]{1,0:T(8,128)S(1)}, f32[256,128]{1,0:T(8,128)S(1)}, u32[]{:S(2)}, u32[]{:S(2)}) collective-permute-start(f32[256,128]{1,0:T(8,128)S(1)} %state.1.refs_3_.refs_1_), channel_id=1, source_target_pairs={{0,16},{8,24},{16,0},{24,8},{1,17},{9,25},{17,1},{25,9},{2,18},{10... | collective-permute-start | bytes 393224 | tf_op jit(solution)/shard_map/ppermute | solution.py:508
  29.5 1.0 %finish00.1.refs_10_ = bf16[1024,256]{1,0:T(8,128)(2,1)S(1)} custom-call(f32[1024,1024]{1,0:T(8,128)S(1)} %get-tuple-element.57.refs_0_, bf16[1024,128]{1,0:T(8,128)(2,1)S(1)} %get-tuple-element.37.refs_0_.refs_1_, f32[2,8,1024]{2,1,0:T(8,128)S(1)} %get-tuple-element.40.refs_3_.refs_2_, f32[8,8,1024]{2,1,0:T(8,128)S(1)} %get-tuple-element.42.refs_5_.refs_3_, ...), custom_call_target="tpu_custom_call" | custom-call | flops 20000000000 | bytes 1000000 | tf_op jit(solution)/shard_map/finish00/pallas_call | solution.py:484
  31.4 1.6 %finish10.1 = (bf16[1024,1024]{1,0:T(8,128)(2,1)}, bf16[1024,256]{1,0:T(8,128)(2,1)S(1)}) custom-call(f32[1024,1024]{1,0:T(8,128)S(1)} %get-tuple-element.57.refs_0_, bf16[1024,128]{1,0:T(8,128)(2,1)S(1)} %get-tuple-element.37.refs_0_.refs_1_, f32[2,8,1024]{2,1,0:T(8,128)S(1)} %get-tuple-element.40.refs_3_.refs_2_, ...), custom_call_target="tpu_custom_call" | custom-call | flops 1000 | bytes 1000000 | tf_op jit(solution)/shard_map/finish10/pallas_call | solution.py:484
  33.4 1.8 %finish01.1.refs_11_ = bf16[1024,1024]{1,0:T(8,128)(2,1)} custom-call(f32[1024,1024]{1,0:T(8,128)S(1)} %get-tuple-element.57.refs_0_, bf16[1024,128]{1,0:T(8,128)(2,1)S(1)} %get-tuple-element.37.refs_0_.refs_1_, f32[2,8,1024]{2,1,0:T(8,128)S(1)} %get-tuple-element.40.refs_3_.refs_2_, ...), custom_call_target="tpu_custom_call", output_to_operand_aliasing={{}: (12, {})} | custom-call | flops 20000000000 | bytes 1000000 | tf_op jit(solution)/shard_map/finish01/pallas_call | solution.py:484
  35.2 1.6 %finish11.1 = bf16[1024,1024]{1,0:T(8,128)(2,1)} custom-call(f32[1024,1024]{1,0:T(8,128)S(1)} %get-tuple-element.57.refs_0_, bf16[1024,128]{1,0:T(8,128)(2,1)S(1)} %get-tuple-element.37.refs_0_.refs_1_, f32[2,8,1024]{2,1,0:T(8,128)S(1)} %get-tuple-element.40.refs_3_.refs_2_, ...), custom_call_target="tpu_custom_call", output_to_operand_aliasing={{}: (11, {})} | custom-call | flops 2000000000 | bytes 1000000 | tf_op jit(solution)/shard_map/finish11/pallas_call | solution.py:484
  (35 shorter events, 2.0 us)
Async XLA Ops:
  2.6 1.7 %collective-permute-start = (f32[520,128]{1,0:T(8,128)S(1)}, f32[520,128]{1,0:T(8,128)S(1)}, u32[]{:S(2)}, u32[]{:S(2)}) collective-permute-start(f32[520,128]{1,0:T(8,128)S(1)} %get-tuple-element.35), channel_id=1, source_target_pairs={{0,8},{8,0},{16,24},{24,16},{1,9},{9,1},{17,25},{25,17},{2,10},{10... | collective-permute-start | bytes 798728 | tf_op jit(solution)/shard_map/ppermute | solution.py:508
  3.1 5.4 %collective-permute-start.1 = (f32[520,128]{1,0:T(8,128)S(1)}, f32[520,128]{1,0:T(8,128)S(1)}, u32[]{:S(2)}, u32[]{:S(2)}) collective-permute-start(f32[520,128]{1,0:T(8,128)S(1)} %get-tuple-element.34.mine_ref), channel_id=1, source_target_pairs={{0,8},{8,0},{16,24},{24,16},{1,9},{9,1},{17,25},{25,17},{2,10},{10... | collective-permute-start | bytes 798728 | tf_op jit(solution)/shard_map/ppermute | solution.py:508
  4.4 5.5 %collective-permute-start.2 = (f32[136,128]{1,0:T(8,128)S(1)}, f32[136,128]{1,0:T(8,128)S(1)}, u32[]{:S(2)}, u32[]{:S(2)}) collective-permute-start(f32[136,128]{1,0:T(8,128)S(1)} %get-tuple-element.46), channel_id=1, source_target_pairs={{0,16},{8,24},{16,0},{24,8},{1,17},{9,25},{17,1},{25,9},{2,18},{10... | collective-permute-start | bytes 208904 | tf_op jit(solution)/shard_map/ppermute | solution.py:508
  7.4 4.8 %collective-permute-start.4 = (f32[136,128]{1,0:T(8,128)S(1)}, f32[136,128]{1,0:T(8,128)S(1)}, u32[]{:S(2)}, u32[]{:S(2)}) collective-permute-start(f32[136,128]{1,0:T(8,128)S(1)} %get-tuple-element.49), channel_id=1, source_target_pairs={{0,16},{8,24},{16,0},{24,8},{1,17},{9,25},{17,1},{25,9},{2,18},{10... | collective-permute-start | bytes 208904 | tf_op jit(solution)/shard_map/ppermute | solution.py:508
  9.9 5.9 %collective-permute-start.3 = (f32[136,128]{1,0:T(8,128)S(1)}, f32[136,128]{1,0:T(8,128)S(1)}, u32[]{:S(2)}, u32[]{:S(2)}) collective-permute-start(f32[136,128]{1,0:T(8,128)S(1)} %merge11.1.refs_10_.refs_3_.refs_0_), channel_id=1, source_target_pairs={{0,1},{8,9},{16,17},{24,25},{1,0},{9,8},{17,16},{25,24},{2,3},{10,... | collective-permute-start | bytes 208904 | tf_op jit(solution)/shard_map/ppermute | solution.py:508
  12.2 5.3 %collective-permute-start.6 = (f32[136,128]{1,0:T(8,128)S(1)}, f32[136,128]{1,0:T(8,128)S(1)}, u32[]{:S(2)}, u32[]{:S(2)}) collective-permute-start(f32[136,128]{1,0:T(8,128)S(1)} %get-tuple-element.52.refs_0_.refs_2_), channel_id=1, source_target_pairs={{0,1},{8,9},{16,17},{24,25},{1,0},{9,8},{17,16},{25,24},{2,3},{10,... | collective-permute-start | bytes 208904 | tf_op jit(solution)/shard_map/ppermute | solution.py:508
  13.3 9.6 %collective-permute-start.8 = (f32[256,128]{1,0:T(8,128)S(1)}, f32[256,128]{1,0:T(8,128)S(1)}, u32[]{:S(2)}, u32[]{:S(2)}) collective-permute-start(f32[256,128]{1,0:T(8,128)S(1)} %rest.1), channel_id=1, source_target_pairs={{0,16},{8,24},{16,0},{24,8},{1,17},{9,25},{17,1},{25,9},{2,18},{10... | collective-permute-start | bytes 393224 | tf_op jit(solution)/shard_map/ppermute | solution.py:508
  15.8 4.4 %collective-permute-start.5 = (f32[136,128]{1,0:T(8,128)S(1)}, f32[136,128]{1,0:T(8,128)S(1)}, u32[]{:S(2)}, u32[]{:S(2)}) collective-permute-start(f32[136,128]{1,0:T(8,128)S(1)} %merge21.1.refs_3_.refs_0_), channel_id=1, source_target_pairs={{0,2},{8,10},{16,18},{24,26},{1,3},{9,11},{17,19},{25,27},{2,0},{1... | collective-permute-start | bytes 208904 | tf_op jit(solution)/shard_map/ppermute | solution.py:508
  17.5 5.4 %collective-permute-start.7 = (f32[136,128]{1,0:T(8,128)S(1)}, f32[136,128]{1,0:T(8,128)S(1)}, u32[]{:S(2)}, u32[]{:S(2)}) collective-permute-start(f32[136,128]{1,0:T(8,128)S(1)} %get-tuple-element.55.refs_0_.refs_2_), channel_id=1, source_target_pairs={{0,2},{8,10},{16,18},{24,26},{1,3},{9,11},{17,19},{25,27},{2,0},{1... | collective-permute-start | bytes 208904 | tf_op jit(solution)/shard_map/ppermute | solution.py:508
  18.3 12.2 %collective-permute-start.9 = (f32[256,128]{1,0:T(8,128)S(1)}, f32[256,128]{1,0:T(8,128)S(1)}, u32[]{:S(2)}, u32[]{:S(2)}) collective-permute-start(f32[256,128]{1,0:T(8,128)S(1)} %found2.1.refs_1_), channel_id=1, source_target_pairs={{0,16},{8,24},{16,0},{24,8},{1,17},{9,25},{17,1},{25,9},{2,18},{10... | collective-permute-start | bytes 393224 | tf_op jit(solution)/shard_map/ppermute | solution.py:508
  20.3 8.0 %collective-permute-start.12 = (f32[136,128]{1,0:T(8,128)S(1)}, f32[136,128]{1,0:T(8,128)S(1)}, u32[]{:S(2)}, u32[]{:S(2)}) collective-permute-start(f32[136,128]{1,0:T(8,128)S(1)} %merge31.1.refs_3_.refs_10_), channel_id=1, source_target_pairs={{0,4},{8,12},{16,20},{24,28},{1,5},{9,13},{17,21},{25,29},{2,6},{1... | collective-permute-start | bytes 208904 | tf_op jit(solution)/shard_map/ppermute | solution.py:508
  23.0 5.3 %collective-permute-start.11 = (f32[136,128]{1,0:T(8,128)S(1)}, f32[136,128]{1,0:T(8,128)S(1)}, u32[]{:S(2)}, u32[]{:S(2)}) collective-permute-start(f32[136,128]{1,0:T(8,128)S(1)} %get-tuple-element.56.refs_2_), channel_id=1, source_target_pairs={{0,4},{8,12},{16,20},{24,28},{1,5},{9,13},{17,21},{25,29},{2,6},{1... | collective-permute-start | bytes 208904 | tf_op jit(solution)/shard_map/ppermute | solution.py:508
  24.9 5.8 %collective-permute-start.10 = (f32[256,128]{1,0:T(8,128)S(1)}, f32[256,128]{1,0:T(8,128)S(1)}, u32[]{:S(2)}, u32[]{:S(2)}) collective-permute-start(f32[256,128]{1,0:T(8,128)S(1)} %found3.1.refs_11_.refs_2_), channel_id=1, source_target_pairs={{0,16},{8,24},{16,0},{24,8},{1,17},{9,25},{17,1},{25,9},{2,18},{10... | collective-permute-start | bytes 393224 | tf_op jit(solution)/shard_map/ppermute | solution.py:508
  28.2 5.0 %collective-permute-start.14 = (f32[256,128]{1,0:T(8,128)S(1)}, f32[256,128]{1,0:T(8,128)S(1)}, u32[]{:S(2)}, u32[]{:S(2)}) collective-permute-start(f32[256,128]{1,0:T(8,128)S(1)} %state.1.refs_3_.refs_1_), channel_id=1, source_target_pairs={{0,16},{8,24},{16,0},{24,8},{1,17},{9,25},{17,1},{25,9},{2,18},{10... | collective-permute-start | bytes 393224 | tf_op jit(solution)/shard_map/ppermute | solution.py:508
  29.4 2.0 %collective-permute-start.15 = (f32[1024,128]{1,0:T(8,128)S(1)}, f32[1024,128]{1,0:T(8,128)S(1)}, u32[]{:S(2)}, u32[]{:S(2)}) collective-permute-start(f32[1024,128]{1,0:T(8,128)S(1)} %joined.1.refs_9_), channel_id=1, source_target_pairs={{0,8},{8,0},{16,24},{24,16},{1,9},{9,1},{17,25},{25,17},{2,10},{10... | collective-permute-start | bytes 1572872 | tf_op jit(solution)/shard_map/ppermute | solution.py:508
  30.6 4.5 %collective-permute-start.13 = (f32[768,128]{1,0:T(8,128)S(1)}, f32[768,128]{1,0:T(8,128)S(1)}, u32[]{:S(2)}, u32[]{:S(2)}) collective-permute-start(f32[768,128]{1,0:T(8,128)S(1)} %theirs.1.refs_9_), channel_id=1, source_target_pairs={{0,8},{8,0},{16,24},{24,16},{1,9},{9,1},{17,25},{25,17},{2,10},{10... | collective-permute-start | bytes 1179656 | tf_op jit(solution)/shard_map/ppermute | solution.py:508
  33.3 1.9 %collective-permute-start.16 = (f32[256,128]{1,0:T(8,128)S(1)}, f32[256,128]{1,0:T(8,128)S(1)}, u32[]{:S(2)}, u32[]{:S(2)}) collective-permute-start(f32[256,128]{1,0:T(8,128)S(1)} %beside.1.refs_10_), channel_id=1, source_target_pairs={{0,8},{8,0},{16,24},{24,16},{1,9},{9,1},{17,25},{25,17},{2,10},{10... | collective-permute-start | bytes 393224 | tf_op jit(solution)/shard_map/ppermute | solution.py:508

commit v27 on v24

--- a/solution.py
+++ b/solution.py
@@ -290,7 +290,7 @@
     return first
 
 
-def chip_kernel(mine_ref, other_ref, *refs):
+def chip_kernel(mine_ref, other_ref, token_ref, *refs):
     *message_refs, next_ref, whole_ref = refs
     heads = next_ref.shape[0]
     width = whole_ref.shape[0]
@@ -318,13 +318,13 @@
         ref[size:] = total
 
 
-def make_chip(mine, other, heads, cuts):
+def make_chip(mine, other, token, heads, cuts):
     rows, lanes = mine.shape
     half = rows - heads
     *messages, prefix = call(
         chip_kernel,
         "chip",
-        [mine, other],
+        [mine, other, token],
         [
             *[((half // 2 // cuts + heads, lanes), jnp.float32)] * (2 * cuts),
             ((heads, lanes), jnp.float32),
@@ -529,8 +529,8 @@
     size = two // CUTS
     sides = [(core, side) for core in (0, 1) for side in (0, 1)]
     other, other_rest = trade(send, 1), trade(keep, 1)
-    chunks, give, prefix = make_chip(keep, other, heads, CUTS)
-    queries, level_weight, gain = load([queries, level_weight, gain], chunks[0])
+    queries, level_weight, gain = load([queries, level_weight, gain], send)
+    chunks, give, prefix = make_chip(keep, other, gain, heads, CUTS)
     shared = (queries, keys, values, sums, totals, level_weight, local, other, other_rest)
     prefixes = [None, prefix]
     found, across = {}, {}

time: 37.2 us -> 37.2 us (level)
  transfers between devices with their start and end apart: 17 -> 17, of which waited for: 7 -> 6; matrix products, arithmetic and copies ran while one was open for 0% -> 0% of each run, Pallas kernels for 26% -> 26%
where the time goes in v27:
time: 37.2 us; the launch traced here: 36.8 us
  starting transfers between devices  19.4 us (52%)
  Pallas kernels  14 us (38%)
  waiting for transfers between devices  3.15 us (8%)
    ppermute x17, starting transfers between devices, trade(): return lax.ppermute(value, AXES, pairs)  19.4 us
    pallas_call x21, Pallas kernels, call(): pl.pallas_call(kernel, in_specs=specs, out_specs=[HELD] * len(outputs), o...  8.04 us
    pallas_call x4, Pallas kernels, finish(): pl.pallas_call(functools.partial(finish_kernel, quarters, first_level, bi...  5.97 us
    ppermute x17, waiting for transfers between devices, trade(): return lax.ppermute(value, AXES, pairs)  3.15 us
  transfers between devices with their start and end apart: 17, of which 6 were waited for; matrix products, arithmetic and copies ran while one was open for 0% of the time, Pallas kernels for 26%

profile of v27, /device:TPU:0, one launch (start us, length us, event | category | flops | bytes accessed | tf_op | source)
XLA Modules:
  0.0 36.8 jit_solution(14309036590318989356)
XLA Ops:
  0.0 2.6 %states.1 = (f32[520,128]{1,0:T(8,128)S(1)}, f32[520,128]{1,0:T(8,128)S(1)}, bf16[3,128,1024]{2,1,0:T(8,128)(2,1)S(1)}, f32[2,8,1024]{2,1,0:T(8,128)S(1)}, f32[4...) custom-call(bf16[1024,128]{1,0:T(8,128)(2,1)} %refs_0_.2, ...), custom_call_target="tpu_custom_call" | custom-call | flops 2000000000 | bytes 1000000 | tf_op jit(solution)/shard_map/states/pallas_call | solution.py:50
  2.6 0.5 %collective-permute-start = (f32[520,128]{1,0:T(8,128)S(1)}, f32[520,128]{1,0:T(8,128)S(1)}, u32[]{:S(2)}, u32[]{:S(2)}) collective-permute-start(f32[520,128]{1,0:T(8,128)S(1)} %get-tuple-element.34.refs_3_), channel_id=1, source_target_pairs={{0,8},{8,0},{16,24},{24,16},{1,9},{9,1},{17,25},{25,17},{2,10},{10... | collective-permute-start | bytes 798728 | tf_op jit(solution)/shard_map/ppermute | solution.py:514
  3.2 1.1 %load.1 = (bf16[1024,128]{1,0:T(8,128)(2,1)S(1)}, f32[8,8,1024]{2,1,0:T(8,128)S(1)}, f32[8,128]{1,0:T(8,128)S(1)}) custom-call(bf16[1024,128]{1,0:T(8,128)(2,1)} %refs_0_.3, f32[8,8,1024]{2,1,0:T(8,128)} %refs_1_.3, f32[8,128]{1,0:T(8,128)} %bitcast.1, f32[520,128]{1,0:T(8,128)S(1)} %get-tuple-element.34.refs_3_), custom_call_target="tpu_custom_call" | custom-call | flops 2000000000 | bytes 1000000 | tf_op jit(solution)/shard_map/load/pallas_call | solution.py:50
  4.4 3.0 %collective-permute-start.2 = (f32[136,128]{1,0:T(8,128)S(1)}, f32[136,128]{1,0:T(8,128)S(1)}, u32[]{:S(2)}, u32[]{:S(2)}) collective-permute-start(f32[136,128]{1,0:T(8,128)S(1)} %get-tuple-element.46), channel_id=1, source_target_pairs={{0,16},{8,24},{16,0},{24,8},{1,17},{9,25},{17,1},{25,9},{2,18},{10... | collective-permute-start | bytes 208904 | tf_op jit(solution)/shard_map/ppermute | solution.py:514
  7.5 0.9 %local0.1 = (f32[1024,1024]{1,0:T(8,128)S(1)}, f32[8,128]{1,0:T(8,128)S(1)}) custom-call(bf16[1024,128]{1,0:T(8,128)(2,1)S(1)} %get-tuple-element.35.refs_0_.refs_1_, bf16[1024,128]{1,0:T(8,128)(2,1)S(1)} %get-tuple-element.36.refs_1_, bf16[1024,1024]{1,0:T(8,128)(2,1)S(1)} %get-tuple-element.37.refs_2_, ...), custom_call_target="tpu_custom_call" | custom-call | flops 1000 | bytes 1000000 | tf_op jit(solution)/shard_map/local0/pallas_call | solution.py:50
  8.4 1.5 %collective-permute-done.2.refs_1_ = f32[136,128]{1,0:T(8,128)S(1)} collective-permute-done((f32[136,128]{1,0:T(8,128)S(1)}, f32[136,128]{1,0:T(8,128)S(1)}, u32[]{:S(2)}, u32[]{:S(2)}) %collective-permute-start.2) | collective-permute-done | bytes 69664 | tf_op jit(solution)/shard_map/ppermute | solution.py:514
  9.9 2.3 %collective-permute-start.3 = (f32[136,128]{1,0:T(8,128)S(1)}, f32[136,128]{1,0:T(8,128)S(1)}, u32[]{:S(2)}, u32[]{:S(2)}) collective-permute-start(f32[136,128]{1,0:T(8,128)S(1)} %merge11.1.refs_10_.refs_3_.refs_0_), channel_id=1, source_target_pairs={{0,1},{8,9},{16,17},{24,25},{1,0},{9,8},{17,16},{25,24},{2,3},{10,... | collective-permute-start | bytes 208904 | tf_op jit(solution)/shard_map/ppermute | solution.py:514
  12.3 1.0 %collective-permute-start.6 = (f32[136,128]{1,0:T(8,128)S(1)}, f32[136,128]{1,0:T(8,128)S(1)}, u32[]{:S(2)}, u32[]{:S(2)}) collective-permute-start(f32[136,128]{1,0:T(8,128)S(1)} %get-tuple-element.53.refs_0_.refs_2_), channel_id=1, source_target_pairs={{0,1},{8,9},{16,17},{24,25},{1,0},{9,8},{17,16},{25,24},{2,3},{10,... | collective-permute-start | bytes 208904 | tf_op jit(solution)/shard_map/ppermute | solution.py:514
  13.3 1.4 %collective-permute-start.8 = (f32[256,128]{1,0:T(8,128)S(1)}, f32[256,128]{1,0:T(8,128)S(1)}, u32[]{:S(2)}, u32[]{:S(2)}) collective-permute-start(f32[256,128]{1,0:T(8,128)S(1)} %rest.1), channel_id=1, source_target_pairs={{0,16},{8,24},{16,0},{24,8},{1,17},{9,25},{17,1},{25,9},{2,18},{10... | collective-permute-start | bytes 393224 | tf_op jit(solution)/shard_map/ppermute | solution.py:514
  14.8 1.0 %local1.1 = (f32[1024,1024]{1,0:T(8,128)S(1)}, f32[8,128]{1,0:T(8,128)S(1)}) custom-call(bf16[1024,128]{1,0:T(8,128)(2,1)S(1)} %get-tuple-element.35.refs_0_.refs_1_, bf16[1024,128]{1,0:T(8,128)(2,1)S(1)} %get-tuple-element.36.refs_1_, bf16[1024,1024]{1,0:T(8,128)(2,1)S(1)} %get-tuple-element.37.refs_2_, ...), custom_call_target="tpu_custom_call", output_to_operand_aliasing={{0}: (9, {})} | custom-call | flops 2000000000 | bytes 1000000 | tf_op jit(solution)/shard_map/local1/pallas_call | solution.py:50
  15.9 1.6 %collective-permute-start.5 = (f32[136,128]{1,0:T(8,128)S(1)}, f32[136,128]{1,0:T(8,128)S(1)}, u32[]{:S(2)}, u32[]{:S(2)}) collective-permute-start(f32[136,128]{1,0:T(8,128)S(1)} %merge21.1.refs_3_.refs_0_), channel_id=1, source_target_pairs={{0,2},{8,10},{16,18},{24,26},{1,3},{9,11},{17,19},{25,27},{2,0},{1... | collective-permute-start | bytes 208904 | tf_op jit(solution)/shard_map/ppermute | solution.py:514
  17.5 0.8 %collective-permute-start.7 = (f32[136,128]{1,0:T(8,128)S(1)}, f32[136,128]{1,0:T(8,128)S(1)}, u32[]{:S(2)}, u32[]{:S(2)}) collective-permute-start(f32[136,128]{1,0:T(8,128)S(1)} %get-tuple-element.56.refs_0_.refs_2_), channel_id=1, source_target_pairs={{0,2},{8,10},{16,18},{24,26},{1,3},{9,11},{17,19},{25,27},{2,0},{1... | collective-permute-start | bytes 208904 | tf_op jit(solution)/shard_map/ppermute | solution.py:514
  18.4 1.7 %collective-permute-start.9 = (f32[256,128]{1,0:T(8,128)S(1)}, f32[256,128]{1,0:T(8,128)S(1)}, u32[]{:S(2)}, u32[]{:S(2)}) collective-permute-start(f32[256,128]{1,0:T(8,128)S(1)} %found2.1.refs_1_), channel_id=1, source_target_pairs={{0,16},{8,24},{16,0},{24,8},{1,17},{9,25},{17,1},{25,9},{2,18},{10... | collective-permute-start | bytes 393224 | tf_op jit(solution)/shard_map/ppermute | solution.py:514
  20.3 2.7 %collective-permute-start.12 = (f32[136,128]{1,0:T(8,128)S(1)}, f32[136,128]{1,0:T(8,128)S(1)}, u32[]{:S(2)}, u32[]{:S(2)}) collective-permute-start(f32[136,128]{1,0:T(8,128)S(1)} %merge31.1.refs_3_.refs_10_), channel_id=1, source_target_pairs={{0,4},{8,12},{16,20},{24,28},{1,5},{9,13},{17,21},{25,29},{2,6},{1... | collective-permute-start | bytes 208904 | tf_op jit(solution)/shard_map/ppermute | solution.py:514
  23.0 1.8 %collective-permute-start.11 = (f32[136,128]{1,0:T(8,128)S(1)}, f32[136,128]{1,0:T(8,128)S(1)}, u32[]{:S(2)}, u32[]{:S(2)}) collective-permute-start(f32[136,128]{1,0:T(8,128)S(1)} %get-tuple-element.57.refs_2_), channel_id=1, source_target_pairs={{0,4},{8,12},{16,20},{24,28},{1,5},{9,13},{17,21},{25,29},{2,6},{1... | collective-permute-start | bytes 208904 | tf_op jit(solution)/shard_map/ppermute | solution.py:514
  24.8 0.8 %collective-permute-start.10 = (f32[256,128]{1,0:T(8,128)S(1)}, f32[256,128]{1,0:T(8,128)S(1)}, u32[]{:S(2)}, u32[]{:S(2)}) collective-permute-start(f32[256,128]{1,0:T(8,128)S(1)} %found3.1.refs_11_.refs_2_), channel_id=1, source_target_pairs={{0,16},{8,24},{16,0},{24,8},{1,17},{9,25},{17,1},{25,9},{2,18},{10... | collective-permute-start | bytes 393224 | tf_op jit(solution)/shard_map/ppermute | solution.py:514
  25.6 2.1 %local2.1 = (f32[1024,1024]{1,0:T(8,128)S(1)}, f32[8,128]{1,0:T(8,128)S(1)}) custom-call(bf16[1024,128]{1,0:T(8,128)(2,1)S(1)} %get-tuple-element.35.refs_0_.refs_1_, bf16[1024,128]{1,0:T(8,128)(2,1)S(1)} %get-tuple-element.36.refs_1_, bf16[1024,1024]{1,0:T(8,128)(2,1)S(1)} %get-tuple-element.37.refs_2_, ...), custom_call_target="tpu_custom_call", output_to_operand_aliasing={{0}: (9, {})} | custom-call | flops 1000 | bytes 1000000 | tf_op jit(solution)/shard_map/local2/pallas_call | solution.py:50
  27.7 0.5 %collective-permute-done.11.refs_0_ = f32[136,128]{1,0:T(8,128)S(1)} collective-permute-done((f32[136,128]{1,0:T(8,128)S(1)}, f32[136,128]{1,0:T(8,128)S(1)}, u32[]{:S(2)}, u32[]{:S(2)}) %collective-permute-start.11) | collective-permute-done | bytes 69664 | tf_op jit(solution)/shard_map/ppermute | solution.py:514
  28.3 1.0 %collective-permute-start.14 = (f32[256,128]{1,0:T(8,128)S(1)}, f32[256,128]{1,0:T(8,128)S(1)}, u32[]{:S(2)}, u32[]{:S(2)}) collective-permute-start(f32[256,128]{1,0:T(8,128)S(1)} %state.1.refs_3_.refs_1_), channel_id=1, source_target_pairs={{0,16},{8,24},{16,0},{24,8},{1,17},{9,25},{17,1},{25,9},{2,18},{10... | collective-permute-start | bytes 393224 | tf_op jit(solution)/shard_map/ppermute | solution.py:514
  29.3 1.0 %finish00.1.refs_10_ = bf16[1024,256]{1,0:T(8,128)(2,1)S(1)} custom-call(f32[1024,1024]{1,0:T(8,128)S(1)} %get-tuple-element.58.refs_0_, bf16[1024,128]{1,0:T(8,128)(2,1)S(1)} %get-tuple-element.35.refs_0_.refs_1_, f32[2,8,1024]{2,1,0:T(8,128)S(1)} %get-tuple-element.38.refs_3_.refs_2_, f32[8,8,1024]{2,1,0:T(8,128)S(1)} %get-tuple-element.40.refs_5_.refs_3_, ...), custom_call_target="tpu_custom_call" | custom-call | flops 20000000000 | bytes 1000000 | tf_op jit(solution)/shard_map/finish00/pallas_call | solution.py:490
  30.5 0.4 %collective-permute-start.13 = (f32[768,128]{1,0:T(8,128)S(1)}, f32[768,128]{1,0:T(8,128)S(1)}, u32[]{:S(2)}, u32[]{:S(2)}) collective-permute-start(f32[768,128]{1,0:T(8,128)S(1)} %theirs.1.refs_9_), channel_id=1, source_target_pairs={{0,8},{8,0},{16,24},{24,16},{1,9},{9,1},{17,25},{25,17},{2,10},{10... | collective-permute-start | bytes 1179656 | tf_op jit(solution)/shard_map/ppermute | solution.py:514
  31.2 1.6 %finish10.1 = (bf16[1024,1024]{1,0:T(8,128)(2,1)}, bf16[1024,256]{1,0:T(8,128)(2,1)S(1)}) custom-call(f32[1024,1024]{1,0:T(8,128)S(1)} %get-tuple-element.58.refs_0_, bf16[1024,128]{1,0:T(8,128)(2,1)S(1)} %get-tuple-element.35.refs_0_.refs_1_, f32[2,8,1024]{2,1,0:T(8,128)S(1)} %get-tuple-element.38.refs_3_.refs_2_, ...), custom_call_target="tpu_custom_call" | custom-call | flops 1000 | bytes 1000000 | tf_op jit(solution)/shard_map/finish10/pallas_call | solution.py:490
  33.4 1.7 %finish01.1.refs_11_ = bf16[1024,1024]{1,0:T(8,128)(2,1)} custom-call(f32[1024,1024]{1,0:T(8,128)S(1)} %get-tuple-element.58.refs_0_, bf16[1024,128]{1,0:T(8,128)(2,1)S(1)} %get-tuple-element.35.refs_0_.refs_1_, f32[2,8,1024]{2,1,0:T(8,128)S(1)} %get-tuple-element.38.refs_3_.refs_2_, ...), custom_call_target="tpu_custom_call", output_to_operand_aliasing={{}: (12, {})} | custom-call | flops 20000000000 | bytes 1000000 | tf_op jit(solution)/shard_map/finish01/pallas_call | solution.py:490
  35.2 1.6 %finish11.1 = bf16[1024,1024]{1,0:T(8,128)(2,1)} custom-call(f32[1024,1024]{1,0:T(8,128)S(1)} %get-tuple-element.58.refs_0_, bf16[1024,128]{1,0:T(8,128)(2,1)S(1)} %get-tuple-element.35.refs_0_.refs_1_, f32[2,8,1024]{2,1,0:T(8,128)S(1)} %get-tuple-element.38.refs_3_.refs_2_, ...), custom_call_target="tpu_custom_call", output_to_operand_aliasing={{}: (11, {})} | custom-call | flops 2000000000 | bytes 1000000 | tf_op jit(solution)/shard_map/finish11/pallas_call | solution.py:490
  (35 shorter events, 1.8 us)
Async XLA Ops:
  2.6 1.7 %collective-permute-start = (f32[520,128]{1,0:T(8,128)S(1)}, f32[520,128]{1,0:T(8,128)S(1)}, u32[]{:S(2)}, u32[]{:S(2)}) collective-permute-start(f32[520,128]{1,0:T(8,128)S(1)} %get-tuple-element.34.refs_3_), channel_id=1, source_target_pairs={{0,8},{8,0},{16,24},{24,16},{1,9},{9,1},{17,25},{25,17},{2,10},{10... | collective-permute-start | bytes 798728 | tf_op jit(solution)/shard_map/ppermute | solution.py:514
  3.1 4.4 %collective-permute-start.1 = (f32[520,128]{1,0:T(8,128)S(1)}, f32[520,128]{1,0:T(8,128)S(1)}, u32[]{:S(2)}, u32[]{:S(2)}) collective-permute-start(f32[520,128]{1,0:T(8,128)S(1)} %get-tuple-element.42.mine_ref), channel_id=1, source_target_pairs={{0,8},{8,0},{16,24},{24,16},{1,9},{9,1},{17,25},{25,17},{2,10},{10... | collective-permute-start | bytes 798728 | tf_op jit(solution)/shard_map/ppermute | solution.py:514
  4.4 5.5 %collective-permute-start.2 = (f32[136,128]{1,0:T(8,128)S(1)}, f32[136,128]{1,0:T(8,128)S(1)}, u32[]{:S(2)}, u32[]{:S(2)}) collective-permute-start(f32[136,128]{1,0:T(8,128)S(1)} %get-tuple-element.46), channel_id=1, source_target_pairs={{0,16},{8,24},{16,0},{24,8},{1,17},{9,25},{17,1},{25,9},{2,18},{10... | collective-permute-start | bytes 208904 | tf_op jit(solution)/shard_map/ppermute | solution.py:514
  7.4 4.8 %collective-permute-start.4 = (f32[136,128]{1,0:T(8,128)S(1)}, f32[136,128]{1,0:T(8,128)S(1)}, u32[]{:S(2)}, u32[]{:S(2)}) collective-permute-start(f32[136,128]{1,0:T(8,128)S(1)} %get-tuple-element.50), channel_id=1, source_target_pairs={{0,16},{8,24},{16,0},{24,8},{1,17},{9,25},{17,1},{25,9},{2,18},{10... | collective-permute-start | bytes 208904 | tf_op jit(solution)/shard_map/ppermute | solution.py:514
  9.9 5.9 %collective-permute-start.3 = (f32[136,128]{1,0:T(8,128)S(1)}, f32[136,128]{1,0:T(8,128)S(1)}, u32[]{:S(2)}, u32[]{:S(2)}) collective-permute-start(f32[136,128]{1,0:T(8,128)S(1)} %merge11.1.refs_10_.refs_3_.refs_0_), channel_id=1, source_target_pairs={{0,1},{8,9},{16,17},{24,25},{1,0},{9,8},{17,16},{25,24},{2,3},{10,... | collective-permute-start | bytes 208904 | tf_op jit(solution)/shard_map/ppermute | solution.py:514
  12.3 5.2 %collective-permute-start.6 = (f32[136,128]{1,0:T(8,128)S(1)}, f32[136,128]{1,0:T(8,128)S(1)}, u32[]{:S(2)}, u32[]{:S(2)}) collective-permute-start(f32[136,128]{1,0:T(8,128)S(1)} %get-tuple-element.53.refs_0_.refs_2_), channel_id=1, source_target_pairs={{0,1},{8,9},{16,17},{24,25},{1,0},{9,8},{17,16},{25,24},{2,3},{10,... | collective-permute-start | bytes 208904 | tf_op jit(solution)/shard_map/ppermute | solution.py:514
  13.3 9.6 %collective-permute-start.8 = (f32[256,128]{1,0:T(8,128)S(1)}, f32[256,128]{1,0:T(8,128)S(1)}, u32[]{:S(2)}, u32[]{:S(2)}) collective-permute-start(f32[256,128]{1,0:T(8,128)S(1)} %rest.1), channel_id=1, source_target_pairs={{0,16},{8,24},{16,0},{24,8},{1,17},{9,25},{17,1},{25,9},{2,18},{10... | collective-permute-start | bytes 393224 | tf_op jit(solution)/shard_map/ppermute | solution.py:514
  15.9 4.4 %collective-permute-start.5 = (f32[136,128]{1,0:T(8,128)S(1)}, f32[136,128]{1,0:T(8,128)S(1)}, u32[]{:S(2)}, u32[]{:S(2)}) collective-permute-start(f32[136,128]{1,0:T(8,128)S(1)} %merge21.1.refs_3_.refs_0_), channel_id=1, source_target_pairs={{0,2},{8,10},{16,18},{24,26},{1,3},{9,11},{17,19},{25,27},{2,0},{1... | collective-permute-start | bytes 208904 | tf_op jit(solution)/shard_map/ppermute | solution.py:514
  17.5 5.4 %collective-permute-start.7 = (f32[136,128]{1,0:T(8,128)S(1)}, f32[136,128]{1,0:T(8,128)S(1)}, u32[]{:S(2)}, u32[]{:S(2)}) collective-permute-start(f32[136,128]{1,0:T(8,128)S(1)} %get-tuple-element.56.refs_0_.refs_2_), channel_id=1, source_target_pairs={{0,2},{8,10},{16,18},{24,26},{1,3},{9,11},{17,19},{25,27},{2,0},{1... | collective-permute-start | bytes 208904 | tf_op jit(solution)/shard_map/ppermute | solution.py:514
  18.4 11.9 %collective-permute-start.9 = (f32[256,128]{1,0:T(8,128)S(1)}, f32[256,128]{1,0:T(8,128)S(1)}, u32[]{:S(2)}, u32[]{:S(2)}) collective-permute-start(f32[256,128]{1,0:T(8,128)S(1)} %found2.1.refs_1_), channel_id=1, source_target_pairs={{0,16},{8,24},{16,0},{24,8},{1,17},{9,25},{17,1},{25,9},{2,18},{10... | collective-permute-start | bytes 393224 | tf_op jit(solution)/shard_map/ppermute | solution.py:514
  20.3 8.0 %collective-permute-start.12 = (f32[136,128]{1,0:T(8,128)S(1)}, f32[136,128]{1,0:T(8,128)S(1)}, u32[]{:S(2)}, u32[]{:S(2)}) collective-permute-start(f32[136,128]{1,0:T(8,128)S(1)} %merge31.1.refs_3_.refs_10_), channel_id=1, source_target_pairs={{0,4},{8,12},{16,20},{24,28},{1,5},{9,13},{17,21},{25,29},{2,6},{1... | collective-permute-start | bytes 208904 | tf_op jit(solution)/shard_map/ppermute | solution.py:514
  23.0 5.3 %collective-permute-start.11 = (f32[136,128]{1,0:T(8,128)S(1)}, f32[136,128]{1,0:T(8,128)S(1)}, u32[]{:S(2)}, u32[]{:S(2)}) collective-permute-start(f32[136,128]{1,0:T(8,128)S(1)} %get-tuple-element.57.refs_2_), channel_id=1, source_target_pairs={{0,4},{8,12},{16,20},{24,28},{1,5},{9,13},{17,21},{25,29},{2,6},{1... | collective-permute-start | bytes 208904 | tf_op jit(solution)/shard_map/ppermute | solution.py:514
  24.8 5.7 %collective-permute-start.10 = (f32[256,128]{1,0:T(8,128)S(1)}, f32[256,128]{1,0:T(8,128)S(1)}, u32[]{:S(2)}, u32[]{:S(2)}) collective-permute-start(f32[256,128]{1,0:T(8,128)S(1)} %found3.1.refs_11_.refs_2_), channel_id=1, source_target_pairs={{0,16},{8,24},{16,0},{24,8},{1,17},{9,25},{17,1},{25,9},{2,18},{10... | collective-permute-start | bytes 393224 | tf_op jit(solution)/shard_map/ppermute | solution.py:514
  28.3 5.0 %collective-permute-start.14 = (f32[256,128]{1,0:T(8,128)S(1)}, f32[256,128]{1,0:T(8,128)S(1)}, u32[]{:S(2)}, u32[]{:S(2)}) collective-permute-start(f32[256,128]{1,0:T(8,128)S(1)} %state.1.refs_3_.refs_1_), channel_id=1, source_target_pairs={{0,16},{8,24},{16,0},{24,8},{1,17},{9,25},{17,1},{25,9},{2,18},{10... | collective-permute-start | bytes 393224 | tf_op jit(solution)/shard_map/ppermute | solution.py:514
  29.3 2.0 %collective-permute-start.15 = (f32[1024,128]{1,0:T(8,128)S(1)}, f32[1024,128]{1,0:T(8,128)S(1)}, u32[]{:S(2)}, u32[]{:S(2)}) collective-permute-start(f32[1024,128]{1,0:T(8,128)S(1)} %joined.1.refs_9_), channel_id=1, source_target_pairs={{0,8},{8,0},{16,24},{24,16},{1,9},{9,1},{17,25},{25,17},{2,10},{10... | collective-permute-start | bytes 1572872 | tf_op jit(solution)/shard_map/ppermute | solution.py:514
  30.5 4.6 %collective-permute-start.13 = (f32[768,128]{1,0:T(8,128)S(1)}, f32[768,128]{1,0:T(8,128)S(1)}, u32[]{:S(2)}, u32[]{:S(2)}) collective-permute-start(f32[768,128]{1,0:T(8,128)S(1)} %theirs.1.refs_9_), channel_id=1, source_target_pairs={{0,8},{8,0},{16,24},{24,16},{1,9},{9,1},{17,25},{25,17},{2,10},{10... | collective-permute-start | bytes 1179656 | tf_op jit(solution)/shard_map/ppermute | solution.py:514
  33.3 1.8 %collective-permute-start.16 = (f32[256,128]{1,0:T(8,128)S(1)}, f32[256,128]{1,0:T(8,128)S(1)}, u32[]{:S(2)}, u32[]{:S(2)}) collective-permute-start(f32[256,128]{1,0:T(8,128)S(1)} %beside.1.refs_10_), channel_id=1, source_target_pairs={{0,8},{8,0},{16,24},{24,16},{1,9},{9,1},{17,25},{25,17},{2,10},{10... | collective-permute-start | bytes 393224 | tf_op jit(solution)/shard_map/ppermute | solution.py:514
